TPU v7x, 32 devices: a whole 2x2x4 slice. The times are simulated.
32 devices in a mesh: seq: 8 (over z, x), exp: 4 (over y, core).
Axes of the slice: x: 2, y: 2, z: 4, core: 2. Of those that a mesh axis runs over, the one named last changes fastest.
Arguments:
- residual: bfloat16 [1024, 2048], P('seq', 'exp'), may hold values from -36 to 36
- queries: bfloat16 [1024, 2048], P('seq', 'exp'), may hold values from -6 to 6
- key_vectors: bfloat16 [1024, 2048], P('seq', 'exp'), may hold values from -6 to 6
- value_vectors: bfloat16 [1024, 2048], P('seq', 'exp'), may hold values from -36 to 36
- head_gain: float32 [2048], P('exp'), may hold values from 0.25 to 1.75
- norm_gain: float32 [2048], replicated, may hold values from 0.25 to 1.75
- routes: int32 [1024, 8], P('seq'), may hold values from 0 to 7, as said below
- route_gates: float32 [1024, 8], P('seq'), may hold values from 0.2 to 1
- expert_in: bfloat16 [8, 2, 2048, 1024], P('seq'), may hold values from -0.125 to 0.125
- expert_out: bfloat16 [8, 1024, 2048], P('seq'), may hold values from -0.1875 to 0.1875
Outputs:
- layer_out: bfloat16 [1024, 2048], P('seq', 'exp')
Inputs may be any that keep to these rules, and one draw needn't show every extreme that they name: `routes`: each row names 8 different experts. In every aligned block of 32 rows no expert is named by more than 32 rows, and the same 2 experts are named by exactly 32 rows in every block.
All inputs are finite; a program needn't handle non-finite values.
Results may differ from a plain program's by a relative error of at most 0.0075.
Values may be sent and summed in bfloat16 or wider, within the bound.
No kernel may reach another device: no remote copies, remote signals or barrier semaphores. Data moves between devices by JAX's collectives and lax.ppermute only.
A program may use at most 128 MiB of HBM per device.

v0:
```python
import jax
import jax.numpy as jnp
from jax import lax
from jax.sharding import PartitionSpec as P

HEAD = 128


def slot_ids(block_routes, expert_count, capacity):
    row_count, top_count = block_routes.shape
    expert_ids = jnp.arange(expert_count, dtype=jnp.int32)
    onehot = (
        (block_routes[:, :, None] == expert_ids[None, None, :])
        .astype(jnp.int32)
        .reshape(row_count * top_count, expert_count)
    )
    earlier = jnp.cumsum(onehot, axis=0) - onehot
    ranking = jnp.sum(earlier * onehot, axis=1).reshape(row_count, top_count)
    return block_routes * capacity + ranking


def weigh_rows(flat_rows, slots, gates):
    picked = flat_rows[slots.reshape(-1)].reshape(
        slots.shape[0], slots.shape[1], flat_rows.shape[1]
    )
    return jnp.sum(picked.astype(jnp.float32) * gates[:, :, None], axis=1)


def per_device(
    residual,
    queries,
    key_vectors,
    value_vectors,
    head_gain,
    norm_gain,
    routes,
    route_gates,
    expert_in,
    expert_out,
):
    row_count, quarter = residual.shape
    head_count = quarter // HEAD
    query_heads = queries.reshape(row_count, head_count, HEAD)
    key_heads = key_vectors.reshape(row_count, head_count, HEAD)
    value_heads = value_vectors.reshape(row_count, head_count, HEAD)
    group_state = jnp.einsum(
        "thd,the->hde", key_heads, value_heads, preferred_element_type=jnp.float32
    )
    my_position = lax.axis_index("seq")
    shard_block = lax.all_gather(group_state[None], "seq", axis=0, tiled=True)
    indices = jnp.arange(shard_block.shape[0], dtype=jnp.int32)
    keeping = (indices < my_position).astype(jnp.float32)
    prior_state = jnp.sum(shard_block * keeping[:, None, None, None], axis=0)
    carried = jnp.einsum(
        "thd,hde->the",
        query_heads.astype(jnp.float32),
        prior_state,
        precision=lax.Precision.HIGHEST,
    )
    positions = jnp.arange(row_count, dtype=jnp.int32)
    causal = (positions[:, None] >= positions[None, :]).astype(jnp.float32)
    scores = (
        jnp.einsum("thd,shd->hts", query_heads, key_heads, preferred_element_type=jnp.float32)
        * causal[None]
    )
    within = jnp.einsum(
        "hts,she->the", scores, value_heads.astype(jnp.float32), precision=lax.Precision.HIGHEST
    )
    raw_output = carried + within
    scaled = raw_output * lax.rsqrt(
        jnp.mean(raw_output * raw_output, axis=-1, keepdims=True) + 1e-06
    )
    attention_out = scaled.reshape(row_count, quarter) * head_gain
    hidden = (residual.astype(jnp.float32) + attention_out).astype(jnp.bfloat16)
    block_rows = lax.all_to_all(hidden, "exp", split_axis=0, concat_axis=1, tiled=True)
    widened = block_rows.astype(jnp.float32)
    normed = (
        widened * lax.rsqrt(jnp.mean(widened * widened, axis=-1, keepdims=True) + 1e-06) * norm_gain
    ).astype(jnp.bfloat16)
    model_width = normed.shape[1]
    part_count = lax.axis_size("exp")
    sub_count = row_count // part_count
    my_index = lax.axis_index("exp")
    expert_count = lax.axis_size("seq") * expert_in.shape[0]
    top_count = routes.shape[1]
    capacity = min(sub_count, max(2, 3 * sub_count * top_count // (2 * expert_count)))
    slot_count = expert_count * capacity
    my_routes = lax.dynamic_slice_in_dim(routes, my_index * sub_count, sub_count, 0)
    my_gates = lax.dynamic_slice_in_dim(route_gates, my_index * sub_count, sub_count, 0)
    my_slots = slot_ids(my_routes, expert_count, capacity)
    columns = jnp.arange(slot_count, dtype=jnp.int32)
    placer = jnp.sum(
        (my_slots[None, :, :] == columns[:, None, None]).astype(jnp.int32), axis=2
    ).astype(jnp.bfloat16)
    outgoing = (
        jnp.dot(placer, normed, preferred_element_type=jnp.float32)
        .astype(jnp.bfloat16)
        .reshape(expert_count, capacity, model_width)
    )
    arrived = lax.all_to_all(outgoing, "seq", split_axis=0, concat_axis=0, tiled=True)
    flat_rows = arrived.reshape(-1, model_width)
    gate_up = jnp.einsum("nd,gdf->gnf", flat_rows, expert_in[0], preferred_element_type=jnp.float32)
    activated = (jax.nn.silu(gate_up[0]) * gate_up[1]).astype(jnp.bfloat16)
    produced = jnp.dot(activated, expert_out[0], preferred_element_type=jnp.float32).astype(
        jnp.bfloat16
    )
    answered = produced.reshape(arrived.shape)
    returned_rows = lax.all_to_all(answered, "seq", split_axis=0, concat_axis=0, tiled=True)
    mixed_rows = weigh_rows(returned_rows.reshape(slot_count, model_width), my_slots, my_gates)
    moe_out = lax.all_to_all(
        mixed_rows.astype(jnp.bfloat16), "exp", split_axis=1, concat_axis=0, tiled=True
    ).astype(mixed_rows.dtype)
    return (hidden.astype(jnp.float32) + moe_out).astype(jnp.bfloat16)


def solution(mesh):
    placed = (
        P("seq", "exp"),
        P("seq", "exp"),
        P("seq", "exp"),
        P("seq", "exp"),
        P("exp"),
        P(),
        P("seq", None),
        P("seq", None),
        P("seq", None, None, None),
        P("seq", None, None),
    )
    return jax.shard_map(
        per_device, mesh=mesh, in_specs=placed, out_specs=P("seq", "exp"), check_vma=False
    )
```

profile of v0, /device:TPU:0, one launch (start us, length us, event | category | flops | bytes accessed | tf_op | source)
XLA Modules:
  0.0 157.4 jit_solution(15334136404828118509)
XLA Ops:
  6.5 0.0 copy-start
  6.5 0.0 copy-start.1
  6.5 0.0 all-gather.3.cloned.1.call-start
  6.5 1.1 copy.63
  7.6 0.0 copy-done
  7.6 1.0 fusion.19
  8.6 0.0 all-gather.3.cloned.1.call-update
  8.6 0.8 constant_dynamic-slice_fusion.1
  9.4 0.1 copy.62
  9.5 0.1 eq.43
  9.5 0.1 eq.39
  9.6 0.6 reduce-window.6
  10.2 0.2 slice_reduce_fusion
  10.5 0.1 fusion.31
  10.6 0.1 reshape.135
  10.7 1.1 convolution_multiply_fusion
  11.8 49.7 %all-gather.3.cloned.1.call-done = f32[32,128,128]{2,1,0:T(8,128)} async-done(((f32[4,128,128]{2,1,0:T(8,128)}), f32[32,128,128]{2,1,0:T(8,128)}) %all-gather.3.cloned.1.call-update) | async-done | bytes 2097168 | tf_op jit(solution)/shard_map/all_gather | solution.py:50
  61.5 0.0 copy-start.2
  61.5 0.0 copy-start.5
  61.5 1.9 %multiply_reduce_fusion = f32[4,128,128]{2,1,0:T(8,128)S(1)} fusion(f32[8,4,128,128]{3,2,1,0:T(8,128)} %bitcast.88, f32[8]{0:T(128)S(1)} %compare_convert_fusion), kind=kLoop, calls=%fused_computation.9 | loop fusion | flops 983040 | bytes 2359328 | tf_op jit(solution)/shard_map/reduce_sum | solution.py:53
  63.4 0.0 copy-done.1
  63.4 0.4 convolution_bitcast_fusion.1
  63.8 0.0 copy-start.3
  63.8 0.4 multiply_reduce_fusion.1
  64.3 0.1 copy.56
  64.4 0.0 copy-done.2
  64.4 0.0 copy-done.5
  64.4 0.7 add_convert_fusion
  65.1 3.3 %all-to-all-start = ((bf16[4,32,512]{2,1,0:T(8,128)(2,1)}), bf16[4,32,512]{2,1,0:T(8,128)(2,1)S(1)}, u32[]{:S(2)}, u32[]{:S(2)}) async-start(bf16[4,32,512]{2,1,0:T(8,128)(2,1)} %bitcast.6), calls=%async_computation | async-start | bytes 262144 | tf_op jit(solution)/shard_map/all_to_all | solution.py:75
  68.5 0.1 convert_reduce_fusion
  68.6 4.4 %all-to-all-done = bf16[4,32,512]{2,1,0:T(8,128)(2,1)S(1)} async-done(((bf16[4,32,512]{2,1,0:T(8,128)(2,1)}), bf16[4,32,512]{2,1,0:T(8,128)(2,1)S(1)}, u32[]{:S(2)}, u32[]{:S(2)}) %all-to-all-start) | async-done | bytes 131104 | tf_op jit(solution)/shard_map/all_to_all | solution.py:75
  73.1 0.1 fusion.15
  73.3 0.0 copy-done.3
  73.3 0.5 convolution_convert_fusion
  73.8 28.3 %all_to_all.33 = bf16[8,32,2048]{2,1,0:T(8,128)(2,1)S(1)} all-to-all(bf16[8,32,2048]{2,1,0:T(8,128)(2,1)S(1)} %bitcast.87), channel_id=1, replica_groups=mesh['seq'=8,'exp'=4] {'seq'}, dimensions={0} | all-to-all | bytes 2097152 | tf_op jit(solution)/shard_map/all_to_all | solution.py:100
  102.1 0.0 copy-start.6
  102.1 5.9 %fusion.8 = f32[2,256,1024]{2,1,0:T(8,128)S(1)} fusion(bf16[256,2048,1]{1,0,2:T(8,128)(2,1)S(1)} %bitcast.92, bf16[1,2,2048,1024]{3,2,1,0:T(8,128)(2,1)} %param.18), kind=kOutput, calls=%fused_computation.10 | convolution fusion | flops 2147483648 | bytes 11534336 | tf_op jit(solution)/shard_map/nd,gdf->gnf/dot_general | solution.py:102
  108.0 0.0 copy-done.6
  108.0 2.3 %fusion.4 = bf16[256,2048]{1,0:T(8,128)(2,1)} fusion(bf16[1,1024,2048]{2,1,0:T(8,128)(2,1)S(1)} %copy-done.6, f32[2,256,1024]{2,1,0:T(8,128)S(1)} %fusion.8), kind=kOutput, calls=%fused_computation.5 | convolution fusion | flops 1075838976 | bytes 7340032 | tf_op jit(solution)/shard_map/dot_general | solution.py:104
  110.4 0.0 copy-start.4
  110.4 3.7 %all-to-all-start.2 = ((bf16[8,32,2048]{2,1,0:T(8,128)(2,1)}), bf16[8,32,2048]{2,1,0:T(8,128)(2,1)S(1)}, u32[]{:S(2)}, u32[]{:S(2)}) async-start(bf16[8,32,2048]{2,1,0:T(8,128)(2,1)} %bitcast.15), calls=%async_computation.2 | async-start | bytes 2097152 | tf_op jit(solution)/shard_map/all_to_all | solution.py:108
  114.1 0.1 reshape.140
  114.1 0.0 copy-done.4
  114.1 0.1 constant_dynamic-slice_fusion
  114.2 0.1 copy.59
  114.3 25.2 %all-to-all-done.2 = bf16[8,32,2048]{2,1,0:T(8,128)(2,1)S(1)} async-done(((bf16[8,32,2048]{2,1,0:T(8,128)(2,1)}), bf16[8,32,2048]{2,1,0:T(8,128)(2,1)S(1)}, u32[]{:S(2)}, u32[]{:S(2)}) %all-to-all-start.2) | async-done | bytes 1048608 | tf_op jit(solution)/shard_map/all_to_all | solution.py:108
  139.5 1.4 gather_fusion
  140.9 1.0 fusion.7
  141.9 7.0 %all_to_all.34 = bf16[32,4,512]{2,0,1:T(8,128)(2,1)S(1)} all-to-all(bf16[32,4,512]{2,0,1:T(8,128)(2,1)S(1)} %bitcast.95), channel_id=1, replica_groups=mesh['seq'=8,'exp'=4] {'exp'}, dimensions={1} | all-to-all | bytes 262144 | tf_op jit(solution)/shard_map/all_to_all | solution.py:110
  148.9 1.6 %fusion.16 = bf16[128,512]{1,0:T(8,128)(2,1)} fusion(bf16[128,512]{1,0:T(8,128)(2,1)} %add_convert_fusion, bf16[32,4,512]{2,0,1:T(8,128)(2,1)S(1)} %all_to_all.34), kind=kLoop, calls=%fused_computation.22 | loop fusion | flops 262144 | bytes 393216 | tf_op jit(solution)/shard_map/convert_element_type | solution.py:113
  (14 shorter events, 0.2 us)
Async XLA Ops:
  6.5 1.1 copy-start
  6.5 56.9 %copy-start.1 = (bf16[128,512]{1,0:T(8,128)(2,1)S(1)}, bf16[128,512]{1,0:T(8,128)(2,1)}, u32[]{:S(2)}) copy-start(bf16[128,512]{1,0:T(8,128)(2,1)} %param.11) | copy-start | bytes 393220
  6.5 55.0 %all-gather.3.cloned.1.call-start = ((), (), s32[]{:S(2)}) async-start(), calls=%async_computation.4 | async-start | bytes 2359296 | tf_op jit(solution)/shard_map/all_gather | solution.py:50
  61.5 2.9 %copy-start.2 = (bf16[128,512]{1,0:T(8,128)(2,1)S(1)}, bf16[128,512]{1,0:T(8,128)(2,1)}, u32[]{:S(2)}) copy-start(bf16[128,512]{1,0:T(8,128)(2,1)} %param.10) | copy-start | bytes 393220
  61.5 2.9 %copy-start.5 = (f32[512]{0:T(512)S(1)}, f32[512]{0:T(512)}, u32[]{:S(2)}) copy-start(f32[512]{0:T(512)} %param.14) | copy-start | bytes 6148
  63.8 9.5 %copy-start.3 = (f32[2048]{0:T(1024)S(1)}, f32[2048]{0:T(1024)}, u32[]{:S(2)}) copy-start(f32[2048]{0:T(1024)} %param.15) | copy-start | bytes 24580
  65.1 7.9 %all-to-all-start = ((bf16[4,32,512]{2,1,0:T(8,128)(2,1)}), bf16[4,32,512]{2,1,0:T(8,128)(2,1)S(1)}, u32[]{:S(2)}, u32[]{:S(2)}) async-start(bf16[4,32,512]{2,1,0:T(8,128)(2,1)} %bitcast.6), calls=%async_computation | async-start | bytes 262144 | tf_op jit(solution)/shard_map/all_to_all | solution.py:75
  102.1 5.9 %copy-start.6 = (bf16[1,1024,2048]{2,1,0:T(8,128)(2,1)S(1)}, bf16[1,1024,2048]{2,1,0:T(8,128)(2,1)}, u32[]{:S(2)}) copy-start(bf16[1,1024,2048]{2,1,0:T(8,128)(2,1)} %param.19) | copy-start | bytes 12582916
  110.4 3.8 %copy-start.4 = (f32[128,8]{0,1:T(8,128)S(1)}, f32[128,8]{0,1:T(8,128)}, u32[]{:S(2)}) copy-start(f32[128,8]{0,1:T(8,128)} %param.17) | copy-start | bytes 12292
  110.4 29.2 %all-to-all-start.2 = ((bf16[8,32,2048]{2,1,0:T(8,128)(2,1)}), bf16[8,32,2048]{2,1,0:T(8,128)(2,1)S(1)}, u32[]{:S(2)}, u32[]{:S(2)}) async-start(bf16[8,32,2048]{2,1,0:T(8,128)(2,1)} %bitcast.15), calls=%async_computation.2 | async-start | bytes 2097152 | tf_op jit(solution)/shard_map/all_to_all | solution.py:108
Sparse Core Ops, SparseCore 0:
  9.5 51.9 all-gather.2
where the time goes:
time: 158 us; the launch traced here: 157 us
  waiting for transfers between devices  79.4 us (50%)
  blocking collectives  35.4 us (22%)
  between operations  13.6 us (9%)
  matrix products  11.6 us (7%)
  starting transfers between devices  7.02 us (4%)
  other arithmetic  6.25 us (4%)
  local copies, waits for them, and re-layouts  4.16 us (3%)
    all_gather x1, waiting for transfers between devices, per_device(): shard_block = lax.all_gather(group_state[None], 'seq', axis=0, tiled=True)  49.7 us
    all_to_all x1, blocking collectives, per_device(): lax.all_to_all(outgoing, 'seq', split_axis=0, concat_axis=0, tiled=True)  28.3 us
    all_to_all x1, waiting for transfers between devices, per_device(): lax.all_to_all(answered, 'seq', split_axis=0, concat_axis=0, tiled=True)  25.2 us
    all_to_all x1, blocking collectives, per_device(): lax.all_to_all(mixed_rows.astype(jnp.bfloat16), 'exp', split_axis=1, conc...  7.02 us
    dot_general x1, matrix products, per_device(): jnp.einsum('nd,gdf->gnf', flat_rows, expert_in[0], preferred_element_type...  5.88 us
    all_to_all x1, waiting for transfers between devices, per_device(): lax.all_to_all(hidden, 'exp', split_axis=0, concat_axis=1, tiled=True)  4.44 us
    all_to_all x1, starting transfers between devices, per_device(): lax.all_to_all(answered, 'seq', split_axis=0, concat_axis=0, tiled=True)  3.69 us
    all_to_all x1, starting transfers between devices, per_device(): lax.all_to_all(hidden, 'exp', split_axis=0, concat_axis=1, tiled=True)  3.33 us
  transfers between devices with their start and end apart: 3, of which 3 were waited for; matrix products, arithmetic and copies ran while one was open for 2% of the time, Pallas kernels for 0%

commit v1 on v0

v1 whole, which is shorter than its diff:
```python
import functools

import jax
import jax.numpy as jnp
from jax import lax
from jax.experimental import pallas as pl
from jax.experimental.pallas import tpu as pltpu
from jax.sharding import PartitionSpec as P

HEAD = 128
F32 = jnp.float32
BF16 = jnp.bfloat16
WHOLE = pl.BlockSpec(memory_space=pltpu.VMEM)
SCALAR = pl.BlockSpec(memory_space=pltpu.SMEM)


def call(kernel, outs, inputs, flops=0, limit=16 << 20):
    moved = sum(a.size * a.dtype.itemsize for a in inputs)
    moved += sum(a.size * a.dtype.itemsize for a in outs)
    return pl.pallas_call(
        kernel,
        out_shape=outs,
        in_specs=[SCALAR] + [WHOLE] * (len(inputs) - 1),
        out_specs=[WHOLE] * len(outs),
        compiler_params=pltpu.CompilerParams(vmem_limit_bytes=limit),
        cost_estimate=pl.CostEstimate(flops=flops, bytes_accessed=moved, transcendentals=0),
    )(*inputs)


def shape(dims, dtype):
    return jax.ShapeDtypeStruct(dims, dtype)


def split(value):
    high = value.astype(BF16)
    return high, (value - high.astype(F32)).astype(BF16)


def state_kernel(scalars, key_ref, value_ref, kept_ref, given_ref):
    width = key_ref.shape[1] // 2
    place = scalars[1]
    for h in range(key_ref.shape[1] // HEAD):
        cols = slice(h * HEAD, (h + 1) * HEAD)
        state = lax.dot_general(
            key_ref[:, cols], value_ref[:, cols], (((0,), (0,)), ((), ())),
            preferred_element_type=F32,
        ).astype(BF16)
        half, inner = divmod(h * HEAD, width)

        @pl.when(place == half)
        def _():
            kept_ref[:, inner:inner + HEAD] = state

        @pl.when(place != half)
        def _():
            given_ref[:, inner:inner + HEAD] = state


def within_kernel(scalars, query_ref, key_ref, value_ref, out_ref):
    rows = query_ref.shape[0]
    causal = lax.broadcasted_iota(jnp.int32, (rows, rows), 0) >= lax.broadcasted_iota(
        jnp.int32, (rows, rows), 1
    )
    for h in range(query_ref.shape[1] // HEAD):
        cols = slice(h * HEAD, (h + 1) * HEAD)
        scores = lax.dot_general(
            query_ref[:, cols], key_ref[:, cols], (((1,), (1,)), ((), ())),
            preferred_element_type=F32,
        )
        high, low = split(jnp.where(causal, scores, 0.0))
        value = value_ref[:, cols]
        out_ref[:, cols] = jnp.dot(high, value, preferred_element_type=F32) + jnp.dot(
            low, value, preferred_element_type=F32
        )


def attend_kernel(
    parts, scalars, query_ref, mine_ref, other_ref, within_ref, residual_ref, gain_ref,
    hidden_ref, own_ref, *piece_refs
):
    place = scalars[1]
    width = query_ref.shape[1] // 2
    mine = mine_ref[...].astype(F32)
    other = other_ref[...].astype(F32)
    halves = [jnp.where(place == 0, mine, other), jnp.where(place == 0, other, mine)]
    for h in range(query_ref.shape[1] // HEAD):
        cols = slice(h * HEAD, (h + 1) * HEAD)
        half, inner = divmod(h * HEAD, width)
        query = query_ref[:, cols]
        high, low = split(halves[half][:, inner:inner + HEAD])
        raw = (
            jnp.dot(query, high, preferred_element_type=F32)
            + jnp.dot(query, low, preferred_element_type=F32)
            + within_ref[:, cols]
        )
        scaled = raw * lax.rsqrt(jnp.mean(raw * raw, axis=-1, keepdims=True) + 1e-06)
        hidden_ref[:, cols] = (
            residual_ref[:, cols].astype(F32) + scaled * gain_ref[:, cols]
        ).astype(BF16)
    count = hidden_ref.shape[0] // parts
    for j in range(parts):
        target = own_ref if j == 0 else piece_refs[j - 1]
        start = pl.multiple_of((scalars[0] ^ j) * count, count)
        target[...] = hidden_ref[pl.ds(start, count), :]


def norm_kernel(parts, scalars, gain_ref, pack_ref, *refs):
    pieces, out_ref = refs[:parts], refs[parts]
    width = pieces[0].shape[1]
    total = 0.0
    for ref in pieces:
        value = ref[...].astype(F32)
        total += jnp.sum(value * value, axis=-1, keepdims=True)
    scale = lax.rsqrt(total / (parts * width) + 1e-06)
    for j in range(parts):
        start = pl.multiple_of((scalars[0] ^ j) * width, width)
        cols = pl.ds(start, width)
        out_ref[:, cols] = (pieces[j][...].astype(F32) * scale * gain_ref[:, cols]).astype(BF16)
    out_ref[:, parts * width:] = pack_ref[...]


def expert_kernel(blocks, scalars, *refs):
    x_refs = refs[:blocks]
    gate_ref, up_ref, down_ref = refs[blocks:blocks + 3]
    out_refs = refs[blocks + 3:2 * blocks + 3]
    rows_ref, acc_ref = refs[2 * blocks + 3:]
    step = pl.program_id(0)
    width = acc_ref.shape[1]
    spans = []
    first = 0
    for ref in x_refs:
        spans.append(slice(first, first + ref.shape[0]))
        first += ref.shape[0]

    @pl.when(step == 0)
    def _():
        for ref, span in zip(x_refs, spans):
            rows_ref[span, :] = ref[:, :width]

    rows = rows_ref[...]
    gate = jnp.dot(rows, gate_ref[0, 0], preferred_element_type=F32)
    up = jnp.dot(rows, up_ref[0, 0], preferred_element_type=F32)
    activated = (gate / (1.0 + jnp.exp(-gate)) * up).astype(BF16)
    part = jnp.dot(activated, down_ref[0], preferred_element_type=F32)

    @pl.when(step == 0)
    def _():
        acc_ref[...] = part

    @pl.when(step > 0)
    def _():
        acc_ref[...] += part

    @pl.when(step == pl.num_programs(0) - 1)
    def _():
        experts = scalars[2]
        for x_ref, out_ref, span in zip(x_refs, out_refs, spans):
            pack = x_ref[:, width:].astype(F32)
            lane = lax.broadcasted_iota(jnp.int32, pack.shape, 1)
            chosen = (lane == scalars[3]) | (lane == scalars[3] + experts)
            weight = jnp.sum(jnp.where(chosen, pack, 0.0), axis=-1, keepdims=True)
            produced = acc_ref[span, :].astype(BF16).astype(F32)
            out_ref[...] = (produced * weight).astype(BF16)


def run_expert(scalars, blocks, expert_in, expert_out):
    width, hidden_units = expert_in.shape[2:]
    total = sum(b.shape[0] for b in blocks)
    chunk = min(hidden_units, 256)
    steps = hidden_units // chunk
    kernel = functools.partial(expert_kernel, len(blocks))
    return pl.pallas_call(
        kernel,
        grid=(steps,),
        out_shape=[shape((b.shape[0], width), BF16) for b in blocks],
        in_specs=[SCALAR]
        + [pl.BlockSpec(b.shape, lambda f: (0, 0)) for b in blocks]
        + [
            pl.BlockSpec((1, 1, width, chunk), lambda f: (0, 0, 0, f)),
            pl.BlockSpec((1, 1, width, chunk), lambda f: (0, 1, 0, f)),
            pl.BlockSpec((1, chunk, width), lambda f: (0, f, 0)),
        ],
        out_specs=[pl.BlockSpec((b.shape[0], width), lambda f: (0, 0)) for b in blocks],
        scratch_shapes=[pltpu.VMEM((total, width), BF16), pltpu.VMEM((total, width), F32)],
        compiler_params=pltpu.CompilerParams(vmem_limit_bytes=32 << 20),
        cost_estimate=pl.CostEstimate(
            flops=6 * total * width * hidden_units,
            bytes_accessed=6 * width * hidden_units + 4 * total * width,
            transcendentals=total * hidden_units,
        ),
    )(scalars, *blocks, expert_in, expert_in, expert_out)


def ring_order(count):
    return list(range(0, count, 2)) + list(range(1, count, 2))[::-1]


def add_rows(*terms):
    return sum(t.astype(F32) for t in terms).astype(BF16)


def dense_experts(block, scalars, expert_in, expert_out):
    count = lax.axis_size("seq")
    width = expert_in.shape[2]
    order = ring_order(count)
    forward = [(order[p], order[(p + 1) % count]) for p in range(count)]
    backward = [(b, a) for a, b in forward]
    half = block.shape[0] // 2
    far = count // 2
    ahead, behind = [block], [block]
    for step in range(1, far):
        ahead.append(lax.ppermute(ahead[-1], "seq", forward))
        behind.append(lax.ppermute(behind[-1], "seq", backward))
    top = lax.ppermute(ahead[-1][:half], "seq", forward)
    bottom = lax.ppermute(behind[-1][half:], "seq", backward)
    blocks = [block] + ahead[1:] + behind[1:] + [top, bottom]
    made = run_expert(scalars, blocks, expert_in, expert_out)
    own, from_ahead, from_behind = made[0], made[1:far], made[far:2 * far - 1]
    top, bottom = made[-2:]
    going, coming = (
        lax.ppermute(top, "seq", forward),
        lax.ppermute(bottom, "seq", backward),
    )
    for distance in range(far - 1, 0, -1):
        to_front, to_back = from_behind[distance - 1], from_ahead[distance - 1]
        if distance == far - 1:
            going = jnp.concatenate([add_rows(going, to_front[:half]), to_front[half:]])
            coming = jnp.concatenate([to_back[:half], add_rows(coming, to_back[half:])])
        else:
            going = add_rows(going, to_front)
            coming = add_rows(coming, to_back)
        going = lax.ppermute(going, "seq", forward)
        coming = lax.ppermute(coming, "seq", backward)
    return own, going, coming


def mix_kernel(parts, scalars, a_ref, b_ref, c_ref, *out_refs):
    width = out_refs[0].shape[1]
    for j, out_ref in enumerate(out_refs):
        start = pl.multiple_of((scalars[0] ^ j) * width, width)
        cols = pl.ds(start, width)
        out_ref[...] = (
            a_ref[:, cols].astype(F32) + b_ref[:, cols].astype(F32) + c_ref[:, cols].astype(F32)
        ).astype(BF16)


def final_kernel(parts, scalars, hidden_ref, *refs):
    out_ref = refs[parts]
    count = out_ref.shape[0] // parts
    for j in range(parts):
        rows = pl.ds(pl.multiple_of((scalars[0] ^ j) * count, count), count)
        out_ref[rows, :] = (
            hidden_ref[rows, :].astype(F32) + refs[j][...].astype(F32)
        ).astype(BF16)


def slot_ids(block_routes, expert_count, capacity):
    row_count, top_count = block_routes.shape
    expert_ids = jnp.arange(expert_count, dtype=jnp.int32)
    onehot = (
        (block_routes[:, :, None] == expert_ids[None, None, :])
        .astype(jnp.int32)
        .reshape(row_count * top_count, expert_count)
    )
    earlier = jnp.cumsum(onehot, axis=0) - onehot
    ranking = jnp.sum(earlier * onehot, axis=1).reshape(row_count, top_count)
    return block_routes * capacity + ranking


def routed_experts(normed, my_routes, my_gates, expert_in, expert_out):
    sub_count, model_width = normed.shape
    expert_count = lax.axis_size("seq") * expert_in.shape[0]
    top_count = my_routes.shape[1]
    capacity = min(sub_count, max(2, 3 * sub_count * top_count // (2 * expert_count)))
    slot_count = expert_count * capacity
    my_slots = slot_ids(my_routes, expert_count, capacity)
    columns = jnp.arange(slot_count, dtype=jnp.int32)
    placer = jnp.sum(
        (my_slots[None, :, :] == columns[:, None, None]).astype(jnp.int32), axis=2
    ).astype(BF16)
    outgoing = (
        jnp.dot(placer, normed, preferred_element_type=F32)
        .astype(BF16)
        .reshape(expert_count, capacity, model_width)
    )
    arrived = lax.all_to_all(outgoing, "seq", split_axis=0, concat_axis=0, tiled=True)
    flat_rows = arrived.reshape(-1, model_width)
    gate_up = jnp.einsum("nd,gdf->gnf", flat_rows, expert_in[0], preferred_element_type=F32)
    activated = (jax.nn.silu(gate_up[0]) * gate_up[1]).astype(BF16)
    produced = jnp.dot(activated, expert_out[0], preferred_element_type=F32).astype(BF16)
    answered = produced.reshape(arrived.shape)
    returned = lax.all_to_all(answered, "seq", split_axis=0, concat_axis=0, tiled=True)
    picked = returned.reshape(slot_count, model_width)[my_slots.reshape(-1)].reshape(
        sub_count, top_count, model_width
    )
    return jnp.sum(picked.astype(F32) * my_gates[:, :, None], axis=1)


def exchange(pieces, axis):
    count = lax.axis_size(axis)
    return [
        lax.ppermute(piece, axis, [(i, i ^ j) for i in range(count)])
        for j, piece in enumerate(pieces, start=1)
    ]


def prior_states(scalars, key_vectors, value_vectors):
    rows, width = key_vectors.shape
    count = lax.axis_size("seq")
    swap = [(i, i ^ 1) for i in range(count)]
    half = shape((HEAD, width // 2), BF16)
    kept, given = call(
        state_kernel, [half, half], [scalars, key_vectors, value_vectors],
        flops=2 * rows * width * HEAD,
    )
    partner = lax.ppermute(given, "seq", swap)
    running = add_rows(kept, partner)
    before = jnp.zeros(half.shape, F32)
    distance = 2
    while distance < count:
        came = lax.ppermute(
            running, "seq", [(i, i + distance) for i in range(count - distance)]
        )
        before = before + came.astype(F32)
        if 2 * distance < count:
            running = add_rows(running, came)
        distance *= 2
    first = scalars[1] == 0
    mine = before + jnp.where(first, 0.0, partner.astype(F32))
    sent = jnp.where(first, before + kept.astype(F32), before).astype(BF16)
    other = lax.ppermute(sent, "seq", swap)
    return mine, other


def per_device(
    residual,
    queries,
    key_vectors,
    value_vectors,
    head_gain,
    norm_gain,
    routes,
    route_gates,
    expert_in,
    expert_out,
):
    rows, width = residual.shape
    parts = lax.axis_size("exp")
    count = rows // parts
    experts = lax.axis_size("seq") * expert_in.shape[0]
    position = lax.axis_index("seq")
    my_index = lax.axis_index("exp")
    scalars = jnp.stack([my_index, position % 2, experts, position]).astype(jnp.int32)
    mine, other = prior_states(scalars, key_vectors, value_vectors)
    [within] = call(
        within_kernel, [shape((rows, width), F32)],
        [scalars, queries, key_vectors, value_vectors], flops=6 * rows * rows * width,
    )
    piece = shape((count, width), BF16)
    hidden, own, *pieces = call(
        functools.partial(attend_kernel, parts),
        [shape((rows, width), BF16), piece] + [piece] * (parts - 1),
        [scalars, queries, mine, other, within, residual, head_gain[None, :]],
        flops=4 * rows * width * HEAD,
    )
    my_routes = lax.dynamic_slice_in_dim(routes, my_index * count, count, 0)
    my_gates = lax.dynamic_slice_in_dim(route_gates, my_index * count, count, 0)
    weights = jnp.sum(
        jnp.where(
            my_routes[:, :, None] == jnp.arange(experts, dtype=jnp.int32),
            my_gates[:, :, None],
            0.0,
        ),
        axis=1,
    )
    high = lax.reduce_precision(weights, 8, 7)
    lanes = -(-2 * experts // HEAD) * HEAD
    pack = jnp.pad(
        jnp.concatenate([high, weights - high], axis=1), ((0, 0), (0, lanes - 2 * experts))
    ).astype(BF16)
    gathered = exchange(pieces, "exp")
    [block] = call(
        functools.partial(norm_kernel, parts),
        [shape((count, width * parts + lanes), BF16)],
        [scalars, norm_gain[None, :], pack, own] + gathered,
    )
    if routes.shape[1] == experts:
        terms = dense_experts(block, scalars, expert_in, expert_out)
    else:
        mixed = routed_experts(
            block[:, : width * parts], my_routes, my_gates, expert_in, expert_out
        )
        nothing = jnp.zeros_like(mixed)
        terms = (mixed, nothing, nothing)
    own, *pieces = call(
        functools.partial(mix_kernel, parts),
        [shape((count, width), BF16)] * parts,
        [scalars, *terms],
    )
    returned = exchange(pieces, "exp")
    [out] = call(
        functools.partial(final_kernel, parts),
        [shape((rows, width), BF16)],
        [scalars, hidden, own] + returned,
    )
    return out


def solution(mesh):
    placed = (
        P("seq", "exp"),
        P("seq", "exp"),
        P("seq", "exp"),
        P("seq", "exp"),
        P("exp"),
        P(),
        P("seq", None),
        P("seq", None),
        P("seq", None, None, None),
        P("seq", None, None),
    )
    return jax.shard_map(
        per_device, mesh=mesh, in_specs=placed, out_specs=P("seq", "exp"), check_vma=False
    )
```

time: 158 us -> 97.8 us (0.62)
  waiting for transfers between devices: 79.4 us -> 36.1 us
  blocking collectives: 35.4 us -> 0 us
  starting transfers between devices: 7.02 us -> 34.7 us
  between operations: 13.6 us -> 0.21 us
  Pallas kernels: 0 us -> 12.5 us
  matrix products: 11.6 us -> 0 us
  local copies, waits for them, and re-layouts: 4.16 us -> 13.4 us
  other arithmetic: 6.25 us -> 0.45 us
    all_gather x1 -> x0, waiting for transfers between devices: 49.7 us -> none  [per_device(): shard_block = lax.all_gather(group_state[None], 'seq', axis=0, tiled=True)]
    ppermute x0 -> x26, waiting for transfers between devices: none -> 36.1 us  [the longest x3 10.2 us: dense_experts(): behind.append(lax.ppermute(behind[-1], 'seq', backward))]
    all_to_all x2 -> x0, blocking collectives: 35.4 us -> none  [the longest x1 28.3 us: per_device(): lax.all_to_all(outgoing, 'seq', split_axis=0, concat_axis=0, tiled=True)]
    ppermute x0 -> x26, starting transfers between devices: none -> 34.7 us  [the longest x2 9.29 us: prior_states(): lax.ppermute(running, 'seq', [(i, i + distance) for i in range(count - di...]
    all_to_all x2 -> x0, waiting for transfers between devices: 29.7 us -> none  [the longest x1 25.2 us: per_device(): lax.all_to_all(answered, 'seq', split_axis=0, concat_axis=0, tiled=True)]
    pallas_call x0 -> x7, Pallas kernels: none -> 12.5 us  [the longest x1 6.9 us: run_expert(): pl.pallas_call(kernel, grid=(steps,), out_shape=[shape((b.shape[0], width...]
    unnamed x15 -> x22, local copies, waits for them, and re-layouts: 0.11 us -> 12.4 us
    dot_general x7 -> x0, matrix products: 11.6 us -> none  [the longest x1 5.88 us: per_device(): jnp.einsum('nd,gdf->gnf', flat_rows, expert_in[0], preferred_element_type...]
  transfers between devices with their start and end apart: 3 -> 26, of which waited for: 3 -> 17; matrix products, arithmetic and copies ran while one was open for 2% -> 1% of each run, Pallas kernels for 0% -> 1%
where the time goes in v1:
time: 97.8 us; the launch traced here: 97.4 us
  waiting for transfers between devices  36.1 us (37%)
  starting transfers between devices  34.7 us (35%)
  local copies, waits for them, and re-layouts  13.4 us (14%)
  Pallas kernels  12.5 us (13%)
    unnamed x22, local copies, waits for them, and re-layouts  12.4 us
    ppermute x3, waiting for transfers between devices, dense_experts(): behind.append(lax.ppermute(behind[-1], 'seq', backward))  10.2 us
    ppermute x2, starting transfers between devices, prior_states(): lax.ppermute(running, 'seq', [(i, i + distance) for i in range(count - di...  9.29 us
    ppermute x3, waiting for transfers between devices, dense_experts(): coming = lax.ppermute(coming, 'seq', backward)  8.84 us
    pallas_call x1, Pallas kernels, run_expert(): pl.pallas_call(kernel, grid=(steps,), out_shape=[shape((b.shape[0], width...  6.9 us
    pallas_call x6, Pallas kernels, call(): pl.pallas_call(kernel, out_shape=outs, in_specs=[SCALAR] + [WHOLE] * (len...  5.6 us
    ppermute x6, waiting for transfers between devices, exchange(): lax.ppermute(piece, axis, [(i, i ^ j) for i in range(count)])  5.53 us
    ppermute x3, starting transfers between devices, dense_experts(): ahead.append(lax.ppermute(ahead[-1], 'seq', forward))  5.17 us
  transfers between devices with their start and end apart: 26, of which 17 were waited for; matrix products, arithmetic and copies ran while one was open for 1% of the time, Pallas kernels for 1%

profile of v1, /device:TPU:0, one launch (start us, length us, event | category | flops | bytes accessed | tf_op | source)
XLA Modules:
  0.0 97.4 jit_solution(13552754341633242000)
XLA Ops:
  0.0 0.1 pad_add_fusion.scalars
  0.1 0.9 copy-done.4
  1.0 0.9 copy-done.6
  1.9 1.3 %shard_map.100 = (bf16[128,256]{1,0:T(8,128)(2,1)S(1)}, bf16[128,256]{1,0:T(8,128)(2,1)S(1)}) custom-call(s32[4]{0:T(128)S(1)} %pad_add_fusion.scalars, bf16[128,512]{1,0:T(8,128)(2,1)S(1)} %copy-done.4, bf16[128,512]{1,0:T(8,128)(2,1)S(1)} %copy-done.6), custom_call_target="tpu_custom_call" | custom-call | flops 16777216 | bytes 393232 | tf_op jit(solution)/shard_map/pallas_call | solution.py:20
  3.2 3.0 %collective-permute-start = (bf16[128,256]{1,0:T(8,128)(2,1)S(1)}, bf16[128,256]{1,0:T(8,128)(2,1)S(1)}, u32[]{:S(2)}, u32[]{:S(2)}) collective-permute-start(bf16[128,256]{1,0:T(8,128)(2,1)S(1)} %get-tuple-element.26), channel_id=1, source_target_pairs={{0,4},{4,0},{8,12},{12,8},{16,20},{20,16},{24,28},{28,24},{1,5},{5... | collective-permute-start | bytes 196616 | tf_op jit(solution)/shard_map/ppermute | solution.py:316
  6.2 0.1 constant_dynamic-slice_fusion.1
  6.3 2.2 %collective-permute-done = bf16[128,256]{1,0:T(8,128)(2,1)S(1)} collective-permute-done((bf16[128,256]{1,0:T(8,128)(2,1)S(1)}, bf16[128,256]{1,0:T(8,128)(2,1)S(1)}, u32[]{:S(2)}, u32[]{:S(2)}) %collective-permute-start) | collective-permute-done | bytes 65568 | tf_op jit(solution)/shard_map/ppermute | solution.py:316
  8.5 4.0 %collective-permute-start.1 = (bf16[128,256]{1,0:T(8,128)(2,1)S(1)}, bf16[128,256]{1,0:T(8,128)(2,1)S(1)}, u32[]{:S(2)}, u32[]{:S(2)}) collective-permute-start(bf16[128,256]{1,0:T(8,128)(2,1)S(1)} %fusion), channel_id=1, source_target_pairs={{0,8},{4,12},{8,16},{12,20},{16,24},{20,28},{1,9},{5,13},{9,17},{1... | collective-permute-start | bytes 196616 | tf_op jit(solution)/shard_map/ppermute | solution.py:321
  12.5 0.8 constant_dynamic-slice_fusion
  13.2 1.1 %collective-permute-done.1 = bf16[128,256]{1,0:T(8,128)(2,1)S(1)} collective-permute-done((bf16[128,256]{1,0:T(8,128)(2,1)S(1)}, bf16[128,256]{1,0:T(8,128)(2,1)S(1)}, u32[]{:S(2)}, u32[]{:S(2)}) %collective-permute-start.1) | collective-permute-done | bytes 65568 | tf_op jit(solution)/shard_map/ppermute | solution.py:321
  14.4 5.3 %collective-permute-start.2 = (bf16[128,256]{1,0:T(8,128)(2,1)S(1)}, bf16[128,256]{1,0:T(8,128)(2,1)S(1)}, u32[]{:S(2)}, u32[]{:S(2)}) collective-permute-start(bf16[128,256]{1,0:T(8,128)(2,1)S(1)} %fusion.2), channel_id=1, source_target_pairs={{0,16},{4,20},{8,24},{12,28},{1,17},{5,21},{9,25},{13,29},{2,18},{... | collective-permute-start | bytes 196616 | tf_op jit(solution)/shard_map/ppermute | solution.py:321
  19.7 0.1 copy.16
  19.8 0.1 copy.15
  19.8 1.7 %collective-permute-done.2 = bf16[128,256]{1,0:T(8,128)(2,1)S(1)} collective-permute-done((bf16[128,256]{1,0:T(8,128)(2,1)S(1)}, bf16[128,256]{1,0:T(8,128)(2,1)S(1)}, u32[]{:S(2)}, u32[]{:S(2)}) %collective-permute-start.2) | collective-permute-done | bytes 65568 | tf_op jit(solution)/shard_map/ppermute | solution.py:321
  21.6 1.6 %collective-permute-start.3 = (bf16[128,256]{1,0:T(8,128)(2,1)S(1)}, bf16[128,256]{1,0:T(8,128)(2,1)S(1)}, u32[]{:S(2)}, u32[]{:S(2)}) collective-permute-start(bf16[128,256]{1,0:T(8,128)(2,1)S(1)} %get-tuple-element.45), channel_id=1, source_target_pairs={{0,4},{4,0},{8,12},{12,8},{16,20},{20,16},{24,28},{28,24},{1,5},{5... | collective-permute-start | bytes 196616 | tf_op jit(solution)/shard_map/ppermute | solution.py:331
  23.2 0.9 copy-done.3
  24.1 0.9 copy-done.5
  25.0 0.9 copy-done.7
  25.9 0.9 shard_map.101.within_ref
  26.8 0.9 copy-done.8
  27.7 0.7 copy-done.10
  28.4 0.9 shard_map.102
  29.3 0.1 collective-permute-start.4
  29.4 1.6 %collective-permute-start.5 = (bf16[32,512]{1,0:T(8,128)(2,1)S(1)}, bf16[32,512]{1,0:T(8,128)(2,1)S(1)}, u32[]{:S(2)}, u32[]{:S(2)}) collective-permute-start(bf16[32,512]{1,0:T(8,128)(2,1)S(1)} %get-tuple-element.30), channel_id=1, source_target_pairs={{0,2},{1,3},{2,0},{3,1},{4,6},{5,7},{6,4},{7,5},{8,10},{9,11},{10,... | collective-permute-start | bytes 98312 | tf_op jit(solution)/shard_map/ppermute | solution.py:302
  31.0 0.3 collective-permute-start.6
  31.3 0.1 fusion.6.pack_ref
  31.3 2.0 %collective-permute-done.5.refs_2_ = bf16[32,512]{1,0:T(8,128)(2,1)S(1)} collective-permute-done((bf16[32,512]{1,0:T(8,128)(2,1)S(1)}, bf16[32,512]{1,0:T(8,128)(2,1)S(1)}, u32[]{:S(2)}, u32[]{:S(2)}) %collective-permute-start.5) | collective-permute-done | bytes 32800 | tf_op jit(solution)/shard_map/ppermute | solution.py:302
  33.4 1.0 collective-permute-done.6.refs_3_
  34.3 0.7 copy-done.9
  35.0 0.7 shard_map.103.refs_0_
  35.7 0.6 collective-permute-start.10
  36.4 1.5 %collective-permute-start.7 = (bf16[32,2176]{1,0:T(8,128)(2,1)S(1)}, bf16[32,2176]{1,0:T(8,128)(2,1)S(1)}, u32[]{:S(2)}, u32[]{:S(2)}) collective-permute-start(bf16[32,2176]{1,0:T(8,128)(2,1)S(1)} %shard_map.103.refs_0_), channel_id=1, source_target_pairs={{0,8},{8,16},{16,24},{24,28},{28,20},{20,12},{12,4},{4,0},{1,9},{9... | collective-permute-start | bytes 417800 | tf_op jit(solution)/shard_map/ppermute | solution.py:212
  37.9 3.9 %collective-permute-done.10.refs_4_ = bf16[32,2176]{1,0:T(8,128)(2,1)S(1)} collective-permute-done((bf16[32,2176]{1,0:T(8,128)(2,1)S(1)}, bf16[32,2176]{1,0:T(8,128)(2,1)S(1)}, u32[]{:S(2)}, u32[]{:S(2)}) %collective-permute-start.10) | collective-permute-done | bytes 139296 | tf_op jit(solution)/shard_map/ppermute | solution.py:213
  41.8 0.3 collective-permute-start.11
  42.1 1.7 %collective-permute-start.8 = (bf16[32,2176]{1,0:T(8,128)(2,1)S(1)}, bf16[32,2176]{1,0:T(8,128)(2,1)S(1)}, u32[]{:S(2)}, u32[]{:S(2)}) collective-permute-start(bf16[32,2176]{1,0:T(8,128)(2,1)S(1)} %collective-permute-done.7.refs_1_), channel_id=1, source_target_pairs={{0,8},{8,16},{16,24},{24,28},{28,20},{20,12},{12,4},{4,0},{1,9},{9... | collective-permute-start | bytes 417800 | tf_op jit(solution)/shard_map/ppermute | solution.py:212
  43.8 3.2 %collective-permute-done.11.refs_5_ = bf16[32,2176]{1,0:T(8,128)(2,1)S(1)} collective-permute-done((bf16[32,2176]{1,0:T(8,128)(2,1)S(1)}, bf16[32,2176]{1,0:T(8,128)(2,1)S(1)}, u32[]{:S(2)}, u32[]{:S(2)}) %collective-permute-start.11) | collective-permute-done | bytes 139296 | tf_op jit(solution)/shard_map/ppermute | solution.py:213
  47.1 0.3 collective-permute-start.12
  47.3 1.9 %collective-permute-start.9 = (bf16[32,2176]{1,0:T(8,128)(2,1)S(1)}, bf16[32,2176]{1,0:T(8,128)(2,1)S(1)}, u32[]{:S(2)}, u32[]{:S(2)}) collective-permute-start(bf16[32,2176]{1,0:T(8,128)(2,1)S(1)} %collective-permute-done.8.refs_2_), channel_id=1, source_target_pairs={{0,8},{8,16},{16,24},{24,28},{28,20},{20,12},{12,4},{4,0},{1,9},{9... | collective-permute-start | bytes 417800 | tf_op jit(solution)/shard_map/ppermute | solution.py:212
  49.3 3.0 %collective-permute-done.12.refs_6_ = bf16[32,2176]{1,0:T(8,128)(2,1)S(1)} collective-permute-done((bf16[32,2176]{1,0:T(8,128)(2,1)S(1)}, bf16[32,2176]{1,0:T(8,128)(2,1)S(1)}, u32[]{:S(2)}, u32[]{:S(2)}) %collective-permute-start.12) | collective-permute-done | bytes 139296 | tf_op jit(solution)/shard_map/ppermute | solution.py:213
  52.3 0.1 collective-permute-start.14
  52.4 2.0 %collective-permute-start.13 = (bf16[16,2176]{1,0:T(8,128)(2,1)S(1)}, bf16[16,2176]{1,0:T(8,128)(2,1)S(1)}, u32[]{:S(2)}, u32[]{:S(2)}) collective-permute-start(bf16[16,2176]{1,0:T(8,128)(2,1)S(1)} %slice.24), channel_id=1, source_target_pairs={{0,8},{8,16},{16,24},{24,28},{28,20},{20,12},{12,4},{4,0},{1,9},{9... | collective-permute-start | bytes 208904 | tf_op jit(solution)/shard_map/ppermute | solution.py:214
  54.4 2.2 %collective-permute-done.14.refs_8_ = bf16[16,2176]{1,0:T(8,128)(2,1)S(1)} collective-permute-done((bf16[16,2176]{1,0:T(8,128)(2,1)S(1)}, bf16[16,2176]{1,0:T(8,128)(2,1)S(1)}, u32[]{:S(2)}, u32[]{:S(2)}) %collective-permute-start.14) | collective-permute-done | bytes 69664 | tf_op jit(solution)/shard_map/ppermute | solution.py:215
  56.6 0.4 collective-permute-done.13.refs_7_
  57.0 3.4 %copy-done.1 = bf16[1,2,2048,1024]{3,2,1,0:T(8,128)(2,1)S(1)} copy-done((bf16[1,2,2048,1024]{3,2,1,0:T(8,128)(2,1)S(1)}, bf16[1,2,2048,1024]{3,2,1,0:T(8,128)(2,1)}, u32[]{:S(2)}) %copy-start.1) | copy-done | bytes 8388632
  60.3 2.2 %copy-done.2 = bf16[1,1024,2048]{2,1,0:T(8,128)(2,1)S(1)} copy-done((bf16[1,1024,2048]{2,1,0:T(8,128)(2,1)S(1)}, bf16[1,1024,2048]{2,1,0:T(8,128)(2,1)}, u32[]{:S(2)}) %copy-start.2) | copy-done | bytes 4194328
  62.5 6.9 %shard_map.104 = (bf16[32,2048]{1,0:T(8,128)(2,1)S(1)}, bf16[32,2048]{1,0:T(8,128)(2,1)S(1)}, bf16[32,2048]{1,0:T(8,128)(2,1)S(1)}, bf16[32,2048]{1,0:T(8,128)(2...) custom-call(s32[4]{0:T(128)S(1)} %pad_add_fusion.scalars, ...), custom_call_target="tpu_custom_call" | custom-call | flops 3221225472 | bytes 14680064 | tf_op jit(solution)/shard_map/pallas_call | solution.py:172
  69.4 2.1 %collective-permute-start.19 = (bf16[16,2048]{1,0:T(8,128)(2,1)S(1)}, bf16[16,2048]{1,0:T(8,128)(2,1)S(1)}, u32[]{:S(2)}, u32[]{:S(2)}) collective-permute-start(bf16[16,2048]{1,0:T(8,128)(2,1)S(1)} %get-tuple-element.38), channel_id=1, source_target_pairs={{8,0},{16,8},{24,16},{28,24},{20,28},{12,20},{4,12},{0,4},{9,1},{1... | collective-permute-start | bytes 196616 | tf_op jit(solution)/shard_map/ppermute | solution.py:222
  71.6 2.6 %collective-permute-done.19 = bf16[16,2048]{1,0:T(8,128)(2,1)S(1)} collective-permute-done((bf16[16,2048]{1,0:T(8,128)(2,1)S(1)}, bf16[16,2048]{1,0:T(8,128)(2,1)S(1)}, u32[]{:S(2)}, u32[]{:S(2)}) %collective-permute-start.19) | collective-permute-done | bytes 65568 | tf_op jit(solution)/shard_map/ppermute | solution.py:222
  74.2 1.6 %collective-permute-start.20 = (bf16[32,2048]{1,0:T(8,128)(2,1)S(1)}, bf16[32,2048]{1,0:T(8,128)(2,1)S(1)}, u32[]{:S(2)}, u32[]{:S(2)}) collective-permute-start(bf16[32,2048]{1,0:T(8,128)(2,1)S(1)} %pad_maximum_fusion.1), channel_id=1, source_target_pairs={{8,0},{16,8},{24,16},{28,24},{20,28},{12,20},{4,12},{0,4},{9,1},{1... | collective-permute-start | bytes 393224 | tf_op jit(solution)/shard_map/ppermute | solution.py:233
  75.9 0.5 collective-permute-start.16
  76.4 3.1 %collective-permute-done.20 = bf16[32,2048]{1,0:T(8,128)(2,1)S(1)} collective-permute-done((bf16[32,2048]{1,0:T(8,128)(2,1)S(1)}, bf16[32,2048]{1,0:T(8,128)(2,1)S(1)}, u32[]{:S(2)}, u32[]{:S(2)}) %collective-permute-start.20) | collective-permute-done | bytes 131104 | tf_op jit(solution)/shard_map/ppermute | solution.py:233
  79.6 1.3 %collective-permute-start.21 = (bf16[32,2048]{1,0:T(8,128)(2,1)S(1)}, bf16[32,2048]{1,0:T(8,128)(2,1)S(1)}, u32[]{:S(2)}, u32[]{:S(2)}) collective-permute-start(bf16[32,2048]{1,0:T(8,128)(2,1)S(1)} %add_convert_fusion.1), channel_id=1, source_target_pairs={{8,0},{16,8},{24,16},{28,24},{20,28},{12,20},{4,12},{0,4},{9,1},{1... | collective-permute-start | bytes 393224 | tf_op jit(solution)/shard_map/ppermute | solution.py:233
  81.0 0.8 collective-permute-start.17
  81.8 2.8 %collective-permute-done.21 = bf16[32,2048]{1,0:T(8,128)(2,1)S(1)} collective-permute-done((bf16[32,2048]{1,0:T(8,128)(2,1)S(1)}, bf16[32,2048]{1,0:T(8,128)(2,1)S(1)}, u32[]{:S(2)}, u32[]{:S(2)}) %collective-permute-start.21) | collective-permute-done | bytes 131104 | tf_op jit(solution)/shard_map/ppermute | solution.py:233
  84.7 1.3 %collective-permute-start.22 = (bf16[32,2048]{1,0:T(8,128)(2,1)S(1)}, bf16[32,2048]{1,0:T(8,128)(2,1)S(1)}, u32[]{:S(2)}, u32[]{:S(2)}) collective-permute-start(bf16[32,2048]{1,0:T(8,128)(2,1)S(1)} %add_convert_fusion), channel_id=1, source_target_pairs={{8,0},{16,8},{24,16},{28,24},{20,28},{12,20},{4,12},{0,4},{9,1},{1... | collective-permute-start | bytes 393224 | tf_op jit(solution)/shard_map/ppermute | solution.py:233
  86.0 0.8 collective-permute-start.18
  86.8 2.8 %collective-permute-done.22.c_ref = bf16[32,2048]{1,0:T(8,128)(2,1)S(1)} collective-permute-done((bf16[32,2048]{1,0:T(8,128)(2,1)S(1)}, bf16[32,2048]{1,0:T(8,128)(2,1)S(1)}, u32[]{:S(2)}, u32[]{:S(2)}) %collective-permute-start.22) | collective-permute-done | bytes 131104 | tf_op jit(solution)/shard_map/ppermute | solution.py:233
  89.7 1.4 %collective-permute-done.18.b_ref = bf16[32,2048]{1,0:T(8,128)(2,1)S(1)} collective-permute-done((bf16[32,2048]{1,0:T(8,128)(2,1)S(1)}, bf16[32,2048]{1,0:T(8,128)(2,1)S(1)}, u32[]{:S(2)}, u32[]{:S(2)}) %collective-permute-start.18) | collective-permute-done | bytes 131104 | tf_op jit(solution)/shard_map/ppermute | solution.py:232
  91.0 0.6 shard_map.105
  91.7 0.9 collective-permute-start.24
  92.7 0.9 collective-permute-start.25
  93.6 2.2 %collective-permute-done.24.refs_2_ = bf16[32,512]{1,0:T(8,128)(2,1)S(1)} collective-permute-done((bf16[32,512]{1,0:T(8,128)(2,1)S(1)}, bf16[32,512]{1,0:T(8,128)(2,1)S(1)}, u32[]{:S(2)}, u32[]{:S(2)}) %collective-permute-start.24) | collective-permute-done | bytes 32800 | tf_op jit(solution)/shard_map/ppermute | solution.py:302
  95.8 0.4 collective-permute-done.25.refs_3_
  96.1 1.2 %shard_map.106 = bf16[128,512]{1,0:T(8,128)(2,1)} custom-call(s32[4]{0:T(128)S(1)} %pad_add_fusion.scalars, bf16[128,512]{1,0:T(8,128)(2,1)S(1)} %get-tuple-element.27.hidden_ref, bf16[32,512]{1,0:T(8,128)(2,1)S(1)} %get-tuple-element.41.refs_0_, bf16[32,512]{1,0:T(8,128)(2,1)S(1)} %collective-permute-done.23.refs_1_, ...), custom_call_target="tpu_custom_call" | custom-call | bytes 393232 | tf_op jit(solution)/shard_map/pallas_call | solution.py:20
  (41 shorter events, 0.5 us)
Async XLA Ops:
  0.0 6.2 %copy-start = (s32[128,8]{0,1:T(8,128)S(1)}, s32[128,8]{0,1:T(8,128)}, u32[]{:S(2)}) copy-start(s32[128,8]{0,1:T(8,128)} %param.16) | copy-start | bytes 12292
  0.1 0.9 copy-start.4
  1.0 0.9 copy-start.6
  3.2 5.3 %collective-permute-start = (bf16[128,256]{1,0:T(8,128)(2,1)S(1)}, bf16[128,256]{1,0:T(8,128)(2,1)S(1)}, u32[]{:S(2)}, u32[]{:S(2)}) collective-permute-start(bf16[128,256]{1,0:T(8,128)(2,1)S(1)} %get-tuple-element.26), channel_id=1, source_target_pairs={{0,4},{4,0},{8,12},{12,8},{16,20},{20,16},{24,28},{28,24},{1,5},{5... | collective-permute-start | bytes 196616 | tf_op jit(solution)/shard_map/ppermute | solution.py:316
  8.5 5.9 %collective-permute-start.1 = (bf16[128,256]{1,0:T(8,128)(2,1)S(1)}, bf16[128,256]{1,0:T(8,128)(2,1)S(1)}, u32[]{:S(2)}, u32[]{:S(2)}) collective-permute-start(bf16[128,256]{1,0:T(8,128)(2,1)S(1)} %fusion), channel_id=1, source_target_pairs={{0,8},{4,12},{8,16},{12,20},{16,24},{20,28},{1,9},{5,13},{9,17},{1... | collective-permute-start | bytes 196616 | tf_op jit(solution)/shard_map/ppermute | solution.py:321
  14.4 7.2 %collective-permute-start.2 = (bf16[128,256]{1,0:T(8,128)(2,1)S(1)}, bf16[128,256]{1,0:T(8,128)(2,1)S(1)}, u32[]{:S(2)}, u32[]{:S(2)}) collective-permute-start(bf16[128,256]{1,0:T(8,128)(2,1)S(1)} %fusion.2), channel_id=1, source_target_pairs={{0,16},{4,20},{8,24},{12,28},{1,17},{5,21},{9,25},{13,29},{2,18},{... | collective-permute-start | bytes 196616 | tf_op jit(solution)/shard_map/ppermute | solution.py:321
  21.6 5.2 %collective-permute-start.3 = (bf16[128,256]{1,0:T(8,128)(2,1)S(1)}, bf16[128,256]{1,0:T(8,128)(2,1)S(1)}, u32[]{:S(2)}, u32[]{:S(2)}) collective-permute-start(bf16[128,256]{1,0:T(8,128)(2,1)S(1)} %get-tuple-element.45), channel_id=1, source_target_pairs={{0,4},{4,0},{8,12},{12,8},{16,20},{20,16},{24,28},{28,24},{1,5},{5... | collective-permute-start | bytes 196616 | tf_op jit(solution)/shard_map/ppermute | solution.py:331
  23.2 0.9 copy-start.3
  24.1 0.9 copy-start.5
  25.0 0.9 copy-start.7
  26.8 0.9 copy-start.8
  27.7 0.7 copy-start.10
  29.3 2.0 %collective-permute-start.4 = (bf16[32,512]{1,0:T(8,128)(2,1)S(1)}, bf16[32,512]{1,0:T(8,128)(2,1)S(1)}, u32[]{:S(2)}, u32[]{:S(2)}) collective-permute-start(bf16[32,512]{1,0:T(8,128)(2,1)S(1)} %get-tuple-element.29), channel_id=1, source_target_pairs={{0,1},{1,0},{2,3},{3,2},{4,5},{5,4},{6,7},{7,6},{8,9},{9,8},{10,11... | collective-permute-start | bytes 98312 | tf_op jit(solution)/shard_map/ppermute | solution.py:302
  29.4 4.0 %collective-permute-start.5 = (bf16[32,512]{1,0:T(8,128)(2,1)S(1)}, bf16[32,512]{1,0:T(8,128)(2,1)S(1)}, u32[]{:S(2)}, u32[]{:S(2)}) collective-permute-start(bf16[32,512]{1,0:T(8,128)(2,1)S(1)} %get-tuple-element.30), channel_id=1, source_target_pairs={{0,2},{1,3},{2,0},{3,1},{4,6},{5,7},{6,4},{7,5},{8,10},{9,11},{10,... | collective-permute-start | bytes 98312 | tf_op jit(solution)/shard_map/ppermute | solution.py:302
  31.0 3.3 %collective-permute-start.6 = (bf16[32,512]{1,0:T(8,128)(2,1)S(1)}, bf16[32,512]{1,0:T(8,128)(2,1)S(1)}, u32[]{:S(2)}, u32[]{:S(2)}) collective-permute-start(bf16[32,512]{1,0:T(8,128)(2,1)S(1)} %get-tuple-element.31), channel_id=1, source_target_pairs={{0,3},{1,2},{2,1},{3,0},{4,7},{5,6},{6,5},{7,4},{8,11},{9,10},{10,... | collective-permute-start | bytes 98312 | tf_op jit(solution)/shard_map/ppermute | solution.py:302
  34.3 0.7 copy-start.9
  35.7 6.1 %collective-permute-start.10 = (bf16[32,2176]{1,0:T(8,128)(2,1)S(1)}, bf16[32,2176]{1,0:T(8,128)(2,1)S(1)}, u32[]{:S(2)}, u32[]{:S(2)}) collective-permute-start(bf16[32,2176]{1,0:T(8,128)(2,1)S(1)} %shard_map.103.refs_0_), channel_id=1, source_target_pairs={{8,0},{16,8},{24,16},{28,24},{20,28},{12,20},{4,12},{0,4},{9,1},{1... | collective-permute-start | bytes 417800 | tf_op jit(solution)/shard_map/ppermute | solution.py:213
  36.4 5.8 %collective-permute-start.7 = (bf16[32,2176]{1,0:T(8,128)(2,1)S(1)}, bf16[32,2176]{1,0:T(8,128)(2,1)S(1)}, u32[]{:S(2)}, u32[]{:S(2)}) collective-permute-start(bf16[32,2176]{1,0:T(8,128)(2,1)S(1)} %shard_map.103.refs_0_), channel_id=1, source_target_pairs={{0,8},{8,16},{16,24},{24,28},{28,20},{20,12},{12,4},{4,0},{1,9},{9... | collective-permute-start | bytes 417800 | tf_op jit(solution)/shard_map/ppermute | solution.py:212
  41.8 5.2 %collective-permute-start.11 = (bf16[32,2176]{1,0:T(8,128)(2,1)S(1)}, bf16[32,2176]{1,0:T(8,128)(2,1)S(1)}, u32[]{:S(2)}, u32[]{:S(2)}) collective-permute-start(bf16[32,2176]{1,0:T(8,128)(2,1)S(1)} %collective-permute-done.10.refs_4_), channel_id=1, source_target_pairs={{8,0},{16,8},{24,16},{28,24},{20,28},{12,20},{4,12},{0,4},{9,1},{1... | collective-permute-start | bytes 417800 | tf_op jit(solution)/shard_map/ppermute | solution.py:213
  42.1 5.2 %collective-permute-start.8 = (bf16[32,2176]{1,0:T(8,128)(2,1)S(1)}, bf16[32,2176]{1,0:T(8,128)(2,1)S(1)}, u32[]{:S(2)}, u32[]{:S(2)}) collective-permute-start(bf16[32,2176]{1,0:T(8,128)(2,1)S(1)} %collective-permute-done.7.refs_1_), channel_id=1, source_target_pairs={{0,8},{8,16},{16,24},{24,28},{28,20},{20,12},{12,4},{4,0},{1,9},{9... | collective-permute-start | bytes 417800 | tf_op jit(solution)/shard_map/ppermute | solution.py:212
  47.1 5.2 %collective-permute-start.12 = (bf16[32,2176]{1,0:T(8,128)(2,1)S(1)}, bf16[32,2176]{1,0:T(8,128)(2,1)S(1)}, u32[]{:S(2)}, u32[]{:S(2)}) collective-permute-start(bf16[32,2176]{1,0:T(8,128)(2,1)S(1)} %collective-permute-done.11.refs_5_), channel_id=1, source_target_pairs={{8,0},{16,8},{24,16},{28,24},{20,28},{12,20},{4,12},{0,4},{9,1},{1... | collective-permute-start | bytes 417800 | tf_op jit(solution)/shard_map/ppermute | solution.py:213
  47.3 5.1 %collective-permute-start.9 = (bf16[32,2176]{1,0:T(8,128)(2,1)S(1)}, bf16[32,2176]{1,0:T(8,128)(2,1)S(1)}, u32[]{:S(2)}, u32[]{:S(2)}) collective-permute-start(bf16[32,2176]{1,0:T(8,128)(2,1)S(1)} %collective-permute-done.8.refs_2_), channel_id=1, source_target_pairs={{0,8},{8,16},{16,24},{24,28},{28,20},{20,12},{12,4},{4,0},{1,9},{9... | collective-permute-start | bytes 417800 | tf_op jit(solution)/shard_map/ppermute | solution.py:212
  52.3 4.3 %collective-permute-start.14 = (bf16[16,2176]{1,0:T(8,128)(2,1)S(1)}, bf16[16,2176]{1,0:T(8,128)(2,1)S(1)}, u32[]{:S(2)}, u32[]{:S(2)}) collective-permute-start(bf16[16,2176]{1,0:T(8,128)(2,1)S(1)} %slice.25), channel_id=1, source_target_pairs={{8,0},{16,8},{24,16},{28,24},{20,28},{12,20},{4,12},{0,4},{9,1},{1... | collective-permute-start | bytes 208904 | tf_op jit(solution)/shard_map/ppermute | solution.py:215
  52.4 4.5 %collective-permute-start.13 = (bf16[16,2176]{1,0:T(8,128)(2,1)S(1)}, bf16[16,2176]{1,0:T(8,128)(2,1)S(1)}, u32[]{:S(2)}, u32[]{:S(2)}) collective-permute-start(bf16[16,2176]{1,0:T(8,128)(2,1)S(1)} %slice.24), channel_id=1, source_target_pairs={{0,8},{8,16},{16,24},{24,28},{28,20},{20,12},{12,4},{4,0},{1,9},{9... | collective-permute-start | bytes 208904 | tf_op jit(solution)/shard_map/ppermute | solution.py:214
  57.0 3.4 %copy-start.1 = (bf16[1,2,2048,1024]{3,2,1,0:T(8,128)(2,1)S(1)}, bf16[1,2,2048,1024]{3,2,1,0:T(8,128)(2,1)}, u32[]{:S(2)}) copy-start(bf16[1,2,2048,1024]{3,2,1,0:T(8,128)(2,1)} %refs_10_.1) | copy-start | bytes 25165828
  60.3 2.2 %copy-start.2 = (bf16[1,1024,2048]{2,1,0:T(8,128)(2,1)S(1)}, bf16[1,1024,2048]{2,1,0:T(8,128)(2,1)}, u32[]{:S(2)}) copy-start(bf16[1,1024,2048]{2,1,0:T(8,128)(2,1)} %refs_11_.1) | copy-start | bytes 12582916
  69.4 4.8 %collective-permute-start.19 = (bf16[16,2048]{1,0:T(8,128)(2,1)S(1)}, bf16[16,2048]{1,0:T(8,128)(2,1)S(1)}, u32[]{:S(2)}, u32[]{:S(2)}) collective-permute-start(bf16[16,2048]{1,0:T(8,128)(2,1)S(1)} %get-tuple-element.38), channel_id=1, source_target_pairs={{8,0},{16,8},{24,16},{28,24},{20,28},{12,20},{4,12},{0,4},{9,1},{1... | collective-permute-start | bytes 196616 | tf_op jit(solution)/shard_map/ppermute | solution.py:222
  71.5 4.3 %collective-permute-start.15 = (bf16[16,2048]{1,0:T(8,128)(2,1)S(1)}, bf16[16,2048]{1,0:T(8,128)(2,1)S(1)}, u32[]{:S(2)}, u32[]{:S(2)}) collective-permute-start(bf16[16,2048]{1,0:T(8,128)(2,1)S(1)} %get-tuple-element.33), channel_id=1, source_target_pairs={{0,8},{8,16},{16,24},{24,28},{28,20},{20,12},{12,4},{4,0},{1,9},{9... | collective-permute-start | bytes 196616 | tf_op jit(solution)/shard_map/ppermute | solution.py:221
  74.2 5.3 %collective-permute-start.20 = (bf16[32,2048]{1,0:T(8,128)(2,1)S(1)}, bf16[32,2048]{1,0:T(8,128)(2,1)S(1)}, u32[]{:S(2)}, u32[]{:S(2)}) collective-permute-start(bf16[32,2048]{1,0:T(8,128)(2,1)S(1)} %pad_maximum_fusion.1), channel_id=1, source_target_pairs={{8,0},{16,8},{24,16},{28,24},{20,28},{12,20},{4,12},{0,4},{9,1},{1... | collective-permute-start | bytes 393224 | tf_op jit(solution)/shard_map/ppermute | solution.py:233
  75.9 5.0 %collective-permute-start.16 = (bf16[32,2048]{1,0:T(8,128)(2,1)S(1)}, bf16[32,2048]{1,0:T(8,128)(2,1)S(1)}, u32[]{:S(2)}, u32[]{:S(2)}) collective-permute-start(bf16[32,2048]{1,0:T(8,128)(2,1)S(1)} %pad_maximum_fusion), channel_id=1, source_target_pairs={{0,8},{8,16},{16,24},{24,28},{28,20},{20,12},{12,4},{4,0},{1,9},{9... | collective-permute-start | bytes 393224 | tf_op jit(solution)/shard_map/ppermute | solution.py:232
  79.6 5.0 %collective-permute-start.21 = (bf16[32,2048]{1,0:T(8,128)(2,1)S(1)}, bf16[32,2048]{1,0:T(8,128)(2,1)S(1)}, u32[]{:S(2)}, u32[]{:S(2)}) collective-permute-start(bf16[32,2048]{1,0:T(8,128)(2,1)S(1)} %add_convert_fusion.1), channel_id=1, source_target_pairs={{8,0},{16,8},{24,16},{28,24},{20,28},{12,20},{4,12},{0,4},{9,1},{1... | collective-permute-start | bytes 393224 | tf_op jit(solution)/shard_map/ppermute | solution.py:233
  81.0 5.0 %collective-permute-start.17 = (bf16[32,2048]{1,0:T(8,128)(2,1)S(1)}, bf16[32,2048]{1,0:T(8,128)(2,1)S(1)}, u32[]{:S(2)}, u32[]{:S(2)}) collective-permute-start(bf16[32,2048]{1,0:T(8,128)(2,1)S(1)} %add_convert_fusion.3), channel_id=1, source_target_pairs={{0,8},{8,16},{16,24},{24,28},{28,20},{20,12},{12,4},{4,0},{1,9},{9... | collective-permute-start | bytes 393224 | tf_op jit(solution)/shard_map/ppermute | solution.py:232
  84.7 5.0 %collective-permute-start.22 = (bf16[32,2048]{1,0:T(8,128)(2,1)S(1)}, bf16[32,2048]{1,0:T(8,128)(2,1)S(1)}, u32[]{:S(2)}, u32[]{:S(2)}) collective-permute-start(bf16[32,2048]{1,0:T(8,128)(2,1)S(1)} %add_convert_fusion), channel_id=1, source_target_pairs={{8,0},{16,8},{24,16},{28,24},{20,28},{12,20},{4,12},{0,4},{9,1},{1... | collective-permute-start | bytes 393224 | tf_op jit(solution)/shard_map/ppermute | solution.py:233
  86.0 5.0 %collective-permute-start.18 = (bf16[32,2048]{1,0:T(8,128)(2,1)S(1)}, bf16[32,2048]{1,0:T(8,128)(2,1)S(1)}, u32[]{:S(2)}, u32[]{:S(2)}) collective-permute-start(bf16[32,2048]{1,0:T(8,128)(2,1)S(1)} %add_convert_fusion.2), channel_id=1, source_target_pairs={{0,8},{8,16},{16,24},{24,28},{28,20},{20,12},{12,4},{4,0},{1,9},{9... | collective-permute-start | bytes 393224 | tf_op jit(solution)/shard_map/ppermute | solution.py:232
  91.7 1.9 %collective-permute-start.23 = (bf16[32,512]{1,0:T(8,128)(2,1)S(1)}, bf16[32,512]{1,0:T(8,128)(2,1)S(1)}, u32[]{:S(2)}, u32[]{:S(2)}) collective-permute-start(bf16[32,512]{1,0:T(8,128)(2,1)S(1)} %get-tuple-element.42), channel_id=1, source_target_pairs={{0,1},{1,0},{2,3},{3,2},{4,5},{5,4},{6,7},{7,6},{8,9},{9,8},{10,11... | collective-permute-start | bytes 98312 | tf_op jit(solution)/shard_map/ppermute | solution.py:302
  91.7 4.0 %collective-permute-start.24 = (bf16[32,512]{1,0:T(8,128)(2,1)S(1)}, bf16[32,512]{1,0:T(8,128)(2,1)S(1)}, u32[]{:S(2)}, u32[]{:S(2)}) collective-permute-start(bf16[32,512]{1,0:T(8,128)(2,1)S(1)} %get-tuple-element.43), channel_id=1, source_target_pairs={{0,2},{1,3},{2,0},{3,1},{4,6},{5,7},{6,4},{7,5},{8,10},{9,11},{10,... | collective-permute-start | bytes 98312 | tf_op jit(solution)/shard_map/ppermute | solution.py:302
  92.7 3.5 %collective-permute-start.25 = (bf16[32,512]{1,0:T(8,128)(2,1)S(1)}, bf16[32,512]{1,0:T(8,128)(2,1)S(1)}, u32[]{:S(2)}, u32[]{:S(2)}) collective-permute-start(bf16[32,512]{1,0:T(8,128)(2,1)S(1)} %get-tuple-element.44), channel_id=1, source_target_pairs={{0,3},{1,2},{2,1},{3,0},{4,7},{5,6},{6,5},{7,4},{8,11},{9,10},{10,... | collective-permute-start | bytes 98312 | tf_op jit(solution)/shard_map/ppermute | solution.py:302

commit v2 on v0

v2 whole, which is shorter than its diff:
```python
import functools

import jax
import jax.numpy as jnp
from jax import lax
from jax.experimental import pallas as pl
from jax.experimental.pallas import tpu as pltpu
from jax.sharding import PartitionSpec as P

HEAD = 128
F32 = jnp.float32
BF16 = jnp.bfloat16
WHOLE = pl.BlockSpec(memory_space=pltpu.VMEM)
FAR = pl.BlockSpec(memory_space=pltpu.HBM)
SCALAR = pl.BlockSpec(memory_space=pltpu.SMEM)


def call(kernel, outs, inputs, far=(), scratch=(), out_specs=None, flops=0, limit=16 << 20):
    moved = sum(a.size * a.dtype.itemsize for a in [*inputs, *outs])
    return pl.pallas_call(
        kernel,
        out_shape=outs,
        in_specs=[
            SCALAR if i == 0 else FAR if i in far else WHOLE for i in range(len(inputs))
        ],
        out_specs=out_specs or [WHOLE] * len(outs),
        scratch_shapes=scratch,
        compiler_params=pltpu.CompilerParams(vmem_limit_bytes=limit),
        cost_estimate=pl.CostEstimate(flops=flops, bytes_accessed=moved, transcendentals=0),
    )(*inputs)


def shape(dims, dtype):
    return jax.ShapeDtypeStruct(dims, dtype)


def split(value):
    high = value.astype(BF16)
    return high, (value - high.astype(F32)).astype(BF16)


def add_rows(*terms):
    return sum(t.astype(F32) for t in terms).astype(BF16)


def run_copies(pairs, sems):
    copies = [pltpu.make_async_copy(a, b, sems.at[i]) for i, (a, b) in enumerate(pairs)]
    for copy in copies:
        copy.start()
    for copy in copies:
        copy.wait()


def state_kernel(scalars, key_ref, value_ref, kept_ref, given_ref, keys, values, sems):
    run_copies([(key_ref, keys), (value_ref, values)], sems)
    width = keys.shape[1] // 2
    place = scalars[1]
    for h in range(keys.shape[1] // HEAD):
        cols = slice(h * HEAD, (h + 1) * HEAD)
        state = lax.dot_general(
            keys[:, cols], values[:, cols], (((0,), (0,)), ((), ())), preferred_element_type=F32
        ).astype(BF16)
        half, inner = divmod(h * HEAD, width)

        @pl.when(place == half)
        def _():
            kept_ref[:, inner:inner + HEAD] = state

        @pl.when(place != half)
        def _():
            given_ref[:, inner:inner + HEAD] = state


def pack_kernel(scalars, *refs):
    sources, out_ref, sems = refs[:-2], refs[-2], refs[-1]
    width = out_ref.shape[1] // len(sources)
    theirs = pl.ds(pl.multiple_of((1 - scalars[1]) * width, width), width)
    run_copies(
        [
            (ref.at[:, theirs], out_ref.at[:, i * width:(i + 1) * width])
            for i, ref in enumerate(sources)
        ],
        sems,
    )


def within_kernel(
    scalars, key_ref, value_ref, query_ref, residual_ref, gain_ref, norm_ref, came_ref,
    out_ref, my_query, my_residual, my_gain, my_norm, keys, values, sems
):
    rows, width = my_query.shape
    mine = pl.ds(pl.multiple_of(scalars[1] * width, width), width)
    run_copies(
        [
            (key_ref.at[:, mine], keys),
            (value_ref.at[:, mine], values),
            (query_ref.at[:, mine], my_query),
            (residual_ref.at[:, mine], my_residual),
            (gain_ref.at[:, mine], my_gain),
            (norm_ref, my_norm),
        ],
        sems,
    )
    causal = lax.broadcasted_iota(jnp.int32, (rows, rows), 0) >= lax.broadcasted_iota(
        jnp.int32, (rows, rows), 1
    )
    for block in range(2):
        for inner in range(0, width, HEAD):
            cols = slice(inner, inner + HEAD)
            if block == 0:
                query, key, value = my_query[:, cols], keys[:, cols], values[:, cols]
            else:
                key, value, query = (
                    came_ref[:, i * width + inner:i * width + inner + HEAD] for i in range(3)
                )
            scores = lax.dot_general(
                query, key, (((1,), (1,)), ((), ())), preferred_element_type=F32
            )
            high, low = split(jnp.where(causal, scores, 0.0))
            out_ref[block, :, cols] = jnp.dot(
                high, value, preferred_element_type=F32
            ) + jnp.dot(low, value, preferred_element_type=F32)


def attend_kernel(
    parts, earlier, scalars, within_ref, my_query, my_residual, my_gain, came_ref, kept_ref,
    partner_ref, *refs
):
    before_refs, piece_refs, hidden = refs[:earlier], refs[earlier:-1], refs[-1]
    rows, width = my_query.shape
    before = sum(ref[...].astype(F32) for ref in before_refs)
    first = scalars[1] == 0
    for block in range(2):
        extra = (partner_ref if block == 0 else kept_ref)[...].astype(F32)
        use = jnp.logical_not(first) if block == 0 else first
        state = before + jnp.where(use, extra, 0.0)
        for inner in range(0, width, HEAD):
            cols = slice(inner, inner + HEAD)
            if block == 0:
                query, residual = my_query[:, cols], my_residual[:, cols]
            else:
                query, residual = (
                    came_ref[:, i * width + inner:i * width + inner + HEAD] for i in (2, 3)
                )
            high, low = split(state[:, cols])
            raw = (
                jnp.dot(query, high, preferred_element_type=F32)
                + jnp.dot(query, low, preferred_element_type=F32)
                + within_ref[block, :, cols]
            )
            scaled = raw * lax.rsqrt(jnp.mean(raw * raw, axis=-1, keepdims=True) + 1e-06)
            hidden[block, :, cols] = (
                residual.astype(F32) + scaled * my_gain[:, cols]
            ).astype(BF16)
    count = rows // parts
    for j, piece in enumerate(piece_refs):
        block, other = divmod(j, parts)
        start = pl.multiple_of((scalars[0] ^ other) * count, count)
        piece[...] = hidden[block, pl.ds(start, count), :]


def norm_kernel(parts, scalars, gain_ref, pack_ref, *refs):
    pieces, hidden_ref, out_ref = refs[:-2], refs[-2], refs[-1]
    width = pieces[0].shape[1]
    model = hidden_ref.shape[1]
    total = 0.0
    for ref in pieces:
        value = ref[...].astype(F32)
        total += jnp.sum(value * value, axis=-1, keepdims=True)
    scale = lax.rsqrt(total / model + 1e-06)
    for j, ref in enumerate(pieces):
        block, other = divmod(j, parts)
        slot = (scalars[0] ^ other) * 2 + (scalars[1] ^ block)
        cols = pl.ds(pl.multiple_of(slot * width, width), width)
        hidden_ref[:, cols] = ref[...]
        out_ref[:, cols] = (ref[...].astype(F32) * scale * gain_ref[:, cols]).astype(BF16)
    out_ref[:, model:] = pack_ref[...]


def load_kernel(scalars, in_ref, out_ref, in_kept, out_kept, sems):
    pairs = []
    for source, target in ((in_ref, in_kept), (out_ref, out_kept)):
        pieces = 4
        step = source.shape[-2] // pieces
        for lead in range(source.shape[0]):
            for i in range(pieces):
                cut = pl.ds(i * step, step)
                pairs.append((source.at[lead, cut], target.at[lead, cut]))
    run_copies(pairs, sems)


def load_weights(scalars, expert_in, expert_out):
    return call(
        load_kernel,
        [shape(expert_in.shape, BF16), shape(expert_out.shape, BF16)],
        [scalars, expert_in, expert_out],
        far=(1, 2),
        scratch=[pltpu.SemaphoreType.DMA((4 * (expert_in.shape[0] + expert_out.shape[0]),))],
    )


def expert_kernel(blocks, scalars, in_ref, down_ref, *refs):
    x_refs = refs[:blocks]
    out_refs = refs[blocks:2 * blocks]
    rows_ref, acc_ref = refs[2 * blocks:]
    width = acc_ref.shape[1]
    units = in_ref.shape[2]
    chunk = min(units, 256)
    spans = []
    first = 0
    for ref in x_refs:
        span = slice(first, first + ref.shape[0])
        rows_ref[span, :] = ref[:, :width]
        spans.append(span)
        first += ref.shape[0]
    acc_ref[...] = jnp.zeros_like(acc_ref)

    @pl.loop(0, units // chunk)
    def _(step):
        cut = pl.ds(pl.multiple_of(step * chunk, chunk), chunk)
        gate = jnp.dot(rows_ref[...], in_ref[0, :, cut], preferred_element_type=F32)
        up = jnp.dot(rows_ref[...], in_ref[1, :, cut], preferred_element_type=F32)
        activated = (gate / (1.0 + jnp.exp(-gate)) * up).astype(BF16)
        acc_ref[...] += jnp.dot(activated, down_ref[0, cut, :], preferred_element_type=F32)

    experts = scalars[2]
    for x_ref, out_ref, span in zip(x_refs, out_refs, spans):
        pack = x_ref[:, width:].astype(F32)
        lane = lax.broadcasted_iota(jnp.int32, pack.shape, 1)
        chosen = (lane == scalars[3]) | (lane == scalars[3] + experts)
        weight = jnp.sum(jnp.where(chosen, pack, 0.0), axis=-1, keepdims=True)
        produced = acc_ref[span, :].astype(BF16).astype(F32)
        out_ref[...] = (produced * weight).astype(BF16)


def run_expert(scalars, blocks, weights_in, weights_out):
    width, units = weights_in.shape[1:]
    total = sum(b.shape[0] for b in blocks)
    return call(
        functools.partial(expert_kernel, len(blocks)),
        [shape((b.shape[0], width), BF16) for b in blocks],
        [scalars, weights_in, weights_out, *blocks],
        scratch=[pltpu.VMEM((total, width), BF16), pltpu.VMEM((total, width), F32)],
        flops=6 * total * width * units,
        limit=24 << 20,
    )


def ring_order(count):
    return list(range(0, count, 2)) + list(range(1, count, 2))[::-1]


def dense_experts(block, scalars, expert_in, expert_out):
    count = lax.axis_size("seq")
    order = ring_order(count)
    half = block.shape[0] // 2
    far = count // 2

    def hop(rows, steps):
        return lax.ppermute(
            rows, "seq", [(order[p], order[(p + steps) % count]) for p in range(count)]
        )

    ahead, behind = [block], [block]
    for distance in range(1, far):
        ahead.append(hop(ahead[-1], 1))
        behind.append(hop(behind[-1], -1))
    top = hop(ahead[-2][:half], 2)
    bottom = hop(behind[-2][half:], -2)
    weights = load_weights(scalars, expert_in[0], expert_out)
    blocks = [block] + ahead[1:] + behind[1:] + [top, bottom]
    made = run_expert(scalars, blocks, *weights)
    own, from_ahead, from_behind = made[0], made[1:far], made[far:2 * far - 1]
    top, bottom = made[-2:]
    early_going, early_coming = hop(bottom, 2), hop(top, -2)
    going, coming = hop(from_behind[-1], 1), hop(from_ahead[-1], -1)
    for distance in range(far - 2, 0, -1):
        to_front, to_back = from_behind[distance - 1], from_ahead[distance - 1]
        if distance == far - 2:
            going = jnp.concatenate(
                [
                    add_rows(going[:half], to_front[:half]),
                    add_rows(going[half:], to_front[half:], early_going),
                ]
            )
            coming = jnp.concatenate(
                [
                    add_rows(coming[:half], to_back[:half], early_coming),
                    add_rows(coming[half:], to_back[half:]),
                ]
            )
        else:
            going = add_rows(going, to_front)
            coming = add_rows(coming, to_back)
        going, coming = hop(going, 1), hop(coming, -1)
    return own, going, coming


def mix_kernel(scalars, hidden_ref, a_ref, b_ref, c_ref, *out_refs):
    width = out_refs[0].shape[1]
    for j, out_ref in enumerate(out_refs):
        cols = pl.ds(pl.multiple_of((scalars[0] ^ j) * width, width), width)
        mixed = a_ref[:, cols].astype(F32) + b_ref[:, cols].astype(F32)
        mixed += c_ref[:, cols].astype(F32)
        out_ref[...] = (hidden_ref[:, cols].astype(F32) + mixed).astype(BF16)


def join_kernel(scalars, *refs):
    pieces, out_ref, sems = refs[:-2], refs[-2], refs[-1]
    count = pieces[0].shape[0]
    pairs = []
    for j, piece in enumerate(pieces):
        rows = pl.ds(pl.multiple_of((scalars[0] ^ j) * count, count), count)
        pairs.append((piece, out_ref.at[rows, :]))
    run_copies(pairs, sems)


def slot_ids(block_routes, expert_count, capacity):
    row_count, top_count = block_routes.shape
    expert_ids = jnp.arange(expert_count, dtype=jnp.int32)
    onehot = (
        (block_routes[:, :, None] == expert_ids[None, None, :])
        .astype(jnp.int32)
        .reshape(row_count * top_count, expert_count)
    )
    earlier = jnp.cumsum(onehot, axis=0) - onehot
    ranking = jnp.sum(earlier * onehot, axis=1).reshape(row_count, top_count)
    return block_routes * capacity + ranking


def routed_experts(normed, my_routes, my_gates, expert_in, expert_out):
    sub_count, model_width = normed.shape
    expert_count = lax.axis_size("seq") * expert_in.shape[0]
    top_count = my_routes.shape[1]
    capacity = min(sub_count, max(2, 3 * sub_count * top_count // (2 * expert_count)))
    slot_count = expert_count * capacity
    my_slots = slot_ids(my_routes, expert_count, capacity)
    columns = jnp.arange(slot_count, dtype=jnp.int32)
    placer = jnp.sum(
        (my_slots[None, :, :] == columns[:, None, None]).astype(jnp.int32), axis=2
    ).astype(BF16)
    outgoing = (
        jnp.dot(placer, normed, preferred_element_type=F32)
        .astype(BF16)
        .reshape(expert_count, capacity, model_width)
    )
    arrived = lax.all_to_all(outgoing, "seq", split_axis=0, concat_axis=0, tiled=True)
    flat_rows = arrived.reshape(-1, model_width)
    gate_up = jnp.einsum("nd,gdf->gnf", flat_rows, expert_in[0], preferred_element_type=F32)
    activated = (jax.nn.silu(gate_up[0]) * gate_up[1]).astype(BF16)
    produced = jnp.dot(activated, expert_out[0], preferred_element_type=F32).astype(BF16)
    answered = produced.reshape(arrived.shape)
    returned = lax.all_to_all(answered, "seq", split_axis=0, concat_axis=0, tiled=True)
    picked = returned.reshape(slot_count, model_width)[my_slots.reshape(-1)].reshape(
        sub_count, top_count, model_width
    )
    return jnp.sum(picked.astype(F32) * my_gates[:, :, None], axis=1)


def prior_states(kept, partner):
    count = lax.axis_size("seq")

    def pass_on(state, distance):
        return lax.ppermute(
            state, "seq", [(i, i + 2 * distance) for i in range(count - 2 * distance)]
        )

    pairs = count // 2
    running = add_rows(kept, partner)
    if pairs <= 4:
        return [pass_on(running, distance) for distance in range(1, pairs)]
    terms = []
    distance = 1
    while distance < pairs:
        terms.append(pass_on(running, distance))
        running = add_rows(running, terms[-1])
        distance *= 2
    return terms


def per_device(
    residual,
    queries,
    key_vectors,
    value_vectors,
    head_gain,
    norm_gain,
    routes,
    route_gates,
    expert_in,
    expert_out,
):
    rows, width = residual.shape
    seq, parts = lax.axis_size("seq"), lax.axis_size("exp")
    count, half, model = rows // parts, width // 2, width * parts
    experts = seq * expert_in.shape[0]
    position = lax.axis_index("seq")
    my_index = lax.axis_index("exp")
    scalars = jnp.stack([my_index, position % 2, experts, position]).astype(jnp.int32)
    swap = [(i, i ^ 1) for i in range(seq)]

    state = shape((HEAD, half), BF16)
    kept, given = call(
        state_kernel, [state, state], [scalars, key_vectors, value_vectors], far=(1, 2),
        scratch=[pltpu.VMEM((rows, width), BF16)] * 2 + [pltpu.SemaphoreType.DMA((2,))],
        flops=2 * rows * width * HEAD,
    )
    partner = lax.ppermute(given, "seq", swap)
    [packed] = call(
        pack_kernel, [shape((rows, 4 * half), BF16)],
        [scalars, key_vectors, value_vectors, queries, residual], far=(1, 2, 3, 4),
        scratch=[pltpu.SemaphoreType.DMA((4,))],
    )
    came = lax.ppermute(packed, "seq", swap)
    before = prior_states(kept, partner)
    within, my_query, my_residual, my_gain, my_norm = call(
        within_kernel,
        [
            shape((2, rows, half), F32),
            shape((rows, half), BF16),
            shape((rows, half), BF16),
            shape((1, half), F32),
            shape((1, model), F32),
        ],
        [
            scalars, key_vectors, value_vectors, queries, residual, head_gain[None, :],
            norm_gain[None, :], came,
        ],
        far=(1, 2, 3, 4, 5, 6),
        scratch=[pltpu.VMEM((rows, half), BF16)] * 2 + [pltpu.SemaphoreType.DMA((6,))],
        flops=6 * rows * rows * width,
    )
    pieces = call(
        functools.partial(attend_kernel, parts, len(before)),
        [shape((count, half), BF16)] * (2 * parts),
        [scalars, within, my_query, my_residual, my_gain, came, kept, partner, *before],
        scratch=[pltpu.VMEM((2, rows, half), BF16)],
        flops=4 * rows * width * HEAD,
    )
    gathered = [pieces[0]]
    for j in range(1, 2 * parts):
        block, other = divmod(j, parts)
        gathered.append(
            lax.ppermute(
                pieces[j],
                ("seq", "exp"),
                [
                    (s * parts + e, (s ^ block) * parts + (e ^ other))
                    for s in range(seq)
                    for e in range(parts)
                ],
            )
        )

    my_routes = lax.dynamic_slice_in_dim(routes, my_index * count, count, 0)
    my_gates = lax.dynamic_slice_in_dim(route_gates, my_index * count, count, 0)
    weights = jnp.sum(
        jnp.where(
            my_routes[:, :, None] == jnp.arange(experts, dtype=jnp.int32),
            my_gates[:, :, None],
            0.0,
        ),
        axis=1,
    )
    high = lax.reduce_precision(weights, 8, 7)
    lanes = -(-2 * experts // HEAD) * HEAD
    pack = jnp.pad(
        jnp.concatenate([high, weights - high], axis=1), ((0, 0), (0, lanes - 2 * experts))
    ).astype(BF16)
    hidden, block = call(
        functools.partial(norm_kernel, parts),
        [shape((count, model), BF16), shape((count, model + lanes), BF16)],
        [scalars, my_norm, pack] + gathered,
    )
    if routes.shape[1] == experts:
        terms = dense_experts(block, scalars, expert_in, expert_out)
    else:
        mixed = routed_experts(block[:, :model], my_routes, my_gates, expert_in, expert_out)
        nothing = jnp.zeros_like(mixed)
        terms = (mixed, nothing, nothing)
    ready = call(
        mix_kernel, [shape((count, width), BF16)] * parts, [scalars, hidden, *terms]
    )
    returned = [ready[0]] + [
        lax.ppermute(ready[j], "exp", [(i, i ^ j) for i in range(parts)])
        for j in range(1, parts)
    ]
    [out] = call(
        join_kernel, [shape((rows, width), BF16)], [scalars] + returned, out_specs=[FAR],
        scratch=[pltpu.SemaphoreType.DMA((parts,))],
    )
    return out


def solution(mesh):
    placed = (
        P("seq", "exp"),
        P("seq", "exp"),
        P("seq", "exp"),
        P("seq", "exp"),
        P("exp"),
        P(),
        P("seq", None),
        P("seq", None),
        P("seq", None, None, None),
        P("seq", None, None),
    )
    return jax.shard_map(
        per_device, mesh=mesh, in_specs=placed, out_specs=P("seq", "exp"), check_vma=False
    )
```

time: 158 us -> 93 us (0.59)
  waiting for transfers between devices: 79.4 us -> 23.8 us
  blocking collectives: 35.4 us -> 0 us
  starting transfers between devices: 7.02 us -> 39 us
  Pallas kernels: 0 us -> 13.8 us
  between operations: 13.6 us -> 0.27 us
  matrix products: 11.6 us -> 0 us
  local copies, waits for them, and re-layouts: 4.16 us -> 15.2 us
  other arithmetic: 6.25 us -> 0.37 us
    all_gather x1 -> x0, waiting for transfers between devices: 49.7 us -> none  [per_device(): shard_block = lax.all_gather(group_state[None], 'seq', axis=0, tiled=True)]
    ppermute x0 -> x31, starting transfers between devices: none -> 39 us  [the longest x16 17.9 us: hop(): lax.ppermute(rows, 'seq', [(order[p], order[(p + steps) % count]) for p i...]
    all_to_all x2 -> x0, blocking collectives: 35.4 us -> none  [the longest x1 28.3 us: per_device(): lax.all_to_all(outgoing, 'seq', split_axis=0, concat_axis=0, tiled=True)]
    all_to_all x2 -> x0, waiting for transfers between devices: 29.7 us -> none  [the longest x1 25.2 us: per_device(): lax.all_to_all(answered, 'seq', split_axis=0, concat_axis=0, tiled=True)]
    ppermute x0 -> x31, waiting for transfers between devices: none -> 23.8 us  [the longest x16 17.7 us: hop(): lax.ppermute(rows, 'seq', [(order[p], order[(p + steps) % count]) for p i...]
    unnamed x15 -> x26, local copies, waits for them, and re-layouts: 0.11 us -> 14.2 us
    pallas_call x0 -> x9, Pallas kernels: none -> 13.8 us  [call(): pl.pallas_call(kernel, out_shape=outs, in_specs=[SCALAR if i == 0 else FA...]
    dot_general x7 -> x0, matrix products: 11.6 us -> none  [the longest x1 5.88 us: per_device(): jnp.einsum('nd,gdf->gnf', flat_rows, expert_in[0], preferred_element_type...]
  transfers between devices with their start and end apart: 3 -> 31, of which waited for: 3 -> 13; matrix products, arithmetic and copies ran while one was open for 2% -> 1% of each run, Pallas kernels for 0% -> 3%
where the time goes in v2:
time: 93 us; the launch traced here: 92.5 us
  starting transfers between devices  39 us (42%)
  waiting for transfers between devices  23.8 us (26%)
  local copies, waits for them, and re-layouts  15.2 us (16%)
  Pallas kernels  13.8 us (15%)
    ppermute x16, starting transfers between devices, hop(): lax.ppermute(rows, 'seq', [(order[p], order[(p + steps) % count]) for p i...  17.9 us
    ppermute x16, waiting for transfers between devices, hop(): lax.ppermute(rows, 'seq', [(order[p], order[(p + steps) % count]) for p i...  17.7 us
    unnamed x26, local copies, waits for them, and re-layouts  14.2 us
    pallas_call x9, Pallas kernels, call(): pl.pallas_call(kernel, out_shape=outs, in_specs=[SCALAR if i == 0 else FA...  13.8 us
    ppermute x3, starting transfers between devices, pass_on(): lax.ppermute(state, 'seq', [(i, i + 2 * distance) for i in range(count -...  9.78 us
    ppermute x7, starting transfers between devices, per_device(): lax.ppermute(pieces[j], ('seq', 'exp'), [(s * parts + e, (s ^ block) * pa...  6.32 us
    ppermute x7, waiting for transfers between devices, per_device(): lax.ppermute(pieces[j], ('seq', 'exp'), [(s * parts + e, (s ^ block) * pa...  3.73 us
    ppermute x1, starting transfers between devices, per_device(): partner = lax.ppermute(given, 'seq', swap)  3 us
  transfers between devices with their start and end apart: 31, of which 13 were waited for; matrix products, arithmetic and copies ran while one was open for 1% of the time, Pallas kernels for 3%

profile of v2, /device:TPU:0, one launch (start us, length us, event | category | flops | bytes accessed | tf_op | source)
XLA Modules:
  0.0 92.5 jit_solution(9972667087605946723)
XLA Ops:
  0.1 0.9 copy-done.3
  1.0 0.9 copy-done.5
  1.9 1.6 %shard_map.102 = (bf16[128,256]{1,0:T(8,128)(2,1)S(1)}, bf16[128,256]{1,0:T(8,128)(2,1)S(1)}) custom-call(s32[4]{0:T(128)S(1)} %pad_add_fusion.scalars, bf16[128,512]{1,0:T(8,128)(2,1)S(1)} %copy-done.3, bf16[128,512]{1,0:T(8,128)(2,1)S(1)} %copy-done.5), custom_call_target="tpu_custom_call" | custom-call | flops 16777216 | bytes 393232 | tf_op jit(solution)/shard_map/pallas_call | solution.py:20
  3.5 3.0 %collective-permute-start.1 = (bf16[128,256]{1,0:T(8,128)(2,1)S(1)}, bf16[128,256]{1,0:T(8,128)(2,1)S(1)}, u32[]{:S(2)}, u32[]{:S(2)}) collective-permute-start(bf16[128,256]{1,0:T(8,128)(2,1)S(1)} %get-tuple-element.43), channel_id=1, source_target_pairs={{0,4},{4,0},{8,12},{12,8},{16,20},{20,16},{24,28},{28,24},{1,5},{5... | collective-permute-start | bytes 196616 | tf_op jit(solution)/shard_map/ppermute | solution.py:408
  6.5 0.9 copy-done.7
  7.5 0.9 copy-done.9
  8.4 0.6 shard_map.100
  9.0 0.1 collective-permute-start
  9.1 0.8 constant_dynamic-slice_fusion
  9.9 6.0 %collective-permute-start.4 = (bf16[128,256]{1,0:T(8,128)(2,1)S(1)}, bf16[128,256]{1,0:T(8,128)(2,1)S(1)}, u32[]{:S(2)}, u32[]{:S(2)}) collective-permute-start(bf16[128,256]{1,0:T(8,128)(2,1)S(1)} %add_convert_fusion.6), channel_id=1, source_target_pairs={{0,24},{4,28},{1,25},{5,29},{2,26},{6,30},{3,27},{7,31}} | collective-permute-start | bytes 196616 | tf_op jit(solution)/shard_map/ppermute | solution.py:364
  16.0 1.3 %collective-permute-start.3 = (bf16[128,256]{1,0:T(8,128)(2,1)S(1)}, bf16[128,256]{1,0:T(8,128)(2,1)S(1)}, u32[]{:S(2)}, u32[]{:S(2)}) collective-permute-start(bf16[128,256]{1,0:T(8,128)(2,1)S(1)} %add_convert_fusion.6), channel_id=1, source_target_pairs={{0,16},{4,20},{8,24},{12,28},{1,17},{5,21},{9,25},{13,29},{2,18},{... | collective-permute-start | bytes 196616 | tf_op jit(solution)/shard_map/ppermute | solution.py:364
  17.3 2.5 %collective-permute-start.2 = (bf16[128,256]{1,0:T(8,128)(2,1)S(1)}, bf16[128,256]{1,0:T(8,128)(2,1)S(1)}, u32[]{:S(2)}, u32[]{:S(2)}) collective-permute-start(bf16[128,256]{1,0:T(8,128)(2,1)S(1)} %add_convert_fusion.6), channel_id=1, source_target_pairs={{0,8},{4,12},{8,16},{12,20},{16,24},{20,28},{1,9},{5,13},{9,17},{1... | collective-permute-start | bytes 196616 | tf_op jit(solution)/shard_map/ppermute | solution.py:364
  19.8 0.1 copy.16
  19.9 0.9 copy-done.4
  20.8 0.9 copy-done.6
  21.7 0.9 copy-done.8
  22.6 0.9 copy-done.10
  23.5 0.7 copy-done.11
  24.2 0.7 copy-done.12
  24.9 1.1 %shard_map.101 = (f32[2,128,256]{2,1,0:T(8,128)S(1)}, bf16[128,256]{1,0:T(8,128)(2,1)S(1)}, bf16[128,256]{1,0:T(8,128)(2,1)S(1)}, f32[1,256]{1,0:T(1,128)S(1)}, f32[1,2048]{1,0:T(1,128)S(1)}) custom-call(s32[4]{0:T(128)S(1)} %pad_add_fusion.scalars, bf16[128,512]{1,0:T(8,128)(2,1)S(1)} %copy-done.4, bf16[128,512]{1,0:T(8,128)(2,1)S(1)} %copy-done.6, ...), custom_call_target="tpu_custom_call" | custom-call | flops 50331648 | bytes 1199120 | tf_op jit(solution)/shard_map/pallas_call | solution.py:20
  26.0 0.9 shard_map.103
  27.0 1.6 %collective-permute-start.6 = (bf16[32,256]{1,0:T(8,128)(2,1)S(1)}, bf16[32,256]{1,0:T(8,128)(2,1)S(1)}, u32[]{:S(2)}, u32[]{:S(2)}) collective-permute-start(bf16[32,256]{1,0:T(8,128)(2,1)S(1)} %get-tuple-element.46), channel_id=1, source_target_pairs={{0,2},{1,3},{2,0},{3,1},{4,6},{5,7},{6,4},{7,5},{8,10},{9,11},{10,... | collective-permute-start | bytes 49160 | tf_op jit(solution)/shard_map/ppermute | solution.py:444
  28.6 0.3 collective-permute-start.7
  28.9 1.5 %collective-permute-start.8 = (bf16[32,256]{1,0:T(8,128)(2,1)S(1)}, bf16[32,256]{1,0:T(8,128)(2,1)S(1)}, u32[]{:S(2)}, u32[]{:S(2)}) collective-permute-start(bf16[32,256]{1,0:T(8,128)(2,1)S(1)} %get-tuple-element.48), channel_id=1, source_target_pairs={{0,4},{1,5},{2,6},{3,7},{4,0},{5,1},{6,2},{7,3},{8,12},{9,13},{10,... | collective-permute-start | bytes 49160 | tf_op jit(solution)/shard_map/ppermute | solution.py:444
  30.4 0.2 collective-permute-start.9
  30.6 2.4 %collective-permute-start.10 = (bf16[32,256]{1,0:T(8,128)(2,1)S(1)}, bf16[32,256]{1,0:T(8,128)(2,1)S(1)}, u32[]{:S(2)}, u32[]{:S(2)}) collective-permute-start(bf16[32,256]{1,0:T(8,128)(2,1)S(1)} %get-tuple-element.50), channel_id=1, source_target_pairs={{0,6},{1,7},{2,4},{3,5},{4,2},{5,3},{6,0},{7,1},{8,14},{9,15},{10,... | collective-permute-start | bytes 49160 | tf_op jit(solution)/shard_map/ppermute | solution.py:444
  33.0 0.3 collective-permute-start.11
  33.3 0.1 fusion.2.pack_ref
  33.4 0.2 collective-permute-done.9.refs_5_
  33.5 1.7 %collective-permute-done.10.refs_6_ = bf16[32,256]{1,0:T(8,128)(2,1)S(1)} collective-permute-done((bf16[32,256]{1,0:T(8,128)(2,1)S(1)}, bf16[32,256]{1,0:T(8,128)(2,1)S(1)}, u32[]{:S(2)}, u32[]{:S(2)}) %collective-permute-start.10) | collective-permute-done | bytes 16416 | tf_op jit(solution)/shard_map/ppermute | solution.py:444
  35.2 1.9 %collective-permute-done.11.refs_7_ = bf16[32,256]{1,0:T(8,128)(2,1)S(1)} collective-permute-done((bf16[32,256]{1,0:T(8,128)(2,1)S(1)}, bf16[32,256]{1,0:T(8,128)(2,1)S(1)}, u32[]{:S(2)}, u32[]{:S(2)}) %collective-permute-start.11) | collective-permute-done | bytes 16416 | tf_op jit(solution)/shard_map/ppermute | solution.py:444
  37.1 0.7 shard_map.104
  37.8 0.6 collective-permute-start.15
  38.4 1.5 %collective-permute-start.12 = (bf16[32,2176]{1,0:T(8,128)(2,1)S(1)}, bf16[32,2176]{1,0:T(8,128)(2,1)S(1)}, u32[]{:S(2)}, u32[]{:S(2)}) collective-permute-start(bf16[32,2176]{1,0:T(8,128)(2,1)S(1)} %get-tuple-element.55.refs_0_), channel_id=1, source_target_pairs={{0,8},{8,16},{16,24},{24,28},{28,20},{20,12},{12,4},{4,0},{1,9},{9... | collective-permute-start | bytes 417800 | tf_op jit(solution)/shard_map/ppermute | solution.py:260
  39.9 3.7 %collective-permute-done.15.refs_4_ = bf16[32,2176]{1,0:T(8,128)(2,1)S(1)} collective-permute-done((bf16[32,2176]{1,0:T(8,128)(2,1)S(1)}, bf16[32,2176]{1,0:T(8,128)(2,1)S(1)}, u32[]{:S(2)}, u32[]{:S(2)}) %collective-permute-start.15) | collective-permute-done | bytes 139296 | tf_op jit(solution)/shard_map/ppermute | solution.py:260
  43.6 0.5 collective-permute-start.16
  44.1 1.5 %collective-permute-start.13 = (bf16[32,2176]{1,0:T(8,128)(2,1)S(1)}, bf16[32,2176]{1,0:T(8,128)(2,1)S(1)}, u32[]{:S(2)}, u32[]{:S(2)}) collective-permute-start(bf16[32,2176]{1,0:T(8,128)(2,1)S(1)} %collective-permute-done.12.refs_1_), channel_id=1, source_target_pairs={{0,8},{8,16},{16,24},{24,28},{28,20},{20,12},{12,4},{4,0},{1,9},{9... | collective-permute-start | bytes 417800 | tf_op jit(solution)/shard_map/ppermute | solution.py:260
  45.6 3.0 %collective-permute-done.16.refs_5_ = bf16[32,2176]{1,0:T(8,128)(2,1)S(1)} collective-permute-done((bf16[32,2176]{1,0:T(8,128)(2,1)S(1)}, bf16[32,2176]{1,0:T(8,128)(2,1)S(1)}, u32[]{:S(2)}, u32[]{:S(2)}) %collective-permute-start.16) | collective-permute-done | bytes 139296 | tf_op jit(solution)/shard_map/ppermute | solution.py:260
  48.6 0.5 collective-permute-start.17
  49.2 1.5 %collective-permute-start.14 = (bf16[32,2176]{1,0:T(8,128)(2,1)S(1)}, bf16[32,2176]{1,0:T(8,128)(2,1)S(1)}, u32[]{:S(2)}, u32[]{:S(2)}) collective-permute-start(bf16[32,2176]{1,0:T(8,128)(2,1)S(1)} %collective-permute-done.13.refs_2_), channel_id=1, source_target_pairs={{0,8},{8,16},{16,24},{24,28},{28,20},{20,12},{12,4},{4,0},{1,9},{9... | collective-permute-start | bytes 417800 | tf_op jit(solution)/shard_map/ppermute | solution.py:260
  50.7 0.4 collective-permute-start.19
  51.1 2.5 %collective-permute-start.18 = (bf16[16,2176]{1,0:T(8,128)(2,1)S(1)}, bf16[16,2176]{1,0:T(8,128)(2,1)S(1)}, u32[]{:S(2)}, u32[]{:S(2)}) collective-permute-start(bf16[16,2176]{1,0:T(8,128)(2,1)S(1)} %slice.40), channel_id=1, source_target_pairs={{0,16},{8,24},{16,28},{24,20},{28,12},{20,4},{12,0},{4,8},{1,17},{... | collective-permute-start | bytes 208904 | tf_op jit(solution)/shard_map/ppermute | solution.py:260
  53.6 3.4 %copy-done.1 = bf16[1,2,2048,1024]{3,2,1,0:T(8,128)(2,1)S(1)} copy-done((bf16[1,2,2048,1024]{3,2,1,0:T(8,128)(2,1)S(1)}, bf16[1,2,2048,1024]{3,2,1,0:T(8,128)(2,1)}, u32[]{:S(2)}) %copy-start.1) | copy-done | bytes 8388632
  57.0 2.2 %copy-done.2 = bf16[1,1024,2048]{2,1,0:T(8,128)(2,1)S(1)} copy-done((bf16[1,1024,2048]{2,1,0:T(8,128)(2,1)S(1)}, bf16[1,1024,2048]{2,1,0:T(8,128)(2,1)}, u32[]{:S(2)}) %copy-start.2) | copy-done | bytes 4194328
  59.2 1.5 %shard_map.105 = (bf16[2,2048,1024]{2,1,0:T(8,128)(2,1)S(1)}, bf16[1,1024,2048]{2,1,0:T(8,128)(2,1)S(1)}) custom-call(s32[4]{0:T(128)S(1)} %pad_add_fusion.scalars, bf16[2,2048,1024]{2,1,0:T(8,128)(2,1)S(1)} %bitcast.6, bf16[1,1024,2048]{2,1,0:T(8,128)(2,1)S(1)} %copy-done.2), custom_call_target="tpu_custom_call" | custom-call | bytes 25165840 | tf_op jit(solution)/shard_map/pallas_call | solution.py:20
  60.8 5.5 %shard_map.106 = (bf16[32,2048]{1,0:T(8,128)(2,1)S(1)}, bf16[32,2048]{1,0:T(8,128)(2,1)S(1)}, bf16[32,2048]{1,0:T(8,128)(2,1)S(1)}, bf16[32,2048]{1,0:T(8,128)(2...) custom-call(s32[4]{0:T(128)S(1)} %pad_add_fusion.scalars, ...), custom_call_target="tpu_custom_call" | custom-call | flops 3221225472 | bytes 14745616 | tf_op jit(solution)/shard_map/pallas_call | solution.py:20
  66.3 0.1 collective-permute-start.20
  66.5 2.9 %collective-permute-start.25 = (bf16[16,2048]{1,0:T(8,128)(2,1)S(1)}, bf16[16,2048]{1,0:T(8,128)(2,1)S(1)}, u32[]{:S(2)}, u32[]{:S(2)}) collective-permute-start(bf16[16,2048]{1,0:T(8,128)(2,1)S(1)} %get-tuple-element.63), channel_id=1, source_target_pairs={{0,12},{8,4},{16,0},{24,8},{28,16},{20,24},{12,28},{4,20},{1,13},{... | collective-permute-start | bytes 196616 | tf_op jit(solution)/shard_map/ppermute | solution.py:260
  69.3 2.0 %collective-permute-start.24 = (bf16[32,2048]{1,0:T(8,128)(2,1)S(1)}, bf16[32,2048]{1,0:T(8,128)(2,1)S(1)}, u32[]{:S(2)}, u32[]{:S(2)}) collective-permute-start(bf16[32,2048]{1,0:T(8,128)(2,1)S(1)} %get-tuple-element.61), channel_id=1, source_target_pairs={{0,4},{8,0},{16,8},{24,16},{28,24},{20,28},{12,20},{4,12},{1,5},{9... | collective-permute-start | bytes 393224 | tf_op jit(solution)/shard_map/ppermute | solution.py:260
  71.3 0.8 collective-permute-done.21
  72.1 0.2 collective-permute-done.20
  72.3 0.6 collective-permute-start.22
  73.0 2.7 %collective-permute-done.24 = bf16[32,2048]{1,0:T(8,128)(2,1)S(1)} collective-permute-done((bf16[32,2048]{1,0:T(8,128)(2,1)S(1)}, bf16[32,2048]{1,0:T(8,128)(2,1)S(1)}, u32[]{:S(2)}, u32[]{:S(2)}) %collective-permute-start.24) | collective-permute-done | bytes 131104 | tf_op jit(solution)/shard_map/ppermute | solution.py:260
  75.8 1.7 %collective-permute-start.26 = (bf16[32,2048]{1,0:T(8,128)(2,1)S(1)}, bf16[32,2048]{1,0:T(8,128)(2,1)S(1)}, u32[]{:S(2)}, u32[]{:S(2)}) collective-permute-start(bf16[32,2048]{1,0:T(8,128)(2,1)S(1)} %pad_maximum_fusion.1), channel_id=1, source_target_pairs={{0,4},{8,0},{16,8},{24,16},{28,24},{20,28},{12,20},{4,12},{1,5},{9... | collective-permute-start | bytes 393224 | tf_op jit(solution)/shard_map/ppermute | solution.py:260
  77.5 1.5 %collective-permute-done.22 = bf16[32,2048]{1,0:T(8,128)(2,1)S(1)} collective-permute-done((bf16[32,2048]{1,0:T(8,128)(2,1)S(1)}, bf16[32,2048]{1,0:T(8,128)(2,1)S(1)}, u32[]{:S(2)}, u32[]{:S(2)}) %collective-permute-start.22) | collective-permute-done | bytes 131104 | tf_op jit(solution)/shard_map/ppermute | solution.py:260
  79.1 2.1 %collective-permute-done.26 = bf16[32,2048]{1,0:T(8,128)(2,1)S(1)} collective-permute-done((bf16[32,2048]{1,0:T(8,128)(2,1)S(1)}, bf16[32,2048]{1,0:T(8,128)(2,1)S(1)}, u32[]{:S(2)}, u32[]{:S(2)}) %collective-permute-start.26) | collective-permute-done | bytes 131104 | tf_op jit(solution)/shard_map/ppermute | solution.py:260
  81.3 1.4 %collective-permute-start.27 = (bf16[32,2048]{1,0:T(8,128)(2,1)S(1)}, bf16[32,2048]{1,0:T(8,128)(2,1)S(1)}, u32[]{:S(2)}, u32[]{:S(2)}) collective-permute-start(bf16[32,2048]{1,0:T(8,128)(2,1)S(1)} %add_convert_fusion), channel_id=1, source_target_pairs={{0,4},{8,0},{16,8},{24,16},{28,24},{20,28},{12,20},{4,12},{1,5},{9... | collective-permute-start | bytes 393224 | tf_op jit(solution)/shard_map/ppermute | solution.py:260
  82.7 1.3 %collective-permute-done.23.b_ref = bf16[32,2048]{1,0:T(8,128)(2,1)S(1)} collective-permute-done((bf16[32,2048]{1,0:T(8,128)(2,1)S(1)}, bf16[32,2048]{1,0:T(8,128)(2,1)S(1)}, u32[]{:S(2)}, u32[]{:S(2)}) %collective-permute-start.23) | collective-permute-done | bytes 131104 | tf_op jit(solution)/shard_map/ppermute | solution.py:260
  84.1 2.2 %collective-permute-done.27.c_ref = bf16[32,2048]{1,0:T(8,128)(2,1)S(1)} collective-permute-done((bf16[32,2048]{1,0:T(8,128)(2,1)S(1)}, bf16[32,2048]{1,0:T(8,128)(2,1)S(1)}, u32[]{:S(2)}, u32[]{:S(2)}) %collective-permute-start.27) | collective-permute-done | bytes 131104 | tf_op jit(solution)/shard_map/ppermute | solution.py:260
  86.3 0.6 shard_map.107
  87.0 0.6 collective-permute-start.29
  87.6 1.3 %collective-permute-start.30 = (bf16[32,512]{1,0:T(8,128)(2,1)S(1)}, bf16[32,512]{1,0:T(8,128)(2,1)S(1)}, u32[]{:S(2)}, u32[]{:S(2)}) collective-permute-start(bf16[32,512]{1,0:T(8,128)(2,1)S(1)} %get-tuple-element.68), channel_id=1, source_target_pairs={{0,3},{1,2},{2,1},{3,0},{4,7},{5,6},{6,5},{7,4},{8,11},{9,10},{10,... | collective-permute-start | bytes 98312 | tf_op jit(solution)/shard_map/ppermute | solution.py:485
  88.9 2.4 %collective-permute-done.29.refs_2_ = bf16[32,512]{1,0:T(8,128)(2,1)S(1)} collective-permute-done((bf16[32,512]{1,0:T(8,128)(2,1)S(1)}, bf16[32,512]{1,0:T(8,128)(2,1)S(1)}, u32[]{:S(2)}, u32[]{:S(2)}) %collective-permute-start.29) | collective-permute-done | bytes 32800 | tf_op jit(solution)/shard_map/ppermute | solution.py:485
  91.3 1.2 %shard_map.108 = bf16[128,512]{1,0:T(8,128)(2,1)} custom-call(s32[4]{0:T(128)S(1)} %pad_add_fusion.scalars, bf16[32,512]{1,0:T(8,128)(2,1)S(1)} %get-tuple-element.65.refs_0_, bf16[32,512]{1,0:T(8,128)(2,1)S(1)} %collective-permute-done.28.refs_1_, bf16[32,512]{1,0:T(8,128)(2,1)S(1)} %collective-permute-done.29.refs_2_, ...), custom_call_target="tpu_custom_call" | custom-call | bytes 262160 | tf_op jit(solution)/shard_map/pallas_call | solution.py:20
  (51 shorter events, 0.8 us)
Async XLA Ops:
  0.0 9.1 %copy-start = (s32[128,8]{0,1:T(8,128)S(1)}, s32[128,8]{0,1:T(8,128)}, u32[]{:S(2)}) copy-start(s32[128,8]{0,1:T(8,128)} %param.16) | copy-start | bytes 12292
  0.1 0.9 copy-start.3
  1.0 0.9 copy-start.5
  3.5 6.4 %collective-permute-start.1 = (bf16[128,256]{1,0:T(8,128)(2,1)S(1)}, bf16[128,256]{1,0:T(8,128)(2,1)S(1)}, u32[]{:S(2)}, u32[]{:S(2)}) collective-permute-start(bf16[128,256]{1,0:T(8,128)(2,1)S(1)} %get-tuple-element.43), channel_id=1, source_target_pairs={{0,4},{4,0},{8,12},{12,8},{16,20},{20,16},{24,28},{28,24},{1,5},{5... | collective-permute-start | bytes 196616 | tf_op jit(solution)/shard_map/ppermute | solution.py:408
  6.5 0.9 copy-start.7
  7.5 0.9 copy-start.9
  9.0 10.9 %collective-permute-start = (bf16[128,1024]{1,0:T(8,128)(2,1)S(1)}, bf16[128,1024]{1,0:T(8,128)(2,1)S(1)}, u32[]{:S(2)}, u32[]{:S(2)}) collective-permute-start(bf16[128,1024]{1,0:T(8,128)(2,1)S(1)} %shard_map.100), channel_id=1, source_target_pairs={{0,4},{4,0},{8,12},{12,8},{16,20},{20,16},{24,28},{28,24},{1,5},{5... | collective-permute-start | bytes 786440 | tf_op jit(solution)/shard_map/ppermute | solution.py:414
  9.9 16.1 %collective-permute-start.4 = (bf16[128,256]{1,0:T(8,128)(2,1)S(1)}, bf16[128,256]{1,0:T(8,128)(2,1)S(1)}, u32[]{:S(2)}, u32[]{:S(2)}) collective-permute-start(bf16[128,256]{1,0:T(8,128)(2,1)S(1)} %add_convert_fusion.6), channel_id=1, source_target_pairs={{0,24},{4,28},{1,25},{5,29},{2,26},{6,30},{3,27},{7,31}} | collective-permute-start | bytes 196616 | tf_op jit(solution)/shard_map/ppermute | solution.py:364
  16.0 10.0 %collective-permute-start.3 = (bf16[128,256]{1,0:T(8,128)(2,1)S(1)}, bf16[128,256]{1,0:T(8,128)(2,1)S(1)}, u32[]{:S(2)}, u32[]{:S(2)}) collective-permute-start(bf16[128,256]{1,0:T(8,128)(2,1)S(1)} %add_convert_fusion.6), channel_id=1, source_target_pairs={{0,16},{4,20},{8,24},{12,28},{1,17},{5,21},{9,25},{13,29},{2,18},{... | collective-permute-start | bytes 196616 | tf_op jit(solution)/shard_map/ppermute | solution.py:364
  17.3 8.7 %collective-permute-start.2 = (bf16[128,256]{1,0:T(8,128)(2,1)S(1)}, bf16[128,256]{1,0:T(8,128)(2,1)S(1)}, u32[]{:S(2)}, u32[]{:S(2)}) collective-permute-start(bf16[128,256]{1,0:T(8,128)(2,1)S(1)} %add_convert_fusion.6), channel_id=1, source_target_pairs={{0,8},{4,12},{8,16},{12,20},{16,24},{20,28},{1,9},{5,13},{9,17},{1... | collective-permute-start | bytes 196616 | tf_op jit(solution)/shard_map/ppermute | solution.py:364
  19.9 0.9 copy-start.4
  20.8 0.9 copy-start.6
  21.7 0.9 copy-start.8
  22.6 0.9 copy-start.10
  23.5 0.7 copy-start.11
  24.2 0.7 copy-start.12
  26.9 3.6 %collective-permute-start.5 = (bf16[32,256]{1,0:T(8,128)(2,1)S(1)}, bf16[32,256]{1,0:T(8,128)(2,1)S(1)}, u32[]{:S(2)}, u32[]{:S(2)}) collective-permute-start(bf16[32,256]{1,0:T(8,128)(2,1)S(1)} %get-tuple-element.45), channel_id=1, source_target_pairs={{0,1},{1,0},{2,3},{3,2},{4,5},{5,4},{6,7},{7,6},{8,9},{9,8},{10,11... | collective-permute-start | bytes 49160 | tf_op jit(solution)/shard_map/ppermute | solution.py:444
  27.0 6.0 %collective-permute-start.6 = (bf16[32,256]{1,0:T(8,128)(2,1)S(1)}, bf16[32,256]{1,0:T(8,128)(2,1)S(1)}, u32[]{:S(2)}, u32[]{:S(2)}) collective-permute-start(bf16[32,256]{1,0:T(8,128)(2,1)S(1)} %get-tuple-element.46), channel_id=1, source_target_pairs={{0,2},{1,3},{2,0},{3,1},{4,6},{5,7},{6,4},{7,5},{8,10},{9,11},{10,... | collective-permute-start | bytes 49160 | tf_op jit(solution)/shard_map/ppermute | solution.py:444
  28.6 4.8 %collective-permute-start.7 = (bf16[32,256]{1,0:T(8,128)(2,1)S(1)}, bf16[32,256]{1,0:T(8,128)(2,1)S(1)}, u32[]{:S(2)}, u32[]{:S(2)}) collective-permute-start(bf16[32,256]{1,0:T(8,128)(2,1)S(1)} %get-tuple-element.47), channel_id=1, source_target_pairs={{0,3},{1,2},{2,1},{3,0},{4,7},{5,6},{6,5},{7,4},{8,11},{9,10},{10,... | collective-permute-start | bytes 49160 | tf_op jit(solution)/shard_map/ppermute | solution.py:444
  28.9 4.5 %collective-permute-start.8 = (bf16[32,256]{1,0:T(8,128)(2,1)S(1)}, bf16[32,256]{1,0:T(8,128)(2,1)S(1)}, u32[]{:S(2)}, u32[]{:S(2)}) collective-permute-start(bf16[32,256]{1,0:T(8,128)(2,1)S(1)} %get-tuple-element.48), channel_id=1, source_target_pairs={{0,4},{1,5},{2,6},{3,7},{4,0},{5,1},{6,2},{7,3},{8,12},{9,13},{10,... | collective-permute-start | bytes 49160 | tf_op jit(solution)/shard_map/ppermute | solution.py:444
  30.4 3.2 %collective-permute-start.9 = (bf16[32,256]{1,0:T(8,128)(2,1)S(1)}, bf16[32,256]{1,0:T(8,128)(2,1)S(1)}, u32[]{:S(2)}, u32[]{:S(2)}) collective-permute-start(bf16[32,256]{1,0:T(8,128)(2,1)S(1)} %get-tuple-element.49), channel_id=1, source_target_pairs={{0,5},{1,4},{2,7},{3,6},{4,1},{5,0},{6,3},{7,2},{8,13},{9,12},{10,... | collective-permute-start | bytes 49160 | tf_op jit(solution)/shard_map/ppermute | solution.py:444
  30.6 4.6 %collective-permute-start.10 = (bf16[32,256]{1,0:T(8,128)(2,1)S(1)}, bf16[32,256]{1,0:T(8,128)(2,1)S(1)}, u32[]{:S(2)}, u32[]{:S(2)}) collective-permute-start(bf16[32,256]{1,0:T(8,128)(2,1)S(1)} %get-tuple-element.50), channel_id=1, source_target_pairs={{0,6},{1,7},{2,4},{3,5},{4,2},{5,3},{6,0},{7,1},{8,14},{9,15},{10,... | collective-permute-start | bytes 49160 | tf_op jit(solution)/shard_map/ppermute | solution.py:444
  33.0 4.1 %collective-permute-start.11 = (bf16[32,256]{1,0:T(8,128)(2,1)S(1)}, bf16[32,256]{1,0:T(8,128)(2,1)S(1)}, u32[]{:S(2)}, u32[]{:S(2)}) collective-permute-start(bf16[32,256]{1,0:T(8,128)(2,1)S(1)} %get-tuple-element.51), channel_id=1, source_target_pairs={{0,7},{1,6},{2,5},{3,4},{4,3},{5,2},{6,1},{7,0},{8,15},{9,14},{10,... | collective-permute-start | bytes 49160 | tf_op jit(solution)/shard_map/ppermute | solution.py:444
  37.8 5.8 %collective-permute-start.15 = (bf16[32,2176]{1,0:T(8,128)(2,1)S(1)}, bf16[32,2176]{1,0:T(8,128)(2,1)S(1)}, u32[]{:S(2)}, u32[]{:S(2)}) collective-permute-start(bf16[32,2176]{1,0:T(8,128)(2,1)S(1)} %get-tuple-element.55.refs_0_), channel_id=1, source_target_pairs={{0,4},{8,0},{16,8},{24,16},{28,24},{20,28},{12,20},{4,12},{1,5},{9... | collective-permute-start | bytes 417800 | tf_op jit(solution)/shard_map/ppermute | solution.py:260
  38.4 5.7 %collective-permute-start.12 = (bf16[32,2176]{1,0:T(8,128)(2,1)S(1)}, bf16[32,2176]{1,0:T(8,128)(2,1)S(1)}, u32[]{:S(2)}, u32[]{:S(2)}) collective-permute-start(bf16[32,2176]{1,0:T(8,128)(2,1)S(1)} %get-tuple-element.55.refs_0_), channel_id=1, source_target_pairs={{0,8},{8,16},{16,24},{24,28},{28,20},{20,12},{12,4},{4,0},{1,9},{9... | collective-permute-start | bytes 417800 | tf_op jit(solution)/shard_map/ppermute | solution.py:260
  43.6 5.1 %collective-permute-start.16 = (bf16[32,2176]{1,0:T(8,128)(2,1)S(1)}, bf16[32,2176]{1,0:T(8,128)(2,1)S(1)}, u32[]{:S(2)}, u32[]{:S(2)}) collective-permute-start(bf16[32,2176]{1,0:T(8,128)(2,1)S(1)} %collective-permute-done.15.refs_4_), channel_id=1, source_target_pairs={{0,4},{8,0},{16,8},{24,16},{28,24},{20,28},{12,20},{4,12},{1,5},{9... | collective-permute-start | bytes 417800 | tf_op jit(solution)/shard_map/ppermute | solution.py:260
  44.1 5.1 %collective-permute-start.13 = (bf16[32,2176]{1,0:T(8,128)(2,1)S(1)}, bf16[32,2176]{1,0:T(8,128)(2,1)S(1)}, u32[]{:S(2)}, u32[]{:S(2)}) collective-permute-start(bf16[32,2176]{1,0:T(8,128)(2,1)S(1)} %collective-permute-done.12.refs_1_), channel_id=1, source_target_pairs={{0,8},{8,16},{16,24},{24,28},{28,20},{20,12},{12,4},{4,0},{1,9},{9... | collective-permute-start | bytes 417800 | tf_op jit(solution)/shard_map/ppermute | solution.py:260
  48.6 12.1 %collective-permute-start.17 = (bf16[32,2176]{1,0:T(8,128)(2,1)S(1)}, bf16[32,2176]{1,0:T(8,128)(2,1)S(1)}, u32[]{:S(2)}, u32[]{:S(2)}) collective-permute-start(bf16[32,2176]{1,0:T(8,128)(2,1)S(1)} %collective-permute-done.16.refs_5_), channel_id=1, source_target_pairs={{0,4},{8,0},{16,8},{24,16},{28,24},{20,28},{12,20},{4,12},{1,5},{9... | collective-permute-start | bytes 417800 | tf_op jit(solution)/shard_map/ppermute | solution.py:260
  49.2 11.6 %collective-permute-start.14 = (bf16[32,2176]{1,0:T(8,128)(2,1)S(1)}, bf16[32,2176]{1,0:T(8,128)(2,1)S(1)}, u32[]{:S(2)}, u32[]{:S(2)}) collective-permute-start(bf16[32,2176]{1,0:T(8,128)(2,1)S(1)} %collective-permute-done.13.refs_2_), channel_id=1, source_target_pairs={{0,8},{8,16},{16,24},{24,28},{28,20},{20,12},{12,4},{4,0},{1,9},{9... | collective-permute-start | bytes 417800 | tf_op jit(solution)/shard_map/ppermute | solution.py:260
  50.7 10.0 %collective-permute-start.19 = (bf16[16,2176]{1,0:T(8,128)(2,1)S(1)}, bf16[16,2176]{1,0:T(8,128)(2,1)S(1)}, u32[]{:S(2)}, u32[]{:S(2)}) collective-permute-start(bf16[16,2176]{1,0:T(8,128)(2,1)S(1)} %slice.41), channel_id=1, source_target_pairs={{0,12},{8,4},{16,0},{24,8},{28,16},{20,24},{12,28},{4,20},{1,13},{... | collective-permute-start | bytes 208904 | tf_op jit(solution)/shard_map/ppermute | solution.py:260
  51.1 9.6 %collective-permute-start.18 = (bf16[16,2176]{1,0:T(8,128)(2,1)S(1)}, bf16[16,2176]{1,0:T(8,128)(2,1)S(1)}, u32[]{:S(2)}, u32[]{:S(2)}) collective-permute-start(bf16[16,2176]{1,0:T(8,128)(2,1)S(1)} %slice.40), channel_id=1, source_target_pairs={{0,16},{8,24},{16,28},{24,20},{28,12},{20,4},{12,0},{4,8},{1,17},{... | collective-permute-start | bytes 208904 | tf_op jit(solution)/shard_map/ppermute | solution.py:260
  53.6 3.4 %copy-start.1 = (bf16[1,2,2048,1024]{3,2,1,0:T(8,128)(2,1)S(1)}, bf16[1,2,2048,1024]{3,2,1,0:T(8,128)(2,1)}, u32[]{:S(2)}) copy-start(bf16[1,2,2048,1024]{3,2,1,0:T(8,128)(2,1)} %param.18) | copy-start | bytes 25165828
  57.0 2.2 %copy-start.2 = (bf16[1,1024,2048]{2,1,0:T(8,128)(2,1)S(1)}, bf16[1,1024,2048]{2,1,0:T(8,128)(2,1)}, u32[]{:S(2)}) copy-start(bf16[1,1024,2048]{2,1,0:T(8,128)(2,1)} %out_ref.1) | copy-start | bytes 12582916
  66.3 6.0 %collective-permute-start.20 = (bf16[32,2048]{1,0:T(8,128)(2,1)S(1)}, bf16[32,2048]{1,0:T(8,128)(2,1)S(1)}, u32[]{:S(2)}, u32[]{:S(2)}) collective-permute-start(bf16[32,2048]{1,0:T(8,128)(2,1)S(1)} %get-tuple-element.57), channel_id=1, source_target_pairs={{0,8},{8,16},{16,24},{24,28},{28,20},{20,12},{12,4},{4,0},{1,9},{9... | collective-permute-start | bytes 393224 | tf_op jit(solution)/shard_map/ppermute | solution.py:260
  66.4 5.7 %collective-permute-start.21 = (bf16[16,2048]{1,0:T(8,128)(2,1)S(1)}, bf16[16,2048]{1,0:T(8,128)(2,1)S(1)}, u32[]{:S(2)}, u32[]{:S(2)}) collective-permute-start(bf16[16,2048]{1,0:T(8,128)(2,1)S(1)} %get-tuple-element.59), channel_id=1, source_target_pairs={{0,16},{8,24},{16,28},{24,20},{28,12},{20,4},{12,0},{4,8},{1,17},{... | collective-permute-start | bytes 196616 | tf_op jit(solution)/shard_map/ppermute | solution.py:260
  66.5 6.5 %collective-permute-start.25 = (bf16[16,2048]{1,0:T(8,128)(2,1)S(1)}, bf16[16,2048]{1,0:T(8,128)(2,1)S(1)}, u32[]{:S(2)}, u32[]{:S(2)}) collective-permute-start(bf16[16,2048]{1,0:T(8,128)(2,1)S(1)} %get-tuple-element.63), channel_id=1, source_target_pairs={{0,12},{8,4},{16,0},{24,8},{28,16},{20,24},{12,28},{4,20},{1,13},{... | collective-permute-start | bytes 196616 | tf_op jit(solution)/shard_map/ppermute | solution.py:260
  69.3 6.3 %collective-permute-start.24 = (bf16[32,2048]{1,0:T(8,128)(2,1)S(1)}, bf16[32,2048]{1,0:T(8,128)(2,1)S(1)}, u32[]{:S(2)}, u32[]{:S(2)}) collective-permute-start(bf16[32,2048]{1,0:T(8,128)(2,1)S(1)} %get-tuple-element.61), channel_id=1, source_target_pairs={{0,4},{8,0},{16,8},{24,16},{28,24},{20,28},{12,20},{4,12},{1,5},{9... | collective-permute-start | bytes 393224 | tf_op jit(solution)/shard_map/ppermute | solution.py:260
  72.3 6.7 %collective-permute-start.22 = (bf16[32,2048]{1,0:T(8,128)(2,1)S(1)}, bf16[32,2048]{1,0:T(8,128)(2,1)S(1)}, u32[]{:S(2)}, u32[]{:S(2)}) collective-permute-start(bf16[32,2048]{1,0:T(8,128)(2,1)S(1)} %pad_maximum_fusion), channel_id=1, source_target_pairs={{0,8},{8,16},{16,24},{24,28},{28,20},{20,12},{12,4},{4,0},{1,9},{9... | collective-permute-start | bytes 393224 | tf_op jit(solution)/shard_map/ppermute | solution.py:260
  75.8 5.5 %collective-permute-start.26 = (bf16[32,2048]{1,0:T(8,128)(2,1)S(1)}, bf16[32,2048]{1,0:T(8,128)(2,1)S(1)}, u32[]{:S(2)}, u32[]{:S(2)}) collective-permute-start(bf16[32,2048]{1,0:T(8,128)(2,1)S(1)} %pad_maximum_fusion.1), channel_id=1, source_target_pairs={{0,4},{8,0},{16,8},{24,16},{28,24},{20,28},{12,20},{4,12},{1,5},{9... | collective-permute-start | bytes 393224 | tf_op jit(solution)/shard_map/ppermute | solution.py:260
  79.1 5.0 %collective-permute-start.23 = (bf16[32,2048]{1,0:T(8,128)(2,1)S(1)}, bf16[32,2048]{1,0:T(8,128)(2,1)S(1)}, u32[]{:S(2)}, u32[]{:S(2)}) collective-permute-start(bf16[32,2048]{1,0:T(8,128)(2,1)S(1)} %add_convert_fusion.1), channel_id=1, source_target_pairs={{0,8},{8,16},{16,24},{24,28},{28,20},{20,12},{12,4},{4,0},{1,9},{9... | collective-permute-start | bytes 393224 | tf_op jit(solution)/shard_map/ppermute | solution.py:260
  81.3 5.0 %collective-permute-start.27 = (bf16[32,2048]{1,0:T(8,128)(2,1)S(1)}, bf16[32,2048]{1,0:T(8,128)(2,1)S(1)}, u32[]{:S(2)}, u32[]{:S(2)}) collective-permute-start(bf16[32,2048]{1,0:T(8,128)(2,1)S(1)} %add_convert_fusion), channel_id=1, source_target_pairs={{0,4},{8,0},{16,8},{24,16},{28,24},{20,28},{12,20},{4,12},{1,5},{9... | collective-permute-start | bytes 393224 | tf_op jit(solution)/shard_map/ppermute | solution.py:260
  86.9 1.9 %collective-permute-start.28 = (bf16[32,512]{1,0:T(8,128)(2,1)S(1)}, bf16[32,512]{1,0:T(8,128)(2,1)S(1)}, u32[]{:S(2)}, u32[]{:S(2)}) collective-permute-start(bf16[32,512]{1,0:T(8,128)(2,1)S(1)} %get-tuple-element.66), channel_id=1, source_target_pairs={{0,1},{1,0},{2,3},{3,2},{4,5},{5,4},{6,7},{7,6},{8,9},{9,8},{10,11... | collective-permute-start | bytes 98312 | tf_op jit(solution)/shard_map/ppermute | solution.py:485
  87.0 4.2 %collective-permute-start.29 = (bf16[32,512]{1,0:T(8,128)(2,1)S(1)}, bf16[32,512]{1,0:T(8,128)(2,1)S(1)}, u32[]{:S(2)}, u32[]{:S(2)}) collective-permute-start(bf16[32,512]{1,0:T(8,128)(2,1)S(1)} %get-tuple-element.67), channel_id=1, source_target_pairs={{0,2},{1,3},{2,0},{3,1},{4,6},{5,7},{6,4},{7,5},{8,10},{9,11},{10,... | collective-permute-start | bytes 98312 | tf_op jit(solution)/shard_map/ppermute | solution.py:485
  87.6 3.7 %collective-permute-start.30 = (bf16[32,512]{1,0:T(8,128)(2,1)S(1)}, bf16[32,512]{1,0:T(8,128)(2,1)S(1)}, u32[]{:S(2)}, u32[]{:S(2)}) collective-permute-start(bf16[32,512]{1,0:T(8,128)(2,1)S(1)} %get-tuple-element.68), channel_id=1, source_target_pairs={{0,3},{1,2},{2,1},{3,0},{4,7},{5,6},{6,5},{7,4},{8,11},{9,10},{10,... | collective-permute-start | bytes 98312 | tf_op jit(solution)/shard_map/ppermute | solution.py:485

commit v3 on v2

--- a/solution.py
+++ b/solution.py
@@ -17,6 +17,10 @@
 
 def call(kernel, outs, inputs, far=(), scratch=(), out_specs=None, flops=0, limit=16 << 20):
     moved = sum(a.size * a.dtype.itemsize for a in [*inputs, *outs])
+    inputs = [
+        pltpu.with_memory_space_constraint(a, pltpu.HBM) if i in far else a
+        for i, a in enumerate(inputs)
+    ]
     return pl.pallas_call(
         kernel,
         out_shape=outs,
@@ -123,7 +127,7 @@
 
 
 def attend_kernel(
-    parts, earlier, scalars, within_ref, my_query, my_residual, my_gain, came_ref, kept_ref,
+    parts, earlier, scalars, loaded_ref, within_ref, my_query, my_residual, my_gain, came_ref, kept_ref,
     partner_ref, *refs
 ):
     before_refs, piece_refs, hidden = refs[:earlier], refs[earlier:-1], refs[-1]
@@ -177,7 +181,8 @@
     out_ref[:, model:] = pack_ref[...]
 
 
-def load_kernel(scalars, in_ref, out_ref, in_kept, out_kept, sems):
+def load_kernel(scalars, in_ref, out_ref, after_ref, in_kept, out_kept, done_ref, sems):
+    done_ref[...] = jnp.zeros_like(done_ref)
     pairs = []
     for source, target in ((in_ref, in_kept), (out_ref, out_kept)):
         pieces = 4
@@ -189,11 +194,11 @@
     run_copies(pairs, sems)
 
 
-def load_weights(scalars, expert_in, expert_out):
+def load_weights(scalars, expert_in, expert_out, after):
     return call(
         load_kernel,
-        [shape(expert_in.shape, BF16), shape(expert_out.shape, BF16)],
-        [scalars, expert_in, expert_out],
+        [shape(expert_in.shape, BF16), shape(expert_out.shape, BF16), shape((8, HEAD), F32)],
+        [scalars, expert_in, expert_out, after],
         far=(1, 2),
         scratch=[pltpu.SemaphoreType.DMA((4 * (expert_in.shape[0] + expert_out.shape[0]),))],
     )
@@ -250,7 +255,7 @@
     return list(range(0, count, 2)) + list(range(1, count, 2))[::-1]
 
 
-def dense_experts(block, scalars, expert_in, expert_out):
+def dense_experts(block, scalars, weights):
     count = lax.axis_size("seq")
     order = ring_order(count)
     half = block.shape[0] // 2
@@ -267,7 +272,6 @@
         behind.append(hop(behind[-1], -1))
     top = hop(ahead[-2][:half], 2)
     bottom = hop(behind[-2][half:], -2)
-    weights = load_weights(scalars, expert_in[0], expert_out)
     blocks = [block] + ahead[1:] + behind[1:] + [top, bottom]
     made = run_expert(scalars, blocks, *weights)
     own, from_ahead, from_behind = made[0], made[1:far], made[far:2 * far - 1]
@@ -430,10 +434,15 @@
         scratch=[pltpu.VMEM((rows, half), BF16)] * 2 + [pltpu.SemaphoreType.DMA((6,))],
         flops=6 * rows * rows * width,
     )
+    dense = routes.shape[1] == experts
+    if dense:
+        *weights, loaded = load_weights(scalars, expert_in[0], expert_out, partner)
+    else:
+        loaded = jnp.zeros((8, HEAD), F32)
     pieces = call(
         functools.partial(attend_kernel, parts, len(before)),
         [shape((count, half), BF16)] * (2 * parts),
-        [scalars, within, my_query, my_residual, my_gain, came, kept, partner, *before],
+        [scalars, loaded, within, my_query, my_residual, my_gain, came, kept, partner, *before],
         scratch=[pltpu.VMEM((2, rows, half), BF16)],
         flops=4 * rows * width * HEAD,
     )
@@ -454,7 +463,7 @@
 
     my_routes = lax.dynamic_slice_in_dim(routes, my_index * count, count, 0)
     my_gates = lax.dynamic_slice_in_dim(route_gates, my_index * count, count, 0)
-    weights = jnp.sum(
+    mixing = jnp.sum(
         jnp.where(
             my_routes[:, :, None] == jnp.arange(experts, dtype=jnp.int32),
             my_gates[:, :, None],
@@ -462,18 +471,18 @@
         ),
         axis=1,
     )
-    high = lax.reduce_precision(weights, 8, 7)
+    high = lax.reduce_precision(mixing, 8, 7)
     lanes = -(-2 * experts // HEAD) * HEAD
     pack = jnp.pad(
-        jnp.concatenate([high, weights - high], axis=1), ((0, 0), (0, lanes - 2 * experts))
+        jnp.concatenate([high, mixing - high], axis=1), ((0, 0), (0, lanes - 2 * experts))
     ).astype(BF16)
     hidden, block = call(
         functools.partial(norm_kernel, parts),
         [shape((count, model), BF16), shape((count, model + lanes), BF16)],
         [scalars, my_norm, pack] + gathered,
     )
-    if routes.shape[1] == experts:
-        terms = dense_experts(block, scalars, expert_in, expert_out)
+    if dense:
+        terms = dense_experts(block, scalars, weights)
     else:
         mixed = routed_experts(block[:, :model], my_routes, my_gates, expert_in, expert_out)
         nothing = jnp.zeros_like(mixed)

time: 93 us -> 89.5 us (0.962)
  local copies, waits for them, and re-layouts: 15.2 us -> 1 us
  Pallas kernels: 13.8 us -> 19.9 us
  waiting for transfers between devices: 23.8 us -> 28.1 us
    unnamed x26 -> x2, local copies, waits for them, and re-layouts: 14.2 us -> 0.01 us
    pallas_call x9, Pallas kernels: 13.8 us -> 19.9 us  [call(): pl.pallas_call(kernel, out_shape=outs, in_specs=[SCALAR if i == 0 else FA...]
    ppermute x16, waiting for transfers between devices: 17.7 us -> 21.9 us  [hop(): lax.ppermute(rows, 'seq', [(order[p], order[(p + steps) % count]) for p i...]
  transfers between devices with their start and end apart: 31 -> 31, of which waited for: 13 -> 16; matrix products, arithmetic and copies ran while one was open for 1% -> 1% of each run, Pallas kernels for 3% -> 10%
where the time goes in v3:
time: 89.5 us; the launch traced here: 89.2 us
  starting transfers between devices  39.6 us (44%)
  waiting for transfers between devices  28.1 us (31%)
  Pallas kernels  19.9 us (22%)
  local copies, waits for them, and re-layouts  1 us (1%)
    ppermute x16, waiting for transfers between devices, hop(): lax.ppermute(rows, 'seq', [(order[p], order[(p + steps) % count]) for p i...  21.9 us
    pallas_call x9, Pallas kernels, call(): pl.pallas_call(kernel, out_shape=outs, in_specs=[SCALAR if i == 0 else FA...  19.9 us
    ppermute x16, starting transfers between devices, hop(): lax.ppermute(rows, 'seq', [(order[p], order[(p + steps) % count]) for p i...  18.4 us
    ppermute x3, starting transfers between devices, pass_on(): lax.ppermute(state, 'seq', [(i, i + 2 * distance) for i in range(count -...  9.78 us
    ppermute x7, starting transfers between devices, per_device(): lax.ppermute(pieces[j], ('seq', 'exp'), [(s * parts + e, (s ^ block) * pa...  6.32 us
    ppermute x7, waiting for transfers between devices, per_device(): lax.ppermute(pieces[j], ('seq', 'exp'), [(s * parts + e, (s ^ block) * pa...  3.74 us
    ppermute x1, starting transfers between devices, per_device(): partner = lax.ppermute(given, 'seq', swap)  3 us
    ppermute x3, waiting for transfers between devices, per_device(): lax.ppermute(ready[j], 'exp', [(i, i ^ j) for i in range(parts)])  2.52 us
  transfers between devices with their start and end apart: 31, of which 16 were waited for; matrix products, arithmetic and copies ran while one was open for 1% of the time, Pallas kernels for 10%

profile of v3, /device:TPU:0, one launch (start us, length us, event | category | flops | bytes accessed | tf_op | source)
XLA Modules:
  0.0 89.2 jit_solution(16728560367303352658)
XLA Ops:
  0.0 0.1 pad_add_fusion.scalars
  0.1 2.3 %shard_map.102 = (bf16[128,256]{1,0:T(8,128)(2,1)S(1)}, bf16[128,256]{1,0:T(8,128)(2,1)S(1)}) custom-call(s32[4]{0:T(128)S(1)} %pad_add_fusion.scalars, bf16[128,512]{1,0:T(8,128)(2,1)} %key_ref.3, bf16[128,512]{1,0:T(8,128)(2,1)} %value_ref.3), custom_call_target="tpu_custom_call" | custom-call | flops 16777216 | bytes 393232 | tf_op jit(solution)/shard_map/pallas_call | solution.py:24
  2.4 3.0 %collective-permute-start.1 = (bf16[128,256]{1,0:T(8,128)(2,1)S(1)}, bf16[128,256]{1,0:T(8,128)(2,1)S(1)}, u32[]{:S(2)}, u32[]{:S(2)}) collective-permute-start(bf16[128,256]{1,0:T(8,128)(2,1)S(1)} %get-tuple-element.39), channel_id=1, source_target_pairs={{0,4},{4,0},{8,12},{12,8},{16,20},{20,16},{24,28},{28,24},{1,5},{5... | collective-permute-start | bytes 196616 | tf_op jit(solution)/shard_map/ppermute | solution.py:412
  5.4 1.5 %shard_map.100 = bf16[128,1024]{1,0:T(8,128)(2,1)S(1)} custom-call(s32[4]{0:T(128)S(1)} %pad_add_fusion.scalars, bf16[128,512]{1,0:T(8,128)(2,1)} %key_ref.3, bf16[128,512]{1,0:T(8,128)(2,1)} %value_ref.3, bf16[128,512]{1,0:T(8,128)(2,1)} %query_ref.1, bf16[128,512]{1,0:T(8,128)(2,1)} %residual_ref.1), custom_call_target="tpu_custom_call" | custom-call | bytes 786448 | tf_op jit(solution)/shard_map/pallas_call | solution.py:24
  6.9 0.1 collective-permute-start
  7.0 0.1 constant_dynamic-slice_fusion.1
  7.0 0.8 constant_dynamic-slice_fusion
  7.8 6.0 %collective-permute-start.4 = (bf16[128,256]{1,0:T(8,128)(2,1)S(1)}, bf16[128,256]{1,0:T(8,128)(2,1)S(1)}, u32[]{:S(2)}, u32[]{:S(2)}) collective-permute-start(bf16[128,256]{1,0:T(8,128)(2,1)S(1)} %add_convert_fusion.6), channel_id=1, source_target_pairs={{0,24},{4,28},{1,25},{5,29},{2,26},{6,30},{3,27},{7,31}} | collective-permute-start | bytes 196616 | tf_op jit(solution)/shard_map/ppermute | solution.py:368
  13.9 1.3 %collective-permute-start.3 = (bf16[128,256]{1,0:T(8,128)(2,1)S(1)}, bf16[128,256]{1,0:T(8,128)(2,1)S(1)}, u32[]{:S(2)}, u32[]{:S(2)}) collective-permute-start(bf16[128,256]{1,0:T(8,128)(2,1)S(1)} %add_convert_fusion.6), channel_id=1, source_target_pairs={{0,16},{4,20},{8,24},{12,28},{1,17},{5,21},{9,25},{13,29},{2,18},{... | collective-permute-start | bytes 196616 | tf_op jit(solution)/shard_map/ppermute | solution.py:368
  15.2 2.5 %collective-permute-start.2 = (bf16[128,256]{1,0:T(8,128)(2,1)S(1)}, bf16[128,256]{1,0:T(8,128)(2,1)S(1)}, u32[]{:S(2)}, u32[]{:S(2)}) collective-permute-start(bf16[128,256]{1,0:T(8,128)(2,1)S(1)} %add_convert_fusion.6), channel_id=1, source_target_pairs={{0,8},{4,12},{8,16},{12,20},{16,24},{20,28},{1,9},{5,13},{9,17},{1... | collective-permute-start | bytes 196616 | tf_op jit(solution)/shard_map/ppermute | solution.py:368
  17.7 0.1 copy.16
  17.7 0.1 copy.15
  17.8 5.2 %shard_map.103 = (bf16[2,2048,1024]{2,1,0:T(8,128)(2,1)S(1)}, bf16[1,1024,2048]{2,1,0:T(8,128)(2,1)S(1)}, f32[8,128]{1,0:T(8,128)S(1)}) custom-call(s32[4]{0:T(128)S(1)} %pad_add_fusion.scalars, bf16[2,2048,1024]{2,1,0:T(8,128)(2,1)} %bitcast.6, bf16[1,1024,2048]{2,1,0:T(8,128)(2,1)} %out_ref.1, bf16[128,256]{1,0:T(8,128)(2,1)S(1)} %collective-permute-done.1.after_ref.partner_ref), custom_call_target="tpu_custom_call" | custom-call | bytes 25235472 | tf_op jit(solution)/shard_map/pallas_call | solution.py:24
  23.1 1.9 %shard_map.101 = (f32[2,128,256]{2,1,0:T(8,128)S(1)}, bf16[128,256]{1,0:T(8,128)(2,1)S(1)}, bf16[128,256]{1,0:T(8,128)(2,1)S(1)}, f32[1,256]{1,0:T(1,128)S(1)}, f32[1,2048]{1,0:T(1,128)S(1)}) custom-call(s32[4]{0:T(128)S(1)} %pad_add_fusion.scalars, bf16[128,512]{1,0:T(8,128)(2,1)} %key_ref.3, bf16[128,512]{1,0:T(8,128)(2,1)} %value_ref.3, ...), custom_call_target="tpu_custom_call" | custom-call | flops 50331648 | bytes 1199120 | tf_op jit(solution)/shard_map/pallas_call | solution.py:24
  25.0 0.0 collective-permute-done.4.refs_2_
  25.1 0.9 %shard_map.104 = (bf16[32,256]{1,0:T(8,128)(2,1)S(1)}, bf16[32,256]{1,0:T(8,128)(2,1)S(1)}, bf16[32,256]{1,0:T(8,128)(2,1)S(1)}, bf16[32,256]{1,0:T(8,128)(2,1)S...) custom-call(s32[4]{0:T(128)S(1)} %pad_add_fusion.scalars, ...), custom_call_target="tpu_custom_call" | custom-call | flops 33554432 | bytes 1119248 | tf_op jit(solution)/shard_map/pallas_call | solution.py:24
  26.0 0.1 collective-permute-start.5
  26.1 1.6 %collective-permute-start.6 = (bf16[32,256]{1,0:T(8,128)(2,1)S(1)}, bf16[32,256]{1,0:T(8,128)(2,1)S(1)}, u32[]{:S(2)}, u32[]{:S(2)}) collective-permute-start(bf16[32,256]{1,0:T(8,128)(2,1)S(1)} %get-tuple-element.48), channel_id=1, source_target_pairs={{0,2},{1,3},{2,0},{3,1},{4,6},{5,7},{6,4},{7,5},{8,10},{9,11},{10,... | collective-permute-start | bytes 49160 | tf_op jit(solution)/shard_map/ppermute | solution.py:453
  27.7 0.3 collective-permute-start.7
  27.9 1.5 %collective-permute-start.8 = (bf16[32,256]{1,0:T(8,128)(2,1)S(1)}, bf16[32,256]{1,0:T(8,128)(2,1)S(1)}, u32[]{:S(2)}, u32[]{:S(2)}) collective-permute-start(bf16[32,256]{1,0:T(8,128)(2,1)S(1)} %get-tuple-element.50), channel_id=1, source_target_pairs={{0,4},{1,5},{2,6},{3,7},{4,0},{5,1},{6,2},{7,3},{8,12},{9,13},{10,... | collective-permute-start | bytes 49160 | tf_op jit(solution)/shard_map/ppermute | solution.py:453
  29.4 0.2 collective-permute-start.9
  29.6 2.5 %collective-permute-start.10 = (bf16[32,256]{1,0:T(8,128)(2,1)S(1)}, bf16[32,256]{1,0:T(8,128)(2,1)S(1)}, u32[]{:S(2)}, u32[]{:S(2)}) collective-permute-start(bf16[32,256]{1,0:T(8,128)(2,1)S(1)} %get-tuple-element.52), channel_id=1, source_target_pairs={{0,6},{1,7},{2,4},{3,5},{4,2},{5,3},{6,0},{7,1},{8,14},{9,15},{10,... | collective-permute-start | bytes 49160 | tf_op jit(solution)/shard_map/ppermute | solution.py:453
  32.1 0.2 collective-permute-start.11
  32.3 0.1 fusion.2.pack_ref
  32.4 0.2 collective-permute-done.9.refs_5_
  32.6 1.7 %collective-permute-done.10.refs_6_ = bf16[32,256]{1,0:T(8,128)(2,1)S(1)} collective-permute-done((bf16[32,256]{1,0:T(8,128)(2,1)S(1)}, bf16[32,256]{1,0:T(8,128)(2,1)S(1)}, u32[]{:S(2)}, u32[]{:S(2)}) %collective-permute-start.10) | collective-permute-done | bytes 16416 | tf_op jit(solution)/shard_map/ppermute | solution.py:453
  34.3 1.9 %collective-permute-done.11.refs_7_ = bf16[32,256]{1,0:T(8,128)(2,1)S(1)} collective-permute-done((bf16[32,256]{1,0:T(8,128)(2,1)S(1)}, bf16[32,256]{1,0:T(8,128)(2,1)S(1)}, u32[]{:S(2)}, u32[]{:S(2)}) %collective-permute-start.11) | collective-permute-done | bytes 16416 | tf_op jit(solution)/shard_map/ppermute | solution.py:453
  36.2 0.7 shard_map.105
  36.9 0.6 collective-permute-start.15
  37.4 1.5 %collective-permute-start.12 = (bf16[32,2176]{1,0:T(8,128)(2,1)S(1)}, bf16[32,2176]{1,0:T(8,128)(2,1)S(1)}, u32[]{:S(2)}, u32[]{:S(2)}) collective-permute-start(bf16[32,2176]{1,0:T(8,128)(2,1)S(1)} %get-tuple-element.57.refs_0_), channel_id=1, source_target_pairs={{0,8},{8,16},{16,24},{24,28},{28,20},{20,12},{12,4},{4,0},{1,9},{9... | collective-permute-start | bytes 417800 | tf_op jit(solution)/shard_map/ppermute | solution.py:265
  38.9 3.7 %collective-permute-done.15.refs_4_ = bf16[32,2176]{1,0:T(8,128)(2,1)S(1)} collective-permute-done((bf16[32,2176]{1,0:T(8,128)(2,1)S(1)}, bf16[32,2176]{1,0:T(8,128)(2,1)S(1)}, u32[]{:S(2)}, u32[]{:S(2)}) %collective-permute-start.15) | collective-permute-done | bytes 139296 | tf_op jit(solution)/shard_map/ppermute | solution.py:265
  42.6 0.5 collective-permute-start.16
  43.2 1.5 %collective-permute-start.13 = (bf16[32,2176]{1,0:T(8,128)(2,1)S(1)}, bf16[32,2176]{1,0:T(8,128)(2,1)S(1)}, u32[]{:S(2)}, u32[]{:S(2)}) collective-permute-start(bf16[32,2176]{1,0:T(8,128)(2,1)S(1)} %collective-permute-done.12.refs_1_), channel_id=1, source_target_pairs={{0,8},{8,16},{16,24},{24,28},{28,20},{20,12},{12,4},{4,0},{1,9},{9... | collective-permute-start | bytes 417800 | tf_op jit(solution)/shard_map/ppermute | solution.py:265
  44.7 3.0 %collective-permute-done.16.refs_5_ = bf16[32,2176]{1,0:T(8,128)(2,1)S(1)} collective-permute-done((bf16[32,2176]{1,0:T(8,128)(2,1)S(1)}, bf16[32,2176]{1,0:T(8,128)(2,1)S(1)}, u32[]{:S(2)}, u32[]{:S(2)}) %collective-permute-start.16) | collective-permute-done | bytes 139296 | tf_op jit(solution)/shard_map/ppermute | solution.py:265
  47.7 0.5 collective-permute-start.17
  48.2 0.0 collective-permute-done.13.refs_2_
  48.2 1.5 %collective-permute-start.14 = (bf16[32,2176]{1,0:T(8,128)(2,1)S(1)}, bf16[32,2176]{1,0:T(8,128)(2,1)S(1)}, u32[]{:S(2)}, u32[]{:S(2)}) collective-permute-start(bf16[32,2176]{1,0:T(8,128)(2,1)S(1)} %collective-permute-done.13.refs_2_), channel_id=1, source_target_pairs={{0,8},{8,16},{16,24},{24,28},{28,20},{20,12},{12,4},{4,0},{1,9},{9... | collective-permute-start | bytes 417800 | tf_op jit(solution)/shard_map/ppermute | solution.py:265
  49.7 0.4 collective-permute-start.19
  50.2 2.5 %collective-permute-start.18 = (bf16[16,2176]{1,0:T(8,128)(2,1)S(1)}, bf16[16,2176]{1,0:T(8,128)(2,1)S(1)}, u32[]{:S(2)}, u32[]{:S(2)}) collective-permute-start(bf16[16,2176]{1,0:T(8,128)(2,1)S(1)} %slice.40), channel_id=1, source_target_pairs={{0,16},{8,24},{16,28},{24,20},{28,12},{20,4},{12,0},{4,8},{1,17},{... | collective-permute-start | bytes 208904 | tf_op jit(solution)/shard_map/ppermute | solution.py:265
  52.7 2.5 %collective-permute-done.19.refs_8_ = bf16[16,2176]{1,0:T(8,128)(2,1)S(1)} collective-permute-done((bf16[16,2176]{1,0:T(8,128)(2,1)S(1)}, bf16[16,2176]{1,0:T(8,128)(2,1)S(1)}, u32[]{:S(2)}, u32[]{:S(2)}) %collective-permute-start.19) | collective-permute-done | bytes 69664 | tf_op jit(solution)/shard_map/ppermute | solution.py:265
  55.2 0.8 collective-permute-done.18.refs_7_
  56.0 5.5 %shard_map.106 = (bf16[32,2048]{1,0:T(8,128)(2,1)S(1)}, bf16[32,2048]{1,0:T(8,128)(2,1)S(1)}, bf16[32,2048]{1,0:T(8,128)(2,1)S(1)}, bf16[32,2048]{1,0:T(8,128)(2...) custom-call(s32[4]{0:T(128)S(1)} %pad_add_fusion.scalars, ...), custom_call_target="tpu_custom_call" | custom-call | flops 3221225472 | bytes 14745616 | tf_op jit(solution)/shard_map/pallas_call | solution.py:24
  61.6 1.0 %collective-permute-start.20 = (bf16[32,2048]{1,0:T(8,128)(2,1)S(1)}, bf16[32,2048]{1,0:T(8,128)(2,1)S(1)}, u32[]{:S(2)}, u32[]{:S(2)}) collective-permute-start(bf16[32,2048]{1,0:T(8,128)(2,1)S(1)} %get-tuple-element.59), channel_id=1, source_target_pairs={{0,8},{8,16},{16,24},{24,28},{28,20},{20,12},{12,4},{4,0},{1,9},{9... | collective-permute-start | bytes 393224 | tf_op jit(solution)/shard_map/ppermute | solution.py:265
  62.5 1.0 %collective-permute-start.21 = (bf16[16,2048]{1,0:T(8,128)(2,1)S(1)}, bf16[16,2048]{1,0:T(8,128)(2,1)S(1)}, u32[]{:S(2)}, u32[]{:S(2)}) collective-permute-start(bf16[16,2048]{1,0:T(8,128)(2,1)S(1)} %get-tuple-element.61), channel_id=1, source_target_pairs={{0,16},{8,24},{16,28},{24,20},{28,12},{20,4},{12,0},{4,8},{1,17},{... | collective-permute-start | bytes 196616 | tf_op jit(solution)/shard_map/ppermute | solution.py:265
  63.5 1.9 %collective-permute-start.25 = (bf16[16,2048]{1,0:T(8,128)(2,1)S(1)}, bf16[16,2048]{1,0:T(8,128)(2,1)S(1)}, u32[]{:S(2)}, u32[]{:S(2)}) collective-permute-start(bf16[16,2048]{1,0:T(8,128)(2,1)S(1)} %get-tuple-element.65), channel_id=1, source_target_pairs={{0,12},{8,4},{16,0},{24,8},{28,16},{20,24},{12,28},{4,20},{1,13},{... | collective-permute-start | bytes 196616 | tf_op jit(solution)/shard_map/ppermute | solution.py:265
  65.5 1.1 %collective-permute-start.24 = (bf16[32,2048]{1,0:T(8,128)(2,1)S(1)}, bf16[32,2048]{1,0:T(8,128)(2,1)S(1)}, u32[]{:S(2)}, u32[]{:S(2)}) collective-permute-start(bf16[32,2048]{1,0:T(8,128)(2,1)S(1)} %get-tuple-element.63), channel_id=1, source_target_pairs={{0,4},{8,0},{16,8},{24,16},{28,24},{20,28},{12,20},{4,12},{1,5},{9... | collective-permute-start | bytes 393224 | tf_op jit(solution)/shard_map/ppermute | solution.py:265
  66.6 1.3 %collective-permute-done.21 = bf16[16,2048]{1,0:T(8,128)(2,1)S(1)} collective-permute-done((bf16[16,2048]{1,0:T(8,128)(2,1)S(1)}, bf16[16,2048]{1,0:T(8,128)(2,1)S(1)}, u32[]{:S(2)}, u32[]{:S(2)}) %collective-permute-start.21) | collective-permute-done | bytes 65568 | tf_op jit(solution)/shard_map/ppermute | solution.py:265
  68.0 1.4 %collective-permute-start.22 = (bf16[32,2048]{1,0:T(8,128)(2,1)S(1)}, bf16[32,2048]{1,0:T(8,128)(2,1)S(1)}, u32[]{:S(2)}, u32[]{:S(2)}) collective-permute-start(bf16[32,2048]{1,0:T(8,128)(2,1)S(1)} %pad_maximum_fusion), channel_id=1, source_target_pairs={{0,8},{8,16},{16,24},{24,28},{28,20},{20,12},{12,4},{4,0},{1,9},{9... | collective-permute-start | bytes 393224 | tf_op jit(solution)/shard_map/ppermute | solution.py:265
  69.3 0.1 collective-permute-done.25
  69.4 3.2 %collective-permute-done.24 = bf16[32,2048]{1,0:T(8,128)(2,1)S(1)} collective-permute-done((bf16[32,2048]{1,0:T(8,128)(2,1)S(1)}, bf16[32,2048]{1,0:T(8,128)(2,1)S(1)}, u32[]{:S(2)}, u32[]{:S(2)}) %collective-permute-start.24) | collective-permute-done | bytes 131104 | tf_op jit(solution)/shard_map/ppermute | solution.py:265
  72.7 0.9 collective-permute-start.26
  73.6 1.0 %collective-permute-done.22 = bf16[32,2048]{1,0:T(8,128)(2,1)S(1)} collective-permute-done((bf16[32,2048]{1,0:T(8,128)(2,1)S(1)}, bf16[32,2048]{1,0:T(8,128)(2,1)S(1)}, u32[]{:S(2)}, u32[]{:S(2)}) %collective-permute-start.22) | collective-permute-done | bytes 131104 | tf_op jit(solution)/shard_map/ppermute | solution.py:265
  74.6 0.9 %collective-permute-start.23 = (bf16[32,2048]{1,0:T(8,128)(2,1)S(1)}, bf16[32,2048]{1,0:T(8,128)(2,1)S(1)}, u32[]{:S(2)}, u32[]{:S(2)}) collective-permute-start(bf16[32,2048]{1,0:T(8,128)(2,1)S(1)} %add_convert_fusion.1), channel_id=1, source_target_pairs={{0,8},{8,16},{16,24},{24,28},{28,20},{20,12},{12,4},{4,0},{1,9},{9... | collective-permute-start | bytes 393224 | tf_op jit(solution)/shard_map/ppermute | solution.py:265
  75.5 2.3 %collective-permute-done.26 = bf16[32,2048]{1,0:T(8,128)(2,1)S(1)} collective-permute-done((bf16[32,2048]{1,0:T(8,128)(2,1)S(1)}, bf16[32,2048]{1,0:T(8,128)(2,1)S(1)}, u32[]{:S(2)}, u32[]{:S(2)}) %collective-permute-start.26) | collective-permute-done | bytes 131104 | tf_op jit(solution)/shard_map/ppermute | solution.py:265
  77.9 1.2 %collective-permute-start.27 = (bf16[32,2048]{1,0:T(8,128)(2,1)S(1)}, bf16[32,2048]{1,0:T(8,128)(2,1)S(1)}, u32[]{:S(2)}, u32[]{:S(2)}) collective-permute-start(bf16[32,2048]{1,0:T(8,128)(2,1)S(1)} %add_convert_fusion), channel_id=1, source_target_pairs={{0,4},{8,0},{16,8},{24,16},{28,24},{20,28},{12,20},{4,12},{1,5},{9... | collective-permute-start | bytes 393224 | tf_op jit(solution)/shard_map/ppermute | solution.py:265
  79.1 0.5 collective-permute-done.23.b_ref
  79.6 3.3 %collective-permute-done.27.c_ref = bf16[32,2048]{1,0:T(8,128)(2,1)S(1)} collective-permute-done((bf16[32,2048]{1,0:T(8,128)(2,1)S(1)}, bf16[32,2048]{1,0:T(8,128)(2,1)S(1)}, u32[]{:S(2)}, u32[]{:S(2)}) %collective-permute-start.27) | collective-permute-done | bytes 131104 | tf_op jit(solution)/shard_map/ppermute | solution.py:265
  82.9 0.6 shard_map.107
  83.5 0.1 collective-permute-start.28
  83.6 0.7 collective-permute-start.29
  84.3 1.2 %collective-permute-start.30 = (bf16[32,512]{1,0:T(8,128)(2,1)S(1)}, bf16[32,512]{1,0:T(8,128)(2,1)S(1)}, u32[]{:S(2)}, u32[]{:S(2)}) collective-permute-start(bf16[32,512]{1,0:T(8,128)(2,1)S(1)} %get-tuple-element.70), channel_id=1, source_target_pairs={{0,3},{1,2},{2,1},{3,0},{4,7},{5,6},{6,5},{7,4},{8,11},{9,10},{10,... | collective-permute-start | bytes 98312 | tf_op jit(solution)/shard_map/ppermute | solution.py:494
  85.5 2.4 %collective-permute-done.29.refs_2_ = bf16[32,512]{1,0:T(8,128)(2,1)S(1)} collective-permute-done((bf16[32,512]{1,0:T(8,128)(2,1)S(1)}, bf16[32,512]{1,0:T(8,128)(2,1)S(1)}, u32[]{:S(2)}, u32[]{:S(2)}) %collective-permute-start.29) | collective-permute-done | bytes 32800 | tf_op jit(solution)/shard_map/ppermute | solution.py:494
  87.9 0.1 collective-permute-done.30.refs_3_
  88.0 1.2 %shard_map.108 = bf16[128,512]{1,0:T(8,128)(2,1)} custom-call(s32[4]{0:T(128)S(1)} %pad_add_fusion.scalars, bf16[32,512]{1,0:T(8,128)(2,1)S(1)} %get-tuple-element.67.refs_0_, bf16[32,512]{1,0:T(8,128)(2,1)S(1)} %collective-permute-done.28.refs_1_, bf16[32,512]{1,0:T(8,128)(2,1)S(1)} %collective-permute-done.29.refs_2_, ...), custom_call_target="tpu_custom_call" | custom-call | bytes 262160 | tf_op jit(solution)/shard_map/pallas_call | solution.py:24
  (27 shorter events, 0.3 us)
Async XLA Ops:
  0.0 7.0 %copy-start = (s32[128,8]{0,1:T(8,128)S(1)}, s32[128,8]{0,1:T(8,128)}, u32[]{:S(2)}) copy-start(s32[128,8]{0,1:T(8,128)} %param.16) | copy-start | bytes 12292
  2.4 5.5 %collective-permute-start.1 = (bf16[128,256]{1,0:T(8,128)(2,1)S(1)}, bf16[128,256]{1,0:T(8,128)(2,1)S(1)}, u32[]{:S(2)}, u32[]{:S(2)}) collective-permute-start(bf16[128,256]{1,0:T(8,128)(2,1)S(1)} %get-tuple-element.39), channel_id=1, source_target_pairs={{0,4},{4,0},{8,12},{12,8},{16,20},{20,16},{24,28},{28,24},{1,5},{5... | collective-permute-start | bytes 196616 | tf_op jit(solution)/shard_map/ppermute | solution.py:412
  6.9 16.2 %collective-permute-start = (bf16[128,1024]{1,0:T(8,128)(2,1)S(1)}, bf16[128,1024]{1,0:T(8,128)(2,1)S(1)}, u32[]{:S(2)}, u32[]{:S(2)}) collective-permute-start(bf16[128,1024]{1,0:T(8,128)(2,1)S(1)} %shard_map.100), channel_id=1, source_target_pairs={{0,4},{4,0},{8,12},{12,8},{16,20},{20,16},{24,28},{28,24},{1,5},{5... | collective-permute-start | bytes 786440 | tf_op jit(solution)/shard_map/ppermute | solution.py:418
  7.8 17.2 %collective-permute-start.4 = (bf16[128,256]{1,0:T(8,128)(2,1)S(1)}, bf16[128,256]{1,0:T(8,128)(2,1)S(1)}, u32[]{:S(2)}, u32[]{:S(2)}) collective-permute-start(bf16[128,256]{1,0:T(8,128)(2,1)S(1)} %add_convert_fusion.6), channel_id=1, source_target_pairs={{0,24},{4,28},{1,25},{5,29},{2,26},{6,30},{3,27},{7,31}} | collective-permute-start | bytes 196616 | tf_op jit(solution)/shard_map/ppermute | solution.py:368
  13.9 11.2 %collective-permute-start.3 = (bf16[128,256]{1,0:T(8,128)(2,1)S(1)}, bf16[128,256]{1,0:T(8,128)(2,1)S(1)}, u32[]{:S(2)}, u32[]{:S(2)}) collective-permute-start(bf16[128,256]{1,0:T(8,128)(2,1)S(1)} %add_convert_fusion.6), channel_id=1, source_target_pairs={{0,16},{4,20},{8,24},{12,28},{1,17},{5,21},{9,25},{13,29},{2,18},{... | collective-permute-start | bytes 196616 | tf_op jit(solution)/shard_map/ppermute | solution.py:368
  15.2 9.9 %collective-permute-start.2 = (bf16[128,256]{1,0:T(8,128)(2,1)S(1)}, bf16[128,256]{1,0:T(8,128)(2,1)S(1)}, u32[]{:S(2)}, u32[]{:S(2)}) collective-permute-start(bf16[128,256]{1,0:T(8,128)(2,1)S(1)} %add_convert_fusion.6), channel_id=1, source_target_pairs={{0,8},{4,12},{8,16},{12,20},{16,24},{20,28},{1,9},{5,13},{9,17},{1... | collective-permute-start | bytes 196616 | tf_op jit(solution)/shard_map/ppermute | solution.py:368
  26.0 3.6 %collective-permute-start.5 = (bf16[32,256]{1,0:T(8,128)(2,1)S(1)}, bf16[32,256]{1,0:T(8,128)(2,1)S(1)}, u32[]{:S(2)}, u32[]{:S(2)}) collective-permute-start(bf16[32,256]{1,0:T(8,128)(2,1)S(1)} %get-tuple-element.47), channel_id=1, source_target_pairs={{0,1},{1,0},{2,3},{3,2},{4,5},{5,4},{6,7},{7,6},{8,9},{9,8},{10,11... | collective-permute-start | bytes 49160 | tf_op jit(solution)/shard_map/ppermute | solution.py:453
  26.1 6.0 %collective-permute-start.6 = (bf16[32,256]{1,0:T(8,128)(2,1)S(1)}, bf16[32,256]{1,0:T(8,128)(2,1)S(1)}, u32[]{:S(2)}, u32[]{:S(2)}) collective-permute-start(bf16[32,256]{1,0:T(8,128)(2,1)S(1)} %get-tuple-element.48), channel_id=1, source_target_pairs={{0,2},{1,3},{2,0},{3,1},{4,6},{5,7},{6,4},{7,5},{8,10},{9,11},{10,... | collective-permute-start | bytes 49160 | tf_op jit(solution)/shard_map/ppermute | solution.py:453
  27.7 4.8 %collective-permute-start.7 = (bf16[32,256]{1,0:T(8,128)(2,1)S(1)}, bf16[32,256]{1,0:T(8,128)(2,1)S(1)}, u32[]{:S(2)}, u32[]{:S(2)}) collective-permute-start(bf16[32,256]{1,0:T(8,128)(2,1)S(1)} %get-tuple-element.49), channel_id=1, source_target_pairs={{0,3},{1,2},{2,1},{3,0},{4,7},{5,6},{6,5},{7,4},{8,11},{9,10},{10,... | collective-permute-start | bytes 49160 | tf_op jit(solution)/shard_map/ppermute | solution.py:453
  27.9 4.5 %collective-permute-start.8 = (bf16[32,256]{1,0:T(8,128)(2,1)S(1)}, bf16[32,256]{1,0:T(8,128)(2,1)S(1)}, u32[]{:S(2)}, u32[]{:S(2)}) collective-permute-start(bf16[32,256]{1,0:T(8,128)(2,1)S(1)} %get-tuple-element.50), channel_id=1, source_target_pairs={{0,4},{1,5},{2,6},{3,7},{4,0},{5,1},{6,2},{7,3},{8,12},{9,13},{10,... | collective-permute-start | bytes 49160 | tf_op jit(solution)/shard_map/ppermute | solution.py:453
  29.4 3.2 %collective-permute-start.9 = (bf16[32,256]{1,0:T(8,128)(2,1)S(1)}, bf16[32,256]{1,0:T(8,128)(2,1)S(1)}, u32[]{:S(2)}, u32[]{:S(2)}) collective-permute-start(bf16[32,256]{1,0:T(8,128)(2,1)S(1)} %get-tuple-element.51), channel_id=1, source_target_pairs={{0,5},{1,4},{2,7},{3,6},{4,1},{5,0},{6,3},{7,2},{8,13},{9,12},{10,... | collective-permute-start | bytes 49160 | tf_op jit(solution)/shard_map/ppermute | solution.py:453
  29.6 4.6 %collective-permute-start.10 = (bf16[32,256]{1,0:T(8,128)(2,1)S(1)}, bf16[32,256]{1,0:T(8,128)(2,1)S(1)}, u32[]{:S(2)}, u32[]{:S(2)}) collective-permute-start(bf16[32,256]{1,0:T(8,128)(2,1)S(1)} %get-tuple-element.52), channel_id=1, source_target_pairs={{0,6},{1,7},{2,4},{3,5},{4,2},{5,3},{6,0},{7,1},{8,14},{9,15},{10,... | collective-permute-start | bytes 49160 | tf_op jit(solution)/shard_map/ppermute | solution.py:453
  32.1 4.1 %collective-permute-start.11 = (bf16[32,256]{1,0:T(8,128)(2,1)S(1)}, bf16[32,256]{1,0:T(8,128)(2,1)S(1)}, u32[]{:S(2)}, u32[]{:S(2)}) collective-permute-start(bf16[32,256]{1,0:T(8,128)(2,1)S(1)} %get-tuple-element.53), channel_id=1, source_target_pairs={{0,7},{1,6},{2,5},{3,4},{4,3},{5,2},{6,1},{7,0},{8,15},{9,14},{10,... | collective-permute-start | bytes 49160 | tf_op jit(solution)/shard_map/ppermute | solution.py:453
  36.9 5.8 %collective-permute-start.15 = (bf16[32,2176]{1,0:T(8,128)(2,1)S(1)}, bf16[32,2176]{1,0:T(8,128)(2,1)S(1)}, u32[]{:S(2)}, u32[]{:S(2)}) collective-permute-start(bf16[32,2176]{1,0:T(8,128)(2,1)S(1)} %get-tuple-element.57.refs_0_), channel_id=1, source_target_pairs={{0,4},{8,0},{16,8},{24,16},{28,24},{20,28},{12,20},{4,12},{1,5},{9... | collective-permute-start | bytes 417800 | tf_op jit(solution)/shard_map/ppermute | solution.py:265
  37.4 5.7 %collective-permute-start.12 = (bf16[32,2176]{1,0:T(8,128)(2,1)S(1)}, bf16[32,2176]{1,0:T(8,128)(2,1)S(1)}, u32[]{:S(2)}, u32[]{:S(2)}) collective-permute-start(bf16[32,2176]{1,0:T(8,128)(2,1)S(1)} %get-tuple-element.57.refs_0_), channel_id=1, source_target_pairs={{0,8},{8,16},{16,24},{24,28},{28,20},{20,12},{12,4},{4,0},{1,9},{9... | collective-permute-start | bytes 417800 | tf_op jit(solution)/shard_map/ppermute | solution.py:265
  42.6 5.1 %collective-permute-start.16 = (bf16[32,2176]{1,0:T(8,128)(2,1)S(1)}, bf16[32,2176]{1,0:T(8,128)(2,1)S(1)}, u32[]{:S(2)}, u32[]{:S(2)}) collective-permute-start(bf16[32,2176]{1,0:T(8,128)(2,1)S(1)} %collective-permute-done.15.refs_4_), channel_id=1, source_target_pairs={{0,4},{8,0},{16,8},{24,16},{28,24},{20,28},{12,20},{4,12},{1,5},{9... | collective-permute-start | bytes 417800 | tf_op jit(solution)/shard_map/ppermute | solution.py:265
  43.2 5.1 %collective-permute-start.13 = (bf16[32,2176]{1,0:T(8,128)(2,1)S(1)}, bf16[32,2176]{1,0:T(8,128)(2,1)S(1)}, u32[]{:S(2)}, u32[]{:S(2)}) collective-permute-start(bf16[32,2176]{1,0:T(8,128)(2,1)S(1)} %collective-permute-done.12.refs_1_), channel_id=1, source_target_pairs={{0,8},{8,16},{16,24},{24,28},{28,20},{20,12},{12,4},{4,0},{1,9},{9... | collective-permute-start | bytes 417800 | tf_op jit(solution)/shard_map/ppermute | solution.py:265
  47.7 8.3 %collective-permute-start.17 = (bf16[32,2176]{1,0:T(8,128)(2,1)S(1)}, bf16[32,2176]{1,0:T(8,128)(2,1)S(1)}, u32[]{:S(2)}, u32[]{:S(2)}) collective-permute-start(bf16[32,2176]{1,0:T(8,128)(2,1)S(1)} %collective-permute-done.16.refs_5_), channel_id=1, source_target_pairs={{0,4},{8,0},{16,8},{24,16},{28,24},{20,28},{12,20},{4,12},{1,5},{9... | collective-permute-start | bytes 417800 | tf_op jit(solution)/shard_map/ppermute | solution.py:265
  48.2 7.8 %collective-permute-start.14 = (bf16[32,2176]{1,0:T(8,128)(2,1)S(1)}, bf16[32,2176]{1,0:T(8,128)(2,1)S(1)}, u32[]{:S(2)}, u32[]{:S(2)}) collective-permute-start(bf16[32,2176]{1,0:T(8,128)(2,1)S(1)} %collective-permute-done.13.refs_2_), channel_id=1, source_target_pairs={{0,8},{8,16},{16,24},{24,28},{28,20},{20,12},{12,4},{4,0},{1,9},{9... | collective-permute-start | bytes 417800 | tf_op jit(solution)/shard_map/ppermute | solution.py:265
  49.7 5.5 %collective-permute-start.19 = (bf16[16,2176]{1,0:T(8,128)(2,1)S(1)}, bf16[16,2176]{1,0:T(8,128)(2,1)S(1)}, u32[]{:S(2)}, u32[]{:S(2)}) collective-permute-start(bf16[16,2176]{1,0:T(8,128)(2,1)S(1)} %slice.41), channel_id=1, source_target_pairs={{0,12},{8,4},{16,0},{24,8},{28,16},{20,24},{12,28},{4,20},{1,13},{... | collective-permute-start | bytes 208904 | tf_op jit(solution)/shard_map/ppermute | solution.py:265
  50.2 5.9 %collective-permute-start.18 = (bf16[16,2176]{1,0:T(8,128)(2,1)S(1)}, bf16[16,2176]{1,0:T(8,128)(2,1)S(1)}, u32[]{:S(2)}, u32[]{:S(2)}) collective-permute-start(bf16[16,2176]{1,0:T(8,128)(2,1)S(1)} %slice.40), channel_id=1, source_target_pairs={{0,16},{8,24},{16,28},{24,20},{28,12},{20,4},{12,0},{4,8},{1,17},{... | collective-permute-start | bytes 208904 | tf_op jit(solution)/shard_map/ppermute | solution.py:265
  61.6 6.3 %collective-permute-start.20 = (bf16[32,2048]{1,0:T(8,128)(2,1)S(1)}, bf16[32,2048]{1,0:T(8,128)(2,1)S(1)}, u32[]{:S(2)}, u32[]{:S(2)}) collective-permute-start(bf16[32,2048]{1,0:T(8,128)(2,1)S(1)} %get-tuple-element.59), channel_id=1, source_target_pairs={{0,8},{8,16},{16,24},{24,28},{28,20},{20,12},{12,4},{4,0},{1,9},{9... | collective-permute-start | bytes 393224 | tf_op jit(solution)/shard_map/ppermute | solution.py:265
  62.5 5.4 %collective-permute-start.21 = (bf16[16,2048]{1,0:T(8,128)(2,1)S(1)}, bf16[16,2048]{1,0:T(8,128)(2,1)S(1)}, u32[]{:S(2)}, u32[]{:S(2)}) collective-permute-start(bf16[16,2048]{1,0:T(8,128)(2,1)S(1)} %get-tuple-element.61), channel_id=1, source_target_pairs={{0,16},{8,24},{16,28},{24,20},{28,12},{20,4},{12,0},{4,8},{1,17},{... | collective-permute-start | bytes 196616 | tf_op jit(solution)/shard_map/ppermute | solution.py:265
  63.5 5.9 %collective-permute-start.25 = (bf16[16,2048]{1,0:T(8,128)(2,1)S(1)}, bf16[16,2048]{1,0:T(8,128)(2,1)S(1)}, u32[]{:S(2)}, u32[]{:S(2)}) collective-permute-start(bf16[16,2048]{1,0:T(8,128)(2,1)S(1)} %get-tuple-element.65), channel_id=1, source_target_pairs={{0,12},{8,4},{16,0},{24,8},{28,16},{20,24},{12,28},{4,20},{1,13},{... | collective-permute-start | bytes 196616 | tf_op jit(solution)/shard_map/ppermute | solution.py:265
  65.5 7.2 %collective-permute-start.24 = (bf16[32,2048]{1,0:T(8,128)(2,1)S(1)}, bf16[32,2048]{1,0:T(8,128)(2,1)S(1)}, u32[]{:S(2)}, u32[]{:S(2)}) collective-permute-start(bf16[32,2048]{1,0:T(8,128)(2,1)S(1)} %get-tuple-element.63), channel_id=1, source_target_pairs={{0,4},{8,0},{16,8},{24,16},{28,24},{20,28},{12,20},{4,12},{1,5},{9... | collective-permute-start | bytes 393224 | tf_op jit(solution)/shard_map/ppermute | solution.py:265
  68.0 6.6 %collective-permute-start.22 = (bf16[32,2048]{1,0:T(8,128)(2,1)S(1)}, bf16[32,2048]{1,0:T(8,128)(2,1)S(1)}, u32[]{:S(2)}, u32[]{:S(2)}) collective-permute-start(bf16[32,2048]{1,0:T(8,128)(2,1)S(1)} %pad_maximum_fusion), channel_id=1, source_target_pairs={{0,8},{8,16},{16,24},{24,28},{28,20},{20,12},{12,4},{4,0},{1,9},{9... | collective-permute-start | bytes 393224 | tf_op jit(solution)/shard_map/ppermute | solution.py:265
  72.7 5.1 %collective-permute-start.26 = (bf16[32,2048]{1,0:T(8,128)(2,1)S(1)}, bf16[32,2048]{1,0:T(8,128)(2,1)S(1)}, u32[]{:S(2)}, u32[]{:S(2)}) collective-permute-start(bf16[32,2048]{1,0:T(8,128)(2,1)S(1)} %pad_maximum_fusion.1), channel_id=1, source_target_pairs={{0,4},{8,0},{16,8},{24,16},{28,24},{20,28},{12,20},{4,12},{1,5},{9... | collective-permute-start | bytes 393224 | tf_op jit(solution)/shard_map/ppermute | solution.py:265
  74.6 5.0 %collective-permute-start.23 = (bf16[32,2048]{1,0:T(8,128)(2,1)S(1)}, bf16[32,2048]{1,0:T(8,128)(2,1)S(1)}, u32[]{:S(2)}, u32[]{:S(2)}) collective-permute-start(bf16[32,2048]{1,0:T(8,128)(2,1)S(1)} %add_convert_fusion.1), channel_id=1, source_target_pairs={{0,8},{8,16},{16,24},{24,28},{28,20},{20,12},{12,4},{4,0},{1,9},{9... | collective-permute-start | bytes 393224 | tf_op jit(solution)/shard_map/ppermute | solution.py:265
  77.9 5.0 %collective-permute-start.27 = (bf16[32,2048]{1,0:T(8,128)(2,1)S(1)}, bf16[32,2048]{1,0:T(8,128)(2,1)S(1)}, u32[]{:S(2)}, u32[]{:S(2)}) collective-permute-start(bf16[32,2048]{1,0:T(8,128)(2,1)S(1)} %add_convert_fusion), channel_id=1, source_target_pairs={{0,4},{8,0},{16,8},{24,16},{28,24},{20,28},{12,20},{4,12},{1,5},{9... | collective-permute-start | bytes 393224 | tf_op jit(solution)/shard_map/ppermute | solution.py:265
  83.5 1.9 %collective-permute-start.28 = (bf16[32,512]{1,0:T(8,128)(2,1)S(1)}, bf16[32,512]{1,0:T(8,128)(2,1)S(1)}, u32[]{:S(2)}, u32[]{:S(2)}) collective-permute-start(bf16[32,512]{1,0:T(8,128)(2,1)S(1)} %get-tuple-element.68), channel_id=1, source_target_pairs={{0,1},{1,0},{2,3},{3,2},{4,5},{5,4},{6,7},{7,6},{8,9},{9,8},{10,11... | collective-permute-start | bytes 98312 | tf_op jit(solution)/shard_map/ppermute | solution.py:494
  83.6 4.3 %collective-permute-start.29 = (bf16[32,512]{1,0:T(8,128)(2,1)S(1)}, bf16[32,512]{1,0:T(8,128)(2,1)S(1)}, u32[]{:S(2)}, u32[]{:S(2)}) collective-permute-start(bf16[32,512]{1,0:T(8,128)(2,1)S(1)} %get-tuple-element.69), channel_id=1, source_target_pairs={{0,2},{1,3},{2,0},{3,1},{4,6},{5,7},{6,4},{7,5},{8,10},{9,11},{10,... | collective-permute-start | bytes 98312 | tf_op jit(solution)/shard_map/ppermute | solution.py:494
  84.3 3.7 %collective-permute-start.30 = (bf16[32,512]{1,0:T(8,128)(2,1)S(1)}, bf16[32,512]{1,0:T(8,128)(2,1)S(1)}, u32[]{:S(2)}, u32[]{:S(2)}) collective-permute-start(bf16[32,512]{1,0:T(8,128)(2,1)S(1)} %get-tuple-element.70), channel_id=1, source_target_pairs={{0,3},{1,2},{2,1},{3,0},{4,7},{5,6},{6,5},{7,4},{8,11},{9,10},{10,... | collective-permute-start | bytes 98312 | tf_op jit(solution)/shard_map/ppermute | solution.py:494

commit v4 on v2

v4 whole, which is shorter than its diff:
```python
import functools

import jax
import jax.numpy as jnp
from jax import lax
from jax.experimental import pallas as pl
from jax.experimental.pallas import tpu as pltpu
from jax.sharding import PartitionSpec as P

HEAD = 128
F32 = jnp.float32
BF16 = jnp.bfloat16
WHOLE = pl.BlockSpec(memory_space=pltpu.VMEM)
FAR = pl.BlockSpec(memory_space=pltpu.HBM)
SCALAR = pl.BlockSpec(memory_space=pltpu.SMEM)


def call(kernel, outs, inputs, far=(), small=(), scratch=(), out_specs=None, flops=0, limit=16 << 20):
    moved = sum(a.size * a.dtype.itemsize for a in [*inputs, *outs])
    inputs = [
        pltpu.with_memory_space_constraint(a, pltpu.HBM) if i in far else a
        for i, a in enumerate(inputs)
    ]
    return pl.pallas_call(
        kernel,
        out_shape=outs,
        in_specs=[
            SCALAR if i == 0 or i in small else FAR if i in far else WHOLE
            for i in range(len(inputs))
        ],
        out_specs=out_specs or [WHOLE] * len(outs),
        scratch_shapes=scratch,
        compiler_params=pltpu.CompilerParams(vmem_limit_bytes=limit),
        cost_estimate=pl.CostEstimate(flops=flops, bytes_accessed=moved, transcendentals=0),
    )(*inputs)


def shape(dims, dtype):
    return jax.ShapeDtypeStruct(dims, dtype)


def split(value):
    high = value.astype(BF16)
    return high, (value - high.astype(F32)).astype(BF16)


def add_rows(*terms):
    return sum(t.astype(F32) for t in terms).astype(BF16)


def run_copies(pairs, sems):
    copies = [pltpu.make_async_copy(a, b, sems.at[i]) for i, (a, b) in enumerate(pairs)]
    for copy in copies:
        copy.start()
    for copy in copies:
        copy.wait()


def open_kernel(
    scalars, key_ref, value_ref, query_ref, residual_ref, gain_ref, norm_ref,
    kept_ref, given_ref, theirs_ref, mine_ref, my_gain, my_norm, keys, values, sems
):
    rows, full = keys.shape
    width = full // 2
    place = scalars[1]
    my_cols = pl.ds(pl.multiple_of(place * width, width), width)
    their_cols = pl.ds(pl.multiple_of((1 - place) * width, width), width)
    pairs = [(key_ref, keys), (value_ref, values)]
    for i, ref in enumerate((key_ref, value_ref, query_ref, residual_ref)):
        spot = slice(i * width, (i + 1) * width)
        pairs.append((ref.at[:, their_cols], theirs_ref.at[:, spot]))
        pairs.append((ref.at[:, my_cols], mine_ref.at[:, spot]))
    pairs += [(gain_ref.at[:, my_cols], my_gain), (norm_ref, my_norm)]
    copies = [pltpu.make_async_copy(a, b, sems.at[i]) for i, (a, b) in enumerate(pairs)]
    for copy in copies:
        copy.start()
    for copy in copies[:2]:
        copy.wait()
    for h in range(full // HEAD):
        cols = slice(h * HEAD, (h + 1) * HEAD)
        state = lax.dot_general(
            keys[:, cols], values[:, cols], (((0,), (0,)), ((), ())), preferred_element_type=F32
        ).astype(BF16)
        half, inner = divmod(h * HEAD, width)

        @pl.when(place == half)
        def _():
            kept_ref[:, inner:inner + HEAD] = state

        @pl.when(place != half)
        def _():
            given_ref[:, inner:inner + HEAD] = state

    for copy in copies[2:]:
        copy.wait()


def within_kernel(scalars, mine_ref, came_ref, out_ref):
    rows, width = out_ref.shape[1:]
    causal = lax.broadcasted_iota(jnp.int32, (rows, rows), 0) >= lax.broadcasted_iota(
        jnp.int32, (rows, rows), 1
    )
    for block, ref in enumerate((mine_ref, came_ref)):
        for inner in range(0, width, HEAD):
            key, value, query = (
                ref[:, i * width + inner:i * width + inner + HEAD] for i in range(3)
            )
            scores = lax.dot_general(
                query, key, (((1,), (1,)), ((), ())), preferred_element_type=F32
            )
            high, low = split(jnp.where(causal, scores, 0.0))
            out_ref[block, :, inner:inner + HEAD] = jnp.dot(
                high, value, preferred_element_type=F32
            ) + jnp.dot(low, value, preferred_element_type=F32)


def attend_kernel(
    parts, earlier, scalars, within_ref, mine_ref, came_ref, my_gain, kept_ref, partner_ref, *refs
):
    before_refs, piece_refs, hidden = refs[:earlier], refs[earlier:-1], refs[-1]
    rows, width = hidden.shape[1:]
    before = sum(ref[...].astype(F32) for ref in before_refs)
    first = scalars[1] == 0
    for block, ref in enumerate((mine_ref, came_ref)):
        extra = (partner_ref if block == 0 else kept_ref)[...].astype(F32)
        use = jnp.logical_not(first) if block == 0 else first
        state = before + jnp.where(use, extra, 0.0)
        for inner in range(0, width, HEAD):
            cols = slice(inner, inner + HEAD)
            query, residual = (
                ref[:, i * width + inner:i * width + inner + HEAD] for i in (2, 3)
            )
            high, low = split(state[:, cols])
            raw = (
                jnp.dot(query, high, preferred_element_type=F32)
                + jnp.dot(query, low, preferred_element_type=F32)
                + within_ref[block, :, cols]
            )
            scaled = raw * lax.rsqrt(jnp.mean(raw * raw, axis=-1, keepdims=True) + 1e-06)
            hidden[block, :, cols] = (
                residual.astype(F32) + scaled * my_gain[:, cols]
            ).astype(BF16)
    count = rows // parts
    for j, piece in enumerate(piece_refs):
        rows_j = pl.ds(pl.multiple_of((scalars[0] ^ j) * count, count), count)
        for block in range(2):
            side = first if block == 0 else jnp.logical_not(first)

            @pl.when(side)
            def _():
                piece[:count, :] = hidden[block, rows_j, :]

            @pl.when(jnp.logical_not(side))
            def _():
                piece[count:, :] = hidden[block, rows_j, :]


def load_kernel(scalars, source, after_ref, target, done_ref, sems):
    done_ref[...] = jnp.zeros_like(done_ref)
    pieces = sems.shape[0]
    step = source.shape[0] // pieces
    run_copies(
        [
            (source.at[pl.ds(i * step, step)], target.at[pl.ds(i * step, step)])
            for i in range(pieces)
        ],
        sems,
    )


def load_near(scalars, source, after):
    return call(
        load_kernel, [shape(source.shape, source.dtype), shape((8, HEAD), F32)],
        [scalars, source, after], far=(1,), scratch=[pltpu.SemaphoreType.DMA((8,))],
    )


def expert_kernel(
    parts, far, scalars, sources, in_ref, down_ref, gain_ref, *refs
):
    count = 2 * far
    messages = refs[:count + 1]
    hidden_ref = refs[count + 1]
    out_refs = refs[count + 2:2 * count + 3]
    rows_ref, gates_ref, act_ref, made_ref = refs[2 * count + 3:]
    model = rows_ref.shape[1]
    width = model // (2 * parts)
    pair = messages[0].shape[0]
    half = pair // 2
    gates_ref[...] = jnp.zeros_like(gates_ref)
    for i, ref in enumerate(messages):
        source = sources[i]
        base = (source // 2) * pair + (half if i == count else 0)
        rows = pl.ds(pl.multiple_of(base, half), ref.shape[0])
        for j in range(parts):
            start = ((scalars[0] ^ j) * 2 + source % 2) * width
            cols = pl.ds(pl.multiple_of(start, width), width)
            rows_ref[rows, cols] = ref[:, j * width:(j + 1) * width]
        gates_ref[rows, :] += ref[:, parts * width:].astype(F32)
    hidden_ref[...] = rows_ref[pl.ds(pl.multiple_of(sources[0] * half, half), half), :]
    for s in range(count):
        rows = slice(s * half, (s + 1) * half)
        value = rows_ref[rows, :].astype(F32)
        scale = lax.rsqrt(jnp.mean(value * value, axis=-1, keepdims=True) + 1e-06)
        rows_ref[rows, :] = (value * scale * gain_ref[...]).astype(BF16)
    lane = lax.broadcasted_iota(jnp.int32, gates_ref.shape, 1)
    chosen = (lane == scalars[3]) | (lane == scalars[3] + scalars[2])
    weight = jnp.sum(jnp.where(chosen, gates_ref[...], 0.0), axis=-1, keepdims=True)

    units = in_ref.shape[1]
    chunk = min(units, 256)

    @pl.loop(0, units // chunk)
    def _(step):
        cut = pl.ds(pl.multiple_of(step * chunk, chunk), chunk)
        gate = jnp.dot(rows_ref[...], in_ref[:model, cut], preferred_element_type=F32)
        up = jnp.dot(rows_ref[...], in_ref[model:, cut], preferred_element_type=F32)
        act_ref[:, cut] = (gate / (1.0 + jnp.exp(-gate)) * up).astype(BF16)

    chunk = min(model, 512)

    @pl.loop(0, model // chunk)
    def _(step):
        cut = pl.ds(pl.multiple_of(step * chunk, chunk), chunk)
        produced = jnp.dot(act_ref[...], down_ref[:, cut], preferred_element_type=F32)
        made_ref[:, cut] = (produced.astype(BF16).astype(F32) * weight).astype(BF16)

    quarter = half // 2
    for i, out_ref in enumerate(out_refs):
        base = sources[i] * half + (quarter if i == count else 0)
        out_ref[...] = made_ref[pl.ds(pl.multiple_of(base, quarter), out_ref.shape[0]), :]


def run_expert(scalars, sources, messages, weights_in, weights_out, norm_gain):
    parts, far = lax.axis_size("exp"), lax.axis_size("seq") // 2
    units, model = weights_out.shape
    half = messages[0].shape[0] // 2
    total = 2 * far * half
    block, part = shape((half, model), BF16), shape((half // 2, model), BF16)
    return call(
        functools.partial(expert_kernel, parts, far),
        [block] + [block] * (2 * far - 1) + [part] * 2,
        [scalars, sources, weights_in, weights_out, norm_gain, *messages],
        small=(1,),
        scratch=[
            pltpu.VMEM((total, model), BF16),
            pltpu.VMEM((total, messages[0].shape[1] - model // 2), F32),
            pltpu.VMEM((total, units), BF16),
            pltpu.VMEM((total, model), BF16),
        ],
        flops=6 * total * model * units,
        limit=24 << 20,
    )


def ring_order(count):
    return list(range(0, count, 2)) + list(range(1, count, 2))[::-1]


def dense_experts(message, scalars, expert_in, expert_out, norm_gain):
    count = lax.axis_size("seq")
    order = ring_order(count)
    far = count // 2
    half = message.shape[0] // 2

    def hop(rows, steps):
        return lax.ppermute(
            rows, "seq", [(order[p], order[(p + steps) % count]) for p in range(count)]
        )

    reach = [0] + [-d for d in range(1, far)] + [d for d in range(1, far)] + [far, far]
    table = [[order[(order.index(s) + d) % count] for d in reach] for s in range(count)]
    sources = jnp.asarray(table, jnp.int32)[scalars[3]]

    weights = [expert_in.reshape(-1, expert_in.shape[-1]), expert_out]
    near, after = [], message
    forward, backward = [message], [message]
    for distance in range(1, far):
        ahead, behind = hop(forward[-1], 1), hop(backward[-1], -1)
        if weights:
            loaded, sign = load_near(scalars, weights.pop(0), after)
            near.append(loaded)
            ahead, behind, after = lax.optimization_barrier((ahead, behind, sign))
        forward.append(ahead)
        backward.append(behind)
    top = hop(forward[-2][:half], 2)
    bottom = hop(backward[-2][half:], -2)
    messages = [message] + forward[1:] + backward[1:] + [top, bottom]
    hidden, *made = run_expert(scalars, sources, messages, *near, norm_gain)
    own, to_back, to_front = made[0], made[1:far], made[far:2 * far - 1]
    top, bottom = made[-2:]
    half = half // 2
    early_going, early_coming = hop(bottom, 2), hop(top, -2)
    going, coming = hop(to_front[-1], 1), hop(to_back[-1], -1)
    for distance in range(far - 2, 0, -1):
        front, back = to_front[distance - 1], to_back[distance - 1]
        if distance == far - 2:
            going = jnp.concatenate(
                [
                    add_rows(going[:half], front[:half]),
                    add_rows(going[half:], front[half:], early_going),
                ]
            )
            coming = jnp.concatenate(
                [
                    add_rows(coming[:half], back[:half], early_coming),
                    add_rows(coming[half:], back[half:]),
                ]
            )
        else:
            going = add_rows(going, front)
            coming = add_rows(coming, back)
        going, coming = lax.optimization_barrier((going, coming))
        going, coming = hop(going, 1), hop(coming, -1)
    return hidden, own, going, coming


def mix_kernel(scalars, hidden_ref, a_ref, b_ref, c_ref, *out_refs):
    width = out_refs[0].shape[1]
    for j, out_ref in enumerate(out_refs):
        cols = pl.ds(pl.multiple_of((scalars[0] ^ j) * width, width), width)
        mixed = a_ref[:, cols].astype(F32) + b_ref[:, cols].astype(F32)
        mixed += c_ref[:, cols].astype(F32)
        out_ref[...] = (hidden_ref[:, cols].astype(F32) + mixed).astype(BF16)


def join_kernel(scalars, *refs):
    pieces, out_ref, sems = refs[:-2], refs[-2], refs[-1]
    count = pieces[0].shape[0]
    pairs = []
    for j, piece in enumerate(pieces):
        rows = pl.ds(pl.multiple_of((scalars[0] ^ j) * count, count), count)
        pairs.append((piece, out_ref.at[rows, :]))
    run_copies(pairs, sems)


def slot_ids(block_routes, expert_count, capacity):
    row_count, top_count = block_routes.shape
    expert_ids = jnp.arange(expert_count, dtype=jnp.int32)
    onehot = (
        (block_routes[:, :, None] == expert_ids[None, None, :])
        .astype(jnp.int32)
        .reshape(row_count * top_count, expert_count)
    )
    earlier = jnp.cumsum(onehot, axis=0) - onehot
    ranking = jnp.sum(earlier * onehot, axis=1).reshape(row_count, top_count)
    return block_routes * capacity + ranking


def routed_experts(normed, my_routes, my_gates, expert_in, expert_out):
    sub_count, model_width = normed.shape
    expert_count = lax.axis_size("seq") * expert_in.shape[0]
    top_count = my_routes.shape[1]
    capacity = min(sub_count, max(2, 3 * sub_count * top_count // (2 * expert_count)))
    slot_count = expert_count * capacity
    my_slots = slot_ids(my_routes, expert_count, capacity)
    columns = jnp.arange(slot_count, dtype=jnp.int32)
    placer = jnp.sum(
        (my_slots[None, :, :] == columns[:, None, None]).astype(jnp.int32), axis=2
    ).astype(BF16)
    outgoing = (
        jnp.dot(placer, normed, preferred_element_type=F32)
        .astype(BF16)
        .reshape(expert_count, capacity, model_width)
    )
    arrived = lax.all_to_all(outgoing, "seq", split_axis=0, concat_axis=0, tiled=True)
    flat_rows = arrived.reshape(-1, model_width)
    gate_up = jnp.einsum("nd,gdf->gnf", flat_rows, expert_in[0], preferred_element_type=F32)
    activated = (jax.nn.silu(gate_up[0]) * gate_up[1]).astype(BF16)
    produced = jnp.dot(activated, expert_out[0], preferred_element_type=F32).astype(BF16)
    answered = produced.reshape(arrived.shape)
    returned = lax.all_to_all(answered, "seq", split_axis=0, concat_axis=0, tiled=True)
    picked = returned.reshape(slot_count, model_width)[my_slots.reshape(-1)].reshape(
        sub_count, top_count, model_width
    )
    return jnp.sum(picked.astype(F32) * my_gates[:, :, None], axis=1)


def prior_states(kept, partner):
    count = lax.axis_size("seq")

    def pass_on(state, distance):
        return lax.ppermute(
            state, "seq", [(i, i + 2 * distance) for i in range(count - 2 * distance)]
        )

    pairs = count // 2
    running = add_rows(kept, partner)
    if pairs <= 4:
        return [pass_on(running, distance) for distance in reversed(range(1, pairs))]
    terms = []
    distance = 1
    while distance < pairs:
        terms.append(pass_on(running, distance))
        running = add_rows(running, terms[-1])
        distance *= 2
    return terms


def spread_rows(pieces):
    parts = len(pieces)
    bit = parts // 2
    held = {(j, 0): piece for j, piece in enumerate(pieces)}
    while bit:
        for (target, source), piece in list(held.items()):
            if target & bit:
                came = lax.ppermute(piece, "exp", [(i, i ^ bit) for i in range(parts)])
                held[(target ^ bit, source ^ bit)] = came
                del held[(target, source)]
        bit //= 2
    return [held[(0, j)] for j in range(parts)]


def own_rows(gathered, place, my_index, swap):
    parts = len(gathered)
    count, width = gathered[0].shape[0] // 2, gathered[0].shape[1]
    stacked = jnp.stack(gathered, axis=1).reshape(2, count, parts, width)
    mine = lax.dynamic_index_in_dim(stacked, place, 0, keepdims=False)
    other = lax.dynamic_index_in_dim(stacked, 1 - place, 0, keepdims=False)
    came = lax.ppermute(other, "seq", swap)
    both = jnp.where(
        place == 0, jnp.stack([mine, came], axis=2), jnp.stack([came, mine], axis=2)
    )
    index = my_index ^ jnp.arange(parts, dtype=jnp.int32)
    return jnp.take(both, index, axis=1).reshape(count, 2 * parts * width)


def per_device(
    residual,
    queries,
    key_vectors,
    value_vectors,
    head_gain,
    norm_gain,
    routes,
    route_gates,
    expert_in,
    expert_out,
):
    rows, width = residual.shape
    seq, parts = lax.axis_size("seq"), lax.axis_size("exp")
    count, half, model = rows // parts, width // 2, width * parts
    experts = seq * expert_in.shape[0]
    position = lax.axis_index("seq")
    my_index = lax.axis_index("exp")
    place = position % 2
    scalars = jnp.stack([my_index, place, experts, position]).astype(jnp.int32)
    swap = [(i, i ^ 1) for i in range(seq)]

    state, packed = shape((HEAD, half), BF16), shape((rows, 4 * half), BF16)
    kept, given, theirs, mine, my_gain, my_norm = call(
        open_kernel,
        [state, state, packed, packed, shape((1, half), F32), shape((1, model), F32)],
        [
            scalars, key_vectors, value_vectors, queries, residual, head_gain[None, :],
            norm_gain[None, :],
        ],
        far=(1, 2, 3, 4, 5, 6),
        scratch=[pltpu.VMEM((rows, width), BF16)] * 2 + [pltpu.SemaphoreType.DMA((12,))],
        flops=2 * rows * width * HEAD,
    )
    partner = lax.ppermute(given, "seq", swap)
    came = lax.ppermute(theirs, "seq", swap)
    before = prior_states(kept, partner)
    [within] = call(
        within_kernel, [shape((2, rows, half), F32)], [scalars, mine, came],
        flops=6 * rows * rows * width,
    )
    pieces = call(
        functools.partial(attend_kernel, parts, len(before)),
        [shape((2 * count, half), BF16)] * parts,
        [scalars, within, mine, came, my_gain, kept, partner, *before],
        scratch=[pltpu.VMEM((2, rows, half), BF16)],
        flops=4 * rows * width * HEAD,
    )
    gathered = spread_rows(pieces)

    my_routes = lax.dynamic_slice_in_dim(routes, my_index * count, count, 0)
    my_gates = lax.dynamic_slice_in_dim(route_gates, my_index * count, count, 0)
    if routes.shape[1] == experts:
        mixing = jnp.sum(
            jnp.where(
                my_routes[:, :, None] == jnp.arange(experts, dtype=jnp.int32),
                my_gates[:, :, None],
                0.0,
            ),
            axis=1,
        )
        mixing = jnp.concatenate(
            [jnp.where(place == 0, mixing, 0.0), jnp.where(place == 0, 0.0, mixing)]
        )
        high = lax.reduce_precision(mixing, 8, 7)
        lanes = -(-2 * experts // HEAD) * HEAD
        pack = jnp.pad(
            jnp.concatenate([high, mixing - high], axis=1), ((0, 0), (0, lanes - 2 * experts))
        ).astype(BF16)
        message = jnp.concatenate(gathered + [pack], axis=1)
        hidden, *terms = dense_experts(message, scalars, expert_in[0], expert_out[0], my_norm)
    else:
        hidden = own_rows(gathered, place, my_index, swap)
        widened = hidden.astype(F32)
        normed = (
            widened
            * lax.rsqrt(jnp.mean(widened * widened, axis=-1, keepdims=True) + 1e-06)
            * norm_gain
        ).astype(BF16)
        mixed = routed_experts(normed, my_routes, my_gates, expert_in, expert_out)
        nothing = jnp.zeros_like(mixed)
        terms = (mixed, nothing, nothing)
    ready = call(
        mix_kernel, [shape((count, width), BF16)] * parts, [scalars, hidden, *terms]
    )
    returned = [ready[0]] + [
        lax.ppermute(ready[j], "exp", [(i, i ^ j) for i in range(parts)])
        for j in range(1, parts)
    ]
    [out] = call(
        join_kernel, [shape((rows, width), BF16)], [scalars] + returned, out_specs=[FAR],
        scratch=[pltpu.SemaphoreType.DMA((parts,))],
    )
    return out


def solution(mesh):
    placed = (
        P("seq", "exp"),
        P("seq", "exp"),
        P("seq", "exp"),
        P("seq", "exp"),
        P("exp"),
        P(),
        P("seq", None),
        P("seq", None),
        P("seq", None, None, None),
        P("seq", None, None),
    )
    return jax.shard_map(
        per_device, mesh=mesh, in_specs=placed, out_specs=P("seq", "exp"), check_vma=False
    )
```

time: 93 us -> 93.7 us (level)
  local copies, waits for them, and re-layouts: 15.2 us -> 8.32 us
  Pallas kernels: 13.8 us -> 19.5 us
  waiting for transfers between devices: 23.8 us -> 28.7 us
  starting transfers between devices: 39 us -> 36.3 us
    unnamed x26 -> x10, local copies, waits for them, and re-layouts: 14.2 us -> 6.67 us
    pallas_call x9 -> x8, Pallas kernels: 13.8 us -> 19.5 us  [call(): pl.pallas_call(kernel, out_shape=outs, in_specs=[SCALAR if i == 0 or i in...]
    ppermute x8 -> x5, starting transfers between devices: 6.41 us -> 2.24 us  [the longest x4 2.16 us: spread_rows(): came = lax.ppermute(piece, 'exp', [(i, i ^ bit) for i in range(parts)])]
    ppermute x16, waiting for transfers between devices: 17.7 us -> 19.4 us  [hop(): lax.ppermute(rows, 'seq', [(order[p], order[(p + steps) % count]) for p i...]
    ppermute x1, waiting for transfers between devices: 0.01 us -> 1.48 us  [per_device(): partner = lax.ppermute(given, 'seq', swap)]
    ppermute x16, starting transfers between devices: 17.9 us -> 18.9 us  [hop(): lax.ppermute(rows, 'seq', [(order[p], order[(p + steps) % count]) for p i...]
    ppermute x8 -> x5, waiting for transfers between devices: 3.73 us -> 4.58 us  [the longest x4 4.58 us: spread_rows(): came = lax.ppermute(piece, 'exp', [(i, i ^ bit) for i in range(parts)])]
  transfers between devices with their start and end apart: 31 -> 28, of which waited for: 13 -> 15; matrix products, arithmetic and copies ran while one was open for 1% -> 2% of each run, Pallas kernels for 3% -> 9%
where the time goes in v4:
time: 93.7 us; the launch traced here: 93.4 us
  starting transfers between devices  36.3 us (39%)
  waiting for transfers between devices  28.7 us (31%)
  Pallas kernels  19.5 us (21%)
  local copies, waits for them, and re-layouts  8.32 us (9%)
    pallas_call x8, Pallas kernels, call(): pl.pallas_call(kernel, out_shape=outs, in_specs=[SCALAR if i == 0 or i in...  19.5 us
    ppermute x16, waiting for transfers between devices, hop(): lax.ppermute(rows, 'seq', [(order[p], order[(p + steps) % count]) for p i...  19.4 us
    ppermute x16, starting transfers between devices, hop(): lax.ppermute(rows, 'seq', [(order[p], order[(p + steps) % count]) for p i...  18.9 us
    ppermute x3, starting transfers between devices, pass_on(): lax.ppermute(state, 'seq', [(i, i + 2 * distance) for i in range(count -...  10.2 us
    unnamed x10, local copies, waits for them, and re-layouts  6.67 us
    ppermute x4, waiting for transfers between devices, spread_rows(): came = lax.ppermute(piece, 'exp', [(i, i ^ bit) for i in range(parts)])  4.58 us
    ppermute x1, starting transfers between devices, per_device(): partner = lax.ppermute(given, 'seq', swap)  3 us
    ppermute x3, waiting for transfers between devices, per_device(): lax.ppermute(ready[j], 'exp', [(i, i ^ j) for i in range(parts)])  2.43 us
  transfers between devices with their start and end apart: 28, of which 15 were waited for; matrix products, arithmetic and copies ran while one was open for 2% of the time, Pallas kernels for 9%

profile of v4, /device:TPU:0, one launch (start us, length us, event | category | flops | bytes accessed | tf_op | source)
XLA Modules:
  0.0 93.4 jit_solution(5786255014122918377)
XLA Ops:
  0.0 0.1 pad_add_fusion.scalars
  0.1 2.4 %shard_map.109 = (bf16[128,256]{1,0:T(8,128)(2,1)S(1)}, bf16[128,256]{1,0:T(8,128)(2,1)S(1)}, bf16[128,1024]{1,0:T(8,128)(2,1)S(1)}, bf16[128,1024]{1,0:T(8,128)...) custom-call(s32[4]{0:T(128)S(1)} %pad_add_fusion.scalars, bf16[128,512]{1,0:T(8,128)(2,1)} %key_ref.1, ...), custom_call_target="tpu_custom_call" | custom-call | flops 16777216 | bytes 1199120 | tf_op jit(solution)/shard_map/pallas_call | solution.py:24
  2.5 3.0 %collective-permute-start.1 = (bf16[128,256]{1,0:T(8,128)(2,1)S(1)}, bf16[128,256]{1,0:T(8,128)(2,1)S(1)}, u32[]{:S(2)}, u32[]{:S(2)}) collective-permute-start(bf16[128,256]{1,0:T(8,128)(2,1)S(1)} %get-tuple-element.45), channel_id=1, source_target_pairs={{0,4},{4,0},{8,12},{12,8},{16,20},{20,16},{24,28},{28,24},{1,5},{5... | collective-permute-start | bytes 196616 | tf_op jit(solution)/shard_map/ppermute | solution.py:462
  5.5 0.1 collective-permute-start
  5.6 0.1 constant_dynamic-slice_fusion.1
  5.6 0.8 constant_dynamic-slice_fusion
  6.4 0.1 reduce-precision_convert_fusion
  6.5 1.5 %collective-permute-done.1.partner_ref = bf16[128,256]{1,0:T(8,128)(2,1)S(1)} collective-permute-done((bf16[128,256]{1,0:T(8,128)(2,1)S(1)}, bf16[128,256]{1,0:T(8,128)(2,1)S(1)}, u32[]{:S(2)}, u32[]{:S(2)}) %collective-permute-start.1) | collective-permute-done | bytes 65568 | tf_op jit(solution)/shard_map/ppermute | solution.py:462
  8.0 4.4 %collective-permute-start.4 = (bf16[128,256]{1,0:T(8,128)(2,1)S(1)}, bf16[128,256]{1,0:T(8,128)(2,1)S(1)}, u32[]{:S(2)}, u32[]{:S(2)}) collective-permute-start(bf16[128,256]{1,0:T(8,128)(2,1)S(1)} %add_convert_fusion.6), channel_id=1, source_target_pairs={{0,8},{4,12},{8,16},{12,20},{16,24},{20,28},{1,9},{5,13},{9,17},{1... | collective-permute-start | bytes 196616 | tf_op jit(solution)/shard_map/ppermute | solution.py:383
  12.4 4.5 %collective-permute-start.3 = (bf16[128,256]{1,0:T(8,128)(2,1)S(1)}, bf16[128,256]{1,0:T(8,128)(2,1)S(1)}, u32[]{:S(2)}, u32[]{:S(2)}) collective-permute-start(bf16[128,256]{1,0:T(8,128)(2,1)S(1)} %add_convert_fusion.6), channel_id=1, source_target_pairs={{0,16},{4,20},{8,24},{12,28},{1,17},{5,21},{9,25},{13,29},{2,18},{... | collective-permute-start | bytes 196616 | tf_op jit(solution)/shard_map/ppermute | solution.py:383
  16.9 1.3 %collective-permute-start.2 = (bf16[128,256]{1,0:T(8,128)(2,1)S(1)}, bf16[128,256]{1,0:T(8,128)(2,1)S(1)}, u32[]{:S(2)}, u32[]{:S(2)}) collective-permute-start(bf16[128,256]{1,0:T(8,128)(2,1)S(1)} %add_convert_fusion.6), channel_id=1, source_target_pairs={{0,24},{4,28},{1,25},{5,29},{2,26},{6,30},{3,27},{7,31}} | collective-permute-start | bytes 196616 | tf_op jit(solution)/shard_map/ppermute | solution.py:383
  18.2 0.1 copy.17
  18.3 0.9 %shard_map.110.within_ref = f32[2,128,256]{2,1,0:T(8,128)S(1)} custom-call(s32[4]{0:T(128)S(1)} %pad_add_fusion.scalars, bf16[128,1024]{1,0:T(8,128)(2,1)S(1)} %get-tuple-element.41.mine_ref, bf16[128,1024]{1,0:T(8,128)(2,1)S(1)} %collective-permute-done.came_ref), custom_call_target="tpu_custom_call" | custom-call | flops 50331648 | bytes 786448 | tf_op jit(solution)/shard_map/pallas_call | solution.py:24
  19.3 0.0 collective-permute-done.4.refs_2_
  19.3 0.8 collective-permute-done.2.refs_0_
  20.1 0.9 %shard_map.111 = (bf16[64,256]{1,0:T(8,128)(2,1)S(1)}, bf16[64,256]{1,0:T(8,128)(2,1)S(1)}, bf16[64,256]{1,0:T(8,128)(2,1)S(1)}, bf16[64,256]{1,0:T(8,128)(2,1)S(1)}) custom-call(s32[4]{0:T(128)S(1)} %pad_add_fusion.scalars, f32[2,128,256]{2,1,0:T(8,128)S(1)} %shard_map.110.within_ref, bf16[128,1024]{1,0:T(8,128)(2,1)S(1)} %get-tuple-element.41.mine_ref, ...), custom_call_target="tpu_custom_call" | custom-call | flops 33554432 | bytes 1246224 | tf_op jit(solution)/shard_map/pallas_call | solution.py:24
  21.0 0.1 collective-permute-start.5
  21.1 1.6 %collective-permute-start.6 = (bf16[64,256]{1,0:T(8,128)(2,1)S(1)}, bf16[64,256]{1,0:T(8,128)(2,1)S(1)}, u32[]{:S(2)}, u32[]{:S(2)}) collective-permute-start(bf16[64,256]{1,0:T(8,128)(2,1)S(1)} %get-tuple-element.48), channel_id=1, source_target_pairs={{0,2},{1,3},{2,0},{3,1},{4,6},{5,7},{6,4},{7,5},{8,10},{9,11},{10,... | collective-permute-start | bytes 98312 | tf_op jit(solution)/shard_map/ppermute | solution.py:407
  22.7 0.5 collective-permute-start.7
  23.2 3.4 %collective-permute-done.7 = bf16[64,256]{1,0:T(8,128)(2,1)S(1)} collective-permute-done((bf16[64,256]{1,0:T(8,128)(2,1)S(1)}, bf16[64,256]{1,0:T(8,128)(2,1)S(1)}, u32[]{:S(2)}, u32[]{:S(2)}) %collective-permute-start.7) | collective-permute-done | bytes 32800 | tf_op jit(solution)/shard_map/ppermute | solution.py:407
  26.6 0.0 collective-permute-start.8
  26.6 0.0 collective-permute-done.5
  26.6 0.0 collective-permute-done.6
  26.6 1.2 %collective-permute-done.8 = bf16[64,256]{1,0:T(8,128)(2,1)S(1)} collective-permute-done((bf16[64,256]{1,0:T(8,128)(2,1)S(1)}, bf16[64,256]{1,0:T(8,128)(2,1)S(1)}, u32[]{:S(2)}, u32[]{:S(2)}) %collective-permute-start.8) | collective-permute-done | bytes 32800 | tf_op jit(solution)/shard_map/ppermute | solution.py:407
  27.8 1.6 %collective-permute-start.10 = (bf16[64,1152]{1,0:T(8,128)(2,1)S(1)}, bf16[64,1152]{1,0:T(8,128)(2,1)S(1)}, u32[]{:S(2)}, u32[]{:S(2)}) collective-permute-start(bf16[64,1152]{1,0:T(8,128)(2,1)S(1)} %pad_dynamic-update-slice_fusion.after_ref.refs_0_), channel_id=1, source_target_pairs={{0,4},{8,0},{16,8},{24,16},{28,24},{20,28},{12,20},{4,12},{1,5},{9... | collective-permute-start | bytes 442376 | tf_op jit(solution)/shard_map/ppermute | solution.py:267
  29.5 0.4 collective-permute-start.9
  29.9 4.0 %shard_map.112 = (bf16[4096,1024]{1,0:T(8,128)(2,1)S(1)}, f32[8,128]{1,0:T(8,128)S(1)}) custom-call(s32[4]{0:T(128)S(1)} %pad_add_fusion.scalars, bf16[4096,1024]{1,0:T(8,128)(2,1)} %bitcast.9, bf16[64,1152]{1,0:T(8,128)(2,1)S(1)} %pad_dynamic-update-slice_fusion.after_ref.refs_0_), custom_call_target="tpu_custom_call" | custom-call | bytes 16928784 | tf_op jit(solution)/shard_map/pallas_call | solution.py:24
  33.9 3.3 %copy-done.1 = bf16[4096,1024]{1,0:T(8,128)(2,1)} copy-done((bf16[4096,1024]{1,0:T(8,128)(2,1)}, bf16[4096,1024]{1,0:T(8,128)(2,1)S(1)}, u32[]{:S(2)}) %copy-start.1) | copy-done | bytes 8388632
  37.2 0.0 collective-permute-done.10.refs_4_
  37.2 0.0 collective-permute-done.9.refs_1_
  37.2 0.6 collective-permute-start.11
  37.8 1.5 %collective-permute-start.12 = (bf16[64,1152]{1,0:T(8,128)(2,1)S(1)}, bf16[64,1152]{1,0:T(8,128)(2,1)S(1)}, u32[]{:S(2)}, u32[]{:S(2)}) collective-permute-start(bf16[64,1152]{1,0:T(8,128)(2,1)S(1)} %collective-permute-done.10.refs_4_), channel_id=1, source_target_pairs={{0,4},{8,0},{16,8},{24,16},{28,24},{20,28},{12,20},{4,12},{1,5},{9... | collective-permute-start | bytes 442376 | tf_op jit(solution)/shard_map/ppermute | solution.py:267
  39.3 3.3 %collective-permute-done.11.refs_2_ = bf16[64,1152]{1,0:T(8,128)(2,1)S(1)} collective-permute-done((bf16[64,1152]{1,0:T(8,128)(2,1)S(1)}, bf16[64,1152]{1,0:T(8,128)(2,1)S(1)}, u32[]{:S(2)}, u32[]{:S(2)}) %collective-permute-start.11) | collective-permute-done | bytes 147488 | tf_op jit(solution)/shard_map/ppermute | solution.py:267
  42.6 1.6 %collective-permute-done.12.refs_5_ = bf16[64,1152]{1,0:T(8,128)(2,1)S(1)} collective-permute-done((bf16[64,1152]{1,0:T(8,128)(2,1)S(1)}, bf16[64,1152]{1,0:T(8,128)(2,1)S(1)}, u32[]{:S(2)}, u32[]{:S(2)}) %collective-permute-start.12) | collective-permute-done | bytes 147488 | tf_op jit(solution)/shard_map/ppermute | solution.py:267
  44.2 1.7 %collective-permute-start.13 = (bf16[64,1152]{1,0:T(8,128)(2,1)S(1)}, bf16[64,1152]{1,0:T(8,128)(2,1)S(1)}, u32[]{:S(2)}, u32[]{:S(2)}) collective-permute-start(bf16[64,1152]{1,0:T(8,128)(2,1)S(1)} %collective-permute-done.11.refs_2_), channel_id=1, source_target_pairs={{0,8},{8,16},{16,24},{24,28},{28,20},{20,12},{12,4},{4,0},{1,9},{9... | collective-permute-start | bytes 442376 | tf_op jit(solution)/shard_map/ppermute | solution.py:267
  45.9 0.3 collective-permute-start.14
  46.2 1.3 %collective-permute-start.16 = (bf16[32,1152]{1,0:T(8,128)(2,1)S(1)}, bf16[32,1152]{1,0:T(8,128)(2,1)S(1)}, u32[]{:S(2)}, u32[]{:S(2)}) collective-permute-start(bf16[32,1152]{1,0:T(8,128)(2,1)S(1)} %slice.31), channel_id=1, source_target_pairs={{0,12},{8,4},{16,0},{24,8},{28,16},{20,24},{12,28},{4,20},{1,13},{... | collective-permute-start | bytes 221192 | tf_op jit(solution)/shard_map/ppermute | solution.py:267
  47.5 1.8 %collective-permute-start.15 = (bf16[32,1152]{1,0:T(8,128)(2,1)S(1)}, bf16[32,1152]{1,0:T(8,128)(2,1)S(1)}, u32[]{:S(2)}, u32[]{:S(2)}) collective-permute-start(bf16[32,1152]{1,0:T(8,128)(2,1)S(1)} %slice.30), channel_id=1, source_target_pairs={{0,16},{8,24},{16,28},{24,20},{28,12},{20,4},{12,0},{4,8},{1,17},{... | collective-permute-start | bytes 221192 | tf_op jit(solution)/shard_map/ppermute | solution.py:267
  49.3 0.7 fusion.1.sources
  50.0 3.3 %shard_map.113 = (bf16[1024,2048]{1,0:T(8,128)(2,1)S(1)}, f32[8,128]{1,0:T(8,128)}) custom-call(s32[4]{0:T(128)S(1)} %pad_add_fusion.scalars, bf16[1024,2048]{1,0:T(8,128)(2,1)} %bitcast.10, f32[8,128]{1,0:T(8,128)S(1)} %get-tuple-element.52.after_ref), custom_call_target="tpu_custom_call" | custom-call | bytes 8396816 | tf_op jit(solution)/shard_map/pallas_call | solution.py:24
  53.3 0.3 collective-permute-done.16.refs_8_
  53.6 0.0 collective-permute-done.15.refs_7_
  53.7 3.4 %copy-done.2 = bf16[4096,1024]{1,0:T(8,128)(2,1)S(1)} copy-done((bf16[4096,1024]{1,0:T(8,128)(2,1)S(1)}, bf16[4096,1024]{1,0:T(8,128)(2,1)}, u32[]{:S(2)}) %copy-start.2) | copy-done | bytes 8388632
  57.0 6.0 %shard_map.114 = (bf16[32,2048]{1,0:T(8,128)(2,1)S(1)}, bf16[32,2048]{1,0:T(8,128)(2,1)S(1)}, bf16[32,2048]{1,0:T(8,128)(2,1)S(1)}, bf16[32,2048]{1,0:T(8,128)(2...) custom-call(s32[4]{0:T(128)S(1)} %pad_add_fusion.scalars, ...), custom_call_target="tpu_custom_call" | custom-call | flops 3221225472 | bytes 14950452 | tf_op jit(solution)/shard_map/pallas_call | solution.py:24
  63.1 1.5 %collective-permute-start.17 = (bf16[32,2048]{1,0:T(8,128)(2,1)S(1)}, bf16[32,2048]{1,0:T(8,128)(2,1)S(1)}, u32[]{:S(2)}, u32[]{:S(2)}) collective-permute-start(bf16[32,2048]{1,0:T(8,128)(2,1)S(1)} %get-tuple-element.61), channel_id=1, source_target_pairs={{0,8},{8,16},{16,24},{24,28},{28,20},{20,12},{12,4},{4,0},{1,9},{9... | collective-permute-start | bytes 393224 | tf_op jit(solution)/shard_map/ppermute | solution.py:267
  64.6 2.7 %collective-permute-start.18 = (bf16[16,2048]{1,0:T(8,128)(2,1)S(1)}, bf16[16,2048]{1,0:T(8,128)(2,1)S(1)}, u32[]{:S(2)}, u32[]{:S(2)}) collective-permute-start(bf16[16,2048]{1,0:T(8,128)(2,1)S(1)} %get-tuple-element.63), channel_id=1, source_target_pairs={{0,16},{8,24},{16,28},{24,20},{28,12},{20,4},{12,0},{4,8},{1,17},{... | collective-permute-start | bytes 196616 | tf_op jit(solution)/shard_map/ppermute | solution.py:267
  67.3 0.2 collective-permute-start.20
  67.5 0.6 collective-permute-start.19
  68.1 1.6 %collective-permute-done.18 = bf16[16,2048]{1,0:T(8,128)(2,1)S(1)} collective-permute-done((bf16[16,2048]{1,0:T(8,128)(2,1)S(1)}, bf16[16,2048]{1,0:T(8,128)(2,1)S(1)}, u32[]{:S(2)}, u32[]{:S(2)}) %collective-permute-start.18) | collective-permute-done | bytes 65568 | tf_op jit(solution)/shard_map/ppermute | solution.py:267
  69.8 3.5 %collective-permute-done.20 = bf16[16,2048]{1,0:T(8,128)(2,1)S(1)} collective-permute-done((bf16[16,2048]{1,0:T(8,128)(2,1)S(1)}, bf16[16,2048]{1,0:T(8,128)(2,1)S(1)}, u32[]{:S(2)}, u32[]{:S(2)}) %collective-permute-start.20) | collective-permute-done | bytes 65568 | tf_op jit(solution)/shard_map/ppermute | solution.py:267
  73.2 0.3 collective-permute-done.19
  73.6 2.7 %collective-permute-start.21 = (bf16[32,2048]{1,0:T(8,128)(2,1)S(1)}, bf16[32,2048]{1,0:T(8,128)(2,1)S(1)}, u32[]{:S(2)}, u32[]{:S(2)}) collective-permute-start(bf16[32,2048]{1,0:T(8,128)(2,1)S(1)} %get-tuple-element.67), channel_id=1, source_target_pairs={{0,8},{8,16},{16,24},{24,28},{28,20},{20,12},{12,4},{4,0},{1,9},{9... | collective-permute-start | bytes 393224 | tf_op jit(solution)/shard_map/ppermute | solution.py:267
  76.3 3.5 %collective-permute-done.21 = bf16[32,2048]{1,0:T(8,128)(2,1)S(1)} collective-permute-done((bf16[32,2048]{1,0:T(8,128)(2,1)S(1)}, bf16[32,2048]{1,0:T(8,128)(2,1)S(1)}, u32[]{:S(2)}, u32[]{:S(2)}) %collective-permute-start.21) | collective-permute-done | bytes 131104 | tf_op jit(solution)/shard_map/ppermute | solution.py:267
  79.9 1.7 %collective-permute-done.22 = bf16[32,2048]{1,0:T(8,128)(2,1)S(1)} collective-permute-done((bf16[32,2048]{1,0:T(8,128)(2,1)S(1)}, bf16[32,2048]{1,0:T(8,128)(2,1)S(1)}, u32[]{:S(2)}, u32[]{:S(2)}) %collective-permute-start.22) | collective-permute-done | bytes 131104 | tf_op jit(solution)/shard_map/ppermute | solution.py:267
  81.6 0.7 collective-permute-start.23
  82.3 1.4 %collective-permute-start.24 = (bf16[32,2048]{1,0:T(8,128)(2,1)S(1)}, bf16[32,2048]{1,0:T(8,128)(2,1)S(1)}, u32[]{:S(2)}, u32[]{:S(2)}) collective-permute-start(bf16[32,2048]{1,0:T(8,128)(2,1)S(1)} %add_convert_fusion), channel_id=1, source_target_pairs={{0,4},{8,0},{16,8},{24,16},{28,24},{20,28},{12,20},{4,12},{1,5},{9... | collective-permute-start | bytes 393224 | tf_op jit(solution)/shard_map/ppermute | solution.py:267
  83.7 2.9 %collective-permute-done.23.b_ref = bf16[32,2048]{1,0:T(8,128)(2,1)S(1)} collective-permute-done((bf16[32,2048]{1,0:T(8,128)(2,1)S(1)}, bf16[32,2048]{1,0:T(8,128)(2,1)S(1)}, u32[]{:S(2)}, u32[]{:S(2)}) %collective-permute-start.23) | collective-permute-done | bytes 131104 | tf_op jit(solution)/shard_map/ppermute | solution.py:267
  86.6 0.6 collective-permute-done.24.c_ref
  87.2 0.6 shard_map.115
  87.8 0.1 collective-permute-start.25
  87.9 0.6 collective-permute-start.26
  88.5 1.3 %collective-permute-start.27 = (bf16[32,512]{1,0:T(8,128)(2,1)S(1)}, bf16[32,512]{1,0:T(8,128)(2,1)S(1)}, u32[]{:S(2)}, u32[]{:S(2)}) collective-permute-start(bf16[32,512]{1,0:T(8,128)(2,1)S(1)} %get-tuple-element.76), channel_id=1, source_target_pairs={{0,3},{1,2},{2,1},{3,0},{4,7},{5,6},{6,5},{7,4},{8,11},{9,10},{10,... | collective-permute-start | bytes 98312 | tf_op jit(solution)/shard_map/ppermute | solution.py:514
  89.8 2.4 %collective-permute-done.26.refs_2_ = bf16[32,512]{1,0:T(8,128)(2,1)S(1)} collective-permute-done((bf16[32,512]{1,0:T(8,128)(2,1)S(1)}, bf16[32,512]{1,0:T(8,128)(2,1)S(1)}, u32[]{:S(2)}, u32[]{:S(2)}) %collective-permute-start.26) | collective-permute-done | bytes 32800 | tf_op jit(solution)/shard_map/ppermute | solution.py:514
  92.2 1.2 %shard_map.116 = bf16[128,512]{1,0:T(8,128)(2,1)} custom-call(s32[4]{0:T(128)S(1)} %pad_add_fusion.scalars, bf16[32,512]{1,0:T(8,128)(2,1)S(1)} %get-tuple-element.73.refs_0_, bf16[32,512]{1,0:T(8,128)(2,1)S(1)} %collective-permute-done.25.refs_1_, bf16[32,512]{1,0:T(8,128)(2,1)S(1)} %collective-permute-done.26.refs_2_, ...), custom_call_target="tpu_custom_call" | custom-call | bytes 262160 | tf_op jit(solution)/shard_map/pallas_call | solution.py:24
  (28 shorter events, 0.3 us)
Async XLA Ops:
  0.0 5.6 %copy-start = (s32[128,8]{0,1:T(8,128)S(1)}, s32[128,8]{0,1:T(8,128)}, u32[]{:S(2)}) copy-start(s32[128,8]{0,1:T(8,128)} %param.17) | copy-start | bytes 12292
  2.5 5.5 %collective-permute-start.1 = (bf16[128,256]{1,0:T(8,128)(2,1)S(1)}, bf16[128,256]{1,0:T(8,128)(2,1)S(1)}, u32[]{:S(2)}, u32[]{:S(2)}) collective-permute-start(bf16[128,256]{1,0:T(8,128)(2,1)S(1)} %get-tuple-element.45), channel_id=1, source_target_pairs={{0,4},{4,0},{8,12},{12,8},{16,20},{20,16},{24,28},{28,24},{1,5},{5... | collective-permute-start | bytes 196616 | tf_op jit(solution)/shard_map/ppermute | solution.py:462
  5.5 12.8 %collective-permute-start = (bf16[128,1024]{1,0:T(8,128)(2,1)S(1)}, bf16[128,1024]{1,0:T(8,128)(2,1)S(1)}, u32[]{:S(2)}, u32[]{:S(2)}) collective-permute-start(bf16[128,1024]{1,0:T(8,128)(2,1)S(1)} %get-tuple-element.42), channel_id=1, source_target_pairs={{0,4},{4,0},{8,12},{12,8},{16,20},{20,16},{24,28},{28,24},{1,5},{5... | collective-permute-start | bytes 786440 | tf_op jit(solution)/shard_map/ppermute | solution.py:463
  8.0 11.3 %collective-permute-start.4 = (bf16[128,256]{1,0:T(8,128)(2,1)S(1)}, bf16[128,256]{1,0:T(8,128)(2,1)S(1)}, u32[]{:S(2)}, u32[]{:S(2)}) collective-permute-start(bf16[128,256]{1,0:T(8,128)(2,1)S(1)} %add_convert_fusion.6), channel_id=1, source_target_pairs={{0,8},{4,12},{8,16},{12,20},{16,24},{20,28},{1,9},{5,13},{9,17},{1... | collective-permute-start | bytes 196616 | tf_op jit(solution)/shard_map/ppermute | solution.py:383
  12.4 6.9 %collective-permute-start.3 = (bf16[128,256]{1,0:T(8,128)(2,1)S(1)}, bf16[128,256]{1,0:T(8,128)(2,1)S(1)}, u32[]{:S(2)}, u32[]{:S(2)}) collective-permute-start(bf16[128,256]{1,0:T(8,128)(2,1)S(1)} %add_convert_fusion.6), channel_id=1, source_target_pairs={{0,16},{4,20},{8,24},{12,28},{1,17},{5,21},{9,25},{13,29},{2,18},{... | collective-permute-start | bytes 196616 | tf_op jit(solution)/shard_map/ppermute | solution.py:383
  16.9 3.2 %collective-permute-start.2 = (bf16[128,256]{1,0:T(8,128)(2,1)S(1)}, bf16[128,256]{1,0:T(8,128)(2,1)S(1)}, u32[]{:S(2)}, u32[]{:S(2)}) collective-permute-start(bf16[128,256]{1,0:T(8,128)(2,1)S(1)} %add_convert_fusion.6), channel_id=1, source_target_pairs={{0,24},{4,28},{1,25},{5,29},{2,26},{6,30},{3,27},{7,31}} | collective-permute-start | bytes 196616 | tf_op jit(solution)/shard_map/ppermute | solution.py:383
  21.0 5.6 %collective-permute-start.5 = (bf16[64,256]{1,0:T(8,128)(2,1)S(1)}, bf16[64,256]{1,0:T(8,128)(2,1)S(1)}, u32[]{:S(2)}, u32[]{:S(2)}) collective-permute-start(bf16[64,256]{1,0:T(8,128)(2,1)S(1)} %get-tuple-element.47), channel_id=1, source_target_pairs={{0,1},{1,0},{2,3},{3,2},{4,5},{5,4},{6,7},{7,6},{8,9},{9,8},{10,11... | collective-permute-start | bytes 98312 | tf_op jit(solution)/shard_map/ppermute | solution.py:407
  21.1 5.5 %collective-permute-start.6 = (bf16[64,256]{1,0:T(8,128)(2,1)S(1)}, bf16[64,256]{1,0:T(8,128)(2,1)S(1)}, u32[]{:S(2)}, u32[]{:S(2)}) collective-permute-start(bf16[64,256]{1,0:T(8,128)(2,1)S(1)} %get-tuple-element.48), channel_id=1, source_target_pairs={{0,2},{1,3},{2,0},{3,1},{4,6},{5,7},{6,4},{7,5},{8,10},{9,11},{10,... | collective-permute-start | bytes 98312 | tf_op jit(solution)/shard_map/ppermute | solution.py:407
  22.7 3.9 %collective-permute-start.7 = (bf16[64,256]{1,0:T(8,128)(2,1)S(1)}, bf16[64,256]{1,0:T(8,128)(2,1)S(1)}, u32[]{:S(2)}, u32[]{:S(2)}) collective-permute-start(bf16[64,256]{1,0:T(8,128)(2,1)S(1)} %get-tuple-element.49), channel_id=1, source_target_pairs={{0,2},{1,3},{2,0},{3,1},{4,6},{5,7},{6,4},{7,5},{8,10},{9,11},{10,... | collective-permute-start | bytes 98312 | tf_op jit(solution)/shard_map/ppermute | solution.py:407
  26.6 1.2 %collective-permute-start.8 = (bf16[64,256]{1,0:T(8,128)(2,1)S(1)}, bf16[64,256]{1,0:T(8,128)(2,1)S(1)}, u32[]{:S(2)}, u32[]{:S(2)}) collective-permute-start(bf16[64,256]{1,0:T(8,128)(2,1)S(1)} %collective-permute-done.7), channel_id=1, source_target_pairs={{0,1},{1,0},{2,3},{3,2},{4,5},{5,4},{6,7},{7,6},{8,9},{9,8},{10,11... | collective-permute-start | bytes 98312 | tf_op jit(solution)/shard_map/ppermute | solution.py:407
  27.8 9.4 %collective-permute-start.10 = (bf16[64,1152]{1,0:T(8,128)(2,1)S(1)}, bf16[64,1152]{1,0:T(8,128)(2,1)S(1)}, u32[]{:S(2)}, u32[]{:S(2)}) collective-permute-start(bf16[64,1152]{1,0:T(8,128)(2,1)S(1)} %pad_dynamic-update-slice_fusion.after_ref.refs_0_), channel_id=1, source_target_pairs={{0,4},{8,0},{16,8},{24,16},{28,24},{20,28},{12,20},{4,12},{1,5},{9... | collective-permute-start | bytes 442376 | tf_op jit(solution)/shard_map/ppermute | solution.py:267
  29.5 7.8 %collective-permute-start.9 = (bf16[64,1152]{1,0:T(8,128)(2,1)S(1)}, bf16[64,1152]{1,0:T(8,128)(2,1)S(1)}, u32[]{:S(2)}, u32[]{:S(2)}) collective-permute-start(bf16[64,1152]{1,0:T(8,128)(2,1)S(1)} %pad_dynamic-update-slice_fusion.after_ref.refs_0_), channel_id=1, source_target_pairs={{0,8},{8,16},{16,24},{24,28},{28,20},{20,12},{12,4},{4,0},{1,9},{9... | collective-permute-start | bytes 442376 | tf_op jit(solution)/shard_map/ppermute | solution.py:267
  33.9 3.3 %copy-start.1 = (bf16[4096,1024]{1,0:T(8,128)(2,1)}, bf16[4096,1024]{1,0:T(8,128)(2,1)S(1)}, u32[]{:S(2)}) copy-start(bf16[4096,1024]{1,0:T(8,128)(2,1)S(1)} %get-tuple-element.50.in_ref) | copy-start | bytes 25165828
  37.2 5.4 %collective-permute-start.11 = (bf16[64,1152]{1,0:T(8,128)(2,1)S(1)}, bf16[64,1152]{1,0:T(8,128)(2,1)S(1)}, u32[]{:S(2)}, u32[]{:S(2)}) collective-permute-start(bf16[64,1152]{1,0:T(8,128)(2,1)S(1)} %collective-permute-done.9.refs_1_), channel_id=1, source_target_pairs={{0,8},{8,16},{16,24},{24,28},{28,20},{20,12},{12,4},{4,0},{1,9},{9... | collective-permute-start | bytes 442376 | tf_op jit(solution)/shard_map/ppermute | solution.py:267
  37.8 6.4 %collective-permute-start.12 = (bf16[64,1152]{1,0:T(8,128)(2,1)S(1)}, bf16[64,1152]{1,0:T(8,128)(2,1)S(1)}, u32[]{:S(2)}, u32[]{:S(2)}) collective-permute-start(bf16[64,1152]{1,0:T(8,128)(2,1)S(1)} %collective-permute-done.10.refs_4_), channel_id=1, source_target_pairs={{0,4},{8,0},{16,8},{24,16},{28,24},{20,28},{12,20},{4,12},{1,5},{9... | collective-permute-start | bytes 442376 | tf_op jit(solution)/shard_map/ppermute | solution.py:267
  44.2 9.5 %collective-permute-start.13 = (bf16[64,1152]{1,0:T(8,128)(2,1)S(1)}, bf16[64,1152]{1,0:T(8,128)(2,1)S(1)}, u32[]{:S(2)}, u32[]{:S(2)}) collective-permute-start(bf16[64,1152]{1,0:T(8,128)(2,1)S(1)} %collective-permute-done.11.refs_2_), channel_id=1, source_target_pairs={{0,8},{8,16},{16,24},{24,28},{28,20},{20,12},{12,4},{4,0},{1,9},{9... | collective-permute-start | bytes 442376 | tf_op jit(solution)/shard_map/ppermute | solution.py:267
  45.9 7.7 %collective-permute-start.14 = (bf16[64,1152]{1,0:T(8,128)(2,1)S(1)}, bf16[64,1152]{1,0:T(8,128)(2,1)S(1)}, u32[]{:S(2)}, u32[]{:S(2)}) collective-permute-start(bf16[64,1152]{1,0:T(8,128)(2,1)S(1)} %collective-permute-done.12.refs_5_), channel_id=1, source_target_pairs={{0,4},{8,0},{16,8},{24,16},{28,24},{20,28},{12,20},{4,12},{1,5},{9... | collective-permute-start | bytes 442376 | tf_op jit(solution)/shard_map/ppermute | solution.py:267
  46.2 7.4 %collective-permute-start.16 = (bf16[32,1152]{1,0:T(8,128)(2,1)S(1)}, bf16[32,1152]{1,0:T(8,128)(2,1)S(1)}, u32[]{:S(2)}, u32[]{:S(2)}) collective-permute-start(bf16[32,1152]{1,0:T(8,128)(2,1)S(1)} %slice.31), channel_id=1, source_target_pairs={{0,12},{8,4},{16,0},{24,8},{28,16},{20,24},{12,28},{4,20},{1,13},{... | collective-permute-start | bytes 221192 | tf_op jit(solution)/shard_map/ppermute | solution.py:267
  47.5 6.1 %collective-permute-start.15 = (bf16[32,1152]{1,0:T(8,128)(2,1)S(1)}, bf16[32,1152]{1,0:T(8,128)(2,1)S(1)}, u32[]{:S(2)}, u32[]{:S(2)}) collective-permute-start(bf16[32,1152]{1,0:T(8,128)(2,1)S(1)} %slice.30), channel_id=1, source_target_pairs={{0,16},{8,24},{16,28},{24,20},{28,12},{20,4},{12,0},{4,8},{1,17},{... | collective-permute-start | bytes 221192 | tf_op jit(solution)/shard_map/ppermute | solution.py:267
  53.6 3.4 %copy-start.2 = (bf16[4096,1024]{1,0:T(8,128)(2,1)S(1)}, bf16[4096,1024]{1,0:T(8,128)(2,1)}, u32[]{:S(2)}) copy-start(bf16[4096,1024]{1,0:T(8,128)(2,1)} %copy-done.1) | copy-start | bytes 25165828
  63.1 6.6 %collective-permute-start.17 = (bf16[32,2048]{1,0:T(8,128)(2,1)S(1)}, bf16[32,2048]{1,0:T(8,128)(2,1)S(1)}, u32[]{:S(2)}, u32[]{:S(2)}) collective-permute-start(bf16[32,2048]{1,0:T(8,128)(2,1)S(1)} %get-tuple-element.61), channel_id=1, source_target_pairs={{0,8},{8,16},{16,24},{24,28},{28,20},{20,12},{12,4},{4,0},{1,9},{9... | collective-permute-start | bytes 393224 | tf_op jit(solution)/shard_map/ppermute | solution.py:267
  64.6 5.2 %collective-permute-start.18 = (bf16[16,2048]{1,0:T(8,128)(2,1)S(1)}, bf16[16,2048]{1,0:T(8,128)(2,1)S(1)}, u32[]{:S(2)}, u32[]{:S(2)}) collective-permute-start(bf16[16,2048]{1,0:T(8,128)(2,1)S(1)} %get-tuple-element.63), channel_id=1, source_target_pairs={{0,16},{8,24},{16,28},{24,20},{28,12},{20,4},{12,0},{4,8},{1,17},{... | collective-permute-start | bytes 196616 | tf_op jit(solution)/shard_map/ppermute | solution.py:267
  67.3 6.0 %collective-permute-start.20 = (bf16[16,2048]{1,0:T(8,128)(2,1)S(1)}, bf16[16,2048]{1,0:T(8,128)(2,1)S(1)}, u32[]{:S(2)}, u32[]{:S(2)}) collective-permute-start(bf16[16,2048]{1,0:T(8,128)(2,1)S(1)} %get-tuple-element.66), channel_id=1, source_target_pairs={{0,12},{8,4},{16,0},{24,8},{28,16},{20,24},{12,28},{4,20},{1,13},{... | collective-permute-start | bytes 196616 | tf_op jit(solution)/shard_map/ppermute | solution.py:267
  67.5 6.0 %collective-permute-start.19 = (bf16[32,2048]{1,0:T(8,128)(2,1)S(1)}, bf16[32,2048]{1,0:T(8,128)(2,1)S(1)}, u32[]{:S(2)}, u32[]{:S(2)}) collective-permute-start(bf16[32,2048]{1,0:T(8,128)(2,1)S(1)} %get-tuple-element.64), channel_id=1, source_target_pairs={{0,4},{8,0},{16,8},{24,16},{28,24},{20,28},{12,20},{4,12},{1,5},{9... | collective-permute-start | bytes 393224 | tf_op jit(solution)/shard_map/ppermute | solution.py:267
  73.6 6.2 %collective-permute-start.21 = (bf16[32,2048]{1,0:T(8,128)(2,1)S(1)}, bf16[32,2048]{1,0:T(8,128)(2,1)S(1)}, u32[]{:S(2)}, u32[]{:S(2)}) collective-permute-start(bf16[32,2048]{1,0:T(8,128)(2,1)S(1)} %get-tuple-element.67), channel_id=1, source_target_pairs={{0,8},{8,16},{16,24},{24,28},{28,20},{20,12},{12,4},{4,0},{1,9},{9... | collective-permute-start | bytes 393224 | tf_op jit(solution)/shard_map/ppermute | solution.py:267
  76.3 5.3 %collective-permute-start.22 = (bf16[32,2048]{1,0:T(8,128)(2,1)S(1)}, bf16[32,2048]{1,0:T(8,128)(2,1)S(1)}, u32[]{:S(2)}, u32[]{:S(2)}) collective-permute-start(bf16[32,2048]{1,0:T(8,128)(2,1)S(1)} %get-tuple-element.69), channel_id=1, source_target_pairs={{0,4},{8,0},{16,8},{24,16},{28,24},{20,28},{12,20},{4,12},{1,5},{9... | collective-permute-start | bytes 393224 | tf_op jit(solution)/shard_map/ppermute | solution.py:267
  81.6 5.0 %collective-permute-start.23 = (bf16[32,2048]{1,0:T(8,128)(2,1)S(1)}, bf16[32,2048]{1,0:T(8,128)(2,1)S(1)}, u32[]{:S(2)}, u32[]{:S(2)}) collective-permute-start(bf16[32,2048]{1,0:T(8,128)(2,1)S(1)} %add_convert_fusion.1), channel_id=1, source_target_pairs={{0,8},{8,16},{16,24},{24,28},{28,20},{20,12},{12,4},{4,0},{1,9},{9... | collective-permute-start | bytes 393224 | tf_op jit(solution)/shard_map/ppermute | solution.py:267
  82.3 5.0 %collective-permute-start.24 = (bf16[32,2048]{1,0:T(8,128)(2,1)S(1)}, bf16[32,2048]{1,0:T(8,128)(2,1)S(1)}, u32[]{:S(2)}, u32[]{:S(2)}) collective-permute-start(bf16[32,2048]{1,0:T(8,128)(2,1)S(1)} %add_convert_fusion), channel_id=1, source_target_pairs={{0,4},{8,0},{16,8},{24,16},{28,24},{20,28},{12,20},{4,12},{1,5},{9... | collective-permute-start | bytes 393224 | tf_op jit(solution)/shard_map/ppermute | solution.py:267
  87.8 1.9 %collective-permute-start.25 = (bf16[32,512]{1,0:T(8,128)(2,1)S(1)}, bf16[32,512]{1,0:T(8,128)(2,1)S(1)}, u32[]{:S(2)}, u32[]{:S(2)}) collective-permute-start(bf16[32,512]{1,0:T(8,128)(2,1)S(1)} %get-tuple-element.74), channel_id=1, source_target_pairs={{0,1},{1,0},{2,3},{3,2},{4,5},{5,4},{6,7},{7,6},{8,9},{9,8},{10,11... | collective-permute-start | bytes 98312 | tf_op jit(solution)/shard_map/ppermute | solution.py:514
  87.9 4.3 %collective-permute-start.26 = (bf16[32,512]{1,0:T(8,128)(2,1)S(1)}, bf16[32,512]{1,0:T(8,128)(2,1)S(1)}, u32[]{:S(2)}, u32[]{:S(2)}) collective-permute-start(bf16[32,512]{1,0:T(8,128)(2,1)S(1)} %get-tuple-element.75), channel_id=1, source_target_pairs={{0,2},{1,3},{2,0},{3,1},{4,6},{5,7},{6,4},{7,5},{8,10},{9,11},{10,... | collective-permute-start | bytes 98312 | tf_op jit(solution)/shard_map/ppermute | solution.py:514
  88.5 3.7 %collective-permute-start.27 = (bf16[32,512]{1,0:T(8,128)(2,1)S(1)}, bf16[32,512]{1,0:T(8,128)(2,1)S(1)}, u32[]{:S(2)}, u32[]{:S(2)}) collective-permute-start(bf16[32,512]{1,0:T(8,128)(2,1)S(1)} %get-tuple-element.76), channel_id=1, source_target_pairs={{0,3},{1,2},{2,1},{3,0},{4,7},{5,6},{6,5},{7,4},{8,11},{9,10},{10,... | collective-permute-start | bytes 98312 | tf_op jit(solution)/shard_map/ppermute | solution.py:514

commit v5 on v4

v5 whole, which is shorter than its diff:
```python
import functools

import jax
import jax.numpy as jnp
from jax import lax
from jax.experimental import pallas as pl
from jax.experimental.pallas import tpu as pltpu
from jax.sharding import PartitionSpec as P

HEAD = 128
F32 = jnp.float32
BF16 = jnp.bfloat16
WHOLE = pl.BlockSpec(memory_space=pltpu.VMEM)
FAR = pl.BlockSpec(memory_space=pltpu.HBM)
SCALAR = pl.BlockSpec(memory_space=pltpu.SMEM)


def call(kernel, outs, inputs, far=(), small=(), scratch=(), out_specs=None, flops=0, limit=16 << 20):
    moved = sum(a.size * a.dtype.itemsize for a in [*inputs, *outs])
    inputs = [
        pltpu.with_memory_space_constraint(a, pltpu.HBM) if i in far else a
        for i, a in enumerate(inputs)
    ]
    return pl.pallas_call(
        kernel,
        out_shape=outs,
        in_specs=[
            SCALAR if i == 0 or i in small else FAR if i in far else WHOLE
            for i in range(len(inputs))
        ],
        out_specs=out_specs or [WHOLE] * len(outs),
        scratch_shapes=scratch,
        compiler_params=pltpu.CompilerParams(vmem_limit_bytes=limit),
        cost_estimate=pl.CostEstimate(flops=flops, bytes_accessed=moved, transcendentals=0),
    )(*inputs)


def shape(dims, dtype):
    return jax.ShapeDtypeStruct(dims, dtype)


def split(value):
    high = value.astype(BF16)
    return high, (value - high.astype(F32)).astype(BF16)


def add_rows(*terms):
    return sum(t.astype(F32) for t in terms).astype(BF16)


def run_copies(pairs, sems):
    copies = [pltpu.make_async_copy(a, b, sems.at[i]) for i, (a, b) in enumerate(pairs)]
    for copy in copies:
        copy.start()
    for copy in copies:
        copy.wait()


def open_kernel(
    scalars, key_ref, value_ref, query_ref, residual_ref, gain_ref, norm_ref,
    kept_ref, given_ref, keys, values, query, residual, gain, norm, sems
):
    pairs = [
        (key_ref, keys), (value_ref, values), (query_ref, query), (residual_ref, residual),
        (gain_ref, gain), (norm_ref, norm),
    ]
    copies = [pltpu.make_async_copy(a, b, sems.at[i]) for i, (a, b) in enumerate(pairs)]
    for copy in copies:
        copy.start()
    for copy in copies[:2]:
        copy.wait()
    width = keys.shape[1] // 2
    place = scalars[1]
    for h in range(keys.shape[1] // HEAD):
        cols = slice(h * HEAD, (h + 1) * HEAD)
        state = lax.dot_general(
            keys[:, cols], values[:, cols], (((0,), (0,)), ((), ())), preferred_element_type=F32
        ).astype(BF16)
        half, inner = divmod(h * HEAD, width)

        @pl.when(place == half)
        def _():
            kept_ref[:, inner:inner + HEAD] = state

        @pl.when(place != half)
        def _():
            given_ref[:, inner:inner + HEAD] = state

    for copy in copies[2:]:
        copy.wait()


def within_kernel(scalars, keys, values, queries, out_ref):
    rows, width = out_ref.shape
    causal = lax.broadcasted_iota(jnp.int32, (rows, rows), 0) >= lax.broadcasted_iota(
        jnp.int32, (rows, rows), 1
    )
    for start in range(0, width, HEAD):
        cols = slice(start, start + HEAD)
        scores = lax.dot_general(
            queries[:, cols], keys[:, cols], (((1,), (1,)), ((), ())), preferred_element_type=F32
        )
        high, low = split(jnp.where(causal, scores, 0.0))
        out_ref[:, cols] = jnp.dot(
            high, values[:, cols], preferred_element_type=F32
        ) + jnp.dot(low, values[:, cols], preferred_element_type=F32)


def back_kernel(earlier, scalars, kept_ref, *refs):
    before_refs, out_ref = refs[:earlier], refs[earlier]
    before = sum(ref[...].astype(F32) for ref in before_refs)
    extra = jnp.where(scalars[1] == 0, kept_ref[...].astype(F32), 0.0)
    out_ref[...] = (before + extra).astype(BF16)


def attend_kernel(
    parts, earlier, scalars, within_ref, queries, residuals, gain_ref, partner_ref, other_ref, *refs
):
    before_refs, piece_refs, hidden = refs[:earlier], refs[earlier:-1], refs[-1]
    rows, full = hidden.shape
    width = full // 2
    first = scalars[1] == 0
    mine = sum(ref[...].astype(F32) for ref in before_refs)
    mine = mine + jnp.where(first, 0.0, partner_ref[...].astype(F32))
    other = other_ref[...].astype(F32)
    halves = [jnp.where(first, mine, other), jnp.where(first, other, mine)]
    for start in range(0, full, HEAD):
        cols = slice(start, start + HEAD)
        half, inner = divmod(start, width)
        high, low = split(halves[half][:, inner:inner + HEAD])
        raw = (
            jnp.dot(queries[:, cols], high, preferred_element_type=F32)
            + jnp.dot(queries[:, cols], low, preferred_element_type=F32)
            + within_ref[:, cols]
        )
        scaled = raw * lax.rsqrt(jnp.mean(raw * raw, axis=-1, keepdims=True) + 1e-06)
        hidden[:, cols] = (residuals[:, cols].astype(F32) + scaled * gain_ref[:, cols]).astype(BF16)
    count = rows // parts
    for j, piece in enumerate(piece_refs):
        piece[...] = hidden[pl.ds(pl.multiple_of((scalars[0] ^ j) * count, count), count), :]


def norm_kernel(scalars, gain_ref, pack_ref, *refs):
    pieces, hidden_ref, out_ref = refs[:-2], refs[-2], refs[-1]
    width = pieces[0].shape[1]
    model = hidden_ref.shape[1]
    total = 0.0
    for ref in pieces:
        value = ref[...].astype(F32)
        total += jnp.sum(value * value, axis=-1, keepdims=True)
    scale = lax.rsqrt(total / model + 1e-06)
    for j, ref in enumerate(pieces):
        cols = pl.ds(pl.multiple_of((scalars[0] ^ j) * width, width), width)
        hidden_ref[:, cols] = ref[...]
        out_ref[:, cols] = (ref[...].astype(F32) * scale * gain_ref[:, cols]).astype(BF16)
    out_ref[:, model:] = pack_ref[...]


def load_kernel(scalars, source, after_ref, target, done_ref, sems):
    done_ref[...] = jnp.zeros_like(done_ref)
    pieces = sems.shape[0]
    step = source.shape[0] // pieces
    run_copies(
        [
            (source.at[pl.ds(i * step, step)], target.at[pl.ds(i * step, step)])
            for i in range(pieces)
        ],
        sems,
    )


def load_near(scalars, source, after):
    return call(
        load_kernel, [shape(source.shape, source.dtype), shape((8, HEAD), F32)],
        [scalars, source, after], far=(1,), scratch=[pltpu.SemaphoreType.DMA((8,))],
    )


def expert_kernel(blocks, scalars, in_ref, down_ref, *refs):
    x_refs, out_refs, done_ref = refs[:blocks], refs[blocks:2 * blocks], refs[2 * blocks]
    rows_ref, act_ref, made_ref = refs[2 * blocks + 1:]
    done_ref[...] = jnp.zeros_like(done_ref)
    model, units = rows_ref.shape[1], in_ref.shape[1]
    spans, packs = [], []
    first = 0
    for ref in x_refs:
        spans.append(slice(first, first + ref.shape[0]))
        rows_ref[spans[-1], :] = ref[:, :model]
        packs.append(ref[:, model:].astype(F32))
        first += ref.shape[0]
    pack = jnp.concatenate(packs)
    lane = lax.broadcasted_iota(jnp.int32, pack.shape, 1)
    chosen = (lane == scalars[3]) | (lane == scalars[3] + scalars[2])
    weight = jnp.sum(jnp.where(chosen, pack, 0.0), axis=-1, keepdims=True)
    chunk = min(units, 256)

    @pl.loop(0, units // chunk)
    def _(step):
        cut = pl.ds(pl.multiple_of(step * chunk, chunk), chunk)
        gate = jnp.dot(rows_ref[...], in_ref[:model, cut], preferred_element_type=F32)
        up = jnp.dot(rows_ref[...], in_ref[model:, cut], preferred_element_type=F32)
        act_ref[:, cut] = (gate / (1.0 + jnp.exp(-gate)) * up).astype(BF16)

    wide = min(model, 512)

    @pl.loop(0, model // wide)
    def _(step):
        cut = pl.ds(pl.multiple_of(step * wide, wide), wide)
        produced = jnp.dot(act_ref[...], down_ref[:, cut], preferred_element_type=F32)
        made_ref[:, cut] = (produced.astype(BF16).astype(F32) * weight).astype(BF16)

    for out_ref, span in zip(out_refs, spans):
        out_ref[...] = made_ref[span, :]


def run_expert(scalars, blocks, weights_in, weights_out):
    units, model = weights_out.shape
    total = sum(b.shape[0] for b in blocks)
    *made, sign = call(
        functools.partial(expert_kernel, len(blocks)),
        [shape((b.shape[0], model), BF16) for b in blocks] + [shape((8, HEAD), F32)],
        [scalars, weights_in, weights_out, *blocks],
        scratch=[
            pltpu.VMEM((total, model), BF16),
            pltpu.VMEM((total, units), BF16),
            pltpu.VMEM((total, model), BF16),
        ],
        flops=6 * total * model * units,
    )
    return made, sign


def ring_order(count):
    return list(range(0, count, 2)) + list(range(1, count, 2))[::-1]


def dense_experts(block, scalars, expert_in, expert_out):
    count = lax.axis_size("seq")
    order = ring_order(count)
    half = block.shape[0] // 2
    far = count // 2

    def hop(rows, steps):
        return lax.ppermute(
            rows, "seq", [(order[p], order[(p + steps) % count]) for p in range(count)]
        )

    weights = [expert_in.reshape(-1, expert_in.shape[-1]), expert_out]
    near, after = [], block
    ahead, behind = [block], [block]
    for distance in range(1, far):
        came, went = hop(ahead[-1], 1), hop(behind[-1], -1)
        if weights:
            loaded, sign = load_near(scalars, weights.pop(0), after)
            near.append(loaded)
            came, went, after = lax.optimization_barrier((came, went, sign))
        ahead.append(came)
        behind.append(went)
    top = hop(ahead[-2][:half], 2)
    bottom = hop(behind[-2][half:], -2)
    (own, *close), sign = run_expert(scalars, ahead[:-1] + behind[1:-1], *near)
    last, first, top, bottom, _ = lax.optimization_barrier(
        (ahead[-1], behind[-1], top, bottom, sign)
    )
    (last, first, top, bottom), _ = run_expert(scalars, [last, first, top, bottom], *near)
    to_back, to_front = close[:far - 2] + [last], close[far - 2:] + [first]
    early_going, early_coming = hop(bottom, 2), hop(top, -2)
    going, coming = hop(to_front[-1], 1), hop(to_back[-1], -1)
    for distance in range(far - 2, 0, -1):
        front, back = to_front[distance - 1], to_back[distance - 1]
        if distance == far - 2:
            going = jnp.concatenate(
                [
                    add_rows(going[:half], front[:half]),
                    add_rows(going[half:], front[half:], early_going),
                ]
            )
            coming = jnp.concatenate(
                [
                    add_rows(coming[:half], back[:half], early_coming),
                    add_rows(coming[half:], back[half:]),
                ]
            )
        else:
            going = add_rows(going, front)
            coming = add_rows(coming, back)
        going, coming = hop(going, 1), hop(coming, -1)
    return own, going, coming


def mix_kernel(scalars, hidden_ref, a_ref, b_ref, c_ref, *out_refs):
    width = out_refs[0].shape[1]
    for j, out_ref in enumerate(out_refs):
        cols = pl.ds(pl.multiple_of((scalars[0] ^ j) * width, width), width)
        mixed = a_ref[:, cols].astype(F32) + b_ref[:, cols].astype(F32)
        mixed += c_ref[:, cols].astype(F32)
        out_ref[...] = (hidden_ref[:, cols].astype(F32) + mixed).astype(BF16)


def join_kernel(scalars, *refs):
    pieces, out_ref, sems = refs[:-2], refs[-2], refs[-1]
    count = pieces[0].shape[0]
    pairs = []
    for j, piece in enumerate(pieces):
        rows = pl.ds(pl.multiple_of((scalars[0] ^ j) * count, count), count)
        pairs.append((piece, out_ref.at[rows, :]))
    run_copies(pairs, sems)


def slot_ids(block_routes, expert_count, capacity):
    row_count, top_count = block_routes.shape
    expert_ids = jnp.arange(expert_count, dtype=jnp.int32)
    onehot = (
        (block_routes[:, :, None] == expert_ids[None, None, :])
        .astype(jnp.int32)
        .reshape(row_count * top_count, expert_count)
    )
    earlier = jnp.cumsum(onehot, axis=0) - onehot
    ranking = jnp.sum(earlier * onehot, axis=1).reshape(row_count, top_count)
    return block_routes * capacity + ranking


def routed_experts(normed, my_routes, my_gates, expert_in, expert_out):
    sub_count, model_width = normed.shape
    expert_count = lax.axis_size("seq") * expert_in.shape[0]
    top_count = my_routes.shape[1]
    capacity = min(sub_count, max(2, 3 * sub_count * top_count // (2 * expert_count)))
    slot_count = expert_count * capacity
    my_slots = slot_ids(my_routes, expert_count, capacity)
    columns = jnp.arange(slot_count, dtype=jnp.int32)
    placer = jnp.sum(
        (my_slots[None, :, :] == columns[:, None, None]).astype(jnp.int32), axis=2
    ).astype(BF16)
    outgoing = (
        jnp.dot(placer, normed, preferred_element_type=F32)
        .astype(BF16)
        .reshape(expert_count, capacity, model_width)
    )
    arrived = lax.all_to_all(outgoing, "seq", split_axis=0, concat_axis=0, tiled=True)
    flat_rows = arrived.reshape(-1, model_width)
    gate_up = jnp.einsum("nd,gdf->gnf", flat_rows, expert_in[0], preferred_element_type=F32)
    activated = (jax.nn.silu(gate_up[0]) * gate_up[1]).astype(BF16)
    produced = jnp.dot(activated, expert_out[0], preferred_element_type=F32).astype(BF16)
    answered = produced.reshape(arrived.shape)
    returned = lax.all_to_all(answered, "seq", split_axis=0, concat_axis=0, tiled=True)
    picked = returned.reshape(slot_count, model_width)[my_slots.reshape(-1)].reshape(
        sub_count, top_count, model_width
    )
    return jnp.sum(picked.astype(F32) * my_gates[:, :, None], axis=1)


def prior_states(kept, partner):
    count = lax.axis_size("seq")

    def pass_on(state, distance):
        return lax.ppermute(
            state, "seq", [(i, i + 2 * distance) for i in range(count - 2 * distance)]
        )

    pairs = count // 2
    running = add_rows(kept, partner)
    if pairs <= 4:
        return [pass_on(running, distance) for distance in reversed(range(1, pairs))]
    terms = []
    distance = 1
    while distance < pairs:
        terms.append(pass_on(running, distance))
        running = add_rows(running, terms[-1])
        distance *= 2
    return terms


def spread_rows(pieces):
    parts = len(pieces)
    bit = parts // 2
    held = {(j, 0): piece for j, piece in enumerate(pieces)}
    while bit:
        for (target, source), piece in list(held.items()):
            if target & bit:
                came = lax.ppermute(piece, "exp", [(i, i ^ bit) for i in range(parts)])
                held[(target ^ bit, source ^ bit)] = came
                del held[(target, source)]
        bit //= 2
    return [held[(0, j)] for j in range(parts)]


def per_device(
    residual,
    queries,
    key_vectors,
    value_vectors,
    head_gain,
    norm_gain,
    routes,
    route_gates,
    expert_in,
    expert_out,
):
    rows, width = residual.shape
    seq, parts = lax.axis_size("seq"), lax.axis_size("exp")
    count, half, model = rows // parts, width // 2, width * parts
    experts = seq * expert_in.shape[0]
    position = lax.axis_index("seq")
    my_index = lax.axis_index("exp")
    place = position % 2
    scalars = jnp.stack([my_index, place, experts, position]).astype(jnp.int32)
    swap = [(i, i ^ 1) for i in range(seq)]

    state, heads = shape((HEAD, half), BF16), shape((rows, width), BF16)
    kept, given, keys, values, query, rest, my_gain, my_norm = call(
        open_kernel,
        [state] * 2 + [heads] * 4 + [shape((1, width), F32), shape((1, model), F32)],
        [
            scalars, key_vectors, value_vectors, queries, residual, head_gain[None, :],
            norm_gain[None, :],
        ],
        far=(1, 2, 3, 4, 5, 6),
        scratch=[pltpu.SemaphoreType.DMA((6,))],
        flops=2 * rows * width * HEAD,
    )
    partner = lax.ppermute(given, "seq", swap)
    [within] = call(
        within_kernel, [shape((rows, width), F32)], [scalars, keys, values, query],
        flops=6 * rows * rows * width,
    )
    before = prior_states(kept, partner)
    [lacked] = call(
        functools.partial(back_kernel, len(before)), [state], [scalars, kept, *before]
    )
    other = lax.ppermute(lacked, "seq", swap)
    pieces = call(
        functools.partial(attend_kernel, parts, len(before)),
        [shape((count, width), BF16)] * parts,
        [scalars, within, query, rest, my_gain, partner, other, *before],
        scratch=[pltpu.VMEM((rows, width), BF16)],
        flops=4 * rows * width * HEAD,
    )
    gathered = spread_rows(pieces)

    my_routes = lax.dynamic_slice_in_dim(routes, my_index * count, count, 0)
    my_gates = lax.dynamic_slice_in_dim(route_gates, my_index * count, count, 0)
    mixing = jnp.sum(
        jnp.where(
            my_routes[:, :, None] == jnp.arange(experts, dtype=jnp.int32),
            my_gates[:, :, None],
            0.0,
        ),
        axis=1,
    )
    high = lax.reduce_precision(mixing, 8, 7)
    lanes = -(-2 * experts // HEAD) * HEAD
    pack = jnp.pad(
        jnp.concatenate([high, mixing - high], axis=1), ((0, 0), (0, lanes - 2 * experts))
    ).astype(BF16)
    hidden, block = call(
        norm_kernel,
        [shape((count, model), BF16), shape((count, model + lanes), BF16)],
        [scalars, my_norm, pack] + gathered,
    )
    if routes.shape[1] == experts:
        terms = dense_experts(block, scalars, expert_in[0], expert_out[0])
    else:
        mixed = routed_experts(block[:, :model], my_routes, my_gates, expert_in, expert_out)
        nothing = jnp.zeros_like(mixed)
        terms = (mixed, nothing, nothing)
    ready = call(
        mix_kernel, [shape((count, width), BF16)] * parts, [scalars, hidden, *terms]
    )
    returned = [ready[0]] + [
        lax.ppermute(ready[j], "exp", [(i, i ^ j) for i in range(parts)])
        for j in range(1, parts)
    ]
    [out] = call(
        join_kernel, [shape((rows, width), BF16)], [scalars] + returned, out_specs=[FAR],
        scratch=[pltpu.SemaphoreType.DMA((parts,))],
    )
    return out


def solution(mesh):
    placed = (
        P("seq", "exp"),
        P("seq", "exp"),
        P("seq", "exp"),
        P("seq", "exp"),
        P("exp"),
        P(),
        P("seq", None),
        P("seq", None),
        P("seq", None, None, None),
        P("seq", None, None),
    )
    return jax.shard_map(
        per_device, mesh=mesh, in_specs=placed, out_specs=P("seq", "exp"), check_vma=False
    )
```

time: 93.7 us -> 91.4 us (0.975)
  local copies, waits for them, and re-layouts: 8.32 us -> 1 us
  Pallas kernels: 19.5 us -> 23.4 us
    unnamed x10 -> x2, local copies, waits for them, and re-layouts: 6.67 us -> 0.01 us
    pallas_call x8 -> x11, Pallas kernels: 19.5 us -> 23.4 us  [call(): pl.pallas_call(kernel, out_shape=outs, in_specs=[SCALAR if i == 0 or i in...]
    ppermute x1, waiting for transfers between devices: 0.01 us -> 1.66 us  [per_device(): other = lax.ppermute(lacked, 'seq', swap)]
    ppermute x1, starting transfers between devices: 0.08 us -> 1.56 us  [per_device(): other = lax.ppermute(lacked, 'seq', swap)]
    ppermute x16, waiting for transfers between devices: 19.4 us -> 18 us  [hop(): lax.ppermute(rows, 'seq', [(order[p], order[(p + steps) % count]) for p i...]
    ppermute x4, waiting for transfers between devices: 4.58 us -> 3.32 us  [spread_rows(): came = lax.ppermute(piece, 'exp', [(i, i ^ bit) for i in range(parts)])]
    ppermute x16, starting transfers between devices: 18.9 us -> 17.9 us  [hop(): lax.ppermute(rows, 'seq', [(order[p], order[(p + steps) % count]) for p i...]
  transfers between devices with their start and end apart: 28 -> 28, of which waited for: 15 -> 15; matrix products, arithmetic and copies ran while one was open for 2% -> 1% of each run, Pallas kernels for 9% -> 14%
where the time goes in v5:
time: 91.4 us; the launch traced here: 91.1 us
  starting transfers between devices  36.6 us (40%)
  waiting for transfers between devices  29.6 us (32%)
  Pallas kernels  23.4 us (26%)
  local copies, waits for them, and re-layouts  1 us (1%)
    pallas_call x11, Pallas kernels, call(): pl.pallas_call(kernel, out_shape=outs, in_specs=[SCALAR if i == 0 or i in...  23.4 us
    ppermute x16, waiting for transfers between devices, hop(): lax.ppermute(rows, 'seq', [(order[p], order[(p + steps) % count]) for p i...  18 us
    ppermute x16, starting transfers between devices, hop(): lax.ppermute(rows, 'seq', [(order[p], order[(p + steps) % count]) for p i...  17.9 us
    ppermute x3, starting transfers between devices, pass_on(): lax.ppermute(state, 'seq', [(i, i + 2 * distance) for i in range(count -...  9.8 us
    ppermute x4, waiting for transfers between devices, spread_rows(): came = lax.ppermute(piece, 'exp', [(i, i ^ bit) for i in range(parts)])  3.32 us
    ppermute x3, waiting for transfers between devices, per_device(): lax.ppermute(ready[j], 'exp', [(i, i ^ j) for i in range(parts)])  3.27 us
    ppermute x1, starting transfers between devices, per_device(): partner = lax.ppermute(given, 'seq', swap)  3 us
    ppermute x3, starting transfers between devices, per_device(): lax.ppermute(ready[j], 'exp', [(i, i ^ j) for i in range(parts)])  2.21 us
  transfers between devices with their start and end apart: 28, of which 15 were waited for; matrix products, arithmetic and copies ran while one was open for 1% of the time, Pallas kernels for 14%

profile of v5, /device:TPU:0, one launch (start us, length us, event | category | flops | bytes accessed | tf_op | source)
XLA Modules:
  0.0 91.1 jit_solution(4291885740260532030)
XLA Ops:
  0.0 0.1 pad_add_fusion.scalars
  0.1 2.3 %shard_map.100 = (bf16[128,256]{1,0:T(8,128)(2,1)S(1)}, bf16[128,256]{1,0:T(8,128)(2,1)S(1)}, bf16[128,512]{1,0:T(8,128)(2,1)S(1)}, bf16[128,512]{1,0:T(8,128)(2...) custom-call(s32[4]{0:T(128)S(1)} %pad_add_fusion.scalars, ...), custom_call_target="tpu_custom_call" | custom-call | flops 16777216 | bytes 1200144 | tf_op jit(solution)/shard_map/pallas_call | solution.py:24
  2.4 3.0 %collective-permute-start = (bf16[128,256]{1,0:T(8,128)(2,1)S(1)}, bf16[128,256]{1,0:T(8,128)(2,1)S(1)}, u32[]{:S(2)}, u32[]{:S(2)}) collective-permute-start(bf16[128,256]{1,0:T(8,128)(2,1)S(1)} %get-tuple-element.50), channel_id=1, source_target_pairs={{0,4},{4,0},{8,12},{12,8},{16,20},{20,16},{24,28},{28,24},{1,5},{5... | collective-permute-start | bytes 196616 | tf_op jit(solution)/shard_map/ppermute | solution.py:421
  5.4 0.1 constant_dynamic-slice_fusion
  5.5 2.2 %collective-permute-done.partner_ref = bf16[128,256]{1,0:T(8,128)(2,1)S(1)} collective-permute-done((bf16[128,256]{1,0:T(8,128)(2,1)S(1)}, bf16[128,256]{1,0:T(8,128)(2,1)S(1)}, u32[]{:S(2)}, u32[]{:S(2)}) %collective-permute-start) | collective-permute-done | bytes 65568 | tf_op jit(solution)/shard_map/ppermute | solution.py:421
  7.7 6.0 %collective-permute-start.1 = (bf16[128,256]{1,0:T(8,128)(2,1)S(1)}, bf16[128,256]{1,0:T(8,128)(2,1)S(1)}, u32[]{:S(2)}, u32[]{:S(2)}) collective-permute-start(bf16[128,256]{1,0:T(8,128)(2,1)S(1)} %add_convert_fusion.6), channel_id=1, source_target_pairs={{0,24},{4,28},{1,25},{5,29},{2,26},{6,30},{3,27},{7,31}} | collective-permute-start | bytes 196616 | tf_op jit(solution)/shard_map/ppermute | solution.py:356
  13.7 1.3 %collective-permute-start.2 = (bf16[128,256]{1,0:T(8,128)(2,1)S(1)}, bf16[128,256]{1,0:T(8,128)(2,1)S(1)}, u32[]{:S(2)}, u32[]{:S(2)}) collective-permute-start(bf16[128,256]{1,0:T(8,128)(2,1)S(1)} %add_convert_fusion.6), channel_id=1, source_target_pairs={{0,16},{4,20},{8,24},{12,28},{1,17},{5,21},{9,25},{13,29},{2,18},{... | collective-permute-start | bytes 196616 | tf_op jit(solution)/shard_map/ppermute | solution.py:356
  15.0 2.5 %collective-permute-start.3 = (bf16[128,256]{1,0:T(8,128)(2,1)S(1)}, bf16[128,256]{1,0:T(8,128)(2,1)S(1)}, u32[]{:S(2)}, u32[]{:S(2)}) collective-permute-start(bf16[128,256]{1,0:T(8,128)(2,1)S(1)} %add_convert_fusion.6), channel_id=1, source_target_pairs={{0,8},{4,12},{8,16},{12,20},{16,24},{20,28},{1,9},{5,13},{9,17},{1... | collective-permute-start | bytes 196616 | tf_op jit(solution)/shard_map/ppermute | solution.py:356
  17.5 0.8 constant_dynamic-slice_fusion.1
  18.3 1.1 %collective-permute-done.3.refs_2_ = bf16[128,256]{1,0:T(8,128)(2,1)S(1)} collective-permute-done((bf16[128,256]{1,0:T(8,128)(2,1)S(1)}, bf16[128,256]{1,0:T(8,128)(2,1)S(1)}, u32[]{:S(2)}, u32[]{:S(2)}) %collective-permute-start.3) | collective-permute-done | bytes 65568 | tf_op jit(solution)/shard_map/ppermute | solution.py:356
  19.4 0.6 shard_map.102
  20.0 1.6 %collective-permute-start.4 = (bf16[128,256]{1,0:T(8,128)(2,1)S(1)}, bf16[128,256]{1,0:T(8,128)(2,1)S(1)}, u32[]{:S(2)}, u32[]{:S(2)}) collective-permute-start(bf16[128,256]{1,0:T(8,128)(2,1)S(1)} %shard_map.102), channel_id=1, source_target_pairs={{0,4},{4,0},{8,12},{12,8},{16,20},{20,16},{24,28},{28,24},{1,5},{5... | collective-permute-start | bytes 196616 | tf_op jit(solution)/shard_map/ppermute | solution.py:430
  21.6 0.1 copy.16
  21.6 0.1 copy.15
  21.7 0.9 %shard_map.101.within_ref = f32[128,512]{1,0:T(8,128)S(1)} custom-call(s32[4]{0:T(128)S(1)} %pad_add_fusion.scalars, bf16[128,512]{1,0:T(8,128)(2,1)S(1)} %get-tuple-element.45.keys, bf16[128,512]{1,0:T(8,128)(2,1)S(1)} %get-tuple-element.46.values, bf16[128,512]{1,0:T(8,128)(2,1)S(1)} %get-tuple-element.47.queries), custom_call_target="tpu_custom_call" | custom-call | flops 50331648 | bytes 655376 | tf_op jit(solution)/shard_map/pallas_call | solution.py:24
  22.6 1.7 %collective-permute-done.4.other_ref = bf16[128,256]{1,0:T(8,128)(2,1)S(1)} collective-permute-done((bf16[128,256]{1,0:T(8,128)(2,1)S(1)}, bf16[128,256]{1,0:T(8,128)(2,1)S(1)}, u32[]{:S(2)}, u32[]{:S(2)}) %collective-permute-start.4) | collective-permute-done | bytes 65568 | tf_op jit(solution)/shard_map/ppermute | solution.py:430
  24.3 0.9 %shard_map.103 = (bf16[32,512]{1,0:T(8,128)(2,1)S(1)}, bf16[32,512]{1,0:T(8,128)(2,1)S(1)}, bf16[32,512]{1,0:T(8,128)(2,1)S(1)}, bf16[32,512]{1,0:T(8,128)(2,1)S(1)}) custom-call(s32[4]{0:T(128)S(1)} %pad_add_fusion.scalars, f32[128,512]{1,0:T(8,128)S(1)} %shard_map.101.within_ref, bf16[128,512]{1,0:T(8,128)(2,1)S(1)} %get-tuple-element.47.queries, ...), custom_call_target="tpu_custom_call" | custom-call | flops 33554432 | bytes 985104 | tf_op jit(solution)/shard_map/pallas_call | solution.py:24
  25.2 1.6 %collective-permute-start.7 = (bf16[32,512]{1,0:T(8,128)(2,1)S(1)}, bf16[32,512]{1,0:T(8,128)(2,1)S(1)}, u32[]{:S(2)}, u32[]{:S(2)}) collective-permute-start(bf16[32,512]{1,0:T(8,128)(2,1)S(1)} %get-tuple-element.55), channel_id=1, source_target_pairs={{0,2},{1,3},{2,0},{3,1},{4,6},{5,7},{6,4},{7,5},{8,10},{9,11},{10,... | collective-permute-start | bytes 98312 | tf_op jit(solution)/shard_map/ppermute | solution.py:380
  26.8 0.0 collective-permute-start.5
  26.8 0.6 collective-permute-start.6
  27.4 1.8 %collective-permute-done.7 = bf16[32,512]{1,0:T(8,128)(2,1)S(1)} collective-permute-done((bf16[32,512]{1,0:T(8,128)(2,1)S(1)}, bf16[32,512]{1,0:T(8,128)(2,1)S(1)}, u32[]{:S(2)}, u32[]{:S(2)}) %collective-permute-start.7) | collective-permute-done | bytes 32800 | tf_op jit(solution)/shard_map/ppermute | solution.py:380
  29.2 0.0 collective-permute-start.8
  29.2 0.1 fusion.2.pack_ref
  29.3 0.0 collective-permute-done.5.refs_1_
  29.3 1.5 %collective-permute-done.6.refs_2_ = bf16[32,512]{1,0:T(8,128)(2,1)S(1)} collective-permute-done((bf16[32,512]{1,0:T(8,128)(2,1)S(1)}, bf16[32,512]{1,0:T(8,128)(2,1)S(1)}, u32[]{:S(2)}, u32[]{:S(2)}) %collective-permute-start.6) | collective-permute-done | bytes 32800 | tf_op jit(solution)/shard_map/ppermute | solution.py:380
  30.8 0.0 collective-permute-done.8.refs_3_
  30.8 0.7 shard_map.104
  31.5 2.4 %collective-permute-start.9 = (bf16[32,2176]{1,0:T(8,128)(2,1)S(1)}, bf16[32,2176]{1,0:T(8,128)(2,1)S(1)}, u32[]{:S(2)}, u32[]{:S(2)}) collective-permute-start(bf16[32,2176]{1,0:T(8,128)(2,1)S(1)} %get-tuple-element.57.after_ref.refs_0_), channel_id=1, source_target_pairs={{0,8},{8,16},{16,24},{24,28},{28,20},{20,12},{12,4},{4,0},{1,9},{9... | collective-permute-start | bytes 417800 | tf_op jit(solution)/shard_map/ppermute | solution.py:244
  33.9 0.0 collective-permute-start.10
  33.9 4.0 %shard_map.105 = (bf16[4096,1024]{1,0:T(8,128)(2,1)S(1)}, f32[8,128]{1,0:T(8,128)S(1)}) custom-call(s32[4]{0:T(128)S(1)} %pad_add_fusion.scalars, bf16[4096,1024]{1,0:T(8,128)(2,1)} %bitcast.7, bf16[32,2176]{1,0:T(8,128)(2,1)S(1)} %get-tuple-element.57.after_ref.refs_0_), custom_call_target="tpu_custom_call" | custom-call | bytes 16920592 | tf_op jit(solution)/shard_map/pallas_call | solution.py:24
  37.9 1.0 %collective-permute-done.10.refs_3_ = bf16[32,2176]{1,0:T(8,128)(2,1)S(1)} collective-permute-done((bf16[32,2176]{1,0:T(8,128)(2,1)S(1)}, bf16[32,2176]{1,0:T(8,128)(2,1)S(1)}, u32[]{:S(2)}, u32[]{:S(2)}) %collective-permute-start.10) | collective-permute-done | bytes 139296 | tf_op jit(solution)/shard_map/ppermute | solution.py:244
  39.0 1.1 %collective-permute-start.11 = (bf16[32,2176]{1,0:T(8,128)(2,1)S(1)}, bf16[32,2176]{1,0:T(8,128)(2,1)S(1)}, u32[]{:S(2)}, u32[]{:S(2)}) collective-permute-start(bf16[32,2176]{1,0:T(8,128)(2,1)S(1)} %collective-permute-done.9.refs_1_), channel_id=1, source_target_pairs={{0,8},{8,16},{16,24},{24,28},{28,20},{20,12},{12,4},{4,0},{1,9},{9... | collective-permute-start | bytes 417800 | tf_op jit(solution)/shard_map/ppermute | solution.py:244
  40.0 1.0 %collective-permute-start.12 = (bf16[32,2176]{1,0:T(8,128)(2,1)S(1)}, bf16[32,2176]{1,0:T(8,128)(2,1)S(1)}, u32[]{:S(2)}, u32[]{:S(2)}) collective-permute-start(bf16[32,2176]{1,0:T(8,128)(2,1)S(1)} %collective-permute-done.10.refs_3_), channel_id=1, source_target_pairs={{0,4},{8,0},{16,8},{24,16},{28,24},{20,28},{12,20},{4,12},{1,5},{9... | collective-permute-start | bytes 417800 | tf_op jit(solution)/shard_map/ppermute | solution.py:244
  41.0 3.0 %collective-permute-done.11.refs_2_ = bf16[32,2176]{1,0:T(8,128)(2,1)S(1)} collective-permute-done((bf16[32,2176]{1,0:T(8,128)(2,1)S(1)}, bf16[32,2176]{1,0:T(8,128)(2,1)S(1)}, u32[]{:S(2)}, u32[]{:S(2)}) %collective-permute-start.11) | collective-permute-done | bytes 139296 | tf_op jit(solution)/shard_map/ppermute | solution.py:244
  44.0 1.1 %collective-permute-done.12.refs_4_ = bf16[32,2176]{1,0:T(8,128)(2,1)S(1)} collective-permute-done((bf16[32,2176]{1,0:T(8,128)(2,1)S(1)}, bf16[32,2176]{1,0:T(8,128)(2,1)S(1)}, u32[]{:S(2)}, u32[]{:S(2)}) %collective-permute-start.12) | collective-permute-done | bytes 139296 | tf_op jit(solution)/shard_map/ppermute | solution.py:244
  45.1 0.5 collective-permute-start.13
  45.6 1.5 %collective-permute-start.14 = (bf16[32,2176]{1,0:T(8,128)(2,1)S(1)}, bf16[32,2176]{1,0:T(8,128)(2,1)S(1)}, u32[]{:S(2)}, u32[]{:S(2)}) collective-permute-start(bf16[32,2176]{1,0:T(8,128)(2,1)S(1)} %collective-permute-done.12.refs_4_), channel_id=1, source_target_pairs={{0,4},{8,0},{16,8},{24,16},{28,24},{20,28},{12,20},{4,12},{1,5},{9... | collective-permute-start | bytes 417800 | tf_op jit(solution)/shard_map/ppermute | solution.py:244
  47.1 1.2 %collective-permute-start.15 = (bf16[16,2176]{1,0:T(8,128)(2,1)S(1)}, bf16[16,2176]{1,0:T(8,128)(2,1)S(1)}, u32[]{:S(2)}, u32[]{:S(2)}) collective-permute-start(bf16[16,2176]{1,0:T(8,128)(2,1)S(1)} %slice.30), channel_id=1, source_target_pairs={{0,16},{8,24},{16,28},{24,20},{28,12},{20,4},{12,0},{4,8},{1,17},{... | collective-permute-start | bytes 208904 | tf_op jit(solution)/shard_map/ppermute | solution.py:244
  48.3 1.8 %collective-permute-start.16 = (bf16[16,2176]{1,0:T(8,128)(2,1)S(1)}, bf16[16,2176]{1,0:T(8,128)(2,1)S(1)}, u32[]{:S(2)}, u32[]{:S(2)}) collective-permute-start(bf16[16,2176]{1,0:T(8,128)(2,1)S(1)} %slice.31), channel_id=1, source_target_pairs={{0,12},{8,4},{16,0},{24,8},{28,16},{20,24},{12,28},{4,20},{1,13},{... | collective-permute-start | bytes 208904 | tf_op jit(solution)/shard_map/ppermute | solution.py:244
  50.1 3.3 %shard_map.106 = (bf16[1024,2048]{1,0:T(8,128)(2,1)S(1)}, f32[8,128]{1,0:T(8,128)}) custom-call(s32[4]{0:T(128)S(1)} %pad_add_fusion.scalars, bf16[1024,2048]{1,0:T(8,128)(2,1)} %bitcast.8, f32[8,128]{1,0:T(8,128)S(1)} %get-tuple-element.60.after_ref), custom_call_target="tpu_custom_call" | custom-call | bytes 8396816 | tf_op jit(solution)/shard_map/pallas_call | solution.py:24
  53.5 0.2 collective-permute-done.16.refs_3_
  53.6 0.0 collective-permute-done.13.refs_0_
  53.6 0.0 collective-permute-done.14.refs_1_
  53.6 4.2 %shard_map.108 = (bf16[32,2048]{1,0:T(8,128)(2,1)S(1)}, bf16[32,2048]{1,0:T(8,128)(2,1)S(1)}, bf16[16,2048]{1,0:T(8,128)(2,1)S(1)}, bf16[16,2048]{1,0:T(8,128)(2,1)S(1)}, f32[8,128]{1,0:T(8,128)}) custom-call(s32[4]{0:T(128)S(1)} %pad_add_fusion.scalars, bf16[4096,1024]{1,0:T(8,128)(2,1)S(1)} %get-tuple-element.58.in_ref, ...), custom_call_target="tpu_custom_call" | custom-call | flops 1207959552 | bytes 13398032 | tf_op jit(solution)/shard_map/pallas_call | solution.py:24
  57.9 1.2 %collective-permute-start.17 = (bf16[32,2048]{1,0:T(8,128)(2,1)S(1)}, bf16[32,2048]{1,0:T(8,128)(2,1)S(1)}, u32[]{:S(2)}, u32[]{:S(2)}) collective-permute-start(bf16[32,2048]{1,0:T(8,128)(2,1)S(1)} %get-tuple-element.71), channel_id=1, source_target_pairs={{0,8},{8,16},{16,24},{24,28},{28,20},{20,12},{12,4},{4,0},{1,9},{9... | collective-permute-start | bytes 393224 | tf_op jit(solution)/shard_map/ppermute | solution.py:244
  59.1 2.2 %collective-permute-start.18 = (bf16[16,2048]{1,0:T(8,128)(2,1)S(1)}, bf16[16,2048]{1,0:T(8,128)(2,1)S(1)}, u32[]{:S(2)}, u32[]{:S(2)}) collective-permute-start(bf16[16,2048]{1,0:T(8,128)(2,1)S(1)} %get-tuple-element.73), channel_id=1, source_target_pairs={{0,16},{8,24},{16,28},{24,20},{28,12},{20,4},{12,0},{4,8},{1,17},{... | collective-permute-start | bytes 196616 | tf_op jit(solution)/shard_map/ppermute | solution.py:244
  61.3 4.5 %shard_map.107 = (bf16[32,2048]{1,0:T(8,128)(2,1)S(1)}, bf16[32,2048]{1,0:T(8,128)(2,1)S(1)}, bf16[32,2048]{1,0:T(8,128)(2,1)S(1)}, bf16[32,2048]{1,0:T(8,128)(2...) custom-call(s32[4]{0:T(128)S(1)} %pad_add_fusion.scalars, bf16[4096,1024]{1,0:T(8,128)(2,1)S(1)} %get-tuple-element.58.in_ref, ...), custom_call_target="tpu_custom_call" | custom-call | flops 2013265920 | bytes 13938704 | tf_op jit(solution)/shard_map/pallas_call | solution.py:24
  65.8 0.7 collective-permute-start.22
  66.5 0.8 collective-permute-start.21
  67.4 1.3 %collective-permute-start.19 = (bf16[32,2048]{1,0:T(8,128)(2,1)S(1)}, bf16[32,2048]{1,0:T(8,128)(2,1)S(1)}, u32[]{:S(2)}, u32[]{:S(2)}) collective-permute-start(bf16[32,2048]{1,0:T(8,128)(2,1)S(1)} %pad_maximum_fusion), channel_id=1, source_target_pairs={{0,8},{8,16},{16,24},{24,28},{28,20},{20,12},{12,4},{4,0},{1,9},{9... | collective-permute-start | bytes 393224 | tf_op jit(solution)/shard_map/ppermute | solution.py:244
  68.7 3.5 %collective-permute-done.22 = bf16[16,2048]{1,0:T(8,128)(2,1)S(1)} collective-permute-done((bf16[16,2048]{1,0:T(8,128)(2,1)S(1)}, bf16[16,2048]{1,0:T(8,128)(2,1)S(1)}, u32[]{:S(2)}, u32[]{:S(2)}) %collective-permute-start.22) | collective-permute-done | bytes 65568 | tf_op jit(solution)/shard_map/ppermute | solution.py:244
  72.2 1.4 %collective-permute-done.21 = bf16[32,2048]{1,0:T(8,128)(2,1)S(1)} collective-permute-done((bf16[32,2048]{1,0:T(8,128)(2,1)S(1)}, bf16[32,2048]{1,0:T(8,128)(2,1)S(1)}, u32[]{:S(2)}, u32[]{:S(2)}) %collective-permute-start.21) | collective-permute-done | bytes 131104 | tf_op jit(solution)/shard_map/ppermute | solution.py:244
  73.7 0.1 collective-permute-start.23
  73.9 2.0 %collective-permute-start.20 = (bf16[32,2048]{1,0:T(8,128)(2,1)S(1)}, bf16[32,2048]{1,0:T(8,128)(2,1)S(1)}, u32[]{:S(2)}, u32[]{:S(2)}) collective-permute-start(bf16[32,2048]{1,0:T(8,128)(2,1)S(1)} %add_convert_fusion.1), channel_id=1, source_target_pairs={{0,8},{8,16},{16,24},{24,28},{28,20},{20,12},{12,4},{4,0},{1,9},{9... | collective-permute-start | bytes 393224 | tf_op jit(solution)/shard_map/ppermute | solution.py:244
  75.9 2.8 %collective-permute-done.23 = bf16[32,2048]{1,0:T(8,128)(2,1)S(1)} collective-permute-done((bf16[32,2048]{1,0:T(8,128)(2,1)S(1)}, bf16[32,2048]{1,0:T(8,128)(2,1)S(1)}, u32[]{:S(2)}, u32[]{:S(2)}) %collective-permute-start.23) | collective-permute-done | bytes 131104 | tf_op jit(solution)/shard_map/ppermute | solution.py:244
  78.8 0.1 collective-permute-start.24
  78.9 4.9 %collective-permute-done.24.c_ref = bf16[32,2048]{1,0:T(8,128)(2,1)S(1)} collective-permute-done((bf16[32,2048]{1,0:T(8,128)(2,1)S(1)}, bf16[32,2048]{1,0:T(8,128)(2,1)S(1)}, u32[]{:S(2)}, u32[]{:S(2)}) %collective-permute-start.24) | collective-permute-done | bytes 131104 | tf_op jit(solution)/shard_map/ppermute | solution.py:244
  83.8 0.6 shard_map.109
  84.4 0.1 collective-permute-start.25
  84.5 2.1 %collective-permute-start.26 = (bf16[32,512]{1,0:T(8,128)(2,1)S(1)}, bf16[32,512]{1,0:T(8,128)(2,1)S(1)}, u32[]{:S(2)}, u32[]{:S(2)}) collective-permute-start(bf16[32,512]{1,0:T(8,128)(2,1)S(1)} %get-tuple-element.81), channel_id=1, source_target_pairs={{0,2},{1,3},{2,0},{3,1},{4,6},{5,7},{6,4},{7,5},{8,10},{9,11},{10,... | collective-permute-start | bytes 98312 | tf_op jit(solution)/shard_map/ppermute | solution.py:470
  86.6 0.1 collective-permute-start.27
  86.6 1.9 %collective-permute-done.26.refs_2_ = bf16[32,512]{1,0:T(8,128)(2,1)S(1)} collective-permute-done((bf16[32,512]{1,0:T(8,128)(2,1)S(1)}, bf16[32,512]{1,0:T(8,128)(2,1)S(1)}, u32[]{:S(2)}, u32[]{:S(2)}) %collective-permute-start.26) | collective-permute-done | bytes 32800 | tf_op jit(solution)/shard_map/ppermute | solution.py:470
  88.5 1.4 %collective-permute-done.27.refs_3_ = bf16[32,512]{1,0:T(8,128)(2,1)S(1)} collective-permute-done((bf16[32,512]{1,0:T(8,128)(2,1)S(1)}, bf16[32,512]{1,0:T(8,128)(2,1)S(1)}, u32[]{:S(2)}, u32[]{:S(2)}) %collective-permute-start.27) | collective-permute-done | bytes 32800 | tf_op jit(solution)/shard_map/ppermute | solution.py:470
  89.9 1.2 %shard_map.110 = bf16[128,512]{1,0:T(8,128)(2,1)} custom-call(s32[4]{0:T(128)S(1)} %pad_add_fusion.scalars, bf16[32,512]{1,0:T(8,128)(2,1)S(1)} %get-tuple-element.79.refs_0_, bf16[32,512]{1,0:T(8,128)(2,1)S(1)} %collective-permute-done.25.refs_1_, bf16[32,512]{1,0:T(8,128)(2,1)S(1)} %collective-permute-done.26.refs_2_, ...), custom_call_target="tpu_custom_call" | custom-call | bytes 262160 | tf_op jit(solution)/shard_map/pallas_call | solution.py:24
  (23 shorter events, 0.3 us)
Async XLA Ops:
  0.0 5.4 %copy-start = (f32[128,8]{0,1:T(8,128)S(1)}, f32[128,8]{0,1:T(8,128)}, u32[]{:S(2)}) copy-start(f32[128,8]{0,1:T(8,128)} %param.17) | copy-start | bytes 12292
  2.4 5.2 %collective-permute-start = (bf16[128,256]{1,0:T(8,128)(2,1)S(1)}, bf16[128,256]{1,0:T(8,128)(2,1)S(1)}, u32[]{:S(2)}, u32[]{:S(2)}) collective-permute-start(bf16[128,256]{1,0:T(8,128)(2,1)S(1)} %get-tuple-element.50), channel_id=1, source_target_pairs={{0,4},{4,0},{8,12},{12,8},{16,20},{20,16},{24,28},{28,24},{1,5},{5... | collective-permute-start | bytes 196616 | tf_op jit(solution)/shard_map/ppermute | solution.py:421
  7.7 10.6 %collective-permute-start.1 = (bf16[128,256]{1,0:T(8,128)(2,1)S(1)}, bf16[128,256]{1,0:T(8,128)(2,1)S(1)}, u32[]{:S(2)}, u32[]{:S(2)}) collective-permute-start(bf16[128,256]{1,0:T(8,128)(2,1)S(1)} %add_convert_fusion.6), channel_id=1, source_target_pairs={{0,24},{4,28},{1,25},{5,29},{2,26},{6,30},{3,27},{7,31}} | collective-permute-start | bytes 196616 | tf_op jit(solution)/shard_map/ppermute | solution.py:356
  13.7 4.6 %collective-permute-start.2 = (bf16[128,256]{1,0:T(8,128)(2,1)S(1)}, bf16[128,256]{1,0:T(8,128)(2,1)S(1)}, u32[]{:S(2)}, u32[]{:S(2)}) collective-permute-start(bf16[128,256]{1,0:T(8,128)(2,1)S(1)} %add_convert_fusion.6), channel_id=1, source_target_pairs={{0,16},{4,20},{8,24},{12,28},{1,17},{5,21},{9,25},{13,29},{2,18},{... | collective-permute-start | bytes 196616 | tf_op jit(solution)/shard_map/ppermute | solution.py:356
  15.0 4.4 %collective-permute-start.3 = (bf16[128,256]{1,0:T(8,128)(2,1)S(1)}, bf16[128,256]{1,0:T(8,128)(2,1)S(1)}, u32[]{:S(2)}, u32[]{:S(2)}) collective-permute-start(bf16[128,256]{1,0:T(8,128)(2,1)S(1)} %add_convert_fusion.6), channel_id=1, source_target_pairs={{0,8},{4,12},{8,16},{12,20},{16,24},{20,28},{1,9},{5,13},{9,17},{1... | collective-permute-start | bytes 196616 | tf_op jit(solution)/shard_map/ppermute | solution.py:356
  20.0 4.3 %collective-permute-start.4 = (bf16[128,256]{1,0:T(8,128)(2,1)S(1)}, bf16[128,256]{1,0:T(8,128)(2,1)S(1)}, u32[]{:S(2)}, u32[]{:S(2)}) collective-permute-start(bf16[128,256]{1,0:T(8,128)(2,1)S(1)} %shard_map.102), channel_id=1, source_target_pairs={{0,4},{4,0},{8,12},{12,8},{16,20},{20,16},{24,28},{28,24},{1,5},{5... | collective-permute-start | bytes 196616 | tf_op jit(solution)/shard_map/ppermute | solution.py:430
  25.2 4.0 %collective-permute-start.7 = (bf16[32,512]{1,0:T(8,128)(2,1)S(1)}, bf16[32,512]{1,0:T(8,128)(2,1)S(1)}, u32[]{:S(2)}, u32[]{:S(2)}) collective-permute-start(bf16[32,512]{1,0:T(8,128)(2,1)S(1)} %get-tuple-element.55), channel_id=1, source_target_pairs={{0,2},{1,3},{2,0},{3,1},{4,6},{5,7},{6,4},{7,5},{8,10},{9,11},{10,... | collective-permute-start | bytes 98312 | tf_op jit(solution)/shard_map/ppermute | solution.py:380
  26.8 2.5 %collective-permute-start.5 = (bf16[32,512]{1,0:T(8,128)(2,1)S(1)}, bf16[32,512]{1,0:T(8,128)(2,1)S(1)}, u32[]{:S(2)}, u32[]{:S(2)}) collective-permute-start(bf16[32,512]{1,0:T(8,128)(2,1)S(1)} %get-tuple-element.53), channel_id=1, source_target_pairs={{0,1},{1,0},{2,3},{3,2},{4,5},{5,4},{6,7},{7,6},{8,9},{9,8},{10,11... | collective-permute-start | bytes 98312 | tf_op jit(solution)/shard_map/ppermute | solution.py:380
  26.8 4.0 %collective-permute-start.6 = (bf16[32,512]{1,0:T(8,128)(2,1)S(1)}, bf16[32,512]{1,0:T(8,128)(2,1)S(1)}, u32[]{:S(2)}, u32[]{:S(2)}) collective-permute-start(bf16[32,512]{1,0:T(8,128)(2,1)S(1)} %get-tuple-element.54), channel_id=1, source_target_pairs={{0,2},{1,3},{2,0},{3,1},{4,6},{5,7},{6,4},{7,5},{8,10},{9,11},{10,... | collective-permute-start | bytes 98312 | tf_op jit(solution)/shard_map/ppermute | solution.py:380
  29.2 1.6 %collective-permute-start.8 = (bf16[32,512]{1,0:T(8,128)(2,1)S(1)}, bf16[32,512]{1,0:T(8,128)(2,1)S(1)}, u32[]{:S(2)}, u32[]{:S(2)}) collective-permute-start(bf16[32,512]{1,0:T(8,128)(2,1)S(1)} %collective-permute-done.7), channel_id=1, source_target_pairs={{0,1},{1,0},{2,3},{3,2},{4,5},{5,4},{6,7},{7,6},{8,9},{9,8},{10,11... | collective-permute-start | bytes 98312 | tf_op jit(solution)/shard_map/ppermute | solution.py:380
  31.5 6.4 %collective-permute-start.9 = (bf16[32,2176]{1,0:T(8,128)(2,1)S(1)}, bf16[32,2176]{1,0:T(8,128)(2,1)S(1)}, u32[]{:S(2)}, u32[]{:S(2)}) collective-permute-start(bf16[32,2176]{1,0:T(8,128)(2,1)S(1)} %get-tuple-element.57.after_ref.refs_0_), channel_id=1, source_target_pairs={{0,8},{8,16},{16,24},{24,28},{28,20},{20,12},{12,4},{4,0},{1,9},{9... | collective-permute-start | bytes 417800 | tf_op jit(solution)/shard_map/ppermute | solution.py:244
  33.9 5.1 %collective-permute-start.10 = (bf16[32,2176]{1,0:T(8,128)(2,1)S(1)}, bf16[32,2176]{1,0:T(8,128)(2,1)S(1)}, u32[]{:S(2)}, u32[]{:S(2)}) collective-permute-start(bf16[32,2176]{1,0:T(8,128)(2,1)S(1)} %get-tuple-element.57.after_ref.refs_0_), channel_id=1, source_target_pairs={{0,4},{8,0},{16,8},{24,16},{28,24},{20,28},{12,20},{4,12},{1,5},{9... | collective-permute-start | bytes 417800 | tf_op jit(solution)/shard_map/ppermute | solution.py:244
  39.0 5.1 %collective-permute-start.11 = (bf16[32,2176]{1,0:T(8,128)(2,1)S(1)}, bf16[32,2176]{1,0:T(8,128)(2,1)S(1)}, u32[]{:S(2)}, u32[]{:S(2)}) collective-permute-start(bf16[32,2176]{1,0:T(8,128)(2,1)S(1)} %collective-permute-done.9.refs_1_), channel_id=1, source_target_pairs={{0,8},{8,16},{16,24},{24,28},{28,20},{20,12},{12,4},{4,0},{1,9},{9... | collective-permute-start | bytes 417800 | tf_op jit(solution)/shard_map/ppermute | solution.py:244
  40.0 5.1 %collective-permute-start.12 = (bf16[32,2176]{1,0:T(8,128)(2,1)S(1)}, bf16[32,2176]{1,0:T(8,128)(2,1)S(1)}, u32[]{:S(2)}, u32[]{:S(2)}) collective-permute-start(bf16[32,2176]{1,0:T(8,128)(2,1)S(1)} %collective-permute-done.10.refs_3_), channel_id=1, source_target_pairs={{0,4},{8,0},{16,8},{24,16},{28,24},{20,28},{12,20},{4,12},{1,5},{9... | collective-permute-start | bytes 417800 | tf_op jit(solution)/shard_map/ppermute | solution.py:244
  45.1 8.5 %collective-permute-start.13 = (bf16[32,2176]{1,0:T(8,128)(2,1)S(1)}, bf16[32,2176]{1,0:T(8,128)(2,1)S(1)}, u32[]{:S(2)}, u32[]{:S(2)}) collective-permute-start(bf16[32,2176]{1,0:T(8,128)(2,1)S(1)} %collective-permute-done.11.refs_2_), channel_id=1, source_target_pairs={{0,8},{8,16},{16,24},{24,28},{28,20},{20,12},{12,4},{4,0},{1,9},{9... | collective-permute-start | bytes 417800 | tf_op jit(solution)/shard_map/ppermute | solution.py:244
  45.6 8.1 %collective-permute-start.14 = (bf16[32,2176]{1,0:T(8,128)(2,1)S(1)}, bf16[32,2176]{1,0:T(8,128)(2,1)S(1)}, u32[]{:S(2)}, u32[]{:S(2)}) collective-permute-start(bf16[32,2176]{1,0:T(8,128)(2,1)S(1)} %collective-permute-done.12.refs_4_), channel_id=1, source_target_pairs={{0,4},{8,0},{16,8},{24,16},{28,24},{20,28},{12,20},{4,12},{1,5},{9... | collective-permute-start | bytes 417800 | tf_op jit(solution)/shard_map/ppermute | solution.py:244
  47.1 6.3 %collective-permute-start.15 = (bf16[16,2176]{1,0:T(8,128)(2,1)S(1)}, bf16[16,2176]{1,0:T(8,128)(2,1)S(1)}, u32[]{:S(2)}, u32[]{:S(2)}) collective-permute-start(bf16[16,2176]{1,0:T(8,128)(2,1)S(1)} %slice.30), channel_id=1, source_target_pairs={{0,16},{8,24},{16,28},{24,20},{28,12},{20,4},{12,0},{4,8},{1,17},{... | collective-permute-start | bytes 208904 | tf_op jit(solution)/shard_map/ppermute | solution.py:244
  48.3 5.3 %collective-permute-start.16 = (bf16[16,2176]{1,0:T(8,128)(2,1)S(1)}, bf16[16,2176]{1,0:T(8,128)(2,1)S(1)}, u32[]{:S(2)}, u32[]{:S(2)}) collective-permute-start(bf16[16,2176]{1,0:T(8,128)(2,1)S(1)} %slice.31), channel_id=1, source_target_pairs={{0,12},{8,4},{16,0},{24,8},{28,16},{20,24},{12,28},{4,20},{1,13},{... | collective-permute-start | bytes 208904 | tf_op jit(solution)/shard_map/ppermute | solution.py:244
  57.9 9.5 %collective-permute-start.17 = (bf16[32,2048]{1,0:T(8,128)(2,1)S(1)}, bf16[32,2048]{1,0:T(8,128)(2,1)S(1)}, u32[]{:S(2)}, u32[]{:S(2)}) collective-permute-start(bf16[32,2048]{1,0:T(8,128)(2,1)S(1)} %get-tuple-element.71), channel_id=1, source_target_pairs={{0,8},{8,16},{16,24},{24,28},{28,20},{20,12},{12,4},{4,0},{1,9},{9... | collective-permute-start | bytes 393224 | tf_op jit(solution)/shard_map/ppermute | solution.py:244
  59.1 8.3 %collective-permute-start.18 = (bf16[16,2048]{1,0:T(8,128)(2,1)S(1)}, bf16[16,2048]{1,0:T(8,128)(2,1)S(1)}, u32[]{:S(2)}, u32[]{:S(2)}) collective-permute-start(bf16[16,2048]{1,0:T(8,128)(2,1)S(1)} %get-tuple-element.73), channel_id=1, source_target_pairs={{0,16},{8,24},{16,28},{24,20},{28,12},{20,4},{12,0},{4,8},{1,17},{... | collective-permute-start | bytes 196616 | tf_op jit(solution)/shard_map/ppermute | solution.py:244
  65.8 6.4 %collective-permute-start.22 = (bf16[16,2048]{1,0:T(8,128)(2,1)S(1)}, bf16[16,2048]{1,0:T(8,128)(2,1)S(1)}, u32[]{:S(2)}, u32[]{:S(2)}) collective-permute-start(bf16[16,2048]{1,0:T(8,128)(2,1)S(1)} %get-tuple-element.77), channel_id=1, source_target_pairs={{0,12},{8,4},{16,0},{24,8},{28,16},{20,24},{12,28},{4,20},{1,13},{... | collective-permute-start | bytes 196616 | tf_op jit(solution)/shard_map/ppermute | solution.py:244
  66.5 7.1 %collective-permute-start.21 = (bf16[32,2048]{1,0:T(8,128)(2,1)S(1)}, bf16[32,2048]{1,0:T(8,128)(2,1)S(1)}, u32[]{:S(2)}, u32[]{:S(2)}) collective-permute-start(bf16[32,2048]{1,0:T(8,128)(2,1)S(1)} %get-tuple-element.75), channel_id=1, source_target_pairs={{0,4},{8,0},{16,8},{24,16},{28,24},{20,28},{12,20},{4,12},{1,5},{9... | collective-permute-start | bytes 393224 | tf_op jit(solution)/shard_map/ppermute | solution.py:244
  67.4 6.4 %collective-permute-start.19 = (bf16[32,2048]{1,0:T(8,128)(2,1)S(1)}, bf16[32,2048]{1,0:T(8,128)(2,1)S(1)}, u32[]{:S(2)}, u32[]{:S(2)}) collective-permute-start(bf16[32,2048]{1,0:T(8,128)(2,1)S(1)} %pad_maximum_fusion), channel_id=1, source_target_pairs={{0,8},{8,16},{16,24},{24,28},{28,20},{20,12},{12,4},{4,0},{1,9},{9... | collective-permute-start | bytes 393224 | tf_op jit(solution)/shard_map/ppermute | solution.py:244
  73.7 5.0 %collective-permute-start.23 = (bf16[32,2048]{1,0:T(8,128)(2,1)S(1)}, bf16[32,2048]{1,0:T(8,128)(2,1)S(1)}, u32[]{:S(2)}, u32[]{:S(2)}) collective-permute-start(bf16[32,2048]{1,0:T(8,128)(2,1)S(1)} %pad_maximum_fusion.1), channel_id=1, source_target_pairs={{0,4},{8,0},{16,8},{24,16},{28,24},{20,28},{12,20},{4,12},{1,5},{9... | collective-permute-start | bytes 393224 | tf_op jit(solution)/shard_map/ppermute | solution.py:244
  73.9 5.0 %collective-permute-start.20 = (bf16[32,2048]{1,0:T(8,128)(2,1)S(1)}, bf16[32,2048]{1,0:T(8,128)(2,1)S(1)}, u32[]{:S(2)}, u32[]{:S(2)}) collective-permute-start(bf16[32,2048]{1,0:T(8,128)(2,1)S(1)} %add_convert_fusion.1), channel_id=1, source_target_pairs={{0,8},{8,16},{16,24},{24,28},{28,20},{20,12},{12,4},{4,0},{1,9},{9... | collective-permute-start | bytes 393224 | tf_op jit(solution)/shard_map/ppermute | solution.py:244
  78.8 5.0 %collective-permute-start.24 = (bf16[32,2048]{1,0:T(8,128)(2,1)S(1)}, bf16[32,2048]{1,0:T(8,128)(2,1)S(1)}, u32[]{:S(2)}, u32[]{:S(2)}) collective-permute-start(bf16[32,2048]{1,0:T(8,128)(2,1)S(1)} %add_convert_fusion), channel_id=1, source_target_pairs={{0,4},{8,0},{16,8},{24,16},{28,24},{20,28},{12,20},{4,12},{1,5},{9... | collective-permute-start | bytes 393224 | tf_op jit(solution)/shard_map/ppermute | solution.py:244
  84.4 2.2 %collective-permute-start.25 = (bf16[32,512]{1,0:T(8,128)(2,1)S(1)}, bf16[32,512]{1,0:T(8,128)(2,1)S(1)}, u32[]{:S(2)}, u32[]{:S(2)}) collective-permute-start(bf16[32,512]{1,0:T(8,128)(2,1)S(1)} %get-tuple-element.80), channel_id=1, source_target_pairs={{0,1},{1,0},{2,3},{3,2},{4,5},{5,4},{6,7},{7,6},{8,9},{9,8},{10,11... | collective-permute-start | bytes 98312 | tf_op jit(solution)/shard_map/ppermute | solution.py:470
  84.5 4.1 %collective-permute-start.26 = (bf16[32,512]{1,0:T(8,128)(2,1)S(1)}, bf16[32,512]{1,0:T(8,128)(2,1)S(1)}, u32[]{:S(2)}, u32[]{:S(2)}) collective-permute-start(bf16[32,512]{1,0:T(8,128)(2,1)S(1)} %get-tuple-element.81), channel_id=1, source_target_pairs={{0,2},{1,3},{2,0},{3,1},{4,6},{5,7},{6,4},{7,5},{8,10},{9,11},{10,... | collective-permute-start | bytes 98312 | tf_op jit(solution)/shard_map/ppermute | solution.py:470
  86.6 3.3 %collective-permute-start.27 = (bf16[32,512]{1,0:T(8,128)(2,1)S(1)}, bf16[32,512]{1,0:T(8,128)(2,1)S(1)}, u32[]{:S(2)}, u32[]{:S(2)}) collective-permute-start(bf16[32,512]{1,0:T(8,128)(2,1)S(1)} %get-tuple-element.82), channel_id=1, source_target_pairs={{0,3},{1,2},{2,1},{3,0},{4,7},{5,6},{6,5},{7,4},{8,11},{9,10},{10,... | collective-permute-start | bytes 98312 | tf_op jit(solution)/shard_map/ppermute | solution.py:470

commit v6 on v5

--- a/solution.py
+++ b/solution.py
@@ -106,7 +106,7 @@
         ) + jnp.dot(low, values[:, cols], preferred_element_type=F32)
 
 
-def back_kernel(earlier, scalars, kept_ref, *refs):
+def back_kernel(earlier, scalars, sign_ref, kept_ref, *refs):
     before_refs, out_ref = refs[:earlier], refs[earlier]
     before = sum(ref[...].astype(F32) for ref in before_refs)
     extra = jnp.where(scalars[1] == 0, kept_ref[...].astype(F32), 0.0)
@@ -177,9 +177,8 @@
 
 
 def expert_kernel(blocks, scalars, in_ref, down_ref, *refs):
-    x_refs, out_refs, done_ref = refs[:blocks], refs[blocks:2 * blocks], refs[2 * blocks]
-    rows_ref, act_ref, made_ref = refs[2 * blocks + 1:]
-    done_ref[...] = jnp.zeros_like(done_ref)
+    x_refs, out_refs = refs[:blocks], refs[blocks:2 * blocks]
+    rows_ref, act_ref, made_ref = refs[2 * blocks:]
     model, units = rows_ref.shape[1], in_ref.shape[1]
     spans, packs = [], []
     first = 0
@@ -192,7 +191,7 @@
     lane = lax.broadcasted_iota(jnp.int32, pack.shape, 1)
     chosen = (lane == scalars[3]) | (lane == scalars[3] + scalars[2])
     weight = jnp.sum(jnp.where(chosen, pack, 0.0), axis=-1, keepdims=True)
-    chunk = min(units, 256)
+    chunk = min(units, 512)
 
     @pl.loop(0, units // chunk)
     def _(step):
@@ -201,7 +200,7 @@
         up = jnp.dot(rows_ref[...], in_ref[model:, cut], preferred_element_type=F32)
         act_ref[:, cut] = (gate / (1.0 + jnp.exp(-gate)) * up).astype(BF16)
 
-    wide = min(model, 512)
+    wide = min(model, 1024)
 
     @pl.loop(0, model // wide)
     def _(step):
@@ -216,9 +215,9 @@
 def run_expert(scalars, blocks, weights_in, weights_out):
     units, model = weights_out.shape
     total = sum(b.shape[0] for b in blocks)
-    *made, sign = call(
+    return call(
         functools.partial(expert_kernel, len(blocks)),
-        [shape((b.shape[0], model), BF16) for b in blocks] + [shape((8, HEAD), F32)],
+        [shape((b.shape[0], model), BF16) for b in blocks],
         [scalars, weights_in, weights_out, *blocks],
         scratch=[
             pltpu.VMEM((total, model), BF16),
@@ -226,15 +225,15 @@
             pltpu.VMEM((total, model), BF16),
         ],
         flops=6 * total * model * units,
-    )
-    return made, sign
+        limit=24 << 20,
+    )
 
 
 def ring_order(count):
     return list(range(0, count, 2)) + list(range(1, count, 2))[::-1]
 
 
-def dense_experts(block, scalars, expert_in, expert_out):
+def dense_experts(block, scalars, weights_in, expert_out):
     count = lax.axis_size("seq")
     order = ring_order(count)
     half = block.shape[0] // 2
@@ -245,25 +244,19 @@
             rows, "seq", [(order[p], order[(p + steps) % count]) for p in range(count)]
         )
 
-    weights = [expert_in.reshape(-1, expert_in.shape[-1]), expert_out]
-    near, after = [], block
     ahead, behind = [block], [block]
     for distance in range(1, far):
         came, went = hop(ahead[-1], 1), hop(behind[-1], -1)
-        if weights:
-            loaded, sign = load_near(scalars, weights.pop(0), after)
-            near.append(loaded)
-            came, went, after = lax.optimization_barrier((came, went, sign))
+        if distance == 1:
+            weights_out, sign = load_near(scalars, expert_out, block)
+            came, went, sign = lax.optimization_barrier((came, went, sign))
         ahead.append(came)
         behind.append(went)
     top = hop(ahead[-2][:half], 2)
     bottom = hop(behind[-2][half:], -2)
-    (own, *close), sign = run_expert(scalars, ahead[:-1] + behind[1:-1], *near)
-    last, first, top, bottom, _ = lax.optimization_barrier(
-        (ahead[-1], behind[-1], top, bottom, sign)
-    )
-    (last, first, top, bottom), _ = run_expert(scalars, [last, first, top, bottom], *near)
-    to_back, to_front = close[:far - 2] + [last], close[far - 2:] + [first]
+    made = run_expert(scalars, ahead + behind[1:] + [top, bottom], weights_in, weights_out)
+    own, to_back, to_front = made[0], made[1:far], made[far:2 * far - 1]
+    top, bottom = made[-2:]
     early_going, early_coming = hop(bottom, 2), hop(top, -2)
     going, coming = hop(to_front[-1], 1), hop(to_back[-1], -1)
     for distance in range(far - 2, 0, -1):
@@ -297,16 +290,6 @@
         out_ref[...] = (hidden_ref[:, cols].astype(F32) + mixed).astype(BF16)
 
 
-def join_kernel(scalars, *refs):
-    pieces, out_ref, sems = refs[:-2], refs[-2], refs[-1]
-    count = pieces[0].shape[0]
-    pairs = []
-    for j, piece in enumerate(pieces):
-        rows = pl.ds(pl.multiple_of((scalars[0] ^ j) * count, count), count)
-        pairs.append((piece, out_ref.at[rows, :]))
-    run_copies(pairs, sems)
-
-
 def slot_ids(block_routes, expert_count, capacity):
     row_count, top_count = block_routes.shape
     expert_ids = jnp.arange(expert_count, dtype=jnp.int32)
@@ -360,7 +343,7 @@
     pairs = count // 2
     running = add_rows(kept, partner)
     if pairs <= 4:
-        return [pass_on(running, distance) for distance in reversed(range(1, pairs))]
+        return [pass_on(running, distance) for distance in range(1, pairs)]
     terms = []
     distance = 1
     while distance < pairs:
@@ -370,18 +353,12 @@
     return terms
 
 
-def spread_rows(pieces):
+def exchange(pieces):
     parts = len(pieces)
-    bit = parts // 2
-    held = {(j, 0): piece for j, piece in enumerate(pieces)}
-    while bit:
-        for (target, source), piece in list(held.items()):
-            if target & bit:
-                came = lax.ppermute(piece, "exp", [(i, i ^ bit) for i in range(parts)])
-                held[(target ^ bit, source ^ bit)] = came
-                del held[(target, source)]
-        bit //= 2
-    return [held[(0, j)] for j in range(parts)]
+    return [pieces[0]] + [
+        lax.ppermute(pieces[j], "exp", [(i, i ^ j) for i in range(parts)])
+        for j in range(1, parts)
+    ]
 
 
 def per_device(
@@ -424,8 +401,14 @@
         flops=6 * rows * rows * width,
     )
     before = prior_states(kept, partner)
+    dense = routes.shape[1] == experts
+    sign = jnp.zeros((8, HEAD), F32)
+    if dense:
+        weights_in, sign = load_near(
+            scalars, expert_in.reshape(-1, expert_in.shape[-1]), partner
+        )
     [lacked] = call(
-        functools.partial(back_kernel, len(before)), [state], [scalars, kept, *before]
+        functools.partial(back_kernel, len(before)), [state], [scalars, sign, kept, *before]
     )
     other = lax.ppermute(lacked, "seq", swap)
     pieces = call(
@@ -435,7 +418,7 @@
         scratch=[pltpu.VMEM((rows, width), BF16)],
         flops=4 * rows * width * HEAD,
     )
-    gathered = spread_rows(pieces)
+    gathered = exchange(pieces)
 
     my_routes = lax.dynamic_slice_in_dim(routes, my_index * count, count, 0)
     my_gates = lax.dynamic_slice_in_dim(route_gates, my_index * count, count, 0)
@@ -457,8 +440,8 @@
         [shape((count, model), BF16), shape((count, model + lanes), BF16)],
         [scalars, my_norm, pack] + gathered,
     )
-    if routes.shape[1] == experts:
-        terms = dense_experts(block, scalars, expert_in[0], expert_out[0])
+    if dense:
+        terms = dense_experts(block, scalars, weights_in, expert_out[0])
     else:
         mixed = routed_experts(block[:, :model], my_routes, my_gates, expert_in, expert_out)
         nothing = jnp.zeros_like(mixed)
@@ -466,15 +449,14 @@
     ready = call(
         mix_kernel, [shape((count, width), BF16)] * parts, [scalars, hidden, *terms]
     )
-    returned = [ready[0]] + [
-        lax.ppermute(ready[j], "exp", [(i, i ^ j) for i in range(parts)])
-        for j in range(1, parts)
-    ]
-    [out] = call(
-        join_kernel, [shape((rows, width), BF16)], [scalars] + returned, out_specs=[FAR],
-        scratch=[pltpu.SemaphoreType.DMA((parts,))],
-    )
-    return out
+    returned = exchange(ready)
+    order = list(range(parts))
+    bit = 1
+    while bit < parts:
+        turn = (my_index & bit) != 0
+        returned = [jnp.where(turn, returned[i ^ bit], returned[i]) for i in order]
+        bit *= 2
+    return jnp.concatenate(returned)
 
 
 def solution(mesh):

time: 91.4 us -> 86.3 us (0.944)
  Pallas kernels: 23.4 us -> 18.1 us
  starting transfers between devices: 36.6 us -> 34 us
  waiting for transfers between devices: 29.6 us -> 31.7 us
    pallas_call x11 -> x9, Pallas kernels: 23.4 us -> 18.1 us  [call(): pl.pallas_call(kernel, out_shape=outs, in_specs=[SCALAR if i == 0 or i in...]
    ppermute x16, waiting for transfers between devices: 18 us -> 23 us  [hop(): lax.ppermute(rows, 'seq', [(order[p], order[(p + steps) % count]) for p i...]
    ppermute x16, starting transfers between devices: 17.9 us -> 15.7 us  [hop(): lax.ppermute(rows, 'seq', [(order[p], order[(p + steps) % count]) for p i...]
    ppermute x7 -> x6, waiting for transfers between devices: 6.6 us -> 5.4 us  [exchange(): lax.ppermute(pieces[j], 'exp', [(i, i ^ j) for i in range(parts)])]
    ppermute x3, waiting for transfers between devices: 1.12 us -> 0.01 us  [pass_on(): lax.ppermute(state, 'seq', [(i, i + 2 * distance) for i in range(count -...]
    ppermute x7 -> x6, starting transfers between devices: 4.37 us -> 3.85 us  [exchange(): lax.ppermute(pieces[j], 'exp', [(i, i ^ j) for i in range(parts)])]
  transfers between devices with their start and end apart: 28 -> 27, of which waited for: 15 -> 16; matrix products, arithmetic and copies ran while one was open for 1% -> 1% of each run, Pallas kernels for 14% -> 10%
where the time goes in v6:
time: 86.3 us; the launch traced here: 86 us
  starting transfers between devices  34 us (39%)
  waiting for transfers between devices  31.7 us (37%)
  Pallas kernels  18.1 us (21%)
  other arithmetic  1.05 us (1%)
  local copies, waits for them, and re-layouts  1 us (1%)
    ppermute x16, waiting for transfers between devices, hop(): lax.ppermute(rows, 'seq', [(order[p], order[(p + steps) % count]) for p i...  23 us
    pallas_call x9, Pallas kernels, call(): pl.pallas_call(kernel, out_shape=outs, in_specs=[SCALAR if i == 0 or i in...  18.1 us
    ppermute x16, starting transfers between devices, hop(): lax.ppermute(rows, 'seq', [(order[p], order[(p + steps) % count]) for p i...  15.7 us
    ppermute x3, starting transfers between devices, pass_on(): lax.ppermute(state, 'seq', [(i, i + 2 * distance) for i in range(count -...  9.8 us
    ppermute x6, waiting for transfers between devices, exchange(): lax.ppermute(pieces[j], 'exp', [(i, i ^ j) for i in range(parts)])  5.4 us
    ppermute x6, starting transfers between devices, exchange(): lax.ppermute(pieces[j], 'exp', [(i, i ^ j) for i in range(parts)])  3.85 us
    ppermute x1, starting transfers between devices, per_device(): partner = lax.ppermute(given, 'seq', swap)  3 us
    ppermute x1, waiting for transfers between devices, per_device(): other = lax.ppermute(lacked, 'seq', swap)  1.82 us
  transfers between devices with their start and end apart: 27, of which 16 were waited for; matrix products, arithmetic and copies ran while one was open for 1% of the time, Pallas kernels for 10%

profile of v6, /device:TPU:0, one launch (start us, length us, event | category | flops | bytes accessed | tf_op | source)
XLA Modules:
  0.0 86.0 jit_solution(6906475624359870656)
XLA Ops:
  0.0 0.1 pad_add_fusion.scalars
  0.1 2.3 %shard_map.100 = (bf16[128,256]{1,0:T(8,128)(2,1)S(1)}, bf16[128,256]{1,0:T(8,128)(2,1)S(1)}, bf16[128,512]{1,0:T(8,128)(2,1)S(1)}, bf16[128,512]{1,0:T(8,128)(2...) custom-call(s32[4]{0:T(128)S(1)} %pad_add_fusion.scalars, ...), custom_call_target="tpu_custom_call" | custom-call | flops 16777216 | bytes 1200144 | tf_op jit(solution)/shard_map/pallas_call | solution.py:24
  2.4 3.0 %collective-permute-start = (bf16[128,256]{1,0:T(8,128)(2,1)S(1)}, bf16[128,256]{1,0:T(8,128)(2,1)S(1)}, u32[]{:S(2)}, u32[]{:S(2)}) collective-permute-start(bf16[128,256]{1,0:T(8,128)(2,1)S(1)} %get-tuple-element.43), channel_id=1, source_target_pairs={{0,4},{4,0},{8,12},{12,8},{16,20},{20,16},{24,28},{28,24},{1,5},{5... | collective-permute-start | bytes 196616 | tf_op jit(solution)/shard_map/ppermute | solution.py:398
  5.4 0.1 constant_dynamic-slice_fusion
  5.5 0.8 constant_dynamic-slice_fusion.1
  6.2 1.4 %collective-permute-done.after_ref.partner_ref = bf16[128,256]{1,0:T(8,128)(2,1)S(1)} collective-permute-done((bf16[128,256]{1,0:T(8,128)(2,1)S(1)}, bf16[128,256]{1,0:T(8,128)(2,1)S(1)}, u32[]{:S(2)}, u32[]{:S(2)}) %collective-permute-start) | collective-permute-done | bytes 65568 | tf_op jit(solution)/shard_map/ppermute | solution.py:398
  7.7 4.0 %collective-permute-start.1 = (bf16[128,256]{1,0:T(8,128)(2,1)S(1)}, bf16[128,256]{1,0:T(8,128)(2,1)S(1)}, u32[]{:S(2)}, u32[]{:S(2)}) collective-permute-start(bf16[128,256]{1,0:T(8,128)(2,1)S(1)} %add_convert_fusion.6), channel_id=1, source_target_pairs={{0,8},{4,12},{8,16},{12,20},{16,24},{20,28},{1,9},{5,13},{9,17},{1... | collective-permute-start | bytes 196616 | tf_op jit(solution)/shard_map/ppermute | solution.py:339
  11.7 4.5 %collective-permute-start.2 = (bf16[128,256]{1,0:T(8,128)(2,1)S(1)}, bf16[128,256]{1,0:T(8,128)(2,1)S(1)}, u32[]{:S(2)}, u32[]{:S(2)}) collective-permute-start(bf16[128,256]{1,0:T(8,128)(2,1)S(1)} %add_convert_fusion.6), channel_id=1, source_target_pairs={{0,16},{4,20},{8,24},{12,28},{1,17},{5,21},{9,25},{13,29},{2,18},{... | collective-permute-start | bytes 196616 | tf_op jit(solution)/shard_map/ppermute | solution.py:339
  16.2 1.3 %collective-permute-start.3 = (bf16[128,256]{1,0:T(8,128)(2,1)S(1)}, bf16[128,256]{1,0:T(8,128)(2,1)S(1)}, u32[]{:S(2)}, u32[]{:S(2)}) collective-permute-start(bf16[128,256]{1,0:T(8,128)(2,1)S(1)} %add_convert_fusion.6), channel_id=1, source_target_pairs={{0,24},{4,28},{1,25},{5,29},{2,26},{6,30},{3,27},{7,31}} | collective-permute-start | bytes 196616 | tf_op jit(solution)/shard_map/ppermute | solution.py:339
  17.5 0.1 copy.16
  17.6 0.1 copy.15
  17.7 4.0 %shard_map.102 = (bf16[4096,1024]{1,0:T(8,128)(2,1)S(1)}, f32[8,128]{1,0:T(8,128)S(1)}) custom-call(s32[4]{0:T(128)S(1)} %pad_add_fusion.scalars, bf16[4096,1024]{1,0:T(8,128)(2,1)} %bitcast.7, bf16[128,256]{1,0:T(8,128)(2,1)S(1)} %collective-permute-done.after_ref.partner_ref), custom_call_target="tpu_custom_call" | custom-call | bytes 16846864 | tf_op jit(solution)/shard_map/pallas_call | solution.py:24
  21.7 0.0 collective-permute-done.1.refs_0_
  21.7 0.0 collective-permute-done.3.refs_2_
  21.7 0.6 shard_map.103
  22.3 1.6 %collective-permute-start.4 = (bf16[128,256]{1,0:T(8,128)(2,1)S(1)}, bf16[128,256]{1,0:T(8,128)(2,1)S(1)}, u32[]{:S(2)}, u32[]{:S(2)}) collective-permute-start(bf16[128,256]{1,0:T(8,128)(2,1)S(1)} %shard_map.103), channel_id=1, source_target_pairs={{0,4},{4,0},{8,12},{12,8},{16,20},{20,16},{24,28},{28,24},{1,5},{5... | collective-permute-start | bytes 196616 | tf_op jit(solution)/shard_map/ppermute | solution.py:413
  23.9 0.9 %shard_map.101.within_ref = f32[128,512]{1,0:T(8,128)S(1)} custom-call(s32[4]{0:T(128)S(1)} %pad_add_fusion.scalars, bf16[128,512]{1,0:T(8,128)(2,1)S(1)} %get-tuple-element.38.keys, bf16[128,512]{1,0:T(8,128)(2,1)S(1)} %get-tuple-element.39.values, bf16[128,512]{1,0:T(8,128)(2,1)S(1)} %get-tuple-element.40.queries), custom_call_target="tpu_custom_call" | custom-call | flops 50331648 | bytes 655376 | tf_op jit(solution)/shard_map/pallas_call | solution.py:24
  24.8 1.8 %collective-permute-done.4.other_ref = bf16[128,256]{1,0:T(8,128)(2,1)S(1)} collective-permute-done((bf16[128,256]{1,0:T(8,128)(2,1)S(1)}, bf16[128,256]{1,0:T(8,128)(2,1)S(1)}, u32[]{:S(2)}, u32[]{:S(2)}) %collective-permute-start.4) | collective-permute-done | bytes 65568 | tf_op jit(solution)/shard_map/ppermute | solution.py:413
  26.7 0.9 %shard_map.104 = (bf16[32,512]{1,0:T(8,128)(2,1)S(1)}, bf16[32,512]{1,0:T(8,128)(2,1)S(1)}, bf16[32,512]{1,0:T(8,128)(2,1)S(1)}, bf16[32,512]{1,0:T(8,128)(2,1)S(1)}) custom-call(s32[4]{0:T(128)S(1)} %pad_add_fusion.scalars, f32[128,512]{1,0:T(8,128)S(1)} %shard_map.101.within_ref, bf16[128,512]{1,0:T(8,128)(2,1)S(1)} %get-tuple-element.40.queries, ...), custom_call_target="tpu_custom_call" | custom-call | flops 33554432 | bytes 985104 | tf_op jit(solution)/shard_map/pallas_call | solution.py:24
  27.6 0.1 collective-permute-start.5
  27.7 1.6 %collective-permute-start.6 = (bf16[32,512]{1,0:T(8,128)(2,1)S(1)}, bf16[32,512]{1,0:T(8,128)(2,1)S(1)}, u32[]{:S(2)}, u32[]{:S(2)}) collective-permute-start(bf16[32,512]{1,0:T(8,128)(2,1)S(1)} %get-tuple-element.48), channel_id=1, source_target_pairs={{0,2},{1,3},{2,0},{3,1},{4,6},{5,7},{6,4},{7,5},{8,10},{9,11},{10,... | collective-permute-start | bytes 98312 | tf_op jit(solution)/shard_map/ppermute | solution.py:359
  29.3 0.3 collective-permute-start.7
  29.5 0.1 fusion.2.pack_ref
  29.6 2.0 %collective-permute-done.6.refs_2_ = bf16[32,512]{1,0:T(8,128)(2,1)S(1)} collective-permute-done((bf16[32,512]{1,0:T(8,128)(2,1)S(1)}, bf16[32,512]{1,0:T(8,128)(2,1)S(1)}, u32[]{:S(2)}, u32[]{:S(2)}) %collective-permute-start.6) | collective-permute-done | bytes 32800 | tf_op jit(solution)/shard_map/ppermute | solution.py:359
  31.6 0.9 %collective-permute-done.7.refs_3_ = bf16[32,512]{1,0:T(8,128)(2,1)S(1)} collective-permute-done((bf16[32,512]{1,0:T(8,128)(2,1)S(1)}, bf16[32,512]{1,0:T(8,128)(2,1)S(1)}, u32[]{:S(2)}, u32[]{:S(2)}) %collective-permute-start.7) | collective-permute-done | bytes 32800 | tf_op jit(solution)/shard_map/ppermute | solution.py:359
  32.6 0.7 shard_map.105
  33.3 0.1 collective-permute-start.8
  33.3 2.0 %collective-permute-start.9 = (bf16[32,2176]{1,0:T(8,128)(2,1)S(1)}, bf16[32,2176]{1,0:T(8,128)(2,1)S(1)}, u32[]{:S(2)}, u32[]{:S(2)}) collective-permute-start(bf16[32,2176]{1,0:T(8,128)(2,1)S(1)} %get-tuple-element.52.after_ref.refs_0_), channel_id=1, source_target_pairs={{0,4},{8,0},{16,8},{24,16},{28,24},{20,28},{12,20},{4,12},{1,5},{9... | collective-permute-start | bytes 417800 | tf_op jit(solution)/shard_map/ppermute | solution.py:243
  35.4 3.7 %collective-permute-done.8.refs_1_ = bf16[32,2176]{1,0:T(8,128)(2,1)S(1)} collective-permute-done((bf16[32,2176]{1,0:T(8,128)(2,1)S(1)}, bf16[32,2176]{1,0:T(8,128)(2,1)S(1)}, u32[]{:S(2)}, u32[]{:S(2)}) %collective-permute-start.8) | collective-permute-done | bytes 139296 | tf_op jit(solution)/shard_map/ppermute | solution.py:243
  39.1 0.1 collective-permute-done.9.refs_4_
  39.1 0.8 collective-permute-start.10
  40.0 1.2 %collective-permute-start.12 = (bf16[32,2176]{1,0:T(8,128)(2,1)S(1)}, bf16[32,2176]{1,0:T(8,128)(2,1)S(1)}, u32[]{:S(2)}, u32[]{:S(2)}) collective-permute-start(bf16[32,2176]{1,0:T(8,128)(2,1)S(1)} %collective-permute-done.9.refs_4_), channel_id=1, source_target_pairs={{0,4},{8,0},{16,8},{24,16},{28,24},{20,28},{12,20},{4,12},{1,5},{9... | collective-permute-start | bytes 417800 | tf_op jit(solution)/shard_map/ppermute | solution.py:243
  41.2 3.0 %collective-permute-done.10.refs_2_ = bf16[32,2176]{1,0:T(8,128)(2,1)S(1)} collective-permute-done((bf16[32,2176]{1,0:T(8,128)(2,1)S(1)}, bf16[32,2176]{1,0:T(8,128)(2,1)S(1)}, u32[]{:S(2)}, u32[]{:S(2)}) %collective-permute-start.10) | collective-permute-done | bytes 139296 | tf_op jit(solution)/shard_map/ppermute | solution.py:243
  44.2 0.8 collective-permute-start.11
  45.0 0.0 collective-permute-done.12.refs_5_
  45.0 1.2 %collective-permute-start.13 = (bf16[32,2176]{1,0:T(8,128)(2,1)S(1)}, bf16[32,2176]{1,0:T(8,128)(2,1)S(1)}, u32[]{:S(2)}, u32[]{:S(2)}) collective-permute-start(bf16[32,2176]{1,0:T(8,128)(2,1)S(1)} %collective-permute-done.12.refs_5_), channel_id=1, source_target_pairs={{0,4},{8,0},{16,8},{24,16},{28,24},{20,28},{12,20},{4,12},{1,5},{9... | collective-permute-start | bytes 417800 | tf_op jit(solution)/shard_map/ppermute | solution.py:243
  46.2 2.0 %collective-permute-start.14 = (bf16[16,2176]{1,0:T(8,128)(2,1)S(1)}, bf16[16,2176]{1,0:T(8,128)(2,1)S(1)}, u32[]{:S(2)}, u32[]{:S(2)}) collective-permute-start(bf16[16,2176]{1,0:T(8,128)(2,1)S(1)} %slice.40), channel_id=1, source_target_pairs={{0,16},{8,24},{16,28},{24,20},{28,12},{20,4},{12,0},{4,8},{1,17},{... | collective-permute-start | bytes 208904 | tf_op jit(solution)/shard_map/ppermute | solution.py:243
  48.3 0.9 %collective-permute-start.15 = (bf16[16,2176]{1,0:T(8,128)(2,1)S(1)}, bf16[16,2176]{1,0:T(8,128)(2,1)S(1)}, u32[]{:S(2)}, u32[]{:S(2)}) collective-permute-start(bf16[16,2176]{1,0:T(8,128)(2,1)S(1)} %slice.41), channel_id=1, source_target_pairs={{0,12},{8,4},{16,0},{24,8},{28,16},{20,24},{12,28},{4,20},{1,13},{... | collective-permute-start | bytes 208904 | tf_op jit(solution)/shard_map/ppermute | solution.py:243
  49.2 3.3 %shard_map.106 = (bf16[1024,2048]{1,0:T(8,128)(2,1)S(1)}, f32[8,128]{1,0:T(8,128)}) custom-call(s32[4]{0:T(128)S(1)} %pad_add_fusion.scalars, bf16[1024,2048]{1,0:T(8,128)(2,1)} %bitcast.8, bf16[32,2176]{1,0:T(8,128)(2,1)S(1)} %get-tuple-element.52.after_ref.refs_0_), custom_call_target="tpu_custom_call" | custom-call | bytes 8531984 | tf_op jit(solution)/shard_map/pallas_call | solution.py:24
  52.5 0.9 %collective-permute-done.15.refs_8_ = bf16[16,2176]{1,0:T(8,128)(2,1)S(1)} collective-permute-done((bf16[16,2176]{1,0:T(8,128)(2,1)S(1)}, bf16[16,2176]{1,0:T(8,128)(2,1)S(1)}, u32[]{:S(2)}, u32[]{:S(2)}) %collective-permute-start.15) | collective-permute-done | bytes 69664 | tf_op jit(solution)/shard_map/ppermute | solution.py:243
  53.5 0.0 collective-permute-done.11.refs_3_
  53.5 0.0 collective-permute-done.13.refs_6_
  53.5 4.7 %shard_map.107 = (bf16[32,2048]{1,0:T(8,128)(2,1)S(1)}, bf16[32,2048]{1,0:T(8,128)(2,1)S(1)}, bf16[32,2048]{1,0:T(8,128)(2,1)S(1)}, bf16[32,2048]{1,0:T(8,128)(2...) custom-call(s32[4]{0:T(128)S(1)} %pad_add_fusion.scalars, ...), custom_call_target="tpu_custom_call" | custom-call | flops 3221225472 | bytes 14745616 | tf_op jit(solution)/shard_map/pallas_call | solution.py:24
  58.2 0.8 collective-permute-start.20
  59.0 1.9 %collective-permute-start.21 = (bf16[16,2048]{1,0:T(8,128)(2,1)S(1)}, bf16[16,2048]{1,0:T(8,128)(2,1)S(1)}, u32[]{:S(2)}, u32[]{:S(2)}) collective-permute-start(bf16[16,2048]{1,0:T(8,128)(2,1)S(1)} %get-tuple-element.63), channel_id=1, source_target_pairs={{0,12},{8,4},{16,0},{24,8},{28,16},{20,24},{12,28},{4,20},{1,13},{... | collective-permute-start | bytes 196616 | tf_op jit(solution)/shard_map/ppermute | solution.py:243
  60.9 1.1 %collective-permute-start.16 = (bf16[32,2048]{1,0:T(8,128)(2,1)S(1)}, bf16[32,2048]{1,0:T(8,128)(2,1)S(1)}, u32[]{:S(2)}, u32[]{:S(2)}) collective-permute-start(bf16[32,2048]{1,0:T(8,128)(2,1)S(1)} %get-tuple-element.57), channel_id=1, source_target_pairs={{0,8},{8,16},{16,24},{24,28},{28,20},{20,12},{12,4},{4,0},{1,9},{9... | collective-permute-start | bytes 393224 | tf_op jit(solution)/shard_map/ppermute | solution.py:243
  62.0 1.2 %collective-permute-start.17 = (bf16[16,2048]{1,0:T(8,128)(2,1)S(1)}, bf16[16,2048]{1,0:T(8,128)(2,1)S(1)}, u32[]{:S(2)}, u32[]{:S(2)}) collective-permute-start(bf16[16,2048]{1,0:T(8,128)(2,1)S(1)} %get-tuple-element.59), channel_id=1, source_target_pairs={{0,16},{8,24},{16,28},{24,20},{28,12},{20,4},{12,0},{4,8},{1,17},{... | collective-permute-start | bytes 196616 | tf_op jit(solution)/shard_map/ppermute | solution.py:243
  63.2 2.8 %collective-permute-done.21 = bf16[16,2048]{1,0:T(8,128)(2,1)S(1)} collective-permute-done((bf16[16,2048]{1,0:T(8,128)(2,1)S(1)}, bf16[16,2048]{1,0:T(8,128)(2,1)S(1)}, u32[]{:S(2)}, u32[]{:S(2)}) %collective-permute-start.21) | collective-permute-done | bytes 65568 | tf_op jit(solution)/shard_map/ppermute | solution.py:243
  66.1 0.7 collective-permute-start.22
  66.8 3.4 %collective-permute-done.17 = bf16[16,2048]{1,0:T(8,128)(2,1)S(1)} collective-permute-done((bf16[16,2048]{1,0:T(8,128)(2,1)S(1)}, bf16[16,2048]{1,0:T(8,128)(2,1)S(1)}, u32[]{:S(2)}, u32[]{:S(2)}) %collective-permute-start.17) | collective-permute-done | bytes 65568 | tf_op jit(solution)/shard_map/ppermute | solution.py:243
  70.3 0.1 collective-permute-start.18
  70.4 1.2 %collective-permute-done.22 = bf16[32,2048]{1,0:T(8,128)(2,1)S(1)} collective-permute-done((bf16[32,2048]{1,0:T(8,128)(2,1)S(1)}, bf16[32,2048]{1,0:T(8,128)(2,1)S(1)}, u32[]{:S(2)}, u32[]{:S(2)}) %collective-permute-start.22) | collective-permute-done | bytes 131104 | tf_op jit(solution)/shard_map/ppermute | solution.py:243
  71.7 0.8 collective-permute-start.23
  72.5 2.8 %collective-permute-done.18 = bf16[32,2048]{1,0:T(8,128)(2,1)S(1)} collective-permute-done((bf16[32,2048]{1,0:T(8,128)(2,1)S(1)}, bf16[32,2048]{1,0:T(8,128)(2,1)S(1)}, u32[]{:S(2)}, u32[]{:S(2)}) %collective-permute-start.18) | collective-permute-done | bytes 131104 | tf_op jit(solution)/shard_map/ppermute | solution.py:243
  75.4 0.1 collective-permute-start.19
  75.4 1.2 %collective-permute-done.23.c_ref = bf16[32,2048]{1,0:T(8,128)(2,1)S(1)} collective-permute-done((bf16[32,2048]{1,0:T(8,128)(2,1)S(1)}, bf16[32,2048]{1,0:T(8,128)(2,1)S(1)}, u32[]{:S(2)}, u32[]{:S(2)}) %collective-permute-start.23) | collective-permute-done | bytes 131104 | tf_op jit(solution)/shard_map/ppermute | solution.py:243
  76.7 3.7 %collective-permute-done.19.b_ref = bf16[32,2048]{1,0:T(8,128)(2,1)S(1)} collective-permute-done((bf16[32,2048]{1,0:T(8,128)(2,1)S(1)}, bf16[32,2048]{1,0:T(8,128)(2,1)S(1)}, u32[]{:S(2)}, u32[]{:S(2)}) %collective-permute-start.19) | collective-permute-done | bytes 131104 | tf_op jit(solution)/shard_map/ppermute | solution.py:243
  80.4 0.6 shard_map.108
  81.0 0.1 collective-permute-start.24
  81.1 0.9 %collective-permute-start.25 = (bf16[32,512]{1,0:T(8,128)(2,1)S(1)}, bf16[32,512]{1,0:T(8,128)(2,1)S(1)}, u32[]{:S(2)}, u32[]{:S(2)}) collective-permute-start(bf16[32,512]{1,0:T(8,128)(2,1)S(1)} %get-tuple-element.66), channel_id=1, source_target_pairs={{0,2},{1,3},{2,0},{3,1},{4,6},{5,7},{6,4},{7,5},{8,10},{9,11},{10,... | collective-permute-start | bytes 98312 | tf_op jit(solution)/shard_map/ppermute | solution.py:359
  82.0 0.9 %collective-permute-start.26 = (bf16[32,512]{1,0:T(8,128)(2,1)S(1)}, bf16[32,512]{1,0:T(8,128)(2,1)S(1)}, u32[]{:S(2)}, u32[]{:S(2)}) collective-permute-start(bf16[32,512]{1,0:T(8,128)(2,1)S(1)} %get-tuple-element.67), channel_id=1, source_target_pairs={{0,1},{1,0},{2,3},{3,2},{4,5},{5,4},{6,7},{7,6},{8,9},{9,8},{10,11... | collective-permute-start | bytes 98312 | tf_op jit(solution)/shard_map/ppermute | solution.py:359
  82.9 1.5 %collective-permute-done.24 = bf16[32,512]{1,0:T(8,128)(2,1)S(1)} collective-permute-done((bf16[32,512]{1,0:T(8,128)(2,1)S(1)}, bf16[32,512]{1,0:T(8,128)(2,1)S(1)}, u32[]{:S(2)}, u32[]{:S(2)}) %collective-permute-start.24) | collective-permute-done | bytes 32800 | tf_op jit(solution)/shard_map/ppermute | solution.py:359
  84.4 0.9 %collective-permute-done.25 = bf16[32,512]{1,0:T(8,128)(2,1)S(1)} collective-permute-done((bf16[32,512]{1,0:T(8,128)(2,1)S(1)}, bf16[32,512]{1,0:T(8,128)(2,1)S(1)}, u32[]{:S(2)}, u32[]{:S(2)}) %collective-permute-start.25) | collective-permute-done | bytes 32800 | tf_op jit(solution)/shard_map/ppermute | solution.py:359
  85.4 0.7 pad_maximum_fusion.2
  (21 shorter events, 0.3 us)
Async XLA Ops:
  0.0 5.4 %copy-start = (f32[128,8]{0,1:T(8,128)S(1)}, f32[128,8]{0,1:T(8,128)}, u32[]{:S(2)}) copy-start(f32[128,8]{0,1:T(8,128)} %param.17) | copy-start | bytes 12292
  2.4 5.2 %collective-permute-start = (bf16[128,256]{1,0:T(8,128)(2,1)S(1)}, bf16[128,256]{1,0:T(8,128)(2,1)S(1)}, u32[]{:S(2)}, u32[]{:S(2)}) collective-permute-start(bf16[128,256]{1,0:T(8,128)(2,1)S(1)} %get-tuple-element.43), channel_id=1, source_target_pairs={{0,4},{4,0},{8,12},{12,8},{16,20},{20,16},{24,28},{28,24},{1,5},{5... | collective-permute-start | bytes 196616 | tf_op jit(solution)/shard_map/ppermute | solution.py:398
  7.7 14.0 %collective-permute-start.1 = (bf16[128,256]{1,0:T(8,128)(2,1)S(1)}, bf16[128,256]{1,0:T(8,128)(2,1)S(1)}, u32[]{:S(2)}, u32[]{:S(2)}) collective-permute-start(bf16[128,256]{1,0:T(8,128)(2,1)S(1)} %add_convert_fusion.6), channel_id=1, source_target_pairs={{0,8},{4,12},{8,16},{12,20},{16,24},{20,28},{1,9},{5,13},{9,17},{1... | collective-permute-start | bytes 196616 | tf_op jit(solution)/shard_map/ppermute | solution.py:339
  11.7 10.0 %collective-permute-start.2 = (bf16[128,256]{1,0:T(8,128)(2,1)S(1)}, bf16[128,256]{1,0:T(8,128)(2,1)S(1)}, u32[]{:S(2)}, u32[]{:S(2)}) collective-permute-start(bf16[128,256]{1,0:T(8,128)(2,1)S(1)} %add_convert_fusion.6), channel_id=1, source_target_pairs={{0,16},{4,20},{8,24},{12,28},{1,17},{5,21},{9,25},{13,29},{2,18},{... | collective-permute-start | bytes 196616 | tf_op jit(solution)/shard_map/ppermute | solution.py:339
  16.2 5.5 %collective-permute-start.3 = (bf16[128,256]{1,0:T(8,128)(2,1)S(1)}, bf16[128,256]{1,0:T(8,128)(2,1)S(1)}, u32[]{:S(2)}, u32[]{:S(2)}) collective-permute-start(bf16[128,256]{1,0:T(8,128)(2,1)S(1)} %add_convert_fusion.6), channel_id=1, source_target_pairs={{0,24},{4,28},{1,25},{5,29},{2,26},{6,30},{3,27},{7,31}} | collective-permute-start | bytes 196616 | tf_op jit(solution)/shard_map/ppermute | solution.py:339
  22.3 4.3 %collective-permute-start.4 = (bf16[128,256]{1,0:T(8,128)(2,1)S(1)}, bf16[128,256]{1,0:T(8,128)(2,1)S(1)}, u32[]{:S(2)}, u32[]{:S(2)}) collective-permute-start(bf16[128,256]{1,0:T(8,128)(2,1)S(1)} %shard_map.103), channel_id=1, source_target_pairs={{0,4},{4,0},{8,12},{12,8},{16,20},{20,16},{24,28},{28,24},{1,5},{5... | collective-permute-start | bytes 196616 | tf_op jit(solution)/shard_map/ppermute | solution.py:413
  27.6 2.0 %collective-permute-start.5 = (bf16[32,512]{1,0:T(8,128)(2,1)S(1)}, bf16[32,512]{1,0:T(8,128)(2,1)S(1)}, u32[]{:S(2)}, u32[]{:S(2)}) collective-permute-start(bf16[32,512]{1,0:T(8,128)(2,1)S(1)} %get-tuple-element.47), channel_id=1, source_target_pairs={{0,1},{1,0},{2,3},{3,2},{4,5},{5,4},{6,7},{7,6},{8,9},{9,8},{10,11... | collective-permute-start | bytes 98312 | tf_op jit(solution)/shard_map/ppermute | solution.py:359
  27.7 4.0 %collective-permute-start.6 = (bf16[32,512]{1,0:T(8,128)(2,1)S(1)}, bf16[32,512]{1,0:T(8,128)(2,1)S(1)}, u32[]{:S(2)}, u32[]{:S(2)}) collective-permute-start(bf16[32,512]{1,0:T(8,128)(2,1)S(1)} %get-tuple-element.48), channel_id=1, source_target_pairs={{0,2},{1,3},{2,0},{3,1},{4,6},{5,7},{6,4},{7,5},{8,10},{9,11},{10,... | collective-permute-start | bytes 98312 | tf_op jit(solution)/shard_map/ppermute | solution.py:359
  29.3 3.3 %collective-permute-start.7 = (bf16[32,512]{1,0:T(8,128)(2,1)S(1)}, bf16[32,512]{1,0:T(8,128)(2,1)S(1)}, u32[]{:S(2)}, u32[]{:S(2)}) collective-permute-start(bf16[32,512]{1,0:T(8,128)(2,1)S(1)} %get-tuple-element.49), channel_id=1, source_target_pairs={{0,3},{1,2},{2,1},{3,0},{4,7},{5,6},{6,5},{7,4},{8,11},{9,10},{10,... | collective-permute-start | bytes 98312 | tf_op jit(solution)/shard_map/ppermute | solution.py:359
  33.3 5.8 %collective-permute-start.8 = (bf16[32,2176]{1,0:T(8,128)(2,1)S(1)}, bf16[32,2176]{1,0:T(8,128)(2,1)S(1)}, u32[]{:S(2)}, u32[]{:S(2)}) collective-permute-start(bf16[32,2176]{1,0:T(8,128)(2,1)S(1)} %get-tuple-element.52.after_ref.refs_0_), channel_id=1, source_target_pairs={{0,8},{8,16},{16,24},{24,28},{28,20},{20,12},{12,4},{4,0},{1,9},{9... | collective-permute-start | bytes 417800 | tf_op jit(solution)/shard_map/ppermute | solution.py:243
  33.3 5.8 %collective-permute-start.9 = (bf16[32,2176]{1,0:T(8,128)(2,1)S(1)}, bf16[32,2176]{1,0:T(8,128)(2,1)S(1)}, u32[]{:S(2)}, u32[]{:S(2)}) collective-permute-start(bf16[32,2176]{1,0:T(8,128)(2,1)S(1)} %get-tuple-element.52.after_ref.refs_0_), channel_id=1, source_target_pairs={{0,4},{8,0},{16,8},{24,16},{28,24},{20,28},{12,20},{4,12},{1,5},{9... | collective-permute-start | bytes 417800 | tf_op jit(solution)/shard_map/ppermute | solution.py:243
  39.1 5.1 %collective-permute-start.10 = (bf16[32,2176]{1,0:T(8,128)(2,1)S(1)}, bf16[32,2176]{1,0:T(8,128)(2,1)S(1)}, u32[]{:S(2)}, u32[]{:S(2)}) collective-permute-start(bf16[32,2176]{1,0:T(8,128)(2,1)S(1)} %collective-permute-done.8.refs_1_), channel_id=1, source_target_pairs={{0,8},{8,16},{16,24},{24,28},{28,20},{20,12},{12,4},{4,0},{1,9},{9... | collective-permute-start | bytes 417800 | tf_op jit(solution)/shard_map/ppermute | solution.py:243
  40.0 5.1 %collective-permute-start.12 = (bf16[32,2176]{1,0:T(8,128)(2,1)S(1)}, bf16[32,2176]{1,0:T(8,128)(2,1)S(1)}, u32[]{:S(2)}, u32[]{:S(2)}) collective-permute-start(bf16[32,2176]{1,0:T(8,128)(2,1)S(1)} %collective-permute-done.9.refs_4_), channel_id=1, source_target_pairs={{0,4},{8,0},{16,8},{24,16},{28,24},{20,28},{12,20},{4,12},{1,5},{9... | collective-permute-start | bytes 417800 | tf_op jit(solution)/shard_map/ppermute | solution.py:243
  44.2 9.3 %collective-permute-start.11 = (bf16[32,2176]{1,0:T(8,128)(2,1)S(1)}, bf16[32,2176]{1,0:T(8,128)(2,1)S(1)}, u32[]{:S(2)}, u32[]{:S(2)}) collective-permute-start(bf16[32,2176]{1,0:T(8,128)(2,1)S(1)} %collective-permute-done.10.refs_2_), channel_id=1, source_target_pairs={{0,8},{8,16},{16,24},{24,28},{28,20},{20,12},{12,4},{4,0},{1,9},{9... | collective-permute-start | bytes 417800 | tf_op jit(solution)/shard_map/ppermute | solution.py:243
  45.0 8.4 %collective-permute-start.13 = (bf16[32,2176]{1,0:T(8,128)(2,1)S(1)}, bf16[32,2176]{1,0:T(8,128)(2,1)S(1)}, u32[]{:S(2)}, u32[]{:S(2)}) collective-permute-start(bf16[32,2176]{1,0:T(8,128)(2,1)S(1)} %collective-permute-done.12.refs_5_), channel_id=1, source_target_pairs={{0,4},{8,0},{16,8},{24,16},{28,24},{20,28},{12,20},{4,12},{1,5},{9... | collective-permute-start | bytes 417800 | tf_op jit(solution)/shard_map/ppermute | solution.py:243
  46.2 6.3 %collective-permute-start.14 = (bf16[16,2176]{1,0:T(8,128)(2,1)S(1)}, bf16[16,2176]{1,0:T(8,128)(2,1)S(1)}, u32[]{:S(2)}, u32[]{:S(2)}) collective-permute-start(bf16[16,2176]{1,0:T(8,128)(2,1)S(1)} %slice.40), channel_id=1, source_target_pairs={{0,16},{8,24},{16,28},{24,20},{28,12},{20,4},{12,0},{4,8},{1,17},{... | collective-permute-start | bytes 208904 | tf_op jit(solution)/shard_map/ppermute | solution.py:243
  48.3 5.2 %collective-permute-start.15 = (bf16[16,2176]{1,0:T(8,128)(2,1)S(1)}, bf16[16,2176]{1,0:T(8,128)(2,1)S(1)}, u32[]{:S(2)}, u32[]{:S(2)}) collective-permute-start(bf16[16,2176]{1,0:T(8,128)(2,1)S(1)} %slice.41), channel_id=1, source_target_pairs={{0,12},{8,4},{16,0},{24,8},{28,16},{20,24},{12,28},{4,20},{1,13},{... | collective-permute-start | bytes 208904 | tf_op jit(solution)/shard_map/ppermute | solution.py:243
  58.2 7.8 %collective-permute-start.20 = (bf16[32,2048]{1,0:T(8,128)(2,1)S(1)}, bf16[32,2048]{1,0:T(8,128)(2,1)S(1)}, u32[]{:S(2)}, u32[]{:S(2)}) collective-permute-start(bf16[32,2048]{1,0:T(8,128)(2,1)S(1)} %get-tuple-element.61), channel_id=1, source_target_pairs={{0,4},{8,0},{16,8},{24,16},{28,24},{20,28},{12,20},{4,12},{1,5},{9... | collective-permute-start | bytes 393224 | tf_op jit(solution)/shard_map/ppermute | solution.py:243
  59.0 7.0 %collective-permute-start.21 = (bf16[16,2048]{1,0:T(8,128)(2,1)S(1)}, bf16[16,2048]{1,0:T(8,128)(2,1)S(1)}, u32[]{:S(2)}, u32[]{:S(2)}) collective-permute-start(bf16[16,2048]{1,0:T(8,128)(2,1)S(1)} %get-tuple-element.63), channel_id=1, source_target_pairs={{0,12},{8,4},{16,0},{24,8},{28,16},{20,24},{12,28},{4,20},{1,13},{... | collective-permute-start | bytes 196616 | tf_op jit(solution)/shard_map/ppermute | solution.py:243
  60.9 9.3 %collective-permute-start.16 = (bf16[32,2048]{1,0:T(8,128)(2,1)S(1)}, bf16[32,2048]{1,0:T(8,128)(2,1)S(1)}, u32[]{:S(2)}, u32[]{:S(2)}) collective-permute-start(bf16[32,2048]{1,0:T(8,128)(2,1)S(1)} %get-tuple-element.57), channel_id=1, source_target_pairs={{0,8},{8,16},{16,24},{24,28},{28,20},{20,12},{12,4},{4,0},{1,9},{9... | collective-permute-start | bytes 393224 | tf_op jit(solution)/shard_map/ppermute | solution.py:243
  62.0 8.3 %collective-permute-start.17 = (bf16[16,2048]{1,0:T(8,128)(2,1)S(1)}, bf16[16,2048]{1,0:T(8,128)(2,1)S(1)}, u32[]{:S(2)}, u32[]{:S(2)}) collective-permute-start(bf16[16,2048]{1,0:T(8,128)(2,1)S(1)} %get-tuple-element.59), channel_id=1, source_target_pairs={{0,16},{8,24},{16,28},{24,20},{28,12},{20,4},{12,0},{4,8},{1,17},{... | collective-permute-start | bytes 196616 | tf_op jit(solution)/shard_map/ppermute | solution.py:243
  66.1 5.5 %collective-permute-start.22 = (bf16[32,2048]{1,0:T(8,128)(2,1)S(1)}, bf16[32,2048]{1,0:T(8,128)(2,1)S(1)}, u32[]{:S(2)}, u32[]{:S(2)}) collective-permute-start(bf16[32,2048]{1,0:T(8,128)(2,1)S(1)} %pad_maximum_fusion.1), channel_id=1, source_target_pairs={{0,4},{8,0},{16,8},{24,16},{28,24},{20,28},{12,20},{4,12},{1,5},{9... | collective-permute-start | bytes 393224 | tf_op jit(solution)/shard_map/ppermute | solution.py:243
  70.3 5.0 %collective-permute-start.18 = (bf16[32,2048]{1,0:T(8,128)(2,1)S(1)}, bf16[32,2048]{1,0:T(8,128)(2,1)S(1)}, u32[]{:S(2)}, u32[]{:S(2)}) collective-permute-start(bf16[32,2048]{1,0:T(8,128)(2,1)S(1)} %pad_maximum_fusion), channel_id=1, source_target_pairs={{0,8},{8,16},{16,24},{24,28},{28,20},{20,12},{12,4},{4,0},{1,9},{9... | collective-permute-start | bytes 393224 | tf_op jit(solution)/shard_map/ppermute | solution.py:243
  71.7 5.0 %collective-permute-start.23 = (bf16[32,2048]{1,0:T(8,128)(2,1)S(1)}, bf16[32,2048]{1,0:T(8,128)(2,1)S(1)}, u32[]{:S(2)}, u32[]{:S(2)}) collective-permute-start(bf16[32,2048]{1,0:T(8,128)(2,1)S(1)} %add_convert_fusion), channel_id=1, source_target_pairs={{0,4},{8,0},{16,8},{24,16},{28,24},{20,28},{12,20},{4,12},{1,5},{9... | collective-permute-start | bytes 393224 | tf_op jit(solution)/shard_map/ppermute | solution.py:243
  75.4 5.0 %collective-permute-start.19 = (bf16[32,2048]{1,0:T(8,128)(2,1)S(1)}, bf16[32,2048]{1,0:T(8,128)(2,1)S(1)}, u32[]{:S(2)}, u32[]{:S(2)}) collective-permute-start(bf16[32,2048]{1,0:T(8,128)(2,1)S(1)} %add_convert_fusion.1), channel_id=1, source_target_pairs={{0,8},{8,16},{16,24},{24,28},{28,20},{20,12},{12,4},{4,0},{1,9},{9... | collective-permute-start | bytes 393224 | tf_op jit(solution)/shard_map/ppermute | solution.py:243
  81.0 3.4 %collective-permute-start.24 = (bf16[32,512]{1,0:T(8,128)(2,1)S(1)}, bf16[32,512]{1,0:T(8,128)(2,1)S(1)}, u32[]{:S(2)}, u32[]{:S(2)}) collective-permute-start(bf16[32,512]{1,0:T(8,128)(2,1)S(1)} %get-tuple-element.65), channel_id=1, source_target_pairs={{0,3},{1,2},{2,1},{3,0},{4,7},{5,6},{6,5},{7,4},{8,11},{9,10},{10,... | collective-permute-start | bytes 98312 | tf_op jit(solution)/shard_map/ppermute | solution.py:359
  81.1 4.3 %collective-permute-start.25 = (bf16[32,512]{1,0:T(8,128)(2,1)S(1)}, bf16[32,512]{1,0:T(8,128)(2,1)S(1)}, u32[]{:S(2)}, u32[]{:S(2)}) collective-permute-start(bf16[32,512]{1,0:T(8,128)(2,1)S(1)} %get-tuple-element.66), channel_id=1, source_target_pairs={{0,2},{1,3},{2,0},{3,1},{4,6},{5,7},{6,4},{7,5},{8,10},{9,11},{10,... | collective-permute-start | bytes 98312 | tf_op jit(solution)/shard_map/ppermute | solution.py:359
  82.0 3.3 %collective-permute-start.26 = (bf16[32,512]{1,0:T(8,128)(2,1)S(1)}, bf16[32,512]{1,0:T(8,128)(2,1)S(1)}, u32[]{:S(2)}, u32[]{:S(2)}) collective-permute-start(bf16[32,512]{1,0:T(8,128)(2,1)S(1)} %get-tuple-element.67), channel_id=1, source_target_pairs={{0,1},{1,0},{2,3},{3,2},{4,5},{5,4},{6,7},{7,6},{8,9},{9,8},{10,11... | collective-permute-start | bytes 98312 | tf_op jit(solution)/shard_map/ppermute | solution.py:359

commit v7 on v6

--- a/solution.py
+++ b/solution.py
@@ -71,21 +71,19 @@
         copy.wait()
     width = keys.shape[1] // 2
     place = scalars[1]
-    for h in range(keys.shape[1] // HEAD):
-        cols = slice(h * HEAD, (h + 1) * HEAD)
-        state = lax.dot_general(
+    sides = []
+    for side in range(2):
+        cols = slice(side * width, (side + 1) * width)
+        square = lax.dot_general(
             keys[:, cols], values[:, cols], (((0,), (0,)), ((), ())), preferred_element_type=F32
-        ).astype(BF16)
-        half, inner = divmod(h * HEAD, width)
-
-        @pl.when(place == half)
-        def _():
-            kept_ref[:, inner:inner + HEAD] = state
-
-        @pl.when(place != half)
-        def _():
-            given_ref[:, inner:inner + HEAD] = state
-
+        )
+        sides.append(
+            jnp.concatenate(
+                [square[h:h + HEAD, h:h + HEAD] for h in range(0, width, HEAD)], axis=1
+            ).astype(BF16)
+        )
+    kept_ref[...] = jnp.where(place == 0, sides[0], sides[1])
+    given_ref[...] = jnp.where(place == 0, sides[1], sides[0])
     for copy in copies[2:]:
         copy.wait()
 
@@ -106,23 +104,14 @@
         ) + jnp.dot(low, values[:, cols], preferred_element_type=F32)
 
 
-def back_kernel(earlier, scalars, sign_ref, kept_ref, *refs):
-    before_refs, out_ref = refs[:earlier], refs[earlier]
-    before = sum(ref[...].astype(F32) for ref in before_refs)
-    extra = jnp.where(scalars[1] == 0, kept_ref[...].astype(F32), 0.0)
-    out_ref[...] = (before + extra).astype(BF16)
-
-
 def attend_kernel(
-    parts, earlier, scalars, within_ref, queries, residuals, gain_ref, partner_ref, other_ref, *refs
+    parts, scalars, sign_ref, within_ref, queries, residuals, gain_ref, mine_ref, other_ref, *refs
 ):
-    before_refs, piece_refs, hidden = refs[:earlier], refs[earlier:-1], refs[-1]
+    piece_refs, hidden = refs[:-1], refs[-1]
     rows, full = hidden.shape
     width = full // 2
     first = scalars[1] == 0
-    mine = sum(ref[...].astype(F32) for ref in before_refs)
-    mine = mine + jnp.where(first, 0.0, partner_ref[...].astype(F32))
-    other = other_ref[...].astype(F32)
+    mine, other = mine_ref[...], other_ref[...].astype(F32)
     halves = [jnp.where(first, mine, other), jnp.where(first, other, mine)]
     for start in range(0, full, HEAD):
         cols = slice(start, start + HEAD)
@@ -156,30 +145,26 @@
     out_ref[:, model:] = pack_ref[...]
 
 
-def load_kernel(scalars, source, after_ref, target, done_ref, sems):
+def load_kernel(lead, scalars, source, after_ref, target, done_ref, sems):
     done_ref[...] = jnp.zeros_like(done_ref)
     pieces = sems.shape[0]
-    step = source.shape[0] // pieces
-    run_copies(
-        [
-            (source.at[pl.ds(i * step, step)], target.at[pl.ds(i * step, step)])
-            for i in range(pieces)
-        ],
-        sems,
-    )
-
-
-def load_near(scalars, source, after):
+    step = target.shape[0] // pieces
+    cuts = [pl.ds(i * step, step) for i in range(pieces)]
+    run_copies([(source.at[lead, cut], target.at[cut]) for cut in cuts], sems)
+
+
+def load_near(scalars, source, lead, after):
     return call(
-        load_kernel, [shape(source.shape, source.dtype), shape((8, HEAD), F32)],
+        functools.partial(load_kernel, lead),
+        [shape(source.shape[1:], source.dtype), shape((8, HEAD), F32)],
         [scalars, source, after], far=(1,), scratch=[pltpu.SemaphoreType.DMA((8,))],
     )
 
 
-def expert_kernel(blocks, scalars, in_ref, down_ref, *refs):
+def expert_kernel(blocks, scalars, gate_ref, up_ref, down_ref, *refs):
     x_refs, out_refs = refs[:blocks], refs[blocks:2 * blocks]
     rows_ref, act_ref, made_ref = refs[2 * blocks:]
-    model, units = rows_ref.shape[1], in_ref.shape[1]
+    model, units = gate_ref.shape
     spans, packs = [], []
     first = 0
     for ref in x_refs:
@@ -196,8 +181,8 @@
     @pl.loop(0, units // chunk)
     def _(step):
         cut = pl.ds(pl.multiple_of(step * chunk, chunk), chunk)
-        gate = jnp.dot(rows_ref[...], in_ref[:model, cut], preferred_element_type=F32)
-        up = jnp.dot(rows_ref[...], in_ref[model:, cut], preferred_element_type=F32)
+        gate = jnp.dot(rows_ref[...], gate_ref[:, cut], preferred_element_type=F32)
+        up = jnp.dot(rows_ref[...], up_ref[:, cut], preferred_element_type=F32)
         act_ref[:, cut] = (gate / (1.0 + jnp.exp(-gate)) * up).astype(BF16)
 
     wide = min(model, 1024)
@@ -212,13 +197,13 @@
         out_ref[...] = made_ref[span, :]
 
 
-def run_expert(scalars, blocks, weights_in, weights_out):
+def run_expert(scalars, blocks, weights_gate, weights_up, weights_out):
     units, model = weights_out.shape
     total = sum(b.shape[0] for b in blocks)
     return call(
         functools.partial(expert_kernel, len(blocks)),
         [shape((b.shape[0], model), BF16) for b in blocks],
-        [scalars, weights_in, weights_out, *blocks],
+        [scalars, weights_gate, weights_up, weights_out, *blocks],
         scratch=[
             pltpu.VMEM((total, model), BF16),
             pltpu.VMEM((total, units), BF16),
@@ -233,61 +218,51 @@
     return list(range(0, count, 2)) + list(range(1, count, 2))[::-1]
 
 
-def dense_experts(block, scalars, weights_in, expert_out):
+def dense_experts(block, scalars, turns, weights_gate, weights_up, expert_out):
     count = lax.axis_size("seq")
     order = ring_order(count)
-    half = block.shape[0] // 2
     far = count // 2
+    parts = lax.axis_size("exp")
 
     def hop(rows, steps):
         return lax.ppermute(
             rows, "seq", [(order[p], order[(p + steps) % count]) for p in range(count)]
         )
+
+    def far_hop(rows):
+        pairs = []
+        for p in range(count):
+            for e in range(parts):
+                target = order[(p + (2 if e % 2 == 0 else -2)) % count]
+                pairs.append((order[p] * parts + e, target * parts + e))
+        return lax.ppermute(rows, ("seq", "exp"), pairs)
 
     ahead, behind = [block], [block]
     for distance in range(1, far):
         came, went = hop(ahead[-1], 1), hop(behind[-1], -1)
         if distance == 1:
-            weights_out, sign = load_near(scalars, expert_out, block)
-            came, went, sign = lax.optimization_barrier((came, went, sign))
+            weights_out, _ = load_near(scalars, expert_out, 0, came)
         ahead.append(came)
         behind.append(went)
-    top = hop(ahead[-2][:half], 2)
-    bottom = hop(behind[-2][half:], -2)
-    made = run_expert(scalars, ahead + behind[1:] + [top, bottom], weights_in, weights_out)
-    own, to_back, to_front = made[0], made[1:far], made[far:2 * far - 1]
-    top, bottom = made[-2:]
-    early_going, early_coming = hop(bottom, 2), hop(top, -2)
+    turned = turns[0]
+    farthest = far_hop(jnp.where(turned, behind[-2], ahead[-2]))
+    made = run_expert(
+        scalars, ahead + behind[1:] + [farthest], weights_gate, weights_up, weights_out
+    )
+    own, to_back, to_front, farthest = made[0], made[1:far], made[far:-1], made[-1]
     going, coming = hop(to_front[-1], 1), hop(to_back[-1], -1)
+    early = far_hop(farthest)
     for distance in range(far - 2, 0, -1):
         front, back = to_front[distance - 1], to_back[distance - 1]
         if distance == far - 2:
-            going = jnp.concatenate(
-                [
-                    add_rows(going[:half], front[:half]),
-                    add_rows(going[half:], front[half:], early_going),
-                ]
-            )
-            coming = jnp.concatenate(
-                [
-                    add_rows(coming[:half], back[:half], early_coming),
-                    add_rows(coming[half:], back[half:]),
-                ]
-            )
+            nothing = jnp.zeros_like(early)
+            going = add_rows(going, front, jnp.where(turned, nothing, early))
+            coming = add_rows(coming, back, jnp.where(turned, early, nothing))
         else:
             going = add_rows(going, front)
             coming = add_rows(coming, back)
         going, coming = hop(going, 1), hop(coming, -1)
     return own, going, coming
-
-
-def mix_kernel(scalars, hidden_ref, a_ref, b_ref, c_ref, *out_refs):
-    width = out_refs[0].shape[1]
-    for j, out_ref in enumerate(out_refs):
-        cols = pl.ds(pl.multiple_of((scalars[0] ^ j) * width, width), width)
-        mixed = a_ref[:, cols].astype(F32) + b_ref[:, cols].astype(F32)
-        mixed += c_ref[:, cols].astype(F32)
-        out_ref[...] = (hidden_ref[:, cols].astype(F32) + mixed).astype(BF16)
 
 
 def slot_ids(block_routes, expert_count, capacity):
@@ -332,25 +307,26 @@
     return jnp.sum(picked.astype(F32) * my_gates[:, :, None], axis=1)
 
 
-def prior_states(kept, partner):
+def swap_pairs(rows, distance):
     count = lax.axis_size("seq")
-
-    def pass_on(state, distance):
-        return lax.ppermute(
-            state, "seq", [(i, i + 2 * distance) for i in range(count - 2 * distance)]
-        )
-
-    pairs = count // 2
-    running = add_rows(kept, partner)
+    return lax.ppermute(rows, "seq", [(i, i ^ (2 * distance)) for i in range(count)])
+
+
+def prior_states(total, later):
+    pairs = lax.axis_size("seq") // 2
+    bits = len(later)
     if pairs <= 4:
-        return [pass_on(running, distance) for distance in range(1, pairs)]
-    terms = []
-    distance = 1
-    while distance < pairs:
-        terms.append(pass_on(running, distance))
-        running = add_rows(running, terms[-1])
-        distance *= 2
-    return terms
+        terms = [
+            swap_pairs(total, distance).astype(F32) * later[distance.bit_length() - 1]
+            for distance in range(1, pairs)
+        ]
+        return sum(terms)
+    before = jnp.zeros(total.shape, F32)
+    for b in range(bits):
+        came = swap_pairs(total, 1 << b)
+        before = before + came.astype(F32) * later[b]
+        total = add_rows(total, came)
+    return before
 
 
 def exchange(pieces):
@@ -359,6 +335,12 @@
         lax.ppermute(pieces[j], "exp", [(i, i ^ j) for i in range(parts)])
         for j in range(1, parts)
     ]
+
+
+def turn_order(items, turns):
+    for b, turn in enumerate(turns):
+        items = [jnp.where(turn, items[i ^ (1 << b)], items[i]) for i in range(len(items))]
+    return items
 
 
 def per_device(
@@ -382,7 +364,15 @@
     place = position % 2
     scalars = jnp.stack([my_index, place, experts, position]).astype(jnp.int32)
     swap = [(i, i ^ 1) for i in range(seq)]
-
+    pair_bits, part_bits = (seq // 2).bit_length() - 1, parts.bit_length() - 1
+    first, second, *later = [
+        flag.astype(F32).reshape(1, 1)
+        for flag in [1 - place, place] + [(position >> (b + 1)) & 1 for b in range(pair_bits)]
+    ]
+    turns = [((my_index >> b) & 1 != 0).reshape(1, 1) for b in range(part_bits)]
+    scalars, first, second, later, turns = lax.optimization_barrier(
+        (scalars, first, second, later, turns)
+    )
     state, heads = shape((HEAD, half), BF16), shape((rows, width), BF16)
     kept, given, keys, values, query, rest, my_gain, my_norm = call(
         open_kernel,
@@ -400,21 +390,21 @@
         within_kernel, [shape((rows, width), F32)], [scalars, keys, values, query],
         flops=6 * rows * rows * width,
     )
-    before = prior_states(kept, partner)
     dense = routes.shape[1] == experts
+    total, within = lax.optimization_barrier((add_rows(kept, partner), within))
+    before = prior_states(total, later)
     sign = jnp.zeros((8, HEAD), F32)
     if dense:
-        weights_in, sign = load_near(
-            scalars, expert_in.reshape(-1, expert_in.shape[-1]), partner
-        )
-    [lacked] = call(
-        functools.partial(back_kernel, len(before)), [state], [scalars, sign, kept, *before]
-    )
+        weights_gate, sign = load_near(scalars, expert_in[0], 0, total)
+    lacked = (before + kept.astype(F32) * first + sign[:1, :1]).astype(BF16)
+    mine = before + partner.astype(F32) * second
+    if dense:
+        weights_up, sign = load_near(scalars, expert_in[0], 1, lacked)
     other = lax.ppermute(lacked, "seq", swap)
     pieces = call(
-        functools.partial(attend_kernel, parts, len(before)),
+        functools.partial(attend_kernel, parts),
         [shape((count, width), BF16)] * parts,
-        [scalars, within, query, rest, my_gain, partner, other, *before],
+        [scalars, sign, within, query, rest, my_gain, mine, other],
         scratch=[pltpu.VMEM((rows, width), BF16)],
         flops=4 * rows * width * HEAD,
     )
@@ -441,22 +431,17 @@
         [scalars, my_norm, pack] + gathered,
     )
     if dense:
-        terms = dense_experts(block, scalars, weights_in, expert_out[0])
+        terms = dense_experts(
+            block, scalars, turns, weights_gate, weights_up, expert_out
+        )
     else:
         mixed = routed_experts(block[:, :model], my_routes, my_gates, expert_in, expert_out)
-        nothing = jnp.zeros_like(mixed)
-        terms = (mixed, nothing, nothing)
-    ready = call(
-        mix_kernel, [shape((count, width), BF16)] * parts, [scalars, hidden, *terms]
-    )
-    returned = exchange(ready)
-    order = list(range(parts))
-    bit = 1
-    while bit < parts:
-        turn = (my_index & bit) != 0
-        returned = [jnp.where(turn, returned[i ^ bit], returned[i]) for i in order]
-        bit *= 2
-    return jnp.concatenate(returned)
+        terms = [mixed]
+    own, *others = terms
+    mixed = own.astype(F32) + sum(t.astype(F32) for t in others)
+    ready = (hidden.astype(F32) + mixed).astype(BF16)
+    columns = [ready[:, i * width:(i + 1) * width] for i in range(parts)]
+    return jnp.concatenate(turn_order(exchange(turn_order(columns, turns)), turns))
 
 
 def solution(mesh):

time: 86.3 us -> 79.8 us (0.925)
  waiting for transfers between devices: 31.7 us -> 27.7 us
  starting transfers between devices: 34 us -> 30.5 us
    ppermute x16 -> x12, waiting for transfers between devices: 23 us -> 14.3 us  [hop(): lax.ppermute(rows, 'seq', [(order[p], order[(p + steps) % count]) for p i...]
    ppermute x3 -> x5, waiting for transfers between devices: 0.01 us -> 7.74 us  [the longest x2 6.64 us: far_hop(): return lax.ppermute(rows, ('seq', 'exp'), pairs)]
    ppermute x16 -> x12, starting transfers between devices: 15.7 us -> 13.3 us  [hop(): lax.ppermute(rows, 'seq', [(order[p], order[(p + steps) % count]) for p i...]
    ppermute x1, waiting for transfers between devices: 1.82 us -> 0.01 us  [per_device(): other = lax.ppermute(lacked, 'seq', swap)]
    ppermute x3 -> x5, starting transfers between devices: 9.8 us -> 8.48 us  [the longest x3 4.83 us: swap_pairs(): lax.ppermute(rows, 'seq', [(i, i ^ 2 * distance) for i in range(count)])]
    ppermute x1, waiting for transfers between devices: 1.41 us -> 0.46 us  [per_device(): partner = lax.ppermute(given, 'seq', swap)]
    pallas_call x9 -> x8, Pallas kernels: 18.1 us -> 17.9 us  [call(): pl.pallas_call(kernel, out_shape=outs, in_specs=[SCALAR if i == 0 or i in...]
  transfers between devices with their start and end apart: 27 -> 25, of which waited for: 16 -> 14; matrix products, arithmetic and copies ran while one was open for 1% -> 2% of each run, Pallas kernels for 10% -> 12%
where the time goes in v7:
time: 79.8 us; the launch traced here: 79.6 us
  starting transfers between devices  30.5 us (38%)
  waiting for transfers between devices  27.7 us (35%)
  Pallas kernels  17.9 us (22%)
  other arithmetic  1.88 us (2%)
  local copies, waits for them, and re-layouts  1.51 us (2%)
    pallas_call x8, Pallas kernels, call(): pl.pallas_call(kernel, out_shape=outs, in_specs=[SCALAR if i == 0 or i in...  17.9 us
    ppermute x12, waiting for transfers between devices, hop(): lax.ppermute(rows, 'seq', [(order[p], order[(p + steps) % count]) for p i...  14.3 us
    ppermute x12, starting transfers between devices, hop(): lax.ppermute(rows, 'seq', [(order[p], order[(p + steps) % count]) for p i...  13.3 us
    ppermute x2, waiting for transfers between devices, far_hop(): return lax.ppermute(rows, ('seq', 'exp'), pairs)  6.64 us
    ppermute x6, waiting for transfers between devices, exchange(): lax.ppermute(pieces[j], 'exp', [(i, i ^ j) for i in range(parts)])  5.11 us
    ppermute x3, starting transfers between devices, swap_pairs(): lax.ppermute(rows, 'seq', [(i, i ^ 2 * distance) for i in range(count)])  4.83 us
    ppermute x6, starting transfers between devices, exchange(): lax.ppermute(pieces[j], 'exp', [(i, i ^ j) for i in range(parts)])  4.14 us
    ppermute x2, starting transfers between devices, far_hop(): return lax.ppermute(rows, ('seq', 'exp'), pairs)  3.65 us
  transfers between devices with their start and end apart: 25, of which 14 were waited for; matrix products, arithmetic and copies ran while one was open for 2% of the time, Pallas kernels for 12%

profile of v7, /device:TPU:0, one launch (start us, length us, event | category | flops | bytes accessed | tf_op | source)
XLA Modules:
  0.0 79.6 jit_solution(9917578001372814648)
XLA Ops:
  0.0 0.1 pad_add_fusion.scalars
  0.1 1.8 %shard_map.100 = (bf16[128,256]{1,0:T(8,128)(2,1)S(1)}, bf16[128,256]{1,0:T(8,128)(2,1)S(1)}, bf16[128,512]{1,0:T(8,128)(2,1)S(1)}, bf16[128,512]{1,0:T(8,128)(2...) custom-call(s32[4]{0:T(128)S(1)} %pad_add_fusion.scalars, ...), custom_call_target="tpu_custom_call" | custom-call | flops 16777216 | bytes 1200144 | tf_op jit(solution)/shard_map/pallas_call | solution.py:24
  1.9 3.0 %collective-permute-start = (bf16[128,256]{1,0:T(8,128)(2,1)S(1)}, bf16[128,256]{1,0:T(8,128)(2,1)S(1)}, u32[]{:S(2)}, u32[]{:S(2)}) collective-permute-start(bf16[128,256]{1,0:T(8,128)(2,1)S(1)} %get-tuple-element.46), channel_id=1, source_target_pairs={{0,4},{4,0},{8,12},{12,8},{16,20},{20,16},{24,28},{28,24},{1,5},{5... | collective-permute-start | bytes 196616 | tf_op jit(solution)/shard_map/ppermute | solution.py:388
  4.9 0.1 constant_dynamic-slice_fusion.1
  5.0 0.9 %shard_map.101.within_ref = f32[128,512]{1,0:T(8,128)S(1)} custom-call(s32[4]{0:T(128)S(1)} %pad_add_fusion.scalars, bf16[128,512]{1,0:T(8,128)(2,1)S(1)} %get-tuple-element.47.keys, bf16[128,512]{1,0:T(8,128)(2,1)S(1)} %get-tuple-element.48.values, bf16[128,512]{1,0:T(8,128)(2,1)S(1)} %get-tuple-element.49.queries), custom_call_target="tpu_custom_call" | custom-call | flops 50331648 | bytes 655376 | tf_op jit(solution)/shard_map/pallas_call | solution.py:24
  5.9 0.8 constant_dynamic-slice_fusion
  6.7 0.5 collective-permute-done
  7.2 4.2 %collective-permute-start.3 = (bf16[128,256]{1,0:T(8,128)(2,1)S(1)}, bf16[128,256]{1,0:T(8,128)(2,1)S(1)}, u32[]{:S(2)}, u32[]{:S(2)}) collective-permute-start(bf16[128,256]{1,0:T(8,128)(2,1)S(1)} %fusion.3.after_ref), channel_id=1, source_target_pairs={{0,24},{4,28},{8,16},{12,20},{16,8},{20,12},{24,0},{28,4},{1,25},{... | collective-permute-start | bytes 196616 | tf_op jit(solution)/shard_map/ppermute | solution.py:312
  11.4 0.0 collective-permute-start.2
  11.4 0.6 collective-permute-start.1
  12.0 0.1 copy.16
  12.1 0.1 copy.15
  12.2 2.8 %shard_map.102 = (bf16[2048,1024]{1,0:T(8,128)(2,1)S(1)}, f32[8,128]{1,0:T(8,128)S(1)}) custom-call(s32[4]{0:T(128)S(1)} %pad_add_fusion.scalars, bf16[2,2048,1024]{2,1,0:T(8,128)(2,1)} %bitcast.19, bf16[128,256]{1,0:T(8,128)(2,1)S(1)} %fusion.3.after_ref), custom_call_target="tpu_custom_call" | custom-call | bytes 12652560 | tf_op jit(solution)/shard_map/pallas_call | solution.py:24
  15.0 0.5 slice.15
  15.5 1.1 %collective-permute-done.2 = bf16[128,256]{1,0:T(8,128)(2,1)S(1)} collective-permute-done((bf16[128,256]{1,0:T(8,128)(2,1)S(1)}, bf16[128,256]{1,0:T(8,128)(2,1)S(1)}, u32[]{:S(2)}, u32[]{:S(2)}) %collective-permute-start.2) | collective-permute-done | bytes 65568 | tf_op jit(solution)/shard_map/ppermute | solution.py:312
  16.6 0.0 collective-permute-done.1
  16.6 0.7 fusion.4
  17.3 1.6 %collective-permute-start.4 = (bf16[128,256]{1,0:T(8,128)(2,1)S(1)}, bf16[128,256]{1,0:T(8,128)(2,1)S(1)}, u32[]{:S(2)}, u32[]{:S(2)}) collective-permute-start(bf16[128,256]{1,0:T(8,128)(2,1)S(1)} %get-tuple-element.81.after_ref), channel_id=1, source_target_pairs={{0,4},{4,0},{8,12},{12,8},{16,20},{20,16},{24,28},{28,24},{1,5},{5... | collective-permute-start | bytes 196616 | tf_op jit(solution)/shard_map/ppermute | solution.py:403
  18.9 2.8 %shard_map.103 = (bf16[2048,1024]{1,0:T(8,128)(2,1)S(1)}, f32[8,128]{1,0:T(8,128)S(1)}) custom-call(s32[4]{0:T(128)S(1)} %pad_add_fusion.scalars, bf16[2,2048,1024]{2,1,0:T(8,128)(2,1)} %bitcast.20, bf16[128,256]{1,0:T(8,128)(2,1)S(1)} %get-tuple-element.81.after_ref), custom_call_target="tpu_custom_call" | custom-call | bytes 12652560 | tf_op jit(solution)/shard_map/pallas_call | solution.py:24
  21.6 0.0 collective-permute-done.4.other_ref
  21.6 0.9 %shard_map.104 = (bf16[32,512]{1,0:T(8,128)(2,1)S(1)}, bf16[32,512]{1,0:T(8,128)(2,1)S(1)}, bf16[32,512]{1,0:T(8,128)(2,1)S(1)}, bf16[32,512]{1,0:T(8,128)(2,1)S(1)}) custom-call(s32[4]{0:T(128)S(1)} %pad_add_fusion.scalars, f32[8,128]{1,0:T(8,128)S(1)} %get-tuple-element.55.sign_ref, f32[128,512]{1,0:T(8,128)S(1)} %shard_map.101.within_ref, ...), custom_call_target="tpu_custom_call" | custom-call | flops 33554432 | bytes 858128 | tf_op jit(solution)/shard_map/pallas_call | solution.py:24
  22.5 0.1 collective-permute-start.5
  22.6 1.6 %collective-permute-start.6 = (bf16[32,512]{1,0:T(8,128)(2,1)S(1)}, bf16[32,512]{1,0:T(8,128)(2,1)S(1)}, u32[]{:S(2)}, u32[]{:S(2)}) collective-permute-start(bf16[32,512]{1,0:T(8,128)(2,1)S(1)} %get-tuple-element.62), channel_id=1, source_target_pairs={{0,2},{1,3},{2,0},{3,1},{4,6},{5,7},{6,4},{7,5},{8,10},{9,11},{10,... | collective-permute-start | bytes 98312 | tf_op jit(solution)/shard_map/ppermute | solution.py:335
  24.2 0.3 collective-permute-start.7
  24.5 0.1 fusion.7.pack_ref
  24.6 0.0 collective-permute-done.5.refs_1_
  24.6 2.0 %collective-permute-done.6.refs_2_ = bf16[32,512]{1,0:T(8,128)(2,1)S(1)} collective-permute-done((bf16[32,512]{1,0:T(8,128)(2,1)S(1)}, bf16[32,512]{1,0:T(8,128)(2,1)S(1)}, u32[]{:S(2)}, u32[]{:S(2)}) %collective-permute-start.6) | collective-permute-done | bytes 32800 | tf_op jit(solution)/shard_map/ppermute | solution.py:335
  26.6 0.9 %collective-permute-done.7.refs_3_ = bf16[32,512]{1,0:T(8,128)(2,1)S(1)} collective-permute-done((bf16[32,512]{1,0:T(8,128)(2,1)S(1)}, bf16[32,512]{1,0:T(8,128)(2,1)S(1)}, u32[]{:S(2)}, u32[]{:S(2)}) %collective-permute-start.7) | collective-permute-done | bytes 32800 | tf_op jit(solution)/shard_map/ppermute | solution.py:335
  27.5 0.7 shard_map.105
  28.2 1.5 %collective-permute-start.11 = (bf16[32,2176]{1,0:T(8,128)(2,1)S(1)}, bf16[32,2176]{1,0:T(8,128)(2,1)S(1)}, u32[]{:S(2)}, u32[]{:S(2)}) collective-permute-start(bf16[32,2176]{1,0:T(8,128)(2,1)S(1)} %get-tuple-element.67.refs_0_), channel_id=1, source_target_pairs={{0,4},{8,0},{16,8},{24,16},{28,24},{20,28},{12,20},{4,12},{1,5},{9... | collective-permute-start | bytes 417800 | tf_op jit(solution)/shard_map/ppermute | solution.py:228
  29.8 0.5 collective-permute-start.8
  30.3 3.7 %collective-permute-done.11.refs_4_ = bf16[32,2176]{1,0:T(8,128)(2,1)S(1)} collective-permute-done((bf16[32,2176]{1,0:T(8,128)(2,1)S(1)}, bf16[32,2176]{1,0:T(8,128)(2,1)S(1)}, u32[]{:S(2)}, u32[]{:S(2)}) %collective-permute-start.11) | collective-permute-done | bytes 139296 | tf_op jit(solution)/shard_map/ppermute | solution.py:228
  34.0 1.5 %collective-permute-start.12 = (bf16[32,2176]{1,0:T(8,128)(2,1)S(1)}, bf16[32,2176]{1,0:T(8,128)(2,1)S(1)}, u32[]{:S(2)}, u32[]{:S(2)}) collective-permute-start(bf16[32,2176]{1,0:T(8,128)(2,1)S(1)} %collective-permute-done.11.refs_4_), channel_id=1, source_target_pairs={{0,4},{8,0},{16,8},{24,16},{28,24},{20,28},{12,20},{4,12},{1,5},{9... | collective-permute-start | bytes 417800 | tf_op jit(solution)/shard_map/ppermute | solution.py:228
  35.5 0.0 collective-permute-done.8.after_ref.refs_1_
  35.5 0.5 collective-permute-start.9
  36.0 3.0 %collective-permute-done.12.refs_5_ = bf16[32,2176]{1,0:T(8,128)(2,1)S(1)} collective-permute-done((bf16[32,2176]{1,0:T(8,128)(2,1)S(1)}, bf16[32,2176]{1,0:T(8,128)(2,1)S(1)}, u32[]{:S(2)}, u32[]{:S(2)}) %collective-permute-start.12) | collective-permute-done | bytes 139296 | tf_op jit(solution)/shard_map/ppermute | solution.py:228
  39.1 1.5 %collective-permute-start.13 = (bf16[32,2176]{1,0:T(8,128)(2,1)S(1)}, bf16[32,2176]{1,0:T(8,128)(2,1)S(1)}, u32[]{:S(2)}, u32[]{:S(2)}) collective-permute-start(bf16[32,2176]{1,0:T(8,128)(2,1)S(1)} %collective-permute-done.12.refs_5_), channel_id=1, source_target_pairs={{0,4},{8,0},{16,8},{24,16},{28,24},{20,28},{12,20},{4,12},{1,5},{9... | collective-permute-start | bytes 417800 | tf_op jit(solution)/shard_map/ppermute | solution.py:228
  40.6 0.0 collective-permute-done.9.refs_2_
  40.6 1.0 %collective-permute-start.14 = (bf16[32,2176]{1,0:T(8,128)(2,1)S(1)}, bf16[32,2176]{1,0:T(8,128)(2,1)S(1)}, u32[]{:S(2)}, u32[]{:S(2)}) collective-permute-start(bf16[32,2176]{1,0:T(8,128)(2,1)S(1)} %broadcast_select_fusion), channel_id=1, source_target_pairs={{0,16},{1,13},{2,18},{3,15},{8,24},{9,5},{10,26},{11,7},{16,28},{1... | collective-permute-start | bytes 417800 | tf_op jit(solution)/shard_map/ppermute | solution.py:238
  41.6 1.6 %collective-permute-start.10 = (bf16[32,2176]{1,0:T(8,128)(2,1)S(1)}, bf16[32,2176]{1,0:T(8,128)(2,1)S(1)}, u32[]{:S(2)}, u32[]{:S(2)}) collective-permute-start(bf16[32,2176]{1,0:T(8,128)(2,1)S(1)} %collective-permute-done.9.refs_2_), channel_id=1, source_target_pairs={{0,8},{8,16},{16,24},{24,28},{28,20},{20,12},{12,4},{4,0},{1,9},{9... | collective-permute-start | bytes 417800 | tf_op jit(solution)/shard_map/ppermute | solution.py:228
  43.2 3.3 %shard_map.106 = (bf16[1024,2048]{1,0:T(8,128)(2,1)S(1)}, f32[8,128]{1,0:T(8,128)}) custom-call(s32[4]{0:T(128)S(1)} %pad_add_fusion.scalars, bf16[1,1024,2048]{2,1,0:T(8,128)(2,1)} %source.1, bf16[32,2176]{1,0:T(8,128)(2,1)S(1)} %collective-permute-done.8.after_ref.refs_1_), custom_call_target="tpu_custom_call" | custom-call | bytes 8531984 | tf_op jit(solution)/shard_map/pallas_call | solution.py:24
  46.5 0.0 collective-permute-done.13.refs_6_
  46.5 1.6 %collective-permute-done.14.refs_7_ = bf16[32,2176]{1,0:T(8,128)(2,1)S(1)} collective-permute-done((bf16[32,2176]{1,0:T(8,128)(2,1)S(1)}, bf16[32,2176]{1,0:T(8,128)(2,1)S(1)}, u32[]{:S(2)}, u32[]{:S(2)}) %collective-permute-start.14) | collective-permute-done | bytes 139296 | tf_op jit(solution)/shard_map/ppermute | solution.py:238
  48.2 0.0 collective-permute-done.10.refs_3_
  48.2 4.7 %shard_map.107 = (bf16[32,2048]{1,0:T(8,128)(2,1)S(1)}, bf16[32,2048]{1,0:T(8,128)(2,1)S(1)}, bf16[32,2048]{1,0:T(8,128)(2,1)S(1)}, bf16[32,2048]{1,0:T(8,128)(2...) custom-call(s32[4]{0:T(128)S(1)} %pad_add_fusion.scalars, ...), custom_call_target="tpu_custom_call" | custom-call | flops 3221225472 | bytes 14745616 | tf_op jit(solution)/shard_map/pallas_call | solution.py:24
  52.9 1.2 %collective-permute-start.15 = (bf16[32,2048]{1,0:T(8,128)(2,1)S(1)}, bf16[32,2048]{1,0:T(8,128)(2,1)S(1)}, u32[]{:S(2)}, u32[]{:S(2)}) collective-permute-start(bf16[32,2048]{1,0:T(8,128)(2,1)S(1)} %get-tuple-element.70), channel_id=1, source_target_pairs={{0,8},{8,16},{16,24},{24,28},{28,20},{20,12},{12,4},{4,0},{1,9},{9... | collective-permute-start | bytes 393224 | tf_op jit(solution)/shard_map/ppermute | solution.py:228
  54.1 2.6 %collective-permute-start.16 = (bf16[32,2048]{1,0:T(8,128)(2,1)S(1)}, bf16[32,2048]{1,0:T(8,128)(2,1)S(1)}, u32[]{:S(2)}, u32[]{:S(2)}) collective-permute-start(bf16[32,2048]{1,0:T(8,128)(2,1)S(1)} %get-tuple-element.72), channel_id=1, source_target_pairs={{0,16},{1,13},{2,18},{3,15},{8,24},{9,5},{10,26},{11,7},{16,28},{1... | collective-permute-start | bytes 393224 | tf_op jit(solution)/shard_map/ppermute | solution.py:238
  56.7 0.8 collective-permute-start.19
  57.5 0.6 collective-permute-done.15
  58.1 5.0 %collective-permute-done.16 = bf16[32,2048]{1,0:T(8,128)(2,1)S(1)} collective-permute-done((bf16[32,2048]{1,0:T(8,128)(2,1)S(1)}, bf16[32,2048]{1,0:T(8,128)(2,1)S(1)}, u32[]{:S(2)}, u32[]{:S(2)}) %collective-permute-start.16) | collective-permute-done | bytes 131104 | tf_op jit(solution)/shard_map/ppermute | solution.py:238
  63.1 0.1 add_convert_fusion.4
  63.2 0.1 collective-permute-start.17
  63.3 2.0 %collective-permute-start.20 = (bf16[32,2048]{1,0:T(8,128)(2,1)S(1)}, bf16[32,2048]{1,0:T(8,128)(2,1)S(1)}, u32[]{:S(2)}, u32[]{:S(2)}) collective-permute-start(bf16[32,2048]{1,0:T(8,128)(2,1)S(1)} %get-tuple-element.89), channel_id=1, source_target_pairs={{0,4},{8,0},{16,8},{24,16},{28,24},{20,28},{12,20},{4,12},{1,5},{9... | collective-permute-start | bytes 393224 | tf_op jit(solution)/shard_map/ppermute | solution.py:228
  65.3 3.6 %collective-permute-done.17 = bf16[32,2048]{1,0:T(8,128)(2,1)S(1)} collective-permute-done((bf16[32,2048]{1,0:T(8,128)(2,1)S(1)}, bf16[32,2048]{1,0:T(8,128)(2,1)S(1)}, u32[]{:S(2)}, u32[]{:S(2)}) %collective-permute-start.17) | collective-permute-done | bytes 131104 | tf_op jit(solution)/shard_map/ppermute | solution.py:228
  69.0 0.4 collective-permute-start.18
  69.5 1.7 %collective-permute-start.21 = (bf16[32,2048]{1,0:T(8,128)(2,1)S(1)}, bf16[32,2048]{1,0:T(8,128)(2,1)S(1)}, u32[]{:S(2)}, u32[]{:S(2)}) collective-permute-start(bf16[32,2048]{1,0:T(8,128)(2,1)S(1)} %add_convert_fusion.1), channel_id=1, source_target_pairs={{0,4},{8,0},{16,8},{24,16},{28,24},{20,28},{12,20},{4,12},{1,5},{9... | collective-permute-start | bytes 393224 | tf_op jit(solution)/shard_map/ppermute | solution.py:228
  71.2 2.8 %collective-permute-done.18 = bf16[32,2048]{1,0:T(8,128)(2,1)S(1)} collective-permute-done((bf16[32,2048]{1,0:T(8,128)(2,1)S(1)}, bf16[32,2048]{1,0:T(8,128)(2,1)S(1)}, u32[]{:S(2)}, u32[]{:S(2)}) %collective-permute-start.18) | collective-permute-done | bytes 131104 | tf_op jit(solution)/shard_map/ppermute | solution.py:228
  74.0 0.5 collective-permute-done.21
  74.5 0.1 add_convert_fusion
  74.6 0.9 %collective-permute-start.23 = (bf16[32,512]{1,0:T(8,128)(2,1)S(1)}, bf16[32,512]{1,0:T(8,128)(2,1)S(1)}, u32[]{:S(2)}, u32[]{:S(2)}) collective-permute-start(bf16[32,512]{1,0:T(8,128)(2,1)S(1)} %get-tuple-element.77), channel_id=1, source_target_pairs={{0,2},{1,3},{2,0},{3,1},{4,6},{5,7},{6,4},{7,5},{8,10},{9,11},{10,... | collective-permute-start | bytes 98312 | tf_op jit(solution)/shard_map/ppermute | solution.py:335
  75.5 1.3 %collective-permute-start.22 = (bf16[32,512]{1,0:T(8,128)(2,1)S(1)}, bf16[32,512]{1,0:T(8,128)(2,1)S(1)}, u32[]{:S(2)}, u32[]{:S(2)}) collective-permute-start(bf16[32,512]{1,0:T(8,128)(2,1)S(1)} %get-tuple-element.87), channel_id=1, source_target_pairs={{0,3},{1,2},{2,1},{3,0},{4,7},{5,6},{6,5},{7,4},{8,11},{9,10},{10,... | collective-permute-start | bytes 98312 | tf_op jit(solution)/shard_map/ppermute | solution.py:335
  76.8 1.8 %collective-permute-done.23 = bf16[32,512]{1,0:T(8,128)(2,1)S(1)} collective-permute-done((bf16[32,512]{1,0:T(8,128)(2,1)S(1)}, bf16[32,512]{1,0:T(8,128)(2,1)S(1)}, u32[]{:S(2)}, u32[]{:S(2)}) %collective-permute-start.23) | collective-permute-done | bytes 32800 | tf_op jit(solution)/shard_map/ppermute | solution.py:335
  78.6 0.3 collective-permute-done.22
  79.0 0.7 pad_maximum_fusion
  (16 shorter events, 0.2 us)
Async XLA Ops:
  0.0 4.9 %copy-start = (s32[128,8]{0,1:T(8,128)S(1)}, s32[128,8]{0,1:T(8,128)}, u32[]{:S(2)}) copy-start(s32[128,8]{0,1:T(8,128)} %param.16) | copy-start | bytes 12292
  1.9 5.3 %collective-permute-start = (bf16[128,256]{1,0:T(8,128)(2,1)S(1)}, bf16[128,256]{1,0:T(8,128)(2,1)S(1)}, u32[]{:S(2)}, u32[]{:S(2)}) collective-permute-start(bf16[128,256]{1,0:T(8,128)(2,1)S(1)} %get-tuple-element.46), channel_id=1, source_target_pairs={{0,4},{4,0},{8,12},{12,8},{16,20},{20,16},{24,28},{28,24},{1,5},{5... | collective-permute-start | bytes 196616 | tf_op jit(solution)/shard_map/ppermute | solution.py:388
  7.2 8.3 %collective-permute-start.3 = (bf16[128,256]{1,0:T(8,128)(2,1)S(1)}, bf16[128,256]{1,0:T(8,128)(2,1)S(1)}, u32[]{:S(2)}, u32[]{:S(2)}) collective-permute-start(bf16[128,256]{1,0:T(8,128)(2,1)S(1)} %fusion.3.after_ref), channel_id=1, source_target_pairs={{0,24},{4,28},{8,16},{12,20},{16,8},{20,12},{24,0},{28,4},{1,25},{... | collective-permute-start | bytes 196616 | tf_op jit(solution)/shard_map/ppermute | solution.py:312
  11.4 5.2 %collective-permute-start.2 = (bf16[128,256]{1,0:T(8,128)(2,1)S(1)}, bf16[128,256]{1,0:T(8,128)(2,1)S(1)}, u32[]{:S(2)}, u32[]{:S(2)}) collective-permute-start(bf16[128,256]{1,0:T(8,128)(2,1)S(1)} %fusion.3.after_ref), channel_id=1, source_target_pairs={{0,16},{4,20},{8,24},{12,28},{16,0},{20,4},{24,8},{28,12},{1,17},{... | collective-permute-start | bytes 196616 | tf_op jit(solution)/shard_map/ppermute | solution.py:312
  11.4 5.2 %collective-permute-start.1 = (bf16[128,256]{1,0:T(8,128)(2,1)S(1)}, bf16[128,256]{1,0:T(8,128)(2,1)S(1)}, u32[]{:S(2)}, u32[]{:S(2)}) collective-permute-start(bf16[128,256]{1,0:T(8,128)(2,1)S(1)} %fusion.3.after_ref), channel_id=1, source_target_pairs={{0,8},{4,12},{8,0},{12,4},{16,24},{20,28},{24,16},{28,20},{1,9},{5... | collective-permute-start | bytes 196616 | tf_op jit(solution)/shard_map/ppermute | solution.py:312
  17.3 4.3 %collective-permute-start.4 = (bf16[128,256]{1,0:T(8,128)(2,1)S(1)}, bf16[128,256]{1,0:T(8,128)(2,1)S(1)}, u32[]{:S(2)}, u32[]{:S(2)}) collective-permute-start(bf16[128,256]{1,0:T(8,128)(2,1)S(1)} %get-tuple-element.81.after_ref), channel_id=1, source_target_pairs={{0,4},{4,0},{8,12},{12,8},{16,20},{20,16},{24,28},{28,24},{1,5},{5... | collective-permute-start | bytes 196616 | tf_op jit(solution)/shard_map/ppermute | solution.py:403
  22.5 2.0 %collective-permute-start.5 = (bf16[32,512]{1,0:T(8,128)(2,1)S(1)}, bf16[32,512]{1,0:T(8,128)(2,1)S(1)}, u32[]{:S(2)}, u32[]{:S(2)}) collective-permute-start(bf16[32,512]{1,0:T(8,128)(2,1)S(1)} %get-tuple-element.61), channel_id=1, source_target_pairs={{0,1},{1,0},{2,3},{3,2},{4,5},{5,4},{6,7},{7,6},{8,9},{9,8},{10,11... | collective-permute-start | bytes 98312 | tf_op jit(solution)/shard_map/ppermute | solution.py:335
  22.6 4.0 %collective-permute-start.6 = (bf16[32,512]{1,0:T(8,128)(2,1)S(1)}, bf16[32,512]{1,0:T(8,128)(2,1)S(1)}, u32[]{:S(2)}, u32[]{:S(2)}) collective-permute-start(bf16[32,512]{1,0:T(8,128)(2,1)S(1)} %get-tuple-element.62), channel_id=1, source_target_pairs={{0,2},{1,3},{2,0},{3,1},{4,6},{5,7},{6,4},{7,5},{8,10},{9,11},{10,... | collective-permute-start | bytes 98312 | tf_op jit(solution)/shard_map/ppermute | solution.py:335
  24.2 3.3 %collective-permute-start.7 = (bf16[32,512]{1,0:T(8,128)(2,1)S(1)}, bf16[32,512]{1,0:T(8,128)(2,1)S(1)}, u32[]{:S(2)}, u32[]{:S(2)}) collective-permute-start(bf16[32,512]{1,0:T(8,128)(2,1)S(1)} %get-tuple-element.63), channel_id=1, source_target_pairs={{0,3},{1,2},{2,1},{3,0},{4,7},{5,6},{6,5},{7,4},{8,11},{9,10},{10,... | collective-permute-start | bytes 98312 | tf_op jit(solution)/shard_map/ppermute | solution.py:335
  28.2 5.8 %collective-permute-start.11 = (bf16[32,2176]{1,0:T(8,128)(2,1)S(1)}, bf16[32,2176]{1,0:T(8,128)(2,1)S(1)}, u32[]{:S(2)}, u32[]{:S(2)}) collective-permute-start(bf16[32,2176]{1,0:T(8,128)(2,1)S(1)} %get-tuple-element.67.refs_0_), channel_id=1, source_target_pairs={{0,4},{8,0},{16,8},{24,16},{28,24},{20,28},{12,20},{4,12},{1,5},{9... | collective-permute-start | bytes 417800 | tf_op jit(solution)/shard_map/ppermute | solution.py:228
  29.8 5.7 %collective-permute-start.8 = (bf16[32,2176]{1,0:T(8,128)(2,1)S(1)}, bf16[32,2176]{1,0:T(8,128)(2,1)S(1)}, u32[]{:S(2)}, u32[]{:S(2)}) collective-permute-start(bf16[32,2176]{1,0:T(8,128)(2,1)S(1)} %get-tuple-element.67.refs_0_), channel_id=1, source_target_pairs={{0,8},{8,16},{16,24},{24,28},{28,20},{20,12},{12,4},{4,0},{1,9},{9... | collective-permute-start | bytes 417800 | tf_op jit(solution)/shard_map/ppermute | solution.py:228
  34.0 5.1 %collective-permute-start.12 = (bf16[32,2176]{1,0:T(8,128)(2,1)S(1)}, bf16[32,2176]{1,0:T(8,128)(2,1)S(1)}, u32[]{:S(2)}, u32[]{:S(2)}) collective-permute-start(bf16[32,2176]{1,0:T(8,128)(2,1)S(1)} %collective-permute-done.11.refs_4_), channel_id=1, source_target_pairs={{0,4},{8,0},{16,8},{24,16},{28,24},{20,28},{12,20},{4,12},{1,5},{9... | collective-permute-start | bytes 417800 | tf_op jit(solution)/shard_map/ppermute | solution.py:228
  35.5 5.1 %collective-permute-start.9 = (bf16[32,2176]{1,0:T(8,128)(2,1)S(1)}, bf16[32,2176]{1,0:T(8,128)(2,1)S(1)}, u32[]{:S(2)}, u32[]{:S(2)}) collective-permute-start(bf16[32,2176]{1,0:T(8,128)(2,1)S(1)} %collective-permute-done.8.after_ref.refs_1_), channel_id=1, source_target_pairs={{0,8},{8,16},{16,24},{24,28},{28,20},{20,12},{12,4},{4,0},{1,9},{9... | collective-permute-start | bytes 417800 | tf_op jit(solution)/shard_map/ppermute | solution.py:228
  39.1 7.5 %collective-permute-start.13 = (bf16[32,2176]{1,0:T(8,128)(2,1)S(1)}, bf16[32,2176]{1,0:T(8,128)(2,1)S(1)}, u32[]{:S(2)}, u32[]{:S(2)}) collective-permute-start(bf16[32,2176]{1,0:T(8,128)(2,1)S(1)} %collective-permute-done.12.refs_5_), channel_id=1, source_target_pairs={{0,4},{8,0},{16,8},{24,16},{28,24},{20,28},{12,20},{4,12},{1,5},{9... | collective-permute-start | bytes 417800 | tf_op jit(solution)/shard_map/ppermute | solution.py:228
  40.6 7.6 %collective-permute-start.14 = (bf16[32,2176]{1,0:T(8,128)(2,1)S(1)}, bf16[32,2176]{1,0:T(8,128)(2,1)S(1)}, u32[]{:S(2)}, u32[]{:S(2)}) collective-permute-start(bf16[32,2176]{1,0:T(8,128)(2,1)S(1)} %broadcast_select_fusion), channel_id=1, source_target_pairs={{0,16},{1,13},{2,18},{3,15},{8,24},{9,5},{10,26},{11,7},{16,28},{1... | collective-permute-start | bytes 417800 | tf_op jit(solution)/shard_map/ppermute | solution.py:238
  41.6 6.5 %collective-permute-start.10 = (bf16[32,2176]{1,0:T(8,128)(2,1)S(1)}, bf16[32,2176]{1,0:T(8,128)(2,1)S(1)}, u32[]{:S(2)}, u32[]{:S(2)}) collective-permute-start(bf16[32,2176]{1,0:T(8,128)(2,1)S(1)} %collective-permute-done.9.refs_2_), channel_id=1, source_target_pairs={{0,8},{8,16},{16,24},{24,28},{28,20},{20,12},{12,4},{4,0},{1,9},{9... | collective-permute-start | bytes 417800 | tf_op jit(solution)/shard_map/ppermute | solution.py:228
  52.9 5.2 %collective-permute-start.15 = (bf16[32,2048]{1,0:T(8,128)(2,1)S(1)}, bf16[32,2048]{1,0:T(8,128)(2,1)S(1)}, u32[]{:S(2)}, u32[]{:S(2)}) collective-permute-start(bf16[32,2048]{1,0:T(8,128)(2,1)S(1)} %get-tuple-element.70), channel_id=1, source_target_pairs={{0,8},{8,16},{16,24},{24,28},{28,20},{20,12},{12,4},{4,0},{1,9},{9... | collective-permute-start | bytes 393224 | tf_op jit(solution)/shard_map/ppermute | solution.py:228
  54.1 9.0 %collective-permute-start.16 = (bf16[32,2048]{1,0:T(8,128)(2,1)S(1)}, bf16[32,2048]{1,0:T(8,128)(2,1)S(1)}, u32[]{:S(2)}, u32[]{:S(2)}) collective-permute-start(bf16[32,2048]{1,0:T(8,128)(2,1)S(1)} %get-tuple-element.72), channel_id=1, source_target_pairs={{0,16},{1,13},{2,18},{3,15},{8,24},{9,5},{10,26},{11,7},{16,28},{1... | collective-permute-start | bytes 393224 | tf_op jit(solution)/shard_map/ppermute | solution.py:238
  56.7 6.4 %collective-permute-start.19 = (bf16[32,2048]{1,0:T(8,128)(2,1)S(1)}, bf16[32,2048]{1,0:T(8,128)(2,1)S(1)}, u32[]{:S(2)}, u32[]{:S(2)}) collective-permute-start(bf16[32,2048]{1,0:T(8,128)(2,1)S(1)} %get-tuple-element.74), channel_id=1, source_target_pairs={{0,4},{8,0},{16,8},{24,16},{28,24},{20,28},{12,20},{4,12},{1,5},{9... | collective-permute-start | bytes 393224 | tf_op jit(solution)/shard_map/ppermute | solution.py:228
  63.2 5.7 %collective-permute-start.17 = (bf16[32,2048]{1,0:T(8,128)(2,1)S(1)}, bf16[32,2048]{1,0:T(8,128)(2,1)S(1)}, u32[]{:S(2)}, u32[]{:S(2)}) collective-permute-start(bf16[32,2048]{1,0:T(8,128)(2,1)S(1)} %get-tuple-element.88), channel_id=1, source_target_pairs={{0,8},{8,16},{16,24},{24,28},{28,20},{20,12},{12,4},{4,0},{1,9},{9... | collective-permute-start | bytes 393224 | tf_op jit(solution)/shard_map/ppermute | solution.py:228
  63.3 6.1 %collective-permute-start.20 = (bf16[32,2048]{1,0:T(8,128)(2,1)S(1)}, bf16[32,2048]{1,0:T(8,128)(2,1)S(1)}, u32[]{:S(2)}, u32[]{:S(2)}) collective-permute-start(bf16[32,2048]{1,0:T(8,128)(2,1)S(1)} %get-tuple-element.89), channel_id=1, source_target_pairs={{0,4},{8,0},{16,8},{24,16},{28,24},{20,28},{12,20},{4,12},{1,5},{9... | collective-permute-start | bytes 393224 | tf_op jit(solution)/shard_map/ppermute | solution.py:228
  69.0 5.0 %collective-permute-start.18 = (bf16[32,2048]{1,0:T(8,128)(2,1)S(1)}, bf16[32,2048]{1,0:T(8,128)(2,1)S(1)}, u32[]{:S(2)}, u32[]{:S(2)}) collective-permute-start(bf16[32,2048]{1,0:T(8,128)(2,1)S(1)} %add_convert_fusion.3), channel_id=1, source_target_pairs={{0,8},{8,16},{16,24},{24,28},{28,20},{20,12},{12,4},{4,0},{1,9},{9... | collective-permute-start | bytes 393224 | tf_op jit(solution)/shard_map/ppermute | solution.py:228
  69.5 5.0 %collective-permute-start.21 = (bf16[32,2048]{1,0:T(8,128)(2,1)S(1)}, bf16[32,2048]{1,0:T(8,128)(2,1)S(1)}, u32[]{:S(2)}, u32[]{:S(2)}) collective-permute-start(bf16[32,2048]{1,0:T(8,128)(2,1)S(1)} %add_convert_fusion.1), channel_id=1, source_target_pairs={{0,4},{8,0},{16,8},{24,16},{28,24},{20,28},{12,20},{4,12},{1,5},{9... | collective-permute-start | bytes 393224 | tf_op jit(solution)/shard_map/ppermute | solution.py:228
  74.6 4.0 %collective-permute-start.23 = (bf16[32,512]{1,0:T(8,128)(2,1)S(1)}, bf16[32,512]{1,0:T(8,128)(2,1)S(1)}, u32[]{:S(2)}, u32[]{:S(2)}) collective-permute-start(bf16[32,512]{1,0:T(8,128)(2,1)S(1)} %get-tuple-element.77), channel_id=1, source_target_pairs={{0,2},{1,3},{2,0},{3,1},{4,6},{5,7},{6,4},{7,5},{8,10},{9,11},{10,... | collective-permute-start | bytes 98312 | tf_op jit(solution)/shard_map/ppermute | solution.py:335
  75.5 3.1 %collective-permute-start.24 = (bf16[32,512]{1,0:T(8,128)(2,1)S(1)}, bf16[32,512]{1,0:T(8,128)(2,1)S(1)}, u32[]{:S(2)}, u32[]{:S(2)}) collective-permute-start(bf16[32,512]{1,0:T(8,128)(2,1)S(1)} %get-tuple-element.86), channel_id=1, source_target_pairs={{0,1},{1,0},{2,3},{3,2},{4,5},{5,4},{6,7},{7,6},{8,9},{9,8},{10,11... | collective-permute-start | bytes 98312 | tf_op jit(solution)/shard_map/ppermute | solution.py:335
  75.5 3.4 %collective-permute-start.22 = (bf16[32,512]{1,0:T(8,128)(2,1)S(1)}, bf16[32,512]{1,0:T(8,128)(2,1)S(1)}, u32[]{:S(2)}, u32[]{:S(2)}) collective-permute-start(bf16[32,512]{1,0:T(8,128)(2,1)S(1)} %get-tuple-element.87), channel_id=1, source_target_pairs={{0,3},{1,2},{2,1},{3,0},{4,7},{5,6},{6,5},{7,4},{8,11},{9,10},{10,... | collective-permute-start | bytes 98312 | tf_op jit(solution)/shard_map/ppermute | solution.py:335

commit v8 on v7

--- a/solution.py
+++ b/solution.py
@@ -104,8 +104,18 @@
         ) + jnp.dot(low, values[:, cols], preferred_element_type=F32)
 
 
+def back_kernel(earlier, scalars, sign_ref, kept_ref, partner_ref, *refs):
+    came_refs, mine_ref, lacked_ref = refs[:earlier], refs[earlier], refs[earlier + 1]
+    before = jnp.zeros(mine_ref.shape, F32)
+    for i, ref in enumerate(came_refs):
+        before += jnp.where(scalars[4 + i] == 1, ref[...].astype(F32), 0.0)
+    first = scalars[1] == 0
+    mine_ref[...] = before + jnp.where(first, 0.0, partner_ref[...].astype(F32))
+    lacked_ref[...] = (before + jnp.where(first, kept_ref[...].astype(F32), 0.0)).astype(BF16)
+
+
 def attend_kernel(
-    parts, scalars, sign_ref, within_ref, queries, residuals, gain_ref, mine_ref, other_ref, *refs
+    parts, scalars, within_ref, queries, residuals, gain_ref, mine_ref, other_ref, *refs
 ):
     piece_refs, hidden = refs[:-1], refs[-1]
     rows, full = hidden.shape
@@ -129,7 +139,7 @@
         piece[...] = hidden[pl.ds(pl.multiple_of((scalars[0] ^ j) * count, count), count), :]
 
 
-def norm_kernel(scalars, gain_ref, pack_ref, *refs):
+def norm_kernel(scalars, sign_ref, gain_ref, pack_ref, *refs):
     pieces, hidden_ref, out_ref = refs[:-2], refs[-2], refs[-1]
     width = pieces[0].shape[1]
     model = hidden_ref.shape[1]
@@ -218,51 +228,61 @@
     return list(range(0, count, 2)) + list(range(1, count, 2))[::-1]
 
 
-def dense_experts(block, scalars, turns, weights_gate, weights_up, expert_out):
-    count = lax.axis_size("seq")
+def far_sides(position, my_index, count):
+    place = jnp.where(position % 2 == 0, position // 2, count - 1 - position // 2)
+    onward = ((place // 2) % 2 == 0) != (my_index % 2 == 1)
+    return onward == (place % 2 == 1)
+
+
+def dense_experts(block, scalars, pick, weights_gate, weights_up, expert_out):
+    count, parts = lax.axis_size("seq"), lax.axis_size("exp")
     order = ring_order(count)
     far = count // 2
-    parts = lax.axis_size("exp")
-
-    def hop(rows, steps):
-        return lax.ppermute(
-            rows, "seq", [(order[p], order[(p + steps) % count]) for p in range(count)]
-        )
-
-    def far_hop(rows):
+
+    def trade(rows, pairs):
+        both = [(order[a], order[b]) for a, b in pairs]
+        return lax.ppermute(rows, "seq", both + [(b, a) for a, b in both])
+
+    def trade_first(rows):
+        return trade(rows, [(p, p + 1) for p in range(0, count, 2)])
+
+    def trade_second(rows):
+        return trade(rows, [(p, (p + 1) % count) for p in range(1, count, 2)])
+
+    def trade_far(rows):
         pairs = []
-        for p in range(count):
-            for e in range(parts):
-                target = order[(p + (2 if e % 2 == 0 else -2)) % count]
-                pairs.append((order[p] * parts + e, target * parts + e))
+        for e in range(parts):
+            for p in range(count):
+                ahead = (p // 2) % 2 == e % 2
+                other = order[(p + (2 if ahead else -2)) % count]
+                pairs.append((order[p] * parts + e, other * parts + e))
         return lax.ppermute(rows, ("seq", "exp"), pairs)
 
-    ahead, behind = [block], [block]
+    first, second = [block], [block]
     for distance in range(1, far):
-        came, went = hop(ahead[-1], 1), hop(behind[-1], -1)
+        came = trade_first(second[-1]), trade_second(first[-1])
         if distance == 1:
-            weights_out, _ = load_near(scalars, expert_out, 0, came)
-        ahead.append(came)
-        behind.append(went)
-    turned = turns[0]
-    farthest = far_hop(jnp.where(turned, behind[-2], ahead[-2]))
-    made = run_expert(
-        scalars, ahead + behind[1:] + [farthest], weights_gate, weights_up, weights_out
-    )
-    own, to_back, to_front, farthest = made[0], made[1:far], made[far:-1], made[-1]
-    going, coming = hop(to_front[-1], 1), hop(to_back[-1], -1)
-    early = far_hop(farthest)
-    for distance in range(far - 2, 0, -1):
-        front, back = to_front[distance - 1], to_back[distance - 1]
+            weights_out, _ = load_near(scalars, expert_out, 0, came[0])
+        first.append(came[0])
+        second.append(came[1])
+    farthest = trade_far(jnp.where(pick, first[-2], second[-2]))
+    own, *made, farthest = run_expert(
+        scalars, first + second[1:] + [farthest], weights_gate, weights_up, weights_out
+    )
+    made_first, made_second = made[:far - 1], made[far - 1:]
+    back_first, back_second = made_first[-1], made_second[-1]
+    early = trade_far(farthest)
+    for distance in range(far - 2, -1, -1):
+        to_second, to_first = trade_first(back_first), trade_second(back_second)
+        if distance == 0:
+            return own, to_second, to_first
+        terms_first = [made_first[distance - 1], to_first]
+        terms_second = [made_second[distance - 1], to_second]
         if distance == far - 2:
             nothing = jnp.zeros_like(early)
-            going = add_rows(going, front, jnp.where(turned, nothing, early))
-            coming = add_rows(coming, back, jnp.where(turned, early, nothing))
-        else:
-            going = add_rows(going, front)
-            coming = add_rows(coming, back)
-        going, coming = hop(going, 1), hop(coming, -1)
-    return own, going, coming
+            terms_first.append(jnp.where(pick, early, nothing))
+            terms_second.append(jnp.where(pick, nothing, early))
+        back_first, back_second = add_rows(*terms_first), add_rows(*terms_second)
 
 
 def slot_ids(block_routes, expert_count, capacity):
@@ -312,21 +332,24 @@
     return lax.ppermute(rows, "seq", [(i, i ^ (2 * distance)) for i in range(count)])
 
 
-def prior_states(total, later):
-    pairs = lax.axis_size("seq") // 2
-    bits = len(later)
-    if pairs <= 4:
-        terms = [
-            swap_pairs(total, distance).astype(F32) * later[distance.bit_length() - 1]
-            for distance in range(1, pairs)
-        ]
-        return sum(terms)
-    before = jnp.zeros(total.shape, F32)
-    for b in range(bits):
-        came = swap_pairs(total, 1 << b)
-        before = before + came.astype(F32) * later[b]
-        total = add_rows(total, came)
-    return before
+def pair_steps(pairs):
+    bits = pairs.bit_length() - 1
+    direct = pairs <= 4
+    steps = range(1, pairs) if direct else [1 << b for b in range(bits)]
+    return direct, [(d, d.bit_length() - 1) for d in steps]
+
+
+def prior_states(total):
+    count = lax.axis_size("seq")
+    direct, steps = pair_steps(count // 2)
+    terms = []
+    for distance, _ in steps:
+        terms.append(
+            lax.ppermute(total, "seq", [(i, i ^ (2 * distance)) for i in range(count)])
+        )
+        if not direct:
+            total = add_rows(total, terms[-1])
+    return terms
 
 
 def exchange(pieces):
@@ -362,17 +385,17 @@
     position = lax.axis_index("seq")
     my_index = lax.axis_index("exp")
     place = position % 2
-    scalars = jnp.stack([my_index, place, experts, position]).astype(jnp.int32)
+    _, steps = pair_steps(seq // 2)
+    scalars = jnp.stack(
+        [my_index, place, experts, position] + [(position >> (bit + 1)) & 1 for _, bit in steps]
+    ).astype(jnp.int32)
     swap = [(i, i ^ 1) for i in range(seq)]
-    pair_bits, part_bits = (seq // 2).bit_length() - 1, parts.bit_length() - 1
-    first, second, *later = [
-        flag.astype(F32).reshape(1, 1)
-        for flag in [1 - place, place] + [(position >> (b + 1)) & 1 for b in range(pair_bits)]
+    turns = [
+        ((my_index >> b) & 1 != 0).reshape(1, 1) for b in range(parts.bit_length() - 1)
     ]
-    turns = [((my_index >> b) & 1 != 0).reshape(1, 1) for b in range(part_bits)]
-    scalars, first, second, later, turns = lax.optimization_barrier(
-        (scalars, first, second, later, turns)
-    )
+    pick = far_sides(position, my_index, seq).reshape(1, 1)
+    my_rows = (my_index * count).astype(jnp.uint32)
+    scalars, turns, pick, my_rows = lax.optimization_barrier((scalars, turns, pick, my_rows))
     state, heads = shape((HEAD, half), BF16), shape((rows, width), BF16)
     kept, given, keys, values, query, rest, my_gain, my_norm = call(
         open_kernel,
@@ -391,27 +414,29 @@
         flops=6 * rows * rows * width,
     )
     dense = routes.shape[1] == experts
-    total, within = lax.optimization_barrier((add_rows(kept, partner), within))
-    before = prior_states(total, later)
-    sign = jnp.zeros((8, HEAD), F32)
+    total, sign = add_rows(kept, partner), jnp.zeros((8, HEAD), F32)
     if dense:
-        weights_gate, sign = load_near(scalars, expert_in[0], 0, total)
-    lacked = (before + kept.astype(F32) * first + sign[:1, :1]).astype(BF16)
-    mine = before + partner.astype(F32) * second
-    if dense:
-        weights_up, sign = load_near(scalars, expert_in[0], 1, lacked)
+        weights_gate, sign = load_near(scalars, expert_in[0], 0, given)
+        total, sign = lax.optimization_barrier((total, sign))
+    before = prior_states(total)
+    mine, lacked = call(
+        functools.partial(back_kernel, len(before)), [shape(state.shape, F32), state],
+        [scalars, sign, kept, partner, *before],
+    )
     other = lax.ppermute(lacked, "seq", swap)
     pieces = call(
         functools.partial(attend_kernel, parts),
         [shape((count, width), BF16)] * parts,
-        [scalars, sign, within, query, rest, my_gain, mine, other],
+        [scalars, within, query, rest, my_gain, mine, other],
         scratch=[pltpu.VMEM((rows, width), BF16)],
         flops=4 * rows * width * HEAD,
     )
     gathered = exchange(pieces)
-
-    my_routes = lax.dynamic_slice_in_dim(routes, my_index * count, count, 0)
-    my_gates = lax.dynamic_slice_in_dim(route_gates, my_index * count, count, 0)
+    if dense:
+        weights_up, sign = load_near(scalars, expert_in[0], 1, pieces[0])
+
+    my_routes = lax.dynamic_slice_in_dim(routes, my_rows, count, 0)
+    my_gates = lax.dynamic_slice_in_dim(route_gates, my_rows, count, 0)
     mixing = jnp.sum(
         jnp.where(
             my_routes[:, :, None] == jnp.arange(experts, dtype=jnp.int32),
@@ -428,11 +453,11 @@
     hidden, block = call(
         norm_kernel,
         [shape((count, model), BF16), shape((count, model + lanes), BF16)],
-        [scalars, my_norm, pack] + gathered,
+        [scalars, sign, my_norm, pack] + gathered,
     )
     if dense:
         terms = dense_experts(
-            block, scalars, turns, weights_gate, weights_up, expert_out
+            block, scalars, pick, weights_gate, weights_up, expert_out
         )
     else:
         mixed = routed_experts(block[:, :model], my_routes, my_gates, expert_in, expert_out)

time: 79.8 us -> 83 us (1.040)
  waiting for transfers between devices: 27.7 us -> 32.4 us
  starting transfers between devices: 30.5 us -> 28.2 us
  local copies, waits for them, and re-layouts: 1.51 us -> 2.35 us
    ppermute x17, waiting for transfers between devices: 22.1 us -> 27.2 us  [the longest x12 17.3 us: trade(): return lax.ppermute(rows, 'seq', both + [(b, a) for a, b in both])]
    ppermute x1, waiting for transfers between devices: 0.01 us -> 2.87 us  [per_device(): other = lax.ppermute(lacked, 'seq', swap)]
    ppermute x6, waiting for transfers between devices: 5.11 us -> 2.36 us  [exchange(): lax.ppermute(pieces[j], 'exp', [(i, i ^ j) for i in range(parts)])]
    unnamed x2 -> x8, local copies, waits for them, and re-layouts: 0.01 us -> 1.97 us
    ppermute x17, starting transfers between devices: 21.8 us -> 20.6 us  [the longest x12 12.5 us: trade(): return lax.ppermute(rows, 'seq', both + [(b, a) for a, b in both])]
    ppermute x1, starting transfers between devices: 1.55 us -> 0.51 us  [per_device(): other = lax.ppermute(lacked, 'seq', swap)]
    pallas_call x8 -> x9, Pallas kernels: 17.9 us -> 18.5 us  [call(): pl.pallas_call(kernel, out_shape=outs, in_specs=[SCALAR if i == 0 or i in...]
  transfers between devices with their start and end apart: 25 -> 25, of which waited for: 14 -> 17; matrix products, arithmetic and copies ran while one was open for 2% -> 1% of each run, Pallas kernels for 12% -> 12%
where the time goes in v8:
time: 83 us; the launch traced here: 82.8 us
  waiting for transfers between devices  32.4 us (39%)
  starting transfers between devices  28.2 us (34%)
  Pallas kernels  18.5 us (22%)
  local copies, waits for them, and re-layouts  2.35 us (3%)
  other arithmetic  1.09 us (1%)
    pallas_call x9, Pallas kernels, call(): pl.pallas_call(kernel, out_shape=outs, in_specs=[SCALAR if i == 0 or i in...  18.5 us
    ppermute x12, waiting for transfers between devices, trade(): return lax.ppermute(rows, 'seq', both + [(b, a) for a, b in both])  17.3 us
    ppermute x12, starting transfers between devices, trade(): return lax.ppermute(rows, 'seq', both + [(b, a) for a, b in both])  12.5 us
    ppermute x2, waiting for transfers between devices, trade_far(): return lax.ppermute(rows, ('seq', 'exp'), pairs)  5.43 us
    ppermute x3, waiting for transfers between devices, prior_states(): lax.ppermute(total, 'seq', [(i, i ^ 2 * distance) for i in range(count)])  4.48 us
    ppermute x3, starting transfers between devices, prior_states(): lax.ppermute(total, 'seq', [(i, i ^ 2 * distance) for i in range(count)])  4.45 us
    ppermute x6, starting transfers between devices, exchange(): lax.ppermute(pieces[j], 'exp', [(i, i ^ j) for i in range(parts)])  4.14 us
    ppermute x2, starting transfers between devices, trade_far(): return lax.ppermute(rows, ('seq', 'exp'), pairs)  3.62 us
  transfers between devices with their start and end apart: 25, of which 17 were waited for; matrix products, arithmetic and copies ran while one was open for 1% of the time, Pallas kernels for 12%

profile of v8, /device:TPU:0, one launch (start us, length us, event | category | flops | bytes accessed | tf_op | source)
XLA Modules:
  0.0 82.8 jit_solution(1485328940116483494)
XLA Ops:
  0.0 0.1 stack.24.scalars
  0.1 1.8 %shard_map.100 = (bf16[128,256]{1,0:T(8,128)(2,1)S(1)}, bf16[128,256]{1,0:T(8,128)(2,1)S(1)}, bf16[128,512]{1,0:T(8,128)(2,1)S(1)}, bf16[128,512]{1,0:T(8,128)(2...) custom-call(s32[7]{0:T(128)S(1)} %stack.24.scalars, ...), custom_call_target="tpu_custom_call" | custom-call | flops 16777216 | bytes 1200156 | tf_op jit(solution)/shard_map/pallas_call | solution.py:24
  1.9 3.0 %collective-permute-start = (bf16[128,256]{1,0:T(8,128)(2,1)S(1)}, bf16[128,256]{1,0:T(8,128)(2,1)S(1)}, u32[]{:S(2)}, u32[]{:S(2)}) collective-permute-start(bf16[128,256]{1,0:T(8,128)(2,1)S(1)} %get-tuple-element.50.after_ref), channel_id=1, source_target_pairs={{0,4},{4,0},{8,12},{12,8},{16,20},{20,16},{24,28},{28,24},{1,5},{5... | collective-permute-start | bytes 196616 | tf_op jit(solution)/shard_map/ppermute | solution.py:411
  4.9 2.8 %shard_map.102 = (bf16[2048,1024]{1,0:T(8,128)(2,1)S(1)}, f32[8,128]{1,0:T(8,128)S(1)}) custom-call(s32[7]{0:T(128)S(1)} %stack.24.scalars, bf16[2,2048,1024]{2,1,0:T(8,128)(2,1)} %bitcast.14, bf16[128,256]{1,0:T(8,128)(2,1)S(1)} %get-tuple-element.50.after_ref), custom_call_target="tpu_custom_call" | custom-call | bytes 12652572 | tf_op jit(solution)/shard_map/pallas_call | solution.py:24
  7.7 2.0 %copy-done.1 = bf16[2048,1024]{1,0:T(8,128)(2,1)} copy-done((bf16[2048,1024]{1,0:T(8,128)(2,1)}, bf16[2048,1024]{1,0:T(8,128)(2,1)S(1)}, u32[]{:S(2)}) %copy-start.1) | copy-done | bytes 4194328
  9.7 0.1 constant_dynamic-slice_fusion
  9.7 0.1 constant_dynamic-slice_fusion.1
  9.8 3.7 %collective-permute-start.3 = (bf16[128,256]{1,0:T(8,128)(2,1)S(1)}, bf16[128,256]{1,0:T(8,128)(2,1)S(1)}, u32[]{:S(2)}, u32[]{:S(2)}) collective-permute-start(bf16[128,256]{1,0:T(8,128)(2,1)S(1)} %add_convert_fusion.5), channel_id=1, source_target_pairs={{0,24},{4,28},{8,16},{12,20},{16,8},{20,12},{24,0},{28,4},{1,25},{... | collective-permute-start | bytes 196616 | tf_op jit(solution)/shard_map/ppermute | solution.py:348
  13.5 0.8 collective-permute-start.1
  14.3 0.1 copy.16
  14.4 0.1 copy.15
  14.5 2.3 %collective-permute-done.3.refs_2_ = bf16[128,256]{1,0:T(8,128)(2,1)S(1)} collective-permute-done((bf16[128,256]{1,0:T(8,128)(2,1)S(1)}, bf16[128,256]{1,0:T(8,128)(2,1)S(1)}, u32[]{:S(2)}, u32[]{:S(2)}) %collective-permute-start.3) | collective-permute-done | bytes 65568 | tf_op jit(solution)/shard_map/ppermute | solution.py:348
  16.8 2.1 %collective-permute-done.2.refs_1_ = bf16[128,256]{1,0:T(8,128)(2,1)S(1)} collective-permute-done((bf16[128,256]{1,0:T(8,128)(2,1)S(1)}, bf16[128,256]{1,0:T(8,128)(2,1)S(1)}, u32[]{:S(2)}, u32[]{:S(2)}) %collective-permute-start.2) | collective-permute-done | bytes 65568 | tf_op jit(solution)/shard_map/ppermute | solution.py:348
  18.9 0.1 collective-permute-done.1.refs_0_
  18.9 0.6 shard_map.103
  19.6 0.5 collective-permute-start.4
  20.1 0.9 %shard_map.101.within_ref = f32[128,512]{1,0:T(8,128)S(1)} custom-call(s32[7]{0:T(128)S(1)} %stack.24.scalars, bf16[128,512]{1,0:T(8,128)(2,1)S(1)} %get-tuple-element.44.keys, bf16[128,512]{1,0:T(8,128)(2,1)S(1)} %get-tuple-element.45.values, bf16[128,512]{1,0:T(8,128)(2,1)S(1)} %get-tuple-element.46.queries), custom_call_target="tpu_custom_call" | custom-call | flops 50331648 | bytes 655388 | tf_op jit(solution)/shard_map/pallas_call | solution.py:24
  21.0 2.9 %collective-permute-done.4.other_ref = bf16[128,256]{1,0:T(8,128)(2,1)S(1)} collective-permute-done((bf16[128,256]{1,0:T(8,128)(2,1)S(1)}, bf16[128,256]{1,0:T(8,128)(2,1)S(1)}, u32[]{:S(2)}, u32[]{:S(2)}) %collective-permute-start.4) | collective-permute-done | bytes 65568 | tf_op jit(solution)/shard_map/ppermute | solution.py:426
  23.9 0.9 %shard_map.104 = (bf16[32,512]{1,0:T(8,128)(2,1)S(1)}, bf16[32,512]{1,0:T(8,128)(2,1)S(1)}, bf16[32,512]{1,0:T(8,128)(2,1)S(1)}, bf16[32,512]{1,0:T(8,128)(2,1)S(1)}) custom-call(s32[7]{0:T(128)S(1)} %stack.24.scalars, f32[128,512]{1,0:T(8,128)S(1)} %shard_map.101.within_ref, bf16[128,512]{1,0:T(8,128)(2,1)S(1)} %get-tuple-element.46.queries, ...), custom_call_target="tpu_custom_call" | custom-call | flops 33554432 | bytes 854044 | tf_op jit(solution)/shard_map/pallas_call | solution.py:24
  24.8 0.1 collective-permute-start.5
  24.9 1.6 %collective-permute-start.6 = (bf16[32,512]{1,0:T(8,128)(2,1)S(1)}, bf16[32,512]{1,0:T(8,128)(2,1)S(1)}, u32[]{:S(2)}, u32[]{:S(2)}) collective-permute-start(bf16[32,512]{1,0:T(8,128)(2,1)S(1)} %get-tuple-element.61), channel_id=1, source_target_pairs={{0,2},{1,3},{2,0},{3,1},{4,6},{5,7},{6,4},{7,5},{8,10},{9,11},{10,... | collective-permute-start | bytes 98312 | tf_op jit(solution)/shard_map/ppermute | solution.py:358
  26.4 0.3 collective-permute-start.7
  26.7 0.1 fusion.2.pack_ref
  26.8 2.8 %shard_map.105 = (bf16[2048,1024]{1,0:T(8,128)(2,1)S(1)}, f32[8,128]{1,0:T(8,128)S(1)}) custom-call(s32[7]{0:T(128)S(1)} %stack.24.scalars, bf16[2,2048,1024]{2,1,0:T(8,128)(2,1)} %bitcast.15, bf16[32,512]{1,0:T(8,128)(2,1)S(1)} %get-tuple-element.56.after_ref.refs_0_), custom_call_target="tpu_custom_call" | custom-call | bytes 12619804 | tf_op jit(solution)/shard_map/pallas_call | solution.py:24
  29.6 0.0 collective-permute-done.5.refs_1_
  29.6 0.2 collective-permute-done.7.refs_3_
  29.8 0.7 shard_map.106
  30.5 0.6 collective-permute-start.9
  31.1 1.8 %collective-permute-start.8 = (bf16[32,2176]{1,0:T(8,128)(2,1)S(1)}, bf16[32,2176]{1,0:T(8,128)(2,1)S(1)}, u32[]{:S(2)}, u32[]{:S(2)}) collective-permute-start(bf16[32,2176]{1,0:T(8,128)(2,1)S(1)} %get-tuple-element.66.refs_0_), channel_id=1, source_target_pairs={{0,8},{16,24},{28,20},{12,4},{8,0},{24,16},{20,28},{4,12},{1,9},{1... | collective-permute-start | bytes 417800 | tf_op jit(solution)/shard_map/ppermute | solution.py:244
  32.8 3.4 %collective-permute-done.9.refs_4_ = bf16[32,2176]{1,0:T(8,128)(2,1)S(1)} collective-permute-done((bf16[32,2176]{1,0:T(8,128)(2,1)S(1)}, bf16[32,2176]{1,0:T(8,128)(2,1)S(1)}, u32[]{:S(2)}, u32[]{:S(2)}) %collective-permute-start.9) | collective-permute-done | bytes 139296 | tf_op jit(solution)/shard_map/ppermute | solution.py:244
  36.3 1.0 %collective-permute-start.10 = (bf16[32,2176]{1,0:T(8,128)(2,1)S(1)}, bf16[32,2176]{1,0:T(8,128)(2,1)S(1)}, u32[]{:S(2)}, u32[]{:S(2)}) collective-permute-start(bf16[32,2176]{1,0:T(8,128)(2,1)S(1)} %collective-permute-done.9.refs_4_), channel_id=1, source_target_pairs={{0,8},{16,24},{28,20},{12,4},{8,0},{24,16},{20,28},{4,12},{1,9},{1... | collective-permute-start | bytes 417800 | tf_op jit(solution)/shard_map/ppermute | solution.py:244
  37.3 0.8 collective-permute-start.11
  38.0 3.3 %collective-permute-done.10.refs_2_ = bf16[32,2176]{1,0:T(8,128)(2,1)S(1)} collective-permute-done((bf16[32,2176]{1,0:T(8,128)(2,1)S(1)}, bf16[32,2176]{1,0:T(8,128)(2,1)S(1)}, u32[]{:S(2)}, u32[]{:S(2)}) %collective-permute-start.10) | collective-permute-done | bytes 139296 | tf_op jit(solution)/shard_map/ppermute | solution.py:244
  41.3 0.5 collective-permute-start.13
  41.9 0.6 collective-permute-done.11.refs_5_
  42.5 2.8 %collective-permute-start.14 = (bf16[32,2176]{1,0:T(8,128)(2,1)S(1)}, bf16[32,2176]{1,0:T(8,128)(2,1)S(1)}, u32[]{:S(2)}, u32[]{:S(2)}) collective-permute-start(bf16[32,2176]{1,0:T(8,128)(2,1)S(1)} %broadcast_select_fusion), channel_id=1, source_target_pairs={{0,16},{8,24},{16,0},{24,8},{28,12},{20,4},{12,28},{4,20},{1,13},{... | collective-permute-start | bytes 417800 | tf_op jit(solution)/shard_map/ppermute | solution.py:259
  45.3 3.3 %shard_map.107 = (bf16[1024,2048]{1,0:T(8,128)(2,1)S(1)}, f32[8,128]{1,0:T(8,128)}) custom-call(s32[7]{0:T(128)S(1)} %stack.24.scalars, bf16[1,1024,2048]{2,1,0:T(8,128)(2,1)} %source.1, bf16[32,2176]{1,0:T(8,128)(2,1)S(1)} %collective-permute-done.8.after_ref.refs_1_), custom_call_target="tpu_custom_call" | custom-call | bytes 8531996 | tf_op jit(solution)/shard_map/pallas_call | solution.py:24
  48.6 0.0 collective-permute-done.13.refs_6_
  48.6 1.4 %collective-permute-done.14.refs_7_ = bf16[32,2176]{1,0:T(8,128)(2,1)S(1)} collective-permute-done((bf16[32,2176]{1,0:T(8,128)(2,1)S(1)}, bf16[32,2176]{1,0:T(8,128)(2,1)S(1)}, u32[]{:S(2)}, u32[]{:S(2)}) %collective-permute-start.14) | collective-permute-done | bytes 139296 | tf_op jit(solution)/shard_map/ppermute | solution.py:259
  50.1 0.8 %collective-permute-done.12.refs_3_ = bf16[32,2176]{1,0:T(8,128)(2,1)S(1)} collective-permute-done((bf16[32,2176]{1,0:T(8,128)(2,1)S(1)}, bf16[32,2176]{1,0:T(8,128)(2,1)S(1)}, u32[]{:S(2)}, u32[]{:S(2)}) %collective-permute-start.12) | collective-permute-done | bytes 139296 | tf_op jit(solution)/shard_map/ppermute | solution.py:244
  50.9 4.8 %shard_map.108 = (bf16[32,2048]{1,0:T(8,128)(2,1)S(1)}, bf16[32,2048]{1,0:T(8,128)(2,1)S(1)}, bf16[32,2048]{1,0:T(8,128)(2,1)S(1)}, bf16[32,2048]{1,0:T(8,128)(2...) custom-call(s32[7]{0:T(128)S(1)} %stack.24.scalars, ...), custom_call_target="tpu_custom_call" | custom-call | flops 3221225472 | bytes 14745628 | tf_op jit(solution)/shard_map/pallas_call | solution.py:24
  55.7 1.0 %collective-permute-start.15 = (bf16[32,2048]{1,0:T(8,128)(2,1)S(1)}, bf16[32,2048]{1,0:T(8,128)(2,1)S(1)}, u32[]{:S(2)}, u32[]{:S(2)}) collective-permute-start(bf16[32,2048]{1,0:T(8,128)(2,1)S(1)} %get-tuple-element.72), channel_id=1, source_target_pairs={{0,8},{16,24},{28,20},{12,4},{8,0},{24,16},{20,28},{4,12},{1,9},{1... | collective-permute-start | bytes 393224 | tf_op jit(solution)/shard_map/ppermute | solution.py:244
  56.6 0.8 collective-permute-start.16
  57.5 1.6 %collective-permute-start.19 = (bf16[32,2048]{1,0:T(8,128)(2,1)S(1)}, bf16[32,2048]{1,0:T(8,128)(2,1)S(1)}, u32[]{:S(2)}, u32[]{:S(2)}) collective-permute-start(bf16[32,2048]{1,0:T(8,128)(2,1)S(1)} %get-tuple-element.76), channel_id=1, source_target_pairs={{8,16},{24,28},{20,12},{4,0},{16,8},{28,24},{12,20},{0,4},{9,17},{... | collective-permute-start | bytes 393224 | tf_op jit(solution)/shard_map/ppermute | solution.py:244
  59.0 1.7 %collective-permute-done.15 = bf16[32,2048]{1,0:T(8,128)(2,1)S(1)} collective-permute-done((bf16[32,2048]{1,0:T(8,128)(2,1)S(1)}, bf16[32,2048]{1,0:T(8,128)(2,1)S(1)}, u32[]{:S(2)}, u32[]{:S(2)}) %collective-permute-start.15) | collective-permute-done | bytes 131104 | tf_op jit(solution)/shard_map/ppermute | solution.py:244
  60.7 4.0 %collective-permute-done.16 = bf16[32,2048]{1,0:T(8,128)(2,1)S(1)} collective-permute-done((bf16[32,2048]{1,0:T(8,128)(2,1)S(1)}, bf16[32,2048]{1,0:T(8,128)(2,1)S(1)}, u32[]{:S(2)}, u32[]{:S(2)}) %collective-permute-start.16) | collective-permute-done | bytes 131104 | tf_op jit(solution)/shard_map/ppermute | solution.py:259
  64.7 0.0 collective-permute-done.19
  64.7 0.1 add_convert_fusion.4
  64.8 1.2 %collective-permute-start.17 = (bf16[32,2048]{1,0:T(8,128)(2,1)S(1)}, bf16[32,2048]{1,0:T(8,128)(2,1)S(1)}, u32[]{:S(2)}, u32[]{:S(2)}) collective-permute-start(bf16[32,2048]{1,0:T(8,128)(2,1)S(1)} %get-tuple-element.86), channel_id=1, source_target_pairs={{8,16},{24,28},{20,12},{4,0},{16,8},{28,24},{12,20},{0,4},{9,17},{... | collective-permute-start | bytes 393224 | tf_op jit(solution)/shard_map/ppermute | solution.py:244
  66.0 1.5 %collective-permute-start.20 = (bf16[32,2048]{1,0:T(8,128)(2,1)S(1)}, bf16[32,2048]{1,0:T(8,128)(2,1)S(1)}, u32[]{:S(2)}, u32[]{:S(2)}) collective-permute-start(bf16[32,2048]{1,0:T(8,128)(2,1)S(1)} %get-tuple-element.87), channel_id=1, source_target_pairs={{0,8},{16,24},{28,20},{12,4},{8,0},{24,16},{20,28},{4,12},{1,9},{1... | collective-permute-start | bytes 393224 | tf_op jit(solution)/shard_map/ppermute | solution.py:244
  67.6 3.0 %collective-permute-done.17 = bf16[32,2048]{1,0:T(8,128)(2,1)S(1)} collective-permute-done((bf16[32,2048]{1,0:T(8,128)(2,1)S(1)}, bf16[32,2048]{1,0:T(8,128)(2,1)S(1)}, u32[]{:S(2)}, u32[]{:S(2)}) %collective-permute-start.17) | collective-permute-done | bytes 131104 | tf_op jit(solution)/shard_map/ppermute | solution.py:244
  70.6 1.9 %collective-permute-start.18 = (bf16[32,2048]{1,0:T(8,128)(2,1)S(1)}, bf16[32,2048]{1,0:T(8,128)(2,1)S(1)}, u32[]{:S(2)}, u32[]{:S(2)}) collective-permute-start(bf16[32,2048]{1,0:T(8,128)(2,1)S(1)} %add_convert_fusion.3), channel_id=1, source_target_pairs={{0,8},{16,24},{28,20},{12,4},{8,0},{24,16},{20,28},{4,12},{1,9},{1... | collective-permute-start | bytes 393224 | tf_op jit(solution)/shard_map/ppermute | solution.py:244
  72.5 0.0 collective-permute-done.20
  72.6 0.6 collective-permute-start.21
  73.2 2.5 %collective-permute-done.18 = bf16[32,2048]{1,0:T(8,128)(2,1)S(1)} collective-permute-done((bf16[32,2048]{1,0:T(8,128)(2,1)S(1)}, bf16[32,2048]{1,0:T(8,128)(2,1)S(1)}, u32[]{:S(2)}, u32[]{:S(2)}) %collective-permute-start.18) | collective-permute-done | bytes 131104 | tf_op jit(solution)/shard_map/ppermute | solution.py:244
  75.7 2.0 %collective-permute-done.21 = bf16[32,2048]{1,0:T(8,128)(2,1)S(1)} collective-permute-done((bf16[32,2048]{1,0:T(8,128)(2,1)S(1)}, bf16[32,2048]{1,0:T(8,128)(2,1)S(1)}, u32[]{:S(2)}, u32[]{:S(2)}) %collective-permute-start.21) | collective-permute-done | bytes 131104 | tf_op jit(solution)/shard_map/ppermute | solution.py:244
  77.6 0.1 add_convert_fusion
  77.7 1.0 %collective-permute-start.23 = (bf16[32,512]{1,0:T(8,128)(2,1)S(1)}, bf16[32,512]{1,0:T(8,128)(2,1)S(1)}, u32[]{:S(2)}, u32[]{:S(2)}) collective-permute-start(bf16[32,512]{1,0:T(8,128)(2,1)S(1)} %get-tuple-element.77), channel_id=1, source_target_pairs={{0,2},{1,3},{2,0},{3,1},{4,6},{5,7},{6,4},{7,5},{8,10},{9,11},{10,... | collective-permute-start | bytes 98312 | tf_op jit(solution)/shard_map/ppermute | solution.py:358
  78.7 0.0 collective-permute-start.24
  78.8 1.2 %collective-permute-start.22 = (bf16[32,512]{1,0:T(8,128)(2,1)S(1)}, bf16[32,512]{1,0:T(8,128)(2,1)S(1)}, u32[]{:S(2)}, u32[]{:S(2)}) collective-permute-start(bf16[32,512]{1,0:T(8,128)(2,1)S(1)} %get-tuple-element.85), channel_id=1, source_target_pairs={{0,3},{1,2},{2,1},{3,0},{4,7},{5,6},{6,5},{7,4},{8,11},{9,10},{10,... | collective-permute-start | bytes 98312 | tf_op jit(solution)/shard_map/ppermute | solution.py:358
  79.9 1.8 %collective-permute-done.23 = bf16[32,512]{1,0:T(8,128)(2,1)S(1)} collective-permute-done((bf16[32,512]{1,0:T(8,128)(2,1)S(1)}, bf16[32,512]{1,0:T(8,128)(2,1)S(1)}, u32[]{:S(2)}, u32[]{:S(2)}) %collective-permute-start.23) | collective-permute-done | bytes 32800 | tf_op jit(solution)/shard_map/ppermute | solution.py:358
  81.7 0.0 collective-permute-done.24
  81.7 0.4 collective-permute-done.22
  82.1 0.7 pad_maximum_fusion
  (21 shorter events, 0.2 us)
Async XLA Ops:
  0.0 9.7 %copy-start = (f32[128,8]{0,1:T(8,128)S(1)}, f32[128,8]{0,1:T(8,128)}, u32[]{:S(2)}) copy-start(f32[128,8]{0,1:T(8,128)} %param.17) | copy-start | bytes 12292
  1.9 7.9 %collective-permute-start = (bf16[128,256]{1,0:T(8,128)(2,1)S(1)}, bf16[128,256]{1,0:T(8,128)(2,1)S(1)}, u32[]{:S(2)}, u32[]{:S(2)}) collective-permute-start(bf16[128,256]{1,0:T(8,128)(2,1)S(1)} %get-tuple-element.50.after_ref), channel_id=1, source_target_pairs={{0,4},{4,0},{8,12},{12,8},{16,20},{20,16},{24,28},{28,24},{1,5},{5... | collective-permute-start | bytes 196616 | tf_op jit(solution)/shard_map/ppermute | solution.py:411
  4.9 4.8 %copy-start.3 = (s32[128,8]{0,1:T(8,128)S(1)}, s32[128,8]{0,1:T(8,128)}, u32[]{:S(2)}) copy-start(s32[128,8]{0,1:T(8,128)} %param.16) | copy-start | bytes 12292
  7.7 2.0 %copy-start.1 = (bf16[2048,1024]{1,0:T(8,128)(2,1)}, bf16[2048,1024]{1,0:T(8,128)(2,1)S(1)}, u32[]{:S(2)}) copy-start(bf16[2048,1024]{1,0:T(8,128)(2,1)S(1)} %get-tuple-element.64.gate_ref) | copy-start | bytes 12582916
  9.8 6.9 %collective-permute-start.3 = (bf16[128,256]{1,0:T(8,128)(2,1)S(1)}, bf16[128,256]{1,0:T(8,128)(2,1)S(1)}, u32[]{:S(2)}, u32[]{:S(2)}) collective-permute-start(bf16[128,256]{1,0:T(8,128)(2,1)S(1)} %add_convert_fusion.5), channel_id=1, source_target_pairs={{0,24},{4,28},{8,16},{12,20},{16,8},{20,12},{24,0},{28,4},{1,25},{... | collective-permute-start | bytes 196616 | tf_op jit(solution)/shard_map/ppermute | solution.py:348
  13.5 5.4 %collective-permute-start.2 = (bf16[128,256]{1,0:T(8,128)(2,1)S(1)}, bf16[128,256]{1,0:T(8,128)(2,1)S(1)}, u32[]{:S(2)}, u32[]{:S(2)}) collective-permute-start(bf16[128,256]{1,0:T(8,128)(2,1)S(1)} %add_convert_fusion.5), channel_id=1, source_target_pairs={{0,16},{4,20},{8,24},{12,28},{16,0},{20,4},{24,8},{28,12},{1,17},{... | collective-permute-start | bytes 196616 | tf_op jit(solution)/shard_map/ppermute | solution.py:348
  13.5 5.4 %collective-permute-start.1 = (bf16[128,256]{1,0:T(8,128)(2,1)S(1)}, bf16[128,256]{1,0:T(8,128)(2,1)S(1)}, u32[]{:S(2)}, u32[]{:S(2)}) collective-permute-start(bf16[128,256]{1,0:T(8,128)(2,1)S(1)} %add_convert_fusion.5), channel_id=1, source_target_pairs={{0,8},{4,12},{8,0},{12,4},{16,24},{20,28},{24,16},{28,20},{1,9},{5... | collective-permute-start | bytes 196616 | tf_op jit(solution)/shard_map/ppermute | solution.py:348
  19.6 4.3 %collective-permute-start.4 = (bf16[128,256]{1,0:T(8,128)(2,1)S(1)}, bf16[128,256]{1,0:T(8,128)(2,1)S(1)}, u32[]{:S(2)}, u32[]{:S(2)}) collective-permute-start(bf16[128,256]{1,0:T(8,128)(2,1)S(1)} %get-tuple-element.55), channel_id=1, source_target_pairs={{0,4},{4,0},{8,12},{12,8},{16,20},{20,16},{24,28},{28,24},{1,5},{5... | collective-permute-start | bytes 196616 | tf_op jit(solution)/shard_map/ppermute | solution.py:426
  24.8 4.8 %collective-permute-start.5 = (bf16[32,512]{1,0:T(8,128)(2,1)S(1)}, bf16[32,512]{1,0:T(8,128)(2,1)S(1)}, u32[]{:S(2)}, u32[]{:S(2)}) collective-permute-start(bf16[32,512]{1,0:T(8,128)(2,1)S(1)} %get-tuple-element.60), channel_id=1, source_target_pairs={{0,1},{1,0},{2,3},{3,2},{4,5},{5,4},{6,7},{7,6},{8,9},{9,8},{10,11... | collective-permute-start | bytes 98312 | tf_op jit(solution)/shard_map/ppermute | solution.py:358
  24.9 4.7 %collective-permute-start.6 = (bf16[32,512]{1,0:T(8,128)(2,1)S(1)}, bf16[32,512]{1,0:T(8,128)(2,1)S(1)}, u32[]{:S(2)}, u32[]{:S(2)}) collective-permute-start(bf16[32,512]{1,0:T(8,128)(2,1)S(1)} %get-tuple-element.61), channel_id=1, source_target_pairs={{0,2},{1,3},{2,0},{3,1},{4,6},{5,7},{6,4},{7,5},{8,10},{9,11},{10,... | collective-permute-start | bytes 98312 | tf_op jit(solution)/shard_map/ppermute | solution.py:358
  26.4 3.3 %collective-permute-start.7 = (bf16[32,512]{1,0:T(8,128)(2,1)S(1)}, bf16[32,512]{1,0:T(8,128)(2,1)S(1)}, u32[]{:S(2)}, u32[]{:S(2)}) collective-permute-start(bf16[32,512]{1,0:T(8,128)(2,1)S(1)} %get-tuple-element.62), channel_id=1, source_target_pairs={{0,3},{1,2},{2,1},{3,0},{4,7},{5,6},{6,5},{7,4},{8,11},{9,10},{10,... | collective-permute-start | bytes 98312 | tf_op jit(solution)/shard_map/ppermute | solution.py:358
  29.6 21.3 %copy-start.2 = (bf16[2048,1024]{1,0:T(8,128)(2,1)S(1)}, bf16[2048,1024]{1,0:T(8,128)(2,1)}, u32[]{:S(2)}) copy-start(bf16[2048,1024]{1,0:T(8,128)(2,1)} %copy-done.1) | copy-start | bytes 12582916
  30.5 5.8 %collective-permute-start.9 = (bf16[32,2176]{1,0:T(8,128)(2,1)S(1)}, bf16[32,2176]{1,0:T(8,128)(2,1)S(1)}, u32[]{:S(2)}, u32[]{:S(2)}) collective-permute-start(bf16[32,2176]{1,0:T(8,128)(2,1)S(1)} %get-tuple-element.66.refs_0_), channel_id=1, source_target_pairs={{8,16},{24,28},{20,12},{4,0},{16,8},{28,24},{12,20},{0,4},{9,17},{... | collective-permute-start | bytes 417800 | tf_op jit(solution)/shard_map/ppermute | solution.py:244
  31.1 6.2 %collective-permute-start.8 = (bf16[32,2176]{1,0:T(8,128)(2,1)S(1)}, bf16[32,2176]{1,0:T(8,128)(2,1)S(1)}, u32[]{:S(2)}, u32[]{:S(2)}) collective-permute-start(bf16[32,2176]{1,0:T(8,128)(2,1)S(1)} %get-tuple-element.66.refs_0_), channel_id=1, source_target_pairs={{0,8},{16,24},{28,20},{12,4},{8,0},{24,16},{20,28},{4,12},{1,9},{1... | collective-permute-start | bytes 417800 | tf_op jit(solution)/shard_map/ppermute | solution.py:244
  36.3 5.1 %collective-permute-start.10 = (bf16[32,2176]{1,0:T(8,128)(2,1)S(1)}, bf16[32,2176]{1,0:T(8,128)(2,1)S(1)}, u32[]{:S(2)}, u32[]{:S(2)}) collective-permute-start(bf16[32,2176]{1,0:T(8,128)(2,1)S(1)} %collective-permute-done.9.refs_4_), channel_id=1, source_target_pairs={{0,8},{16,24},{28,20},{12,4},{8,0},{24,16},{20,28},{4,12},{1,9},{1... | collective-permute-start | bytes 417800 | tf_op jit(solution)/shard_map/ppermute | solution.py:244
  37.3 5.2 %collective-permute-start.11 = (bf16[32,2176]{1,0:T(8,128)(2,1)S(1)}, bf16[32,2176]{1,0:T(8,128)(2,1)S(1)}, u32[]{:S(2)}, u32[]{:S(2)}) collective-permute-start(bf16[32,2176]{1,0:T(8,128)(2,1)S(1)} %collective-permute-done.8.after_ref.refs_1_), channel_id=1, source_target_pairs={{8,16},{24,28},{20,12},{4,0},{16,8},{28,24},{12,20},{0,4},{9,17},{... | collective-permute-start | bytes 417800 | tf_op jit(solution)/shard_map/ppermute | solution.py:244
  41.3 7.3 %collective-permute-start.13 = (bf16[32,2176]{1,0:T(8,128)(2,1)S(1)}, bf16[32,2176]{1,0:T(8,128)(2,1)S(1)}, u32[]{:S(2)}, u32[]{:S(2)}) collective-permute-start(bf16[32,2176]{1,0:T(8,128)(2,1)S(1)} %collective-permute-done.10.refs_2_), channel_id=1, source_target_pairs={{8,16},{24,28},{20,12},{4,0},{16,8},{28,24},{12,20},{0,4},{9,17},{... | collective-permute-start | bytes 417800 | tf_op jit(solution)/shard_map/ppermute | solution.py:244
  42.5 7.6 %collective-permute-start.14 = (bf16[32,2176]{1,0:T(8,128)(2,1)S(1)}, bf16[32,2176]{1,0:T(8,128)(2,1)S(1)}, u32[]{:S(2)}, u32[]{:S(2)}) collective-permute-start(bf16[32,2176]{1,0:T(8,128)(2,1)S(1)} %broadcast_select_fusion), channel_id=1, source_target_pairs={{0,16},{8,24},{16,0},{24,8},{28,12},{20,4},{12,28},{4,20},{1,13},{... | collective-permute-start | bytes 417800 | tf_op jit(solution)/shard_map/ppermute | solution.py:259
  45.3 5.6 %collective-permute-start.12 = (bf16[32,2176]{1,0:T(8,128)(2,1)S(1)}, bf16[32,2176]{1,0:T(8,128)(2,1)S(1)}, u32[]{:S(2)}, u32[]{:S(2)}) collective-permute-start(bf16[32,2176]{1,0:T(8,128)(2,1)S(1)} %collective-permute-done.11.refs_5_), channel_id=1, source_target_pairs={{0,8},{16,24},{28,20},{12,4},{8,0},{24,16},{20,28},{4,12},{1,9},{1... | collective-permute-start | bytes 417800 | tf_op jit(solution)/shard_map/ppermute | solution.py:244
  55.7 5.0 %collective-permute-start.15 = (bf16[32,2048]{1,0:T(8,128)(2,1)S(1)}, bf16[32,2048]{1,0:T(8,128)(2,1)S(1)}, u32[]{:S(2)}, u32[]{:S(2)}) collective-permute-start(bf16[32,2048]{1,0:T(8,128)(2,1)S(1)} %get-tuple-element.72), channel_id=1, source_target_pairs={{0,8},{16,24},{28,20},{12,4},{8,0},{24,16},{20,28},{4,12},{1,9},{1... | collective-permute-start | bytes 393224 | tf_op jit(solution)/shard_map/ppermute | solution.py:244
  56.6 8.1 %collective-permute-start.16 = (bf16[32,2048]{1,0:T(8,128)(2,1)S(1)}, bf16[32,2048]{1,0:T(8,128)(2,1)S(1)}, u32[]{:S(2)}, u32[]{:S(2)}) collective-permute-start(bf16[32,2048]{1,0:T(8,128)(2,1)S(1)} %get-tuple-element.73), channel_id=1, source_target_pairs={{0,16},{8,24},{16,0},{24,8},{28,12},{20,4},{12,28},{4,20},{1,13},{... | collective-permute-start | bytes 393224 | tf_op jit(solution)/shard_map/ppermute | solution.py:259
  57.5 7.2 %collective-permute-start.19 = (bf16[32,2048]{1,0:T(8,128)(2,1)S(1)}, bf16[32,2048]{1,0:T(8,128)(2,1)S(1)}, u32[]{:S(2)}, u32[]{:S(2)}) collective-permute-start(bf16[32,2048]{1,0:T(8,128)(2,1)S(1)} %get-tuple-element.76), channel_id=1, source_target_pairs={{8,16},{24,28},{20,12},{4,0},{16,8},{28,24},{12,20},{0,4},{9,17},{... | collective-permute-start | bytes 393224 | tf_op jit(solution)/shard_map/ppermute | solution.py:244
  64.8 5.8 %collective-permute-start.17 = (bf16[32,2048]{1,0:T(8,128)(2,1)S(1)}, bf16[32,2048]{1,0:T(8,128)(2,1)S(1)}, u32[]{:S(2)}, u32[]{:S(2)}) collective-permute-start(bf16[32,2048]{1,0:T(8,128)(2,1)S(1)} %get-tuple-element.86), channel_id=1, source_target_pairs={{8,16},{24,28},{20,12},{4,0},{16,8},{28,24},{12,20},{0,4},{9,17},{... | collective-permute-start | bytes 393224 | tf_op jit(solution)/shard_map/ppermute | solution.py:244
  66.0 6.5 %collective-permute-start.20 = (bf16[32,2048]{1,0:T(8,128)(2,1)S(1)}, bf16[32,2048]{1,0:T(8,128)(2,1)S(1)}, u32[]{:S(2)}, u32[]{:S(2)}) collective-permute-start(bf16[32,2048]{1,0:T(8,128)(2,1)S(1)} %get-tuple-element.87), channel_id=1, source_target_pairs={{0,8},{16,24},{28,20},{12,4},{8,0},{24,16},{20,28},{4,12},{1,9},{1... | collective-permute-start | bytes 393224 | tf_op jit(solution)/shard_map/ppermute | solution.py:244
  70.6 5.0 %collective-permute-start.18 = (bf16[32,2048]{1,0:T(8,128)(2,1)S(1)}, bf16[32,2048]{1,0:T(8,128)(2,1)S(1)}, u32[]{:S(2)}, u32[]{:S(2)}) collective-permute-start(bf16[32,2048]{1,0:T(8,128)(2,1)S(1)} %add_convert_fusion.3), channel_id=1, source_target_pairs={{0,8},{16,24},{28,20},{12,4},{8,0},{24,16},{20,28},{4,12},{1,9},{1... | collective-permute-start | bytes 393224 | tf_op jit(solution)/shard_map/ppermute | solution.py:244
  72.6 5.0 %collective-permute-start.21 = (bf16[32,2048]{1,0:T(8,128)(2,1)S(1)}, bf16[32,2048]{1,0:T(8,128)(2,1)S(1)}, u32[]{:S(2)}, u32[]{:S(2)}) collective-permute-start(bf16[32,2048]{1,0:T(8,128)(2,1)S(1)} %add_convert_fusion.1), channel_id=1, source_target_pairs={{8,16},{24,28},{20,12},{4,0},{16,8},{28,24},{12,20},{0,4},{9,17},{... | collective-permute-start | bytes 393224 | tf_op jit(solution)/shard_map/ppermute | solution.py:244
  77.7 4.0 %collective-permute-start.23 = (bf16[32,512]{1,0:T(8,128)(2,1)S(1)}, bf16[32,512]{1,0:T(8,128)(2,1)S(1)}, u32[]{:S(2)}, u32[]{:S(2)}) collective-permute-start(bf16[32,512]{1,0:T(8,128)(2,1)S(1)} %get-tuple-element.77), channel_id=1, source_target_pairs={{0,2},{1,3},{2,0},{3,1},{4,6},{5,7},{6,4},{7,5},{8,10},{9,11},{10,... | collective-permute-start | bytes 98312 | tf_op jit(solution)/shard_map/ppermute | solution.py:358
  78.7 2.9 %collective-permute-start.24 = (bf16[32,512]{1,0:T(8,128)(2,1)S(1)}, bf16[32,512]{1,0:T(8,128)(2,1)S(1)}, u32[]{:S(2)}, u32[]{:S(2)}) collective-permute-start(bf16[32,512]{1,0:T(8,128)(2,1)S(1)} %get-tuple-element.84), channel_id=1, source_target_pairs={{0,1},{1,0},{2,3},{3,2},{4,5},{5,4},{6,7},{7,6},{8,9},{9,8},{10,11... | collective-permute-start | bytes 98312 | tf_op jit(solution)/shard_map/ppermute | solution.py:358
  78.8 3.3 %collective-permute-start.22 = (bf16[32,512]{1,0:T(8,128)(2,1)S(1)}, bf16[32,512]{1,0:T(8,128)(2,1)S(1)}, u32[]{:S(2)}, u32[]{:S(2)}) collective-permute-start(bf16[32,512]{1,0:T(8,128)(2,1)S(1)} %get-tuple-element.85), channel_id=1, source_target_pairs={{0,3},{1,2},{2,1},{3,0},{4,7},{5,6},{6,5},{7,4},{8,11},{9,10},{10,... | collective-permute-start | bytes 98312 | tf_op jit(solution)/shard_map/ppermute | solution.py:358

commit v9 on v8

--- a/solution.py
+++ b/solution.py
@@ -115,7 +115,7 @@
 
 
 def attend_kernel(
-    parts, scalars, within_ref, queries, residuals, gain_ref, mine_ref, other_ref, *refs
+    parts, scalars, sign_ref, within_ref, queries, residuals, gain_ref, mine_ref, other_ref, *refs
 ):
     piece_refs, hidden = refs[:-1], refs[-1]
     rows, full = hidden.shape
@@ -139,7 +139,7 @@
         piece[...] = hidden[pl.ds(pl.multiple_of((scalars[0] ^ j) * count, count), count), :]
 
 
-def norm_kernel(scalars, sign_ref, gain_ref, pack_ref, *refs):
+def norm_kernel(scalars, gain_ref, pack_ref, *refs):
     pieces, hidden_ref, out_ref = refs[:-2], refs[-2], refs[-1]
     width = pieces[0].shape[1]
     model = hidden_ref.shape[1]
@@ -188,18 +188,16 @@
     weight = jnp.sum(jnp.where(chosen, pack, 0.0), axis=-1, keepdims=True)
     chunk = min(units, 512)
 
-    @pl.loop(0, units // chunk)
-    def _(step):
-        cut = pl.ds(pl.multiple_of(step * chunk, chunk), chunk)
+    for step in range(units // chunk):
+        cut = slice(step * chunk, (step + 1) * chunk)
         gate = jnp.dot(rows_ref[...], gate_ref[:, cut], preferred_element_type=F32)
         up = jnp.dot(rows_ref[...], up_ref[:, cut], preferred_element_type=F32)
         act_ref[:, cut] = (gate / (1.0 + jnp.exp(-gate)) * up).astype(BF16)
 
     wide = min(model, 1024)
 
-    @pl.loop(0, model // wide)
-    def _(step):
-        cut = pl.ds(pl.multiple_of(step * wide, wide), wide)
+    for step in range(model // wide):
+        cut = slice(step * wide, (step + 1) * wide)
         produced = jnp.dot(act_ref[...], down_ref[:, cut], preferred_element_type=F32)
         made_ref[:, cut] = (produced.astype(BF16).astype(F32) * weight).astype(BF16)
 
@@ -228,61 +226,38 @@
     return list(range(0, count, 2)) + list(range(1, count, 2))[::-1]
 
 
-def far_sides(position, my_index, count):
-    place = jnp.where(position % 2 == 0, position // 2, count - 1 - position // 2)
-    onward = ((place // 2) % 2 == 0) != (my_index % 2 == 1)
-    return onward == (place % 2 == 1)
-
-
-def dense_experts(block, scalars, pick, weights_gate, weights_up, expert_out):
+def dense_experts(block, scalars, weights_gate, weights_up, expert_out):
     count, parts = lax.axis_size("seq"), lax.axis_size("exp")
     order = ring_order(count)
     far = count // 2
 
-    def trade(rows, pairs):
-        both = [(order[a], order[b]) for a, b in pairs]
-        return lax.ppermute(rows, "seq", both + [(b, a) for a, b in both])
-
-    def trade_first(rows):
-        return trade(rows, [(p, p + 1) for p in range(0, count, 2)])
-
-    def trade_second(rows):
-        return trade(rows, [(p, (p + 1) % count) for p in range(1, count, 2)])
-
-    def trade_far(rows):
+    def hop(rows, steps):
         pairs = []
         for e in range(parts):
             for p in range(count):
-                ahead = (p // 2) % 2 == e % 2
-                other = order[(p + (2 if ahead else -2)) % count]
-                pairs.append((order[p] * parts + e, other * parts + e))
+                target = order[(p + (steps if e % 2 == 0 else -steps)) % count]
+                pairs.append((order[p] * parts + e, target * parts + e))
         return lax.ppermute(rows, ("seq", "exp"), pairs)
 
     first, second = [block], [block]
     for distance in range(1, far):
-        came = trade_first(second[-1]), trade_second(first[-1])
+        first.append(hop(first[-1], 1))
+        second.append(hop(second[-1], -1))
         if distance == 1:
-            weights_out, _ = load_near(scalars, expert_out, 0, came[0])
-        first.append(came[0])
-        second.append(came[1])
-    farthest = trade_far(jnp.where(pick, first[-2], second[-2]))
+            weights_out, _ = load_near(scalars, expert_out, 0, first[-1])
+    farthest = hop(first[-2], 2)
     own, *made, farthest = run_expert(
         scalars, first + second[1:] + [farthest], weights_gate, weights_up, weights_out
     )
     made_first, made_second = made[:far - 1], made[far - 1:]
-    back_first, back_second = made_first[-1], made_second[-1]
-    early = trade_far(farthest)
-    for distance in range(far - 2, -1, -1):
-        to_second, to_first = trade_first(back_first), trade_second(back_second)
-        if distance == 0:
-            return own, to_second, to_first
-        terms_first = [made_first[distance - 1], to_first]
-        terms_second = [made_second[distance - 1], to_second]
-        if distance == far - 2:
-            nothing = jnp.zeros_like(early)
-            terms_first.append(jnp.where(pick, early, nothing))
-            terms_second.append(jnp.where(pick, nothing, early))
-        back_first, back_second = add_rows(*terms_first), add_rows(*terms_second)
+    back_first, back_second = hop(made_first[-1], -1), hop(made_second[-1], 1)
+    early = [hop(farthest, -2)]
+    for distance in range(far - 2, 0, -1):
+        back_first = add_rows(back_first, made_first[distance - 1], *early)
+        back_second = add_rows(back_second, made_second[distance - 1])
+        back_first, back_second = hop(back_first, -1), hop(back_second, 1)
+        early = []
+    return own, back_first, back_second
 
 
 def slot_ids(block_routes, expert_count, capacity):
@@ -393,9 +368,8 @@
     turns = [
         ((my_index >> b) & 1 != 0).reshape(1, 1) for b in range(parts.bit_length() - 1)
     ]
-    pick = far_sides(position, my_index, seq).reshape(1, 1)
     my_rows = (my_index * count).astype(jnp.uint32)
-    scalars, turns, pick, my_rows = lax.optimization_barrier((scalars, turns, pick, my_rows))
+    scalars, turns, my_rows = lax.optimization_barrier((scalars, turns, my_rows))
     state, heads = shape((HEAD, half), BF16), shape((rows, width), BF16)
     kept, given, keys, values, query, rest, my_gain, my_norm = call(
         open_kernel,
@@ -414,26 +388,26 @@
         flops=6 * rows * rows * width,
     )
     dense = routes.shape[1] == experts
-    total, sign = add_rows(kept, partner), jnp.zeros((8, HEAD), F32)
+    total, within = lax.optimization_barrier((add_rows(kept, partner), within))
+    sign = jnp.zeros((8, HEAD), F32)
     if dense:
-        weights_gate, sign = load_near(scalars, expert_in[0], 0, given)
-        total, sign = lax.optimization_barrier((total, sign))
+        weights_gate, sign = load_near(scalars, expert_in[0], 0, total)
     before = prior_states(total)
     mine, lacked = call(
         functools.partial(back_kernel, len(before)), [shape(state.shape, F32), state],
         [scalars, sign, kept, partner, *before],
     )
     other = lax.ppermute(lacked, "seq", swap)
+    if dense:
+        weights_up, sign = load_near(scalars, expert_in[0], 1, lacked)
     pieces = call(
         functools.partial(attend_kernel, parts),
         [shape((count, width), BF16)] * parts,
-        [scalars, within, query, rest, my_gain, mine, other],
+        [scalars, sign, within, query, rest, my_gain, mine, other],
         scratch=[pltpu.VMEM((rows, width), BF16)],
         flops=4 * rows * width * HEAD,
     )
     gathered = exchange(pieces)
-    if dense:
-        weights_up, sign = load_near(scalars, expert_in[0], 1, pieces[0])
 
     my_routes = lax.dynamic_slice_in_dim(routes, my_rows, count, 0)
     my_gates = lax.dynamic_slice_in_dim(route_gates, my_rows, count, 0)
@@ -453,11 +427,11 @@
     hidden, block = call(
         norm_kernel,
         [shape((count, model), BF16), shape((count, model + lanes), BF16)],
-        [scalars, sign, my_norm, pack] + gathered,
+        [scalars, my_norm, pack] + gathered,
     )
     if dense:
         terms = dense_experts(
-            block, scalars, pick, weights_gate, weights_up, expert_out
+            block, scalars, weights_gate, weights_up, expert_out
         )
     else:
         mixed = routed_experts(block[:, :model], my_routes, my_gates, expert_in, expert_out)

time: 83 us -> 80.4 us (0.969)
  waiting for transfers between devices: 32.4 us -> 30 us
  starting transfers between devices: 28.2 us -> 30 us
  local copies, waits for them, and re-layouts: 2.35 us -> 1.08 us
    ppermute x3, waiting for transfers between devices: 4.48 us -> 1.6 us  [prior_states(): lax.ppermute(total, 'seq', [(i, i ^ 2 * distance) for i in range(count)])]
    ppermute x1, waiting for transfers between devices: 2.87 us -> 0.01 us  [per_device(): other = lax.ppermute(lacked, 'seq', swap)]
    ppermute x6, waiting for transfers between devices: 2.36 us -> 5.11 us  [exchange(): lax.ppermute(pieces[j], 'exp', [(i, i ^ j) for i in range(parts)])]
    unnamed x8 -> x2, local copies, waits for them, and re-layouts: 1.97 us -> 0.01 us
    ppermute x1, starting transfers between devices: 0.51 us -> 1.55 us  [per_device(): other = lax.ppermute(lacked, 'seq', swap)]
  transfers between devices with their start and end apart: 25 -> 25, of which waited for: 17 -> 15; matrix products, arithmetic and copies ran while one was open for 1% -> 2% of each run, Pallas kernels for 12% -> 12%
where the time goes in v9:
time: 80.4 us; the launch traced here: 80.2 us
  starting transfers between devices  30 us (37%)
  waiting for transfers between devices  30 us (37%)
  Pallas kernels  17.9 us (22%)
  local copies, waits for them, and re-layouts  1.08 us (1%)
  other arithmetic  1.05 us (1%)
    ppermute x14, waiting for transfers between devices, hop(): return lax.ppermute(rows, ('seq', 'exp'), pairs)  22.8 us
    pallas_call x9, Pallas kernels, call(): pl.pallas_call(kernel, out_shape=outs, in_specs=[SCALAR if i == 0 or i in...  17.9 us
    ppermute x14, starting transfers between devices, hop(): return lax.ppermute(rows, ('seq', 'exp'), pairs)  16.5 us
    ppermute x6, waiting for transfers between devices, exchange(): lax.ppermute(pieces[j], 'exp', [(i, i ^ j) for i in range(parts)])  5.11 us
    ppermute x3, starting transfers between devices, prior_states(): lax.ppermute(total, 'seq', [(i, i ^ 2 * distance) for i in range(count)])  4.84 us
    ppermute x6, starting transfers between devices, exchange(): lax.ppermute(pieces[j], 'exp', [(i, i ^ j) for i in range(parts)])  4.14 us
    ppermute x1, starting transfers between devices, per_device(): partner = lax.ppermute(given, 'seq', swap)  3.01 us
  transfers between devices with their start and end apart: 25, of which 15 were waited for; matrix products, arithmetic and copies ran while one was open for 2% of the time, Pallas kernels for 12%

profile of v9, /device:TPU:0, one launch (start us, length us, event | category | flops | bytes accessed | tf_op | source)
XLA Modules:
  0.0 80.2 jit_solution(9165890127471117798)
XLA Ops:
  0.0 0.1 stack.24.scalars
  0.1 1.8 %shard_map.100 = (bf16[128,256]{1,0:T(8,128)(2,1)S(1)}, bf16[128,256]{1,0:T(8,128)(2,1)S(1)}, bf16[128,512]{1,0:T(8,128)(2,1)S(1)}, bf16[128,512]{1,0:T(8,128)(2...) custom-call(s32[7]{0:T(128)S(1)} %stack.24.scalars, ...), custom_call_target="tpu_custom_call" | custom-call | flops 16777216 | bytes 1200156 | tf_op jit(solution)/shard_map/pallas_call | solution.py:24
  1.9 3.0 %collective-permute-start = (bf16[128,256]{1,0:T(8,128)(2,1)S(1)}, bf16[128,256]{1,0:T(8,128)(2,1)S(1)}, u32[]{:S(2)}, u32[]{:S(2)}) collective-permute-start(bf16[128,256]{1,0:T(8,128)(2,1)S(1)} %get-tuple-element.46), channel_id=1, source_target_pairs={{0,4},{4,0},{8,12},{12,8},{16,20},{20,16},{24,28},{28,24},{1,5},{5... | collective-permute-start | bytes 196616 | tf_op jit(solution)/shard_map/ppermute | solution.py:385
  4.9 0.1 constant_dynamic-slice_fusion
  5.0 0.9 %shard_map.101.within_ref = f32[128,512]{1,0:T(8,128)S(1)} custom-call(s32[7]{0:T(128)S(1)} %stack.24.scalars, bf16[128,512]{1,0:T(8,128)(2,1)S(1)} %get-tuple-element.47.keys, bf16[128,512]{1,0:T(8,128)(2,1)S(1)} %get-tuple-element.48.values, bf16[128,512]{1,0:T(8,128)(2,1)S(1)} %get-tuple-element.49.queries), custom_call_target="tpu_custom_call" | custom-call | flops 50331648 | bytes 655388 | tf_op jit(solution)/shard_map/pallas_call | solution.py:24
  5.9 0.8 constant_dynamic-slice_fusion.1
  6.7 0.5 collective-permute-done.partner_ref
  7.2 4.2 %collective-permute-start.3 = (bf16[128,256]{1,0:T(8,128)(2,1)S(1)}, bf16[128,256]{1,0:T(8,128)(2,1)S(1)}, u32[]{:S(2)}, u32[]{:S(2)}) collective-permute-start(bf16[128,256]{1,0:T(8,128)(2,1)S(1)} %add_convert_fusion.5.after_ref), channel_id=1, source_target_pairs={{0,24},{4,28},{8,16},{12,20},{16,8},{20,12},{24,0},{28,4},{1,25},{... | collective-permute-start | bytes 196616 | tf_op jit(solution)/shard_map/ppermute | solution.py:323
  11.4 0.0 collective-permute-start.2
  11.4 0.6 collective-permute-start.1
  12.1 0.1 copy.16
  12.1 0.1 copy.15
  12.2 2.8 %shard_map.102 = (bf16[2048,1024]{1,0:T(8,128)(2,1)S(1)}, f32[8,128]{1,0:T(8,128)S(1)}) custom-call(s32[7]{0:T(128)S(1)} %stack.24.scalars, bf16[2,2048,1024]{2,1,0:T(8,128)(2,1)} %bitcast.12, bf16[128,256]{1,0:T(8,128)(2,1)S(1)} %add_convert_fusion.5.after_ref), custom_call_target="tpu_custom_call" | custom-call | bytes 12652572 | tf_op jit(solution)/shard_map/pallas_call | solution.py:24
  15.0 0.0 collective-permute-done.3.refs_2_
  15.0 1.6 %collective-permute-done.2.refs_1_ = bf16[128,256]{1,0:T(8,128)(2,1)S(1)} collective-permute-done((bf16[128,256]{1,0:T(8,128)(2,1)S(1)}, bf16[128,256]{1,0:T(8,128)(2,1)S(1)}, u32[]{:S(2)}, u32[]{:S(2)}) %collective-permute-start.2) | collective-permute-done | bytes 65568 | tf_op jit(solution)/shard_map/ppermute | solution.py:323
  16.6 0.6 shard_map.103
  17.2 1.6 %collective-permute-start.4 = (bf16[128,256]{1,0:T(8,128)(2,1)S(1)}, bf16[128,256]{1,0:T(8,128)(2,1)S(1)}, u32[]{:S(2)}, u32[]{:S(2)}) collective-permute-start(bf16[128,256]{1,0:T(8,128)(2,1)S(1)} %get-tuple-element.52.after_ref), channel_id=1, source_target_pairs={{0,4},{4,0},{8,12},{12,8},{16,20},{20,16},{24,28},{28,24},{1,5},{5... | collective-permute-start | bytes 196616 | tf_op jit(solution)/shard_map/ppermute | solution.py:400
  18.8 2.8 %shard_map.104 = (bf16[2048,1024]{1,0:T(8,128)(2,1)S(1)}, f32[8,128]{1,0:T(8,128)S(1)}) custom-call(s32[7]{0:T(128)S(1)} %stack.24.scalars, bf16[2,2048,1024]{2,1,0:T(8,128)(2,1)} %bitcast.13, bf16[128,256]{1,0:T(8,128)(2,1)S(1)} %get-tuple-element.52.after_ref), custom_call_target="tpu_custom_call" | custom-call | bytes 12652572 | tf_op jit(solution)/shard_map/pallas_call | solution.py:24
  21.5 0.0 collective-permute-done.4.other_ref
  21.5 0.9 %shard_map.105 = (bf16[32,512]{1,0:T(8,128)(2,1)S(1)}, bf16[32,512]{1,0:T(8,128)(2,1)S(1)}, bf16[32,512]{1,0:T(8,128)(2,1)S(1)}, bf16[32,512]{1,0:T(8,128)(2,1)S(1)}) custom-call(s32[7]{0:T(128)S(1)} %stack.24.scalars, f32[8,128]{1,0:T(8,128)S(1)} %get-tuple-element.53.sign_ref, f32[128,512]{1,0:T(8,128)S(1)} %shard_map.101.within_ref, ...), custom_call_target="tpu_custom_call" | custom-call | flops 33554432 | bytes 858140 | tf_op jit(solution)/shard_map/pallas_call | solution.py:24
  22.4 0.1 collective-permute-start.5
  22.5 1.6 %collective-permute-start.6 = (bf16[32,512]{1,0:T(8,128)(2,1)S(1)}, bf16[32,512]{1,0:T(8,128)(2,1)S(1)}, u32[]{:S(2)}, u32[]{:S(2)}) collective-permute-start(bf16[32,512]{1,0:T(8,128)(2,1)S(1)} %get-tuple-element.60), channel_id=1, source_target_pairs={{0,2},{1,3},{2,0},{3,1},{4,6},{5,7},{6,4},{7,5},{8,10},{9,11},{10,... | collective-permute-start | bytes 98312 | tf_op jit(solution)/shard_map/ppermute | solution.py:333
  24.1 0.3 collective-permute-start.7
  24.4 0.1 fusion.2.pack_ref
  24.4 0.0 collective-permute-done.5.refs_1_
  24.5 2.0 %collective-permute-done.6.refs_2_ = bf16[32,512]{1,0:T(8,128)(2,1)S(1)} collective-permute-done((bf16[32,512]{1,0:T(8,128)(2,1)S(1)}, bf16[32,512]{1,0:T(8,128)(2,1)S(1)}, u32[]{:S(2)}, u32[]{:S(2)}) %collective-permute-start.6) | collective-permute-done | bytes 32800 | tf_op jit(solution)/shard_map/ppermute | solution.py:333
  26.5 0.9 %collective-permute-done.7.refs_3_ = bf16[32,512]{1,0:T(8,128)(2,1)S(1)} collective-permute-done((bf16[32,512]{1,0:T(8,128)(2,1)S(1)}, bf16[32,512]{1,0:T(8,128)(2,1)S(1)}, u32[]{:S(2)}, u32[]{:S(2)}) %collective-permute-start.7) | collective-permute-done | bytes 32800 | tf_op jit(solution)/shard_map/ppermute | solution.py:333
  27.4 0.7 shard_map.106
  28.1 1.5 %collective-permute-start.11 = (bf16[32,2176]{1,0:T(8,128)(2,1)S(1)}, bf16[32,2176]{1,0:T(8,128)(2,1)S(1)}, u32[]{:S(2)}, u32[]{:S(2)}) collective-permute-start(bf16[32,2176]{1,0:T(8,128)(2,1)S(1)} %get-tuple-element.65.refs_0_), channel_id=1, source_target_pairs={{0,4},{8,0},{16,8},{24,16},{28,24},{20,28},{12,20},{4,12},{1,9},{9... | collective-permute-start | bytes 417800 | tf_op jit(solution)/shard_map/ppermute | solution.py:240
  29.6 0.5 collective-permute-start.8
  30.2 4.3 %collective-permute-done.11.refs_4_ = bf16[32,2176]{1,0:T(8,128)(2,1)S(1)} collective-permute-done((bf16[32,2176]{1,0:T(8,128)(2,1)S(1)}, bf16[32,2176]{1,0:T(8,128)(2,1)S(1)}, u32[]{:S(2)}, u32[]{:S(2)}) %collective-permute-start.11) | collective-permute-done | bytes 139296 | tf_op jit(solution)/shard_map/ppermute | solution.py:240
  34.5 1.2 %collective-permute-start.12 = (bf16[32,2176]{1,0:T(8,128)(2,1)S(1)}, bf16[32,2176]{1,0:T(8,128)(2,1)S(1)}, u32[]{:S(2)}, u32[]{:S(2)}) collective-permute-start(bf16[32,2176]{1,0:T(8,128)(2,1)S(1)} %collective-permute-done.11.refs_4_), channel_id=1, source_target_pairs={{0,4},{8,0},{16,8},{24,16},{28,24},{20,28},{12,20},{4,12},{1,9},{9... | collective-permute-start | bytes 417800 | tf_op jit(solution)/shard_map/ppermute | solution.py:240
  35.7 0.0 collective-permute-done.8.after_ref.refs_1_
  35.7 0.8 %collective-permute-start.9 = (bf16[32,2176]{1,0:T(8,128)(2,1)S(1)}, bf16[32,2176]{1,0:T(8,128)(2,1)S(1)}, u32[]{:S(2)}, u32[]{:S(2)}) collective-permute-start(bf16[32,2176]{1,0:T(8,128)(2,1)S(1)} %collective-permute-done.8.after_ref.refs_1_), channel_id=1, source_target_pairs={{0,8},{8,16},{16,24},{24,28},{28,20},{20,12},{12,4},{4,0},{1,5},{9... | collective-permute-start | bytes 417800 | tf_op jit(solution)/shard_map/ppermute | solution.py:240
  36.5 3.4 %collective-permute-done.12.refs_5_ = bf16[32,2176]{1,0:T(8,128)(2,1)S(1)} collective-permute-done((bf16[32,2176]{1,0:T(8,128)(2,1)S(1)}, bf16[32,2176]{1,0:T(8,128)(2,1)S(1)}, u32[]{:S(2)}, u32[]{:S(2)}) %collective-permute-start.12) | collective-permute-done | bytes 139296 | tf_op jit(solution)/shard_map/ppermute | solution.py:240
  39.9 1.0 %collective-permute-start.13 = (bf16[32,2176]{1,0:T(8,128)(2,1)S(1)}, bf16[32,2176]{1,0:T(8,128)(2,1)S(1)}, u32[]{:S(2)}, u32[]{:S(2)}) collective-permute-start(bf16[32,2176]{1,0:T(8,128)(2,1)S(1)} %collective-permute-done.12.refs_5_), channel_id=1, source_target_pairs={{0,4},{8,0},{16,8},{24,16},{28,24},{20,28},{12,20},{4,12},{1,9},{9... | collective-permute-start | bytes 417800 | tf_op jit(solution)/shard_map/ppermute | solution.py:240
  40.9 1.1 %collective-permute-done.9.refs_2_ = bf16[32,2176]{1,0:T(8,128)(2,1)S(1)} collective-permute-done((bf16[32,2176]{1,0:T(8,128)(2,1)S(1)}, bf16[32,2176]{1,0:T(8,128)(2,1)S(1)}, u32[]{:S(2)}, u32[]{:S(2)}) %collective-permute-start.9) | collective-permute-done | bytes 139296 | tf_op jit(solution)/shard_map/ppermute | solution.py:240
  42.0 0.5 collective-permute-start.14
  42.5 2.4 %collective-permute-start.10 = (bf16[32,2176]{1,0:T(8,128)(2,1)S(1)}, bf16[32,2176]{1,0:T(8,128)(2,1)S(1)}, u32[]{:S(2)}, u32[]{:S(2)}) collective-permute-start(bf16[32,2176]{1,0:T(8,128)(2,1)S(1)} %collective-permute-done.9.refs_2_), channel_id=1, source_target_pairs={{0,8},{8,16},{16,24},{24,28},{28,20},{20,12},{12,4},{4,0},{1,5},{9... | collective-permute-start | bytes 417800 | tf_op jit(solution)/shard_map/ppermute | solution.py:240
  44.9 3.3 %shard_map.107 = (bf16[1024,2048]{1,0:T(8,128)(2,1)S(1)}, f32[8,128]{1,0:T(8,128)}) custom-call(s32[7]{0:T(128)S(1)} %stack.24.scalars, bf16[1,1024,2048]{2,1,0:T(8,128)(2,1)} %source.1, bf16[32,2176]{1,0:T(8,128)(2,1)S(1)} %collective-permute-done.8.after_ref.refs_1_), custom_call_target="tpu_custom_call" | custom-call | bytes 8531996 | tf_op jit(solution)/shard_map/pallas_call | solution.py:24
  48.3 0.0 collective-permute-done.13.refs_6_
  48.3 0.9 %collective-permute-done.14.refs_7_ = bf16[32,2176]{1,0:T(8,128)(2,1)S(1)} collective-permute-done((bf16[32,2176]{1,0:T(8,128)(2,1)S(1)}, bf16[32,2176]{1,0:T(8,128)(2,1)S(1)}, u32[]{:S(2)}, u32[]{:S(2)}) %collective-permute-start.14) | collective-permute-done | bytes 139296 | tf_op jit(solution)/shard_map/ppermute | solution.py:240
  49.3 0.0 collective-permute-done.10.refs_3_
  49.3 4.1 %shard_map.108 = (bf16[32,2048]{1,0:T(8,128)(2,1)S(1)}, bf16[32,2048]{1,0:T(8,128)(2,1)S(1)}, bf16[32,2048]{1,0:T(8,128)(2,1)S(1)}, bf16[32,2048]{1,0:T(8,128)(2...) custom-call(s32[7]{0:T(128)S(1)} %stack.24.scalars, ...), custom_call_target="tpu_custom_call" | custom-call | flops 3221225472 | bytes 14745628 | tf_op jit(solution)/shard_map/pallas_call | solution.py:24
  53.4 2.1 %collective-permute-start.15 = (bf16[32,2048]{1,0:T(8,128)(2,1)S(1)}, bf16[32,2048]{1,0:T(8,128)(2,1)S(1)}, u32[]{:S(2)}, u32[]{:S(2)}) collective-permute-start(bf16[32,2048]{1,0:T(8,128)(2,1)S(1)} %get-tuple-element.68), channel_id=1, source_target_pairs={{0,4},{8,0},{16,8},{24,16},{28,24},{20,28},{12,20},{4,12},{1,9},{9... | collective-permute-start | bytes 393224 | tf_op jit(solution)/shard_map/ppermute | solution.py:240
  55.5 0.5 collective-permute-start.16
  56.0 1.5 %collective-permute-start.19 = (bf16[32,2048]{1,0:T(8,128)(2,1)S(1)}, bf16[32,2048]{1,0:T(8,128)(2,1)S(1)}, u32[]{:S(2)}, u32[]{:S(2)}) collective-permute-start(bf16[32,2048]{1,0:T(8,128)(2,1)S(1)} %get-tuple-element.72), channel_id=1, source_target_pairs={{0,8},{8,16},{16,24},{24,28},{28,20},{20,12},{12,4},{4,0},{1,5},{9... | collective-permute-start | bytes 393224 | tf_op jit(solution)/shard_map/ppermute | solution.py:240
  57.6 2.2 %collective-permute-done.15 = bf16[32,2048]{1,0:T(8,128)(2,1)S(1)} collective-permute-done((bf16[32,2048]{1,0:T(8,128)(2,1)S(1)}, bf16[32,2048]{1,0:T(8,128)(2,1)S(1)}, u32[]{:S(2)}, u32[]{:S(2)}) %collective-permute-start.15) | collective-permute-done | bytes 131104 | tf_op jit(solution)/shard_map/ppermute | solution.py:240
  59.8 3.1 %collective-permute-done.16 = bf16[32,2048]{1,0:T(8,128)(2,1)S(1)} collective-permute-done((bf16[32,2048]{1,0:T(8,128)(2,1)S(1)}, bf16[32,2048]{1,0:T(8,128)(2,1)S(1)}, u32[]{:S(2)}, u32[]{:S(2)}) %collective-permute-start.16) | collective-permute-done | bytes 131104 | tf_op jit(solution)/shard_map/ppermute | solution.py:240
  62.8 0.1 add_convert_fusion.4
  62.9 0.9 %collective-permute-start.17 = (bf16[32,2048]{1,0:T(8,128)(2,1)S(1)}, bf16[32,2048]{1,0:T(8,128)(2,1)S(1)}, u32[]{:S(2)}, u32[]{:S(2)}) collective-permute-start(bf16[32,2048]{1,0:T(8,128)(2,1)S(1)} %add_convert_fusion.4), channel_id=1, source_target_pairs={{0,4},{8,0},{16,8},{24,16},{28,24},{20,28},{12,20},{4,12},{1,9},{9... | collective-permute-start | bytes 393224 | tf_op jit(solution)/shard_map/ppermute | solution.py:240
  63.8 0.0 collective-permute-done.19
  63.8 1.3 %collective-permute-start.20 = (bf16[32,2048]{1,0:T(8,128)(2,1)S(1)}, bf16[32,2048]{1,0:T(8,128)(2,1)S(1)}, u32[]{:S(2)}, u32[]{:S(2)}) collective-permute-start(bf16[32,2048]{1,0:T(8,128)(2,1)S(1)} %add_convert_fusion.2), channel_id=1, source_target_pairs={{0,8},{8,16},{16,24},{24,28},{28,20},{20,12},{12,4},{4,0},{1,5},{9... | collective-permute-start | bytes 393224 | tf_op jit(solution)/shard_map/ppermute | solution.py:240
  65.1 4.0 %collective-permute-done.17 = bf16[32,2048]{1,0:T(8,128)(2,1)S(1)} collective-permute-done((bf16[32,2048]{1,0:T(8,128)(2,1)S(1)}, bf16[32,2048]{1,0:T(8,128)(2,1)S(1)}, u32[]{:S(2)}, u32[]{:S(2)}) %collective-permute-start.17) | collective-permute-done | bytes 131104 | tf_op jit(solution)/shard_map/ppermute | solution.py:240
  69.1 0.9 %collective-permute-start.18 = (bf16[32,2048]{1,0:T(8,128)(2,1)S(1)}, bf16[32,2048]{1,0:T(8,128)(2,1)S(1)}, u32[]{:S(2)}, u32[]{:S(2)}) collective-permute-start(bf16[32,2048]{1,0:T(8,128)(2,1)S(1)} %add_convert_fusion.3), channel_id=1, source_target_pairs={{0,4},{8,0},{16,8},{24,16},{28,24},{20,28},{12,20},{4,12},{1,9},{9... | collective-permute-start | bytes 393224 | tf_op jit(solution)/shard_map/ppermute | solution.py:240
  70.0 1.3 %collective-permute-start.21 = (bf16[32,2048]{1,0:T(8,128)(2,1)S(1)}, bf16[32,2048]{1,0:T(8,128)(2,1)S(1)}, u32[]{:S(2)}, u32[]{:S(2)}) collective-permute-start(bf16[32,2048]{1,0:T(8,128)(2,1)S(1)} %add_convert_fusion.1), channel_id=1, source_target_pairs={{0,8},{8,16},{16,24},{24,28},{28,20},{20,12},{12,4},{4,0},{1,5},{9... | collective-permute-start | bytes 393224 | tf_op jit(solution)/shard_map/ppermute | solution.py:240
  71.3 2.8 %collective-permute-done.18 = bf16[32,2048]{1,0:T(8,128)(2,1)S(1)} collective-permute-done((bf16[32,2048]{1,0:T(8,128)(2,1)S(1)}, bf16[32,2048]{1,0:T(8,128)(2,1)S(1)}, u32[]{:S(2)}, u32[]{:S(2)}) %collective-permute-start.18) | collective-permute-done | bytes 131104 | tf_op jit(solution)/shard_map/ppermute | solution.py:240
  74.2 0.9 %collective-permute-done.21 = bf16[32,2048]{1,0:T(8,128)(2,1)S(1)} collective-permute-done((bf16[32,2048]{1,0:T(8,128)(2,1)S(1)}, bf16[32,2048]{1,0:T(8,128)(2,1)S(1)}, u32[]{:S(2)}, u32[]{:S(2)}) %collective-permute-start.21) | collective-permute-done | bytes 131104 | tf_op jit(solution)/shard_map/ppermute | solution.py:240
  75.1 0.1 add_convert_fusion
  75.2 0.9 %collective-permute-start.23 = (bf16[32,512]{1,0:T(8,128)(2,1)S(1)}, bf16[32,512]{1,0:T(8,128)(2,1)S(1)}, u32[]{:S(2)}, u32[]{:S(2)}) collective-permute-start(bf16[32,512]{1,0:T(8,128)(2,1)S(1)} %get-tuple-element.75), channel_id=1, source_target_pairs={{0,2},{1,3},{2,0},{3,1},{4,6},{5,7},{6,4},{7,5},{8,10},{9,11},{10,... | collective-permute-start | bytes 98312 | tf_op jit(solution)/shard_map/ppermute | solution.py:333
  76.1 1.3 %collective-permute-start.22 = (bf16[32,512]{1,0:T(8,128)(2,1)S(1)}, bf16[32,512]{1,0:T(8,128)(2,1)S(1)}, u32[]{:S(2)}, u32[]{:S(2)}) collective-permute-start(bf16[32,512]{1,0:T(8,128)(2,1)S(1)} %get-tuple-element.83), channel_id=1, source_target_pairs={{0,3},{1,2},{2,1},{3,0},{4,7},{5,6},{6,5},{7,4},{8,11},{9,10},{10,... | collective-permute-start | bytes 98312 | tf_op jit(solution)/shard_map/ppermute | solution.py:333
  77.4 1.8 %collective-permute-done.23 = bf16[32,512]{1,0:T(8,128)(2,1)S(1)} collective-permute-done((bf16[32,512]{1,0:T(8,128)(2,1)S(1)}, bf16[32,512]{1,0:T(8,128)(2,1)S(1)}, u32[]{:S(2)}, u32[]{:S(2)}) %collective-permute-start.23) | collective-permute-done | bytes 32800 | tf_op jit(solution)/shard_map/ppermute | solution.py:333
  79.2 0.3 collective-permute-done.22
  79.5 0.7 pad_maximum_fusion
  (15 shorter events, 0.2 us)
Async XLA Ops:
  0.0 4.9 %copy-start = (f32[128,8]{0,1:T(8,128)S(1)}, f32[128,8]{0,1:T(8,128)}, u32[]{:S(2)}) copy-start(f32[128,8]{0,1:T(8,128)} %param.17) | copy-start | bytes 12292
  1.9 5.3 %collective-permute-start = (bf16[128,256]{1,0:T(8,128)(2,1)S(1)}, bf16[128,256]{1,0:T(8,128)(2,1)S(1)}, u32[]{:S(2)}, u32[]{:S(2)}) collective-permute-start(bf16[128,256]{1,0:T(8,128)(2,1)S(1)} %get-tuple-element.46), channel_id=1, source_target_pairs={{0,4},{4,0},{8,12},{12,8},{16,20},{20,16},{24,28},{28,24},{1,5},{5... | collective-permute-start | bytes 196616 | tf_op jit(solution)/shard_map/ppermute | solution.py:385
  7.2 7.8 %collective-permute-start.3 = (bf16[128,256]{1,0:T(8,128)(2,1)S(1)}, bf16[128,256]{1,0:T(8,128)(2,1)S(1)}, u32[]{:S(2)}, u32[]{:S(2)}) collective-permute-start(bf16[128,256]{1,0:T(8,128)(2,1)S(1)} %add_convert_fusion.5.after_ref), channel_id=1, source_target_pairs={{0,24},{4,28},{8,16},{12,20},{16,8},{20,12},{24,0},{28,4},{1,25},{... | collective-permute-start | bytes 196616 | tf_op jit(solution)/shard_map/ppermute | solution.py:323
  11.4 5.2 %collective-permute-start.2 = (bf16[128,256]{1,0:T(8,128)(2,1)S(1)}, bf16[128,256]{1,0:T(8,128)(2,1)S(1)}, u32[]{:S(2)}, u32[]{:S(2)}) collective-permute-start(bf16[128,256]{1,0:T(8,128)(2,1)S(1)} %add_convert_fusion.5.after_ref), channel_id=1, source_target_pairs={{0,16},{4,20},{8,24},{12,28},{16,0},{20,4},{24,8},{28,12},{1,17},{... | collective-permute-start | bytes 196616 | tf_op jit(solution)/shard_map/ppermute | solution.py:323
  11.4 5.2 %collective-permute-start.1 = (bf16[128,256]{1,0:T(8,128)(2,1)S(1)}, bf16[128,256]{1,0:T(8,128)(2,1)S(1)}, u32[]{:S(2)}, u32[]{:S(2)}) collective-permute-start(bf16[128,256]{1,0:T(8,128)(2,1)S(1)} %add_convert_fusion.5.after_ref), channel_id=1, source_target_pairs={{0,8},{4,12},{8,0},{12,4},{16,24},{20,28},{24,16},{28,20},{1,9},{5... | collective-permute-start | bytes 196616 | tf_op jit(solution)/shard_map/ppermute | solution.py:323
  17.2 4.3 %collective-permute-start.4 = (bf16[128,256]{1,0:T(8,128)(2,1)S(1)}, bf16[128,256]{1,0:T(8,128)(2,1)S(1)}, u32[]{:S(2)}, u32[]{:S(2)}) collective-permute-start(bf16[128,256]{1,0:T(8,128)(2,1)S(1)} %get-tuple-element.52.after_ref), channel_id=1, source_target_pairs={{0,4},{4,0},{8,12},{12,8},{16,20},{20,16},{24,28},{28,24},{1,5},{5... | collective-permute-start | bytes 196616 | tf_op jit(solution)/shard_map/ppermute | solution.py:400
  22.4 2.0 %collective-permute-start.5 = (bf16[32,512]{1,0:T(8,128)(2,1)S(1)}, bf16[32,512]{1,0:T(8,128)(2,1)S(1)}, u32[]{:S(2)}, u32[]{:S(2)}) collective-permute-start(bf16[32,512]{1,0:T(8,128)(2,1)S(1)} %get-tuple-element.59), channel_id=1, source_target_pairs={{0,1},{1,0},{2,3},{3,2},{4,5},{5,4},{6,7},{7,6},{8,9},{9,8},{10,11... | collective-permute-start | bytes 98312 | tf_op jit(solution)/shard_map/ppermute | solution.py:333
  22.5 4.0 %collective-permute-start.6 = (bf16[32,512]{1,0:T(8,128)(2,1)S(1)}, bf16[32,512]{1,0:T(8,128)(2,1)S(1)}, u32[]{:S(2)}, u32[]{:S(2)}) collective-permute-start(bf16[32,512]{1,0:T(8,128)(2,1)S(1)} %get-tuple-element.60), channel_id=1, source_target_pairs={{0,2},{1,3},{2,0},{3,1},{4,6},{5,7},{6,4},{7,5},{8,10},{9,11},{10,... | collective-permute-start | bytes 98312 | tf_op jit(solution)/shard_map/ppermute | solution.py:333
  24.1 3.3 %collective-permute-start.7 = (bf16[32,512]{1,0:T(8,128)(2,1)S(1)}, bf16[32,512]{1,0:T(8,128)(2,1)S(1)}, u32[]{:S(2)}, u32[]{:S(2)}) collective-permute-start(bf16[32,512]{1,0:T(8,128)(2,1)S(1)} %get-tuple-element.61), channel_id=1, source_target_pairs={{0,3},{1,2},{2,1},{3,0},{4,7},{5,6},{6,5},{7,4},{8,11},{9,10},{10,... | collective-permute-start | bytes 98312 | tf_op jit(solution)/shard_map/ppermute | solution.py:333
  28.1 6.3 %collective-permute-start.11 = (bf16[32,2176]{1,0:T(8,128)(2,1)S(1)}, bf16[32,2176]{1,0:T(8,128)(2,1)S(1)}, u32[]{:S(2)}, u32[]{:S(2)}) collective-permute-start(bf16[32,2176]{1,0:T(8,128)(2,1)S(1)} %get-tuple-element.65.refs_0_), channel_id=1, source_target_pairs={{0,4},{8,0},{16,8},{24,16},{28,24},{20,28},{12,20},{4,12},{1,9},{9... | collective-permute-start | bytes 417800 | tf_op jit(solution)/shard_map/ppermute | solution.py:240
  29.6 6.0 %collective-permute-start.8 = (bf16[32,2176]{1,0:T(8,128)(2,1)S(1)}, bf16[32,2176]{1,0:T(8,128)(2,1)S(1)}, u32[]{:S(2)}, u32[]{:S(2)}) collective-permute-start(bf16[32,2176]{1,0:T(8,128)(2,1)S(1)} %get-tuple-element.65.refs_0_), channel_id=1, source_target_pairs={{0,8},{8,16},{16,24},{24,28},{28,20},{20,12},{12,4},{4,0},{1,5},{9... | collective-permute-start | bytes 417800 | tf_op jit(solution)/shard_map/ppermute | solution.py:240
  34.5 5.4 %collective-permute-start.12 = (bf16[32,2176]{1,0:T(8,128)(2,1)S(1)}, bf16[32,2176]{1,0:T(8,128)(2,1)S(1)}, u32[]{:S(2)}, u32[]{:S(2)}) collective-permute-start(bf16[32,2176]{1,0:T(8,128)(2,1)S(1)} %collective-permute-done.11.refs_4_), channel_id=1, source_target_pairs={{0,4},{8,0},{16,8},{24,16},{28,24},{20,28},{12,20},{4,12},{1,9},{9... | collective-permute-start | bytes 417800 | tf_op jit(solution)/shard_map/ppermute | solution.py:240
  35.7 6.3 %collective-permute-start.9 = (bf16[32,2176]{1,0:T(8,128)(2,1)S(1)}, bf16[32,2176]{1,0:T(8,128)(2,1)S(1)}, u32[]{:S(2)}, u32[]{:S(2)}) collective-permute-start(bf16[32,2176]{1,0:T(8,128)(2,1)S(1)} %collective-permute-done.8.after_ref.refs_1_), channel_id=1, source_target_pairs={{0,8},{8,16},{16,24},{24,28},{28,20},{20,12},{12,4},{4,0},{1,5},{9... | collective-permute-start | bytes 417800 | tf_op jit(solution)/shard_map/ppermute | solution.py:240
  39.9 8.4 %collective-permute-start.13 = (bf16[32,2176]{1,0:T(8,128)(2,1)S(1)}, bf16[32,2176]{1,0:T(8,128)(2,1)S(1)}, u32[]{:S(2)}, u32[]{:S(2)}) collective-permute-start(bf16[32,2176]{1,0:T(8,128)(2,1)S(1)} %collective-permute-done.12.refs_5_), channel_id=1, source_target_pairs={{0,4},{8,0},{16,8},{24,16},{28,24},{20,28},{12,20},{4,12},{1,9},{9... | collective-permute-start | bytes 417800 | tf_op jit(solution)/shard_map/ppermute | solution.py:240
  42.0 7.2 %collective-permute-start.14 = (bf16[32,2176]{1,0:T(8,128)(2,1)S(1)}, bf16[32,2176]{1,0:T(8,128)(2,1)S(1)}, u32[]{:S(2)}, u32[]{:S(2)}) collective-permute-start(bf16[32,2176]{1,0:T(8,128)(2,1)S(1)} %collective-permute-done.9.refs_2_), channel_id=1, source_target_pairs={{0,16},{8,24},{16,28},{24,20},{28,12},{20,4},{12,0},{4,8},{1,13},{... | collective-permute-start | bytes 417800 | tf_op jit(solution)/shard_map/ppermute | solution.py:240
  42.5 6.7 %collective-permute-start.10 = (bf16[32,2176]{1,0:T(8,128)(2,1)S(1)}, bf16[32,2176]{1,0:T(8,128)(2,1)S(1)}, u32[]{:S(2)}, u32[]{:S(2)}) collective-permute-start(bf16[32,2176]{1,0:T(8,128)(2,1)S(1)} %collective-permute-done.9.refs_2_), channel_id=1, source_target_pairs={{0,8},{8,16},{16,24},{24,28},{28,20},{20,12},{12,4},{4,0},{1,5},{9... | collective-permute-start | bytes 417800 | tf_op jit(solution)/shard_map/ppermute | solution.py:240
  53.4 6.4 %collective-permute-start.15 = (bf16[32,2048]{1,0:T(8,128)(2,1)S(1)}, bf16[32,2048]{1,0:T(8,128)(2,1)S(1)}, u32[]{:S(2)}, u32[]{:S(2)}) collective-permute-start(bf16[32,2048]{1,0:T(8,128)(2,1)S(1)} %get-tuple-element.68), channel_id=1, source_target_pairs={{0,4},{8,0},{16,8},{24,16},{28,24},{20,28},{12,20},{4,12},{1,9},{9... | collective-permute-start | bytes 393224 | tf_op jit(solution)/shard_map/ppermute | solution.py:240
  55.5 7.3 %collective-permute-start.16 = (bf16[32,2048]{1,0:T(8,128)(2,1)S(1)}, bf16[32,2048]{1,0:T(8,128)(2,1)S(1)}, u32[]{:S(2)}, u32[]{:S(2)}) collective-permute-start(bf16[32,2048]{1,0:T(8,128)(2,1)S(1)} %get-tuple-element.70), channel_id=1, source_target_pairs={{0,12},{8,4},{16,0},{24,8},{28,16},{20,24},{12,28},{4,20},{1,17},{... | collective-permute-start | bytes 393224 | tf_op jit(solution)/shard_map/ppermute | solution.py:240
  56.0 7.8 %collective-permute-start.19 = (bf16[32,2048]{1,0:T(8,128)(2,1)S(1)}, bf16[32,2048]{1,0:T(8,128)(2,1)S(1)}, u32[]{:S(2)}, u32[]{:S(2)}) collective-permute-start(bf16[32,2048]{1,0:T(8,128)(2,1)S(1)} %get-tuple-element.72), channel_id=1, source_target_pairs={{0,8},{8,16},{16,24},{24,28},{28,20},{20,12},{12,4},{4,0},{1,5},{9... | collective-permute-start | bytes 393224 | tf_op jit(solution)/shard_map/ppermute | solution.py:240
  62.9 6.2 %collective-permute-start.17 = (bf16[32,2048]{1,0:T(8,128)(2,1)S(1)}, bf16[32,2048]{1,0:T(8,128)(2,1)S(1)}, u32[]{:S(2)}, u32[]{:S(2)}) collective-permute-start(bf16[32,2048]{1,0:T(8,128)(2,1)S(1)} %add_convert_fusion.4), channel_id=1, source_target_pairs={{0,4},{8,0},{16,8},{24,16},{28,24},{20,28},{12,20},{4,12},{1,9},{9... | collective-permute-start | bytes 393224 | tf_op jit(solution)/shard_map/ppermute | solution.py:240
  63.8 6.2 %collective-permute-start.20 = (bf16[32,2048]{1,0:T(8,128)(2,1)S(1)}, bf16[32,2048]{1,0:T(8,128)(2,1)S(1)}, u32[]{:S(2)}, u32[]{:S(2)}) collective-permute-start(bf16[32,2048]{1,0:T(8,128)(2,1)S(1)} %add_convert_fusion.2), channel_id=1, source_target_pairs={{0,8},{8,16},{16,24},{24,28},{28,20},{20,12},{12,4},{4,0},{1,5},{9... | collective-permute-start | bytes 393224 | tf_op jit(solution)/shard_map/ppermute | solution.py:240
  69.1 5.0 %collective-permute-start.18 = (bf16[32,2048]{1,0:T(8,128)(2,1)S(1)}, bf16[32,2048]{1,0:T(8,128)(2,1)S(1)}, u32[]{:S(2)}, u32[]{:S(2)}) collective-permute-start(bf16[32,2048]{1,0:T(8,128)(2,1)S(1)} %add_convert_fusion.3), channel_id=1, source_target_pairs={{0,4},{8,0},{16,8},{24,16},{28,24},{20,28},{12,20},{4,12},{1,9},{9... | collective-permute-start | bytes 393224 | tf_op jit(solution)/shard_map/ppermute | solution.py:240
  70.0 5.0 %collective-permute-start.21 = (bf16[32,2048]{1,0:T(8,128)(2,1)S(1)}, bf16[32,2048]{1,0:T(8,128)(2,1)S(1)}, u32[]{:S(2)}, u32[]{:S(2)}) collective-permute-start(bf16[32,2048]{1,0:T(8,128)(2,1)S(1)} %add_convert_fusion.1), channel_id=1, source_target_pairs={{0,8},{8,16},{16,24},{24,28},{28,20},{20,12},{12,4},{4,0},{1,5},{9... | collective-permute-start | bytes 393224 | tf_op jit(solution)/shard_map/ppermute | solution.py:240
  75.2 4.0 %collective-permute-start.23 = (bf16[32,512]{1,0:T(8,128)(2,1)S(1)}, bf16[32,512]{1,0:T(8,128)(2,1)S(1)}, u32[]{:S(2)}, u32[]{:S(2)}) collective-permute-start(bf16[32,512]{1,0:T(8,128)(2,1)S(1)} %get-tuple-element.75), channel_id=1, source_target_pairs={{0,2},{1,3},{2,0},{3,1},{4,6},{5,7},{6,4},{7,5},{8,10},{9,11},{10,... | collective-permute-start | bytes 98312 | tf_op jit(solution)/shard_map/ppermute | solution.py:333
  76.1 3.1 %collective-permute-start.24 = (bf16[32,512]{1,0:T(8,128)(2,1)S(1)}, bf16[32,512]{1,0:T(8,128)(2,1)S(1)}, u32[]{:S(2)}, u32[]{:S(2)}) collective-permute-start(bf16[32,512]{1,0:T(8,128)(2,1)S(1)} %get-tuple-element.82), channel_id=1, source_target_pairs={{0,1},{1,0},{2,3},{3,2},{4,5},{5,4},{6,7},{7,6},{8,9},{9,8},{10,11... | collective-permute-start | bytes 98312 | tf_op jit(solution)/shard_map/ppermute | solution.py:333
  76.1 3.4 %collective-permute-start.22 = (bf16[32,512]{1,0:T(8,128)(2,1)S(1)}, bf16[32,512]{1,0:T(8,128)(2,1)S(1)}, u32[]{:S(2)}, u32[]{:S(2)}) collective-permute-start(bf16[32,512]{1,0:T(8,128)(2,1)S(1)} %get-tuple-element.83), channel_id=1, source_target_pairs={{0,3},{1,2},{2,1},{3,0},{4,7},{5,6},{6,5},{7,4},{8,11},{9,10},{10,... | collective-permute-start | bytes 98312 | tf_op jit(solution)/shard_map/ppermute | solution.py:333

commit v10 on v9

--- a/solution.py
+++ b/solution.py
@@ -57,16 +57,19 @@
 
 
 def open_kernel(
-    scalars, key_ref, value_ref, query_ref, residual_ref, gain_ref, norm_ref,
-    kept_ref, given_ref, keys, values, query, residual, gain, norm, sems
+    scalars, key_ref, value_ref, query_ref, residual_ref, gain_ref,
+    kept_ref, given_ref, keys, values, query, residual, gain, flags_ref, sems
 ):
     pairs = [
         (key_ref, keys), (value_ref, values), (query_ref, query), (residual_ref, residual),
-        (gain_ref, gain), (norm_ref, norm),
+        (gain_ref, gain),
     ]
     copies = [pltpu.make_async_copy(a, b, sems.at[i]) for i, (a, b) in enumerate(pairs)]
     for copy in copies:
         copy.start()
+    for i in range(flags_ref.shape[0]):
+        value = 1 - scalars[1] if i == 1 else scalars[1 if i == 0 else 2 + i]
+        flags_ref[i:i + 1, :] = jnp.full((1, flags_ref.shape[1]), value, jnp.int32).astype(F32)
     for copy in copies[:2]:
         copy.wait()
     width = keys.shape[1] // 2
@@ -104,20 +107,10 @@
         ) + jnp.dot(low, values[:, cols], preferred_element_type=F32)
 
 
-def back_kernel(earlier, scalars, sign_ref, kept_ref, partner_ref, *refs):
-    came_refs, mine_ref, lacked_ref = refs[:earlier], refs[earlier], refs[earlier + 1]
-    before = jnp.zeros(mine_ref.shape, F32)
-    for i, ref in enumerate(came_refs):
-        before += jnp.where(scalars[4 + i] == 1, ref[...].astype(F32), 0.0)
-    first = scalars[1] == 0
-    mine_ref[...] = before + jnp.where(first, 0.0, partner_ref[...].astype(F32))
-    lacked_ref[...] = (before + jnp.where(first, kept_ref[...].astype(F32), 0.0)).astype(BF16)
-
-
 def attend_kernel(
-    parts, scalars, sign_ref, within_ref, queries, residuals, gain_ref, mine_ref, other_ref, *refs
+    parts, scalars, within_ref, queries, residuals, gain_ref, mine_ref, other_ref, *refs
 ):
-    piece_refs, hidden = refs[:-1], refs[-1]
+    piece_refs, hidden = refs[-1 - parts:-1], refs[-1]
     rows, full = hidden.shape
     width = full // 2
     first = scalars[1] == 0
@@ -137,22 +130,6 @@
     count = rows // parts
     for j, piece in enumerate(piece_refs):
         piece[...] = hidden[pl.ds(pl.multiple_of((scalars[0] ^ j) * count, count), count), :]
-
-
-def norm_kernel(scalars, gain_ref, pack_ref, *refs):
-    pieces, hidden_ref, out_ref = refs[:-2], refs[-2], refs[-1]
-    width = pieces[0].shape[1]
-    model = hidden_ref.shape[1]
-    total = 0.0
-    for ref in pieces:
-        value = ref[...].astype(F32)
-        total += jnp.sum(value * value, axis=-1, keepdims=True)
-    scale = lax.rsqrt(total / model + 1e-06)
-    for j, ref in enumerate(pieces):
-        cols = pl.ds(pl.multiple_of((scalars[0] ^ j) * width, width), width)
-        hidden_ref[:, cols] = ref[...]
-        out_ref[:, cols] = (ref[...].astype(F32) * scale * gain_ref[:, cols]).astype(BF16)
-    out_ref[:, model:] = pack_ref[...]
 
 
 def load_kernel(lead, scalars, source, after_ref, target, done_ref, sems):
@@ -226,38 +203,51 @@
     return list(range(0, count, 2)) + list(range(1, count, 2))[::-1]
 
 
-def dense_experts(block, scalars, weights_gate, weights_up, expert_out):
-    count, parts = lax.axis_size("seq"), lax.axis_size("exp")
+def dense_experts(block, scalars, turns, weights_gate, weights_up, expert_out):
+    count = lax.axis_size("seq")
     order = ring_order(count)
     far = count // 2
+    parts = lax.axis_size("exp")
 
     def hop(rows, steps):
+        return lax.ppermute(
+            rows, "seq", [(order[p], order[(p + steps) % count]) for p in range(count)]
+        )
+
+    def far_hop(rows):
         pairs = []
-        for e in range(parts):
-            for p in range(count):
-                target = order[(p + (steps if e % 2 == 0 else -steps)) % count]
+        for p in range(count):
+            for e in range(parts):
+                target = order[(p + (2 if e % 2 == 0 else -2)) % count]
                 pairs.append((order[p] * parts + e, target * parts + e))
         return lax.ppermute(rows, ("seq", "exp"), pairs)
 
-    first, second = [block], [block]
+    ahead, behind = [block], [block]
     for distance in range(1, far):
-        first.append(hop(first[-1], 1))
-        second.append(hop(second[-1], -1))
+        came, went = hop(ahead[-1], 1), hop(behind[-1], -1)
         if distance == 1:
-            weights_out, _ = load_near(scalars, expert_out, 0, first[-1])
-    farthest = hop(first[-2], 2)
-    own, *made, farthest = run_expert(
-        scalars, first + second[1:] + [farthest], weights_gate, weights_up, weights_out
-    )
-    made_first, made_second = made[:far - 1], made[far - 1:]
-    back_first, back_second = hop(made_first[-1], -1), hop(made_second[-1], 1)
-    early = [hop(farthest, -2)]
+            weights_out, _ = load_near(scalars, expert_out, 0, came)
+        ahead.append(came)
+        behind.append(went)
+    turned = turns[0]
+    farthest = far_hop(jnp.where(turned, behind[-2], ahead[-2]))
+    made = run_expert(
+        scalars, ahead + behind[1:] + [farthest], weights_gate, weights_up, weights_out
+    )
+    own, to_back, to_front, farthest = made[0], made[1:far], made[far:-1], made[-1]
+    going, coming = hop(to_front[-1], 1), hop(to_back[-1], -1)
+    early = far_hop(farthest)
     for distance in range(far - 2, 0, -1):
-        back_first = add_rows(back_first, made_first[distance - 1], *early)
-        back_second = add_rows(back_second, made_second[distance - 1])
-        back_first, back_second = hop(back_first, -1), hop(back_second, 1)
-        early = []
-    return own, back_first, back_second
+        front, back = to_front[distance - 1], to_back[distance - 1]
+        if distance == far - 2:
+            nothing = jnp.zeros_like(early)
+            going = add_rows(going, front, jnp.where(turned, nothing, early))
+            coming = add_rows(coming, back, jnp.where(turned, early, nothing))
+        else:
+            going = add_rows(going, front)
+            coming = add_rows(coming, back)
+        going, coming = hop(going, 1), hop(coming, -1)
+    return own, going, coming
 
 
 def slot_ids(block_routes, expert_count, capacity):
@@ -371,15 +361,13 @@
     my_rows = (my_index * count).astype(jnp.uint32)
     scalars, turns, my_rows = lax.optimization_barrier((scalars, turns, my_rows))
     state, heads = shape((HEAD, half), BF16), shape((rows, width), BF16)
-    kept, given, keys, values, query, rest, my_gain, my_norm = call(
+    kept, given, keys, values, query, rest, my_gain, flags = call(
         open_kernel,
-        [state] * 2 + [heads] * 4 + [shape((1, width), F32), shape((1, model), F32)],
-        [
-            scalars, key_vectors, value_vectors, queries, residual, head_gain[None, :],
-            norm_gain[None, :],
-        ],
-        far=(1, 2, 3, 4, 5, 6),
-        scratch=[pltpu.SemaphoreType.DMA((6,))],
+        [state] * 2 + [heads] * 4
+        + [shape((1, width), F32), shape((2 + len(steps), half), F32)],
+        [scalars, key_vectors, value_vectors, queries, residual, head_gain[None, :]],
+        far=(1, 2, 3, 4, 5),
+        scratch=[pltpu.SemaphoreType.DMA((5,))],
         flops=2 * rows * width * HEAD,
     )
     partner = lax.ppermute(given, "seq", swap)
@@ -392,18 +380,21 @@
     sign = jnp.zeros((8, HEAD), F32)
     if dense:
         weights_gate, sign = load_near(scalars, expert_in[0], 0, total)
-    before = prior_states(total)
-    mine, lacked = call(
-        functools.partial(back_kernel, len(before)), [shape(state.shape, F32), state],
-        [scalars, sign, kept, partner, *before],
-    )
+    before = sum(
+        came.astype(F32) * flags[2 + i:3 + i] for i, came in enumerate(prior_states(total))
+    )
+    mine = before + partner.astype(F32) * flags[:1]
+    lacked = (before + kept.astype(F32) * flags[1:2]).astype(BF16)
+    lacked, sign = lax.optimization_barrier((lacked, sign))
     other = lax.ppermute(lacked, "seq", swap)
+    signs = [sign]
     if dense:
         weights_up, sign = load_near(scalars, expert_in[0], 1, lacked)
+        signs.append(sign)
     pieces = call(
         functools.partial(attend_kernel, parts),
         [shape((count, width), BF16)] * parts,
-        [scalars, sign, within, query, rest, my_gain, mine, other],
+        [scalars, within, query, rest, my_gain, mine, other, *signs],
         scratch=[pltpu.VMEM((rows, width), BF16)],
         flops=4 * rows * width * HEAD,
     )
@@ -424,17 +415,20 @@
     pack = jnp.pad(
         jnp.concatenate([high, mixing - high], axis=1), ((0, 0), (0, lanes - 2 * experts))
     ).astype(BF16)
-    hidden, block = call(
-        norm_kernel,
-        [shape((count, model), BF16), shape((count, model + lanes), BF16)],
-        [scalars, my_norm, pack] + gathered,
-    )
+    hidden = jnp.concatenate(turn_order(gathered, turns), axis=1)
+    widened = hidden.astype(F32)
+    normed = (
+        widened
+        * lax.rsqrt(jnp.mean(widened * widened, axis=-1, keepdims=True) + 1e-06)
+        * norm_gain
+    ).astype(BF16)
     if dense:
+        block = jnp.concatenate([normed, pack], axis=1)
         terms = dense_experts(
-            block, scalars, weights_gate, weights_up, expert_out
+            block, scalars, turns, weights_gate, weights_up, expert_out
         )
     else:
-        mixed = routed_experts(block[:, :model], my_routes, my_gates, expert_in, expert_out)
+        mixed = routed_experts(normed, my_routes, my_gates, expert_in, expert_out)
         terms = [mixed]
     own, *others = terms
     mixed = own.astype(F32) + sum(t.astype(F32) for t in others)

time: 80.4 us -> 78.2 us (0.973)
  waiting for transfers between devices: 30 us -> 28.2 us
  Pallas kernels: 17.9 us -> 16.6 us
    ppermute x14, waiting for transfers between devices: 22.8 us -> 21.5 us  [the longest x12 14.8 us: hop(): lax.ppermute(rows, 'seq', [(order[p], order[(p + steps) % count]) for p i...]
    pallas_call x9 -> x7, Pallas kernels: 17.9 us -> 16.6 us  [call(): pl.pallas_call(kernel, out_shape=outs, in_specs=[SCALAR if i == 0 or i in...]
  transfers between devices with their start and end apart: 25 -> 25, of which waited for: 15 -> 15; matrix products, arithmetic and copies ran while one was open for 2% -> 2% of each run, Pallas kernels for 12% -> 13%
where the time goes in v10:
time: 78.2 us; the launch traced here: 78 us
  starting transfers between devices  30.4 us (39%)
  waiting for transfers between devices  28.2 us (36%)
  Pallas kernels  16.6 us (21%)
  other arithmetic  1.43 us (2%)
  local copies, waits for them, and re-layouts  1.09 us (1%)
    pallas_call x7, Pallas kernels, call(): pl.pallas_call(kernel, out_shape=outs, in_specs=[SCALAR if i == 0 or i in...  16.6 us
    ppermute x12, waiting for transfers between devices, hop(): lax.ppermute(rows, 'seq', [(order[p], order[(p + steps) % count]) for p i...  14.8 us
    ppermute x12, starting transfers between devices, hop(): lax.ppermute(rows, 'seq', [(order[p], order[(p + steps) % count]) for p i...  13.7 us
    ppermute x2, waiting for transfers between devices, far_hop(): return lax.ppermute(rows, ('seq', 'exp'), pairs)  6.66 us
    ppermute x3, starting transfers between devices, prior_states(): lax.ppermute(total, 'seq', [(i, i ^ 2 * distance) for i in range(count)])  4.84 us
    ppermute x6, waiting for transfers between devices, exchange(): lax.ppermute(pieces[j], 'exp', [(i, i ^ j) for i in range(parts)])  4.68 us
    ppermute x6, starting transfers between devices, exchange(): lax.ppermute(pieces[j], 'exp', [(i, i ^ j) for i in range(parts)])  4.13 us
    ppermute x2, starting transfers between devices, far_hop(): return lax.ppermute(rows, ('seq', 'exp'), pairs)  3.23 us
  transfers between devices with their start and end apart: 25, of which 15 were waited for; matrix products, arithmetic and copies ran while one was open for 2% of the time, Pallas kernels for 13%

profile of v10, /device:TPU:0, one launch (start us, length us, event | category | flops | bytes accessed | tf_op | source)
XLA Modules:
  0.0 78.0 jit_solution(6316977971141612478)
XLA Ops:
  0.0 0.1 stack.24.scalars
  0.1 1.8 %shard_map.100 = (bf16[128,256]{1,0:T(8,128)(2,1)S(1)}, bf16[128,256]{1,0:T(8,128)(2,1)S(1)}, bf16[128,512]{1,0:T(8,128)(2,1)S(1)}, bf16[128,512]{1,0:T(8,128)(2...) custom-call(s32[7]{0:T(128)S(1)} %stack.24.scalars, ...), custom_call_target="tpu_custom_call" | custom-call | flops 16777216 | bytes 1188892 | tf_op jit(solution)/shard_map/pallas_call | solution.py:24
  1.9 3.0 %collective-permute-start = (bf16[128,256]{1,0:T(8,128)(2,1)S(1)}, bf16[128,256]{1,0:T(8,128)(2,1)S(1)}, u32[]{:S(2)}, u32[]{:S(2)}) collective-permute-start(bf16[128,256]{1,0:T(8,128)(2,1)S(1)} %get-tuple-element.42), channel_id=1, source_target_pairs={{0,4},{4,0},{8,12},{12,8},{16,20},{20,16},{24,28},{28,24},{1,5},{5... | collective-permute-start | bytes 196616 | tf_op jit(solution)/shard_map/ppermute | solution.py:373
  4.9 0.1 constant_dynamic-slice_fusion
  5.0 0.9 %shard_map.101.within_ref = f32[128,512]{1,0:T(8,128)S(1)} custom-call(s32[7]{0:T(128)S(1)} %stack.24.scalars, bf16[128,512]{1,0:T(8,128)(2,1)S(1)} %get-tuple-element.43.keys, bf16[128,512]{1,0:T(8,128)(2,1)S(1)} %get-tuple-element.44.values, bf16[128,512]{1,0:T(8,128)(2,1)S(1)} %get-tuple-element.45.queries), custom_call_target="tpu_custom_call" | custom-call | flops 50331648 | bytes 655388 | tf_op jit(solution)/shard_map/pallas_call | solution.py:24
  5.9 0.8 constant_dynamic-slice_fusion.1
  6.7 0.5 collective-permute-done
  7.2 4.2 %collective-permute-start.3 = (bf16[128,256]{1,0:T(8,128)(2,1)S(1)}, bf16[128,256]{1,0:T(8,128)(2,1)S(1)}, u32[]{:S(2)}, u32[]{:S(2)}) collective-permute-start(bf16[128,256]{1,0:T(8,128)(2,1)S(1)} %fusion.6.after_ref), channel_id=1, source_target_pairs={{0,24},{4,28},{8,16},{12,20},{16,8},{20,12},{24,0},{28,4},{1,25},{... | collective-permute-start | bytes 196616 | tf_op jit(solution)/shard_map/ppermute | solution.py:313
  11.4 0.0 collective-permute-start.2
  11.4 0.6 collective-permute-start.1
  12.0 0.1 copy.16
  12.1 0.1 copy.15
  12.2 2.8 %shard_map.102 = (bf16[2048,1024]{1,0:T(8,128)(2,1)S(1)}, f32[8,128]{1,0:T(8,128)S(1)}) custom-call(s32[7]{0:T(128)S(1)} %stack.24.scalars, bf16[2,2048,1024]{2,1,0:T(8,128)(2,1)} %bitcast.16, bf16[128,256]{1,0:T(8,128)(2,1)S(1)} %fusion.6.after_ref), custom_call_target="tpu_custom_call" | custom-call | bytes 12652572 | tf_op jit(solution)/shard_map/pallas_call | solution.py:24
  15.0 1.6 %collective-permute-done.2 = bf16[128,256]{1,0:T(8,128)(2,1)S(1)} collective-permute-done((bf16[128,256]{1,0:T(8,128)(2,1)S(1)}, bf16[128,256]{1,0:T(8,128)(2,1)S(1)}, u32[]{:S(2)}, u32[]{:S(2)}) %collective-permute-start.2) | collective-permute-done | bytes 65568 | tf_op jit(solution)/shard_map/ppermute | solution.py:313
  16.6 0.0 collective-permute-done.1
  16.6 0.1 fusion.7
  16.6 1.6 %collective-permute-start.4 = (bf16[128,256]{1,0:T(8,128)(2,1)S(1)}, bf16[128,256]{1,0:T(8,128)(2,1)S(1)}, u32[]{:S(2)}, u32[]{:S(2)}) collective-permute-start(bf16[128,256]{1,0:T(8,128)(2,1)S(1)} %get-tuple-element.52.after_ref), channel_id=1, source_target_pairs={{0,4},{4,0},{8,12},{12,8},{16,20},{20,16},{24,28},{28,24},{1,5},{5... | collective-permute-start | bytes 196616 | tf_op jit(solution)/shard_map/ppermute | solution.py:389
  18.2 2.8 %shard_map.103 = (bf16[2048,1024]{1,0:T(8,128)(2,1)S(1)}, f32[8,128]{1,0:T(8,128)S(1)}) custom-call(s32[7]{0:T(128)S(1)} %stack.24.scalars, bf16[2,2048,1024]{2,1,0:T(8,128)(2,1)} %bitcast.17, bf16[128,256]{1,0:T(8,128)(2,1)S(1)} %get-tuple-element.52.after_ref), custom_call_target="tpu_custom_call" | custom-call | bytes 12652572 | tf_op jit(solution)/shard_map/pallas_call | solution.py:24
  21.0 0.0 collective-permute-done.4.other_ref
  21.0 0.9 %shard_map.104 = (bf16[32,512]{1,0:T(8,128)(2,1)S(1)}, bf16[32,512]{1,0:T(8,128)(2,1)S(1)}, bf16[32,512]{1,0:T(8,128)(2,1)S(1)}, bf16[32,512]{1,0:T(8,128)(2,1)S(1)}) custom-call(s32[7]{0:T(128)S(1)} %stack.24.scalars, f32[128,512]{1,0:T(8,128)S(1)} %shard_map.101.within_ref, bf16[128,512]{1,0:T(8,128)(2,1)S(1)} %get-tuple-element.45.queries, ...), custom_call_target="tpu_custom_call" | custom-call | flops 33554432 | bytes 862236 | tf_op jit(solution)/shard_map/pallas_call | solution.py:24
  21.9 0.1 collective-permute-start.5
  22.0 1.6 %collective-permute-start.6 = (bf16[32,512]{1,0:T(8,128)(2,1)S(1)}, bf16[32,512]{1,0:T(8,128)(2,1)S(1)}, u32[]{:S(2)}, u32[]{:S(2)}) collective-permute-start(bf16[32,512]{1,0:T(8,128)(2,1)S(1)} %get-tuple-element.56), channel_id=1, source_target_pairs={{0,2},{1,3},{2,0},{3,1},{4,6},{5,7},{6,4},{7,5},{8,10},{9,11},{10,... | collective-permute-start | bytes 98312 | tf_op jit(solution)/shard_map/ppermute | solution.py:323
  23.5 0.3 collective-permute-start.7
  23.8 0.1 fusion.10
  23.9 1.7 %collective-permute-done.5 = bf16[32,512]{1,0:T(8,128)(2,1)S(1)} collective-permute-done((bf16[32,512]{1,0:T(8,128)(2,1)S(1)}, bf16[32,512]{1,0:T(8,128)(2,1)S(1)}, u32[]{:S(2)}, u32[]{:S(2)}) %collective-permute-start.5) | collective-permute-done | bytes 32800 | tf_op jit(solution)/shard_map/ppermute | solution.py:323
  25.6 0.4 collective-permute-done.6
  26.0 0.1 fusion
  26.2 0.1 fusion.2
  26.3 1.5 %collective-permute-start.11 = (bf16[32,2176]{1,0:T(8,128)(2,1)S(1)}, bf16[32,2176]{1,0:T(8,128)(2,1)S(1)}, u32[]{:S(2)}, u32[]{:S(2)}) collective-permute-start(bf16[32,2176]{1,0:T(8,128)(2,1)S(1)} %pad_maximum_fusion.refs_0_), channel_id=1, source_target_pairs={{0,4},{8,0},{16,8},{24,16},{28,24},{20,28},{12,20},{4,12},{1,5},{9... | collective-permute-start | bytes 417800 | tf_op jit(solution)/shard_map/ppermute | solution.py:213
  27.8 0.6 collective-permute-start.8
  28.4 3.9 %collective-permute-done.11.refs_4_ = bf16[32,2176]{1,0:T(8,128)(2,1)S(1)} collective-permute-done((bf16[32,2176]{1,0:T(8,128)(2,1)S(1)}, bf16[32,2176]{1,0:T(8,128)(2,1)S(1)}, u32[]{:S(2)}, u32[]{:S(2)}) %collective-permute-start.11) | collective-permute-done | bytes 139296 | tf_op jit(solution)/shard_map/ppermute | solution.py:213
  32.3 1.5 %collective-permute-start.12 = (bf16[32,2176]{1,0:T(8,128)(2,1)S(1)}, bf16[32,2176]{1,0:T(8,128)(2,1)S(1)}, u32[]{:S(2)}, u32[]{:S(2)}) collective-permute-start(bf16[32,2176]{1,0:T(8,128)(2,1)S(1)} %collective-permute-done.11.refs_4_), channel_id=1, source_target_pairs={{0,4},{8,0},{16,8},{24,16},{28,24},{20,28},{12,20},{4,12},{1,5},{9... | collective-permute-start | bytes 417800 | tf_op jit(solution)/shard_map/ppermute | solution.py:213
  33.8 0.0 collective-permute-done.8.after_ref.refs_1_
  33.8 0.6 collective-permute-start.9
  34.3 3.1 %collective-permute-done.12.refs_5_ = bf16[32,2176]{1,0:T(8,128)(2,1)S(1)} collective-permute-done((bf16[32,2176]{1,0:T(8,128)(2,1)S(1)}, bf16[32,2176]{1,0:T(8,128)(2,1)S(1)}, u32[]{:S(2)}, u32[]{:S(2)}) %collective-permute-start.12) | collective-permute-done | bytes 139296 | tf_op jit(solution)/shard_map/ppermute | solution.py:213
  37.4 1.5 %collective-permute-start.13 = (bf16[32,2176]{1,0:T(8,128)(2,1)S(1)}, bf16[32,2176]{1,0:T(8,128)(2,1)S(1)}, u32[]{:S(2)}, u32[]{:S(2)}) collective-permute-start(bf16[32,2176]{1,0:T(8,128)(2,1)S(1)} %collective-permute-done.12.refs_5_), channel_id=1, source_target_pairs={{0,4},{8,0},{16,8},{24,16},{28,24},{20,28},{12,20},{4,12},{1,5},{9... | collective-permute-start | bytes 417800 | tf_op jit(solution)/shard_map/ppermute | solution.py:213
  38.9 1.1 %collective-permute-start.14 = (bf16[32,2176]{1,0:T(8,128)(2,1)S(1)}, bf16[32,2176]{1,0:T(8,128)(2,1)S(1)}, u32[]{:S(2)}, u32[]{:S(2)}) collective-permute-start(bf16[32,2176]{1,0:T(8,128)(2,1)S(1)} %broadcast_select_fusion), channel_id=1, source_target_pairs={{0,16},{1,13},{2,18},{3,15},{8,24},{9,5},{10,26},{11,7},{16,28},{1... | collective-permute-start | bytes 417800 | tf_op jit(solution)/shard_map/ppermute | solution.py:223
  40.0 1.5 %collective-permute-start.10 = (bf16[32,2176]{1,0:T(8,128)(2,1)S(1)}, bf16[32,2176]{1,0:T(8,128)(2,1)S(1)}, u32[]{:S(2)}, u32[]{:S(2)}) collective-permute-start(bf16[32,2176]{1,0:T(8,128)(2,1)S(1)} %collective-permute-done.9.refs_2_), channel_id=1, source_target_pairs={{0,8},{8,16},{16,24},{24,28},{28,20},{20,12},{12,4},{4,0},{1,9},{9... | collective-permute-start | bytes 417800 | tf_op jit(solution)/shard_map/ppermute | solution.py:213
  41.5 3.3 %shard_map.105 = (bf16[1024,2048]{1,0:T(8,128)(2,1)S(1)}, f32[8,128]{1,0:T(8,128)}) custom-call(s32[7]{0:T(128)S(1)} %stack.24.scalars, bf16[1,1024,2048]{2,1,0:T(8,128)(2,1)} %source.1, bf16[32,2176]{1,0:T(8,128)(2,1)S(1)} %collective-permute-done.8.after_ref.refs_1_), custom_call_target="tpu_custom_call" | custom-call | bytes 8531996 | tf_op jit(solution)/shard_map/pallas_call | solution.py:24
  44.9 0.0 collective-permute-done.13.refs_6_
  44.9 1.6 %collective-permute-done.14.refs_7_ = bf16[32,2176]{1,0:T(8,128)(2,1)S(1)} collective-permute-done((bf16[32,2176]{1,0:T(8,128)(2,1)S(1)}, bf16[32,2176]{1,0:T(8,128)(2,1)S(1)}, u32[]{:S(2)}, u32[]{:S(2)}) %collective-permute-start.14) | collective-permute-done | bytes 139296 | tf_op jit(solution)/shard_map/ppermute | solution.py:223
  46.5 0.1 collective-permute-done.10.refs_3_
  46.5 4.1 %shard_map.106 = (bf16[32,2048]{1,0:T(8,128)(2,1)S(1)}, bf16[32,2048]{1,0:T(8,128)(2,1)S(1)}, bf16[32,2048]{1,0:T(8,128)(2,1)S(1)}, bf16[32,2048]{1,0:T(8,128)(2...) custom-call(s32[7]{0:T(128)S(1)} %stack.24.scalars, ...), custom_call_target="tpu_custom_call" | custom-call | flops 3221225472 | bytes 14745628 | tf_op jit(solution)/shard_map/pallas_call | solution.py:24
  50.7 1.1 %collective-permute-start.15 = (bf16[32,2048]{1,0:T(8,128)(2,1)S(1)}, bf16[32,2048]{1,0:T(8,128)(2,1)S(1)}, u32[]{:S(2)}, u32[]{:S(2)}) collective-permute-start(bf16[32,2048]{1,0:T(8,128)(2,1)S(1)} %get-tuple-element.64), channel_id=1, source_target_pairs={{0,8},{8,16},{16,24},{24,28},{28,20},{20,12},{12,4},{4,0},{1,9},{9... | collective-permute-start | bytes 393224 | tf_op jit(solution)/shard_map/ppermute | solution.py:213
  51.8 2.1 %collective-permute-start.16 = (bf16[32,2048]{1,0:T(8,128)(2,1)S(1)}, bf16[32,2048]{1,0:T(8,128)(2,1)S(1)}, u32[]{:S(2)}, u32[]{:S(2)}) collective-permute-start(bf16[32,2048]{1,0:T(8,128)(2,1)S(1)} %get-tuple-element.66), channel_id=1, source_target_pairs={{0,16},{1,13},{2,18},{3,15},{8,24},{9,5},{10,26},{11,7},{16,28},{1... | collective-permute-start | bytes 393224 | tf_op jit(solution)/shard_map/ppermute | solution.py:223
  53.9 1.3 %collective-permute-start.19 = (bf16[32,2048]{1,0:T(8,128)(2,1)S(1)}, bf16[32,2048]{1,0:T(8,128)(2,1)S(1)}, u32[]{:S(2)}, u32[]{:S(2)}) collective-permute-start(bf16[32,2048]{1,0:T(8,128)(2,1)S(1)} %get-tuple-element.68), channel_id=1, source_target_pairs={{0,4},{8,0},{16,8},{24,16},{28,24},{20,28},{12,20},{4,12},{1,5},{9... | collective-permute-start | bytes 393224 | tf_op jit(solution)/shard_map/ppermute | solution.py:213
  55.2 0.5 collective-permute-done.15
  55.7 5.0 %collective-permute-done.16 = bf16[32,2048]{1,0:T(8,128)(2,1)S(1)} collective-permute-done((bf16[32,2048]{1,0:T(8,128)(2,1)S(1)}, bf16[32,2048]{1,0:T(8,128)(2,1)S(1)}, u32[]{:S(2)}, u32[]{:S(2)}) %collective-permute-start.16) | collective-permute-done | bytes 131104 | tf_op jit(solution)/shard_map/ppermute | solution.py:223
  60.7 0.0 collective-permute-done.19
  60.7 0.1 add_convert_fusion.3
  60.9 0.1 collective-permute-start.17
  60.9 2.0 %collective-permute-start.20 = (bf16[32,2048]{1,0:T(8,128)(2,1)S(1)}, bf16[32,2048]{1,0:T(8,128)(2,1)S(1)}, u32[]{:S(2)}, u32[]{:S(2)}) collective-permute-start(bf16[32,2048]{1,0:T(8,128)(2,1)S(1)} %get-tuple-element.86), channel_id=1, source_target_pairs={{0,4},{8,0},{16,8},{24,16},{28,24},{20,28},{12,20},{4,12},{1,5},{9... | collective-permute-start | bytes 393224 | tf_op jit(solution)/shard_map/ppermute | solution.py:213
  62.9 4.1 %collective-permute-done.17 = bf16[32,2048]{1,0:T(8,128)(2,1)S(1)} collective-permute-done((bf16[32,2048]{1,0:T(8,128)(2,1)S(1)}, bf16[32,2048]{1,0:T(8,128)(2,1)S(1)}, u32[]{:S(2)}, u32[]{:S(2)}) %collective-permute-start.17) | collective-permute-done | bytes 131104 | tf_op jit(solution)/shard_map/ppermute | solution.py:213
  67.1 0.2 collective-permute-start.18
  67.4 1.9 %collective-permute-start.21 = (bf16[32,2048]{1,0:T(8,128)(2,1)S(1)}, bf16[32,2048]{1,0:T(8,128)(2,1)S(1)}, u32[]{:S(2)}, u32[]{:S(2)}) collective-permute-start(bf16[32,2048]{1,0:T(8,128)(2,1)S(1)} %add_convert_fusion), channel_id=1, source_target_pairs={{0,4},{8,0},{16,8},{24,16},{28,24},{20,28},{12,20},{4,12},{1,5},{9... | collective-permute-start | bytes 393224 | tf_op jit(solution)/shard_map/ppermute | solution.py:213
  69.3 2.8 %collective-permute-done.18 = bf16[32,2048]{1,0:T(8,128)(2,1)S(1)} collective-permute-done((bf16[32,2048]{1,0:T(8,128)(2,1)S(1)}, bf16[32,2048]{1,0:T(8,128)(2,1)S(1)}, u32[]{:S(2)}, u32[]{:S(2)}) %collective-permute-start.18) | collective-permute-done | bytes 131104 | tf_op jit(solution)/shard_map/ppermute | solution.py:213
  72.1 0.3 collective-permute-done.21
  72.4 0.1 fusion.3
  72.5 0.1 collective-permute-start.24
  72.6 0.8 %collective-permute-start.22 = (bf16[32,512]{1,0:T(8,128)(2,1)S(1)}, bf16[32,512]{1,0:T(8,128)(2,1)S(1)}, u32[]{:S(2)}, u32[]{:S(2)}) collective-permute-start(bf16[32,512]{1,0:T(8,128)(2,1)S(1)} %get-tuple-element.81), channel_id=1, source_target_pairs={{0,3},{1,2},{2,1},{3,0},{4,7},{5,6},{6,5},{7,4},{8,11},{9,10},{10,... | collective-permute-start | bytes 98312 | tf_op jit(solution)/shard_map/ppermute | solution.py:323
  73.4 1.3 %collective-permute-start.23 = (bf16[32,512]{1,0:T(8,128)(2,1)S(1)}, bf16[32,512]{1,0:T(8,128)(2,1)S(1)}, u32[]{:S(2)}, u32[]{:S(2)}) collective-permute-start(bf16[32,512]{1,0:T(8,128)(2,1)S(1)} %get-tuple-element.82), channel_id=1, source_target_pairs={{0,2},{1,3},{2,0},{3,1},{4,6},{5,7},{6,4},{7,5},{8,10},{9,11},{10,... | collective-permute-start | bytes 98312 | tf_op jit(solution)/shard_map/ppermute | solution.py:323
  74.7 1.3 %collective-permute-done.22 = bf16[32,512]{1,0:T(8,128)(2,1)S(1)} collective-permute-done((bf16[32,512]{1,0:T(8,128)(2,1)S(1)}, bf16[32,512]{1,0:T(8,128)(2,1)S(1)}, u32[]{:S(2)}, u32[]{:S(2)}) %collective-permute-start.22) | collective-permute-done | bytes 32800 | tf_op jit(solution)/shard_map/ppermute | solution.py:323
  76.0 1.3 %collective-permute-done.23 = bf16[32,512]{1,0:T(8,128)(2,1)S(1)} collective-permute-done((bf16[32,512]{1,0:T(8,128)(2,1)S(1)}, bf16[32,512]{1,0:T(8,128)(2,1)S(1)}, u32[]{:S(2)}, u32[]{:S(2)}) %collective-permute-start.23) | collective-permute-done | bytes 32800 | tf_op jit(solution)/shard_map/ppermute | solution.py:323
  77.3 0.7 pad_maximum_fusion.2
  (22 shorter events, 0.2 us)
Async XLA Ops:
  0.0 4.9 %copy-start = (f32[128,8]{0,1:T(8,128)S(1)}, f32[128,8]{0,1:T(8,128)}, u32[]{:S(2)}) copy-start(f32[128,8]{0,1:T(8,128)} %param.17) | copy-start | bytes 12292
  1.9 5.3 %collective-permute-start = (bf16[128,256]{1,0:T(8,128)(2,1)S(1)}, bf16[128,256]{1,0:T(8,128)(2,1)S(1)}, u32[]{:S(2)}, u32[]{:S(2)}) collective-permute-start(bf16[128,256]{1,0:T(8,128)(2,1)S(1)} %get-tuple-element.42), channel_id=1, source_target_pairs={{0,4},{4,0},{8,12},{12,8},{16,20},{20,16},{24,28},{28,24},{1,5},{5... | collective-permute-start | bytes 196616 | tf_op jit(solution)/shard_map/ppermute | solution.py:373
  7.2 7.8 %collective-permute-start.3 = (bf16[128,256]{1,0:T(8,128)(2,1)S(1)}, bf16[128,256]{1,0:T(8,128)(2,1)S(1)}, u32[]{:S(2)}, u32[]{:S(2)}) collective-permute-start(bf16[128,256]{1,0:T(8,128)(2,1)S(1)} %fusion.6.after_ref), channel_id=1, source_target_pairs={{0,24},{4,28},{8,16},{12,20},{16,8},{20,12},{24,0},{28,4},{1,25},{... | collective-permute-start | bytes 196616 | tf_op jit(solution)/shard_map/ppermute | solution.py:313
  11.4 5.2 %collective-permute-start.2 = (bf16[128,256]{1,0:T(8,128)(2,1)S(1)}, bf16[128,256]{1,0:T(8,128)(2,1)S(1)}, u32[]{:S(2)}, u32[]{:S(2)}) collective-permute-start(bf16[128,256]{1,0:T(8,128)(2,1)S(1)} %fusion.6.after_ref), channel_id=1, source_target_pairs={{0,16},{4,20},{8,24},{12,28},{16,0},{20,4},{24,8},{28,12},{1,17},{... | collective-permute-start | bytes 196616 | tf_op jit(solution)/shard_map/ppermute | solution.py:313
  11.4 5.2 %collective-permute-start.1 = (bf16[128,256]{1,0:T(8,128)(2,1)S(1)}, bf16[128,256]{1,0:T(8,128)(2,1)S(1)}, u32[]{:S(2)}, u32[]{:S(2)}) collective-permute-start(bf16[128,256]{1,0:T(8,128)(2,1)S(1)} %fusion.6.after_ref), channel_id=1, source_target_pairs={{0,8},{4,12},{8,0},{12,4},{16,24},{20,28},{24,16},{28,20},{1,9},{5... | collective-permute-start | bytes 196616 | tf_op jit(solution)/shard_map/ppermute | solution.py:313
  16.6 4.3 %collective-permute-start.4 = (bf16[128,256]{1,0:T(8,128)(2,1)S(1)}, bf16[128,256]{1,0:T(8,128)(2,1)S(1)}, u32[]{:S(2)}, u32[]{:S(2)}) collective-permute-start(bf16[128,256]{1,0:T(8,128)(2,1)S(1)} %get-tuple-element.52.after_ref), channel_id=1, source_target_pairs={{0,4},{4,0},{8,12},{12,8},{16,20},{20,16},{24,28},{28,24},{1,5},{5... | collective-permute-start | bytes 196616 | tf_op jit(solution)/shard_map/ppermute | solution.py:389
  18.2 8.0 %copy-start.1 = (f32[2048]{0:T(1024)S(1)}, f32[2048]{0:T(1024)}, u32[]{:S(2)}) copy-start(f32[2048]{0:T(1024)} %param.15) | copy-start | bytes 24580
  21.9 3.7 %collective-permute-start.5 = (bf16[32,512]{1,0:T(8,128)(2,1)S(1)}, bf16[32,512]{1,0:T(8,128)(2,1)S(1)}, u32[]{:S(2)}, u32[]{:S(2)}) collective-permute-start(bf16[32,512]{1,0:T(8,128)(2,1)S(1)} %get-tuple-element.55), channel_id=1, source_target_pairs={{0,3},{1,2},{2,1},{3,0},{4,7},{5,6},{6,5},{7,4},{8,11},{9,10},{10,... | collective-permute-start | bytes 98312 | tf_op jit(solution)/shard_map/ppermute | solution.py:323
  22.0 4.0 %collective-permute-start.6 = (bf16[32,512]{1,0:T(8,128)(2,1)S(1)}, bf16[32,512]{1,0:T(8,128)(2,1)S(1)}, u32[]{:S(2)}, u32[]{:S(2)}) collective-permute-start(bf16[32,512]{1,0:T(8,128)(2,1)S(1)} %get-tuple-element.56), channel_id=1, source_target_pairs={{0,2},{1,3},{2,0},{3,1},{4,6},{5,7},{6,4},{7,5},{8,10},{9,11},{10,... | collective-permute-start | bytes 98312 | tf_op jit(solution)/shard_map/ppermute | solution.py:323
  23.5 2.4 %collective-permute-start.7 = (bf16[32,512]{1,0:T(8,128)(2,1)S(1)}, bf16[32,512]{1,0:T(8,128)(2,1)S(1)}, u32[]{:S(2)}, u32[]{:S(2)}) collective-permute-start(bf16[32,512]{1,0:T(8,128)(2,1)S(1)} %get-tuple-element.57), channel_id=1, source_target_pairs={{0,1},{1,0},{2,3},{3,2},{4,5},{5,4},{6,7},{7,6},{8,9},{9,8},{10,11... | collective-permute-start | bytes 98312 | tf_op jit(solution)/shard_map/ppermute | solution.py:323
  26.3 6.0 %collective-permute-start.11 = (bf16[32,2176]{1,0:T(8,128)(2,1)S(1)}, bf16[32,2176]{1,0:T(8,128)(2,1)S(1)}, u32[]{:S(2)}, u32[]{:S(2)}) collective-permute-start(bf16[32,2176]{1,0:T(8,128)(2,1)S(1)} %pad_maximum_fusion.refs_0_), channel_id=1, source_target_pairs={{0,4},{8,0},{16,8},{24,16},{28,24},{20,28},{12,20},{4,12},{1,5},{9... | collective-permute-start | bytes 417800 | tf_op jit(solution)/shard_map/ppermute | solution.py:213
  27.8 5.9 %collective-permute-start.8 = (bf16[32,2176]{1,0:T(8,128)(2,1)S(1)}, bf16[32,2176]{1,0:T(8,128)(2,1)S(1)}, u32[]{:S(2)}, u32[]{:S(2)}) collective-permute-start(bf16[32,2176]{1,0:T(8,128)(2,1)S(1)} %pad_maximum_fusion.refs_0_), channel_id=1, source_target_pairs={{0,8},{8,16},{16,24},{24,28},{28,20},{20,12},{12,4},{4,0},{1,9},{9... | collective-permute-start | bytes 417800 | tf_op jit(solution)/shard_map/ppermute | solution.py:213
  32.3 5.1 %collective-permute-start.12 = (bf16[32,2176]{1,0:T(8,128)(2,1)S(1)}, bf16[32,2176]{1,0:T(8,128)(2,1)S(1)}, u32[]{:S(2)}, u32[]{:S(2)}) collective-permute-start(bf16[32,2176]{1,0:T(8,128)(2,1)S(1)} %collective-permute-done.11.refs_4_), channel_id=1, source_target_pairs={{0,4},{8,0},{16,8},{24,16},{28,24},{20,28},{12,20},{4,12},{1,5},{9... | collective-permute-start | bytes 417800 | tf_op jit(solution)/shard_map/ppermute | solution.py:213
  33.8 5.1 %collective-permute-start.9 = (bf16[32,2176]{1,0:T(8,128)(2,1)S(1)}, bf16[32,2176]{1,0:T(8,128)(2,1)S(1)}, u32[]{:S(2)}, u32[]{:S(2)}) collective-permute-start(bf16[32,2176]{1,0:T(8,128)(2,1)S(1)} %collective-permute-done.8.after_ref.refs_1_), channel_id=1, source_target_pairs={{0,8},{8,16},{16,24},{24,28},{28,20},{20,12},{12,4},{4,0},{1,9},{9... | collective-permute-start | bytes 417800 | tf_op jit(solution)/shard_map/ppermute | solution.py:213
  37.4 7.5 %collective-permute-start.13 = (bf16[32,2176]{1,0:T(8,128)(2,1)S(1)}, bf16[32,2176]{1,0:T(8,128)(2,1)S(1)}, u32[]{:S(2)}, u32[]{:S(2)}) collective-permute-start(bf16[32,2176]{1,0:T(8,128)(2,1)S(1)} %collective-permute-done.12.refs_5_), channel_id=1, source_target_pairs={{0,4},{8,0},{16,8},{24,16},{28,24},{20,28},{12,20},{4,12},{1,5},{9... | collective-permute-start | bytes 417800 | tf_op jit(solution)/shard_map/ppermute | solution.py:213
  38.9 7.6 %collective-permute-start.14 = (bf16[32,2176]{1,0:T(8,128)(2,1)S(1)}, bf16[32,2176]{1,0:T(8,128)(2,1)S(1)}, u32[]{:S(2)}, u32[]{:S(2)}) collective-permute-start(bf16[32,2176]{1,0:T(8,128)(2,1)S(1)} %broadcast_select_fusion), channel_id=1, source_target_pairs={{0,16},{1,13},{2,18},{3,15},{8,24},{9,5},{10,26},{11,7},{16,28},{1... | collective-permute-start | bytes 417800 | tf_op jit(solution)/shard_map/ppermute | solution.py:223
  40.0 6.5 %collective-permute-start.10 = (bf16[32,2176]{1,0:T(8,128)(2,1)S(1)}, bf16[32,2176]{1,0:T(8,128)(2,1)S(1)}, u32[]{:S(2)}, u32[]{:S(2)}) collective-permute-start(bf16[32,2176]{1,0:T(8,128)(2,1)S(1)} %collective-permute-done.9.refs_2_), channel_id=1, source_target_pairs={{0,8},{8,16},{16,24},{24,28},{28,20},{20,12},{12,4},{4,0},{1,9},{9... | collective-permute-start | bytes 417800 | tf_op jit(solution)/shard_map/ppermute | solution.py:213
  50.7 5.0 %collective-permute-start.15 = (bf16[32,2048]{1,0:T(8,128)(2,1)S(1)}, bf16[32,2048]{1,0:T(8,128)(2,1)S(1)}, u32[]{:S(2)}, u32[]{:S(2)}) collective-permute-start(bf16[32,2048]{1,0:T(8,128)(2,1)S(1)} %get-tuple-element.64), channel_id=1, source_target_pairs={{0,8},{8,16},{16,24},{24,28},{28,20},{20,12},{12,4},{4,0},{1,9},{9... | collective-permute-start | bytes 393224 | tf_op jit(solution)/shard_map/ppermute | solution.py:213
  51.8 9.0 %collective-permute-start.16 = (bf16[32,2048]{1,0:T(8,128)(2,1)S(1)}, bf16[32,2048]{1,0:T(8,128)(2,1)S(1)}, u32[]{:S(2)}, u32[]{:S(2)}) collective-permute-start(bf16[32,2048]{1,0:T(8,128)(2,1)S(1)} %get-tuple-element.66), channel_id=1, source_target_pairs={{0,16},{1,13},{2,18},{3,15},{8,24},{9,5},{10,26},{11,7},{16,28},{1... | collective-permute-start | bytes 393224 | tf_op jit(solution)/shard_map/ppermute | solution.py:223
  53.9 6.8 %collective-permute-start.19 = (bf16[32,2048]{1,0:T(8,128)(2,1)S(1)}, bf16[32,2048]{1,0:T(8,128)(2,1)S(1)}, u32[]{:S(2)}, u32[]{:S(2)}) collective-permute-start(bf16[32,2048]{1,0:T(8,128)(2,1)S(1)} %get-tuple-element.68), channel_id=1, source_target_pairs={{0,4},{8,0},{16,8},{24,16},{28,24},{20,28},{12,20},{4,12},{1,5},{9... | collective-permute-start | bytes 393224 | tf_op jit(solution)/shard_map/ppermute | solution.py:213
  60.9 6.2 %collective-permute-start.17 = (bf16[32,2048]{1,0:T(8,128)(2,1)S(1)}, bf16[32,2048]{1,0:T(8,128)(2,1)S(1)}, u32[]{:S(2)}, u32[]{:S(2)}) collective-permute-start(bf16[32,2048]{1,0:T(8,128)(2,1)S(1)} %get-tuple-element.85), channel_id=1, source_target_pairs={{0,8},{8,16},{16,24},{24,28},{28,20},{20,12},{12,4},{4,0},{1,9},{9... | collective-permute-start | bytes 393224 | tf_op jit(solution)/shard_map/ppermute | solution.py:213
  60.9 6.4 %collective-permute-start.20 = (bf16[32,2048]{1,0:T(8,128)(2,1)S(1)}, bf16[32,2048]{1,0:T(8,128)(2,1)S(1)}, u32[]{:S(2)}, u32[]{:S(2)}) collective-permute-start(bf16[32,2048]{1,0:T(8,128)(2,1)S(1)} %get-tuple-element.86), channel_id=1, source_target_pairs={{0,4},{8,0},{16,8},{24,16},{28,24},{20,28},{12,20},{4,12},{1,5},{9... | collective-permute-start | bytes 393224 | tf_op jit(solution)/shard_map/ppermute | solution.py:213
  67.1 5.0 %collective-permute-start.18 = (bf16[32,2048]{1,0:T(8,128)(2,1)S(1)}, bf16[32,2048]{1,0:T(8,128)(2,1)S(1)}, u32[]{:S(2)}, u32[]{:S(2)}) collective-permute-start(bf16[32,2048]{1,0:T(8,128)(2,1)S(1)} %add_convert_fusion.2), channel_id=1, source_target_pairs={{0,8},{8,16},{16,24},{24,28},{28,20},{20,12},{12,4},{4,0},{1,9},{9... | collective-permute-start | bytes 393224 | tf_op jit(solution)/shard_map/ppermute | solution.py:213
  67.4 5.0 %collective-permute-start.21 = (bf16[32,2048]{1,0:T(8,128)(2,1)S(1)}, bf16[32,2048]{1,0:T(8,128)(2,1)S(1)}, u32[]{:S(2)}, u32[]{:S(2)}) collective-permute-start(bf16[32,2048]{1,0:T(8,128)(2,1)S(1)} %add_convert_fusion), channel_id=1, source_target_pairs={{0,4},{8,0},{16,8},{24,16},{28,24},{20,28},{12,20},{4,12},{1,5},{9... | collective-permute-start | bytes 393224 | tf_op jit(solution)/shard_map/ppermute | solution.py:213
  72.5 2.2 %collective-permute-start.24 = (bf16[32,512]{1,0:T(8,128)(2,1)S(1)}, bf16[32,512]{1,0:T(8,128)(2,1)S(1)}, u32[]{:S(2)}, u32[]{:S(2)}) collective-permute-start(bf16[32,512]{1,0:T(8,128)(2,1)S(1)} %get-tuple-element.80), channel_id=1, source_target_pairs={{0,1},{1,0},{2,3},{3,2},{4,5},{5,4},{6,7},{7,6},{8,9},{9,8},{10,11... | collective-permute-start | bytes 98312 | tf_op jit(solution)/shard_map/ppermute | solution.py:323
  72.6 3.4 %collective-permute-start.22 = (bf16[32,512]{1,0:T(8,128)(2,1)S(1)}, bf16[32,512]{1,0:T(8,128)(2,1)S(1)}, u32[]{:S(2)}, u32[]{:S(2)}) collective-permute-start(bf16[32,512]{1,0:T(8,128)(2,1)S(1)} %get-tuple-element.81), channel_id=1, source_target_pairs={{0,3},{1,2},{2,1},{3,0},{4,7},{5,6},{6,5},{7,4},{8,11},{9,10},{10,... | collective-permute-start | bytes 98312 | tf_op jit(solution)/shard_map/ppermute | solution.py:323
  73.4 3.9 %collective-permute-start.23 = (bf16[32,512]{1,0:T(8,128)(2,1)S(1)}, bf16[32,512]{1,0:T(8,128)(2,1)S(1)}, u32[]{:S(2)}, u32[]{:S(2)}) collective-permute-start(bf16[32,512]{1,0:T(8,128)(2,1)S(1)} %get-tuple-element.82), channel_id=1, source_target_pairs={{0,2},{1,3},{2,0},{3,1},{4,6},{5,7},{6,4},{7,5},{8,10},{9,11},{10,... | collective-permute-start | bytes 98312 | tf_op jit(solution)/shard_map/ppermute | solution.py:323

commit v11 on v10

--- a/solution.py
+++ b/solution.py
@@ -204,10 +204,10 @@
 
 
 def dense_experts(block, scalars, turns, weights_gate, weights_up, expert_out):
-    count = lax.axis_size("seq")
+    count, parts = lax.axis_size("seq"), lax.axis_size("exp")
     order = ring_order(count)
     far = count // 2
-    parts = lax.axis_size("exp")
+    turned = turns[0]
 
     def hop(rows, steps):
         return lax.ppermute(
@@ -222,32 +222,35 @@
                 pairs.append((order[p] * parts + e, target * parts + e))
         return lax.ppermute(rows, ("seq", "exp"), pairs)
 
-    ahead, behind = [block], [block]
-    for distance in range(1, far):
-        came, went = hop(ahead[-1], 1), hop(behind[-1], -1)
-        if distance == 1:
-            weights_out, _ = load_near(scalars, expert_out, 0, came)
-        ahead.append(came)
-        behind.append(went)
-    turned = turns[0]
-    farthest = far_hop(jnp.where(turned, behind[-2], ahead[-2]))
-    made = run_expert(
-        scalars, ahead + behind[1:] + [farthest], weights_gate, weights_up, weights_out
-    )
-    own, to_back, to_front, farthest = made[0], made[1:far], made[far:-1], made[-1]
-    going, coming = hop(to_front[-1], 1), hop(to_back[-1], -1)
-    early = far_hop(farthest)
-    for distance in range(far - 2, 0, -1):
-        front, back = to_front[distance - 1], to_back[distance - 1]
-        if distance == far - 2:
-            nothing = jnp.zeros_like(early)
-            going = add_rows(going, front, jnp.where(turned, nothing, early))
-            coming = add_rows(coming, back, jnp.where(turned, early, nothing))
-        else:
-            going = add_rows(going, front)
-            coming = add_rows(coming, back)
-        going, coming = hop(going, 1), hop(coming, -1)
-    return own, going, coming
+    def gather(rows):
+        ahead, behind = [rows], [rows]
+        for distance in range(1, far):
+            ahead.append(hop(ahead[-1], 1))
+            behind.append(hop(behind[-1], -1))
+        return ahead + behind[1:] + [far_hop(jnp.where(turned, behind[-2], ahead[-2]))]
+
+    def scatter(made):
+        own, to_back, to_front, farthest = made[0], made[1:far], made[far:-1], made[-1]
+        going, coming = hop(to_front[-1], 1), hop(to_back[-1], -1)
+        early = far_hop(farthest)
+        nothing = jnp.zeros_like(early)
+        for distance in range(far - 2, 0, -1):
+            front, back = [to_front[distance - 1]], [to_back[distance - 1]]
+            if distance == far - 2:
+                front.append(jnp.where(turned, nothing, early))
+                back.append(jnp.where(turned, early, nothing))
+            going, coming = add_rows(going, *front), add_rows(coming, *back)
+            going, coming = hop(going, 1), hop(coming, -1)
+        return own, going, coming
+
+    half = block.shape[0] // 2
+    streams = [gather(rows) for rows in (block[:half], block[half:])]
+    weights_out, _ = load_near(scalars, expert_out, 0, streams[0][1])
+    terms = [
+        scatter(run_expert(scalars, blocks, weights_gate, weights_up, weights_out))
+        for blocks in streams
+    ]
+    return [jnp.concatenate(pair) for pair in zip(*terms)]
 
 
 def slot_ids(block_routes, expert_count, capacity):

time: 78.2 us -> 80.2 us (1.026)
  starting transfers between devices: 30.4 us -> 42.8 us
  waiting for transfers between devices: 28.2 us -> 17 us
  Pallas kernels: 16.6 us -> 17.5 us
    ppermute x12 -> x24, starting transfers between devices: 13.7 us -> 24.3 us  [hop(): lax.ppermute(rows, 'seq', [(order[p], order[(p + steps) % count]) for p i...]
    ppermute x12 -> x24, waiting for transfers between devices: 14.8 us -> 5.78 us  [hop(): lax.ppermute(rows, 'seq', [(order[p], order[(p + steps) % count]) for p i...]
    ppermute x2 -> x4, waiting for transfers between devices: 6.66 us -> 3.13 us  [far_hop(): return lax.ppermute(rows, ('seq', 'exp'), pairs)]
    ppermute x2 -> x4, starting transfers between devices: 3.23 us -> 5.36 us  [far_hop(): return lax.ppermute(rows, ('seq', 'exp'), pairs)]
    ppermute x3, waiting for transfers between devices: 1.6 us -> 3.11 us  [prior_states(): lax.ppermute(total, 'seq', [(i, i ^ 2 * distance) for i in range(count)])]
    pallas_call x7 -> x8, Pallas kernels: 16.6 us -> 17.5 us  [call(): pl.pallas_call(kernel, out_shape=outs, in_specs=[SCALAR if i == 0 or i in...]
  transfers between devices with their start and end apart: 25 -> 39, of which waited for: 15 -> 16; matrix products, arithmetic and copies ran while one was open for 2% -> 2% of each run, Pallas kernels for 13% -> 18%
where the time goes in v11:
time: 80.2 us; the launch traced here: 80 us
  starting transfers between devices  42.8 us (53%)
  Pallas kernels  17.5 us (22%)
  waiting for transfers between devices  17 us (21%)
  other arithmetic  1.45 us (2%)
  local copies, waits for them, and re-layouts  1.09 us (1%)
    ppermute x24, starting transfers between devices, hop(): lax.ppermute(rows, 'seq', [(order[p], order[(p + steps) % count]) for p i...  24.3 us
    pallas_call x8, Pallas kernels, call(): pl.pallas_call(kernel, out_shape=outs, in_specs=[SCALAR if i == 0 or i in...  17.5 us
    ppermute x24, waiting for transfers between devices, hop(): lax.ppermute(rows, 'seq', [(order[p], order[(p + steps) % count]) for p i...  5.78 us
    ppermute x4, starting transfers between devices, far_hop(): return lax.ppermute(rows, ('seq', 'exp'), pairs)  5.36 us
    ppermute x3, starting transfers between devices, prior_states(): lax.ppermute(total, 'seq', [(i, i ^ 2 * distance) for i in range(count)])  4.76 us
    ppermute x6, waiting for transfers between devices, exchange(): lax.ppermute(pieces[j], 'exp', [(i, i ^ j) for i in range(parts)])  4.54 us
    ppermute x6, starting transfers between devices, exchange(): lax.ppermute(pieces[j], 'exp', [(i, i ^ j) for i in range(parts)])  3.84 us
    ppermute x4, waiting for transfers between devices, far_hop(): return lax.ppermute(rows, ('seq', 'exp'), pairs)  3.13 us
  transfers between devices with their start and end apart: 39, of which 16 were waited for; matrix products, arithmetic and copies ran while one was open for 2% of the time, Pallas kernels for 18%

profile of v11, /device:TPU:0, one launch (start us, length us, event | category | flops | bytes accessed | tf_op | source)
XLA Modules:
  0.0 80.0 jit_solution(17091248143792789952)
XLA Ops:
  0.0 0.1 stack.24.scalars
  0.1 1.8 %shard_map.100 = (bf16[128,256]{1,0:T(8,128)(2,1)S(1)}, bf16[128,256]{1,0:T(8,128)(2,1)S(1)}, bf16[128,512]{1,0:T(8,128)(2,1)S(1)}, bf16[128,512]{1,0:T(8,128)(2...) custom-call(s32[7]{0:T(128)S(1)} %stack.24.scalars, ...), custom_call_target="tpu_custom_call" | custom-call | flops 16777216 | bytes 1188892 | tf_op jit(solution)/shard_map/pallas_call | solution.py:24
  1.9 3.0 %collective-permute-start = (bf16[128,256]{1,0:T(8,128)(2,1)S(1)}, bf16[128,256]{1,0:T(8,128)(2,1)S(1)}, u32[]{:S(2)}, u32[]{:S(2)}) collective-permute-start(bf16[128,256]{1,0:T(8,128)(2,1)S(1)} %get-tuple-element.50), channel_id=1, source_target_pairs={{0,4},{4,0},{8,12},{12,8},{16,20},{20,16},{24,28},{28,24},{1,5},{5... | collective-permute-start | bytes 196616 | tf_op jit(solution)/shard_map/ppermute | solution.py:376
  5.0 0.9 %shard_map.101.within_ref = f32[128,512]{1,0:T(8,128)S(1)} custom-call(s32[7]{0:T(128)S(1)} %stack.24.scalars, bf16[128,512]{1,0:T(8,128)(2,1)S(1)} %get-tuple-element.51.keys, bf16[128,512]{1,0:T(8,128)(2,1)S(1)} %get-tuple-element.52.values, bf16[128,512]{1,0:T(8,128)(2,1)S(1)} %get-tuple-element.53.queries), custom_call_target="tpu_custom_call" | custom-call | flops 50331648 | bytes 655388 | tf_op jit(solution)/shard_map/pallas_call | solution.py:24
  5.9 0.8 constant_dynamic-slice_fusion.1
  6.7 0.5 collective-permute-done
  7.2 2.2 %collective-permute-start.1 = (bf16[128,256]{1,0:T(8,128)(2,1)S(1)}, bf16[128,256]{1,0:T(8,128)(2,1)S(1)}, u32[]{:S(2)}, u32[]{:S(2)}) collective-permute-start(bf16[128,256]{1,0:T(8,128)(2,1)S(1)} %fusion.6.after_ref), channel_id=1, source_target_pairs={{0,8},{4,12},{8,0},{12,4},{16,24},{20,28},{24,16},{28,20},{1,9},{5... | collective-permute-start | bytes 196616 | tf_op jit(solution)/shard_map/ppermute | solution.py:316
  9.3 2.6 %collective-permute-start.2 = (bf16[128,256]{1,0:T(8,128)(2,1)S(1)}, bf16[128,256]{1,0:T(8,128)(2,1)S(1)}, u32[]{:S(2)}, u32[]{:S(2)}) collective-permute-start(bf16[128,256]{1,0:T(8,128)(2,1)S(1)} %fusion.6.after_ref), channel_id=1, source_target_pairs={{0,16},{4,20},{8,24},{12,28},{16,0},{20,4},{24,8},{28,12},{1,17},{... | collective-permute-start | bytes 196616 | tf_op jit(solution)/shard_map/ppermute | solution.py:316
  12.1 2.8 %shard_map.102 = (bf16[2048,1024]{1,0:T(8,128)(2,1)S(1)}, f32[8,128]{1,0:T(8,128)S(1)}) custom-call(s32[7]{0:T(128)S(1)} %stack.24.scalars, bf16[2,2048,1024]{2,1,0:T(8,128)(2,1)} %bitcast.16, bf16[128,256]{1,0:T(8,128)(2,1)S(1)} %fusion.6.after_ref), custom_call_target="tpu_custom_call" | custom-call | bytes 12652572 | tf_op jit(solution)/shard_map/pallas_call | solution.py:24
  14.9 1.0 %collective-permute-done.2 = bf16[128,256]{1,0:T(8,128)(2,1)S(1)} collective-permute-done((bf16[128,256]{1,0:T(8,128)(2,1)S(1)}, bf16[128,256]{1,0:T(8,128)(2,1)S(1)}, u32[]{:S(2)}, u32[]{:S(2)}) %collective-permute-start.2) | collective-permute-done | bytes 65568 | tf_op jit(solution)/shard_map/ppermute | solution.py:316
  15.9 2.1 %collective-permute-done.3 = bf16[128,256]{1,0:T(8,128)(2,1)S(1)} collective-permute-done((bf16[128,256]{1,0:T(8,128)(2,1)S(1)}, bf16[128,256]{1,0:T(8,128)(2,1)S(1)}, u32[]{:S(2)}, u32[]{:S(2)}) %collective-permute-start.3) | collective-permute-done | bytes 65568 | tf_op jit(solution)/shard_map/ppermute | solution.py:316
  18.1 1.6 %collective-permute-start.4 = (bf16[128,256]{1,0:T(8,128)(2,1)S(1)}, bf16[128,256]{1,0:T(8,128)(2,1)S(1)}, u32[]{:S(2)}, u32[]{:S(2)}) collective-permute-start(bf16[128,256]{1,0:T(8,128)(2,1)S(1)} %get-tuple-element.60.after_ref), channel_id=1, source_target_pairs={{0,4},{4,0},{8,12},{12,8},{16,20},{20,16},{24,28},{28,24},{1,5},{5... | collective-permute-start | bytes 196616 | tf_op jit(solution)/shard_map/ppermute | solution.py:392
  19.6 2.8 %shard_map.103 = (bf16[2048,1024]{1,0:T(8,128)(2,1)S(1)}, f32[8,128]{1,0:T(8,128)S(1)}) custom-call(s32[7]{0:T(128)S(1)} %stack.24.scalars, bf16[2,2048,1024]{2,1,0:T(8,128)(2,1)} %bitcast.17, bf16[128,256]{1,0:T(8,128)(2,1)S(1)} %get-tuple-element.60.after_ref), custom_call_target="tpu_custom_call" | custom-call | bytes 12652572 | tf_op jit(solution)/shard_map/pallas_call | solution.py:24
  22.4 0.9 %shard_map.104 = (bf16[32,512]{1,0:T(8,128)(2,1)S(1)}, bf16[32,512]{1,0:T(8,128)(2,1)S(1)}, bf16[32,512]{1,0:T(8,128)(2,1)S(1)}, bf16[32,512]{1,0:T(8,128)(2,1)S(1)}) custom-call(s32[7]{0:T(128)S(1)} %stack.24.scalars, f32[128,512]{1,0:T(8,128)S(1)} %shard_map.101.within_ref, bf16[128,512]{1,0:T(8,128)(2,1)S(1)} %get-tuple-element.53.queries, ...), custom_call_target="tpu_custom_call" | custom-call | flops 33554432 | bytes 862236 | tf_op jit(solution)/shard_map/pallas_call | solution.py:24
  23.4 1.6 %collective-permute-start.6 = (bf16[32,512]{1,0:T(8,128)(2,1)S(1)}, bf16[32,512]{1,0:T(8,128)(2,1)S(1)}, u32[]{:S(2)}, u32[]{:S(2)}) collective-permute-start(bf16[32,512]{1,0:T(8,128)(2,1)S(1)} %get-tuple-element.64), channel_id=1, source_target_pairs={{0,2},{1,3},{2,0},{3,1},{4,6},{5,7},{6,4},{7,5},{8,10},{9,11},{10,... | collective-permute-start | bytes 98312 | tf_op jit(solution)/shard_map/ppermute | solution.py:326
  25.0 0.3 collective-permute-start.7
  25.3 1.7 %collective-permute-done.5 = bf16[32,512]{1,0:T(8,128)(2,1)S(1)} collective-permute-done((bf16[32,512]{1,0:T(8,128)(2,1)S(1)}, bf16[32,512]{1,0:T(8,128)(2,1)S(1)}, u32[]{:S(2)}, u32[]{:S(2)}) %collective-permute-start.5) | collective-permute-done | bytes 32800 | tf_op jit(solution)/shard_map/ppermute | solution.py:326
  27.0 0.4 collective-permute-done.6
  27.5 0.1 fusion
  27.6 0.1 fusion.2
  27.7 1.5 %collective-permute-start.11 = (bf16[16,2176]{1,0:T(8,128)(2,1)S(1)}, bf16[16,2176]{1,0:T(8,128)(2,1)S(1)}, u32[]{:S(2)}, u32[]{:S(2)}) collective-permute-start(bf16[16,2176]{1,0:T(8,128)(2,1)S(1)} %get-tuple-element.97.refs_0_), channel_id=1, source_target_pairs={{0,4},{8,0},{16,8},{24,16},{28,24},{20,28},{12,20},{4,12},{1,5},{9... | collective-permute-start | bytes 208904 | tf_op jit(solution)/shard_map/ppermute | solution.py:213
  29.3 0.5 collective-permute-start.8
  29.8 2.0 %collective-permute-start.18 = (bf16[16,2176]{1,0:T(8,128)(2,1)S(1)}, bf16[16,2176]{1,0:T(8,128)(2,1)S(1)}, u32[]{:S(2)}, u32[]{:S(2)}) collective-permute-start(bf16[16,2176]{1,0:T(8,128)(2,1)S(1)} %get-tuple-element.96.refs_0_), channel_id=1, source_target_pairs={{0,4},{8,0},{16,8},{24,16},{28,24},{20,28},{12,20},{4,12},{1,5},{9... | collective-permute-start | bytes 208904 | tf_op jit(solution)/shard_map/ppermute | solution.py:213
  31.8 0.4 collective-permute-done.11.refs_4_
  32.2 1.5 %collective-permute-start.12 = (bf16[16,2176]{1,0:T(8,128)(2,1)S(1)}, bf16[16,2176]{1,0:T(8,128)(2,1)S(1)}, u32[]{:S(2)}, u32[]{:S(2)}) collective-permute-start(bf16[16,2176]{1,0:T(8,128)(2,1)S(1)} %collective-permute-done.11.refs_4_), channel_id=1, source_target_pairs={{0,4},{8,0},{16,8},{24,16},{28,24},{20,28},{12,20},{4,12},{1,5},{9... | collective-permute-start | bytes 208904 | tf_op jit(solution)/shard_map/ppermute | solution.py:213
  33.7 0.5 collective-permute-done.8.after_ref.refs_1_
  34.2 0.6 collective-permute-start.9
  34.7 3.3 %shard_map.105 = (bf16[1024,2048]{1,0:T(8,128)(2,1)S(1)}, f32[8,128]{1,0:T(8,128)}) custom-call(s32[7]{0:T(128)S(1)} %stack.24.scalars, bf16[1,1024,2048]{2,1,0:T(8,128)(2,1)} %source.1, bf16[16,2176]{1,0:T(8,128)(2,1)S(1)} %collective-permute-done.8.after_ref.refs_1_), custom_call_target="tpu_custom_call" | custom-call | bytes 8462364 | tf_op jit(solution)/shard_map/pallas_call | solution.py:24
  38.1 0.1 collective-permute-start.16
  38.2 1.9 %collective-permute-start.19 = (bf16[16,2176]{1,0:T(8,128)(2,1)S(1)}, bf16[16,2176]{1,0:T(8,128)(2,1)S(1)}, u32[]{:S(2)}, u32[]{:S(2)}) collective-permute-start(bf16[16,2176]{1,0:T(8,128)(2,1)S(1)} %collective-permute-done.18.refs_4_), channel_id=1, source_target_pairs={{0,4},{8,0},{16,8},{24,16},{28,24},{20,28},{12,20},{4,12},{1,5},{9... | collective-permute-start | bytes 208904 | tf_op jit(solution)/shard_map/ppermute | solution.py:213
  40.2 0.8 collective-permute-start.14
  41.0 0.6 collective-permute-start.10
  41.6 1.4 %collective-permute-start.13 = (bf16[16,2176]{1,0:T(8,128)(2,1)S(1)}, bf16[16,2176]{1,0:T(8,128)(2,1)S(1)}, u32[]{:S(2)}, u32[]{:S(2)}) collective-permute-start(bf16[16,2176]{1,0:T(8,128)(2,1)S(1)} %collective-permute-done.12.refs_5_), channel_id=1, source_target_pairs={{0,4},{8,0},{16,8},{24,16},{28,24},{20,28},{12,20},{4,12},{1,5},{9... | collective-permute-start | bytes 208904 | tf_op jit(solution)/shard_map/ppermute | solution.py:213
  43.0 1.0 %collective-permute-done.19.refs_5_ = bf16[16,2176]{1,0:T(8,128)(2,1)S(1)} collective-permute-done((bf16[16,2176]{1,0:T(8,128)(2,1)S(1)}, bf16[16,2176]{1,0:T(8,128)(2,1)S(1)}, u32[]{:S(2)}, u32[]{:S(2)}) %collective-permute-start.19) | collective-permute-done | bytes 69664 | tf_op jit(solution)/shard_map/ppermute | solution.py:213
  44.1 0.8 collective-permute-start.21
  44.8 1.2 %collective-permute-start.17 = (bf16[16,2176]{1,0:T(8,128)(2,1)S(1)}, bf16[16,2176]{1,0:T(8,128)(2,1)S(1)}, u32[]{:S(2)}, u32[]{:S(2)}) collective-permute-start(bf16[16,2176]{1,0:T(8,128)(2,1)S(1)} %collective-permute-done.16.refs_2_), channel_id=1, source_target_pairs={{0,8},{8,16},{16,24},{24,28},{28,20},{20,12},{12,4},{4,0},{1,9},{9... | collective-permute-start | bytes 208904 | tf_op jit(solution)/shard_map/ppermute | solution.py:213
  46.1 0.2 collective-permute-done.14.refs_7_
  46.2 1.7 %collective-permute-start.20 = (bf16[16,2176]{1,0:T(8,128)(2,1)S(1)}, bf16[16,2176]{1,0:T(8,128)(2,1)S(1)}, u32[]{:S(2)}, u32[]{:S(2)}) collective-permute-start(bf16[16,2176]{1,0:T(8,128)(2,1)S(1)} %collective-permute-done.19.refs_5_), channel_id=1, source_target_pairs={{0,4},{8,0},{16,8},{24,16},{28,24},{20,28},{12,20},{4,12},{1,5},{9... | collective-permute-start | bytes 208904 | tf_op jit(solution)/shard_map/ppermute | solution.py:213
  47.9 2.5 %shard_map.106 = (bf16[16,2048]{1,0:T(8,128)(2,1)S(1)}, bf16[16,2048]{1,0:T(8,128)(2,1)S(1)}, bf16[16,2048]{1,0:T(8,128)(2,1)S(1)}, bf16[16,2048]{1,0:T(8,128)(2...) custom-call(s32[7]{0:T(128)S(1)} %stack.24.scalars, ...), custom_call_target="tpu_custom_call" | custom-call | flops 1610612736 | bytes 13664284 | tf_op jit(solution)/shard_map/pallas_call | solution.py:24
  50.5 0.5 collective-permute-start.22
  50.9 1.9 %collective-permute-start.23 = (bf16[16,2048]{1,0:T(8,128)(2,1)S(1)}, bf16[16,2048]{1,0:T(8,128)(2,1)S(1)}, u32[]{:S(2)}, u32[]{:S(2)}) collective-permute-start(bf16[16,2048]{1,0:T(8,128)(2,1)S(1)} %get-tuple-element.75), channel_id=1, source_target_pairs={{0,16},{1,13},{2,18},{3,15},{8,24},{9,5},{10,26},{11,7},{16,28},{1... | collective-permute-start | bytes 196616 | tf_op jit(solution)/shard_map/ppermute | solution.py:223
  52.8 0.6 collective-permute-start.30
  53.4 2.5 %shard_map.107 = (bf16[16,2048]{1,0:T(8,128)(2,1)S(1)}, bf16[16,2048]{1,0:T(8,128)(2,1)S(1)}, bf16[16,2048]{1,0:T(8,128)(2,1)S(1)}, bf16[16,2048]{1,0:T(8,128)(2...) custom-call(s32[7]{0:T(128)S(1)} %stack.24.scalars, ...), custom_call_target="tpu_custom_call" | custom-call | flops 1610612736 | bytes 13664284 | tf_op jit(solution)/shard_map/pallas_call | solution.py:24
  55.9 1.5 %collective-permute-start.26 = (bf16[16,2048]{1,0:T(8,128)(2,1)S(1)}, bf16[16,2048]{1,0:T(8,128)(2,1)S(1)}, u32[]{:S(2)}, u32[]{:S(2)}) collective-permute-start(bf16[16,2048]{1,0:T(8,128)(2,1)S(1)} %get-tuple-element.77), channel_id=1, source_target_pairs={{0,8},{8,16},{16,24},{24,28},{28,20},{20,12},{12,4},{4,0},{1,9},{9... | collective-permute-start | bytes 196616 | tf_op jit(solution)/shard_map/ppermute | solution.py:213
  57.4 1.9 %collective-permute-start.27 = (bf16[16,2048]{1,0:T(8,128)(2,1)S(1)}, bf16[16,2048]{1,0:T(8,128)(2,1)S(1)}, u32[]{:S(2)}, u32[]{:S(2)}) collective-permute-start(bf16[16,2048]{1,0:T(8,128)(2,1)S(1)} %get-tuple-element.79), channel_id=1, source_target_pairs={{0,16},{1,13},{2,18},{3,15},{8,24},{9,5},{10,26},{11,7},{16,28},{1... | collective-permute-start | bytes 196616 | tf_op jit(solution)/shard_map/ppermute | solution.py:223
  59.3 0.7 collective-permute-start.33
  60.0 1.0 %collective-permute-start.31 = (bf16[16,2048]{1,0:T(8,128)(2,1)S(1)}, bf16[16,2048]{1,0:T(8,128)(2,1)S(1)}, u32[]{:S(2)}, u32[]{:S(2)}) collective-permute-start(bf16[16,2048]{1,0:T(8,128)(2,1)S(1)} %get-tuple-element.107), channel_id=1, source_target_pairs={{0,4},{8,0},{16,8},{24,16},{28,24},{20,28},{12,20},{4,12},{1,5},{9... | collective-permute-start | bytes 196616 | tf_op jit(solution)/shard_map/ppermute | solution.py:213
  61.0 3.0 %collective-permute-done.27 = bf16[16,2048]{1,0:T(8,128)(2,1)S(1)} collective-permute-done((bf16[16,2048]{1,0:T(8,128)(2,1)S(1)}, bf16[16,2048]{1,0:T(8,128)(2,1)S(1)}, u32[]{:S(2)}, u32[]{:S(2)}) %collective-permute-start.27) | collective-permute-done | bytes 65568 | tf_op jit(solution)/shard_map/ppermute | solution.py:223
  64.0 0.3 collective-permute-start.34
  64.4 1.8 %collective-permute-start.24 = (bf16[16,2048]{1,0:T(8,128)(2,1)S(1)}, bf16[16,2048]{1,0:T(8,128)(2,1)S(1)}, u32[]{:S(2)}, u32[]{:S(2)}) collective-permute-start(bf16[16,2048]{1,0:T(8,128)(2,1)S(1)} %get-tuple-element.108), channel_id=1, source_target_pairs={{0,8},{8,16},{16,24},{24,28},{28,20},{20,12},{12,4},{4,0},{1,9},{9... | collective-permute-start | bytes 196616 | tf_op jit(solution)/shard_map/ppermute | solution.py:213
  66.1 0.2 collective-permute-start.28
  66.4 1.9 %collective-permute-start.32 = (bf16[16,2048]{1,0:T(8,128)(2,1)S(1)}, bf16[16,2048]{1,0:T(8,128)(2,1)S(1)}, u32[]{:S(2)}, u32[]{:S(2)}) collective-permute-start(bf16[16,2048]{1,0:T(8,128)(2,1)S(1)} %add_convert_fusion.2), channel_id=1, source_target_pairs={{0,4},{8,0},{16,8},{24,16},{28,24},{20,28},{12,20},{4,12},{1,5},{9... | collective-permute-start | bytes 196616 | tf_op jit(solution)/shard_map/ppermute | solution.py:213
  68.2 0.1 collective-permute-done.34
  68.4 0.3 collective-permute-start.35
  68.7 1.8 %collective-permute-start.25 = (bf16[16,2048]{1,0:T(8,128)(2,1)S(1)}, bf16[16,2048]{1,0:T(8,128)(2,1)S(1)}, u32[]{:S(2)}, u32[]{:S(2)}) collective-permute-start(bf16[16,2048]{1,0:T(8,128)(2,1)S(1)} %add_convert_fusion.6), channel_id=1, source_target_pairs={{0,8},{8,16},{16,24},{24,28},{28,20},{20,12},{12,4},{4,0},{1,9},{9... | collective-permute-start | bytes 196616 | tf_op jit(solution)/shard_map/ppermute | solution.py:213
  70.6 0.6 collective-permute-start.29
  71.2 1.5 %collective-permute-done.35 = bf16[16,2048]{1,0:T(8,128)(2,1)S(1)} collective-permute-done((bf16[16,2048]{1,0:T(8,128)(2,1)S(1)}, bf16[16,2048]{1,0:T(8,128)(2,1)S(1)}, u32[]{:S(2)}, u32[]{:S(2)}) %collective-permute-start.35) | collective-permute-done | bytes 65568 | tf_op jit(solution)/shard_map/ppermute | solution.py:213
  72.7 0.3 collective-permute-done.25
  73.0 1.8 %collective-permute-done.29 = bf16[16,2048]{1,0:T(8,128)(2,1)S(1)} collective-permute-done((bf16[16,2048]{1,0:T(8,128)(2,1)S(1)}, bf16[16,2048]{1,0:T(8,128)(2,1)S(1)}, u32[]{:S(2)}, u32[]{:S(2)}) %collective-permute-start.29) | collective-permute-done | bytes 65568 | tf_op jit(solution)/shard_map/ppermute | solution.py:213
  75.1 1.0 %collective-permute-start.37 = (bf16[32,512]{1,0:T(8,128)(2,1)S(1)}, bf16[32,512]{1,0:T(8,128)(2,1)S(1)}, u32[]{:S(2)}, u32[]{:S(2)}) collective-permute-start(bf16[32,512]{1,0:T(8,128)(2,1)S(1)} %get-tuple-element.100), channel_id=1, source_target_pairs={{0,2},{1,3},{2,0},{3,1},{4,6},{5,7},{6,4},{7,5},{8,10},{9,11},{10,... | collective-permute-start | bytes 98312 | tf_op jit(solution)/shard_map/ppermute | solution.py:326
  76.1 0.8 %collective-permute-start.38 = (bf16[32,512]{1,0:T(8,128)(2,1)S(1)}, bf16[32,512]{1,0:T(8,128)(2,1)S(1)}, u32[]{:S(2)}, u32[]{:S(2)}) collective-permute-start(bf16[32,512]{1,0:T(8,128)(2,1)S(1)} %get-tuple-element.98), channel_id=1, source_target_pairs={{0,1},{1,0},{2,3},{3,2},{4,5},{5,4},{6,7},{7,6},{8,9},{9,8},{10,11... | collective-permute-start | bytes 98312 | tf_op jit(solution)/shard_map/ppermute | solution.py:326
  76.9 1.5 %collective-permute-done.36 = bf16[32,512]{1,0:T(8,128)(2,1)S(1)} collective-permute-done((bf16[32,512]{1,0:T(8,128)(2,1)S(1)}, bf16[32,512]{1,0:T(8,128)(2,1)S(1)}, u32[]{:S(2)}, u32[]{:S(2)}) %collective-permute-start.36) | collective-permute-done | bytes 32800 | tf_op jit(solution)/shard_map/ppermute | solution.py:326
  78.4 1.0 %collective-permute-done.37 = bf16[32,512]{1,0:T(8,128)(2,1)S(1)} collective-permute-done((bf16[32,512]{1,0:T(8,128)(2,1)S(1)}, bf16[32,512]{1,0:T(8,128)(2,1)S(1)}, u32[]{:S(2)}, u32[]{:S(2)}) %collective-permute-start.37) | collective-permute-done | bytes 32800 | tf_op jit(solution)/shard_map/ppermute | solution.py:326
  79.4 0.7 pad_maximum_fusion.1
  (55 shorter events, 1.0 us)
Async XLA Ops:
  0.0 4.9 %copy-start = (f32[128,8]{0,1:T(8,128)S(1)}, f32[128,8]{0,1:T(8,128)}, u32[]{:S(2)}) copy-start(f32[128,8]{0,1:T(8,128)} %param.17) | copy-start | bytes 12292
  1.9 5.3 %collective-permute-start = (bf16[128,256]{1,0:T(8,128)(2,1)S(1)}, bf16[128,256]{1,0:T(8,128)(2,1)S(1)}, u32[]{:S(2)}, u32[]{:S(2)}) collective-permute-start(bf16[128,256]{1,0:T(8,128)(2,1)S(1)} %get-tuple-element.50), channel_id=1, source_target_pairs={{0,4},{4,0},{8,12},{12,8},{16,20},{20,16},{24,28},{28,24},{1,5},{5... | collective-permute-start | bytes 196616 | tf_op jit(solution)/shard_map/ppermute | solution.py:376
  7.2 7.7 %collective-permute-start.1 = (bf16[128,256]{1,0:T(8,128)(2,1)S(1)}, bf16[128,256]{1,0:T(8,128)(2,1)S(1)}, u32[]{:S(2)}, u32[]{:S(2)}) collective-permute-start(bf16[128,256]{1,0:T(8,128)(2,1)S(1)} %fusion.6.after_ref), channel_id=1, source_target_pairs={{0,8},{4,12},{8,0},{12,4},{16,24},{20,28},{24,16},{28,20},{1,9},{5... | collective-permute-start | bytes 196616 | tf_op jit(solution)/shard_map/ppermute | solution.py:316
  9.3 6.6 %collective-permute-start.2 = (bf16[128,256]{1,0:T(8,128)(2,1)S(1)}, bf16[128,256]{1,0:T(8,128)(2,1)S(1)}, u32[]{:S(2)}, u32[]{:S(2)}) collective-permute-start(bf16[128,256]{1,0:T(8,128)(2,1)S(1)} %fusion.6.after_ref), channel_id=1, source_target_pairs={{0,16},{4,20},{8,24},{12,28},{16,0},{20,4},{24,8},{28,12},{1,17},{... | collective-permute-start | bytes 196616 | tf_op jit(solution)/shard_map/ppermute | solution.py:316
  11.9 6.1 %collective-permute-start.3 = (bf16[128,256]{1,0:T(8,128)(2,1)S(1)}, bf16[128,256]{1,0:T(8,128)(2,1)S(1)}, u32[]{:S(2)}, u32[]{:S(2)}) collective-permute-start(bf16[128,256]{1,0:T(8,128)(2,1)S(1)} %fusion.6.after_ref), channel_id=1, source_target_pairs={{0,24},{4,28},{8,16},{12,20},{16,8},{20,12},{24,0},{28,4},{1,25},{... | collective-permute-start | bytes 196616 | tf_op jit(solution)/shard_map/ppermute | solution.py:316
  18.1 4.3 %collective-permute-start.4 = (bf16[128,256]{1,0:T(8,128)(2,1)S(1)}, bf16[128,256]{1,0:T(8,128)(2,1)S(1)}, u32[]{:S(2)}, u32[]{:S(2)}) collective-permute-start(bf16[128,256]{1,0:T(8,128)(2,1)S(1)} %get-tuple-element.60.after_ref), channel_id=1, source_target_pairs={{0,4},{4,0},{8,12},{12,8},{16,20},{20,16},{24,28},{28,24},{1,5},{5... | collective-permute-start | bytes 196616 | tf_op jit(solution)/shard_map/ppermute | solution.py:392
  19.6 8.0 %copy-start.1 = (f32[2048]{0:T(1024)S(1)}, f32[2048]{0:T(1024)}, u32[]{:S(2)}) copy-start(f32[2048]{0:T(1024)} %param.15) | copy-start | bytes 24580
  23.3 3.7 %collective-permute-start.5 = (bf16[32,512]{1,0:T(8,128)(2,1)S(1)}, bf16[32,512]{1,0:T(8,128)(2,1)S(1)}, u32[]{:S(2)}, u32[]{:S(2)}) collective-permute-start(bf16[32,512]{1,0:T(8,128)(2,1)S(1)} %get-tuple-element.63), channel_id=1, source_target_pairs={{0,3},{1,2},{2,1},{3,0},{4,7},{5,6},{6,5},{7,4},{8,11},{9,10},{10,... | collective-permute-start | bytes 98312 | tf_op jit(solution)/shard_map/ppermute | solution.py:326
  23.4 4.0 %collective-permute-start.6 = (bf16[32,512]{1,0:T(8,128)(2,1)S(1)}, bf16[32,512]{1,0:T(8,128)(2,1)S(1)}, u32[]{:S(2)}, u32[]{:S(2)}) collective-permute-start(bf16[32,512]{1,0:T(8,128)(2,1)S(1)} %get-tuple-element.64), channel_id=1, source_target_pairs={{0,2},{1,3},{2,0},{3,1},{4,6},{5,7},{6,4},{7,5},{8,10},{9,11},{10,... | collective-permute-start | bytes 98312 | tf_op jit(solution)/shard_map/ppermute | solution.py:326
  25.0 2.4 %collective-permute-start.7 = (bf16[32,512]{1,0:T(8,128)(2,1)S(1)}, bf16[32,512]{1,0:T(8,128)(2,1)S(1)}, u32[]{:S(2)}, u32[]{:S(2)}) collective-permute-start(bf16[32,512]{1,0:T(8,128)(2,1)S(1)} %get-tuple-element.65), channel_id=1, source_target_pairs={{0,1},{1,0},{2,3},{3,2},{4,5},{5,4},{6,7},{7,6},{8,9},{9,8},{10,11... | collective-permute-start | bytes 98312 | tf_op jit(solution)/shard_map/ppermute | solution.py:326
  27.7 4.5 %collective-permute-start.11 = (bf16[16,2176]{1,0:T(8,128)(2,1)S(1)}, bf16[16,2176]{1,0:T(8,128)(2,1)S(1)}, u32[]{:S(2)}, u32[]{:S(2)}) collective-permute-start(bf16[16,2176]{1,0:T(8,128)(2,1)S(1)} %get-tuple-element.97.refs_0_), channel_id=1, source_target_pairs={{0,4},{8,0},{16,8},{24,16},{28,24},{20,28},{12,20},{4,12},{1,5},{9... | collective-permute-start | bytes 208904 | tf_op jit(solution)/shard_map/ppermute | solution.py:213
  29.3 4.9 %collective-permute-start.8 = (bf16[16,2176]{1,0:T(8,128)(2,1)S(1)}, bf16[16,2176]{1,0:T(8,128)(2,1)S(1)}, u32[]{:S(2)}, u32[]{:S(2)}) collective-permute-start(bf16[16,2176]{1,0:T(8,128)(2,1)S(1)} %get-tuple-element.97.refs_0_), channel_id=1, source_target_pairs={{0,8},{8,16},{16,24},{24,28},{28,20},{20,12},{12,4},{4,0},{1,9},{9... | collective-permute-start | bytes 208904 | tf_op jit(solution)/shard_map/ppermute | solution.py:213
  29.8 8.3 %collective-permute-start.15 = (bf16[16,2176]{1,0:T(8,128)(2,1)S(1)}, bf16[16,2176]{1,0:T(8,128)(2,1)S(1)}, u32[]{:S(2)}, u32[]{:S(2)}) collective-permute-start(bf16[16,2176]{1,0:T(8,128)(2,1)S(1)} %get-tuple-element.96.refs_0_), channel_id=1, source_target_pairs={{0,8},{8,16},{16,24},{24,28},{28,20},{20,12},{12,4},{4,0},{1,9},{9... | collective-permute-start | bytes 208904 | tf_op jit(solution)/shard_map/ppermute | solution.py:213
  29.8 8.4 %collective-permute-start.18 = (bf16[16,2176]{1,0:T(8,128)(2,1)S(1)}, bf16[16,2176]{1,0:T(8,128)(2,1)S(1)}, u32[]{:S(2)}, u32[]{:S(2)}) collective-permute-start(bf16[16,2176]{1,0:T(8,128)(2,1)S(1)} %get-tuple-element.96.refs_0_), channel_id=1, source_target_pairs={{0,4},{8,0},{16,8},{24,16},{28,24},{20,28},{12,20},{4,12},{1,5},{9... | collective-permute-start | bytes 208904 | tf_op jit(solution)/shard_map/ppermute | solution.py:213
  32.2 7.9 %collective-permute-start.12 = (bf16[16,2176]{1,0:T(8,128)(2,1)S(1)}, bf16[16,2176]{1,0:T(8,128)(2,1)S(1)}, u32[]{:S(2)}, u32[]{:S(2)}) collective-permute-start(bf16[16,2176]{1,0:T(8,128)(2,1)S(1)} %collective-permute-done.11.refs_4_), channel_id=1, source_target_pairs={{0,4},{8,0},{16,8},{24,16},{28,24},{20,28},{12,20},{4,12},{1,5},{9... | collective-permute-start | bytes 208904 | tf_op jit(solution)/shard_map/ppermute | solution.py:213
  34.2 6.0 %collective-permute-start.9 = (bf16[16,2176]{1,0:T(8,128)(2,1)S(1)}, bf16[16,2176]{1,0:T(8,128)(2,1)S(1)}, u32[]{:S(2)}, u32[]{:S(2)}) collective-permute-start(bf16[16,2176]{1,0:T(8,128)(2,1)S(1)} %collective-permute-done.8.after_ref.refs_1_), channel_id=1, source_target_pairs={{0,8},{8,16},{16,24},{24,28},{28,20},{20,12},{12,4},{4,0},{1,9},{9... | collective-permute-start | bytes 208904 | tf_op jit(solution)/shard_map/ppermute | solution.py:213
  38.1 4.9 %collective-permute-start.16 = (bf16[16,2176]{1,0:T(8,128)(2,1)S(1)}, bf16[16,2176]{1,0:T(8,128)(2,1)S(1)}, u32[]{:S(2)}, u32[]{:S(2)}) collective-permute-start(bf16[16,2176]{1,0:T(8,128)(2,1)S(1)} %collective-permute-done.15.refs_1_), channel_id=1, source_target_pairs={{0,8},{8,16},{16,24},{24,28},{28,20},{20,12},{12,4},{4,0},{1,9},{9... | collective-permute-start | bytes 208904 | tf_op jit(solution)/shard_map/ppermute | solution.py:213
  38.2 5.8 %collective-permute-start.19 = (bf16[16,2176]{1,0:T(8,128)(2,1)S(1)}, bf16[16,2176]{1,0:T(8,128)(2,1)S(1)}, u32[]{:S(2)}, u32[]{:S(2)}) collective-permute-start(bf16[16,2176]{1,0:T(8,128)(2,1)S(1)} %collective-permute-done.18.refs_4_), channel_id=1, source_target_pairs={{0,4},{8,0},{16,8},{24,16},{28,24},{20,28},{12,20},{4,12},{1,5},{9... | collective-permute-start | bytes 208904 | tf_op jit(solution)/shard_map/ppermute | solution.py:213
  40.2 6.0 %collective-permute-start.14 = (bf16[16,2176]{1,0:T(8,128)(2,1)S(1)}, bf16[16,2176]{1,0:T(8,128)(2,1)S(1)}, u32[]{:S(2)}, u32[]{:S(2)}) collective-permute-start(bf16[16,2176]{1,0:T(8,128)(2,1)S(1)} %broadcast_select_fusion.1), channel_id=1, source_target_pairs={{0,16},{1,13},{2,18},{3,15},{8,24},{9,5},{10,26},{11,7},{16,28},{1... | collective-permute-start | bytes 208904 | tf_op jit(solution)/shard_map/ppermute | solution.py:223
  41.0 7.0 %collective-permute-start.10 = (bf16[16,2176]{1,0:T(8,128)(2,1)S(1)}, bf16[16,2176]{1,0:T(8,128)(2,1)S(1)}, u32[]{:S(2)}, u32[]{:S(2)}) collective-permute-start(bf16[16,2176]{1,0:T(8,128)(2,1)S(1)} %collective-permute-done.9.refs_2_), channel_id=1, source_target_pairs={{0,8},{8,16},{16,24},{24,28},{28,20},{20,12},{12,4},{4,0},{1,9},{9... | collective-permute-start | bytes 208904 | tf_op jit(solution)/shard_map/ppermute | solution.py:213
  41.6 6.3 %collective-permute-start.13 = (bf16[16,2176]{1,0:T(8,128)(2,1)S(1)}, bf16[16,2176]{1,0:T(8,128)(2,1)S(1)}, u32[]{:S(2)}, u32[]{:S(2)}) collective-permute-start(bf16[16,2176]{1,0:T(8,128)(2,1)S(1)} %collective-permute-done.12.refs_5_), channel_id=1, source_target_pairs={{0,4},{8,0},{16,8},{24,16},{28,24},{20,28},{12,20},{4,12},{1,5},{9... | collective-permute-start | bytes 208904 | tf_op jit(solution)/shard_map/ppermute | solution.py:213
  44.1 8.8 %collective-permute-start.21 = (bf16[16,2176]{1,0:T(8,128)(2,1)S(1)}, bf16[16,2176]{1,0:T(8,128)(2,1)S(1)}, u32[]{:S(2)}, u32[]{:S(2)}) collective-permute-start(bf16[16,2176]{1,0:T(8,128)(2,1)S(1)} %broadcast_select_fusion), channel_id=1, source_target_pairs={{0,16},{1,13},{2,18},{3,15},{8,24},{9,5},{10,26},{11,7},{16,28},{1... | collective-permute-start | bytes 208904 | tf_op jit(solution)/shard_map/ppermute | solution.py:223
  44.8 8.6 %collective-permute-start.17 = (bf16[16,2176]{1,0:T(8,128)(2,1)S(1)}, bf16[16,2176]{1,0:T(8,128)(2,1)S(1)}, u32[]{:S(2)}, u32[]{:S(2)}) collective-permute-start(bf16[16,2176]{1,0:T(8,128)(2,1)S(1)} %collective-permute-done.16.refs_2_), channel_id=1, source_target_pairs={{0,8},{8,16},{16,24},{24,28},{28,20},{20,12},{12,4},{4,0},{1,9},{9... | collective-permute-start | bytes 208904 | tf_op jit(solution)/shard_map/ppermute | solution.py:213
  46.2 7.2 %collective-permute-start.20 = (bf16[16,2176]{1,0:T(8,128)(2,1)S(1)}, bf16[16,2176]{1,0:T(8,128)(2,1)S(1)}, u32[]{:S(2)}, u32[]{:S(2)}) collective-permute-start(bf16[16,2176]{1,0:T(8,128)(2,1)S(1)} %collective-permute-done.19.refs_5_), channel_id=1, source_target_pairs={{0,4},{8,0},{16,8},{24,16},{28,24},{20,28},{12,20},{4,12},{1,5},{9... | collective-permute-start | bytes 208904 | tf_op jit(solution)/shard_map/ppermute | solution.py:213
  50.5 8.9 %collective-permute-start.22 = (bf16[16,2048]{1,0:T(8,128)(2,1)S(1)}, bf16[16,2048]{1,0:T(8,128)(2,1)S(1)}, u32[]{:S(2)}, u32[]{:S(2)}) collective-permute-start(bf16[16,2048]{1,0:T(8,128)(2,1)S(1)} %get-tuple-element.73), channel_id=1, source_target_pairs={{0,8},{8,16},{16,24},{24,28},{28,20},{20,12},{12,4},{4,0},{1,9},{9... | collective-permute-start | bytes 196616 | tf_op jit(solution)/shard_map/ppermute | solution.py:213
  50.9 9.1 %collective-permute-start.23 = (bf16[16,2048]{1,0:T(8,128)(2,1)S(1)}, bf16[16,2048]{1,0:T(8,128)(2,1)S(1)}, u32[]{:S(2)}, u32[]{:S(2)}) collective-permute-start(bf16[16,2048]{1,0:T(8,128)(2,1)S(1)} %get-tuple-element.75), channel_id=1, source_target_pairs={{0,16},{1,13},{2,18},{3,15},{8,24},{9,5},{10,26},{11,7},{16,28},{1... | collective-permute-start | bytes 196616 | tf_op jit(solution)/shard_map/ppermute | solution.py:223
  52.8 7.2 %collective-permute-start.30 = (bf16[16,2048]{1,0:T(8,128)(2,1)S(1)}, bf16[16,2048]{1,0:T(8,128)(2,1)S(1)}, u32[]{:S(2)}, u32[]{:S(2)}) collective-permute-start(bf16[16,2048]{1,0:T(8,128)(2,1)S(1)} %get-tuple-element.81), channel_id=1, source_target_pairs={{0,4},{8,0},{16,8},{24,16},{28,24},{20,28},{12,20},{4,12},{1,5},{9... | collective-permute-start | bytes 196616 | tf_op jit(solution)/shard_map/ppermute | solution.py:213
  55.9 5.1 %collective-permute-start.26 = (bf16[16,2048]{1,0:T(8,128)(2,1)S(1)}, bf16[16,2048]{1,0:T(8,128)(2,1)S(1)}, u32[]{:S(2)}, u32[]{:S(2)}) collective-permute-start(bf16[16,2048]{1,0:T(8,128)(2,1)S(1)} %get-tuple-element.77), channel_id=1, source_target_pairs={{0,8},{8,16},{16,24},{24,28},{28,20},{20,12},{12,4},{4,0},{1,9},{9... | collective-permute-start | bytes 196616 | tf_op jit(solution)/shard_map/ppermute | solution.py:213
  57.4 6.6 %collective-permute-start.27 = (bf16[16,2048]{1,0:T(8,128)(2,1)S(1)}, bf16[16,2048]{1,0:T(8,128)(2,1)S(1)}, u32[]{:S(2)}, u32[]{:S(2)}) collective-permute-start(bf16[16,2048]{1,0:T(8,128)(2,1)S(1)} %get-tuple-element.79), channel_id=1, source_target_pairs={{0,16},{1,13},{2,18},{3,15},{8,24},{9,5},{10,26},{11,7},{16,28},{1... | collective-permute-start | bytes 196616 | tf_op jit(solution)/shard_map/ppermute | solution.py:223
  59.3 4.7 %collective-permute-start.33 = (bf16[16,2048]{1,0:T(8,128)(2,1)S(1)}, bf16[16,2048]{1,0:T(8,128)(2,1)S(1)}, u32[]{:S(2)}, u32[]{:S(2)}) collective-permute-start(bf16[16,2048]{1,0:T(8,128)(2,1)S(1)} %get-tuple-element.84), channel_id=1, source_target_pairs={{0,4},{8,0},{16,8},{24,16},{28,24},{20,28},{12,20},{4,12},{1,5},{9... | collective-permute-start | bytes 196616 | tf_op jit(solution)/shard_map/ppermute | solution.py:213
  60.0 6.3 %collective-permute-start.31 = (bf16[16,2048]{1,0:T(8,128)(2,1)S(1)}, bf16[16,2048]{1,0:T(8,128)(2,1)S(1)}, u32[]{:S(2)}, u32[]{:S(2)}) collective-permute-start(bf16[16,2048]{1,0:T(8,128)(2,1)S(1)} %get-tuple-element.107), channel_id=1, source_target_pairs={{0,4},{8,0},{16,8},{24,16},{28,24},{20,28},{12,20},{4,12},{1,5},{9... | collective-permute-start | bytes 196616 | tf_op jit(solution)/shard_map/ppermute | solution.py:213
  64.0 4.3 %collective-permute-start.34 = (bf16[16,2048]{1,0:T(8,128)(2,1)S(1)}, bf16[16,2048]{1,0:T(8,128)(2,1)S(1)}, u32[]{:S(2)}, u32[]{:S(2)}) collective-permute-start(bf16[16,2048]{1,0:T(8,128)(2,1)S(1)} %get-tuple-element.109), channel_id=1, source_target_pairs={{0,4},{8,0},{16,8},{24,16},{28,24},{20,28},{12,20},{4,12},{1,5},{9... | collective-permute-start | bytes 196616 | tf_op jit(solution)/shard_map/ppermute | solution.py:213
  64.4 4.3 %collective-permute-start.24 = (bf16[16,2048]{1,0:T(8,128)(2,1)S(1)}, bf16[16,2048]{1,0:T(8,128)(2,1)S(1)}, u32[]{:S(2)}, u32[]{:S(2)}) collective-permute-start(bf16[16,2048]{1,0:T(8,128)(2,1)S(1)} %get-tuple-element.108), channel_id=1, source_target_pairs={{0,8},{8,16},{16,24},{24,28},{28,20},{20,12},{12,4},{4,0},{1,9},{9... | collective-permute-start | bytes 196616 | tf_op jit(solution)/shard_map/ppermute | solution.py:213
  66.1 4.4 %collective-permute-start.28 = (bf16[16,2048]{1,0:T(8,128)(2,1)S(1)}, bf16[16,2048]{1,0:T(8,128)(2,1)S(1)}, u32[]{:S(2)}, u32[]{:S(2)}) collective-permute-start(bf16[16,2048]{1,0:T(8,128)(2,1)S(1)} %get-tuple-element.110), channel_id=1, source_target_pairs={{0,8},{8,16},{16,24},{24,28},{28,20},{20,12},{12,4},{4,0},{1,9},{9... | collective-permute-start | bytes 196616 | tf_op jit(solution)/shard_map/ppermute | solution.py:213
  66.4 4.8 %collective-permute-start.32 = (bf16[16,2048]{1,0:T(8,128)(2,1)S(1)}, bf16[16,2048]{1,0:T(8,128)(2,1)S(1)}, u32[]{:S(2)}, u32[]{:S(2)}) collective-permute-start(bf16[16,2048]{1,0:T(8,128)(2,1)S(1)} %add_convert_fusion.2), channel_id=1, source_target_pairs={{0,4},{8,0},{16,8},{24,16},{28,24},{20,28},{12,20},{4,12},{1,5},{9... | collective-permute-start | bytes 196616 | tf_op jit(solution)/shard_map/ppermute | solution.py:213
  68.4 4.3 %collective-permute-start.35 = (bf16[16,2048]{1,0:T(8,128)(2,1)S(1)}, bf16[16,2048]{1,0:T(8,128)(2,1)S(1)}, u32[]{:S(2)}, u32[]{:S(2)}) collective-permute-start(bf16[16,2048]{1,0:T(8,128)(2,1)S(1)} %add_convert_fusion), channel_id=1, source_target_pairs={{0,4},{8,0},{16,8},{24,16},{28,24},{20,28},{12,20},{4,12},{1,5},{9... | collective-permute-start | bytes 196616 | tf_op jit(solution)/shard_map/ppermute | solution.py:213
  68.7 4.3 %collective-permute-start.25 = (bf16[16,2048]{1,0:T(8,128)(2,1)S(1)}, bf16[16,2048]{1,0:T(8,128)(2,1)S(1)}, u32[]{:S(2)}, u32[]{:S(2)}) collective-permute-start(bf16[16,2048]{1,0:T(8,128)(2,1)S(1)} %add_convert_fusion.6), channel_id=1, source_target_pairs={{0,8},{8,16},{16,24},{24,28},{28,20},{20,12},{12,4},{4,0},{1,9},{9... | collective-permute-start | bytes 196616 | tf_op jit(solution)/shard_map/ppermute | solution.py:213
  70.6 4.3 %collective-permute-start.29 = (bf16[16,2048]{1,0:T(8,128)(2,1)S(1)}, bf16[16,2048]{1,0:T(8,128)(2,1)S(1)}, u32[]{:S(2)}, u32[]{:S(2)}) collective-permute-start(bf16[16,2048]{1,0:T(8,128)(2,1)S(1)} %add_convert_fusion.4), channel_id=1, source_target_pairs={{0,8},{8,16},{16,24},{24,28},{28,20},{20,12},{12,4},{4,0},{1,9},{9... | collective-permute-start | bytes 196616 | tf_op jit(solution)/shard_map/ppermute | solution.py:213
  75.0 3.4 %collective-permute-start.36 = (bf16[32,512]{1,0:T(8,128)(2,1)S(1)}, bf16[32,512]{1,0:T(8,128)(2,1)S(1)}, u32[]{:S(2)}, u32[]{:S(2)}) collective-permute-start(bf16[32,512]{1,0:T(8,128)(2,1)S(1)} %get-tuple-element.99), channel_id=1, source_target_pairs={{0,3},{1,2},{2,1},{3,0},{4,7},{5,6},{6,5},{7,4},{8,11},{9,10},{10,... | collective-permute-start | bytes 98312 | tf_op jit(solution)/shard_map/ppermute | solution.py:326
  75.1 4.3 %collective-permute-start.37 = (bf16[32,512]{1,0:T(8,128)(2,1)S(1)}, bf16[32,512]{1,0:T(8,128)(2,1)S(1)}, u32[]{:S(2)}, u32[]{:S(2)}) collective-permute-start(bf16[32,512]{1,0:T(8,128)(2,1)S(1)} %get-tuple-element.100), channel_id=1, source_target_pairs={{0,2},{1,3},{2,0},{3,1},{4,6},{5,7},{6,4},{7,5},{8,10},{9,11},{10,... | collective-permute-start | bytes 98312 | tf_op jit(solution)/shard_map/ppermute | solution.py:326
  76.1 3.2 %collective-permute-start.38 = (bf16[32,512]{1,0:T(8,128)(2,1)S(1)}, bf16[32,512]{1,0:T(8,128)(2,1)S(1)}, u32[]{:S(2)}, u32[]{:S(2)}) collective-permute-start(bf16[32,512]{1,0:T(8,128)(2,1)S(1)} %get-tuple-element.98), channel_id=1, source_target_pairs={{0,1},{1,0},{2,3},{3,2},{4,5},{5,4},{6,7},{7,6},{8,9},{9,8},{10,11... | collective-permute-start | bytes 98312 | tf_op jit(solution)/shard_map/ppermute | solution.py:326

commit v12 on v10

--- a/solution.py
+++ b/solution.py
@@ -148,9 +148,10 @@
     )
 
 
-def expert_kernel(blocks, scalars, gate_ref, up_ref, down_ref, *refs):
-    x_refs, out_refs = refs[:blocks], refs[blocks:2 * blocks]
-    rows_ref, act_ref, made_ref = refs[2 * blocks:]
+def expert_kernel(blocks, scalars, sign_ref, gate_ref, up_ref, down_ref, *refs):
+    x_refs, out_refs, done_ref = refs[:blocks], refs[blocks:2 * blocks], refs[2 * blocks]
+    rows_ref, act_ref, made_ref = refs[2 * blocks + 1:]
+    done_ref[...] = jnp.zeros_like(done_ref)
     model, units = gate_ref.shape
     spans, packs = [], []
     first = 0
@@ -182,13 +183,13 @@
         out_ref[...] = made_ref[span, :]
 
 
-def run_expert(scalars, blocks, weights_gate, weights_up, weights_out):
+def run_expert(scalars, sign, blocks, weights_gate, weights_up, weights_out):
     units, model = weights_out.shape
     total = sum(b.shape[0] for b in blocks)
-    return call(
+    *made, sign = call(
         functools.partial(expert_kernel, len(blocks)),
-        [shape((b.shape[0], model), BF16) for b in blocks],
-        [scalars, weights_gate, weights_up, weights_out, *blocks],
+        [shape((b.shape[0], model), BF16) for b in blocks] + [shape((8, HEAD), F32)],
+        [scalars, sign, weights_gate, weights_up, weights_out, *blocks],
         scratch=[
             pltpu.VMEM((total, model), BF16),
             pltpu.VMEM((total, units), BF16),
@@ -197,6 +198,7 @@
         flops=6 * total * model * units,
         limit=24 << 20,
     )
+    return made, sign
 
 
 def ring_order(count):
@@ -223,18 +225,21 @@
         return lax.ppermute(rows, ("seq", "exp"), pairs)
 
     ahead, behind = [block], [block]
-    for distance in range(1, far):
+    for distance in range(1, far - 1):
         came, went = hop(ahead[-1], 1), hop(behind[-1], -1)
-        if distance == 1:
-            weights_out, _ = load_near(scalars, expert_out, 0, came)
+        if distance == far - 2:
+            weights_out, sign = load_near(scalars, expert_out, 0, ahead[-1])
+            came, went, sign = lax.optimization_barrier((came, went, sign))
         ahead.append(came)
         behind.append(went)
+    last = hop(ahead[-1], 1), hop(behind[-1], -1)
     turned = turns[0]
-    farthest = far_hop(jnp.where(turned, behind[-2], ahead[-2]))
-    made = run_expert(
-        scalars, ahead + behind[1:] + [farthest], weights_gate, weights_up, weights_out
-    )
-    own, to_back, to_front, farthest = made[0], made[1:far], made[far:-1], made[-1]
+    farthest = far_hop(jnp.where(turned, behind[-1], ahead[-1]))
+    weights = weights_gate, weights_up, weights_out
+    (own, *near), sign = run_expert(scalars, sign, ahead + behind[1:], *weights)
+    *last, farthest, sign = lax.optimization_barrier((*last, farthest, sign))
+    (back, front, farthest), _ = run_expert(scalars, sign, [*last, farthest], *weights)
+    to_back, to_front = near[:far - 2] + [back], near[far - 2:] + [front]
     going, coming = hop(to_front[-1], 1), hop(to_back[-1], -1)
     early = far_hop(farthest)
     for distance in range(far - 2, 0, -1):

time: 78.2 us -> 75.9 us (0.971)
  waiting for transfers between devices: 28.2 us -> 25.1 us
  Pallas kernels: 16.6 us -> 18 us
    ppermute x12, starting transfers between devices: 13.7 us -> 11.4 us  [hop(): lax.ppermute(rows, 'seq', [(order[p], order[(p + steps) % count]) for p i...]
    ppermute x2, starting transfers between devices: 3.23 us -> 5.33 us  [far_hop(): return lax.ppermute(rows, ('seq', 'exp'), pairs)]
    ppermute x2, waiting for transfers between devices: 6.66 us -> 4.84 us  [far_hop(): return lax.ppermute(rows, ('seq', 'exp'), pairs)]
    pallas_call x7 -> x8, Pallas kernels: 16.6 us -> 18 us  [call(): pl.pallas_call(kernel, out_shape=outs, in_specs=[SCALAR if i == 0 or i in...]
    ppermute x12, waiting for transfers between devices: 14.8 us -> 13.9 us  [hop(): lax.ppermute(rows, 'seq', [(order[p], order[(p + steps) % count]) for p i...]
  transfers between devices with their start and end apart: 25 -> 25, of which waited for: 15 -> 16; matrix products, arithmetic and copies ran while one was open for 2% -> 2% of each run, Pallas kernels for 13% -> 16%
where the time goes in v12:
time: 75.9 us; the launch traced here: 75.8 us
  starting transfers between devices  29.9 us (39%)
  waiting for transfers between devices  25.1 us (33%)
  Pallas kernels  18 us (24%)
  other arithmetic  1.44 us (2%)
  local copies, waits for them, and re-layouts  1.09 us (1%)
    pallas_call x8, Pallas kernels, call(): pl.pallas_call(kernel, out_shape=outs, in_specs=[SCALAR if i == 0 or i in...  18 us
    ppermute x12, waiting for transfers between devices, hop(): lax.ppermute(rows, 'seq', [(order[p], order[(p + steps) % count]) for p i...  13.9 us
    ppermute x12, starting transfers between devices, hop(): lax.ppermute(rows, 'seq', [(order[p], order[(p + steps) % count]) for p i...  11.4 us
    ppermute x2, starting transfers between devices, far_hop(): return lax.ppermute(rows, ('seq', 'exp'), pairs)  5.33 us
    ppermute x3, starting transfers between devices, prior_states(): lax.ppermute(total, 'seq', [(i, i ^ 2 * distance) for i in range(count)])  4.84 us
    ppermute x2, waiting for transfers between devices, far_hop(): return lax.ppermute(rows, ('seq', 'exp'), pairs)  4.84 us
    ppermute x6, waiting for transfers between devices, exchange(): lax.ppermute(pieces[j], 'exp', [(i, i ^ j) for i in range(parts)])  4.28 us
    ppermute x6, starting transfers between devices, exchange(): lax.ppermute(pieces[j], 'exp', [(i, i ^ j) for i in range(parts)])  3.84 us
  transfers between devices with their start and end apart: 25, of which 16 were waited for; matrix products, arithmetic and copies ran while one was open for 2% of the time, Pallas kernels for 16%

profile of v12, /device:TPU:0, one launch (start us, length us, event | category | flops | bytes accessed | tf_op | source)
XLA Modules:
  0.0 75.8 jit_solution(12650883459143154064)
XLA Ops:
  0.0 0.1 stack.24.scalars
  0.1 1.8 %shard_map.100 = (bf16[128,256]{1,0:T(8,128)(2,1)S(1)}, bf16[128,256]{1,0:T(8,128)(2,1)S(1)}, bf16[128,512]{1,0:T(8,128)(2,1)S(1)}, bf16[128,512]{1,0:T(8,128)(2...) custom-call(s32[7]{0:T(128)S(1)} %stack.24.scalars, ...), custom_call_target="tpu_custom_call" | custom-call | flops 16777216 | bytes 1188892 | tf_op jit(solution)/shard_map/pallas_call | solution.py:24
  1.9 3.0 %collective-permute-start = (bf16[128,256]{1,0:T(8,128)(2,1)S(1)}, bf16[128,256]{1,0:T(8,128)(2,1)S(1)}, u32[]{:S(2)}, u32[]{:S(2)}) collective-permute-start(bf16[128,256]{1,0:T(8,128)(2,1)S(1)} %get-tuple-element.51), channel_id=1, source_target_pairs={{0,4},{4,0},{8,12},{12,8},{16,20},{20,16},{24,28},{28,24},{1,5},{5... | collective-permute-start | bytes 196616 | tf_op jit(solution)/shard_map/ppermute | solution.py:378
  4.9 0.1 constant_dynamic-slice_fusion
  5.0 0.9 %shard_map.101.within_ref = f32[128,512]{1,0:T(8,128)S(1)} custom-call(s32[7]{0:T(128)S(1)} %stack.24.scalars, bf16[128,512]{1,0:T(8,128)(2,1)S(1)} %get-tuple-element.52.keys, bf16[128,512]{1,0:T(8,128)(2,1)S(1)} %get-tuple-element.53.values, bf16[128,512]{1,0:T(8,128)(2,1)S(1)} %get-tuple-element.54.queries), custom_call_target="tpu_custom_call" | custom-call | flops 50331648 | bytes 655388 | tf_op jit(solution)/shard_map/pallas_call | solution.py:24
  5.9 0.8 %constant_dynamic-slice_fusion.1 = s32[32,8]{0,1:T(8,128)S(1)} fusion(s32[128,8]{0,1:T(8,128)} %param.16, u32[]{:T(128)S(6)} %convert_element_type.90), kind=kLoop, calls=%fused_computation.55 | loop fusion | bytes 2052 | tf_op jit(solution)/shard_map/dynamic_slice | solution.py:408
  6.7 0.5 collective-permute-done
  7.2 4.2 %collective-permute-start.3 = (bf16[128,256]{1,0:T(8,128)(2,1)S(1)}, bf16[128,256]{1,0:T(8,128)(2,1)S(1)}, u32[]{:S(2)}, u32[]{:S(2)}) collective-permute-start(bf16[128,256]{1,0:T(8,128)(2,1)S(1)} %fusion.6.after_ref), channel_id=1, source_target_pairs={{0,24},{4,28},{8,16},{12,20},{16,8},{20,12},{24,0},{28,4},{1,25},{... | collective-permute-start | bytes 196616 | tf_op jit(solution)/shard_map/ppermute | solution.py:318
  11.4 0.0 collective-permute-start.2
  11.4 0.6 collective-permute-start.1
  12.0 0.1 copy.16
  12.1 0.1 copy.15
  12.2 2.8 %shard_map.102 = (bf16[2048,1024]{1,0:T(8,128)(2,1)S(1)}, f32[8,128]{1,0:T(8,128)S(1)}) custom-call(s32[7]{0:T(128)S(1)} %stack.24.scalars, bf16[2,2048,1024]{2,1,0:T(8,128)(2,1)} %bitcast.16, bf16[128,256]{1,0:T(8,128)(2,1)S(1)} %fusion.6.after_ref), custom_call_target="tpu_custom_call" | custom-call | bytes 12652572 | tf_op jit(solution)/shard_map/pallas_call | solution.py:24
  15.0 0.0 collective-permute-done.3
  15.0 1.6 %collective-permute-done.2 = bf16[128,256]{1,0:T(8,128)(2,1)S(1)} collective-permute-done((bf16[128,256]{1,0:T(8,128)(2,1)S(1)}, bf16[128,256]{1,0:T(8,128)(2,1)S(1)}, u32[]{:S(2)}, u32[]{:S(2)}) %collective-permute-start.2) | collective-permute-done | bytes 65568 | tf_op jit(solution)/shard_map/ppermute | solution.py:318
  16.6 0.0 collective-permute-done.1
  16.6 0.1 fusion.5
  16.6 1.6 %collective-permute-start.4 = (bf16[128,256]{1,0:T(8,128)(2,1)S(1)}, bf16[128,256]{1,0:T(8,128)(2,1)S(1)}, u32[]{:S(2)}, u32[]{:S(2)}) collective-permute-start(bf16[128,256]{1,0:T(8,128)(2,1)S(1)} %get-tuple-element.61.after_ref), channel_id=1, source_target_pairs={{0,4},{4,0},{8,12},{12,8},{16,20},{20,16},{24,28},{28,24},{1,5},{5... | collective-permute-start | bytes 196616 | tf_op jit(solution)/shard_map/ppermute | solution.py:394
  18.2 2.8 %shard_map.103 = (bf16[2048,1024]{1,0:T(8,128)(2,1)S(1)}, f32[8,128]{1,0:T(8,128)S(1)}) custom-call(s32[7]{0:T(128)S(1)} %stack.24.scalars, bf16[2,2048,1024]{2,1,0:T(8,128)(2,1)} %bitcast.17, bf16[128,256]{1,0:T(8,128)(2,1)S(1)} %get-tuple-element.61.after_ref), custom_call_target="tpu_custom_call" | custom-call | bytes 12652572 | tf_op jit(solution)/shard_map/pallas_call | solution.py:24
  21.0 0.9 %shard_map.104 = (bf16[32,512]{1,0:T(8,128)(2,1)S(1)}, bf16[32,512]{1,0:T(8,128)(2,1)S(1)}, bf16[32,512]{1,0:T(8,128)(2,1)S(1)}, bf16[32,512]{1,0:T(8,128)(2,1)S(1)}) custom-call(s32[7]{0:T(128)S(1)} %stack.24.scalars, f32[128,512]{1,0:T(8,128)S(1)} %shard_map.101.within_ref, bf16[128,512]{1,0:T(8,128)(2,1)S(1)} %get-tuple-element.54.queries, ...), custom_call_target="tpu_custom_call" | custom-call | flops 33554432 | bytes 862236 | tf_op jit(solution)/shard_map/pallas_call | solution.py:24
  21.9 0.1 collective-permute-start.5
  22.0 1.6 %collective-permute-start.6 = (bf16[32,512]{1,0:T(8,128)(2,1)S(1)}, bf16[32,512]{1,0:T(8,128)(2,1)S(1)}, u32[]{:S(2)}, u32[]{:S(2)}) collective-permute-start(bf16[32,512]{1,0:T(8,128)(2,1)S(1)} %get-tuple-element.65), channel_id=1, source_target_pairs={{0,2},{1,3},{2,0},{3,1},{4,6},{5,7},{6,4},{7,5},{8,10},{9,11},{10,... | collective-permute-start | bytes 98312 | tf_op jit(solution)/shard_map/ppermute | solution.py:328
  23.5 0.3 collective-permute-start.7
  23.8 0.1 fusion.10
  23.9 1.7 %collective-permute-done.5 = bf16[32,512]{1,0:T(8,128)(2,1)S(1)} collective-permute-done((bf16[32,512]{1,0:T(8,128)(2,1)S(1)}, bf16[32,512]{1,0:T(8,128)(2,1)S(1)}, u32[]{:S(2)}, u32[]{:S(2)}) %collective-permute-start.5) | collective-permute-done | bytes 32800 | tf_op jit(solution)/shard_map/ppermute | solution.py:328
  25.6 0.4 collective-permute-done.6
  26.0 0.1 fusion
  26.2 0.1 fusion.2
  26.3 0.6 collective-permute-start.8
  26.9 1.5 %collective-permute-start.10 = (bf16[32,2176]{1,0:T(8,128)(2,1)S(1)}, bf16[32,2176]{1,0:T(8,128)(2,1)S(1)}, u32[]{:S(2)}, u32[]{:S(2)}) collective-permute-start(bf16[32,2176]{1,0:T(8,128)(2,1)S(1)} %pad_maximum_fusion.refs_0_), channel_id=1, source_target_pairs={{0,4},{8,0},{16,8},{24,16},{28,24},{20,28},{12,20},{4,12},{1,5},{9... | collective-permute-start | bytes 417800 | tf_op jit(solution)/shard_map/ppermute | solution.py:215
  28.4 3.9 %collective-permute-done.8.after_ref.refs_1_ = bf16[32,2176]{1,0:T(8,128)(2,1)S(1)} collective-permute-done((bf16[32,2176]{1,0:T(8,128)(2,1)S(1)}, bf16[32,2176]{1,0:T(8,128)(2,1)S(1)}, u32[]{:S(2)}, u32[]{:S(2)}) %collective-permute-start.8) | collective-permute-done | bytes 139296 | tf_op jit(solution)/shard_map/ppermute | solution.py:215
  32.3 0.5 collective-permute-start.9
  32.8 0.0 collective-permute-done.10.refs_3_
  32.8 1.5 %collective-permute-start.11 = (bf16[32,2176]{1,0:T(8,128)(2,1)S(1)}, bf16[32,2176]{1,0:T(8,128)(2,1)S(1)}, u32[]{:S(2)}, u32[]{:S(2)}) collective-permute-start(bf16[32,2176]{1,0:T(8,128)(2,1)S(1)} %collective-permute-done.10.refs_3_), channel_id=1, source_target_pairs={{0,4},{8,0},{16,8},{24,16},{28,24},{20,28},{12,20},{4,12},{1,5},{9... | collective-permute-start | bytes 417800 | tf_op jit(solution)/shard_map/ppermute | solution.py:215
  34.3 2.8 %shard_map.105 = (bf16[1024,2048]{1,0:T(8,128)(2,1)S(1)}, f32[8,128]{1,0:T(8,128)S(1)}) custom-call(s32[7]{0:T(128)S(1)} %stack.24.scalars, bf16[1,1024,2048]{2,1,0:T(8,128)(2,1)} %source.1, bf16[32,2176]{1,0:T(8,128)(2,1)S(1)} %collective-permute-done.8.after_ref.refs_1_), custom_call_target="tpu_custom_call" | custom-call | bytes 8531996 | tf_op jit(solution)/shard_map/pallas_call | solution.py:24
  37.1 0.3 collective-permute-done.9.refs_2_
  37.4 0.5 collective-permute-done.11.refs_4_
  37.9 2.0 %collective-permute-start.12 = (bf16[32,2176]{1,0:T(8,128)(2,1)S(1)}, bf16[32,2176]{1,0:T(8,128)(2,1)S(1)}, u32[]{:S(2)}, u32[]{:S(2)}) collective-permute-start(bf16[32,2176]{1,0:T(8,128)(2,1)S(1)} %collective-permute-done.9.refs_2_), channel_id=1, source_target_pairs={{0,8},{8,16},{16,24},{24,28},{28,20},{20,12},{12,4},{4,0},{1,9},{9... | collective-permute-start | bytes 417800 | tf_op jit(solution)/shard_map/ppermute | solution.py:215
  39.9 0.1 collective-permute-start.13
  40.0 2.2 %collective-permute-start.14 = (bf16[32,2176]{1,0:T(8,128)(2,1)S(1)}, bf16[32,2176]{1,0:T(8,128)(2,1)S(1)}, u32[]{:S(2)}, u32[]{:S(2)}) collective-permute-start(bf16[32,2176]{1,0:T(8,128)(2,1)S(1)} %broadcast_select_fusion), channel_id=1, source_target_pairs={{0,16},{1,13},{2,18},{3,15},{8,24},{9,5},{10,26},{11,7},{16,28},{1... | collective-permute-start | bytes 417800 | tf_op jit(solution)/shard_map/ppermute | solution.py:225
  42.2 2.9 %shard_map.106 = (bf16[32,2048]{1,0:T(8,128)(2,1)S(1)}, bf16[32,2048]{1,0:T(8,128)(2,1)S(1)}, bf16[32,2048]{1,0:T(8,128)(2,1)S(1)}, bf16[32,2048]{1,0:T(8,128)(2...) custom-call(s32[7]{0:T(128)S(1)} %stack.24.scalars, f32[8,128]{1,0:T(8,128)S(1)} %get-tuple-element.70.sign_ref, ...), custom_call_target="tpu_custom_call" | custom-call | flops 2013265920 | bytes 13942812 | tf_op jit(solution)/shard_map/pallas_call | solution.py:24
  45.1 1.3 %collective-permute-done.13.refs_1_ = bf16[32,2176]{1,0:T(8,128)(2,1)S(1)} collective-permute-done((bf16[32,2176]{1,0:T(8,128)(2,1)S(1)}, bf16[32,2176]{1,0:T(8,128)(2,1)S(1)}, u32[]{:S(2)}, u32[]{:S(2)}) %collective-permute-start.13) | collective-permute-done | bytes 139296 | tf_op jit(solution)/shard_map/ppermute | solution.py:215
  46.3 0.7 collective-permute-done.14.refs_2_
  47.0 3.2 %shard_map.107 = (bf16[32,2048]{1,0:T(8,128)(2,1)S(1)}, bf16[32,2048]{1,0:T(8,128)(2,1)S(1)}, bf16[32,2048]{1,0:T(8,128)(2,1)S(1)}, f32[8,128]{1,0:T(8,128)}) custom-call(s32[7]{0:T(128)S(1)} %stack.24.scalars, f32[8,128]{1,0:T(8,128)S(1)} %get-tuple-element.78.sign_ref, bf16[2048,1024]{1,0:T(8,128)(2,1)S(1)} %get-tuple-element.71.gate_ref, ...), custom_call_target="tpu_custom_call" | custom-call | flops 1207959552 | bytes 13402140 | tf_op jit(solution)/shard_map/pallas_call | solution.py:24
  50.2 1.0 %collective-permute-start.15 = (bf16[32,2048]{1,0:T(8,128)(2,1)S(1)}, bf16[32,2048]{1,0:T(8,128)(2,1)S(1)}, u32[]{:S(2)}, u32[]{:S(2)}) collective-permute-start(bf16[32,2048]{1,0:T(8,128)(2,1)S(1)} %get-tuple-element.82), channel_id=1, source_target_pairs={{0,8},{8,16},{16,24},{24,28},{28,20},{20,12},{12,4},{4,0},{1,9},{9... | collective-permute-start | bytes 393224 | tf_op jit(solution)/shard_map/ppermute | solution.py:215
  51.2 3.1 %collective-permute-start.16 = (bf16[32,2048]{1,0:T(8,128)(2,1)S(1)}, bf16[32,2048]{1,0:T(8,128)(2,1)S(1)}, u32[]{:S(2)}, u32[]{:S(2)}) collective-permute-start(bf16[32,2048]{1,0:T(8,128)(2,1)S(1)} %get-tuple-element.84), channel_id=1, source_target_pairs={{0,16},{1,13},{2,18},{3,15},{8,24},{9,5},{10,26},{11,7},{16,28},{1... | collective-permute-start | bytes 393224 | tf_op jit(solution)/shard_map/ppermute | solution.py:225
  54.3 0.9 %collective-permute-done.15 = bf16[32,2048]{1,0:T(8,128)(2,1)S(1)} collective-permute-done((bf16[32,2048]{1,0:T(8,128)(2,1)S(1)}, bf16[32,2048]{1,0:T(8,128)(2,1)S(1)}, u32[]{:S(2)}, u32[]{:S(2)}) %collective-permute-start.15) | collective-permute-done | bytes 131104 | tf_op jit(solution)/shard_map/ppermute | solution.py:215
  55.2 4.2 %collective-permute-done.16 = bf16[32,2048]{1,0:T(8,128)(2,1)S(1)} collective-permute-done((bf16[32,2048]{1,0:T(8,128)(2,1)S(1)}, bf16[32,2048]{1,0:T(8,128)(2,1)S(1)}, u32[]{:S(2)}, u32[]{:S(2)}) %collective-permute-start.16) | collective-permute-done | bytes 131104 | tf_op jit(solution)/shard_map/ppermute | solution.py:225
  59.3 0.1 add_convert_fusion.3
  59.4 0.1 collective-permute-start.20
  59.5 2.0 %collective-permute-start.17 = (bf16[32,2048]{1,0:T(8,128)(2,1)S(1)}, bf16[32,2048]{1,0:T(8,128)(2,1)S(1)}, u32[]{:S(2)}, u32[]{:S(2)}) collective-permute-start(bf16[32,2048]{1,0:T(8,128)(2,1)S(1)} %get-tuple-element.103), channel_id=1, source_target_pairs={{0,8},{8,16},{16,24},{24,28},{28,20},{20,12},{12,4},{4,0},{1,9},{9... | collective-permute-start | bytes 393224 | tf_op jit(solution)/shard_map/ppermute | solution.py:215
  61.5 4.1 %collective-permute-done.20 = bf16[32,2048]{1,0:T(8,128)(2,1)S(1)} collective-permute-done((bf16[32,2048]{1,0:T(8,128)(2,1)S(1)}, bf16[32,2048]{1,0:T(8,128)(2,1)S(1)}, u32[]{:S(2)}, u32[]{:S(2)}) %collective-permute-start.20) | collective-permute-done | bytes 131104 | tf_op jit(solution)/shard_map/ppermute | solution.py:215
  65.7 0.1 collective-permute-start.21
  65.8 0.0 collective-permute-done.17
  65.8 2.1 %collective-permute-start.18 = (bf16[32,2048]{1,0:T(8,128)(2,1)S(1)}, bf16[32,2048]{1,0:T(8,128)(2,1)S(1)}, u32[]{:S(2)}, u32[]{:S(2)}) collective-permute-start(bf16[32,2048]{1,0:T(8,128)(2,1)S(1)} %add_convert_fusion.2), channel_id=1, source_target_pairs={{0,8},{8,16},{16,24},{24,28},{28,20},{20,12},{12,4},{4,0},{1,9},{9... | collective-permute-start | bytes 393224 | tf_op jit(solution)/shard_map/ppermute | solution.py:215
  68.0 2.8 %collective-permute-done.21 = bf16[32,2048]{1,0:T(8,128)(2,1)S(1)} collective-permute-done((bf16[32,2048]{1,0:T(8,128)(2,1)S(1)}, bf16[32,2048]{1,0:T(8,128)(2,1)S(1)}, u32[]{:S(2)}, u32[]{:S(2)}) %collective-permute-start.21) | collective-permute-done | bytes 131104 | tf_op jit(solution)/shard_map/ppermute | solution.py:215
  70.7 0.1 collective-permute-done.18
  70.8 0.1 fusion.3
  71.0 0.1 collective-permute-start.22
  71.0 1.6 %collective-permute-start.23 = (bf16[32,512]{1,0:T(8,128)(2,1)S(1)}, bf16[32,512]{1,0:T(8,128)(2,1)S(1)}, u32[]{:S(2)}, u32[]{:S(2)}) collective-permute-start(bf16[32,512]{1,0:T(8,128)(2,1)S(1)} %get-tuple-element.100), channel_id=1, source_target_pairs={{0,2},{1,3},{2,0},{3,1},{4,6},{5,7},{6,4},{7,5},{8,10},{9,11},{10,... | collective-permute-start | bytes 98312 | tf_op jit(solution)/shard_map/ppermute | solution.py:328
  72.7 0.2 collective-permute-start.24
  72.9 1.7 %collective-permute-done.22 = bf16[32,512]{1,0:T(8,128)(2,1)S(1)} collective-permute-done((bf16[32,512]{1,0:T(8,128)(2,1)S(1)}, bf16[32,512]{1,0:T(8,128)(2,1)S(1)}, u32[]{:S(2)}, u32[]{:S(2)}) %collective-permute-start.22) | collective-permute-done | bytes 32800 | tf_op jit(solution)/shard_map/ppermute | solution.py:328
  74.6 0.5 collective-permute-done.23
  75.1 0.7 pad_maximum_fusion.2
  (23 shorter events, 0.2 us)
Async XLA Ops:
  0.0 4.9 %copy-start = (f32[128,8]{0,1:T(8,128)S(1)}, f32[128,8]{0,1:T(8,128)}, u32[]{:S(2)}) copy-start(f32[128,8]{0,1:T(8,128)} %param.17) | copy-start | bytes 12292
  1.9 5.3 %collective-permute-start = (bf16[128,256]{1,0:T(8,128)(2,1)S(1)}, bf16[128,256]{1,0:T(8,128)(2,1)S(1)}, u32[]{:S(2)}, u32[]{:S(2)}) collective-permute-start(bf16[128,256]{1,0:T(8,128)(2,1)S(1)} %get-tuple-element.51), channel_id=1, source_target_pairs={{0,4},{4,0},{8,12},{12,8},{16,20},{20,16},{24,28},{28,24},{1,5},{5... | collective-permute-start | bytes 196616 | tf_op jit(solution)/shard_map/ppermute | solution.py:378
  7.2 7.8 %collective-permute-start.3 = (bf16[128,256]{1,0:T(8,128)(2,1)S(1)}, bf16[128,256]{1,0:T(8,128)(2,1)S(1)}, u32[]{:S(2)}, u32[]{:S(2)}) collective-permute-start(bf16[128,256]{1,0:T(8,128)(2,1)S(1)} %fusion.6.after_ref), channel_id=1, source_target_pairs={{0,24},{4,28},{8,16},{12,20},{16,8},{20,12},{24,0},{28,4},{1,25},{... | collective-permute-start | bytes 196616 | tf_op jit(solution)/shard_map/ppermute | solution.py:318
  11.4 5.2 %collective-permute-start.2 = (bf16[128,256]{1,0:T(8,128)(2,1)S(1)}, bf16[128,256]{1,0:T(8,128)(2,1)S(1)}, u32[]{:S(2)}, u32[]{:S(2)}) collective-permute-start(bf16[128,256]{1,0:T(8,128)(2,1)S(1)} %fusion.6.after_ref), channel_id=1, source_target_pairs={{0,16},{4,20},{8,24},{12,28},{16,0},{20,4},{24,8},{28,12},{1,17},{... | collective-permute-start | bytes 196616 | tf_op jit(solution)/shard_map/ppermute | solution.py:318
  11.4 5.2 %collective-permute-start.1 = (bf16[128,256]{1,0:T(8,128)(2,1)S(1)}, bf16[128,256]{1,0:T(8,128)(2,1)S(1)}, u32[]{:S(2)}, u32[]{:S(2)}) collective-permute-start(bf16[128,256]{1,0:T(8,128)(2,1)S(1)} %fusion.6.after_ref), channel_id=1, source_target_pairs={{0,8},{4,12},{8,0},{12,4},{16,24},{20,28},{24,16},{28,20},{1,9},{5... | collective-permute-start | bytes 196616 | tf_op jit(solution)/shard_map/ppermute | solution.py:318
  16.6 4.3 %collective-permute-start.4 = (bf16[128,256]{1,0:T(8,128)(2,1)S(1)}, bf16[128,256]{1,0:T(8,128)(2,1)S(1)}, u32[]{:S(2)}, u32[]{:S(2)}) collective-permute-start(bf16[128,256]{1,0:T(8,128)(2,1)S(1)} %get-tuple-element.61.after_ref), channel_id=1, source_target_pairs={{0,4},{4,0},{8,12},{12,8},{16,20},{20,16},{24,28},{28,24},{1,5},{5... | collective-permute-start | bytes 196616 | tf_op jit(solution)/shard_map/ppermute | solution.py:394
  18.2 8.0 %copy-start.1 = (f32[2048]{0:T(1024)S(1)}, f32[2048]{0:T(1024)}, u32[]{:S(2)}) copy-start(f32[2048]{0:T(1024)} %param.15) | copy-start | bytes 24580
  21.9 3.7 %collective-permute-start.5 = (bf16[32,512]{1,0:T(8,128)(2,1)S(1)}, bf16[32,512]{1,0:T(8,128)(2,1)S(1)}, u32[]{:S(2)}, u32[]{:S(2)}) collective-permute-start(bf16[32,512]{1,0:T(8,128)(2,1)S(1)} %get-tuple-element.64), channel_id=1, source_target_pairs={{0,3},{1,2},{2,1},{3,0},{4,7},{5,6},{6,5},{7,4},{8,11},{9,10},{10,... | collective-permute-start | bytes 98312 | tf_op jit(solution)/shard_map/ppermute | solution.py:328
  22.0 4.0 %collective-permute-start.6 = (bf16[32,512]{1,0:T(8,128)(2,1)S(1)}, bf16[32,512]{1,0:T(8,128)(2,1)S(1)}, u32[]{:S(2)}, u32[]{:S(2)}) collective-permute-start(bf16[32,512]{1,0:T(8,128)(2,1)S(1)} %get-tuple-element.65), channel_id=1, source_target_pairs={{0,2},{1,3},{2,0},{3,1},{4,6},{5,7},{6,4},{7,5},{8,10},{9,11},{10,... | collective-permute-start | bytes 98312 | tf_op jit(solution)/shard_map/ppermute | solution.py:328
  23.5 2.4 %collective-permute-start.7 = (bf16[32,512]{1,0:T(8,128)(2,1)S(1)}, bf16[32,512]{1,0:T(8,128)(2,1)S(1)}, u32[]{:S(2)}, u32[]{:S(2)}) collective-permute-start(bf16[32,512]{1,0:T(8,128)(2,1)S(1)} %get-tuple-element.66), channel_id=1, source_target_pairs={{0,1},{1,0},{2,3},{3,2},{4,5},{5,4},{6,7},{7,6},{8,9},{9,8},{10,11... | collective-permute-start | bytes 98312 | tf_op jit(solution)/shard_map/ppermute | solution.py:328
  26.3 6.0 %collective-permute-start.8 = (bf16[32,2176]{1,0:T(8,128)(2,1)S(1)}, bf16[32,2176]{1,0:T(8,128)(2,1)S(1)}, u32[]{:S(2)}, u32[]{:S(2)}) collective-permute-start(bf16[32,2176]{1,0:T(8,128)(2,1)S(1)} %pad_maximum_fusion.refs_0_), channel_id=1, source_target_pairs={{0,8},{8,16},{16,24},{24,28},{28,20},{20,12},{12,4},{4,0},{1,9},{9... | collective-permute-start | bytes 417800 | tf_op jit(solution)/shard_map/ppermute | solution.py:215
  26.9 5.9 %collective-permute-start.10 = (bf16[32,2176]{1,0:T(8,128)(2,1)S(1)}, bf16[32,2176]{1,0:T(8,128)(2,1)S(1)}, u32[]{:S(2)}, u32[]{:S(2)}) collective-permute-start(bf16[32,2176]{1,0:T(8,128)(2,1)S(1)} %pad_maximum_fusion.refs_0_), channel_id=1, source_target_pairs={{0,4},{8,0},{16,8},{24,16},{28,24},{20,28},{12,20},{4,12},{1,5},{9... | collective-permute-start | bytes 417800 | tf_op jit(solution)/shard_map/ppermute | solution.py:215
  32.3 5.1 %collective-permute-start.9 = (bf16[32,2176]{1,0:T(8,128)(2,1)S(1)}, bf16[32,2176]{1,0:T(8,128)(2,1)S(1)}, u32[]{:S(2)}, u32[]{:S(2)}) collective-permute-start(bf16[32,2176]{1,0:T(8,128)(2,1)S(1)} %collective-permute-done.8.after_ref.refs_1_), channel_id=1, source_target_pairs={{0,8},{8,16},{16,24},{24,28},{28,20},{20,12},{12,4},{4,0},{1,9},{9... | collective-permute-start | bytes 417800 | tf_op jit(solution)/shard_map/ppermute | solution.py:215
  32.8 5.1 %collective-permute-start.11 = (bf16[32,2176]{1,0:T(8,128)(2,1)S(1)}, bf16[32,2176]{1,0:T(8,128)(2,1)S(1)}, u32[]{:S(2)}, u32[]{:S(2)}) collective-permute-start(bf16[32,2176]{1,0:T(8,128)(2,1)S(1)} %collective-permute-done.10.refs_3_), channel_id=1, source_target_pairs={{0,4},{8,0},{16,8},{24,16},{28,24},{20,28},{12,20},{4,12},{1,5},{9... | collective-permute-start | bytes 417800 | tf_op jit(solution)/shard_map/ppermute | solution.py:215
  37.9 7.1 %collective-permute-start.12 = (bf16[32,2176]{1,0:T(8,128)(2,1)S(1)}, bf16[32,2176]{1,0:T(8,128)(2,1)S(1)}, u32[]{:S(2)}, u32[]{:S(2)}) collective-permute-start(bf16[32,2176]{1,0:T(8,128)(2,1)S(1)} %collective-permute-done.9.refs_2_), channel_id=1, source_target_pairs={{0,8},{8,16},{16,24},{24,28},{28,20},{20,12},{12,4},{4,0},{1,9},{9... | collective-permute-start | bytes 417800 | tf_op jit(solution)/shard_map/ppermute | solution.py:215
  39.9 6.4 %collective-permute-start.13 = (bf16[32,2176]{1,0:T(8,128)(2,1)S(1)}, bf16[32,2176]{1,0:T(8,128)(2,1)S(1)}, u32[]{:S(2)}, u32[]{:S(2)}) collective-permute-start(bf16[32,2176]{1,0:T(8,128)(2,1)S(1)} %collective-permute-done.11.refs_4_), channel_id=1, source_target_pairs={{0,4},{8,0},{16,8},{24,16},{28,24},{20,28},{12,20},{4,12},{1,5},{9... | collective-permute-start | bytes 417800 | tf_op jit(solution)/shard_map/ppermute | solution.py:215
  40.0 7.0 %collective-permute-start.14 = (bf16[32,2176]{1,0:T(8,128)(2,1)S(1)}, bf16[32,2176]{1,0:T(8,128)(2,1)S(1)}, u32[]{:S(2)}, u32[]{:S(2)}) collective-permute-start(bf16[32,2176]{1,0:T(8,128)(2,1)S(1)} %broadcast_select_fusion), channel_id=1, source_target_pairs={{0,16},{1,13},{2,18},{3,15},{8,24},{9,5},{10,26},{11,7},{16,28},{1... | collective-permute-start | bytes 417800 | tf_op jit(solution)/shard_map/ppermute | solution.py:225
  50.2 5.0 %collective-permute-start.15 = (bf16[32,2048]{1,0:T(8,128)(2,1)S(1)}, bf16[32,2048]{1,0:T(8,128)(2,1)S(1)}, u32[]{:S(2)}, u32[]{:S(2)}) collective-permute-start(bf16[32,2048]{1,0:T(8,128)(2,1)S(1)} %get-tuple-element.82), channel_id=1, source_target_pairs={{0,8},{8,16},{16,24},{24,28},{28,20},{20,12},{12,4},{4,0},{1,9},{9... | collective-permute-start | bytes 393224 | tf_op jit(solution)/shard_map/ppermute | solution.py:215
  51.2 8.2 %collective-permute-start.16 = (bf16[32,2048]{1,0:T(8,128)(2,1)S(1)}, bf16[32,2048]{1,0:T(8,128)(2,1)S(1)}, u32[]{:S(2)}, u32[]{:S(2)}) collective-permute-start(bf16[32,2048]{1,0:T(8,128)(2,1)S(1)} %get-tuple-element.84), channel_id=1, source_target_pairs={{0,16},{1,13},{2,18},{3,15},{8,24},{9,5},{10,26},{11,7},{16,28},{1... | collective-permute-start | bytes 393224 | tf_op jit(solution)/shard_map/ppermute | solution.py:225
  54.3 5.0 %collective-permute-start.19 = (bf16[32,2048]{1,0:T(8,128)(2,1)S(1)}, bf16[32,2048]{1,0:T(8,128)(2,1)S(1)}, u32[]{:S(2)}, u32[]{:S(2)}) collective-permute-start(bf16[32,2048]{1,0:T(8,128)(2,1)S(1)} %get-tuple-element.86), channel_id=1, source_target_pairs={{0,4},{8,0},{16,8},{24,16},{28,24},{20,28},{12,20},{4,12},{1,5},{9... | collective-permute-start | bytes 393224 | tf_op jit(solution)/shard_map/ppermute | solution.py:215
  59.4 6.2 %collective-permute-start.20 = (bf16[32,2048]{1,0:T(8,128)(2,1)S(1)}, bf16[32,2048]{1,0:T(8,128)(2,1)S(1)}, u32[]{:S(2)}, u32[]{:S(2)}) collective-permute-start(bf16[32,2048]{1,0:T(8,128)(2,1)S(1)} %get-tuple-element.104), channel_id=1, source_target_pairs={{0,4},{8,0},{16,8},{24,16},{28,24},{20,28},{12,20},{4,12},{1,5},{9... | collective-permute-start | bytes 393224 | tf_op jit(solution)/shard_map/ppermute | solution.py:215
  59.5 6.3 %collective-permute-start.17 = (bf16[32,2048]{1,0:T(8,128)(2,1)S(1)}, bf16[32,2048]{1,0:T(8,128)(2,1)S(1)}, u32[]{:S(2)}, u32[]{:S(2)}) collective-permute-start(bf16[32,2048]{1,0:T(8,128)(2,1)S(1)} %get-tuple-element.103), channel_id=1, source_target_pairs={{0,8},{8,16},{16,24},{24,28},{28,20},{20,12},{12,4},{4,0},{1,9},{9... | collective-permute-start | bytes 393224 | tf_op jit(solution)/shard_map/ppermute | solution.py:215
  65.7 5.0 %collective-permute-start.21 = (bf16[32,2048]{1,0:T(8,128)(2,1)S(1)}, bf16[32,2048]{1,0:T(8,128)(2,1)S(1)}, u32[]{:S(2)}, u32[]{:S(2)}) collective-permute-start(bf16[32,2048]{1,0:T(8,128)(2,1)S(1)} %add_convert_fusion), channel_id=1, source_target_pairs={{0,4},{8,0},{16,8},{24,16},{28,24},{20,28},{12,20},{4,12},{1,5},{9... | collective-permute-start | bytes 393224 | tf_op jit(solution)/shard_map/ppermute | solution.py:215
  65.8 5.0 %collective-permute-start.18 = (bf16[32,2048]{1,0:T(8,128)(2,1)S(1)}, bf16[32,2048]{1,0:T(8,128)(2,1)S(1)}, u32[]{:S(2)}, u32[]{:S(2)}) collective-permute-start(bf16[32,2048]{1,0:T(8,128)(2,1)S(1)} %add_convert_fusion.2), channel_id=1, source_target_pairs={{0,8},{8,16},{16,24},{24,28},{28,20},{20,12},{12,4},{4,0},{1,9},{9... | collective-permute-start | bytes 393224 | tf_op jit(solution)/shard_map/ppermute | solution.py:215
  71.0 3.6 %collective-permute-start.22 = (bf16[32,512]{1,0:T(8,128)(2,1)S(1)}, bf16[32,512]{1,0:T(8,128)(2,1)S(1)}, u32[]{:S(2)}, u32[]{:S(2)}) collective-permute-start(bf16[32,512]{1,0:T(8,128)(2,1)S(1)} %get-tuple-element.99), channel_id=1, source_target_pairs={{0,3},{1,2},{2,1},{3,0},{4,7},{5,6},{6,5},{7,4},{8,11},{9,10},{10,... | collective-permute-start | bytes 98312 | tf_op jit(solution)/shard_map/ppermute | solution.py:328
  71.0 4.0 %collective-permute-start.23 = (bf16[32,512]{1,0:T(8,128)(2,1)S(1)}, bf16[32,512]{1,0:T(8,128)(2,1)S(1)}, u32[]{:S(2)}, u32[]{:S(2)}) collective-permute-start(bf16[32,512]{1,0:T(8,128)(2,1)S(1)} %get-tuple-element.100), channel_id=1, source_target_pairs={{0,2},{1,3},{2,0},{3,1},{4,6},{5,7},{6,4},{7,5},{8,10},{9,11},{10,... | collective-permute-start | bytes 98312 | tf_op jit(solution)/shard_map/ppermute | solution.py:328
  72.7 2.4 %collective-permute-start.24 = (bf16[32,512]{1,0:T(8,128)(2,1)S(1)}, bf16[32,512]{1,0:T(8,128)(2,1)S(1)}, u32[]{:S(2)}, u32[]{:S(2)}) collective-permute-start(bf16[32,512]{1,0:T(8,128)(2,1)S(1)} %get-tuple-element.98), channel_id=1, source_target_pairs={{0,1},{1,0},{2,3},{3,2},{4,5},{5,4},{6,7},{7,6},{8,9},{9,8},{10,11... | collective-permute-start | bytes 98312 | tf_op jit(solution)/shard_map/ppermute | solution.py:328

commit v13 on v12

--- a/solution.py
+++ b/solution.py
@@ -160,6 +160,10 @@
         rows_ref[spans[-1], :] = ref[:, :model]
         packs.append(ref[:, model:].astype(F32))
         first += ref.shape[0]
+    spare = rows_ref.shape[0] - first
+    if spare:
+        rows_ref[first:, :] = jnp.zeros((spare, model), BF16)
+        packs.append(jnp.zeros((spare, packs[0].shape[1]), F32))
     pack = jnp.concatenate(packs)
     lane = lax.broadcasted_iota(jnp.int32, pack.shape, 1)
     chosen = (lane == scalars[3]) | (lane == scalars[3] + scalars[2])
@@ -185,7 +189,7 @@
 
 def run_expert(scalars, sign, blocks, weights_gate, weights_up, weights_out):
     units, model = weights_out.shape
-    total = sum(b.shape[0] for b in blocks)
+    total = -(-sum(b.shape[0] for b in blocks) // HEAD) * HEAD
     *made, sign = call(
         functools.partial(expert_kernel, len(blocks)),
         [shape((b.shape[0], model), BF16) for b in blocks] + [shape((8, HEAD), F32)],
@@ -205,26 +209,18 @@
     return list(range(0, count, 2)) + list(range(1, count, 2))[::-1]
 
 
-def dense_experts(block, scalars, turns, weights_gate, weights_up, expert_out):
+def dense_experts(block, scalars, weights_gate, weights_up, expert_out):
     count = lax.axis_size("seq")
     order = ring_order(count)
     far = count // 2
-    parts = lax.axis_size("exp")
 
     def hop(rows, steps):
         return lax.ppermute(
             rows, "seq", [(order[p], order[(p + steps) % count]) for p in range(count)]
         )
 
-    def far_hop(rows):
-        pairs = []
-        for p in range(count):
-            for e in range(parts):
-                target = order[(p + (2 if e % 2 == 0 else -2)) % count]
-                pairs.append((order[p] * parts + e, target * parts + e))
-        return lax.ppermute(rows, ("seq", "exp"), pairs)
-
     ahead, behind = [block], [block]
+    farthest = hop(block, far)
     for distance in range(1, far - 1):
         came, went = hop(ahead[-1], 1), hop(behind[-1], -1)
         if distance == far - 2:
@@ -233,26 +229,18 @@
         ahead.append(came)
         behind.append(went)
     last = hop(ahead[-1], 1), hop(behind[-1], -1)
-    turned = turns[0]
-    farthest = far_hop(jnp.where(turned, behind[-1], ahead[-1]))
     weights = weights_gate, weights_up, weights_out
     (own, *near), sign = run_expert(scalars, sign, ahead + behind[1:], *weights)
     *last, farthest, sign = lax.optimization_barrier((*last, farthest, sign))
     (back, front, farthest), _ = run_expert(scalars, sign, [*last, farthest], *weights)
     to_back, to_front = near[:far - 2] + [back], near[far - 2:] + [front]
     going, coming = hop(to_front[-1], 1), hop(to_back[-1], -1)
-    early = far_hop(farthest)
-    for distance in range(far - 2, 0, -1):
-        front, back = to_front[distance - 1], to_back[distance - 1]
-        if distance == far - 2:
-            nothing = jnp.zeros_like(early)
-            going = add_rows(going, front, jnp.where(turned, nothing, early))
-            coming = add_rows(coming, back, jnp.where(turned, early, nothing))
-        else:
-            going = add_rows(going, front)
-            coming = add_rows(coming, back)
-        going, coming = hop(going, 1), hop(coming, -1)
-    return own, going, coming
+    straight = hop(farthest, far)
+    for distance in range(far - 2, -1, -1):
+        if distance == 0:
+            return own, going, coming, straight
+        going = hop(add_rows(going, to_front[distance - 1]), 1)
+        coming = hop(add_rows(coming, to_back[distance - 1]), -1)
 
 
 def slot_ids(block_routes, expert_count, capacity):
@@ -430,7 +418,7 @@
     if dense:
         block = jnp.concatenate([normed, pack], axis=1)
         terms = dense_experts(
-            block, scalars, turns, weights_gate, weights_up, expert_out
+            block, scalars, weights_gate, weights_up, expert_out
         )
     else:
         mixed = routed_experts(normed, my_routes, my_gates, expert_in, expert_out)

time: 75.9 us -> 75.4 us (level)
  waiting for transfers between devices: 25.1 us -> 22.7 us
  starting transfers between devices: 29.9 us -> 30.9 us
  Pallas kernels: 18 us -> 18.9 us
    ppermute x12 -> x14, starting transfers between devices: 11.4 us -> 17.7 us  [hop(): lax.ppermute(rows, 'seq', [(order[p], order[(p + steps) % count]) for p i...]
    ppermute x2 -> x0, starting transfers between devices: 5.33 us -> none  [far_hop(): return lax.ppermute(rows, ('seq', 'exp'), pairs)]
    ppermute x2 -> x0, waiting for transfers between devices: 4.84 us -> none  [far_hop(): return lax.ppermute(rows, ('seq', 'exp'), pairs)]
    ppermute x3, waiting for transfers between devices: 1.6 us -> 3.11 us  [prior_states(): lax.ppermute(total, 'seq', [(i, i ^ 2 * distance) for i in range(count)])]
    pallas_call x8, Pallas kernels: 18 us -> 18.9 us  [call(): pl.pallas_call(kernel, out_shape=outs, in_specs=[SCALAR if i == 0 or i in...]
    ppermute x12 -> x14, waiting for transfers between devices: 13.9 us -> 14.5 us  [hop(): lax.ppermute(rows, 'seq', [(order[p], order[(p + steps) % count]) for p i...]
  transfers between devices with their start and end apart: 25 -> 25, of which waited for: 16 -> 16; matrix products, arithmetic and copies ran while one was open for 2% -> 2% of each run, Pallas kernels for 16% -> 18%
where the time goes in v13:
time: 75.4 us; the launch traced here: 75.2 us
  starting transfers between devices  30.9 us (41%)
  waiting for transfers between devices  22.7 us (30%)
  Pallas kernels  18.9 us (25%)
  other arithmetic  1.4 us (2%)
  local copies, waits for them, and re-layouts  1.09 us (1%)
    pallas_call x8, Pallas kernels, call(): pl.pallas_call(kernel, out_shape=outs, in_specs=[SCALAR if i == 0 or i in...  18.9 us
    ppermute x14, starting transfers between devices, hop(): lax.ppermute(rows, 'seq', [(order[p], order[(p + steps) % count]) for p i...  17.7 us
    ppermute x14, waiting for transfers between devices, hop(): lax.ppermute(rows, 'seq', [(order[p], order[(p + steps) % count]) for p i...  14.5 us
    ppermute x3, starting transfers between devices, prior_states(): lax.ppermute(total, 'seq', [(i, i ^ 2 * distance) for i in range(count)])  4.76 us
    ppermute x6, waiting for transfers between devices, exchange(): lax.ppermute(pieces[j], 'exp', [(i, i ^ j) for i in range(parts)])  4.57 us
    ppermute x6, starting transfers between devices, exchange(): lax.ppermute(pieces[j], 'exp', [(i, i ^ j) for i in range(parts)])  3.84 us
    ppermute x3, waiting for transfers between devices, prior_states(): lax.ppermute(total, 'seq', [(i, i ^ 2 * distance) for i in range(count)])  3.11 us
    ppermute x1, starting transfers between devices, per_device(): partner = lax.ppermute(given, 'seq', swap)  3.01 us
  transfers between devices with their start and end apart: 25, of which 16 were waited for; matrix products, arithmetic and copies ran while one was open for 2% of the time, Pallas kernels for 18%

profile of v13, /device:TPU:0, one launch (start us, length us, event | category | flops | bytes accessed | tf_op | source)
XLA Modules:
  0.0 75.2 jit_solution(10257675932065608304)
XLA Ops:
  0.0 0.1 stack.24.scalars
  0.1 1.8 %shard_map.100 = (bf16[128,256]{1,0:T(8,128)(2,1)S(1)}, bf16[128,256]{1,0:T(8,128)(2,1)S(1)}, bf16[128,512]{1,0:T(8,128)(2,1)S(1)}, bf16[128,512]{1,0:T(8,128)(2...) custom-call(s32[7]{0:T(128)S(1)} %stack.24.scalars, ...), custom_call_target="tpu_custom_call" | custom-call | flops 16777216 | bytes 1188892 | tf_op jit(solution)/shard_map/pallas_call | solution.py:24
  1.9 3.0 %collective-permute-start = (bf16[128,256]{1,0:T(8,128)(2,1)S(1)}, bf16[128,256]{1,0:T(8,128)(2,1)S(1)}, u32[]{:S(2)}, u32[]{:S(2)}) collective-permute-start(bf16[128,256]{1,0:T(8,128)(2,1)S(1)} %get-tuple-element.51), channel_id=1, source_target_pairs={{0,4},{4,0},{8,12},{12,8},{16,20},{20,16},{24,28},{28,24},{1,5},{5... | collective-permute-start | bytes 196616 | tf_op jit(solution)/shard_map/ppermute | solution.py:366
  4.9 0.1 constant_dynamic-slice_fusion
  5.0 0.9 %shard_map.101.within_ref = f32[128,512]{1,0:T(8,128)S(1)} custom-call(s32[7]{0:T(128)S(1)} %stack.24.scalars, bf16[128,512]{1,0:T(8,128)(2,1)S(1)} %get-tuple-element.52.keys, bf16[128,512]{1,0:T(8,128)(2,1)S(1)} %get-tuple-element.53.values, bf16[128,512]{1,0:T(8,128)(2,1)S(1)} %get-tuple-element.54.queries), custom_call_target="tpu_custom_call" | custom-call | flops 50331648 | bytes 655388 | tf_op jit(solution)/shard_map/pallas_call | solution.py:24
  5.9 0.8 %constant_dynamic-slice_fusion.1 = s32[32,8]{0,1:T(8,128)S(1)} fusion(s32[128,8]{0,1:T(8,128)} %param.16, u32[]{:T(128)S(6)} %convert_element_type.87), kind=kLoop, calls=%fused_computation.54 | loop fusion | bytes 2052 | tf_op jit(solution)/shard_map/dynamic_slice | solution.py:396
  6.7 0.5 collective-permute-done
  7.2 2.2 %collective-permute-start.1 = (bf16[128,256]{1,0:T(8,128)(2,1)S(1)}, bf16[128,256]{1,0:T(8,128)(2,1)S(1)}, u32[]{:S(2)}, u32[]{:S(2)}) collective-permute-start(bf16[128,256]{1,0:T(8,128)(2,1)S(1)} %fusion.6.after_ref), channel_id=1, source_target_pairs={{0,8},{4,12},{8,0},{12,4},{16,24},{20,28},{24,16},{28,20},{1,9},{5... | collective-permute-start | bytes 196616 | tf_op jit(solution)/shard_map/ppermute | solution.py:306
  9.3 2.6 %collective-permute-start.2 = (bf16[128,256]{1,0:T(8,128)(2,1)S(1)}, bf16[128,256]{1,0:T(8,128)(2,1)S(1)}, u32[]{:S(2)}, u32[]{:S(2)}) collective-permute-start(bf16[128,256]{1,0:T(8,128)(2,1)S(1)} %fusion.6.after_ref), channel_id=1, source_target_pairs={{0,16},{4,20},{8,24},{12,28},{16,0},{20,4},{24,8},{28,12},{1,17},{... | collective-permute-start | bytes 196616 | tf_op jit(solution)/shard_map/ppermute | solution.py:306
  12.0 0.1 copy.16
  12.0 0.1 copy.15
  12.1 2.8 %shard_map.102 = (bf16[2048,1024]{1,0:T(8,128)(2,1)S(1)}, f32[8,128]{1,0:T(8,128)S(1)}) custom-call(s32[7]{0:T(128)S(1)} %stack.24.scalars, bf16[2,2048,1024]{2,1,0:T(8,128)(2,1)} %bitcast.16, bf16[128,256]{1,0:T(8,128)(2,1)S(1)} %fusion.6.after_ref), custom_call_target="tpu_custom_call" | custom-call | bytes 12652572 | tf_op jit(solution)/shard_map/pallas_call | solution.py:24
  14.9 0.0 collective-permute-done.1
  14.9 1.0 %collective-permute-done.2 = bf16[128,256]{1,0:T(8,128)(2,1)S(1)} collective-permute-done((bf16[128,256]{1,0:T(8,128)(2,1)S(1)}, bf16[128,256]{1,0:T(8,128)(2,1)S(1)}, u32[]{:S(2)}, u32[]{:S(2)}) %collective-permute-start.2) | collective-permute-done | bytes 65568 | tf_op jit(solution)/shard_map/ppermute | solution.py:306
  15.9 2.1 %collective-permute-done.3 = bf16[128,256]{1,0:T(8,128)(2,1)S(1)} collective-permute-done((bf16[128,256]{1,0:T(8,128)(2,1)S(1)}, bf16[128,256]{1,0:T(8,128)(2,1)S(1)}, u32[]{:S(2)}, u32[]{:S(2)}) %collective-permute-start.3) | collective-permute-done | bytes 65568 | tf_op jit(solution)/shard_map/ppermute | solution.py:306
  18.0 0.1 fusion.5
  18.1 1.6 %collective-permute-start.4 = (bf16[128,256]{1,0:T(8,128)(2,1)S(1)}, bf16[128,256]{1,0:T(8,128)(2,1)S(1)}, u32[]{:S(2)}, u32[]{:S(2)}) collective-permute-start(bf16[128,256]{1,0:T(8,128)(2,1)S(1)} %get-tuple-element.61.after_ref), channel_id=1, source_target_pairs={{0,4},{4,0},{8,12},{12,8},{16,20},{20,16},{24,28},{28,24},{1,5},{5... | collective-permute-start | bytes 196616 | tf_op jit(solution)/shard_map/ppermute | solution.py:382
  19.6 2.8 %shard_map.103 = (bf16[2048,1024]{1,0:T(8,128)(2,1)S(1)}, f32[8,128]{1,0:T(8,128)S(1)}) custom-call(s32[7]{0:T(128)S(1)} %stack.24.scalars, bf16[2,2048,1024]{2,1,0:T(8,128)(2,1)} %bitcast.17, bf16[128,256]{1,0:T(8,128)(2,1)S(1)} %get-tuple-element.61.after_ref), custom_call_target="tpu_custom_call" | custom-call | bytes 12652572 | tf_op jit(solution)/shard_map/pallas_call | solution.py:24
  22.4 0.9 %shard_map.104 = (bf16[32,512]{1,0:T(8,128)(2,1)S(1)}, bf16[32,512]{1,0:T(8,128)(2,1)S(1)}, bf16[32,512]{1,0:T(8,128)(2,1)S(1)}, bf16[32,512]{1,0:T(8,128)(2,1)S(1)}) custom-call(s32[7]{0:T(128)S(1)} %stack.24.scalars, f32[128,512]{1,0:T(8,128)S(1)} %shard_map.101.within_ref, bf16[128,512]{1,0:T(8,128)(2,1)S(1)} %get-tuple-element.54.queries, ...), custom_call_target="tpu_custom_call" | custom-call | flops 33554432 | bytes 862236 | tf_op jit(solution)/shard_map/pallas_call | solution.py:24
  23.3 0.1 collective-permute-start.5
  23.4 1.6 %collective-permute-start.6 = (bf16[32,512]{1,0:T(8,128)(2,1)S(1)}, bf16[32,512]{1,0:T(8,128)(2,1)S(1)}, u32[]{:S(2)}, u32[]{:S(2)}) collective-permute-start(bf16[32,512]{1,0:T(8,128)(2,1)S(1)} %get-tuple-element.65), channel_id=1, source_target_pairs={{0,2},{1,3},{2,0},{3,1},{4,6},{5,7},{6,4},{7,5},{8,10},{9,11},{10,... | collective-permute-start | bytes 98312 | tf_op jit(solution)/shard_map/ppermute | solution.py:316
  25.0 0.3 collective-permute-start.7
  25.2 0.1 fusion.10
  25.3 1.7 %collective-permute-done.5 = bf16[32,512]{1,0:T(8,128)(2,1)S(1)} collective-permute-done((bf16[32,512]{1,0:T(8,128)(2,1)S(1)}, bf16[32,512]{1,0:T(8,128)(2,1)S(1)}, u32[]{:S(2)}, u32[]{:S(2)}) %collective-permute-start.5) | collective-permute-done | bytes 32800 | tf_op jit(solution)/shard_map/ppermute | solution.py:316
  27.0 0.4 collective-permute-done.6
  27.4 0.0 collective-permute-done.7
  27.5 0.1 fusion
  27.6 0.1 fusion.2
  27.7 1.5 %collective-permute-start.10 = (bf16[32,2176]{1,0:T(8,128)(2,1)S(1)}, bf16[32,2176]{1,0:T(8,128)(2,1)S(1)}, u32[]{:S(2)}, u32[]{:S(2)}) collective-permute-start(bf16[32,2176]{1,0:T(8,128)(2,1)S(1)} %pad_maximum_fusion.refs_0_), channel_id=1, source_target_pairs={{0,4},{8,0},{16,8},{24,16},{28,24},{20,28},{12,20},{4,12},{1,5},{9... | collective-permute-start | bytes 417800 | tf_op jit(solution)/shard_map/ppermute | solution.py:218
  29.3 0.5 collective-permute-start.8
  29.8 3.9 %collective-permute-done.10.refs_3_ = bf16[32,2176]{1,0:T(8,128)(2,1)S(1)} collective-permute-done((bf16[32,2176]{1,0:T(8,128)(2,1)S(1)}, bf16[32,2176]{1,0:T(8,128)(2,1)S(1)}, u32[]{:S(2)}, u32[]{:S(2)}) %collective-permute-start.10) | collective-permute-done | bytes 139296 | tf_op jit(solution)/shard_map/ppermute | solution.py:218
  33.7 1.5 %collective-permute-start.11 = (bf16[32,2176]{1,0:T(8,128)(2,1)S(1)}, bf16[32,2176]{1,0:T(8,128)(2,1)S(1)}, u32[]{:S(2)}, u32[]{:S(2)}) collective-permute-start(bf16[32,2176]{1,0:T(8,128)(2,1)S(1)} %collective-permute-done.10.refs_3_), channel_id=1, source_target_pairs={{0,4},{8,0},{16,8},{24,16},{28,24},{20,28},{12,20},{4,12},{1,5},{9... | collective-permute-start | bytes 417800 | tf_op jit(solution)/shard_map/ppermute | solution.py:218
  35.2 0.6 collective-permute-start.9
  35.8 1.8 %collective-permute-start.14 = (bf16[32,2176]{1,0:T(8,128)(2,1)S(1)}, bf16[32,2176]{1,0:T(8,128)(2,1)S(1)}, u32[]{:S(2)}, u32[]{:S(2)}) collective-permute-start(bf16[32,2176]{1,0:T(8,128)(2,1)S(1)} %pad_maximum_fusion.refs_0_), channel_id=1, source_target_pairs={{0,28},{8,20},{16,12},{24,4},{28,0},{20,8},{12,16},{4,24},{1,29},{... | collective-permute-start | bytes 417800 | tf_op jit(solution)/shard_map/ppermute | solution.py:218
  37.6 2.8 %shard_map.105 = (bf16[1024,2048]{1,0:T(8,128)(2,1)S(1)}, f32[8,128]{1,0:T(8,128)S(1)}) custom-call(s32[7]{0:T(128)S(1)} %stack.24.scalars, bf16[1,1024,2048]{2,1,0:T(8,128)(2,1)} %source.1, bf16[32,2176]{1,0:T(8,128)(2,1)S(1)} %collective-permute-done.8.after_ref.refs_1_), custom_call_target="tpu_custom_call" | custom-call | bytes 8531996 | tf_op jit(solution)/shard_map/pallas_call | solution.py:24
  40.4 0.0 collective-permute-done.11.refs_4_
  40.4 0.1 collective-permute-done.9.refs_2_
  40.5 1.7 %collective-permute-start.12 = (bf16[32,2176]{1,0:T(8,128)(2,1)S(1)}, bf16[32,2176]{1,0:T(8,128)(2,1)S(1)}, u32[]{:S(2)}, u32[]{:S(2)}) collective-permute-start(bf16[32,2176]{1,0:T(8,128)(2,1)S(1)} %collective-permute-done.9.refs_2_), channel_id=1, source_target_pairs={{0,8},{8,16},{16,24},{24,28},{28,20},{20,12},{12,4},{4,0},{1,9},{9... | collective-permute-start | bytes 417800 | tf_op jit(solution)/shard_map/ppermute | solution.py:218
  42.2 0.4 collective-permute-start.13
  42.5 4.1 %shard_map.106 = (bf16[32,2048]{1,0:T(8,128)(2,1)S(1)}, bf16[32,2048]{1,0:T(8,128)(2,1)S(1)}, bf16[32,2048]{1,0:T(8,128)(2,1)S(1)}, bf16[32,2048]{1,0:T(8,128)(2...) custom-call(s32[7]{0:T(128)S(1)} %stack.24.scalars, f32[8,128]{1,0:T(8,128)S(1)} %get-tuple-element.70.sign_ref, ...), custom_call_target="tpu_custom_call" | custom-call | flops 3221225472 | bytes 13942812 | tf_op jit(solution)/shard_map/pallas_call | solution.py:24
  46.6 0.0 collective-permute-done.14.refs_2_
  46.6 0.6 collective-permute-done.13.refs_1_
  47.2 2.9 %shard_map.107 = (bf16[32,2048]{1,0:T(8,128)(2,1)S(1)}, bf16[32,2048]{1,0:T(8,128)(2,1)S(1)}, bf16[32,2048]{1,0:T(8,128)(2,1)S(1)}, f32[8,128]{1,0:T(8,128)}) custom-call(s32[7]{0:T(128)S(1)} %stack.24.scalars, f32[8,128]{1,0:T(8,128)S(1)} %get-tuple-element.78.sign_ref, bf16[2048,1024]{1,0:T(8,128)(2,1)S(1)} %get-tuple-element.71.gate_ref, ...), custom_call_target="tpu_custom_call" | custom-call | flops 1610612736 | bytes 13402140 | tf_op jit(solution)/shard_map/pallas_call | solution.py:24
  50.1 1.7 %collective-permute-start.15 = (bf16[32,2048]{1,0:T(8,128)(2,1)S(1)}, bf16[32,2048]{1,0:T(8,128)(2,1)S(1)}, u32[]{:S(2)}, u32[]{:S(2)}) collective-permute-start(bf16[32,2048]{1,0:T(8,128)(2,1)S(1)} %get-tuple-element.82), channel_id=1, source_target_pairs={{0,8},{8,16},{16,24},{24,28},{28,20},{20,12},{12,4},{4,0},{1,9},{9... | collective-permute-start | bytes 393224 | tf_op jit(solution)/shard_map/ppermute | solution.py:218
  51.8 1.3 %collective-permute-start.18 = (bf16[32,2048]{1,0:T(8,128)(2,1)S(1)}, bf16[32,2048]{1,0:T(8,128)(2,1)S(1)}, u32[]{:S(2)}, u32[]{:S(2)}) collective-permute-start(bf16[32,2048]{1,0:T(8,128)(2,1)S(1)} %get-tuple-element.85), channel_id=1, source_target_pairs={{0,4},{8,0},{16,8},{24,16},{28,24},{20,28},{12,20},{4,12},{1,5},{9... | collective-permute-start | bytes 393224 | tf_op jit(solution)/shard_map/ppermute | solution.py:218
  53.2 3.3 %collective-permute-start.21 = (bf16[32,2048]{1,0:T(8,128)(2,1)S(1)}, bf16[32,2048]{1,0:T(8,128)(2,1)S(1)}, u32[]{:S(2)}, u32[]{:S(2)}) collective-permute-start(bf16[32,2048]{1,0:T(8,128)(2,1)S(1)} %get-tuple-element.88), channel_id=1, source_target_pairs={{0,28},{8,20},{16,12},{24,4},{28,0},{20,8},{12,16},{4,24},{1,29},{... | collective-permute-start | bytes 393224 | tf_op jit(solution)/shard_map/ppermute | solution.py:218
  56.5 1.7 %collective-permute-done.15 = bf16[32,2048]{1,0:T(8,128)(2,1)S(1)} collective-permute-done((bf16[32,2048]{1,0:T(8,128)(2,1)S(1)}, bf16[32,2048]{1,0:T(8,128)(2,1)S(1)}, u32[]{:S(2)}, u32[]{:S(2)}) %collective-permute-start.15) | collective-permute-done | bytes 131104 | tf_op jit(solution)/shard_map/ppermute | solution.py:218
  58.2 0.1 collective-permute-start.16
  58.3 1.1 %collective-permute-done.18 = bf16[32,2048]{1,0:T(8,128)(2,1)S(1)} collective-permute-done((bf16[32,2048]{1,0:T(8,128)(2,1)S(1)}, bf16[32,2048]{1,0:T(8,128)(2,1)S(1)}, u32[]{:S(2)}, u32[]{:S(2)}) %collective-permute-start.18) | collective-permute-done | bytes 131104 | tf_op jit(solution)/shard_map/ppermute | solution.py:218
  59.4 1.5 %collective-permute-start.19 = (bf16[32,2048]{1,0:T(8,128)(2,1)S(1)}, bf16[32,2048]{1,0:T(8,128)(2,1)S(1)}, u32[]{:S(2)}, u32[]{:S(2)}) collective-permute-start(bf16[32,2048]{1,0:T(8,128)(2,1)S(1)} %add_convert_fusion.1), channel_id=1, source_target_pairs={{0,4},{8,0},{16,8},{24,16},{28,24},{20,28},{12,20},{4,12},{1,5},{9... | collective-permute-start | bytes 393224 | tf_op jit(solution)/shard_map/ppermute | solution.py:218
  60.9 3.6 %collective-permute-done.16 = bf16[32,2048]{1,0:T(8,128)(2,1)S(1)} collective-permute-done((bf16[32,2048]{1,0:T(8,128)(2,1)S(1)}, bf16[32,2048]{1,0:T(8,128)(2,1)S(1)}, u32[]{:S(2)}, u32[]{:S(2)}) %collective-permute-start.16) | collective-permute-done | bytes 131104 | tf_op jit(solution)/shard_map/ppermute | solution.py:218
  64.5 0.1 collective-permute-start.17
  64.6 0.3 collective-permute-done.19
  65.0 1.8 %collective-permute-start.20 = (bf16[32,2048]{1,0:T(8,128)(2,1)S(1)}, bf16[32,2048]{1,0:T(8,128)(2,1)S(1)}, u32[]{:S(2)}, u32[]{:S(2)}) collective-permute-start(bf16[32,2048]{1,0:T(8,128)(2,1)S(1)} %add_convert_fusion), channel_id=1, source_target_pairs={{0,4},{8,0},{16,8},{24,16},{28,24},{20,28},{12,20},{4,12},{1,5},{9... | collective-permute-start | bytes 393224 | tf_op jit(solution)/shard_map/ppermute | solution.py:218
  66.7 2.8 %collective-permute-done.17 = bf16[32,2048]{1,0:T(8,128)(2,1)S(1)} collective-permute-done((bf16[32,2048]{1,0:T(8,128)(2,1)S(1)}, bf16[32,2048]{1,0:T(8,128)(2,1)S(1)}, u32[]{:S(2)}, u32[]{:S(2)}) %collective-permute-start.17) | collective-permute-done | bytes 131104 | tf_op jit(solution)/shard_map/ppermute | solution.py:218
  69.6 0.4 collective-permute-done.20
  70.0 0.1 fusion.3
  70.1 0.1 collective-permute-start.22
  70.2 1.0 %collective-permute-start.23 = (bf16[32,512]{1,0:T(8,128)(2,1)S(1)}, bf16[32,512]{1,0:T(8,128)(2,1)S(1)}, u32[]{:S(2)}, u32[]{:S(2)}) collective-permute-start(bf16[32,512]{1,0:T(8,128)(2,1)S(1)} %get-tuple-element.100), channel_id=1, source_target_pairs={{0,2},{1,3},{2,0},{3,1},{4,6},{5,7},{6,4},{7,5},{8,10},{9,11},{10,... | collective-permute-start | bytes 98312 | tf_op jit(solution)/shard_map/ppermute | solution.py:316
  71.2 0.9 %collective-permute-start.24 = (bf16[32,512]{1,0:T(8,128)(2,1)S(1)}, bf16[32,512]{1,0:T(8,128)(2,1)S(1)}, u32[]{:S(2)}, u32[]{:S(2)}) collective-permute-start(bf16[32,512]{1,0:T(8,128)(2,1)S(1)} %get-tuple-element.98), channel_id=1, source_target_pairs={{0,1},{1,0},{2,3},{3,2},{4,5},{5,4},{6,7},{7,6},{8,9},{9,8},{10,11... | collective-permute-start | bytes 98312 | tf_op jit(solution)/shard_map/ppermute | solution.py:316
  72.0 1.5 %collective-permute-done.22 = bf16[32,512]{1,0:T(8,128)(2,1)S(1)} collective-permute-done((bf16[32,512]{1,0:T(8,128)(2,1)S(1)}, bf16[32,512]{1,0:T(8,128)(2,1)S(1)}, u32[]{:S(2)}, u32[]{:S(2)}) %collective-permute-start.22) | collective-permute-done | bytes 32800 | tf_op jit(solution)/shard_map/ppermute | solution.py:316
  73.5 1.0 %collective-permute-done.23 = bf16[32,512]{1,0:T(8,128)(2,1)S(1)} collective-permute-done((bf16[32,512]{1,0:T(8,128)(2,1)S(1)}, bf16[32,512]{1,0:T(8,128)(2,1)S(1)}, u32[]{:S(2)}, u32[]{:S(2)}) %collective-permute-start.23) | collective-permute-done | bytes 32800 | tf_op jit(solution)/shard_map/ppermute | solution.py:316
  74.5 0.0 collective-permute-done.24
  74.5 0.7 pad_maximum_fusion.2
  (23 shorter events, 0.3 us)
Async XLA Ops:
  0.0 4.9 %copy-start = (f32[128,8]{0,1:T(8,128)S(1)}, f32[128,8]{0,1:T(8,128)}, u32[]{:S(2)}) copy-start(f32[128,8]{0,1:T(8,128)} %param.17) | copy-start | bytes 12292
  1.9 5.3 %collective-permute-start = (bf16[128,256]{1,0:T(8,128)(2,1)S(1)}, bf16[128,256]{1,0:T(8,128)(2,1)S(1)}, u32[]{:S(2)}, u32[]{:S(2)}) collective-permute-start(bf16[128,256]{1,0:T(8,128)(2,1)S(1)} %get-tuple-element.51), channel_id=1, source_target_pairs={{0,4},{4,0},{8,12},{12,8},{16,20},{20,16},{24,28},{28,24},{1,5},{5... | collective-permute-start | bytes 196616 | tf_op jit(solution)/shard_map/ppermute | solution.py:366
  7.2 7.7 %collective-permute-start.1 = (bf16[128,256]{1,0:T(8,128)(2,1)S(1)}, bf16[128,256]{1,0:T(8,128)(2,1)S(1)}, u32[]{:S(2)}, u32[]{:S(2)}) collective-permute-start(bf16[128,256]{1,0:T(8,128)(2,1)S(1)} %fusion.6.after_ref), channel_id=1, source_target_pairs={{0,8},{4,12},{8,0},{12,4},{16,24},{20,28},{24,16},{28,20},{1,9},{5... | collective-permute-start | bytes 196616 | tf_op jit(solution)/shard_map/ppermute | solution.py:306
  9.3 6.6 %collective-permute-start.2 = (bf16[128,256]{1,0:T(8,128)(2,1)S(1)}, bf16[128,256]{1,0:T(8,128)(2,1)S(1)}, u32[]{:S(2)}, u32[]{:S(2)}) collective-permute-start(bf16[128,256]{1,0:T(8,128)(2,1)S(1)} %fusion.6.after_ref), channel_id=1, source_target_pairs={{0,16},{4,20},{8,24},{12,28},{16,0},{20,4},{24,8},{28,12},{1,17},{... | collective-permute-start | bytes 196616 | tf_op jit(solution)/shard_map/ppermute | solution.py:306
  11.9 6.1 %collective-permute-start.3 = (bf16[128,256]{1,0:T(8,128)(2,1)S(1)}, bf16[128,256]{1,0:T(8,128)(2,1)S(1)}, u32[]{:S(2)}, u32[]{:S(2)}) collective-permute-start(bf16[128,256]{1,0:T(8,128)(2,1)S(1)} %fusion.6.after_ref), channel_id=1, source_target_pairs={{0,24},{4,28},{8,16},{12,20},{16,8},{20,12},{24,0},{28,4},{1,25},{... | collective-permute-start | bytes 196616 | tf_op jit(solution)/shard_map/ppermute | solution.py:306
  18.1 4.3 %collective-permute-start.4 = (bf16[128,256]{1,0:T(8,128)(2,1)S(1)}, bf16[128,256]{1,0:T(8,128)(2,1)S(1)}, u32[]{:S(2)}, u32[]{:S(2)}) collective-permute-start(bf16[128,256]{1,0:T(8,128)(2,1)S(1)} %get-tuple-element.61.after_ref), channel_id=1, source_target_pairs={{0,4},{4,0},{8,12},{12,8},{16,20},{20,16},{24,28},{28,24},{1,5},{5... | collective-permute-start | bytes 196616 | tf_op jit(solution)/shard_map/ppermute | solution.py:382
  19.6 8.0 %copy-start.1 = (f32[2048]{0:T(1024)S(1)}, f32[2048]{0:T(1024)}, u32[]{:S(2)}) copy-start(f32[2048]{0:T(1024)} %param.15) | copy-start | bytes 24580
  23.3 3.7 %collective-permute-start.5 = (bf16[32,512]{1,0:T(8,128)(2,1)S(1)}, bf16[32,512]{1,0:T(8,128)(2,1)S(1)}, u32[]{:S(2)}, u32[]{:S(2)}) collective-permute-start(bf16[32,512]{1,0:T(8,128)(2,1)S(1)} %get-tuple-element.64), channel_id=1, source_target_pairs={{0,3},{1,2},{2,1},{3,0},{4,7},{5,6},{6,5},{7,4},{8,11},{9,10},{10,... | collective-permute-start | bytes 98312 | tf_op jit(solution)/shard_map/ppermute | solution.py:316
  23.4 4.0 %collective-permute-start.6 = (bf16[32,512]{1,0:T(8,128)(2,1)S(1)}, bf16[32,512]{1,0:T(8,128)(2,1)S(1)}, u32[]{:S(2)}, u32[]{:S(2)}) collective-permute-start(bf16[32,512]{1,0:T(8,128)(2,1)S(1)} %get-tuple-element.65), channel_id=1, source_target_pairs={{0,2},{1,3},{2,0},{3,1},{4,6},{5,7},{6,4},{7,5},{8,10},{9,11},{10,... | collective-permute-start | bytes 98312 | tf_op jit(solution)/shard_map/ppermute | solution.py:316
  25.0 2.4 %collective-permute-start.7 = (bf16[32,512]{1,0:T(8,128)(2,1)S(1)}, bf16[32,512]{1,0:T(8,128)(2,1)S(1)}, u32[]{:S(2)}, u32[]{:S(2)}) collective-permute-start(bf16[32,512]{1,0:T(8,128)(2,1)S(1)} %get-tuple-element.66), channel_id=1, source_target_pairs={{0,1},{1,0},{2,3},{3,2},{4,5},{5,4},{6,7},{7,6},{8,9},{9,8},{10,11... | collective-permute-start | bytes 98312 | tf_op jit(solution)/shard_map/ppermute | solution.py:316
  27.7 6.0 %collective-permute-start.10 = (bf16[32,2176]{1,0:T(8,128)(2,1)S(1)}, bf16[32,2176]{1,0:T(8,128)(2,1)S(1)}, u32[]{:S(2)}, u32[]{:S(2)}) collective-permute-start(bf16[32,2176]{1,0:T(8,128)(2,1)S(1)} %pad_maximum_fusion.refs_0_), channel_id=1, source_target_pairs={{0,4},{8,0},{16,8},{24,16},{28,24},{20,28},{12,20},{4,12},{1,5},{9... | collective-permute-start | bytes 417800 | tf_op jit(solution)/shard_map/ppermute | solution.py:218
  29.3 5.9 %collective-permute-start.8 = (bf16[32,2176]{1,0:T(8,128)(2,1)S(1)}, bf16[32,2176]{1,0:T(8,128)(2,1)S(1)}, u32[]{:S(2)}, u32[]{:S(2)}) collective-permute-start(bf16[32,2176]{1,0:T(8,128)(2,1)S(1)} %pad_maximum_fusion.refs_0_), channel_id=1, source_target_pairs={{0,8},{8,16},{16,24},{24,28},{28,20},{20,12},{12,4},{4,0},{1,9},{9... | collective-permute-start | bytes 417800 | tf_op jit(solution)/shard_map/ppermute | solution.py:218
  33.7 6.6 %collective-permute-start.11 = (bf16[32,2176]{1,0:T(8,128)(2,1)S(1)}, bf16[32,2176]{1,0:T(8,128)(2,1)S(1)}, u32[]{:S(2)}, u32[]{:S(2)}) collective-permute-start(bf16[32,2176]{1,0:T(8,128)(2,1)S(1)} %collective-permute-done.10.refs_3_), channel_id=1, source_target_pairs={{0,4},{8,0},{16,8},{24,16},{28,24},{20,28},{12,20},{4,12},{1,5},{9... | collective-permute-start | bytes 417800 | tf_op jit(solution)/shard_map/ppermute | solution.py:218
  35.2 5.3 %collective-permute-start.9 = (bf16[32,2176]{1,0:T(8,128)(2,1)S(1)}, bf16[32,2176]{1,0:T(8,128)(2,1)S(1)}, u32[]{:S(2)}, u32[]{:S(2)}) collective-permute-start(bf16[32,2176]{1,0:T(8,128)(2,1)S(1)} %collective-permute-done.8.after_ref.refs_1_), channel_id=1, source_target_pairs={{0,8},{8,16},{16,24},{24,28},{28,20},{20,12},{12,4},{4,0},{1,9},{9... | collective-permute-start | bytes 417800 | tf_op jit(solution)/shard_map/ppermute | solution.py:218
  35.8 10.9 %collective-permute-start.14 = (bf16[32,2176]{1,0:T(8,128)(2,1)S(1)}, bf16[32,2176]{1,0:T(8,128)(2,1)S(1)}, u32[]{:S(2)}, u32[]{:S(2)}) collective-permute-start(bf16[32,2176]{1,0:T(8,128)(2,1)S(1)} %pad_maximum_fusion.refs_0_), channel_id=1, source_target_pairs={{0,28},{8,20},{16,12},{24,4},{28,0},{20,8},{12,16},{4,24},{1,29},{... | collective-permute-start | bytes 417800 | tf_op jit(solution)/shard_map/ppermute | solution.py:218
  40.5 6.1 %collective-permute-start.12 = (bf16[32,2176]{1,0:T(8,128)(2,1)S(1)}, bf16[32,2176]{1,0:T(8,128)(2,1)S(1)}, u32[]{:S(2)}, u32[]{:S(2)}) collective-permute-start(bf16[32,2176]{1,0:T(8,128)(2,1)S(1)} %collective-permute-done.9.refs_2_), channel_id=1, source_target_pairs={{0,8},{8,16},{16,24},{24,28},{28,20},{20,12},{12,4},{4,0},{1,9},{9... | collective-permute-start | bytes 417800 | tf_op jit(solution)/shard_map/ppermute | solution.py:218
  42.2 5.1 %collective-permute-start.13 = (bf16[32,2176]{1,0:T(8,128)(2,1)S(1)}, bf16[32,2176]{1,0:T(8,128)(2,1)S(1)}, u32[]{:S(2)}, u32[]{:S(2)}) collective-permute-start(bf16[32,2176]{1,0:T(8,128)(2,1)S(1)} %collective-permute-done.11.refs_4_), channel_id=1, source_target_pairs={{0,4},{8,0},{16,8},{24,16},{28,24},{20,28},{12,20},{4,12},{1,5},{9... | collective-permute-start | bytes 417800 | tf_op jit(solution)/shard_map/ppermute | solution.py:218
  50.1 8.0 %collective-permute-start.15 = (bf16[32,2048]{1,0:T(8,128)(2,1)S(1)}, bf16[32,2048]{1,0:T(8,128)(2,1)S(1)}, u32[]{:S(2)}, u32[]{:S(2)}) collective-permute-start(bf16[32,2048]{1,0:T(8,128)(2,1)S(1)} %get-tuple-element.82), channel_id=1, source_target_pairs={{0,8},{8,16},{16,24},{24,28},{28,20},{20,12},{12,4},{4,0},{1,9},{9... | collective-permute-start | bytes 393224 | tf_op jit(solution)/shard_map/ppermute | solution.py:218
  51.8 7.5 %collective-permute-start.18 = (bf16[32,2048]{1,0:T(8,128)(2,1)S(1)}, bf16[32,2048]{1,0:T(8,128)(2,1)S(1)}, u32[]{:S(2)}, u32[]{:S(2)}) collective-permute-start(bf16[32,2048]{1,0:T(8,128)(2,1)S(1)} %get-tuple-element.85), channel_id=1, source_target_pairs={{0,4},{8,0},{16,8},{24,16},{28,24},{20,28},{12,20},{4,12},{1,5},{9... | collective-permute-start | bytes 393224 | tf_op jit(solution)/shard_map/ppermute | solution.py:218
  53.2 13.6 %collective-permute-start.21 = (bf16[32,2048]{1,0:T(8,128)(2,1)S(1)}, bf16[32,2048]{1,0:T(8,128)(2,1)S(1)}, u32[]{:S(2)}, u32[]{:S(2)}) collective-permute-start(bf16[32,2048]{1,0:T(8,128)(2,1)S(1)} %get-tuple-element.88), channel_id=1, source_target_pairs={{0,28},{8,20},{16,12},{24,4},{28,0},{20,8},{12,16},{4,24},{1,29},{... | collective-permute-start | bytes 393224 | tf_op jit(solution)/shard_map/ppermute | solution.py:218
  58.2 6.3 %collective-permute-start.16 = (bf16[32,2048]{1,0:T(8,128)(2,1)S(1)}, bf16[32,2048]{1,0:T(8,128)(2,1)S(1)}, u32[]{:S(2)}, u32[]{:S(2)}) collective-permute-start(bf16[32,2048]{1,0:T(8,128)(2,1)S(1)} %add_convert_fusion.3), channel_id=1, source_target_pairs={{0,8},{8,16},{16,24},{24,28},{28,20},{20,12},{12,4},{4,0},{1,9},{9... | collective-permute-start | bytes 393224 | tf_op jit(solution)/shard_map/ppermute | solution.py:218
  59.4 5.5 %collective-permute-start.19 = (bf16[32,2048]{1,0:T(8,128)(2,1)S(1)}, bf16[32,2048]{1,0:T(8,128)(2,1)S(1)}, u32[]{:S(2)}, u32[]{:S(2)}) collective-permute-start(bf16[32,2048]{1,0:T(8,128)(2,1)S(1)} %add_convert_fusion.1), channel_id=1, source_target_pairs={{0,4},{8,0},{16,8},{24,16},{28,24},{20,28},{12,20},{4,12},{1,5},{9... | collective-permute-start | bytes 393224 | tf_op jit(solution)/shard_map/ppermute | solution.py:218
  64.5 5.0 %collective-permute-start.17 = (bf16[32,2048]{1,0:T(8,128)(2,1)S(1)}, bf16[32,2048]{1,0:T(8,128)(2,1)S(1)}, u32[]{:S(2)}, u32[]{:S(2)}) collective-permute-start(bf16[32,2048]{1,0:T(8,128)(2,1)S(1)} %add_convert_fusion.2), channel_id=1, source_target_pairs={{0,8},{8,16},{16,24},{24,28},{28,20},{20,12},{12,4},{4,0},{1,9},{9... | collective-permute-start | bytes 393224 | tf_op jit(solution)/shard_map/ppermute | solution.py:218
  65.0 5.0 %collective-permute-start.20 = (bf16[32,2048]{1,0:T(8,128)(2,1)S(1)}, bf16[32,2048]{1,0:T(8,128)(2,1)S(1)}, u32[]{:S(2)}, u32[]{:S(2)}) collective-permute-start(bf16[32,2048]{1,0:T(8,128)(2,1)S(1)} %add_convert_fusion), channel_id=1, source_target_pairs={{0,4},{8,0},{16,8},{24,16},{28,24},{20,28},{12,20},{4,12},{1,5},{9... | collective-permute-start | bytes 393224 | tf_op jit(solution)/shard_map/ppermute | solution.py:218
  70.1 3.4 %collective-permute-start.22 = (bf16[32,512]{1,0:T(8,128)(2,1)S(1)}, bf16[32,512]{1,0:T(8,128)(2,1)S(1)}, u32[]{:S(2)}, u32[]{:S(2)}) collective-permute-start(bf16[32,512]{1,0:T(8,128)(2,1)S(1)} %get-tuple-element.99), channel_id=1, source_target_pairs={{0,3},{1,2},{2,1},{3,0},{4,7},{5,6},{6,5},{7,4},{8,11},{9,10},{10,... | collective-permute-start | bytes 98312 | tf_op jit(solution)/shard_map/ppermute | solution.py:316
  70.2 4.3 %collective-permute-start.23 = (bf16[32,512]{1,0:T(8,128)(2,1)S(1)}, bf16[32,512]{1,0:T(8,128)(2,1)S(1)}, u32[]{:S(2)}, u32[]{:S(2)}) collective-permute-start(bf16[32,512]{1,0:T(8,128)(2,1)S(1)} %get-tuple-element.100), channel_id=1, source_target_pairs={{0,2},{1,3},{2,0},{3,1},{4,6},{5,7},{6,4},{7,5},{8,10},{9,11},{10,... | collective-permute-start | bytes 98312 | tf_op jit(solution)/shard_map/ppermute | solution.py:316
  71.2 3.3 %collective-permute-start.24 = (bf16[32,512]{1,0:T(8,128)(2,1)S(1)}, bf16[32,512]{1,0:T(8,128)(2,1)S(1)}, u32[]{:S(2)}, u32[]{:S(2)}) collective-permute-start(bf16[32,512]{1,0:T(8,128)(2,1)S(1)} %get-tuple-element.98), channel_id=1, source_target_pairs={{0,1},{1,0},{2,3},{3,2},{4,5},{5,4},{6,7},{7,6},{8,9},{9,8},{10,11... | collective-permute-start | bytes 98312 | tf_op jit(solution)/shard_map/ppermute | solution.py:316

commit v14 on v13

--- a/solution.py
+++ b/solution.py
@@ -189,7 +189,7 @@
 
 def run_expert(scalars, sign, blocks, weights_gate, weights_up, weights_out):
     units, model = weights_out.shape
-    total = -(-sum(b.shape[0] for b in blocks) // HEAD) * HEAD
+    total = max(HEAD, sum(b.shape[0] for b in blocks))
     *made, sign = call(
         functools.partial(expert_kernel, len(blocks)),
         [shape((b.shape[0], model), BF16) for b in blocks] + [shape((8, HEAD), F32)],
@@ -225,7 +225,7 @@
         came, went = hop(ahead[-1], 1), hop(behind[-1], -1)
         if distance == far - 2:
             weights_out, sign = load_near(scalars, expert_out, 0, ahead[-1])
-            came, went, sign = lax.optimization_barrier((came, went, sign))
+            came, went, sign, farthest = lax.optimization_barrier((came, went, sign, farthest))
         ahead.append(came)
         behind.append(went)
     last = hop(ahead[-1], 1), hop(behind[-1], -1)

time: 75.4 us -> 74.8 us (level)
  starting transfers between devices: 30.9 us -> 32.2 us
  Pallas kernels: 18.9 us -> 17.7 us
    ppermute x14, starting transfers between devices: 17.7 us -> 19.1 us  [hop(): lax.ppermute(rows, 'seq', [(order[p], order[(p + steps) % count]) for p i...]
    pallas_call x8, Pallas kernels: 18.9 us -> 17.7 us  [call(): pl.pallas_call(kernel, out_shape=outs, in_specs=[SCALAR if i == 0 or i in...]
  transfers between devices with their start and end apart: 25 -> 25, of which waited for: 16 -> 17; matrix products, arithmetic and copies ran while one was open for 2% -> 2% of each run, Pallas kernels for 18% -> 16%
where the time goes in v14:
time: 74.8 us; the launch traced here: 74.6 us
  starting transfers between devices  32.2 us (43%)
  waiting for transfers between devices  22 us (29%)
  Pallas kernels  17.7 us (24%)
  other arithmetic  1.4 us (2%)
  local copies, waits for them, and re-layouts  1.09 us (1%)
    ppermute x14, starting transfers between devices, hop(): lax.ppermute(rows, 'seq', [(order[p], order[(p + steps) % count]) for p i...  19.1 us
    pallas_call x8, Pallas kernels, call(): pl.pallas_call(kernel, out_shape=outs, in_specs=[SCALAR if i == 0 or i in...  17.7 us
    ppermute x14, waiting for transfers between devices, hop(): lax.ppermute(rows, 'seq', [(order[p], order[(p + steps) % count]) for p i...  14 us
    ppermute x3, starting transfers between devices, prior_states(): lax.ppermute(total, 'seq', [(i, i ^ 2 * distance) for i in range(count)])  4.76 us
    ppermute x6, waiting for transfers between devices, exchange(): lax.ppermute(pieces[j], 'exp', [(i, i ^ j) for i in range(parts)])  4.43 us
    ppermute x6, starting transfers between devices, exchange(): lax.ppermute(pieces[j], 'exp', [(i, i ^ j) for i in range(parts)])  3.84 us
    ppermute x3, waiting for transfers between devices, prior_states(): lax.ppermute(total, 'seq', [(i, i ^ 2 * distance) for i in range(count)])  3.11 us
    ppermute x1, starting transfers between devices, per_device(): partner = lax.ppermute(given, 'seq', swap)  3.01 us
  transfers between devices with their start and end apart: 25, of which 17 were waited for; matrix products, arithmetic and copies ran while one was open for 2% of the time, Pallas kernels for 16%

profile of v14, /device:TPU:0, one launch (start us, length us, event | category | flops | bytes accessed | tf_op | source)
XLA Modules:
  0.0 74.6 jit_solution(3600930419704464729)
XLA Ops:
  0.0 0.1 stack.24.scalars
  0.1 1.8 %shard_map.100 = (bf16[128,256]{1,0:T(8,128)(2,1)S(1)}, bf16[128,256]{1,0:T(8,128)(2,1)S(1)}, bf16[128,512]{1,0:T(8,128)(2,1)S(1)}, bf16[128,512]{1,0:T(8,128)(2...) custom-call(s32[7]{0:T(128)S(1)} %stack.24.scalars, ...), custom_call_target="tpu_custom_call" | custom-call | flops 16777216 | bytes 1188892 | tf_op jit(solution)/shard_map/pallas_call | solution.py:24
  1.9 3.0 %collective-permute-start = (bf16[128,256]{1,0:T(8,128)(2,1)S(1)}, bf16[128,256]{1,0:T(8,128)(2,1)S(1)}, u32[]{:S(2)}, u32[]{:S(2)}) collective-permute-start(bf16[128,256]{1,0:T(8,128)(2,1)S(1)} %get-tuple-element.52), channel_id=1, source_target_pairs={{0,4},{4,0},{8,12},{12,8},{16,20},{20,16},{24,28},{28,24},{1,5},{5... | collective-permute-start | bytes 196616 | tf_op jit(solution)/shard_map/ppermute | solution.py:366
  4.9 0.1 constant_dynamic-slice_fusion
  5.0 0.9 %shard_map.101.within_ref = f32[128,512]{1,0:T(8,128)S(1)} custom-call(s32[7]{0:T(128)S(1)} %stack.24.scalars, bf16[128,512]{1,0:T(8,128)(2,1)S(1)} %get-tuple-element.53.keys, bf16[128,512]{1,0:T(8,128)(2,1)S(1)} %get-tuple-element.54.values, bf16[128,512]{1,0:T(8,128)(2,1)S(1)} %get-tuple-element.55.queries), custom_call_target="tpu_custom_call" | custom-call | flops 50331648 | bytes 655388 | tf_op jit(solution)/shard_map/pallas_call | solution.py:24
  5.9 0.8 %constant_dynamic-slice_fusion.1 = s32[32,8]{0,1:T(8,128)S(1)} fusion(s32[128,8]{0,1:T(8,128)} %param.16, u32[]{:T(128)S(6)} %convert_element_type.87), kind=kLoop, calls=%fused_computation.54 | loop fusion | bytes 2052 | tf_op jit(solution)/shard_map/dynamic_slice | solution.py:396
  6.7 0.5 collective-permute-done
  7.2 2.2 %collective-permute-start.1 = (bf16[128,256]{1,0:T(8,128)(2,1)S(1)}, bf16[128,256]{1,0:T(8,128)(2,1)S(1)}, u32[]{:S(2)}, u32[]{:S(2)}) collective-permute-start(bf16[128,256]{1,0:T(8,128)(2,1)S(1)} %fusion.6.after_ref), channel_id=1, source_target_pairs={{0,8},{4,12},{8,0},{12,4},{16,24},{20,28},{24,16},{28,20},{1,9},{5... | collective-permute-start | bytes 196616 | tf_op jit(solution)/shard_map/ppermute | solution.py:306
  9.3 2.6 %collective-permute-start.2 = (bf16[128,256]{1,0:T(8,128)(2,1)S(1)}, bf16[128,256]{1,0:T(8,128)(2,1)S(1)}, u32[]{:S(2)}, u32[]{:S(2)}) collective-permute-start(bf16[128,256]{1,0:T(8,128)(2,1)S(1)} %fusion.6.after_ref), channel_id=1, source_target_pairs={{0,16},{4,20},{8,24},{12,28},{16,0},{20,4},{24,8},{28,12},{1,17},{... | collective-permute-start | bytes 196616 | tf_op jit(solution)/shard_map/ppermute | solution.py:306
  11.9 0.0 collective-permute-start.3
  12.0 0.1 copy.16
  12.0 0.1 copy.15
  12.1 2.8 %shard_map.102 = (bf16[2048,1024]{1,0:T(8,128)(2,1)S(1)}, f32[8,128]{1,0:T(8,128)S(1)}) custom-call(s32[7]{0:T(128)S(1)} %stack.24.scalars, bf16[2,2048,1024]{2,1,0:T(8,128)(2,1)} %bitcast.16, bf16[128,256]{1,0:T(8,128)(2,1)S(1)} %fusion.6.after_ref), custom_call_target="tpu_custom_call" | custom-call | bytes 12652572 | tf_op jit(solution)/shard_map/pallas_call | solution.py:24
  14.9 0.0 collective-permute-done.1
  14.9 1.0 %collective-permute-done.2 = bf16[128,256]{1,0:T(8,128)(2,1)S(1)} collective-permute-done((bf16[128,256]{1,0:T(8,128)(2,1)S(1)}, bf16[128,256]{1,0:T(8,128)(2,1)S(1)}, u32[]{:S(2)}, u32[]{:S(2)}) %collective-permute-start.2) | collective-permute-done | bytes 65568 | tf_op jit(solution)/shard_map/ppermute | solution.py:306
  15.9 2.1 %collective-permute-done.3 = bf16[128,256]{1,0:T(8,128)(2,1)S(1)} collective-permute-done((bf16[128,256]{1,0:T(8,128)(2,1)S(1)}, bf16[128,256]{1,0:T(8,128)(2,1)S(1)}, u32[]{:S(2)}, u32[]{:S(2)}) %collective-permute-start.3) | collective-permute-done | bytes 65568 | tf_op jit(solution)/shard_map/ppermute | solution.py:306
  18.0 0.1 fusion.5
  18.1 1.6 %collective-permute-start.4 = (bf16[128,256]{1,0:T(8,128)(2,1)S(1)}, bf16[128,256]{1,0:T(8,128)(2,1)S(1)}, u32[]{:S(2)}, u32[]{:S(2)}) collective-permute-start(bf16[128,256]{1,0:T(8,128)(2,1)S(1)} %get-tuple-element.62.after_ref), channel_id=1, source_target_pairs={{0,4},{4,0},{8,12},{12,8},{16,20},{20,16},{24,28},{28,24},{1,5},{5... | collective-permute-start | bytes 196616 | tf_op jit(solution)/shard_map/ppermute | solution.py:382
  19.6 2.8 %shard_map.103 = (bf16[2048,1024]{1,0:T(8,128)(2,1)S(1)}, f32[8,128]{1,0:T(8,128)S(1)}) custom-call(s32[7]{0:T(128)S(1)} %stack.24.scalars, bf16[2,2048,1024]{2,1,0:T(8,128)(2,1)} %bitcast.17, bf16[128,256]{1,0:T(8,128)(2,1)S(1)} %get-tuple-element.62.after_ref), custom_call_target="tpu_custom_call" | custom-call | bytes 12652572 | tf_op jit(solution)/shard_map/pallas_call | solution.py:24
  22.4 0.0 collective-permute-done.4.other_ref
  22.4 0.9 %shard_map.104 = (bf16[32,512]{1,0:T(8,128)(2,1)S(1)}, bf16[32,512]{1,0:T(8,128)(2,1)S(1)}, bf16[32,512]{1,0:T(8,128)(2,1)S(1)}, bf16[32,512]{1,0:T(8,128)(2,1)S(1)}) custom-call(s32[7]{0:T(128)S(1)} %stack.24.scalars, f32[128,512]{1,0:T(8,128)S(1)} %shard_map.101.within_ref, bf16[128,512]{1,0:T(8,128)(2,1)S(1)} %get-tuple-element.55.queries, ...), custom_call_target="tpu_custom_call" | custom-call | flops 33554432 | bytes 862236 | tf_op jit(solution)/shard_map/pallas_call | solution.py:24
  23.3 0.1 collective-permute-start.5
  23.4 1.6 %collective-permute-start.6 = (bf16[32,512]{1,0:T(8,128)(2,1)S(1)}, bf16[32,512]{1,0:T(8,128)(2,1)S(1)}, u32[]{:S(2)}, u32[]{:S(2)}) collective-permute-start(bf16[32,512]{1,0:T(8,128)(2,1)S(1)} %get-tuple-element.66), channel_id=1, source_target_pairs={{0,2},{1,3},{2,0},{3,1},{4,6},{5,7},{6,4},{7,5},{8,10},{9,11},{10,... | collective-permute-start | bytes 98312 | tf_op jit(solution)/shard_map/ppermute | solution.py:316
  25.0 0.3 collective-permute-start.7
  25.2 0.1 fusion.10
  25.3 1.7 %collective-permute-done.5 = bf16[32,512]{1,0:T(8,128)(2,1)S(1)} collective-permute-done((bf16[32,512]{1,0:T(8,128)(2,1)S(1)}, bf16[32,512]{1,0:T(8,128)(2,1)S(1)}, u32[]{:S(2)}, u32[]{:S(2)}) %collective-permute-start.5) | collective-permute-done | bytes 32800 | tf_op jit(solution)/shard_map/ppermute | solution.py:316
  27.0 0.4 collective-permute-done.6
  27.5 0.1 fusion
  27.6 0.1 fusion.2
  27.7 1.5 %collective-permute-start.10 = (bf16[32,2176]{1,0:T(8,128)(2,1)S(1)}, bf16[32,2176]{1,0:T(8,128)(2,1)S(1)}, u32[]{:S(2)}, u32[]{:S(2)}) collective-permute-start(bf16[32,2176]{1,0:T(8,128)(2,1)S(1)} %pad_maximum_fusion.refs_0_), channel_id=1, source_target_pairs={{0,4},{8,0},{16,8},{24,16},{28,24},{20,28},{12,20},{4,12},{1,5},{9... | collective-permute-start | bytes 417800 | tf_op jit(solution)/shard_map/ppermute | solution.py:218
  29.3 0.5 collective-permute-start.8
  29.8 1.8 %collective-permute-start.12 = (bf16[32,2176]{1,0:T(8,128)(2,1)S(1)}, bf16[32,2176]{1,0:T(8,128)(2,1)S(1)}, u32[]{:S(2)}, u32[]{:S(2)}) collective-permute-start(bf16[32,2176]{1,0:T(8,128)(2,1)S(1)} %pad_maximum_fusion.refs_0_), channel_id=1, source_target_pairs={{0,28},{8,20},{16,12},{24,4},{28,0},{20,8},{12,16},{4,24},{1,29},{... | collective-permute-start | bytes 417800 | tf_op jit(solution)/shard_map/ppermute | solution.py:218
  31.7 2.1 %collective-permute-done.10.refs_3_ = bf16[32,2176]{1,0:T(8,128)(2,1)S(1)} collective-permute-done((bf16[32,2176]{1,0:T(8,128)(2,1)S(1)}, bf16[32,2176]{1,0:T(8,128)(2,1)S(1)}, u32[]{:S(2)}, u32[]{:S(2)}) %collective-permute-start.10) | collective-permute-done | bytes 139296 | tf_op jit(solution)/shard_map/ppermute | solution.py:218
  33.7 1.5 %collective-permute-start.11 = (bf16[32,2176]{1,0:T(8,128)(2,1)S(1)}, bf16[32,2176]{1,0:T(8,128)(2,1)S(1)}, u32[]{:S(2)}, u32[]{:S(2)}) collective-permute-start(bf16[32,2176]{1,0:T(8,128)(2,1)S(1)} %collective-permute-done.10.refs_3_), channel_id=1, source_target_pairs={{0,4},{8,0},{16,8},{24,16},{28,24},{20,28},{12,20},{4,12},{1,5},{9... | collective-permute-start | bytes 417800 | tf_op jit(solution)/shard_map/ppermute | solution.py:218
  35.2 1.1 %collective-permute-start.9 = (bf16[32,2176]{1,0:T(8,128)(2,1)S(1)}, bf16[32,2176]{1,0:T(8,128)(2,1)S(1)}, u32[]{:S(2)}, u32[]{:S(2)}) collective-permute-start(bf16[32,2176]{1,0:T(8,128)(2,1)S(1)} %collective-permute-done.8.after_ref.refs_1_), channel_id=1, source_target_pairs={{0,8},{8,16},{16,24},{24,28},{28,20},{20,12},{12,4},{4,0},{1,9},{9... | collective-permute-start | bytes 417800 | tf_op jit(solution)/shard_map/ppermute | solution.py:218
  36.3 2.8 %shard_map.105 = (bf16[1024,2048]{1,0:T(8,128)(2,1)S(1)}, f32[8,128]{1,0:T(8,128)S(1)}) custom-call(s32[7]{0:T(128)S(1)} %stack.24.scalars, bf16[1,1024,2048]{2,1,0:T(8,128)(2,1)} %source.1, bf16[32,2176]{1,0:T(8,128)(2,1)S(1)} %collective-permute-done.8.after_ref.refs_1_), custom_call_target="tpu_custom_call" | custom-call | bytes 8531996 | tf_op jit(solution)/shard_map/pallas_call | solution.py:24
  39.1 0.0 collective-permute-done.12.refs_2_
  39.1 1.9 %collective-permute-done.11.refs_4_ = bf16[32,2176]{1,0:T(8,128)(2,1)S(1)} collective-permute-done((bf16[32,2176]{1,0:T(8,128)(2,1)S(1)}, bf16[32,2176]{1,0:T(8,128)(2,1)S(1)}, u32[]{:S(2)}, u32[]{:S(2)}) %collective-permute-start.11) | collective-permute-done | bytes 139296 | tf_op jit(solution)/shard_map/ppermute | solution.py:218
  41.0 0.4 collective-permute-done.9.refs_2_
  41.4 1.2 %collective-permute-start.13 = (bf16[32,2176]{1,0:T(8,128)(2,1)S(1)}, bf16[32,2176]{1,0:T(8,128)(2,1)S(1)}, u32[]{:S(2)}, u32[]{:S(2)}) collective-permute-start(bf16[32,2176]{1,0:T(8,128)(2,1)S(1)} %collective-permute-done.9.refs_2_), channel_id=1, source_target_pairs={{0,8},{8,16},{16,24},{24,28},{28,20},{20,12},{12,4},{4,0},{1,9},{9... | collective-permute-start | bytes 417800 | tf_op jit(solution)/shard_map/ppermute | solution.py:218
  42.5 0.9 %collective-permute-start.14 = (bf16[32,2176]{1,0:T(8,128)(2,1)S(1)}, bf16[32,2176]{1,0:T(8,128)(2,1)S(1)}, u32[]{:S(2)}, u32[]{:S(2)}) collective-permute-start(bf16[32,2176]{1,0:T(8,128)(2,1)S(1)} %collective-permute-done.11.refs_4_), channel_id=1, source_target_pairs={{0,4},{8,0},{16,8},{24,16},{28,24},{20,28},{12,20},{4,12},{1,5},{9... | collective-permute-start | bytes 417800 | tf_op jit(solution)/shard_map/ppermute | solution.py:218
  43.4 2.9 %shard_map.106 = (bf16[32,2048]{1,0:T(8,128)(2,1)S(1)}, bf16[32,2048]{1,0:T(8,128)(2,1)S(1)}, bf16[32,2048]{1,0:T(8,128)(2,1)S(1)}, bf16[32,2048]{1,0:T(8,128)(2...) custom-call(s32[7]{0:T(128)S(1)} %stack.24.scalars, f32[8,128]{1,0:T(8,128)S(1)} %get-tuple-element.71.sign_ref, ...), custom_call_target="tpu_custom_call" | custom-call | flops 2013265920 | bytes 13942812 | tf_op jit(solution)/shard_map/pallas_call | solution.py:24
  46.2 0.2 collective-permute-done.13.refs_0_
  46.5 1.3 %collective-permute-done.14.refs_1_ = bf16[32,2176]{1,0:T(8,128)(2,1)S(1)} collective-permute-done((bf16[32,2176]{1,0:T(8,128)(2,1)S(1)}, bf16[32,2176]{1,0:T(8,128)(2,1)S(1)}, u32[]{:S(2)}, u32[]{:S(2)}) %collective-permute-start.14) | collective-permute-done | bytes 139296 | tf_op jit(solution)/shard_map/ppermute | solution.py:218
  47.8 2.9 %shard_map.107 = (bf16[32,2048]{1,0:T(8,128)(2,1)S(1)}, bf16[32,2048]{1,0:T(8,128)(2,1)S(1)}, bf16[32,2048]{1,0:T(8,128)(2,1)S(1)}, f32[8,128]{1,0:T(8,128)}) custom-call(s32[7]{0:T(128)S(1)} %stack.24.scalars, f32[8,128]{1,0:T(8,128)S(1)} %get-tuple-element.80.sign_ref, bf16[2048,1024]{1,0:T(8,128)(2,1)S(1)} %get-tuple-element.72.gate_ref, ...), custom_call_target="tpu_custom_call" | custom-call | flops 1610612736 | bytes 13402140 | tf_op jit(solution)/shard_map/pallas_call | solution.py:24
  50.7 2.0 %collective-permute-start.15 = (bf16[32,2048]{1,0:T(8,128)(2,1)S(1)}, bf16[32,2048]{1,0:T(8,128)(2,1)S(1)}, u32[]{:S(2)}, u32[]{:S(2)}) collective-permute-start(bf16[32,2048]{1,0:T(8,128)(2,1)S(1)} %get-tuple-element.84), channel_id=1, source_target_pairs={{0,8},{8,16},{16,24},{24,28},{28,20},{20,12},{12,4},{4,0},{1,9},{9... | collective-permute-start | bytes 393224 | tf_op jit(solution)/shard_map/ppermute | solution.py:218
  52.7 0.1 collective-permute-start.18
  52.8 3.0 %collective-permute-start.21 = (bf16[32,2048]{1,0:T(8,128)(2,1)S(1)}, bf16[32,2048]{1,0:T(8,128)(2,1)S(1)}, u32[]{:S(2)}, u32[]{:S(2)}) collective-permute-start(bf16[32,2048]{1,0:T(8,128)(2,1)S(1)} %get-tuple-element.90), channel_id=1, source_target_pairs={{0,28},{8,20},{16,12},{24,4},{28,0},{20,8},{12,16},{4,24},{1,29},{... | collective-permute-start | bytes 393224 | tf_op jit(solution)/shard_map/ppermute | solution.py:218
  55.8 0.8 %collective-permute-done.15 = bf16[32,2048]{1,0:T(8,128)(2,1)S(1)} collective-permute-done((bf16[32,2048]{1,0:T(8,128)(2,1)S(1)}, bf16[32,2048]{1,0:T(8,128)(2,1)S(1)}, u32[]{:S(2)}, u32[]{:S(2)}) %collective-permute-start.15) | collective-permute-done | bytes 131104 | tf_op jit(solution)/shard_map/ppermute | solution.py:218
  56.6 2.5 %collective-permute-start.16 = (bf16[32,2048]{1,0:T(8,128)(2,1)S(1)}, bf16[32,2048]{1,0:T(8,128)(2,1)S(1)}, u32[]{:S(2)}, u32[]{:S(2)}) collective-permute-start(bf16[32,2048]{1,0:T(8,128)(2,1)S(1)} %add_convert_fusion.3), channel_id=1, source_target_pairs={{0,8},{8,16},{16,24},{24,28},{28,20},{20,12},{12,4},{4,0},{1,9},{9... | collective-permute-start | bytes 393224 | tf_op jit(solution)/shard_map/ppermute | solution.py:218
  59.2 1.0 %collective-permute-start.19 = (bf16[32,2048]{1,0:T(8,128)(2,1)S(1)}, bf16[32,2048]{1,0:T(8,128)(2,1)S(1)}, u32[]{:S(2)}, u32[]{:S(2)}) collective-permute-start(bf16[32,2048]{1,0:T(8,128)(2,1)S(1)} %add_convert_fusion.1), channel_id=1, source_target_pairs={{0,4},{8,0},{16,8},{24,16},{28,24},{20,28},{12,20},{4,12},{1,5},{9... | collective-permute-start | bytes 393224 | tf_op jit(solution)/shard_map/ppermute | solution.py:218
  60.2 3.5 %collective-permute-done.16 = bf16[32,2048]{1,0:T(8,128)(2,1)S(1)} collective-permute-done((bf16[32,2048]{1,0:T(8,128)(2,1)S(1)}, bf16[32,2048]{1,0:T(8,128)(2,1)S(1)}, u32[]{:S(2)}, u32[]{:S(2)}) %collective-permute-start.16) | collective-permute-done | bytes 131104 | tf_op jit(solution)/shard_map/ppermute | solution.py:218
  63.8 0.4 collective-permute-start.17
  64.2 0.2 collective-permute-done.19
  64.5 1.5 %collective-permute-start.20 = (bf16[32,2048]{1,0:T(8,128)(2,1)S(1)}, bf16[32,2048]{1,0:T(8,128)(2,1)S(1)}, u32[]{:S(2)}, u32[]{:S(2)}) collective-permute-start(bf16[32,2048]{1,0:T(8,128)(2,1)S(1)} %add_convert_fusion), channel_id=1, source_target_pairs={{0,4},{8,0},{16,8},{24,16},{28,24},{20,28},{12,20},{4,12},{1,5},{9... | collective-permute-start | bytes 393224 | tf_op jit(solution)/shard_map/ppermute | solution.py:218
  66.0 2.8 %collective-permute-done.17 = bf16[32,2048]{1,0:T(8,128)(2,1)S(1)} collective-permute-done((bf16[32,2048]{1,0:T(8,128)(2,1)S(1)}, bf16[32,2048]{1,0:T(8,128)(2,1)S(1)}, u32[]{:S(2)}, u32[]{:S(2)}) %collective-permute-start.17) | collective-permute-done | bytes 131104 | tf_op jit(solution)/shard_map/ppermute | solution.py:218
  68.8 0.7 collective-permute-done.20
  69.5 0.1 fusion.3
  69.6 0.1 collective-permute-start.22
  69.7 1.2 %collective-permute-start.23 = (bf16[32,512]{1,0:T(8,128)(2,1)S(1)}, bf16[32,512]{1,0:T(8,128)(2,1)S(1)}, u32[]{:S(2)}, u32[]{:S(2)}) collective-permute-start(bf16[32,512]{1,0:T(8,128)(2,1)S(1)} %get-tuple-element.102), channel_id=1, source_target_pairs={{0,2},{1,3},{2,0},{3,1},{4,6},{5,7},{6,4},{7,5},{8,10},{9,11},{10,... | collective-permute-start | bytes 98312 | tf_op jit(solution)/shard_map/ppermute | solution.py:316
  70.9 0.7 collective-permute-start.24
  71.6 1.5 %collective-permute-done.22 = bf16[32,512]{1,0:T(8,128)(2,1)S(1)} collective-permute-done((bf16[32,512]{1,0:T(8,128)(2,1)S(1)}, bf16[32,512]{1,0:T(8,128)(2,1)S(1)}, u32[]{:S(2)}, u32[]{:S(2)}) %collective-permute-start.22) | collective-permute-done | bytes 32800 | tf_op jit(solution)/shard_map/ppermute | solution.py:316
  73.0 0.9 %collective-permute-done.23 = bf16[32,512]{1,0:T(8,128)(2,1)S(1)} collective-permute-done((bf16[32,512]{1,0:T(8,128)(2,1)S(1)}, bf16[32,512]{1,0:T(8,128)(2,1)S(1)}, u32[]{:S(2)}, u32[]{:S(2)}) %collective-permute-start.23) | collective-permute-done | bytes 32800 | tf_op jit(solution)/shard_map/ppermute | solution.py:316
  73.9 0.7 pad_maximum_fusion.2
  (23 shorter events, 0.3 us)
Async XLA Ops:
  0.0 4.9 %copy-start = (f32[128,8]{0,1:T(8,128)S(1)}, f32[128,8]{0,1:T(8,128)}, u32[]{:S(2)}) copy-start(f32[128,8]{0,1:T(8,128)} %param.17) | copy-start | bytes 12292
  1.9 5.3 %collective-permute-start = (bf16[128,256]{1,0:T(8,128)(2,1)S(1)}, bf16[128,256]{1,0:T(8,128)(2,1)S(1)}, u32[]{:S(2)}, u32[]{:S(2)}) collective-permute-start(bf16[128,256]{1,0:T(8,128)(2,1)S(1)} %get-tuple-element.52), channel_id=1, source_target_pairs={{0,4},{4,0},{8,12},{12,8},{16,20},{20,16},{24,28},{28,24},{1,5},{5... | collective-permute-start | bytes 196616 | tf_op jit(solution)/shard_map/ppermute | solution.py:366
  7.2 7.7 %collective-permute-start.1 = (bf16[128,256]{1,0:T(8,128)(2,1)S(1)}, bf16[128,256]{1,0:T(8,128)(2,1)S(1)}, u32[]{:S(2)}, u32[]{:S(2)}) collective-permute-start(bf16[128,256]{1,0:T(8,128)(2,1)S(1)} %fusion.6.after_ref), channel_id=1, source_target_pairs={{0,8},{4,12},{8,0},{12,4},{16,24},{20,28},{24,16},{28,20},{1,9},{5... | collective-permute-start | bytes 196616 | tf_op jit(solution)/shard_map/ppermute | solution.py:306
  9.3 6.6 %collective-permute-start.2 = (bf16[128,256]{1,0:T(8,128)(2,1)S(1)}, bf16[128,256]{1,0:T(8,128)(2,1)S(1)}, u32[]{:S(2)}, u32[]{:S(2)}) collective-permute-start(bf16[128,256]{1,0:T(8,128)(2,1)S(1)} %fusion.6.after_ref), channel_id=1, source_target_pairs={{0,16},{4,20},{8,24},{12,28},{16,0},{20,4},{24,8},{28,12},{1,17},{... | collective-permute-start | bytes 196616 | tf_op jit(solution)/shard_map/ppermute | solution.py:306
  11.9 6.1 %collective-permute-start.3 = (bf16[128,256]{1,0:T(8,128)(2,1)S(1)}, bf16[128,256]{1,0:T(8,128)(2,1)S(1)}, u32[]{:S(2)}, u32[]{:S(2)}) collective-permute-start(bf16[128,256]{1,0:T(8,128)(2,1)S(1)} %fusion.6.after_ref), channel_id=1, source_target_pairs={{0,24},{4,28},{8,16},{12,20},{16,8},{20,12},{24,0},{28,4},{1,25},{... | collective-permute-start | bytes 196616 | tf_op jit(solution)/shard_map/ppermute | solution.py:306
  18.1 4.3 %collective-permute-start.4 = (bf16[128,256]{1,0:T(8,128)(2,1)S(1)}, bf16[128,256]{1,0:T(8,128)(2,1)S(1)}, u32[]{:S(2)}, u32[]{:S(2)}) collective-permute-start(bf16[128,256]{1,0:T(8,128)(2,1)S(1)} %get-tuple-element.62.after_ref), channel_id=1, source_target_pairs={{0,4},{4,0},{8,12},{12,8},{16,20},{20,16},{24,28},{28,24},{1,5},{5... | collective-permute-start | bytes 196616 | tf_op jit(solution)/shard_map/ppermute | solution.py:382
  19.6 8.0 %copy-start.1 = (f32[2048]{0:T(1024)S(1)}, f32[2048]{0:T(1024)}, u32[]{:S(2)}) copy-start(f32[2048]{0:T(1024)} %param.15) | copy-start | bytes 24580
  23.3 3.7 %collective-permute-start.5 = (bf16[32,512]{1,0:T(8,128)(2,1)S(1)}, bf16[32,512]{1,0:T(8,128)(2,1)S(1)}, u32[]{:S(2)}, u32[]{:S(2)}) collective-permute-start(bf16[32,512]{1,0:T(8,128)(2,1)S(1)} %get-tuple-element.65), channel_id=1, source_target_pairs={{0,3},{1,2},{2,1},{3,0},{4,7},{5,6},{6,5},{7,4},{8,11},{9,10},{10,... | collective-permute-start | bytes 98312 | tf_op jit(solution)/shard_map/ppermute | solution.py:316
  23.4 4.0 %collective-permute-start.6 = (bf16[32,512]{1,0:T(8,128)(2,1)S(1)}, bf16[32,512]{1,0:T(8,128)(2,1)S(1)}, u32[]{:S(2)}, u32[]{:S(2)}) collective-permute-start(bf16[32,512]{1,0:T(8,128)(2,1)S(1)} %get-tuple-element.66), channel_id=1, source_target_pairs={{0,2},{1,3},{2,0},{3,1},{4,6},{5,7},{6,4},{7,5},{8,10},{9,11},{10,... | collective-permute-start | bytes 98312 | tf_op jit(solution)/shard_map/ppermute | solution.py:316
  25.0 2.4 %collective-permute-start.7 = (bf16[32,512]{1,0:T(8,128)(2,1)S(1)}, bf16[32,512]{1,0:T(8,128)(2,1)S(1)}, u32[]{:S(2)}, u32[]{:S(2)}) collective-permute-start(bf16[32,512]{1,0:T(8,128)(2,1)S(1)} %get-tuple-element.67), channel_id=1, source_target_pairs={{0,1},{1,0},{2,3},{3,2},{4,5},{5,4},{6,7},{7,6},{8,9},{9,8},{10,11... | collective-permute-start | bytes 98312 | tf_op jit(solution)/shard_map/ppermute | solution.py:316
  27.7 6.0 %collective-permute-start.10 = (bf16[32,2176]{1,0:T(8,128)(2,1)S(1)}, bf16[32,2176]{1,0:T(8,128)(2,1)S(1)}, u32[]{:S(2)}, u32[]{:S(2)}) collective-permute-start(bf16[32,2176]{1,0:T(8,128)(2,1)S(1)} %pad_maximum_fusion.refs_0_), channel_id=1, source_target_pairs={{0,4},{8,0},{16,8},{24,16},{28,24},{20,28},{12,20},{4,12},{1,5},{9... | collective-permute-start | bytes 417800 | tf_op jit(solution)/shard_map/ppermute | solution.py:218
  29.3 5.9 %collective-permute-start.8 = (bf16[32,2176]{1,0:T(8,128)(2,1)S(1)}, bf16[32,2176]{1,0:T(8,128)(2,1)S(1)}, u32[]{:S(2)}, u32[]{:S(2)}) collective-permute-start(bf16[32,2176]{1,0:T(8,128)(2,1)S(1)} %pad_maximum_fusion.refs_0_), channel_id=1, source_target_pairs={{0,8},{8,16},{16,24},{24,28},{28,20},{20,12},{12,4},{4,0},{1,9},{9... | collective-permute-start | bytes 417800 | tf_op jit(solution)/shard_map/ppermute | solution.py:218
  29.8 9.3 %collective-permute-start.12 = (bf16[32,2176]{1,0:T(8,128)(2,1)S(1)}, bf16[32,2176]{1,0:T(8,128)(2,1)S(1)}, u32[]{:S(2)}, u32[]{:S(2)}) collective-permute-start(bf16[32,2176]{1,0:T(8,128)(2,1)S(1)} %pad_maximum_fusion.refs_0_), channel_id=1, source_target_pairs={{0,28},{8,20},{16,12},{24,4},{28,0},{20,8},{12,16},{4,24},{1,29},{... | collective-permute-start | bytes 417800 | tf_op jit(solution)/shard_map/ppermute | solution.py:218
  33.7 7.3 %collective-permute-start.11 = (bf16[32,2176]{1,0:T(8,128)(2,1)S(1)}, bf16[32,2176]{1,0:T(8,128)(2,1)S(1)}, u32[]{:S(2)}, u32[]{:S(2)}) collective-permute-start(bf16[32,2176]{1,0:T(8,128)(2,1)S(1)} %collective-permute-done.10.refs_3_), channel_id=1, source_target_pairs={{0,4},{8,0},{16,8},{24,16},{28,24},{20,28},{12,20},{4,12},{1,5},{9... | collective-permute-start | bytes 417800 | tf_op jit(solution)/shard_map/ppermute | solution.py:218
  35.2 6.2 %collective-permute-start.9 = (bf16[32,2176]{1,0:T(8,128)(2,1)S(1)}, bf16[32,2176]{1,0:T(8,128)(2,1)S(1)}, u32[]{:S(2)}, u32[]{:S(2)}) collective-permute-start(bf16[32,2176]{1,0:T(8,128)(2,1)S(1)} %collective-permute-done.8.after_ref.refs_1_), channel_id=1, source_target_pairs={{0,8},{8,16},{16,24},{24,28},{28,20},{20,12},{12,4},{4,0},{1,9},{9... | collective-permute-start | bytes 417800 | tf_op jit(solution)/shard_map/ppermute | solution.py:218
  41.4 5.1 %collective-permute-start.13 = (bf16[32,2176]{1,0:T(8,128)(2,1)S(1)}, bf16[32,2176]{1,0:T(8,128)(2,1)S(1)}, u32[]{:S(2)}, u32[]{:S(2)}) collective-permute-start(bf16[32,2176]{1,0:T(8,128)(2,1)S(1)} %collective-permute-done.9.refs_2_), channel_id=1, source_target_pairs={{0,8},{8,16},{16,24},{24,28},{28,20},{20,12},{12,4},{4,0},{1,9},{9... | collective-permute-start | bytes 417800 | tf_op jit(solution)/shard_map/ppermute | solution.py:218
  42.5 5.3 %collective-permute-start.14 = (bf16[32,2176]{1,0:T(8,128)(2,1)S(1)}, bf16[32,2176]{1,0:T(8,128)(2,1)S(1)}, u32[]{:S(2)}, u32[]{:S(2)}) collective-permute-start(bf16[32,2176]{1,0:T(8,128)(2,1)S(1)} %collective-permute-done.11.refs_4_), channel_id=1, source_target_pairs={{0,4},{8,0},{16,8},{24,16},{28,24},{20,28},{12,20},{4,12},{1,5},{9... | collective-permute-start | bytes 417800 | tf_op jit(solution)/shard_map/ppermute | solution.py:218
  50.7 5.8 %collective-permute-start.15 = (bf16[32,2048]{1,0:T(8,128)(2,1)S(1)}, bf16[32,2048]{1,0:T(8,128)(2,1)S(1)}, u32[]{:S(2)}, u32[]{:S(2)}) collective-permute-start(bf16[32,2048]{1,0:T(8,128)(2,1)S(1)} %get-tuple-element.84), channel_id=1, source_target_pairs={{0,8},{8,16},{16,24},{24,28},{28,20},{20,12},{12,4},{4,0},{1,9},{9... | collective-permute-start | bytes 393224 | tf_op jit(solution)/shard_map/ppermute | solution.py:218
  52.7 6.5 %collective-permute-start.18 = (bf16[32,2048]{1,0:T(8,128)(2,1)S(1)}, bf16[32,2048]{1,0:T(8,128)(2,1)S(1)}, u32[]{:S(2)}, u32[]{:S(2)}) collective-permute-start(bf16[32,2048]{1,0:T(8,128)(2,1)S(1)} %get-tuple-element.87), channel_id=1, source_target_pairs={{0,4},{8,0},{16,8},{24,16},{28,24},{20,28},{12,20},{4,12},{1,5},{9... | collective-permute-start | bytes 393224 | tf_op jit(solution)/shard_map/ppermute | solution.py:218
  52.8 13.2 %collective-permute-start.21 = (bf16[32,2048]{1,0:T(8,128)(2,1)S(1)}, bf16[32,2048]{1,0:T(8,128)(2,1)S(1)}, u32[]{:S(2)}, u32[]{:S(2)}) collective-permute-start(bf16[32,2048]{1,0:T(8,128)(2,1)S(1)} %get-tuple-element.90), channel_id=1, source_target_pairs={{0,28},{8,20},{16,12},{24,4},{28,0},{20,8},{12,16},{4,24},{1,29},{... | collective-permute-start | bytes 393224 | tf_op jit(solution)/shard_map/ppermute | solution.py:218
  56.6 7.1 %collective-permute-start.16 = (bf16[32,2048]{1,0:T(8,128)(2,1)S(1)}, bf16[32,2048]{1,0:T(8,128)(2,1)S(1)}, u32[]{:S(2)}, u32[]{:S(2)}) collective-permute-start(bf16[32,2048]{1,0:T(8,128)(2,1)S(1)} %add_convert_fusion.3), channel_id=1, source_target_pairs={{0,8},{8,16},{16,24},{24,28},{28,20},{20,12},{12,4},{4,0},{1,9},{9... | collective-permute-start | bytes 393224 | tf_op jit(solution)/shard_map/ppermute | solution.py:218
  59.2 5.3 %collective-permute-start.19 = (bf16[32,2048]{1,0:T(8,128)(2,1)S(1)}, bf16[32,2048]{1,0:T(8,128)(2,1)S(1)}, u32[]{:S(2)}, u32[]{:S(2)}) collective-permute-start(bf16[32,2048]{1,0:T(8,128)(2,1)S(1)} %add_convert_fusion.1), channel_id=1, source_target_pairs={{0,4},{8,0},{16,8},{24,16},{28,24},{20,28},{12,20},{4,12},{1,5},{9... | collective-permute-start | bytes 393224 | tf_op jit(solution)/shard_map/ppermute | solution.py:218
  63.8 5.0 %collective-permute-start.17 = (bf16[32,2048]{1,0:T(8,128)(2,1)S(1)}, bf16[32,2048]{1,0:T(8,128)(2,1)S(1)}, u32[]{:S(2)}, u32[]{:S(2)}) collective-permute-start(bf16[32,2048]{1,0:T(8,128)(2,1)S(1)} %add_convert_fusion.2), channel_id=1, source_target_pairs={{0,8},{8,16},{16,24},{24,28},{28,20},{20,12},{12,4},{4,0},{1,9},{9... | collective-permute-start | bytes 393224 | tf_op jit(solution)/shard_map/ppermute | solution.py:218
  64.5 5.0 %collective-permute-start.20 = (bf16[32,2048]{1,0:T(8,128)(2,1)S(1)}, bf16[32,2048]{1,0:T(8,128)(2,1)S(1)}, u32[]{:S(2)}, u32[]{:S(2)}) collective-permute-start(bf16[32,2048]{1,0:T(8,128)(2,1)S(1)} %add_convert_fusion), channel_id=1, source_target_pairs={{0,4},{8,0},{16,8},{24,16},{28,24},{20,28},{12,20},{4,12},{1,5},{9... | collective-permute-start | bytes 393224 | tf_op jit(solution)/shard_map/ppermute | solution.py:218
  69.6 3.4 %collective-permute-start.22 = (bf16[32,512]{1,0:T(8,128)(2,1)S(1)}, bf16[32,512]{1,0:T(8,128)(2,1)S(1)}, u32[]{:S(2)}, u32[]{:S(2)}) collective-permute-start(bf16[32,512]{1,0:T(8,128)(2,1)S(1)} %get-tuple-element.101), channel_id=1, source_target_pairs={{0,3},{1,2},{2,1},{3,0},{4,7},{5,6},{6,5},{7,4},{8,11},{9,10},{10,... | collective-permute-start | bytes 98312 | tf_op jit(solution)/shard_map/ppermute | solution.py:316
  69.7 4.2 %collective-permute-start.23 = (bf16[32,512]{1,0:T(8,128)(2,1)S(1)}, bf16[32,512]{1,0:T(8,128)(2,1)S(1)}, u32[]{:S(2)}, u32[]{:S(2)}) collective-permute-start(bf16[32,512]{1,0:T(8,128)(2,1)S(1)} %get-tuple-element.102), channel_id=1, source_target_pairs={{0,2},{1,3},{2,0},{3,1},{4,6},{5,7},{6,4},{7,5},{8,10},{9,11},{10,... | collective-permute-start | bytes 98312 | tf_op jit(solution)/shard_map/ppermute | solution.py:316
  70.9 3.0 %collective-permute-start.24 = (bf16[32,512]{1,0:T(8,128)(2,1)S(1)}, bf16[32,512]{1,0:T(8,128)(2,1)S(1)}, u32[]{:S(2)}, u32[]{:S(2)}) collective-permute-start(bf16[32,512]{1,0:T(8,128)(2,1)S(1)} %get-tuple-element.100), channel_id=1, source_target_pairs={{0,1},{1,0},{2,3},{3,2},{4,5},{5,4},{6,7},{7,6},{8,9},{9,8},{10,11... | collective-permute-start | bytes 98312 | tf_op jit(solution)/shard_map/ppermute | solution.py:316

commit v15 on v14

--- a/solution.py
+++ b/solution.py
@@ -293,7 +293,7 @@
 def pair_steps(pairs):
     bits = pairs.bit_length() - 1
     direct = pairs <= 4
-    steps = range(1, pairs) if direct else [1 << b for b in range(bits)]
+    steps = range(pairs - 1, 0, -1) if direct else [1 << b for b in range(bits)]
     return direct, [(d, d.bit_length() - 1) for d in steps]
 
 

time: 74.8 us -> 74.1 us (level)
  waiting for transfers between devices: 22 us -> 18.6 us
  starting transfers between devices: 32.2 us -> 35 us
    ppermute x14, starting transfers between devices: 19.1 us -> 21.8 us  [hop(): lax.ppermute(rows, 'seq', [(order[p], order[(p + steps) % count]) for p i...]
    ppermute x14, waiting for transfers between devices: 14 us -> 12.3 us  [hop(): lax.ppermute(rows, 'seq', [(order[p], order[(p + steps) % count]) for p i...]
    ppermute x3, waiting for transfers between devices: 3.11 us -> 1.6 us  [prior_states(): lax.ppermute(total, 'seq', [(i, i ^ 2 * distance) for i in range(count)])]
where the time goes in v15:
time: 74.1 us; the launch traced here: 74 us
  starting transfers between devices  35 us (47%)
  waiting for transfers between devices  18.6 us (25%)
  Pallas kernels  17.7 us (24%)
  other arithmetic  1.4 us (2%)
  local copies, waits for them, and re-layouts  1.09 us (1%)
    ppermute x14, starting transfers between devices, hop(): lax.ppermute(rows, 'seq', [(order[p], order[(p + steps) % count]) for p i...  21.8 us
    pallas_call x8, Pallas kernels, call(): pl.pallas_call(kernel, out_shape=outs, in_specs=[SCALAR if i == 0 or i in...  17.7 us
    ppermute x14, waiting for transfers between devices, hop(): lax.ppermute(rows, 'seq', [(order[p], order[(p + steps) % count]) for p i...  12.3 us
    ppermute x3, starting transfers between devices, prior_states(): lax.ppermute(total, 'seq', [(i, i ^ 2 * distance) for i in range(count)])  4.84 us
    ppermute x6, waiting for transfers between devices, exchange(): lax.ppermute(pieces[j], 'exp', [(i, i ^ j) for i in range(parts)])  4.25 us
    ppermute x6, starting transfers between devices, exchange(): lax.ppermute(pieces[j], 'exp', [(i, i ^ j) for i in range(parts)])  3.84 us
    ppermute x1, starting transfers between devices, per_device(): partner = lax.ppermute(given, 'seq', swap)  3.01 us
    ppermute x3, waiting for transfers between devices, prior_states(): lax.ppermute(total, 'seq', [(i, i ^ 2 * distance) for i in range(count)])  1.6 us
  transfers between devices with their start and end apart: 25, of which 17 were waited for; matrix products, arithmetic and copies ran while one was open for 2% of the time, Pallas kernels for 16%

profile of v15, /device:TPU:0, one launch (start us, length us, event | category | flops | bytes accessed | tf_op | source)
XLA Modules:
  0.0 74.0 jit_solution(14525069946168769716)
XLA Ops:
  0.0 0.1 stack.24.scalars
  0.1 1.8 %shard_map.100 = (bf16[128,256]{1,0:T(8,128)(2,1)S(1)}, bf16[128,256]{1,0:T(8,128)(2,1)S(1)}, bf16[128,512]{1,0:T(8,128)(2,1)S(1)}, bf16[128,512]{1,0:T(8,128)(2...) custom-call(s32[7]{0:T(128)S(1)} %stack.24.scalars, ...), custom_call_target="tpu_custom_call" | custom-call | flops 16777216 | bytes 1188892 | tf_op jit(solution)/shard_map/pallas_call | solution.py:24
  1.9 3.0 %collective-permute-start = (bf16[128,256]{1,0:T(8,128)(2,1)S(1)}, bf16[128,256]{1,0:T(8,128)(2,1)S(1)}, u32[]{:S(2)}, u32[]{:S(2)}) collective-permute-start(bf16[128,256]{1,0:T(8,128)(2,1)S(1)} %get-tuple-element.52), channel_id=1, source_target_pairs={{0,4},{4,0},{8,12},{12,8},{16,20},{20,16},{24,28},{28,24},{1,5},{5... | collective-permute-start | bytes 196616 | tf_op jit(solution)/shard_map/ppermute | solution.py:366
  4.9 0.1 constant_dynamic-slice_fusion
  5.0 0.9 %shard_map.101.within_ref = f32[128,512]{1,0:T(8,128)S(1)} custom-call(s32[7]{0:T(128)S(1)} %stack.24.scalars, bf16[128,512]{1,0:T(8,128)(2,1)S(1)} %get-tuple-element.53.keys, bf16[128,512]{1,0:T(8,128)(2,1)S(1)} %get-tuple-element.54.values, bf16[128,512]{1,0:T(8,128)(2,1)S(1)} %get-tuple-element.55.queries), custom_call_target="tpu_custom_call" | custom-call | flops 50331648 | bytes 655388 | tf_op jit(solution)/shard_map/pallas_call | solution.py:24
  5.9 0.8 %constant_dynamic-slice_fusion.1 = s32[32,8]{0,1:T(8,128)S(1)} fusion(s32[128,8]{0,1:T(8,128)} %param.16, u32[]{:T(128)S(6)} %convert_element_type.87), kind=kLoop, calls=%fused_computation.54 | loop fusion | bytes 2052 | tf_op jit(solution)/shard_map/dynamic_slice | solution.py:396
  6.7 0.5 collective-permute-done
  7.2 4.2 %collective-permute-start.1 = (bf16[128,256]{1,0:T(8,128)(2,1)S(1)}, bf16[128,256]{1,0:T(8,128)(2,1)S(1)}, u32[]{:S(2)}, u32[]{:S(2)}) collective-permute-start(bf16[128,256]{1,0:T(8,128)(2,1)S(1)} %fusion.6.after_ref), channel_id=1, source_target_pairs={{0,24},{4,28},{8,16},{12,20},{16,8},{20,12},{24,0},{28,4},{1,25},{... | collective-permute-start | bytes 196616 | tf_op jit(solution)/shard_map/ppermute | solution.py:306
  11.4 0.0 collective-permute-start.2
  11.4 0.6 collective-permute-start.3
  12.0 0.1 copy.16
  12.1 0.1 copy.15
  12.2 2.8 %shard_map.102 = (bf16[2048,1024]{1,0:T(8,128)(2,1)S(1)}, f32[8,128]{1,0:T(8,128)S(1)}) custom-call(s32[7]{0:T(128)S(1)} %stack.24.scalars, bf16[2,2048,1024]{2,1,0:T(8,128)(2,1)} %bitcast.16, bf16[128,256]{1,0:T(8,128)(2,1)S(1)} %fusion.6.after_ref), custom_call_target="tpu_custom_call" | custom-call | bytes 12652572 | tf_op jit(solution)/shard_map/pallas_call | solution.py:24
  15.0 1.6 %collective-permute-done.2 = bf16[128,256]{1,0:T(8,128)(2,1)S(1)} collective-permute-done((bf16[128,256]{1,0:T(8,128)(2,1)S(1)}, bf16[128,256]{1,0:T(8,128)(2,1)S(1)}, u32[]{:S(2)}, u32[]{:S(2)}) %collective-permute-start.2) | collective-permute-done | bytes 65568 | tf_op jit(solution)/shard_map/ppermute | solution.py:306
  16.6 0.0 collective-permute-done.3
  16.6 0.1 fusion.5
  16.6 1.6 %collective-permute-start.4 = (bf16[128,256]{1,0:T(8,128)(2,1)S(1)}, bf16[128,256]{1,0:T(8,128)(2,1)S(1)}, u32[]{:S(2)}, u32[]{:S(2)}) collective-permute-start(bf16[128,256]{1,0:T(8,128)(2,1)S(1)} %get-tuple-element.62.after_ref), channel_id=1, source_target_pairs={{0,4},{4,0},{8,12},{12,8},{16,20},{20,16},{24,28},{28,24},{1,5},{5... | collective-permute-start | bytes 196616 | tf_op jit(solution)/shard_map/ppermute | solution.py:382
  18.2 2.8 %shard_map.103 = (bf16[2048,1024]{1,0:T(8,128)(2,1)S(1)}, f32[8,128]{1,0:T(8,128)S(1)}) custom-call(s32[7]{0:T(128)S(1)} %stack.24.scalars, bf16[2,2048,1024]{2,1,0:T(8,128)(2,1)} %bitcast.17, bf16[128,256]{1,0:T(8,128)(2,1)S(1)} %get-tuple-element.62.after_ref), custom_call_target="tpu_custom_call" | custom-call | bytes 12652572 | tf_op jit(solution)/shard_map/pallas_call | solution.py:24
  21.0 0.9 %shard_map.104 = (bf16[32,512]{1,0:T(8,128)(2,1)S(1)}, bf16[32,512]{1,0:T(8,128)(2,1)S(1)}, bf16[32,512]{1,0:T(8,128)(2,1)S(1)}, bf16[32,512]{1,0:T(8,128)(2,1)S(1)}) custom-call(s32[7]{0:T(128)S(1)} %stack.24.scalars, f32[128,512]{1,0:T(8,128)S(1)} %shard_map.101.within_ref, bf16[128,512]{1,0:T(8,128)(2,1)S(1)} %get-tuple-element.55.queries, ...), custom_call_target="tpu_custom_call" | custom-call | flops 33554432 | bytes 862236 | tf_op jit(solution)/shard_map/pallas_call | solution.py:24
  21.9 0.1 collective-permute-start.5
  22.0 1.6 %collective-permute-start.6 = (bf16[32,512]{1,0:T(8,128)(2,1)S(1)}, bf16[32,512]{1,0:T(8,128)(2,1)S(1)}, u32[]{:S(2)}, u32[]{:S(2)}) collective-permute-start(bf16[32,512]{1,0:T(8,128)(2,1)S(1)} %get-tuple-element.66), channel_id=1, source_target_pairs={{0,2},{1,3},{2,0},{3,1},{4,6},{5,7},{6,4},{7,5},{8,10},{9,11},{10,... | collective-permute-start | bytes 98312 | tf_op jit(solution)/shard_map/ppermute | solution.py:316
  23.5 0.3 collective-permute-start.7
  23.8 0.1 fusion.10
  23.9 1.7 %collective-permute-done.5 = bf16[32,512]{1,0:T(8,128)(2,1)S(1)} collective-permute-done((bf16[32,512]{1,0:T(8,128)(2,1)S(1)}, bf16[32,512]{1,0:T(8,128)(2,1)S(1)}, u32[]{:S(2)}, u32[]{:S(2)}) %collective-permute-start.5) | collective-permute-done | bytes 32800 | tf_op jit(solution)/shard_map/ppermute | solution.py:316
  25.6 0.4 collective-permute-done.6
  26.0 0.1 fusion
  26.2 0.1 fusion.2
  26.3 1.5 %collective-permute-start.10 = (bf16[32,2176]{1,0:T(8,128)(2,1)S(1)}, bf16[32,2176]{1,0:T(8,128)(2,1)S(1)}, u32[]{:S(2)}, u32[]{:S(2)}) collective-permute-start(bf16[32,2176]{1,0:T(8,128)(2,1)S(1)} %pad_maximum_fusion.refs_0_), channel_id=1, source_target_pairs={{0,4},{8,0},{16,8},{24,16},{28,24},{20,28},{12,20},{4,12},{1,5},{9... | collective-permute-start | bytes 417800 | tf_op jit(solution)/shard_map/ppermute | solution.py:218
  27.8 0.6 collective-permute-start.8
  28.4 3.1 %collective-permute-start.12 = (bf16[32,2176]{1,0:T(8,128)(2,1)S(1)}, bf16[32,2176]{1,0:T(8,128)(2,1)S(1)}, u32[]{:S(2)}, u32[]{:S(2)}) collective-permute-start(bf16[32,2176]{1,0:T(8,128)(2,1)S(1)} %pad_maximum_fusion.refs_0_), channel_id=1, source_target_pairs={{0,28},{8,20},{16,12},{24,4},{28,0},{20,8},{12,16},{4,24},{1,29},{... | collective-permute-start | bytes 417800 | tf_op jit(solution)/shard_map/ppermute | solution.py:218
  31.5 0.8 %collective-permute-done.10.refs_3_ = bf16[32,2176]{1,0:T(8,128)(2,1)S(1)} collective-permute-done((bf16[32,2176]{1,0:T(8,128)(2,1)S(1)}, bf16[32,2176]{1,0:T(8,128)(2,1)S(1)}, u32[]{:S(2)}, u32[]{:S(2)}) %collective-permute-start.10) | collective-permute-done | bytes 139296 | tf_op jit(solution)/shard_map/ppermute | solution.py:218
  32.3 1.5 %collective-permute-start.11 = (bf16[32,2176]{1,0:T(8,128)(2,1)S(1)}, bf16[32,2176]{1,0:T(8,128)(2,1)S(1)}, u32[]{:S(2)}, u32[]{:S(2)}) collective-permute-start(bf16[32,2176]{1,0:T(8,128)(2,1)S(1)} %collective-permute-done.10.refs_3_), channel_id=1, source_target_pairs={{0,4},{8,0},{16,8},{24,16},{28,24},{20,28},{12,20},{4,12},{1,5},{9... | collective-permute-start | bytes 417800 | tf_op jit(solution)/shard_map/ppermute | solution.py:218
  33.8 0.0 collective-permute-done.8.after_ref.refs_1_
  33.8 0.6 collective-permute-start.9
  34.3 2.8 %shard_map.105 = (bf16[1024,2048]{1,0:T(8,128)(2,1)S(1)}, f32[8,128]{1,0:T(8,128)S(1)}) custom-call(s32[7]{0:T(128)S(1)} %stack.24.scalars, bf16[1,1024,2048]{2,1,0:T(8,128)(2,1)} %source.1, bf16[32,2176]{1,0:T(8,128)(2,1)S(1)} %collective-permute-done.8.after_ref.refs_1_), custom_call_target="tpu_custom_call" | custom-call | bytes 8531996 | tf_op jit(solution)/shard_map/pallas_call | solution.py:24
  37.1 1.9 %collective-permute-done.12.refs_2_ = bf16[32,2176]{1,0:T(8,128)(2,1)S(1)} collective-permute-done((bf16[32,2176]{1,0:T(8,128)(2,1)S(1)}, bf16[32,2176]{1,0:T(8,128)(2,1)S(1)}, u32[]{:S(2)}, u32[]{:S(2)}) %collective-permute-start.12) | collective-permute-done | bytes 139296 | tf_op jit(solution)/shard_map/ppermute | solution.py:218
  38.9 0.8 %collective-permute-done.11.refs_4_ = bf16[32,2176]{1,0:T(8,128)(2,1)S(1)} collective-permute-done((bf16[32,2176]{1,0:T(8,128)(2,1)S(1)}, bf16[32,2176]{1,0:T(8,128)(2,1)S(1)}, u32[]{:S(2)}, u32[]{:S(2)}) %collective-permute-start.11) | collective-permute-done | bytes 139296 | tf_op jit(solution)/shard_map/ppermute | solution.py:218
  39.8 1.1 %collective-permute-done.9.refs_2_ = bf16[32,2176]{1,0:T(8,128)(2,1)S(1)} collective-permute-done((bf16[32,2176]{1,0:T(8,128)(2,1)S(1)}, bf16[32,2176]{1,0:T(8,128)(2,1)S(1)}, u32[]{:S(2)}, u32[]{:S(2)}) %collective-permute-start.9) | collective-permute-done | bytes 139296 | tf_op jit(solution)/shard_map/ppermute | solution.py:218
  40.9 1.5 %collective-permute-start.13 = (bf16[32,2176]{1,0:T(8,128)(2,1)S(1)}, bf16[32,2176]{1,0:T(8,128)(2,1)S(1)}, u32[]{:S(2)}, u32[]{:S(2)}) collective-permute-start(bf16[32,2176]{1,0:T(8,128)(2,1)S(1)} %collective-permute-done.9.refs_2_), channel_id=1, source_target_pairs={{0,8},{8,16},{16,24},{24,28},{28,20},{20,12},{12,4},{4,0},{1,9},{9... | collective-permute-start | bytes 417800 | tf_op jit(solution)/shard_map/ppermute | solution.py:218
  42.3 0.6 collective-permute-start.14
  42.9 2.9 %shard_map.106 = (bf16[32,2048]{1,0:T(8,128)(2,1)S(1)}, bf16[32,2048]{1,0:T(8,128)(2,1)S(1)}, bf16[32,2048]{1,0:T(8,128)(2,1)S(1)}, bf16[32,2048]{1,0:T(8,128)(2...) custom-call(s32[7]{0:T(128)S(1)} %stack.24.scalars, f32[8,128]{1,0:T(8,128)S(1)} %get-tuple-element.71.sign_ref, ...), custom_call_target="tpu_custom_call" | custom-call | flops 2013265920 | bytes 13942812 | tf_op jit(solution)/shard_map/pallas_call | solution.py:24
  45.8 0.2 collective-permute-done.13.refs_0_
  45.9 1.5 %collective-permute-done.14.refs_1_ = bf16[32,2176]{1,0:T(8,128)(2,1)S(1)} collective-permute-done((bf16[32,2176]{1,0:T(8,128)(2,1)S(1)}, bf16[32,2176]{1,0:T(8,128)(2,1)S(1)}, u32[]{:S(2)}, u32[]{:S(2)}) %collective-permute-start.14) | collective-permute-done | bytes 139296 | tf_op jit(solution)/shard_map/ppermute | solution.py:218
  47.4 2.9 %shard_map.107 = (bf16[32,2048]{1,0:T(8,128)(2,1)S(1)}, bf16[32,2048]{1,0:T(8,128)(2,1)S(1)}, bf16[32,2048]{1,0:T(8,128)(2,1)S(1)}, f32[8,128]{1,0:T(8,128)}) custom-call(s32[7]{0:T(128)S(1)} %stack.24.scalars, f32[8,128]{1,0:T(8,128)S(1)} %get-tuple-element.80.sign_ref, bf16[2048,1024]{1,0:T(8,128)(2,1)S(1)} %get-tuple-element.72.gate_ref, ...), custom_call_target="tpu_custom_call" | custom-call | flops 1610612736 | bytes 13402140 | tf_op jit(solution)/shard_map/pallas_call | solution.py:24
  50.3 1.5 %collective-permute-start.15 = (bf16[32,2048]{1,0:T(8,128)(2,1)S(1)}, bf16[32,2048]{1,0:T(8,128)(2,1)S(1)}, u32[]{:S(2)}, u32[]{:S(2)}) collective-permute-start(bf16[32,2048]{1,0:T(8,128)(2,1)S(1)} %get-tuple-element.84), channel_id=1, source_target_pairs={{0,8},{8,16},{16,24},{24,28},{28,20},{20,12},{12,4},{4,0},{1,9},{9... | collective-permute-start | bytes 393224 | tf_op jit(solution)/shard_map/ppermute | solution.py:218
  51.9 0.5 collective-permute-start.18
  52.4 3.3 %collective-permute-start.21 = (bf16[32,2048]{1,0:T(8,128)(2,1)S(1)}, bf16[32,2048]{1,0:T(8,128)(2,1)S(1)}, u32[]{:S(2)}, u32[]{:S(2)}) collective-permute-start(bf16[32,2048]{1,0:T(8,128)(2,1)S(1)} %get-tuple-element.90), channel_id=1, source_target_pairs={{0,28},{8,20},{16,12},{24,4},{28,0},{20,8},{12,16},{4,24},{1,29},{... | collective-permute-start | bytes 393224 | tf_op jit(solution)/shard_map/ppermute | solution.py:218
  55.6 0.1 collective-permute-done.15
  55.8 2.5 %collective-permute-start.16 = (bf16[32,2048]{1,0:T(8,128)(2,1)S(1)}, bf16[32,2048]{1,0:T(8,128)(2,1)S(1)}, u32[]{:S(2)}, u32[]{:S(2)}) collective-permute-start(bf16[32,2048]{1,0:T(8,128)(2,1)S(1)} %add_convert_fusion.3), channel_id=1, source_target_pairs={{0,8},{8,16},{16,24},{24,28},{28,20},{20,12},{12,4},{4,0},{1,9},{9... | collective-permute-start | bytes 393224 | tf_op jit(solution)/shard_map/ppermute | solution.py:218
  58.3 0.0 collective-permute-done.18
  58.4 1.9 %collective-permute-start.19 = (bf16[32,2048]{1,0:T(8,128)(2,1)S(1)}, bf16[32,2048]{1,0:T(8,128)(2,1)S(1)}, u32[]{:S(2)}, u32[]{:S(2)}) collective-permute-start(bf16[32,2048]{1,0:T(8,128)(2,1)S(1)} %add_convert_fusion.1), channel_id=1, source_target_pairs={{0,4},{8,0},{16,8},{24,16},{28,24},{20,28},{12,20},{4,12},{1,5},{9... | collective-permute-start | bytes 393224 | tf_op jit(solution)/shard_map/ppermute | solution.py:218
  60.2 2.8 %collective-permute-done.16 = bf16[32,2048]{1,0:T(8,128)(2,1)S(1)} collective-permute-done((bf16[32,2048]{1,0:T(8,128)(2,1)S(1)}, bf16[32,2048]{1,0:T(8,128)(2,1)S(1)}, u32[]{:S(2)}, u32[]{:S(2)}) %collective-permute-start.16) | collective-permute-done | bytes 131104 | tf_op jit(solution)/shard_map/ppermute | solution.py:218
  63.0 0.3 collective-permute-start.17
  63.4 0.6 collective-permute-done.19
  64.0 2.5 %collective-permute-start.20 = (bf16[32,2048]{1,0:T(8,128)(2,1)S(1)}, bf16[32,2048]{1,0:T(8,128)(2,1)S(1)}, u32[]{:S(2)}, u32[]{:S(2)}) collective-permute-start(bf16[32,2048]{1,0:T(8,128)(2,1)S(1)} %add_convert_fusion), channel_id=1, source_target_pairs={{0,4},{8,0},{16,8},{24,16},{28,24},{20,28},{12,20},{4,12},{1,5},{9... | collective-permute-start | bytes 393224 | tf_op jit(solution)/shard_map/ppermute | solution.py:218
  66.6 1.5 %collective-permute-done.17 = bf16[32,2048]{1,0:T(8,128)(2,1)S(1)} collective-permute-done((bf16[32,2048]{1,0:T(8,128)(2,1)S(1)}, bf16[32,2048]{1,0:T(8,128)(2,1)S(1)}, u32[]{:S(2)}, u32[]{:S(2)}) %collective-permute-start.17) | collective-permute-done | bytes 131104 | tf_op jit(solution)/shard_map/ppermute | solution.py:218
  68.1 1.0 %collective-permute-done.20 = bf16[32,2048]{1,0:T(8,128)(2,1)S(1)} collective-permute-done((bf16[32,2048]{1,0:T(8,128)(2,1)S(1)}, bf16[32,2048]{1,0:T(8,128)(2,1)S(1)}, u32[]{:S(2)}, u32[]{:S(2)}) %collective-permute-start.20) | collective-permute-done | bytes 131104 | tf_op jit(solution)/shard_map/ppermute | solution.py:218
  69.1 0.1 fusion.3
  69.2 0.1 collective-permute-start.22
  69.3 1.3 %collective-permute-start.23 = (bf16[32,512]{1,0:T(8,128)(2,1)S(1)}, bf16[32,512]{1,0:T(8,128)(2,1)S(1)}, u32[]{:S(2)}, u32[]{:S(2)}) collective-permute-start(bf16[32,512]{1,0:T(8,128)(2,1)S(1)} %get-tuple-element.102), channel_id=1, source_target_pairs={{0,2},{1,3},{2,0},{3,1},{4,6},{5,7},{6,4},{7,5},{8,10},{9,11},{10,... | collective-permute-start | bytes 98312 | tf_op jit(solution)/shard_map/ppermute | solution.py:316
  70.6 0.5 collective-permute-start.24
  71.1 1.7 %collective-permute-done.22 = bf16[32,512]{1,0:T(8,128)(2,1)S(1)} collective-permute-done((bf16[32,512]{1,0:T(8,128)(2,1)S(1)}, bf16[32,512]{1,0:T(8,128)(2,1)S(1)}, u32[]{:S(2)}, u32[]{:S(2)}) %collective-permute-start.22) | collective-permute-done | bytes 32800 | tf_op jit(solution)/shard_map/ppermute | solution.py:316
  72.8 0.5 collective-permute-done.23
  73.3 0.7 pad_maximum_fusion.2
  (23 shorter events, 0.3 us)
Async XLA Ops:
  0.0 4.9 %copy-start = (f32[128,8]{0,1:T(8,128)S(1)}, f32[128,8]{0,1:T(8,128)}, u32[]{:S(2)}) copy-start(f32[128,8]{0,1:T(8,128)} %param.17) | copy-start | bytes 12292
  1.9 5.3 %collective-permute-start = (bf16[128,256]{1,0:T(8,128)(2,1)S(1)}, bf16[128,256]{1,0:T(8,128)(2,1)S(1)}, u32[]{:S(2)}, u32[]{:S(2)}) collective-permute-start(bf16[128,256]{1,0:T(8,128)(2,1)S(1)} %get-tuple-element.52), channel_id=1, source_target_pairs={{0,4},{4,0},{8,12},{12,8},{16,20},{20,16},{24,28},{28,24},{1,5},{5... | collective-permute-start | bytes 196616 | tf_op jit(solution)/shard_map/ppermute | solution.py:366
  7.2 7.8 %collective-permute-start.1 = (bf16[128,256]{1,0:T(8,128)(2,1)S(1)}, bf16[128,256]{1,0:T(8,128)(2,1)S(1)}, u32[]{:S(2)}, u32[]{:S(2)}) collective-permute-start(bf16[128,256]{1,0:T(8,128)(2,1)S(1)} %fusion.6.after_ref), channel_id=1, source_target_pairs={{0,24},{4,28},{8,16},{12,20},{16,8},{20,12},{24,0},{28,4},{1,25},{... | collective-permute-start | bytes 196616 | tf_op jit(solution)/shard_map/ppermute | solution.py:306
  11.4 5.2 %collective-permute-start.2 = (bf16[128,256]{1,0:T(8,128)(2,1)S(1)}, bf16[128,256]{1,0:T(8,128)(2,1)S(1)}, u32[]{:S(2)}, u32[]{:S(2)}) collective-permute-start(bf16[128,256]{1,0:T(8,128)(2,1)S(1)} %fusion.6.after_ref), channel_id=1, source_target_pairs={{0,16},{4,20},{8,24},{12,28},{16,0},{20,4},{24,8},{28,12},{1,17},{... | collective-permute-start | bytes 196616 | tf_op jit(solution)/shard_map/ppermute | solution.py:306
  11.4 5.2 %collective-permute-start.3 = (bf16[128,256]{1,0:T(8,128)(2,1)S(1)}, bf16[128,256]{1,0:T(8,128)(2,1)S(1)}, u32[]{:S(2)}, u32[]{:S(2)}) collective-permute-start(bf16[128,256]{1,0:T(8,128)(2,1)S(1)} %fusion.6.after_ref), channel_id=1, source_target_pairs={{0,8},{4,12},{8,0},{12,4},{16,24},{20,28},{24,16},{28,20},{1,9},{5... | collective-permute-start | bytes 196616 | tf_op jit(solution)/shard_map/ppermute | solution.py:306
  16.6 4.3 %collective-permute-start.4 = (bf16[128,256]{1,0:T(8,128)(2,1)S(1)}, bf16[128,256]{1,0:T(8,128)(2,1)S(1)}, u32[]{:S(2)}, u32[]{:S(2)}) collective-permute-start(bf16[128,256]{1,0:T(8,128)(2,1)S(1)} %get-tuple-element.62.after_ref), channel_id=1, source_target_pairs={{0,4},{4,0},{8,12},{12,8},{16,20},{20,16},{24,28},{28,24},{1,5},{5... | collective-permute-start | bytes 196616 | tf_op jit(solution)/shard_map/ppermute | solution.py:382
  18.2 8.0 %copy-start.1 = (f32[2048]{0:T(1024)S(1)}, f32[2048]{0:T(1024)}, u32[]{:S(2)}) copy-start(f32[2048]{0:T(1024)} %param.15) | copy-start | bytes 24580
  21.9 3.7 %collective-permute-start.5 = (bf16[32,512]{1,0:T(8,128)(2,1)S(1)}, bf16[32,512]{1,0:T(8,128)(2,1)S(1)}, u32[]{:S(2)}, u32[]{:S(2)}) collective-permute-start(bf16[32,512]{1,0:T(8,128)(2,1)S(1)} %get-tuple-element.65), channel_id=1, source_target_pairs={{0,3},{1,2},{2,1},{3,0},{4,7},{5,6},{6,5},{7,4},{8,11},{9,10},{10,... | collective-permute-start | bytes 98312 | tf_op jit(solution)/shard_map/ppermute | solution.py:316
  22.0 4.0 %collective-permute-start.6 = (bf16[32,512]{1,0:T(8,128)(2,1)S(1)}, bf16[32,512]{1,0:T(8,128)(2,1)S(1)}, u32[]{:S(2)}, u32[]{:S(2)}) collective-permute-start(bf16[32,512]{1,0:T(8,128)(2,1)S(1)} %get-tuple-element.66), channel_id=1, source_target_pairs={{0,2},{1,3},{2,0},{3,1},{4,6},{5,7},{6,4},{7,5},{8,10},{9,11},{10,... | collective-permute-start | bytes 98312 | tf_op jit(solution)/shard_map/ppermute | solution.py:316
  23.5 2.4 %collective-permute-start.7 = (bf16[32,512]{1,0:T(8,128)(2,1)S(1)}, bf16[32,512]{1,0:T(8,128)(2,1)S(1)}, u32[]{:S(2)}, u32[]{:S(2)}) collective-permute-start(bf16[32,512]{1,0:T(8,128)(2,1)S(1)} %get-tuple-element.67), channel_id=1, source_target_pairs={{0,1},{1,0},{2,3},{3,2},{4,5},{5,4},{6,7},{7,6},{8,9},{9,8},{10,11... | collective-permute-start | bytes 98312 | tf_op jit(solution)/shard_map/ppermute | solution.py:316
  26.3 6.0 %collective-permute-start.10 = (bf16[32,2176]{1,0:T(8,128)(2,1)S(1)}, bf16[32,2176]{1,0:T(8,128)(2,1)S(1)}, u32[]{:S(2)}, u32[]{:S(2)}) collective-permute-start(bf16[32,2176]{1,0:T(8,128)(2,1)S(1)} %pad_maximum_fusion.refs_0_), channel_id=1, source_target_pairs={{0,4},{8,0},{16,8},{24,16},{28,24},{20,28},{12,20},{4,12},{1,5},{9... | collective-permute-start | bytes 417800 | tf_op jit(solution)/shard_map/ppermute | solution.py:218
  27.8 5.9 %collective-permute-start.8 = (bf16[32,2176]{1,0:T(8,128)(2,1)S(1)}, bf16[32,2176]{1,0:T(8,128)(2,1)S(1)}, u32[]{:S(2)}, u32[]{:S(2)}) collective-permute-start(bf16[32,2176]{1,0:T(8,128)(2,1)S(1)} %pad_maximum_fusion.refs_0_), channel_id=1, source_target_pairs={{0,8},{8,16},{16,24},{24,28},{28,20},{20,12},{12,4},{4,0},{1,9},{9... | collective-permute-start | bytes 417800 | tf_op jit(solution)/shard_map/ppermute | solution.py:218
  28.4 10.6 %collective-permute-start.12 = (bf16[32,2176]{1,0:T(8,128)(2,1)S(1)}, bf16[32,2176]{1,0:T(8,128)(2,1)S(1)}, u32[]{:S(2)}, u32[]{:S(2)}) collective-permute-start(bf16[32,2176]{1,0:T(8,128)(2,1)S(1)} %pad_maximum_fusion.refs_0_), channel_id=1, source_target_pairs={{0,28},{8,20},{16,12},{24,4},{28,0},{20,8},{12,16},{4,24},{1,29},{... | collective-permute-start | bytes 417800 | tf_op jit(solution)/shard_map/ppermute | solution.py:218
  32.3 7.5 %collective-permute-start.11 = (bf16[32,2176]{1,0:T(8,128)(2,1)S(1)}, bf16[32,2176]{1,0:T(8,128)(2,1)S(1)}, u32[]{:S(2)}, u32[]{:S(2)}) collective-permute-start(bf16[32,2176]{1,0:T(8,128)(2,1)S(1)} %collective-permute-done.10.refs_3_), channel_id=1, source_target_pairs={{0,4},{8,0},{16,8},{24,16},{28,24},{20,28},{12,20},{4,12},{1,5},{9... | collective-permute-start | bytes 417800 | tf_op jit(solution)/shard_map/ppermute | solution.py:218
  33.8 7.1 %collective-permute-start.9 = (bf16[32,2176]{1,0:T(8,128)(2,1)S(1)}, bf16[32,2176]{1,0:T(8,128)(2,1)S(1)}, u32[]{:S(2)}, u32[]{:S(2)}) collective-permute-start(bf16[32,2176]{1,0:T(8,128)(2,1)S(1)} %collective-permute-done.8.after_ref.refs_1_), channel_id=1, source_target_pairs={{0,8},{8,16},{16,24},{24,28},{28,20},{20,12},{12,4},{4,0},{1,9},{9... | collective-permute-start | bytes 417800 | tf_op jit(solution)/shard_map/ppermute | solution.py:218
  40.9 5.1 %collective-permute-start.13 = (bf16[32,2176]{1,0:T(8,128)(2,1)S(1)}, bf16[32,2176]{1,0:T(8,128)(2,1)S(1)}, u32[]{:S(2)}, u32[]{:S(2)}) collective-permute-start(bf16[32,2176]{1,0:T(8,128)(2,1)S(1)} %collective-permute-done.9.refs_2_), channel_id=1, source_target_pairs={{0,8},{8,16},{16,24},{24,28},{28,20},{20,12},{12,4},{4,0},{1,9},{9... | collective-permute-start | bytes 417800 | tf_op jit(solution)/shard_map/ppermute | solution.py:218
  42.3 5.1 %collective-permute-start.14 = (bf16[32,2176]{1,0:T(8,128)(2,1)S(1)}, bf16[32,2176]{1,0:T(8,128)(2,1)S(1)}, u32[]{:S(2)}, u32[]{:S(2)}) collective-permute-start(bf16[32,2176]{1,0:T(8,128)(2,1)S(1)} %collective-permute-done.11.refs_4_), channel_id=1, source_target_pairs={{0,4},{8,0},{16,8},{24,16},{28,24},{20,28},{12,20},{4,12},{1,5},{9... | collective-permute-start | bytes 417800 | tf_op jit(solution)/shard_map/ppermute | solution.py:218
  50.3 5.4 %collective-permute-start.15 = (bf16[32,2048]{1,0:T(8,128)(2,1)S(1)}, bf16[32,2048]{1,0:T(8,128)(2,1)S(1)}, u32[]{:S(2)}, u32[]{:S(2)}) collective-permute-start(bf16[32,2048]{1,0:T(8,128)(2,1)S(1)} %get-tuple-element.84), channel_id=1, source_target_pairs={{0,8},{8,16},{16,24},{24,28},{28,20},{20,12},{12,4},{4,0},{1,9},{9... | collective-permute-start | bytes 393224 | tf_op jit(solution)/shard_map/ppermute | solution.py:218
  51.9 6.5 %collective-permute-start.18 = (bf16[32,2048]{1,0:T(8,128)(2,1)S(1)}, bf16[32,2048]{1,0:T(8,128)(2,1)S(1)}, u32[]{:S(2)}, u32[]{:S(2)}) collective-permute-start(bf16[32,2048]{1,0:T(8,128)(2,1)S(1)} %get-tuple-element.87), channel_id=1, source_target_pairs={{0,4},{8,0},{16,8},{24,16},{28,24},{20,28},{12,20},{4,12},{1,5},{9... | collective-permute-start | bytes 393224 | tf_op jit(solution)/shard_map/ppermute | solution.py:218
  52.4 14.2 %collective-permute-start.21 = (bf16[32,2048]{1,0:T(8,128)(2,1)S(1)}, bf16[32,2048]{1,0:T(8,128)(2,1)S(1)}, u32[]{:S(2)}, u32[]{:S(2)}) collective-permute-start(bf16[32,2048]{1,0:T(8,128)(2,1)S(1)} %get-tuple-element.90), channel_id=1, source_target_pairs={{0,28},{8,20},{16,12},{24,4},{28,0},{20,8},{12,16},{4,24},{1,29},{... | collective-permute-start | bytes 393224 | tf_op jit(solution)/shard_map/ppermute | solution.py:218
  55.8 7.2 %collective-permute-start.16 = (bf16[32,2048]{1,0:T(8,128)(2,1)S(1)}, bf16[32,2048]{1,0:T(8,128)(2,1)S(1)}, u32[]{:S(2)}, u32[]{:S(2)}) collective-permute-start(bf16[32,2048]{1,0:T(8,128)(2,1)S(1)} %add_convert_fusion.3), channel_id=1, source_target_pairs={{0,8},{8,16},{16,24},{24,28},{28,20},{20,12},{12,4},{4,0},{1,9},{9... | collective-permute-start | bytes 393224 | tf_op jit(solution)/shard_map/ppermute | solution.py:218
  58.4 5.6 %collective-permute-start.19 = (bf16[32,2048]{1,0:T(8,128)(2,1)S(1)}, bf16[32,2048]{1,0:T(8,128)(2,1)S(1)}, u32[]{:S(2)}, u32[]{:S(2)}) collective-permute-start(bf16[32,2048]{1,0:T(8,128)(2,1)S(1)} %add_convert_fusion.1), channel_id=1, source_target_pairs={{0,4},{8,0},{16,8},{24,16},{28,24},{20,28},{12,20},{4,12},{1,5},{9... | collective-permute-start | bytes 393224 | tf_op jit(solution)/shard_map/ppermute | solution.py:218
  63.0 5.0 %collective-permute-start.17 = (bf16[32,2048]{1,0:T(8,128)(2,1)S(1)}, bf16[32,2048]{1,0:T(8,128)(2,1)S(1)}, u32[]{:S(2)}, u32[]{:S(2)}) collective-permute-start(bf16[32,2048]{1,0:T(8,128)(2,1)S(1)} %add_convert_fusion.2), channel_id=1, source_target_pairs={{0,8},{8,16},{16,24},{24,28},{28,20},{20,12},{12,4},{4,0},{1,9},{9... | collective-permute-start | bytes 393224 | tf_op jit(solution)/shard_map/ppermute | solution.py:218
  64.0 5.1 %collective-permute-start.20 = (bf16[32,2048]{1,0:T(8,128)(2,1)S(1)}, bf16[32,2048]{1,0:T(8,128)(2,1)S(1)}, u32[]{:S(2)}, u32[]{:S(2)}) collective-permute-start(bf16[32,2048]{1,0:T(8,128)(2,1)S(1)} %add_convert_fusion), channel_id=1, source_target_pairs={{0,4},{8,0},{16,8},{24,16},{28,24},{20,28},{12,20},{4,12},{1,5},{9... | collective-permute-start | bytes 393224 | tf_op jit(solution)/shard_map/ppermute | solution.py:218
  69.2 3.6 %collective-permute-start.22 = (bf16[32,512]{1,0:T(8,128)(2,1)S(1)}, bf16[32,512]{1,0:T(8,128)(2,1)S(1)}, u32[]{:S(2)}, u32[]{:S(2)}) collective-permute-start(bf16[32,512]{1,0:T(8,128)(2,1)S(1)} %get-tuple-element.101), channel_id=1, source_target_pairs={{0,3},{1,2},{2,1},{3,0},{4,7},{5,6},{6,5},{7,4},{8,11},{9,10},{10,... | collective-permute-start | bytes 98312 | tf_op jit(solution)/shard_map/ppermute | solution.py:316
  69.3 4.0 %collective-permute-start.23 = (bf16[32,512]{1,0:T(8,128)(2,1)S(1)}, bf16[32,512]{1,0:T(8,128)(2,1)S(1)}, u32[]{:S(2)}, u32[]{:S(2)}) collective-permute-start(bf16[32,512]{1,0:T(8,128)(2,1)S(1)} %get-tuple-element.102), channel_id=1, source_target_pairs={{0,2},{1,3},{2,0},{3,1},{4,6},{5,7},{6,4},{7,5},{8,10},{9,11},{10,... | collective-permute-start | bytes 98312 | tf_op jit(solution)/shard_map/ppermute | solution.py:316
  70.6 2.7 %collective-permute-start.24 = (bf16[32,512]{1,0:T(8,128)(2,1)S(1)}, bf16[32,512]{1,0:T(8,128)(2,1)S(1)}, u32[]{:S(2)}, u32[]{:S(2)}) collective-permute-start(bf16[32,512]{1,0:T(8,128)(2,1)S(1)} %get-tuple-element.100), channel_id=1, source_target_pairs={{0,1},{1,0},{2,3},{3,2},{4,5},{5,4},{6,7},{7,6},{8,9},{9,8},{10,11... | collective-permute-start | bytes 98312 | tf_op jit(solution)/shard_map/ppermute | solution.py:316

commit v16 on v15

--- a/solution.py
+++ b/solution.py
@@ -225,7 +225,7 @@
         came, went = hop(ahead[-1], 1), hop(behind[-1], -1)
         if distance == far - 2:
             weights_out, sign = load_near(scalars, expert_out, 0, ahead[-1])
-            came, went, sign, farthest = lax.optimization_barrier((came, went, sign, farthest))
+            came, went, sign = lax.optimization_barrier((came, went, sign))
         ahead.append(came)
         behind.append(went)
     last = hop(ahead[-1], 1), hop(behind[-1], -1)

time: 74.1 us -> 74.7 us (level)
  waiting for transfers between devices: 18.6 us -> 21.1 us
  starting transfers between devices: 35 us -> 33.1 us
    ppermute x14, waiting for transfers between devices: 12.3 us -> 14.6 us  [hop(): lax.ppermute(rows, 'seq', [(order[p], order[(p + steps) % count]) for p i...]
    ppermute x14, starting transfers between devices: 21.8 us -> 19.8 us  [hop(): lax.ppermute(rows, 'seq', [(order[p], order[(p + steps) % count]) for p i...]
  transfers between devices with their start and end apart: 25 -> 25, of which waited for: 17 -> 14; matrix products, arithmetic and copies ran while one was open for 2% -> 2% of each run, Pallas kernels for 16% -> 16%
where the time goes in v16:
time: 74.7 us; the launch traced here: 74.5 us
  starting transfers between devices  33.1 us (44%)
  waiting for transfers between devices  21.1 us (28%)
  Pallas kernels  17.7 us (24%)
  other arithmetic  1.4 us (2%)
  local copies, waits for them, and re-layouts  1.09 us (1%)
    ppermute x14, starting transfers between devices, hop(): lax.ppermute(rows, 'seq', [(order[p], order[(p + steps) % count]) for p i...  19.8 us
    pallas_call x8, Pallas kernels, call(): pl.pallas_call(kernel, out_shape=outs, in_specs=[SCALAR if i == 0 or i in...  17.7 us
    ppermute x14, waiting for transfers between devices, hop(): lax.ppermute(rows, 'seq', [(order[p], order[(p + steps) % count]) for p i...  14.6 us
    ppermute x3, starting transfers between devices, prior_states(): lax.ppermute(total, 'seq', [(i, i ^ 2 * distance) for i in range(count)])  4.84 us
    ppermute x6, waiting for transfers between devices, exchange(): lax.ppermute(pieces[j], 'exp', [(i, i ^ j) for i in range(parts)])  4.38 us
    ppermute x6, starting transfers between devices, exchange(): lax.ppermute(pieces[j], 'exp', [(i, i ^ j) for i in range(parts)])  3.84 us
    ppermute x1, starting transfers between devices, per_device(): partner = lax.ppermute(given, 'seq', swap)  3.01 us
    ppermute x3, waiting for transfers between devices, prior_states(): lax.ppermute(total, 'seq', [(i, i ^ 2 * distance) for i in range(count)])  1.6 us
  transfers between devices with their start and end apart: 25, of which 14 were waited for; matrix products, arithmetic and copies ran while one was open for 2% of the time, Pallas kernels for 16%

profile of v16, /device:TPU:0, one launch (start us, length us, event | category | flops | bytes accessed | tf_op | source)
XLA Modules:
  0.0 74.5 jit_solution(5761311740157688493)
XLA Ops:
  0.0 0.1 stack.24.scalars
  0.1 1.8 %shard_map.100 = (bf16[128,256]{1,0:T(8,128)(2,1)S(1)}, bf16[128,256]{1,0:T(8,128)(2,1)S(1)}, bf16[128,512]{1,0:T(8,128)(2,1)S(1)}, bf16[128,512]{1,0:T(8,128)(2...) custom-call(s32[7]{0:T(128)S(1)} %stack.24.scalars, ...), custom_call_target="tpu_custom_call" | custom-call | flops 16777216 | bytes 1188892 | tf_op jit(solution)/shard_map/pallas_call | solution.py:24
  1.9 3.0 %collective-permute-start = (bf16[128,256]{1,0:T(8,128)(2,1)S(1)}, bf16[128,256]{1,0:T(8,128)(2,1)S(1)}, u32[]{:S(2)}, u32[]{:S(2)}) collective-permute-start(bf16[128,256]{1,0:T(8,128)(2,1)S(1)} %get-tuple-element.51), channel_id=1, source_target_pairs={{0,4},{4,0},{8,12},{12,8},{16,20},{20,16},{24,28},{28,24},{1,5},{5... | collective-permute-start | bytes 196616 | tf_op jit(solution)/shard_map/ppermute | solution.py:366
  4.9 0.1 constant_dynamic-slice_fusion
  5.0 0.9 %shard_map.101.within_ref = f32[128,512]{1,0:T(8,128)S(1)} custom-call(s32[7]{0:T(128)S(1)} %stack.24.scalars, bf16[128,512]{1,0:T(8,128)(2,1)S(1)} %get-tuple-element.52.keys, bf16[128,512]{1,0:T(8,128)(2,1)S(1)} %get-tuple-element.53.values, bf16[128,512]{1,0:T(8,128)(2,1)S(1)} %get-tuple-element.54.queries), custom_call_target="tpu_custom_call" | custom-call | flops 50331648 | bytes 655388 | tf_op jit(solution)/shard_map/pallas_call | solution.py:24
  5.9 0.8 %constant_dynamic-slice_fusion.1 = s32[32,8]{0,1:T(8,128)S(1)} fusion(s32[128,8]{0,1:T(8,128)} %param.16, u32[]{:T(128)S(6)} %convert_element_type.87), kind=kLoop, calls=%fused_computation.54 | loop fusion | bytes 2052 | tf_op jit(solution)/shard_map/dynamic_slice | solution.py:396
  6.7 0.5 collective-permute-done
  7.2 4.2 %collective-permute-start.1 = (bf16[128,256]{1,0:T(8,128)(2,1)S(1)}, bf16[128,256]{1,0:T(8,128)(2,1)S(1)}, u32[]{:S(2)}, u32[]{:S(2)}) collective-permute-start(bf16[128,256]{1,0:T(8,128)(2,1)S(1)} %fusion.6.after_ref), channel_id=1, source_target_pairs={{0,24},{4,28},{8,16},{12,20},{16,8},{20,12},{24,0},{28,4},{1,25},{... | collective-permute-start | bytes 196616 | tf_op jit(solution)/shard_map/ppermute | solution.py:306
  11.4 0.6 collective-permute-start.3
  12.0 0.1 copy.16
  12.1 0.1 copy.15
  12.2 2.8 %shard_map.102 = (bf16[2048,1024]{1,0:T(8,128)(2,1)S(1)}, f32[8,128]{1,0:T(8,128)S(1)}) custom-call(s32[7]{0:T(128)S(1)} %stack.24.scalars, bf16[2,2048,1024]{2,1,0:T(8,128)(2,1)} %bitcast.16, bf16[128,256]{1,0:T(8,128)(2,1)S(1)} %fusion.6.after_ref), custom_call_target="tpu_custom_call" | custom-call | bytes 12652572 | tf_op jit(solution)/shard_map/pallas_call | solution.py:24
  15.0 1.6 %collective-permute-done.2 = bf16[128,256]{1,0:T(8,128)(2,1)S(1)} collective-permute-done((bf16[128,256]{1,0:T(8,128)(2,1)S(1)}, bf16[128,256]{1,0:T(8,128)(2,1)S(1)}, u32[]{:S(2)}, u32[]{:S(2)}) %collective-permute-start.2) | collective-permute-done | bytes 65568 | tf_op jit(solution)/shard_map/ppermute | solution.py:306
  16.6 0.0 collective-permute-done.3
  16.6 0.1 fusion.5
  16.6 1.6 %collective-permute-start.4 = (bf16[128,256]{1,0:T(8,128)(2,1)S(1)}, bf16[128,256]{1,0:T(8,128)(2,1)S(1)}, u32[]{:S(2)}, u32[]{:S(2)}) collective-permute-start(bf16[128,256]{1,0:T(8,128)(2,1)S(1)} %get-tuple-element.61.after_ref), channel_id=1, source_target_pairs={{0,4},{4,0},{8,12},{12,8},{16,20},{20,16},{24,28},{28,24},{1,5},{5... | collective-permute-start | bytes 196616 | tf_op jit(solution)/shard_map/ppermute | solution.py:382
  18.2 2.8 %shard_map.103 = (bf16[2048,1024]{1,0:T(8,128)(2,1)S(1)}, f32[8,128]{1,0:T(8,128)S(1)}) custom-call(s32[7]{0:T(128)S(1)} %stack.24.scalars, bf16[2,2048,1024]{2,1,0:T(8,128)(2,1)} %bitcast.17, bf16[128,256]{1,0:T(8,128)(2,1)S(1)} %get-tuple-element.61.after_ref), custom_call_target="tpu_custom_call" | custom-call | bytes 12652572 | tf_op jit(solution)/shard_map/pallas_call | solution.py:24
  21.0 0.0 collective-permute-done.4.other_ref
  21.0 0.9 %shard_map.104 = (bf16[32,512]{1,0:T(8,128)(2,1)S(1)}, bf16[32,512]{1,0:T(8,128)(2,1)S(1)}, bf16[32,512]{1,0:T(8,128)(2,1)S(1)}, bf16[32,512]{1,0:T(8,128)(2,1)S(1)}) custom-call(s32[7]{0:T(128)S(1)} %stack.24.scalars, f32[128,512]{1,0:T(8,128)S(1)} %shard_map.101.within_ref, bf16[128,512]{1,0:T(8,128)(2,1)S(1)} %get-tuple-element.54.queries, ...), custom_call_target="tpu_custom_call" | custom-call | flops 33554432 | bytes 862236 | tf_op jit(solution)/shard_map/pallas_call | solution.py:24
  21.9 0.1 collective-permute-start.5
  22.0 1.6 %collective-permute-start.6 = (bf16[32,512]{1,0:T(8,128)(2,1)S(1)}, bf16[32,512]{1,0:T(8,128)(2,1)S(1)}, u32[]{:S(2)}, u32[]{:S(2)}) collective-permute-start(bf16[32,512]{1,0:T(8,128)(2,1)S(1)} %get-tuple-element.65), channel_id=1, source_target_pairs={{0,2},{1,3},{2,0},{3,1},{4,6},{5,7},{6,4},{7,5},{8,10},{9,11},{10,... | collective-permute-start | bytes 98312 | tf_op jit(solution)/shard_map/ppermute | solution.py:316
  23.5 0.3 collective-permute-start.7
  23.8 0.1 fusion.10
  23.9 1.7 %collective-permute-done.5 = bf16[32,512]{1,0:T(8,128)(2,1)S(1)} collective-permute-done((bf16[32,512]{1,0:T(8,128)(2,1)S(1)}, bf16[32,512]{1,0:T(8,128)(2,1)S(1)}, u32[]{:S(2)}, u32[]{:S(2)}) %collective-permute-start.5) | collective-permute-done | bytes 32800 | tf_op jit(solution)/shard_map/ppermute | solution.py:316
  25.6 0.4 collective-permute-done.6
  26.0 0.0 collective-permute-done.7
  26.0 0.1 fusion
  26.2 0.1 fusion.2
  26.3 1.5 %collective-permute-start.10 = (bf16[32,2176]{1,0:T(8,128)(2,1)S(1)}, bf16[32,2176]{1,0:T(8,128)(2,1)S(1)}, u32[]{:S(2)}, u32[]{:S(2)}) collective-permute-start(bf16[32,2176]{1,0:T(8,128)(2,1)S(1)} %pad_maximum_fusion.refs_0_), channel_id=1, source_target_pairs={{0,4},{8,0},{16,8},{24,16},{28,24},{20,28},{12,20},{4,12},{1,5},{9... | collective-permute-start | bytes 417800 | tf_op jit(solution)/shard_map/ppermute | solution.py:218
  27.8 0.6 collective-permute-start.8
  28.4 3.9 %collective-permute-done.10.refs_3_ = bf16[32,2176]{1,0:T(8,128)(2,1)S(1)} collective-permute-done((bf16[32,2176]{1,0:T(8,128)(2,1)S(1)}, bf16[32,2176]{1,0:T(8,128)(2,1)S(1)}, u32[]{:S(2)}, u32[]{:S(2)}) %collective-permute-start.10) | collective-permute-done | bytes 139296 | tf_op jit(solution)/shard_map/ppermute | solution.py:218
  32.3 1.5 %collective-permute-start.11 = (bf16[32,2176]{1,0:T(8,128)(2,1)S(1)}, bf16[32,2176]{1,0:T(8,128)(2,1)S(1)}, u32[]{:S(2)}, u32[]{:S(2)}) collective-permute-start(bf16[32,2176]{1,0:T(8,128)(2,1)S(1)} %collective-permute-done.10.refs_3_), channel_id=1, source_target_pairs={{0,4},{8,0},{16,8},{24,16},{28,24},{20,28},{12,20},{4,12},{1,5},{9... | collective-permute-start | bytes 417800 | tf_op jit(solution)/shard_map/ppermute | solution.py:218
  33.8 0.0 collective-permute-done.8.after_ref.refs_1_
  33.8 0.6 collective-permute-start.9
  34.3 3.1 %collective-permute-start.14 = (bf16[32,2176]{1,0:T(8,128)(2,1)S(1)}, bf16[32,2176]{1,0:T(8,128)(2,1)S(1)}, u32[]{:S(2)}, u32[]{:S(2)}) collective-permute-start(bf16[32,2176]{1,0:T(8,128)(2,1)S(1)} %pad_maximum_fusion.refs_0_), channel_id=1, source_target_pairs={{0,28},{8,20},{16,12},{24,4},{28,0},{20,8},{12,16},{4,24},{1,29},{... | collective-permute-start | bytes 417800 | tf_op jit(solution)/shard_map/ppermute | solution.py:218
  37.4 2.8 %shard_map.105 = (bf16[1024,2048]{1,0:T(8,128)(2,1)S(1)}, f32[8,128]{1,0:T(8,128)S(1)}) custom-call(s32[7]{0:T(128)S(1)} %stack.24.scalars, bf16[1,1024,2048]{2,1,0:T(8,128)(2,1)} %source.1, bf16[32,2176]{1,0:T(8,128)(2,1)S(1)} %collective-permute-done.8.after_ref.refs_1_), custom_call_target="tpu_custom_call" | custom-call | bytes 8531996 | tf_op jit(solution)/shard_map/pallas_call | solution.py:24
  40.2 0.0 collective-permute-done.9.refs_2_
  40.2 0.4 collective-permute-start.12
  40.6 1.6 %collective-permute-start.13 = (bf16[32,2176]{1,0:T(8,128)(2,1)S(1)}, bf16[32,2176]{1,0:T(8,128)(2,1)S(1)}, u32[]{:S(2)}, u32[]{:S(2)}) collective-permute-start(bf16[32,2176]{1,0:T(8,128)(2,1)S(1)} %collective-permute-done.11.refs_4_), channel_id=1, source_target_pairs={{0,4},{8,0},{16,8},{24,16},{28,24},{20,28},{12,20},{4,12},{1,5},{9... | collective-permute-start | bytes 417800 | tf_op jit(solution)/shard_map/ppermute | solution.py:218
  42.3 2.9 %shard_map.106 = (bf16[32,2048]{1,0:T(8,128)(2,1)S(1)}, bf16[32,2048]{1,0:T(8,128)(2,1)S(1)}, bf16[32,2048]{1,0:T(8,128)(2,1)S(1)}, bf16[32,2048]{1,0:T(8,128)(2...) custom-call(s32[7]{0:T(128)S(1)} %stack.24.scalars, f32[8,128]{1,0:T(8,128)S(1)} %get-tuple-element.70.sign_ref, ...), custom_call_target="tpu_custom_call" | custom-call | flops 2013265920 | bytes 13942812 | tf_op jit(solution)/shard_map/pallas_call | solution.py:24
  45.1 0.9 %collective-permute-done.12.refs_0_ = bf16[32,2176]{1,0:T(8,128)(2,1)S(1)} collective-permute-done((bf16[32,2176]{1,0:T(8,128)(2,1)S(1)}, bf16[32,2176]{1,0:T(8,128)(2,1)S(1)}, u32[]{:S(2)}, u32[]{:S(2)}) %collective-permute-start.12) | collective-permute-done | bytes 139296 | tf_op jit(solution)/shard_map/ppermute | solution.py:218
  46.0 0.8 %collective-permute-done.13.refs_1_ = bf16[32,2176]{1,0:T(8,128)(2,1)S(1)} collective-permute-done((bf16[32,2176]{1,0:T(8,128)(2,1)S(1)}, bf16[32,2176]{1,0:T(8,128)(2,1)S(1)}, u32[]{:S(2)}, u32[]{:S(2)}) %collective-permute-start.13) | collective-permute-done | bytes 139296 | tf_op jit(solution)/shard_map/ppermute | solution.py:218
  46.8 2.9 %shard_map.107 = (bf16[32,2048]{1,0:T(8,128)(2,1)S(1)}, bf16[32,2048]{1,0:T(8,128)(2,1)S(1)}, bf16[32,2048]{1,0:T(8,128)(2,1)S(1)}, f32[8,128]{1,0:T(8,128)}) custom-call(s32[7]{0:T(128)S(1)} %stack.24.scalars, f32[8,128]{1,0:T(8,128)S(1)} %get-tuple-element.78.sign_ref, bf16[2048,1024]{1,0:T(8,128)(2,1)S(1)} %get-tuple-element.71.gate_ref, ...), custom_call_target="tpu_custom_call" | custom-call | flops 1610612736 | bytes 13402140 | tf_op jit(solution)/shard_map/pallas_call | solution.py:24
  49.7 2.0 %collective-permute-start.15 = (bf16[32,2048]{1,0:T(8,128)(2,1)S(1)}, bf16[32,2048]{1,0:T(8,128)(2,1)S(1)}, u32[]{:S(2)}, u32[]{:S(2)}) collective-permute-start(bf16[32,2048]{1,0:T(8,128)(2,1)S(1)} %get-tuple-element.82), channel_id=1, source_target_pairs={{0,8},{8,16},{16,24},{24,28},{28,20},{20,12},{12,4},{4,0},{1,9},{9... | collective-permute-start | bytes 393224 | tf_op jit(solution)/shard_map/ppermute | solution.py:218
  51.7 4.6 %collective-permute-start.21 = (bf16[32,2048]{1,0:T(8,128)(2,1)S(1)}, bf16[32,2048]{1,0:T(8,128)(2,1)S(1)}, u32[]{:S(2)}, u32[]{:S(2)}) collective-permute-start(bf16[32,2048]{1,0:T(8,128)(2,1)S(1)} %get-tuple-element.88), channel_id=1, source_target_pairs={{0,28},{8,20},{16,12},{24,4},{28,0},{20,8},{12,16},{4,24},{1,29},{... | collective-permute-start | bytes 393224 | tf_op jit(solution)/shard_map/ppermute | solution.py:218
  56.3 0.1 collective-permute-done.15
  56.5 1.6 %collective-permute-start.16 = (bf16[32,2048]{1,0:T(8,128)(2,1)S(1)}, bf16[32,2048]{1,0:T(8,128)(2,1)S(1)}, u32[]{:S(2)}, u32[]{:S(2)}) collective-permute-start(bf16[32,2048]{1,0:T(8,128)(2,1)S(1)} %add_convert_fusion.3), channel_id=1, source_target_pairs={{0,8},{8,16},{16,24},{24,28},{28,20},{20,12},{12,4},{4,0},{1,9},{9... | collective-permute-start | bytes 393224 | tf_op jit(solution)/shard_map/ppermute | solution.py:218
  58.1 0.8 %collective-permute-done.18 = bf16[32,2048]{1,0:T(8,128)(2,1)S(1)} collective-permute-done((bf16[32,2048]{1,0:T(8,128)(2,1)S(1)}, bf16[32,2048]{1,0:T(8,128)(2,1)S(1)}, u32[]{:S(2)}, u32[]{:S(2)}) %collective-permute-start.18) | collective-permute-done | bytes 131104 | tf_op jit(solution)/shard_map/ppermute | solution.py:218
  59.0 0.2 collective-permute-start.19
  59.2 4.4 %collective-permute-done.16 = bf16[32,2048]{1,0:T(8,128)(2,1)S(1)} collective-permute-done((bf16[32,2048]{1,0:T(8,128)(2,1)S(1)}, bf16[32,2048]{1,0:T(8,128)(2,1)S(1)}, u32[]{:S(2)}, u32[]{:S(2)}) %collective-permute-start.16) | collective-permute-done | bytes 131104 | tf_op jit(solution)/shard_map/ppermute | solution.py:218
  63.6 0.8 %collective-permute-start.17 = (bf16[32,2048]{1,0:T(8,128)(2,1)S(1)}, bf16[32,2048]{1,0:T(8,128)(2,1)S(1)}, u32[]{:S(2)}, u32[]{:S(2)}) collective-permute-start(bf16[32,2048]{1,0:T(8,128)(2,1)S(1)} %add_convert_fusion.2), channel_id=1, source_target_pairs={{0,8},{8,16},{16,24},{24,28},{28,20},{20,12},{12,4},{4,0},{1,9},{9... | collective-permute-start | bytes 393224 | tf_op jit(solution)/shard_map/ppermute | solution.py:218
  64.5 0.0 collective-permute-done.19
  64.5 1.3 %collective-permute-start.20 = (bf16[32,2048]{1,0:T(8,128)(2,1)S(1)}, bf16[32,2048]{1,0:T(8,128)(2,1)S(1)}, u32[]{:S(2)}, u32[]{:S(2)}) collective-permute-start(bf16[32,2048]{1,0:T(8,128)(2,1)S(1)} %add_convert_fusion), channel_id=1, source_target_pairs={{0,4},{8,0},{16,8},{24,16},{28,24},{20,28},{12,20},{4,12},{1,5},{9... | collective-permute-start | bytes 393224 | tf_op jit(solution)/shard_map/ppermute | solution.py:218
  65.8 0.0 collective-permute-done.21
  65.8 2.8 %collective-permute-done.17 = bf16[32,2048]{1,0:T(8,128)(2,1)S(1)} collective-permute-done((bf16[32,2048]{1,0:T(8,128)(2,1)S(1)}, bf16[32,2048]{1,0:T(8,128)(2,1)S(1)}, u32[]{:S(2)}, u32[]{:S(2)}) %collective-permute-start.17) | collective-permute-done | bytes 131104 | tf_op jit(solution)/shard_map/ppermute | solution.py:218
  68.6 0.9 %collective-permute-done.20 = bf16[32,2048]{1,0:T(8,128)(2,1)S(1)} collective-permute-done((bf16[32,2048]{1,0:T(8,128)(2,1)S(1)}, bf16[32,2048]{1,0:T(8,128)(2,1)S(1)}, u32[]{:S(2)}, u32[]{:S(2)}) %collective-permute-start.20) | collective-permute-done | bytes 131104 | tf_op jit(solution)/shard_map/ppermute | solution.py:218
  69.5 0.1 fusion.3
  69.6 0.1 collective-permute-start.22
  69.7 0.8 %collective-permute-start.23 = (bf16[32,512]{1,0:T(8,128)(2,1)S(1)}, bf16[32,512]{1,0:T(8,128)(2,1)S(1)}, u32[]{:S(2)}, u32[]{:S(2)}) collective-permute-start(bf16[32,512]{1,0:T(8,128)(2,1)S(1)} %get-tuple-element.100), channel_id=1, source_target_pairs={{0,2},{1,3},{2,0},{3,1},{4,6},{5,7},{6,4},{7,5},{8,10},{9,11},{10,... | collective-permute-start | bytes 98312 | tf_op jit(solution)/shard_map/ppermute | solution.py:316
  70.5 1.1 %collective-permute-start.24 = (bf16[32,512]{1,0:T(8,128)(2,1)S(1)}, bf16[32,512]{1,0:T(8,128)(2,1)S(1)}, u32[]{:S(2)}, u32[]{:S(2)}) collective-permute-start(bf16[32,512]{1,0:T(8,128)(2,1)S(1)} %get-tuple-element.98), channel_id=1, source_target_pairs={{0,1},{1,0},{2,3},{3,2},{4,5},{5,4},{6,7},{7,6},{8,9},{9,8},{10,11... | collective-permute-start | bytes 98312 | tf_op jit(solution)/shard_map/ppermute | solution.py:316
  71.6 1.5 %collective-permute-done.22 = bf16[32,512]{1,0:T(8,128)(2,1)S(1)} collective-permute-done((bf16[32,512]{1,0:T(8,128)(2,1)S(1)}, bf16[32,512]{1,0:T(8,128)(2,1)S(1)}, u32[]{:S(2)}, u32[]{:S(2)}) %collective-permute-start.22) | collective-permute-done | bytes 32800 | tf_op jit(solution)/shard_map/ppermute | solution.py:316
  73.1 0.8 %collective-permute-done.23 = bf16[32,512]{1,0:T(8,128)(2,1)S(1)} collective-permute-done((bf16[32,512]{1,0:T(8,128)(2,1)S(1)}, bf16[32,512]{1,0:T(8,128)(2,1)S(1)}, u32[]{:S(2)}, u32[]{:S(2)}) %collective-permute-start.23) | collective-permute-done | bytes 32800 | tf_op jit(solution)/shard_map/ppermute | solution.py:316
  73.9 0.0 collective-permute-done.24
  73.9 0.7 pad_maximum_fusion.2
  (23 shorter events, 0.3 us)
Async XLA Ops:
  0.0 4.9 %copy-start = (f32[128,8]{0,1:T(8,128)S(1)}, f32[128,8]{0,1:T(8,128)}, u32[]{:S(2)}) copy-start(f32[128,8]{0,1:T(8,128)} %param.17) | copy-start | bytes 12292
  1.9 5.3 %collective-permute-start = (bf16[128,256]{1,0:T(8,128)(2,1)S(1)}, bf16[128,256]{1,0:T(8,128)(2,1)S(1)}, u32[]{:S(2)}, u32[]{:S(2)}) collective-permute-start(bf16[128,256]{1,0:T(8,128)(2,1)S(1)} %get-tuple-element.51), channel_id=1, source_target_pairs={{0,4},{4,0},{8,12},{12,8},{16,20},{20,16},{24,28},{28,24},{1,5},{5... | collective-permute-start | bytes 196616 | tf_op jit(solution)/shard_map/ppermute | solution.py:366
  7.2 7.8 %collective-permute-start.1 = (bf16[128,256]{1,0:T(8,128)(2,1)S(1)}, bf16[128,256]{1,0:T(8,128)(2,1)S(1)}, u32[]{:S(2)}, u32[]{:S(2)}) collective-permute-start(bf16[128,256]{1,0:T(8,128)(2,1)S(1)} %fusion.6.after_ref), channel_id=1, source_target_pairs={{0,24},{4,28},{8,16},{12,20},{16,8},{20,12},{24,0},{28,4},{1,25},{... | collective-permute-start | bytes 196616 | tf_op jit(solution)/shard_map/ppermute | solution.py:306
  11.4 5.2 %collective-permute-start.2 = (bf16[128,256]{1,0:T(8,128)(2,1)S(1)}, bf16[128,256]{1,0:T(8,128)(2,1)S(1)}, u32[]{:S(2)}, u32[]{:S(2)}) collective-permute-start(bf16[128,256]{1,0:T(8,128)(2,1)S(1)} %fusion.6.after_ref), channel_id=1, source_target_pairs={{0,16},{4,20},{8,24},{12,28},{16,0},{20,4},{24,8},{28,12},{1,17},{... | collective-permute-start | bytes 196616 | tf_op jit(solution)/shard_map/ppermute | solution.py:306
  11.4 5.2 %collective-permute-start.3 = (bf16[128,256]{1,0:T(8,128)(2,1)S(1)}, bf16[128,256]{1,0:T(8,128)(2,1)S(1)}, u32[]{:S(2)}, u32[]{:S(2)}) collective-permute-start(bf16[128,256]{1,0:T(8,128)(2,1)S(1)} %fusion.6.after_ref), channel_id=1, source_target_pairs={{0,8},{4,12},{8,0},{12,4},{16,24},{20,28},{24,16},{28,20},{1,9},{5... | collective-permute-start | bytes 196616 | tf_op jit(solution)/shard_map/ppermute | solution.py:306
  16.6 4.3 %collective-permute-start.4 = (bf16[128,256]{1,0:T(8,128)(2,1)S(1)}, bf16[128,256]{1,0:T(8,128)(2,1)S(1)}, u32[]{:S(2)}, u32[]{:S(2)}) collective-permute-start(bf16[128,256]{1,0:T(8,128)(2,1)S(1)} %get-tuple-element.61.after_ref), channel_id=1, source_target_pairs={{0,4},{4,0},{8,12},{12,8},{16,20},{20,16},{24,28},{28,24},{1,5},{5... | collective-permute-start | bytes 196616 | tf_op jit(solution)/shard_map/ppermute | solution.py:382
  18.2 8.0 %copy-start.1 = (f32[2048]{0:T(1024)S(1)}, f32[2048]{0:T(1024)}, u32[]{:S(2)}) copy-start(f32[2048]{0:T(1024)} %param.15) | copy-start | bytes 24580
  21.9 3.7 %collective-permute-start.5 = (bf16[32,512]{1,0:T(8,128)(2,1)S(1)}, bf16[32,512]{1,0:T(8,128)(2,1)S(1)}, u32[]{:S(2)}, u32[]{:S(2)}) collective-permute-start(bf16[32,512]{1,0:T(8,128)(2,1)S(1)} %get-tuple-element.64), channel_id=1, source_target_pairs={{0,3},{1,2},{2,1},{3,0},{4,7},{5,6},{6,5},{7,4},{8,11},{9,10},{10,... | collective-permute-start | bytes 98312 | tf_op jit(solution)/shard_map/ppermute | solution.py:316
  22.0 4.0 %collective-permute-start.6 = (bf16[32,512]{1,0:T(8,128)(2,1)S(1)}, bf16[32,512]{1,0:T(8,128)(2,1)S(1)}, u32[]{:S(2)}, u32[]{:S(2)}) collective-permute-start(bf16[32,512]{1,0:T(8,128)(2,1)S(1)} %get-tuple-element.65), channel_id=1, source_target_pairs={{0,2},{1,3},{2,0},{3,1},{4,6},{5,7},{6,4},{7,5},{8,10},{9,11},{10,... | collective-permute-start | bytes 98312 | tf_op jit(solution)/shard_map/ppermute | solution.py:316
  23.5 2.4 %collective-permute-start.7 = (bf16[32,512]{1,0:T(8,128)(2,1)S(1)}, bf16[32,512]{1,0:T(8,128)(2,1)S(1)}, u32[]{:S(2)}, u32[]{:S(2)}) collective-permute-start(bf16[32,512]{1,0:T(8,128)(2,1)S(1)} %get-tuple-element.66), channel_id=1, source_target_pairs={{0,1},{1,0},{2,3},{3,2},{4,5},{5,4},{6,7},{7,6},{8,9},{9,8},{10,11... | collective-permute-start | bytes 98312 | tf_op jit(solution)/shard_map/ppermute | solution.py:316
  26.3 6.0 %collective-permute-start.10 = (bf16[32,2176]{1,0:T(8,128)(2,1)S(1)}, bf16[32,2176]{1,0:T(8,128)(2,1)S(1)}, u32[]{:S(2)}, u32[]{:S(2)}) collective-permute-start(bf16[32,2176]{1,0:T(8,128)(2,1)S(1)} %pad_maximum_fusion.refs_0_), channel_id=1, source_target_pairs={{0,4},{8,0},{16,8},{24,16},{28,24},{20,28},{12,20},{4,12},{1,5},{9... | collective-permute-start | bytes 417800 | tf_op jit(solution)/shard_map/ppermute | solution.py:218
  27.8 5.9 %collective-permute-start.8 = (bf16[32,2176]{1,0:T(8,128)(2,1)S(1)}, bf16[32,2176]{1,0:T(8,128)(2,1)S(1)}, u32[]{:S(2)}, u32[]{:S(2)}) collective-permute-start(bf16[32,2176]{1,0:T(8,128)(2,1)S(1)} %pad_maximum_fusion.refs_0_), channel_id=1, source_target_pairs={{0,8},{8,16},{16,24},{24,28},{28,20},{20,12},{12,4},{4,0},{1,9},{9... | collective-permute-start | bytes 417800 | tf_op jit(solution)/shard_map/ppermute | solution.py:218
  32.3 7.9 %collective-permute-start.11 = (bf16[32,2176]{1,0:T(8,128)(2,1)S(1)}, bf16[32,2176]{1,0:T(8,128)(2,1)S(1)}, u32[]{:S(2)}, u32[]{:S(2)}) collective-permute-start(bf16[32,2176]{1,0:T(8,128)(2,1)S(1)} %collective-permute-done.10.refs_3_), channel_id=1, source_target_pairs={{0,4},{8,0},{16,8},{24,16},{28,24},{20,28},{12,20},{4,12},{1,5},{9... | collective-permute-start | bytes 417800 | tf_op jit(solution)/shard_map/ppermute | solution.py:218
  33.8 6.4 %collective-permute-start.9 = (bf16[32,2176]{1,0:T(8,128)(2,1)S(1)}, bf16[32,2176]{1,0:T(8,128)(2,1)S(1)}, u32[]{:S(2)}, u32[]{:S(2)}) collective-permute-start(bf16[32,2176]{1,0:T(8,128)(2,1)S(1)} %collective-permute-done.8.after_ref.refs_1_), channel_id=1, source_target_pairs={{0,8},{8,16},{16,24},{24,28},{28,20},{20,12},{12,4},{4,0},{1,9},{9... | collective-permute-start | bytes 417800 | tf_op jit(solution)/shard_map/ppermute | solution.py:218
  34.3 10.8 %collective-permute-start.14 = (bf16[32,2176]{1,0:T(8,128)(2,1)S(1)}, bf16[32,2176]{1,0:T(8,128)(2,1)S(1)}, u32[]{:S(2)}, u32[]{:S(2)}) collective-permute-start(bf16[32,2176]{1,0:T(8,128)(2,1)S(1)} %pad_maximum_fusion.refs_0_), channel_id=1, source_target_pairs={{0,28},{8,20},{16,12},{24,4},{28,0},{20,8},{12,16},{4,24},{1,29},{... | collective-permute-start | bytes 417800 | tf_op jit(solution)/shard_map/ppermute | solution.py:218
  40.2 5.8 %collective-permute-start.12 = (bf16[32,2176]{1,0:T(8,128)(2,1)S(1)}, bf16[32,2176]{1,0:T(8,128)(2,1)S(1)}, u32[]{:S(2)}, u32[]{:S(2)}) collective-permute-start(bf16[32,2176]{1,0:T(8,128)(2,1)S(1)} %collective-permute-done.9.refs_2_), channel_id=1, source_target_pairs={{0,8},{8,16},{16,24},{24,28},{28,20},{20,12},{12,4},{4,0},{1,9},{9... | collective-permute-start | bytes 417800 | tf_op jit(solution)/shard_map/ppermute | solution.py:218
  40.6 6.1 %collective-permute-start.13 = (bf16[32,2176]{1,0:T(8,128)(2,1)S(1)}, bf16[32,2176]{1,0:T(8,128)(2,1)S(1)}, u32[]{:S(2)}, u32[]{:S(2)}) collective-permute-start(bf16[32,2176]{1,0:T(8,128)(2,1)S(1)} %collective-permute-done.11.refs_4_), channel_id=1, source_target_pairs={{0,4},{8,0},{16,8},{24,16},{28,24},{20,28},{12,20},{4,12},{1,5},{9... | collective-permute-start | bytes 417800 | tf_op jit(solution)/shard_map/ppermute | solution.py:218
  49.7 6.7 %collective-permute-start.15 = (bf16[32,2048]{1,0:T(8,128)(2,1)S(1)}, bf16[32,2048]{1,0:T(8,128)(2,1)S(1)}, u32[]{:S(2)}, u32[]{:S(2)}) collective-permute-start(bf16[32,2048]{1,0:T(8,128)(2,1)S(1)} %get-tuple-element.82), channel_id=1, source_target_pairs={{0,8},{8,16},{16,24},{24,28},{28,20},{20,12},{12,4},{4,0},{1,9},{9... | collective-permute-start | bytes 393224 | tf_op jit(solution)/shard_map/ppermute | solution.py:218
  51.7 7.2 %collective-permute-start.18 = (bf16[32,2048]{1,0:T(8,128)(2,1)S(1)}, bf16[32,2048]{1,0:T(8,128)(2,1)S(1)}, u32[]{:S(2)}, u32[]{:S(2)}) collective-permute-start(bf16[32,2048]{1,0:T(8,128)(2,1)S(1)} %get-tuple-element.85), channel_id=1, source_target_pairs={{0,4},{8,0},{16,8},{24,16},{28,24},{20,28},{12,20},{4,12},{1,5},{9... | collective-permute-start | bytes 393224 | tf_op jit(solution)/shard_map/ppermute | solution.py:218
  51.7 14.1 %collective-permute-start.21 = (bf16[32,2048]{1,0:T(8,128)(2,1)S(1)}, bf16[32,2048]{1,0:T(8,128)(2,1)S(1)}, u32[]{:S(2)}, u32[]{:S(2)}) collective-permute-start(bf16[32,2048]{1,0:T(8,128)(2,1)S(1)} %get-tuple-element.88), channel_id=1, source_target_pairs={{0,28},{8,20},{16,12},{24,4},{28,0},{20,8},{12,16},{4,24},{1,29},{... | collective-permute-start | bytes 393224 | tf_op jit(solution)/shard_map/ppermute | solution.py:218
  56.5 7.1 %collective-permute-start.16 = (bf16[32,2048]{1,0:T(8,128)(2,1)S(1)}, bf16[32,2048]{1,0:T(8,128)(2,1)S(1)}, u32[]{:S(2)}, u32[]{:S(2)}) collective-permute-start(bf16[32,2048]{1,0:T(8,128)(2,1)S(1)} %add_convert_fusion.3), channel_id=1, source_target_pairs={{0,8},{8,16},{16,24},{24,28},{28,20},{20,12},{12,4},{4,0},{1,9},{9... | collective-permute-start | bytes 393224 | tf_op jit(solution)/shard_map/ppermute | solution.py:218
  59.0 5.5 %collective-permute-start.19 = (bf16[32,2048]{1,0:T(8,128)(2,1)S(1)}, bf16[32,2048]{1,0:T(8,128)(2,1)S(1)}, u32[]{:S(2)}, u32[]{:S(2)}) collective-permute-start(bf16[32,2048]{1,0:T(8,128)(2,1)S(1)} %add_convert_fusion.1), channel_id=1, source_target_pairs={{0,4},{8,0},{16,8},{24,16},{28,24},{20,28},{12,20},{4,12},{1,5},{9... | collective-permute-start | bytes 393224 | tf_op jit(solution)/shard_map/ppermute | solution.py:218
  63.6 5.0 %collective-permute-start.17 = (bf16[32,2048]{1,0:T(8,128)(2,1)S(1)}, bf16[32,2048]{1,0:T(8,128)(2,1)S(1)}, u32[]{:S(2)}, u32[]{:S(2)}) collective-permute-start(bf16[32,2048]{1,0:T(8,128)(2,1)S(1)} %add_convert_fusion.2), channel_id=1, source_target_pairs={{0,8},{8,16},{16,24},{24,28},{28,20},{20,12},{12,4},{4,0},{1,9},{9... | collective-permute-start | bytes 393224 | tf_op jit(solution)/shard_map/ppermute | solution.py:218
  64.5 5.0 %collective-permute-start.20 = (bf16[32,2048]{1,0:T(8,128)(2,1)S(1)}, bf16[32,2048]{1,0:T(8,128)(2,1)S(1)}, u32[]{:S(2)}, u32[]{:S(2)}) collective-permute-start(bf16[32,2048]{1,0:T(8,128)(2,1)S(1)} %add_convert_fusion), channel_id=1, source_target_pairs={{0,4},{8,0},{16,8},{24,16},{28,24},{20,28},{12,20},{4,12},{1,5},{9... | collective-permute-start | bytes 393224 | tf_op jit(solution)/shard_map/ppermute | solution.py:218
  69.6 3.4 %collective-permute-start.22 = (bf16[32,512]{1,0:T(8,128)(2,1)S(1)}, bf16[32,512]{1,0:T(8,128)(2,1)S(1)}, u32[]{:S(2)}, u32[]{:S(2)}) collective-permute-start(bf16[32,512]{1,0:T(8,128)(2,1)S(1)} %get-tuple-element.99), channel_id=1, source_target_pairs={{0,3},{1,2},{2,1},{3,0},{4,7},{5,6},{6,5},{7,4},{8,11},{9,10},{10,... | collective-permute-start | bytes 98312 | tf_op jit(solution)/shard_map/ppermute | solution.py:316
  69.7 4.1 %collective-permute-start.23 = (bf16[32,512]{1,0:T(8,128)(2,1)S(1)}, bf16[32,512]{1,0:T(8,128)(2,1)S(1)}, u32[]{:S(2)}, u32[]{:S(2)}) collective-permute-start(bf16[32,512]{1,0:T(8,128)(2,1)S(1)} %get-tuple-element.100), channel_id=1, source_target_pairs={{0,2},{1,3},{2,0},{3,1},{4,6},{5,7},{6,4},{7,5},{8,10},{9,11},{10,... | collective-permute-start | bytes 98312 | tf_op jit(solution)/shard_map/ppermute | solution.py:316
  70.5 3.3 %collective-permute-start.24 = (bf16[32,512]{1,0:T(8,128)(2,1)S(1)}, bf16[32,512]{1,0:T(8,128)(2,1)S(1)}, u32[]{:S(2)}, u32[]{:S(2)}) collective-permute-start(bf16[32,512]{1,0:T(8,128)(2,1)S(1)} %get-tuple-element.98), channel_id=1, source_target_pairs={{0,1},{1,0},{2,3},{3,2},{4,5},{5,4},{6,7},{7,6},{8,9},{9,8},{10,11... | collective-permute-start | bytes 98312 | tf_op jit(solution)/shard_map/ppermute | solution.py:316

commit v17 on v16

--- a/solution.py
+++ b/solution.py
@@ -209,8 +209,8 @@
     return list(range(0, count, 2)) + list(range(1, count, 2))[::-1]
 
 
-def dense_experts(block, scalars, weights_gate, weights_up, expert_out):
-    count = lax.axis_size("seq")
+def dense_experts(block, scalars, turns, weights_gate, weights_up, expert_out):
+    count, parts = lax.axis_size("seq"), lax.axis_size("exp")
     order = ring_order(count)
     far = count // 2
 
@@ -219,8 +219,15 @@
             rows, "seq", [(order[p], order[(p + steps) % count]) for p in range(count)]
         )
 
+    def far_hop(rows):
+        pairs = []
+        for p in range(count):
+            for e in range(parts):
+                target = order[(p + (2 if e % 2 == 0 else -2)) % count]
+                pairs.append((order[p] * parts + e, target * parts + e))
+        return lax.ppermute(rows, ("seq", "exp"), pairs)
+
     ahead, behind = [block], [block]
-    farthest = hop(block, far)
     for distance in range(1, far - 1):
         came, went = hop(ahead[-1], 1), hop(behind[-1], -1)
         if distance == far - 2:
@@ -229,6 +236,7 @@
         ahead.append(came)
         behind.append(went)
     last = hop(ahead[-1], 1), hop(behind[-1], -1)
+    farthest = far_hop(jnp.where(turns[0], behind[-1], ahead[-1]))
     weights = weights_gate, weights_up, weights_out
     (own, *near), sign = run_expert(scalars, sign, ahead + behind[1:], *weights)
     *last, farthest, sign = lax.optimization_barrier((*last, farthest, sign))
@@ -418,7 +426,7 @@
     if dense:
         block = jnp.concatenate([normed, pack], axis=1)
         terms = dense_experts(
-            block, scalars, weights_gate, weights_up, expert_out
+            block, scalars, turns, weights_gate, weights_up, expert_out
         )
     else:
         mixed = routed_experts(normed, my_routes, my_gates, expert_in, expert_out)

time: 74.7 us -> 75.1 us (level)
  starting transfers between devices: 33.1 us -> 27.4 us
  waiting for transfers between devices: 21.1 us -> 26.7 us
    ppermute x14 -> x13, starting transfers between devices: 19.8 us -> 13.3 us  [hop(): lax.ppermute(rows, 'seq', [(order[p], order[(p + steps) % count]) for p i...]
    ppermute x0 -> x1, waiting for transfers between devices: none -> 3.7 us  [far_hop(): return lax.ppermute(rows, ('seq', 'exp'), pairs)]
    ppermute x14 -> x13, waiting for transfers between devices: 14.6 us -> 16.7 us  [hop(): lax.ppermute(rows, 'seq', [(order[p], order[(p + steps) % count]) for p i...]
    ppermute x0 -> x1, starting transfers between devices: none -> 0.83 us  [far_hop(): return lax.ppermute(rows, ('seq', 'exp'), pairs)]
  transfers between devices with their start and end apart: 25 -> 25, of which waited for: 14 -> 15; matrix products, arithmetic and copies ran while one was open for 2% -> 2% of each run, Pallas kernels for 16% -> 16%
where the time goes in v17:
time: 75.1 us; the launch traced here: 74.5 us
  starting transfers between devices  27.4 us (36%)
  waiting for transfers between devices  26.7 us (36%)
  Pallas kernels  17.7 us (24%)
  other arithmetic  1.42 us (2%)
  local copies, waits for them, and re-layouts  1.09 us (1%)
    pallas_call x8, Pallas kernels, call(): pl.pallas_call(kernel, out_shape=outs, in_specs=[SCALAR if i == 0 or i in...  17.7 us
    ppermute x13, waiting for transfers between devices, hop(): lax.ppermute(rows, 'seq', [(order[p], order[(p + steps) % count]) for p i...  16.7 us
    ppermute x13, starting transfers between devices, hop(): lax.ppermute(rows, 'seq', [(order[p], order[(p + steps) % count]) for p i...  13.3 us
    ppermute x3, starting transfers between devices, prior_states(): lax.ppermute(total, 'seq', [(i, i ^ 2 * distance) for i in range(count)])  4.84 us
    ppermute x6, waiting for transfers between devices, exchange(): lax.ppermute(pieces[j], 'exp', [(i, i ^ j) for i in range(parts)])  4.28 us
    ppermute x6, starting transfers between devices, exchange(): lax.ppermute(pieces[j], 'exp', [(i, i ^ j) for i in range(parts)])  3.84 us
    ppermute x1, waiting for transfers between devices, far_hop(): return lax.ppermute(rows, ('seq', 'exp'), pairs)  3.7 us
    ppermute x1, starting transfers between devices, per_device(): partner = lax.ppermute(given, 'seq', swap)  3.01 us
  transfers between devices with their start and end apart: 25, of which 15 were waited for; matrix products, arithmetic and copies ran while one was open for 2% of the time, Pallas kernels for 16%

profile of v17, /device:TPU:0, one launch (start us, length us, event | category | flops | bytes accessed | tf_op | source)
XLA Modules:
  0.0 74.5 jit_solution(14562792501688260621)
XLA Ops:
  0.0 0.1 stack.24.scalars
  0.1 1.8 %shard_map.100 = (bf16[128,256]{1,0:T(8,128)(2,1)S(1)}, bf16[128,256]{1,0:T(8,128)(2,1)S(1)}, bf16[128,512]{1,0:T(8,128)(2,1)S(1)}, bf16[128,512]{1,0:T(8,128)(2...) custom-call(s32[7]{0:T(128)S(1)} %stack.24.scalars, ...), custom_call_target="tpu_custom_call" | custom-call | flops 16777216 | bytes 1188892 | tf_op jit(solution)/shard_map/pallas_call | solution.py:24
  1.9 3.0 %collective-permute-start = (bf16[128,256]{1,0:T(8,128)(2,1)S(1)}, bf16[128,256]{1,0:T(8,128)(2,1)S(1)}, u32[]{:S(2)}, u32[]{:S(2)}) collective-permute-start(bf16[128,256]{1,0:T(8,128)(2,1)S(1)} %get-tuple-element.51), channel_id=1, source_target_pairs={{0,4},{4,0},{8,12},{12,8},{16,20},{20,16},{24,28},{28,24},{1,5},{5... | collective-permute-start | bytes 196616 | tf_op jit(solution)/shard_map/ppermute | solution.py:374
  4.9 0.1 constant_dynamic-slice_fusion
  5.0 0.9 %shard_map.101.within_ref = f32[128,512]{1,0:T(8,128)S(1)} custom-call(s32[7]{0:T(128)S(1)} %stack.24.scalars, bf16[128,512]{1,0:T(8,128)(2,1)S(1)} %get-tuple-element.52.keys, bf16[128,512]{1,0:T(8,128)(2,1)S(1)} %get-tuple-element.53.values, bf16[128,512]{1,0:T(8,128)(2,1)S(1)} %get-tuple-element.54.queries), custom_call_target="tpu_custom_call" | custom-call | flops 50331648 | bytes 655388 | tf_op jit(solution)/shard_map/pallas_call | solution.py:24
  5.9 0.8 %constant_dynamic-slice_fusion.1 = s32[32,8]{0,1:T(8,128)S(1)} fusion(s32[128,8]{0,1:T(8,128)} %param.16, u32[]{:T(128)S(6)} %convert_element_type.87), kind=kLoop, calls=%fused_computation.55 | loop fusion | bytes 2052 | tf_op jit(solution)/shard_map/dynamic_slice | solution.py:404
  6.7 0.5 collective-permute-done
  7.2 4.2 %collective-permute-start.1 = (bf16[128,256]{1,0:T(8,128)(2,1)S(1)}, bf16[128,256]{1,0:T(8,128)(2,1)S(1)}, u32[]{:S(2)}, u32[]{:S(2)}) collective-permute-start(bf16[128,256]{1,0:T(8,128)(2,1)S(1)} %fusion.6.after_ref), channel_id=1, source_target_pairs={{0,24},{4,28},{8,16},{12,20},{16,8},{20,12},{24,0},{28,4},{1,25},{... | collective-permute-start | bytes 196616 | tf_op jit(solution)/shard_map/ppermute | solution.py:314
  11.4 0.6 collective-permute-start.3
  12.0 0.1 copy.16
  12.1 0.1 copy.15
  12.2 2.8 %shard_map.102 = (bf16[2048,1024]{1,0:T(8,128)(2,1)S(1)}, f32[8,128]{1,0:T(8,128)S(1)}) custom-call(s32[7]{0:T(128)S(1)} %stack.24.scalars, bf16[2,2048,1024]{2,1,0:T(8,128)(2,1)} %bitcast.16, bf16[128,256]{1,0:T(8,128)(2,1)S(1)} %fusion.6.after_ref), custom_call_target="tpu_custom_call" | custom-call | bytes 12652572 | tf_op jit(solution)/shard_map/pallas_call | solution.py:24
  15.0 1.6 %collective-permute-done.2 = bf16[128,256]{1,0:T(8,128)(2,1)S(1)} collective-permute-done((bf16[128,256]{1,0:T(8,128)(2,1)S(1)}, bf16[128,256]{1,0:T(8,128)(2,1)S(1)}, u32[]{:S(2)}, u32[]{:S(2)}) %collective-permute-start.2) | collective-permute-done | bytes 65568 | tf_op jit(solution)/shard_map/ppermute | solution.py:314
  16.6 0.0 collective-permute-done.3
  16.6 0.1 fusion.5
  16.6 1.6 %collective-permute-start.4 = (bf16[128,256]{1,0:T(8,128)(2,1)S(1)}, bf16[128,256]{1,0:T(8,128)(2,1)S(1)}, u32[]{:S(2)}, u32[]{:S(2)}) collective-permute-start(bf16[128,256]{1,0:T(8,128)(2,1)S(1)} %get-tuple-element.61.after_ref), channel_id=1, source_target_pairs={{0,4},{4,0},{8,12},{12,8},{16,20},{20,16},{24,28},{28,24},{1,5},{5... | collective-permute-start | bytes 196616 | tf_op jit(solution)/shard_map/ppermute | solution.py:390
  18.2 2.8 %shard_map.103 = (bf16[2048,1024]{1,0:T(8,128)(2,1)S(1)}, f32[8,128]{1,0:T(8,128)S(1)}) custom-call(s32[7]{0:T(128)S(1)} %stack.24.scalars, bf16[2,2048,1024]{2,1,0:T(8,128)(2,1)} %bitcast.17, bf16[128,256]{1,0:T(8,128)(2,1)S(1)} %get-tuple-element.61.after_ref), custom_call_target="tpu_custom_call" | custom-call | bytes 12652572 | tf_op jit(solution)/shard_map/pallas_call | solution.py:24
  21.0 0.0 collective-permute-done.4.other_ref
  21.0 0.9 %shard_map.104 = (bf16[32,512]{1,0:T(8,128)(2,1)S(1)}, bf16[32,512]{1,0:T(8,128)(2,1)S(1)}, bf16[32,512]{1,0:T(8,128)(2,1)S(1)}, bf16[32,512]{1,0:T(8,128)(2,1)S(1)}) custom-call(s32[7]{0:T(128)S(1)} %stack.24.scalars, f32[128,512]{1,0:T(8,128)S(1)} %shard_map.101.within_ref, bf16[128,512]{1,0:T(8,128)(2,1)S(1)} %get-tuple-element.54.queries, ...), custom_call_target="tpu_custom_call" | custom-call | flops 33554432 | bytes 862236 | tf_op jit(solution)/shard_map/pallas_call | solution.py:24
  21.9 0.1 collective-permute-start.5
  22.0 1.6 %collective-permute-start.6 = (bf16[32,512]{1,0:T(8,128)(2,1)S(1)}, bf16[32,512]{1,0:T(8,128)(2,1)S(1)}, u32[]{:S(2)}, u32[]{:S(2)}) collective-permute-start(bf16[32,512]{1,0:T(8,128)(2,1)S(1)} %get-tuple-element.65), channel_id=1, source_target_pairs={{0,2},{1,3},{2,0},{3,1},{4,6},{5,7},{6,4},{7,5},{8,10},{9,11},{10,... | collective-permute-start | bytes 98312 | tf_op jit(solution)/shard_map/ppermute | solution.py:324
  23.5 0.3 collective-permute-start.7
  23.8 0.1 fusion.10
  23.9 1.7 %collective-permute-done.5 = bf16[32,512]{1,0:T(8,128)(2,1)S(1)} collective-permute-done((bf16[32,512]{1,0:T(8,128)(2,1)S(1)}, bf16[32,512]{1,0:T(8,128)(2,1)S(1)}, u32[]{:S(2)}, u32[]{:S(2)}) %collective-permute-start.5) | collective-permute-done | bytes 32800 | tf_op jit(solution)/shard_map/ppermute | solution.py:324
  25.6 0.4 collective-permute-done.6
  26.0 0.1 fusion
  26.2 0.1 fusion.2
  26.3 1.5 %collective-permute-start.10 = (bf16[32,2176]{1,0:T(8,128)(2,1)S(1)}, bf16[32,2176]{1,0:T(8,128)(2,1)S(1)}, u32[]{:S(2)}, u32[]{:S(2)}) collective-permute-start(bf16[32,2176]{1,0:T(8,128)(2,1)S(1)} %pad_maximum_fusion.refs_0_), channel_id=1, source_target_pairs={{0,4},{8,0},{16,8},{24,16},{28,24},{20,28},{12,20},{4,12},{1,5},{9... | collective-permute-start | bytes 417800 | tf_op jit(solution)/shard_map/ppermute | solution.py:218
  27.8 0.6 collective-permute-start.8
  28.4 3.9 %collective-permute-done.10.refs_3_ = bf16[32,2176]{1,0:T(8,128)(2,1)S(1)} collective-permute-done((bf16[32,2176]{1,0:T(8,128)(2,1)S(1)}, bf16[32,2176]{1,0:T(8,128)(2,1)S(1)}, u32[]{:S(2)}, u32[]{:S(2)}) %collective-permute-start.10) | collective-permute-done | bytes 139296 | tf_op jit(solution)/shard_map/ppermute | solution.py:218
  32.3 1.5 %collective-permute-start.11 = (bf16[32,2176]{1,0:T(8,128)(2,1)S(1)}, bf16[32,2176]{1,0:T(8,128)(2,1)S(1)}, u32[]{:S(2)}, u32[]{:S(2)}) collective-permute-start(bf16[32,2176]{1,0:T(8,128)(2,1)S(1)} %collective-permute-done.10.refs_3_), channel_id=1, source_target_pairs={{0,4},{8,0},{16,8},{24,16},{28,24},{20,28},{12,20},{4,12},{1,5},{9... | collective-permute-start | bytes 417800 | tf_op jit(solution)/shard_map/ppermute | solution.py:218
  33.8 0.0 collective-permute-done.8.after_ref.refs_1_
  33.8 0.6 collective-permute-start.9
  34.3 2.8 %shard_map.105 = (bf16[1024,2048]{1,0:T(8,128)(2,1)S(1)}, f32[8,128]{1,0:T(8,128)S(1)}) custom-call(s32[7]{0:T(128)S(1)} %stack.24.scalars, bf16[1,1024,2048]{2,1,0:T(8,128)(2,1)} %source.1, bf16[32,2176]{1,0:T(8,128)(2,1)S(1)} %collective-permute-done.8.after_ref.refs_1_), custom_call_target="tpu_custom_call" | custom-call | bytes 8531996 | tf_op jit(solution)/shard_map/pallas_call | solution.py:24
  37.1 0.3 collective-permute-done.11.refs_4_
  37.4 1.4 %collective-permute-done.9.refs_2_ = bf16[32,2176]{1,0:T(8,128)(2,1)S(1)} collective-permute-done((bf16[32,2176]{1,0:T(8,128)(2,1)S(1)}, bf16[32,2176]{1,0:T(8,128)(2,1)S(1)}, u32[]{:S(2)}, u32[]{:S(2)}) %collective-permute-start.9) | collective-permute-done | bytes 139296 | tf_op jit(solution)/shard_map/ppermute | solution.py:218
  38.8 0.6 collective-permute-start.12
  39.4 1.5 %collective-permute-start.13 = (bf16[32,2176]{1,0:T(8,128)(2,1)S(1)}, bf16[32,2176]{1,0:T(8,128)(2,1)S(1)}, u32[]{:S(2)}, u32[]{:S(2)}) collective-permute-start(bf16[32,2176]{1,0:T(8,128)(2,1)S(1)} %collective-permute-done.11.refs_4_), channel_id=1, source_target_pairs={{0,4},{8,0},{16,8},{24,16},{28,24},{20,28},{12,20},{4,12},{1,5},{9... | collective-permute-start | bytes 417800 | tf_op jit(solution)/shard_map/ppermute | solution.py:218
  40.9 0.8 %collective-permute-start.14 = (bf16[32,2176]{1,0:T(8,128)(2,1)S(1)}, bf16[32,2176]{1,0:T(8,128)(2,1)S(1)}, u32[]{:S(2)}, u32[]{:S(2)}) collective-permute-start(bf16[32,2176]{1,0:T(8,128)(2,1)S(1)} %broadcast_select_fusion), channel_id=1, source_target_pairs={{0,16},{1,13},{2,18},{3,15},{8,24},{9,5},{10,26},{11,7},{16,28},{1... | collective-permute-start | bytes 417800 | tf_op jit(solution)/shard_map/ppermute | solution.py:228
  41.8 2.9 %shard_map.106 = (bf16[32,2048]{1,0:T(8,128)(2,1)S(1)}, bf16[32,2048]{1,0:T(8,128)(2,1)S(1)}, bf16[32,2048]{1,0:T(8,128)(2,1)S(1)}, bf16[32,2048]{1,0:T(8,128)(2...) custom-call(s32[7]{0:T(128)S(1)} %stack.24.scalars, f32[8,128]{1,0:T(8,128)S(1)} %get-tuple-element.70.sign_ref, ...), custom_call_target="tpu_custom_call" | custom-call | flops 2013265920 | bytes 13942812 | tf_op jit(solution)/shard_map/pallas_call | solution.py:24
  44.6 3.7 %collective-permute-done.14.refs_2_ = bf16[32,2176]{1,0:T(8,128)(2,1)S(1)} collective-permute-done((bf16[32,2176]{1,0:T(8,128)(2,1)S(1)}, bf16[32,2176]{1,0:T(8,128)(2,1)S(1)}, u32[]{:S(2)}, u32[]{:S(2)}) %collective-permute-start.14) | collective-permute-done | bytes 139296 | tf_op jit(solution)/shard_map/ppermute | solution.py:228
  48.3 0.0 collective-permute-done.12.refs_0_
  48.3 0.0 collective-permute-done.13.refs_1_
  48.3 2.9 %shard_map.107 = (bf16[32,2048]{1,0:T(8,128)(2,1)S(1)}, bf16[32,2048]{1,0:T(8,128)(2,1)S(1)}, bf16[32,2048]{1,0:T(8,128)(2,1)S(1)}, f32[8,128]{1,0:T(8,128)}) custom-call(s32[7]{0:T(128)S(1)} %stack.24.scalars, f32[8,128]{1,0:T(8,128)S(1)} %get-tuple-element.78.sign_ref, bf16[2048,1024]{1,0:T(8,128)(2,1)S(1)} %get-tuple-element.71.gate_ref, ...), custom_call_target="tpu_custom_call" | custom-call | flops 1610612736 | bytes 13402140 | tf_op jit(solution)/shard_map/pallas_call | solution.py:24
  51.3 2.0 %collective-permute-start.18 = (bf16[32,2048]{1,0:T(8,128)(2,1)S(1)}, bf16[32,2048]{1,0:T(8,128)(2,1)S(1)}, u32[]{:S(2)}, u32[]{:S(2)}) collective-permute-start(bf16[32,2048]{1,0:T(8,128)(2,1)S(1)} %get-tuple-element.85), channel_id=1, source_target_pairs={{0,4},{8,0},{16,8},{24,16},{28,24},{20,28},{12,20},{4,12},{1,5},{9... | collective-permute-start | bytes 393224 | tf_op jit(solution)/shard_map/ppermute | solution.py:218
  53.3 1.5 %collective-permute-start.21 = (bf16[32,2048]{1,0:T(8,128)(2,1)S(1)}, bf16[32,2048]{1,0:T(8,128)(2,1)S(1)}, u32[]{:S(2)}, u32[]{:S(2)}) collective-permute-start(bf16[32,2048]{1,0:T(8,128)(2,1)S(1)} %get-tuple-element.88), channel_id=1, source_target_pairs={{0,28},{8,20},{16,12},{24,4},{28,0},{20,8},{12,16},{4,24},{1,29},{... | collective-permute-start | bytes 393224 | tf_op jit(solution)/shard_map/ppermute | solution.py:218
  54.8 3.2 %collective-permute-done.15 = bf16[32,2048]{1,0:T(8,128)(2,1)S(1)} collective-permute-done((bf16[32,2048]{1,0:T(8,128)(2,1)S(1)}, bf16[32,2048]{1,0:T(8,128)(2,1)S(1)}, u32[]{:S(2)}, u32[]{:S(2)}) %collective-permute-start.15) | collective-permute-done | bytes 131104 | tf_op jit(solution)/shard_map/ppermute | solution.py:218
  58.0 0.1 collective-permute-start.16
  58.1 0.8 %collective-permute-done.18 = bf16[32,2048]{1,0:T(8,128)(2,1)S(1)} collective-permute-done((bf16[32,2048]{1,0:T(8,128)(2,1)S(1)}, bf16[32,2048]{1,0:T(8,128)(2,1)S(1)}, u32[]{:S(2)}, u32[]{:S(2)}) %collective-permute-start.18) | collective-permute-done | bytes 131104 | tf_op jit(solution)/shard_map/ppermute | solution.py:218
  58.9 1.4 %collective-permute-start.19 = (bf16[32,2048]{1,0:T(8,128)(2,1)S(1)}, bf16[32,2048]{1,0:T(8,128)(2,1)S(1)}, u32[]{:S(2)}, u32[]{:S(2)}) collective-permute-start(bf16[32,2048]{1,0:T(8,128)(2,1)S(1)} %add_convert_fusion.1), channel_id=1, source_target_pairs={{0,4},{8,0},{16,8},{24,16},{28,24},{20,28},{12,20},{4,12},{1,5},{9... | collective-permute-start | bytes 393224 | tf_op jit(solution)/shard_map/ppermute | solution.py:218
  60.3 4.1 %collective-permute-done.16 = bf16[32,2048]{1,0:T(8,128)(2,1)S(1)} collective-permute-done((bf16[32,2048]{1,0:T(8,128)(2,1)S(1)}, bf16[32,2048]{1,0:T(8,128)(2,1)S(1)}, u32[]{:S(2)}, u32[]{:S(2)}) %collective-permute-start.16) | collective-permute-done | bytes 131104 | tf_op jit(solution)/shard_map/ppermute | solution.py:218
  64.4 0.1 collective-permute-start.17
  64.5 0.0 collective-permute-done.19
  64.6 2.1 %collective-permute-start.20 = (bf16[32,2048]{1,0:T(8,128)(2,1)S(1)}, bf16[32,2048]{1,0:T(8,128)(2,1)S(1)}, u32[]{:S(2)}, u32[]{:S(2)}) collective-permute-start(bf16[32,2048]{1,0:T(8,128)(2,1)S(1)} %add_convert_fusion), channel_id=1, source_target_pairs={{0,4},{8,0},{16,8},{24,16},{28,24},{20,28},{12,20},{4,12},{1,5},{9... | collective-permute-start | bytes 393224 | tf_op jit(solution)/shard_map/ppermute | solution.py:218
  66.6 0.0 collective-permute-done.21
  66.6 2.8 %collective-permute-done.17 = bf16[32,2048]{1,0:T(8,128)(2,1)S(1)} collective-permute-done((bf16[32,2048]{1,0:T(8,128)(2,1)S(1)}, bf16[32,2048]{1,0:T(8,128)(2,1)S(1)}, u32[]{:S(2)}, u32[]{:S(2)}) %collective-permute-start.17) | collective-permute-done | bytes 131104 | tf_op jit(solution)/shard_map/ppermute | solution.py:218
  69.5 0.1 collective-permute-done.20
  69.6 0.1 fusion.3
  69.7 0.1 collective-permute-start.22
  69.8 1.6 %collective-permute-start.23 = (bf16[32,512]{1,0:T(8,128)(2,1)S(1)}, bf16[32,512]{1,0:T(8,128)(2,1)S(1)}, u32[]{:S(2)}, u32[]{:S(2)}) collective-permute-start(bf16[32,512]{1,0:T(8,128)(2,1)S(1)} %get-tuple-element.100), channel_id=1, source_target_pairs={{0,2},{1,3},{2,0},{3,1},{4,6},{5,7},{6,4},{7,5},{8,10},{9,11},{10,... | collective-permute-start | bytes 98312 | tf_op jit(solution)/shard_map/ppermute | solution.py:324
  71.4 0.2 collective-permute-start.24
  71.6 1.7 %collective-permute-done.22 = bf16[32,512]{1,0:T(8,128)(2,1)S(1)} collective-permute-done((bf16[32,512]{1,0:T(8,128)(2,1)S(1)}, bf16[32,512]{1,0:T(8,128)(2,1)S(1)}, u32[]{:S(2)}, u32[]{:S(2)}) %collective-permute-start.22) | collective-permute-done | bytes 32800 | tf_op jit(solution)/shard_map/ppermute | solution.py:324
  73.4 0.4 collective-permute-done.23
  73.8 0.7 pad_maximum_fusion.2
  (24 shorter events, 0.3 us)
Async XLA Ops:
  0.0 4.9 %copy-start = (f32[128,8]{0,1:T(8,128)S(1)}, f32[128,8]{0,1:T(8,128)}, u32[]{:S(2)}) copy-start(f32[128,8]{0,1:T(8,128)} %param.17) | copy-start | bytes 12292
  1.9 5.3 %collective-permute-start = (bf16[128,256]{1,0:T(8,128)(2,1)S(1)}, bf16[128,256]{1,0:T(8,128)(2,1)S(1)}, u32[]{:S(2)}, u32[]{:S(2)}) collective-permute-start(bf16[128,256]{1,0:T(8,128)(2,1)S(1)} %get-tuple-element.51), channel_id=1, source_target_pairs={{0,4},{4,0},{8,12},{12,8},{16,20},{20,16},{24,28},{28,24},{1,5},{5... | collective-permute-start | bytes 196616 | tf_op jit(solution)/shard_map/ppermute | solution.py:374
  7.2 7.8 %collective-permute-start.1 = (bf16[128,256]{1,0:T(8,128)(2,1)S(1)}, bf16[128,256]{1,0:T(8,128)(2,1)S(1)}, u32[]{:S(2)}, u32[]{:S(2)}) collective-permute-start(bf16[128,256]{1,0:T(8,128)(2,1)S(1)} %fusion.6.after_ref), channel_id=1, source_target_pairs={{0,24},{4,28},{8,16},{12,20},{16,8},{20,12},{24,0},{28,4},{1,25},{... | collective-permute-start | bytes 196616 | tf_op jit(solution)/shard_map/ppermute | solution.py:314
  11.4 5.2 %collective-permute-start.2 = (bf16[128,256]{1,0:T(8,128)(2,1)S(1)}, bf16[128,256]{1,0:T(8,128)(2,1)S(1)}, u32[]{:S(2)}, u32[]{:S(2)}) collective-permute-start(bf16[128,256]{1,0:T(8,128)(2,1)S(1)} %fusion.6.after_ref), channel_id=1, source_target_pairs={{0,16},{4,20},{8,24},{12,28},{16,0},{20,4},{24,8},{28,12},{1,17},{... | collective-permute-start | bytes 196616 | tf_op jit(solution)/shard_map/ppermute | solution.py:314
  11.4 5.2 %collective-permute-start.3 = (bf16[128,256]{1,0:T(8,128)(2,1)S(1)}, bf16[128,256]{1,0:T(8,128)(2,1)S(1)}, u32[]{:S(2)}, u32[]{:S(2)}) collective-permute-start(bf16[128,256]{1,0:T(8,128)(2,1)S(1)} %fusion.6.after_ref), channel_id=1, source_target_pairs={{0,8},{4,12},{8,0},{12,4},{16,24},{20,28},{24,16},{28,20},{1,9},{5... | collective-permute-start | bytes 196616 | tf_op jit(solution)/shard_map/ppermute | solution.py:314
  16.6 4.3 %collective-permute-start.4 = (bf16[128,256]{1,0:T(8,128)(2,1)S(1)}, bf16[128,256]{1,0:T(8,128)(2,1)S(1)}, u32[]{:S(2)}, u32[]{:S(2)}) collective-permute-start(bf16[128,256]{1,0:T(8,128)(2,1)S(1)} %get-tuple-element.61.after_ref), channel_id=1, source_target_pairs={{0,4},{4,0},{8,12},{12,8},{16,20},{20,16},{24,28},{28,24},{1,5},{5... | collective-permute-start | bytes 196616 | tf_op jit(solution)/shard_map/ppermute | solution.py:390
  18.2 8.0 %copy-start.1 = (f32[2048]{0:T(1024)S(1)}, f32[2048]{0:T(1024)}, u32[]{:S(2)}) copy-start(f32[2048]{0:T(1024)} %param.15) | copy-start | bytes 24580
  21.9 3.7 %collective-permute-start.5 = (bf16[32,512]{1,0:T(8,128)(2,1)S(1)}, bf16[32,512]{1,0:T(8,128)(2,1)S(1)}, u32[]{:S(2)}, u32[]{:S(2)}) collective-permute-start(bf16[32,512]{1,0:T(8,128)(2,1)S(1)} %get-tuple-element.64), channel_id=1, source_target_pairs={{0,3},{1,2},{2,1},{3,0},{4,7},{5,6},{6,5},{7,4},{8,11},{9,10},{10,... | collective-permute-start | bytes 98312 | tf_op jit(solution)/shard_map/ppermute | solution.py:324
  22.0 4.0 %collective-permute-start.6 = (bf16[32,512]{1,0:T(8,128)(2,1)S(1)}, bf16[32,512]{1,0:T(8,128)(2,1)S(1)}, u32[]{:S(2)}, u32[]{:S(2)}) collective-permute-start(bf16[32,512]{1,0:T(8,128)(2,1)S(1)} %get-tuple-element.65), channel_id=1, source_target_pairs={{0,2},{1,3},{2,0},{3,1},{4,6},{5,7},{6,4},{7,5},{8,10},{9,11},{10,... | collective-permute-start | bytes 98312 | tf_op jit(solution)/shard_map/ppermute | solution.py:324
  23.5 2.4 %collective-permute-start.7 = (bf16[32,512]{1,0:T(8,128)(2,1)S(1)}, bf16[32,512]{1,0:T(8,128)(2,1)S(1)}, u32[]{:S(2)}, u32[]{:S(2)}) collective-permute-start(bf16[32,512]{1,0:T(8,128)(2,1)S(1)} %get-tuple-element.66), channel_id=1, source_target_pairs={{0,1},{1,0},{2,3},{3,2},{4,5},{5,4},{6,7},{7,6},{8,9},{9,8},{10,11... | collective-permute-start | bytes 98312 | tf_op jit(solution)/shard_map/ppermute | solution.py:324
  26.3 6.0 %collective-permute-start.10 = (bf16[32,2176]{1,0:T(8,128)(2,1)S(1)}, bf16[32,2176]{1,0:T(8,128)(2,1)S(1)}, u32[]{:S(2)}, u32[]{:S(2)}) collective-permute-start(bf16[32,2176]{1,0:T(8,128)(2,1)S(1)} %pad_maximum_fusion.refs_0_), channel_id=1, source_target_pairs={{0,4},{8,0},{16,8},{24,16},{28,24},{20,28},{12,20},{4,12},{1,5},{9... | collective-permute-start | bytes 417800 | tf_op jit(solution)/shard_map/ppermute | solution.py:218
  27.8 5.9 %collective-permute-start.8 = (bf16[32,2176]{1,0:T(8,128)(2,1)S(1)}, bf16[32,2176]{1,0:T(8,128)(2,1)S(1)}, u32[]{:S(2)}, u32[]{:S(2)}) collective-permute-start(bf16[32,2176]{1,0:T(8,128)(2,1)S(1)} %pad_maximum_fusion.refs_0_), channel_id=1, source_target_pairs={{0,8},{8,16},{16,24},{24,28},{28,20},{20,12},{12,4},{4,0},{1,9},{9... | collective-permute-start | bytes 417800 | tf_op jit(solution)/shard_map/ppermute | solution.py:218
  32.3 5.1 %collective-permute-start.11 = (bf16[32,2176]{1,0:T(8,128)(2,1)S(1)}, bf16[32,2176]{1,0:T(8,128)(2,1)S(1)}, u32[]{:S(2)}, u32[]{:S(2)}) collective-permute-start(bf16[32,2176]{1,0:T(8,128)(2,1)S(1)} %collective-permute-done.10.refs_3_), channel_id=1, source_target_pairs={{0,4},{8,0},{16,8},{24,16},{28,24},{20,28},{12,20},{4,12},{1,5},{9... | collective-permute-start | bytes 417800 | tf_op jit(solution)/shard_map/ppermute | solution.py:218
  33.8 5.1 %collective-permute-start.9 = (bf16[32,2176]{1,0:T(8,128)(2,1)S(1)}, bf16[32,2176]{1,0:T(8,128)(2,1)S(1)}, u32[]{:S(2)}, u32[]{:S(2)}) collective-permute-start(bf16[32,2176]{1,0:T(8,128)(2,1)S(1)} %collective-permute-done.8.after_ref.refs_1_), channel_id=1, source_target_pairs={{0,8},{8,16},{16,24},{24,28},{28,20},{20,12},{12,4},{4,0},{1,9},{9... | collective-permute-start | bytes 417800 | tf_op jit(solution)/shard_map/ppermute | solution.py:218
  38.8 9.5 %collective-permute-start.12 = (bf16[32,2176]{1,0:T(8,128)(2,1)S(1)}, bf16[32,2176]{1,0:T(8,128)(2,1)S(1)}, u32[]{:S(2)}, u32[]{:S(2)}) collective-permute-start(bf16[32,2176]{1,0:T(8,128)(2,1)S(1)} %collective-permute-done.9.refs_2_), channel_id=1, source_target_pairs={{0,8},{8,16},{16,24},{24,28},{28,20},{20,12},{12,4},{4,0},{1,9},{9... | collective-permute-start | bytes 417800 | tf_op jit(solution)/shard_map/ppermute | solution.py:218
  39.4 8.9 %collective-permute-start.13 = (bf16[32,2176]{1,0:T(8,128)(2,1)S(1)}, bf16[32,2176]{1,0:T(8,128)(2,1)S(1)}, u32[]{:S(2)}, u32[]{:S(2)}) collective-permute-start(bf16[32,2176]{1,0:T(8,128)(2,1)S(1)} %collective-permute-done.11.refs_4_), channel_id=1, source_target_pairs={{0,4},{8,0},{16,8},{24,16},{28,24},{20,28},{12,20},{4,12},{1,5},{9... | collective-permute-start | bytes 417800 | tf_op jit(solution)/shard_map/ppermute | solution.py:218
  40.9 7.4 %collective-permute-start.14 = (bf16[32,2176]{1,0:T(8,128)(2,1)S(1)}, bf16[32,2176]{1,0:T(8,128)(2,1)S(1)}, u32[]{:S(2)}, u32[]{:S(2)}) collective-permute-start(bf16[32,2176]{1,0:T(8,128)(2,1)S(1)} %broadcast_select_fusion), channel_id=1, source_target_pairs={{0,16},{1,13},{2,18},{3,15},{8,24},{9,5},{10,26},{11,7},{16,28},{1... | collective-permute-start | bytes 417800 | tf_op jit(solution)/shard_map/ppermute | solution.py:228
  51.2 6.7 %collective-permute-start.15 = (bf16[32,2048]{1,0:T(8,128)(2,1)S(1)}, bf16[32,2048]{1,0:T(8,128)(2,1)S(1)}, u32[]{:S(2)}, u32[]{:S(2)}) collective-permute-start(bf16[32,2048]{1,0:T(8,128)(2,1)S(1)} %get-tuple-element.82), channel_id=1, source_target_pairs={{0,8},{8,16},{16,24},{24,28},{28,20},{20,12},{12,4},{4,0},{1,9},{9... | collective-permute-start | bytes 393224 | tf_op jit(solution)/shard_map/ppermute | solution.py:218
  51.3 7.6 %collective-permute-start.18 = (bf16[32,2048]{1,0:T(8,128)(2,1)S(1)}, bf16[32,2048]{1,0:T(8,128)(2,1)S(1)}, u32[]{:S(2)}, u32[]{:S(2)}) collective-permute-start(bf16[32,2048]{1,0:T(8,128)(2,1)S(1)} %get-tuple-element.85), channel_id=1, source_target_pairs={{0,4},{8,0},{16,8},{24,16},{28,24},{20,28},{12,20},{4,12},{1,5},{9... | collective-permute-start | bytes 393224 | tf_op jit(solution)/shard_map/ppermute | solution.py:218
  53.3 13.3 %collective-permute-start.21 = (bf16[32,2048]{1,0:T(8,128)(2,1)S(1)}, bf16[32,2048]{1,0:T(8,128)(2,1)S(1)}, u32[]{:S(2)}, u32[]{:S(2)}) collective-permute-start(bf16[32,2048]{1,0:T(8,128)(2,1)S(1)} %get-tuple-element.88), channel_id=1, source_target_pairs={{0,28},{8,20},{16,12},{24,4},{28,0},{20,8},{12,16},{4,24},{1,29},{... | collective-permute-start | bytes 393224 | tf_op jit(solution)/shard_map/ppermute | solution.py:218
  58.0 6.4 %collective-permute-start.16 = (bf16[32,2048]{1,0:T(8,128)(2,1)S(1)}, bf16[32,2048]{1,0:T(8,128)(2,1)S(1)}, u32[]{:S(2)}, u32[]{:S(2)}) collective-permute-start(bf16[32,2048]{1,0:T(8,128)(2,1)S(1)} %add_convert_fusion.3), channel_id=1, source_target_pairs={{0,8},{8,16},{16,24},{24,28},{28,20},{20,12},{12,4},{4,0},{1,9},{9... | collective-permute-start | bytes 393224 | tf_op jit(solution)/shard_map/ppermute | solution.py:218
  58.9 5.6 %collective-permute-start.19 = (bf16[32,2048]{1,0:T(8,128)(2,1)S(1)}, bf16[32,2048]{1,0:T(8,128)(2,1)S(1)}, u32[]{:S(2)}, u32[]{:S(2)}) collective-permute-start(bf16[32,2048]{1,0:T(8,128)(2,1)S(1)} %add_convert_fusion.1), channel_id=1, source_target_pairs={{0,4},{8,0},{16,8},{24,16},{28,24},{20,28},{12,20},{4,12},{1,5},{9... | collective-permute-start | bytes 393224 | tf_op jit(solution)/shard_map/ppermute | solution.py:218
  64.4 5.0 %collective-permute-start.17 = (bf16[32,2048]{1,0:T(8,128)(2,1)S(1)}, bf16[32,2048]{1,0:T(8,128)(2,1)S(1)}, u32[]{:S(2)}, u32[]{:S(2)}) collective-permute-start(bf16[32,2048]{1,0:T(8,128)(2,1)S(1)} %add_convert_fusion.2), channel_id=1, source_target_pairs={{0,8},{8,16},{16,24},{24,28},{28,20},{20,12},{12,4},{4,0},{1,9},{9... | collective-permute-start | bytes 393224 | tf_op jit(solution)/shard_map/ppermute | solution.py:218
  64.6 5.0 %collective-permute-start.20 = (bf16[32,2048]{1,0:T(8,128)(2,1)S(1)}, bf16[32,2048]{1,0:T(8,128)(2,1)S(1)}, u32[]{:S(2)}, u32[]{:S(2)}) collective-permute-start(bf16[32,2048]{1,0:T(8,128)(2,1)S(1)} %add_convert_fusion), channel_id=1, source_target_pairs={{0,4},{8,0},{16,8},{24,16},{28,24},{20,28},{12,20},{4,12},{1,5},{9... | collective-permute-start | bytes 393224 | tf_op jit(solution)/shard_map/ppermute | solution.py:218
  69.7 3.7 %collective-permute-start.22 = (bf16[32,512]{1,0:T(8,128)(2,1)S(1)}, bf16[32,512]{1,0:T(8,128)(2,1)S(1)}, u32[]{:S(2)}, u32[]{:S(2)}) collective-permute-start(bf16[32,512]{1,0:T(8,128)(2,1)S(1)} %get-tuple-element.99), channel_id=1, source_target_pairs={{0,3},{1,2},{2,1},{3,0},{4,7},{5,6},{6,5},{7,4},{8,11},{9,10},{10,... | collective-permute-start | bytes 98312 | tf_op jit(solution)/shard_map/ppermute | solution.py:324
  69.8 4.0 %collective-permute-start.23 = (bf16[32,512]{1,0:T(8,128)(2,1)S(1)}, bf16[32,512]{1,0:T(8,128)(2,1)S(1)}, u32[]{:S(2)}, u32[]{:S(2)}) collective-permute-start(bf16[32,512]{1,0:T(8,128)(2,1)S(1)} %get-tuple-element.100), channel_id=1, source_target_pairs={{0,2},{1,3},{2,0},{3,1},{4,6},{5,7},{6,4},{7,5},{8,10},{9,11},{10,... | collective-permute-start | bytes 98312 | tf_op jit(solution)/shard_map/ppermute | solution.py:324
  71.4 2.4 %collective-permute-start.24 = (bf16[32,512]{1,0:T(8,128)(2,1)S(1)}, bf16[32,512]{1,0:T(8,128)(2,1)S(1)}, u32[]{:S(2)}, u32[]{:S(2)}) collective-permute-start(bf16[32,512]{1,0:T(8,128)(2,1)S(1)} %get-tuple-element.98), channel_id=1, source_target_pairs={{0,1},{1,0},{2,3},{3,2},{4,5},{5,4},{6,7},{7,6},{8,9},{9,8},{10,11... | collective-permute-start | bytes 98312 | tf_op jit(solution)/shard_map/ppermute | solution.py:324

commit v18 on v15

--- a/solution.py
+++ b/solution.py
@@ -150,7 +150,7 @@
 
 def expert_kernel(blocks, scalars, sign_ref, gate_ref, up_ref, down_ref, *refs):
     x_refs, out_refs, done_ref = refs[:blocks], refs[blocks:2 * blocks], refs[2 * blocks]
-    rows_ref, act_ref, made_ref = refs[2 * blocks + 1:]
+    rows_ref, act_ref = refs[2 * blocks + 1:]
     done_ref[...] = jnp.zeros_like(done_ref)
     model, units = gate_ref.shape
     spans, packs = [], []
@@ -181,10 +181,9 @@
     for step in range(model // wide):
         cut = slice(step * wide, (step + 1) * wide)
         produced = jnp.dot(act_ref[...], down_ref[:, cut], preferred_element_type=F32)
-        made_ref[:, cut] = (produced.astype(BF16).astype(F32) * weight).astype(BF16)
-
-    for out_ref, span in zip(out_refs, spans):
-        out_ref[...] = made_ref[span, :]
+        made = (produced.astype(BF16).astype(F32) * weight).astype(BF16)
+        for out_ref, span in zip(out_refs, spans):
+            out_ref[:, cut] = made[span, :]
 
 
 def run_expert(scalars, sign, blocks, weights_gate, weights_up, weights_out):
@@ -197,7 +196,6 @@
         scratch=[
             pltpu.VMEM((total, model), BF16),
             pltpu.VMEM((total, units), BF16),
-            pltpu.VMEM((total, model), BF16),
         ],
         flops=6 * total * model * units,
         limit=24 << 20,

time: 74.1 us -> 74.1 us (level)
  no operation moved by 1% of the time
where the time goes in v18:
time: 74.1 us; the launch traced here: 74 us
  starting transfers between devices  35 us (47%)
  waiting for transfers between devices  18.6 us (25%)
  Pallas kernels  17.7 us (24%)
  other arithmetic  1.4 us (2%)
  local copies, waits for them, and re-layouts  1.09 us (1%)
    ppermute x14, starting transfers between devices, hop(): lax.ppermute(rows, 'seq', [(order[p], order[(p + steps) % count]) for p i...  21.8 us
    pallas_call x8, Pallas kernels, call(): pl.pallas_call(kernel, out_shape=outs, in_specs=[SCALAR if i == 0 or i in...  17.7 us
    ppermute x14, waiting for transfers between devices, hop(): lax.ppermute(rows, 'seq', [(order[p], order[(p + steps) % count]) for p i...  12.3 us
    ppermute x3, starting transfers between devices, prior_states(): lax.ppermute(total, 'seq', [(i, i ^ 2 * distance) for i in range(count)])  4.84 us
    ppermute x6, waiting for transfers between devices, exchange(): lax.ppermute(pieces[j], 'exp', [(i, i ^ j) for i in range(parts)])  4.25 us
    ppermute x6, starting transfers between devices, exchange(): lax.ppermute(pieces[j], 'exp', [(i, i ^ j) for i in range(parts)])  3.84 us
    ppermute x1, starting transfers between devices, per_device(): partner = lax.ppermute(given, 'seq', swap)  3.01 us
    ppermute x3, waiting for transfers between devices, prior_states(): lax.ppermute(total, 'seq', [(i, i ^ 2 * distance) for i in range(count)])  1.6 us
  transfers between devices with their start and end apart: 25, of which 17 were waited for; matrix products, arithmetic and copies ran while one was open for 2% of the time, Pallas kernels for 16%

profile of v18, /device:TPU:0, one launch (start us, length us, event | category | flops | bytes accessed | tf_op | source)
XLA Modules:
  0.0 74.0 jit_solution(14525069946168769716)
XLA Ops:
  0.0 0.1 stack.24.scalars
  0.1 1.8 %shard_map.100 = (bf16[128,256]{1,0:T(8,128)(2,1)S(1)}, bf16[128,256]{1,0:T(8,128)(2,1)S(1)}, bf16[128,512]{1,0:T(8,128)(2,1)S(1)}, bf16[128,512]{1,0:T(8,128)(2...) custom-call(s32[7]{0:T(128)S(1)} %stack.24.scalars, ...), custom_call_target="tpu_custom_call" | custom-call | flops 16777216 | bytes 1188892 | tf_op jit(solution)/shard_map/pallas_call | solution.py:24
  1.9 3.0 %collective-permute-start = (bf16[128,256]{1,0:T(8,128)(2,1)S(1)}, bf16[128,256]{1,0:T(8,128)(2,1)S(1)}, u32[]{:S(2)}, u32[]{:S(2)}) collective-permute-start(bf16[128,256]{1,0:T(8,128)(2,1)S(1)} %get-tuple-element.52), channel_id=1, source_target_pairs={{0,4},{4,0},{8,12},{12,8},{16,20},{20,16},{24,28},{28,24},{1,5},{5... | collective-permute-start | bytes 196616 | tf_op jit(solution)/shard_map/ppermute | solution.py:364
  4.9 0.1 constant_dynamic-slice_fusion
  5.0 0.9 %shard_map.101.within_ref = f32[128,512]{1,0:T(8,128)S(1)} custom-call(s32[7]{0:T(128)S(1)} %stack.24.scalars, bf16[128,512]{1,0:T(8,128)(2,1)S(1)} %get-tuple-element.53.keys, bf16[128,512]{1,0:T(8,128)(2,1)S(1)} %get-tuple-element.54.values, bf16[128,512]{1,0:T(8,128)(2,1)S(1)} %get-tuple-element.55.queries), custom_call_target="tpu_custom_call" | custom-call | flops 50331648 | bytes 655388 | tf_op jit(solution)/shard_map/pallas_call | solution.py:24
  5.9 0.8 %constant_dynamic-slice_fusion.1 = s32[32,8]{0,1:T(8,128)S(1)} fusion(s32[128,8]{0,1:T(8,128)} %param.16, u32[]{:T(128)S(6)} %convert_element_type.87), kind=kLoop, calls=%fused_computation.54 | loop fusion | bytes 2052 | tf_op jit(solution)/shard_map/dynamic_slice | solution.py:394
  6.7 0.5 collective-permute-done
  7.2 4.2 %collective-permute-start.1 = (bf16[128,256]{1,0:T(8,128)(2,1)S(1)}, bf16[128,256]{1,0:T(8,128)(2,1)S(1)}, u32[]{:S(2)}, u32[]{:S(2)}) collective-permute-start(bf16[128,256]{1,0:T(8,128)(2,1)S(1)} %fusion.6.after_ref), channel_id=1, source_target_pairs={{0,24},{4,28},{8,16},{12,20},{16,8},{20,12},{24,0},{28,4},{1,25},{... | collective-permute-start | bytes 196616 | tf_op jit(solution)/shard_map/ppermute | solution.py:304
  11.4 0.0 collective-permute-start.2
  11.4 0.6 collective-permute-start.3
  12.0 0.1 copy.16
  12.1 0.1 copy.15
  12.2 2.8 %shard_map.102 = (bf16[2048,1024]{1,0:T(8,128)(2,1)S(1)}, f32[8,128]{1,0:T(8,128)S(1)}) custom-call(s32[7]{0:T(128)S(1)} %stack.24.scalars, bf16[2,2048,1024]{2,1,0:T(8,128)(2,1)} %bitcast.16, bf16[128,256]{1,0:T(8,128)(2,1)S(1)} %fusion.6.after_ref), custom_call_target="tpu_custom_call" | custom-call | bytes 12652572 | tf_op jit(solution)/shard_map/pallas_call | solution.py:24
  15.0 1.6 %collective-permute-done.2 = bf16[128,256]{1,0:T(8,128)(2,1)S(1)} collective-permute-done((bf16[128,256]{1,0:T(8,128)(2,1)S(1)}, bf16[128,256]{1,0:T(8,128)(2,1)S(1)}, u32[]{:S(2)}, u32[]{:S(2)}) %collective-permute-start.2) | collective-permute-done | bytes 65568 | tf_op jit(solution)/shard_map/ppermute | solution.py:304
  16.6 0.0 collective-permute-done.3
  16.6 0.1 fusion.5
  16.6 1.6 %collective-permute-start.4 = (bf16[128,256]{1,0:T(8,128)(2,1)S(1)}, bf16[128,256]{1,0:T(8,128)(2,1)S(1)}, u32[]{:S(2)}, u32[]{:S(2)}) collective-permute-start(bf16[128,256]{1,0:T(8,128)(2,1)S(1)} %get-tuple-element.62.after_ref), channel_id=1, source_target_pairs={{0,4},{4,0},{8,12},{12,8},{16,20},{20,16},{24,28},{28,24},{1,5},{5... | collective-permute-start | bytes 196616 | tf_op jit(solution)/shard_map/ppermute | solution.py:380
  18.2 2.8 %shard_map.103 = (bf16[2048,1024]{1,0:T(8,128)(2,1)S(1)}, f32[8,128]{1,0:T(8,128)S(1)}) custom-call(s32[7]{0:T(128)S(1)} %stack.24.scalars, bf16[2,2048,1024]{2,1,0:T(8,128)(2,1)} %bitcast.17, bf16[128,256]{1,0:T(8,128)(2,1)S(1)} %get-tuple-element.62.after_ref), custom_call_target="tpu_custom_call" | custom-call | bytes 12652572 | tf_op jit(solution)/shard_map/pallas_call | solution.py:24
  21.0 0.9 %shard_map.104 = (bf16[32,512]{1,0:T(8,128)(2,1)S(1)}, bf16[32,512]{1,0:T(8,128)(2,1)S(1)}, bf16[32,512]{1,0:T(8,128)(2,1)S(1)}, bf16[32,512]{1,0:T(8,128)(2,1)S(1)}) custom-call(s32[7]{0:T(128)S(1)} %stack.24.scalars, f32[128,512]{1,0:T(8,128)S(1)} %shard_map.101.within_ref, bf16[128,512]{1,0:T(8,128)(2,1)S(1)} %get-tuple-element.55.queries, ...), custom_call_target="tpu_custom_call" | custom-call | flops 33554432 | bytes 862236 | tf_op jit(solution)/shard_map/pallas_call | solution.py:24
  21.9 0.1 collective-permute-start.5
  22.0 1.6 %collective-permute-start.6 = (bf16[32,512]{1,0:T(8,128)(2,1)S(1)}, bf16[32,512]{1,0:T(8,128)(2,1)S(1)}, u32[]{:S(2)}, u32[]{:S(2)}) collective-permute-start(bf16[32,512]{1,0:T(8,128)(2,1)S(1)} %get-tuple-element.66), channel_id=1, source_target_pairs={{0,2},{1,3},{2,0},{3,1},{4,6},{5,7},{6,4},{7,5},{8,10},{9,11},{10,... | collective-permute-start | bytes 98312 | tf_op jit(solution)/shard_map/ppermute | solution.py:314
  23.5 0.3 collective-permute-start.7
  23.8 0.1 fusion.10
  23.9 1.7 %collective-permute-done.5 = bf16[32,512]{1,0:T(8,128)(2,1)S(1)} collective-permute-done((bf16[32,512]{1,0:T(8,128)(2,1)S(1)}, bf16[32,512]{1,0:T(8,128)(2,1)S(1)}, u32[]{:S(2)}, u32[]{:S(2)}) %collective-permute-start.5) | collective-permute-done | bytes 32800 | tf_op jit(solution)/shard_map/ppermute | solution.py:314
  25.6 0.4 collective-permute-done.6
  26.0 0.1 fusion
  26.2 0.1 fusion.2
  26.3 1.5 %collective-permute-start.10 = (bf16[32,2176]{1,0:T(8,128)(2,1)S(1)}, bf16[32,2176]{1,0:T(8,128)(2,1)S(1)}, u32[]{:S(2)}, u32[]{:S(2)}) collective-permute-start(bf16[32,2176]{1,0:T(8,128)(2,1)S(1)} %pad_maximum_fusion.refs_0_), channel_id=1, source_target_pairs={{0,4},{8,0},{16,8},{24,16},{28,24},{20,28},{12,20},{4,12},{1,5},{9... | collective-permute-start | bytes 417800 | tf_op jit(solution)/shard_map/ppermute | solution.py:216
  27.8 0.6 collective-permute-start.8
  28.4 3.1 %collective-permute-start.12 = (bf16[32,2176]{1,0:T(8,128)(2,1)S(1)}, bf16[32,2176]{1,0:T(8,128)(2,1)S(1)}, u32[]{:S(2)}, u32[]{:S(2)}) collective-permute-start(bf16[32,2176]{1,0:T(8,128)(2,1)S(1)} %pad_maximum_fusion.refs_0_), channel_id=1, source_target_pairs={{0,28},{8,20},{16,12},{24,4},{28,0},{20,8},{12,16},{4,24},{1,29},{... | collective-permute-start | bytes 417800 | tf_op jit(solution)/shard_map/ppermute | solution.py:216
  31.5 0.8 %collective-permute-done.10.refs_3_ = bf16[32,2176]{1,0:T(8,128)(2,1)S(1)} collective-permute-done((bf16[32,2176]{1,0:T(8,128)(2,1)S(1)}, bf16[32,2176]{1,0:T(8,128)(2,1)S(1)}, u32[]{:S(2)}, u32[]{:S(2)}) %collective-permute-start.10) | collective-permute-done | bytes 139296 | tf_op jit(solution)/shard_map/ppermute | solution.py:216
  32.3 1.5 %collective-permute-start.11 = (bf16[32,2176]{1,0:T(8,128)(2,1)S(1)}, bf16[32,2176]{1,0:T(8,128)(2,1)S(1)}, u32[]{:S(2)}, u32[]{:S(2)}) collective-permute-start(bf16[32,2176]{1,0:T(8,128)(2,1)S(1)} %collective-permute-done.10.refs_3_), channel_id=1, source_target_pairs={{0,4},{8,0},{16,8},{24,16},{28,24},{20,28},{12,20},{4,12},{1,5},{9... | collective-permute-start | bytes 417800 | tf_op jit(solution)/shard_map/ppermute | solution.py:216
  33.8 0.0 collective-permute-done.8.after_ref.refs_1_
  33.8 0.6 collective-permute-start.9
  34.3 2.8 %shard_map.105 = (bf16[1024,2048]{1,0:T(8,128)(2,1)S(1)}, f32[8,128]{1,0:T(8,128)S(1)}) custom-call(s32[7]{0:T(128)S(1)} %stack.24.scalars, bf16[1,1024,2048]{2,1,0:T(8,128)(2,1)} %source.1, bf16[32,2176]{1,0:T(8,128)(2,1)S(1)} %collective-permute-done.8.after_ref.refs_1_), custom_call_target="tpu_custom_call" | custom-call | bytes 8531996 | tf_op jit(solution)/shard_map/pallas_call | solution.py:24
  37.1 1.9 %collective-permute-done.12.refs_2_ = bf16[32,2176]{1,0:T(8,128)(2,1)S(1)} collective-permute-done((bf16[32,2176]{1,0:T(8,128)(2,1)S(1)}, bf16[32,2176]{1,0:T(8,128)(2,1)S(1)}, u32[]{:S(2)}, u32[]{:S(2)}) %collective-permute-start.12) | collective-permute-done | bytes 139296 | tf_op jit(solution)/shard_map/ppermute | solution.py:216
  38.9 0.8 %collective-permute-done.11.refs_4_ = bf16[32,2176]{1,0:T(8,128)(2,1)S(1)} collective-permute-done((bf16[32,2176]{1,0:T(8,128)(2,1)S(1)}, bf16[32,2176]{1,0:T(8,128)(2,1)S(1)}, u32[]{:S(2)}, u32[]{:S(2)}) %collective-permute-start.11) | collective-permute-done | bytes 139296 | tf_op jit(solution)/shard_map/ppermute | solution.py:216
  39.8 1.1 %collective-permute-done.9.refs_2_ = bf16[32,2176]{1,0:T(8,128)(2,1)S(1)} collective-permute-done((bf16[32,2176]{1,0:T(8,128)(2,1)S(1)}, bf16[32,2176]{1,0:T(8,128)(2,1)S(1)}, u32[]{:S(2)}, u32[]{:S(2)}) %collective-permute-start.9) | collective-permute-done | bytes 139296 | tf_op jit(solution)/shard_map/ppermute | solution.py:216
  40.9 1.5 %collective-permute-start.13 = (bf16[32,2176]{1,0:T(8,128)(2,1)S(1)}, bf16[32,2176]{1,0:T(8,128)(2,1)S(1)}, u32[]{:S(2)}, u32[]{:S(2)}) collective-permute-start(bf16[32,2176]{1,0:T(8,128)(2,1)S(1)} %collective-permute-done.9.refs_2_), channel_id=1, source_target_pairs={{0,8},{8,16},{16,24},{24,28},{28,20},{20,12},{12,4},{4,0},{1,9},{9... | collective-permute-start | bytes 417800 | tf_op jit(solution)/shard_map/ppermute | solution.py:216
  42.3 0.6 collective-permute-start.14
  42.9 2.9 %shard_map.106 = (bf16[32,2048]{1,0:T(8,128)(2,1)S(1)}, bf16[32,2048]{1,0:T(8,128)(2,1)S(1)}, bf16[32,2048]{1,0:T(8,128)(2,1)S(1)}, bf16[32,2048]{1,0:T(8,128)(2...) custom-call(s32[7]{0:T(128)S(1)} %stack.24.scalars, f32[8,128]{1,0:T(8,128)S(1)} %get-tuple-element.71.sign_ref, ...), custom_call_target="tpu_custom_call" | custom-call | flops 2013265920 | bytes 13942812 | tf_op jit(solution)/shard_map/pallas_call | solution.py:24
  45.8 0.2 collective-permute-done.13.refs_0_
  45.9 1.5 %collective-permute-done.14.refs_1_ = bf16[32,2176]{1,0:T(8,128)(2,1)S(1)} collective-permute-done((bf16[32,2176]{1,0:T(8,128)(2,1)S(1)}, bf16[32,2176]{1,0:T(8,128)(2,1)S(1)}, u32[]{:S(2)}, u32[]{:S(2)}) %collective-permute-start.14) | collective-permute-done | bytes 139296 | tf_op jit(solution)/shard_map/ppermute | solution.py:216
  47.4 2.9 %shard_map.107 = (bf16[32,2048]{1,0:T(8,128)(2,1)S(1)}, bf16[32,2048]{1,0:T(8,128)(2,1)S(1)}, bf16[32,2048]{1,0:T(8,128)(2,1)S(1)}, f32[8,128]{1,0:T(8,128)}) custom-call(s32[7]{0:T(128)S(1)} %stack.24.scalars, f32[8,128]{1,0:T(8,128)S(1)} %get-tuple-element.80.sign_ref, bf16[2048,1024]{1,0:T(8,128)(2,1)S(1)} %get-tuple-element.72.gate_ref, ...), custom_call_target="tpu_custom_call" | custom-call | flops 1610612736 | bytes 13402140 | tf_op jit(solution)/shard_map/pallas_call | solution.py:24
  50.3 1.5 %collective-permute-start.15 = (bf16[32,2048]{1,0:T(8,128)(2,1)S(1)}, bf16[32,2048]{1,0:T(8,128)(2,1)S(1)}, u32[]{:S(2)}, u32[]{:S(2)}) collective-permute-start(bf16[32,2048]{1,0:T(8,128)(2,1)S(1)} %get-tuple-element.84), channel_id=1, source_target_pairs={{0,8},{8,16},{16,24},{24,28},{28,20},{20,12},{12,4},{4,0},{1,9},{9... | collective-permute-start | bytes 393224 | tf_op jit(solution)/shard_map/ppermute | solution.py:216
  51.9 0.5 collective-permute-start.18
  52.4 3.3 %collective-permute-start.21 = (bf16[32,2048]{1,0:T(8,128)(2,1)S(1)}, bf16[32,2048]{1,0:T(8,128)(2,1)S(1)}, u32[]{:S(2)}, u32[]{:S(2)}) collective-permute-start(bf16[32,2048]{1,0:T(8,128)(2,1)S(1)} %get-tuple-element.90), channel_id=1, source_target_pairs={{0,28},{8,20},{16,12},{24,4},{28,0},{20,8},{12,16},{4,24},{1,29},{... | collective-permute-start | bytes 393224 | tf_op jit(solution)/shard_map/ppermute | solution.py:216
  55.6 0.1 collective-permute-done.15
  55.8 2.5 %collective-permute-start.16 = (bf16[32,2048]{1,0:T(8,128)(2,1)S(1)}, bf16[32,2048]{1,0:T(8,128)(2,1)S(1)}, u32[]{:S(2)}, u32[]{:S(2)}) collective-permute-start(bf16[32,2048]{1,0:T(8,128)(2,1)S(1)} %add_convert_fusion.3), channel_id=1, source_target_pairs={{0,8},{8,16},{16,24},{24,28},{28,20},{20,12},{12,4},{4,0},{1,9},{9... | collective-permute-start | bytes 393224 | tf_op jit(solution)/shard_map/ppermute | solution.py:216
  58.3 0.0 collective-permute-done.18
  58.4 1.9 %collective-permute-start.19 = (bf16[32,2048]{1,0:T(8,128)(2,1)S(1)}, bf16[32,2048]{1,0:T(8,128)(2,1)S(1)}, u32[]{:S(2)}, u32[]{:S(2)}) collective-permute-start(bf16[32,2048]{1,0:T(8,128)(2,1)S(1)} %add_convert_fusion.1), channel_id=1, source_target_pairs={{0,4},{8,0},{16,8},{24,16},{28,24},{20,28},{12,20},{4,12},{1,5},{9... | collective-permute-start | bytes 393224 | tf_op jit(solution)/shard_map/ppermute | solution.py:216
  60.2 2.8 %collective-permute-done.16 = bf16[32,2048]{1,0:T(8,128)(2,1)S(1)} collective-permute-done((bf16[32,2048]{1,0:T(8,128)(2,1)S(1)}, bf16[32,2048]{1,0:T(8,128)(2,1)S(1)}, u32[]{:S(2)}, u32[]{:S(2)}) %collective-permute-start.16) | collective-permute-done | bytes 131104 | tf_op jit(solution)/shard_map/ppermute | solution.py:216
  63.0 0.3 collective-permute-start.17
  63.4 0.6 collective-permute-done.19
  64.0 2.5 %collective-permute-start.20 = (bf16[32,2048]{1,0:T(8,128)(2,1)S(1)}, bf16[32,2048]{1,0:T(8,128)(2,1)S(1)}, u32[]{:S(2)}, u32[]{:S(2)}) collective-permute-start(bf16[32,2048]{1,0:T(8,128)(2,1)S(1)} %add_convert_fusion), channel_id=1, source_target_pairs={{0,4},{8,0},{16,8},{24,16},{28,24},{20,28},{12,20},{4,12},{1,5},{9... | collective-permute-start | bytes 393224 | tf_op jit(solution)/shard_map/ppermute | solution.py:216
  66.6 1.5 %collective-permute-done.17 = bf16[32,2048]{1,0:T(8,128)(2,1)S(1)} collective-permute-done((bf16[32,2048]{1,0:T(8,128)(2,1)S(1)}, bf16[32,2048]{1,0:T(8,128)(2,1)S(1)}, u32[]{:S(2)}, u32[]{:S(2)}) %collective-permute-start.17) | collective-permute-done | bytes 131104 | tf_op jit(solution)/shard_map/ppermute | solution.py:216
  68.1 1.0 %collective-permute-done.20 = bf16[32,2048]{1,0:T(8,128)(2,1)S(1)} collective-permute-done((bf16[32,2048]{1,0:T(8,128)(2,1)S(1)}, bf16[32,2048]{1,0:T(8,128)(2,1)S(1)}, u32[]{:S(2)}, u32[]{:S(2)}) %collective-permute-start.20) | collective-permute-done | bytes 131104 | tf_op jit(solution)/shard_map/ppermute | solution.py:216
  69.1 0.1 fusion.3
  69.2 0.1 collective-permute-start.22
  69.3 1.3 %collective-permute-start.23 = (bf16[32,512]{1,0:T(8,128)(2,1)S(1)}, bf16[32,512]{1,0:T(8,128)(2,1)S(1)}, u32[]{:S(2)}, u32[]{:S(2)}) collective-permute-start(bf16[32,512]{1,0:T(8,128)(2,1)S(1)} %get-tuple-element.102), channel_id=1, source_target_pairs={{0,2},{1,3},{2,0},{3,1},{4,6},{5,7},{6,4},{7,5},{8,10},{9,11},{10,... | collective-permute-start | bytes 98312 | tf_op jit(solution)/shard_map/ppermute | solution.py:314
  70.6 0.5 collective-permute-start.24
  71.1 1.7 %collective-permute-done.22 = bf16[32,512]{1,0:T(8,128)(2,1)S(1)} collective-permute-done((bf16[32,512]{1,0:T(8,128)(2,1)S(1)}, bf16[32,512]{1,0:T(8,128)(2,1)S(1)}, u32[]{:S(2)}, u32[]{:S(2)}) %collective-permute-start.22) | collective-permute-done | bytes 32800 | tf_op jit(solution)/shard_map/ppermute | solution.py:314
  72.8 0.5 collective-permute-done.23
  73.3 0.7 pad_maximum_fusion.2
  (23 shorter events, 0.3 us)
Async XLA Ops:
  0.0 4.9 %copy-start = (f32[128,8]{0,1:T(8,128)S(1)}, f32[128,8]{0,1:T(8,128)}, u32[]{:S(2)}) copy-start(f32[128,8]{0,1:T(8,128)} %param.17) | copy-start | bytes 12292
  1.9 5.3 %collective-permute-start = (bf16[128,256]{1,0:T(8,128)(2,1)S(1)}, bf16[128,256]{1,0:T(8,128)(2,1)S(1)}, u32[]{:S(2)}, u32[]{:S(2)}) collective-permute-start(bf16[128,256]{1,0:T(8,128)(2,1)S(1)} %get-tuple-element.52), channel_id=1, source_target_pairs={{0,4},{4,0},{8,12},{12,8},{16,20},{20,16},{24,28},{28,24},{1,5},{5... | collective-permute-start | bytes 196616 | tf_op jit(solution)/shard_map/ppermute | solution.py:364
  7.2 7.8 %collective-permute-start.1 = (bf16[128,256]{1,0:T(8,128)(2,1)S(1)}, bf16[128,256]{1,0:T(8,128)(2,1)S(1)}, u32[]{:S(2)}, u32[]{:S(2)}) collective-permute-start(bf16[128,256]{1,0:T(8,128)(2,1)S(1)} %fusion.6.after_ref), channel_id=1, source_target_pairs={{0,24},{4,28},{8,16},{12,20},{16,8},{20,12},{24,0},{28,4},{1,25},{... | collective-permute-start | bytes 196616 | tf_op jit(solution)/shard_map/ppermute | solution.py:304
  11.4 5.2 %collective-permute-start.2 = (bf16[128,256]{1,0:T(8,128)(2,1)S(1)}, bf16[128,256]{1,0:T(8,128)(2,1)S(1)}, u32[]{:S(2)}, u32[]{:S(2)}) collective-permute-start(bf16[128,256]{1,0:T(8,128)(2,1)S(1)} %fusion.6.after_ref), channel_id=1, source_target_pairs={{0,16},{4,20},{8,24},{12,28},{16,0},{20,4},{24,8},{28,12},{1,17},{... | collective-permute-start | bytes 196616 | tf_op jit(solution)/shard_map/ppermute | solution.py:304
  11.4 5.2 %collective-permute-start.3 = (bf16[128,256]{1,0:T(8,128)(2,1)S(1)}, bf16[128,256]{1,0:T(8,128)(2,1)S(1)}, u32[]{:S(2)}, u32[]{:S(2)}) collective-permute-start(bf16[128,256]{1,0:T(8,128)(2,1)S(1)} %fusion.6.after_ref), channel_id=1, source_target_pairs={{0,8},{4,12},{8,0},{12,4},{16,24},{20,28},{24,16},{28,20},{1,9},{5... | collective-permute-start | bytes 196616 | tf_op jit(solution)/shard_map/ppermute | solution.py:304
  16.6 4.3 %collective-permute-start.4 = (bf16[128,256]{1,0:T(8,128)(2,1)S(1)}, bf16[128,256]{1,0:T(8,128)(2,1)S(1)}, u32[]{:S(2)}, u32[]{:S(2)}) collective-permute-start(bf16[128,256]{1,0:T(8,128)(2,1)S(1)} %get-tuple-element.62.after_ref), channel_id=1, source_target_pairs={{0,4},{4,0},{8,12},{12,8},{16,20},{20,16},{24,28},{28,24},{1,5},{5... | collective-permute-start | bytes 196616 | tf_op jit(solution)/shard_map/ppermute | solution.py:380
  18.2 8.0 %copy-start.1 = (f32[2048]{0:T(1024)S(1)}, f32[2048]{0:T(1024)}, u32[]{:S(2)}) copy-start(f32[2048]{0:T(1024)} %param.15) | copy-start | bytes 24580
  21.9 3.7 %collective-permute-start.5 = (bf16[32,512]{1,0:T(8,128)(2,1)S(1)}, bf16[32,512]{1,0:T(8,128)(2,1)S(1)}, u32[]{:S(2)}, u32[]{:S(2)}) collective-permute-start(bf16[32,512]{1,0:T(8,128)(2,1)S(1)} %get-tuple-element.65), channel_id=1, source_target_pairs={{0,3},{1,2},{2,1},{3,0},{4,7},{5,6},{6,5},{7,4},{8,11},{9,10},{10,... | collective-permute-start | bytes 98312 | tf_op jit(solution)/shard_map/ppermute | solution.py:314
  22.0 4.0 %collective-permute-start.6 = (bf16[32,512]{1,0:T(8,128)(2,1)S(1)}, bf16[32,512]{1,0:T(8,128)(2,1)S(1)}, u32[]{:S(2)}, u32[]{:S(2)}) collective-permute-start(bf16[32,512]{1,0:T(8,128)(2,1)S(1)} %get-tuple-element.66), channel_id=1, source_target_pairs={{0,2},{1,3},{2,0},{3,1},{4,6},{5,7},{6,4},{7,5},{8,10},{9,11},{10,... | collective-permute-start | bytes 98312 | tf_op jit(solution)/shard_map/ppermute | solution.py:314
  23.5 2.4 %collective-permute-start.7 = (bf16[32,512]{1,0:T(8,128)(2,1)S(1)}, bf16[32,512]{1,0:T(8,128)(2,1)S(1)}, u32[]{:S(2)}, u32[]{:S(2)}) collective-permute-start(bf16[32,512]{1,0:T(8,128)(2,1)S(1)} %get-tuple-element.67), channel_id=1, source_target_pairs={{0,1},{1,0},{2,3},{3,2},{4,5},{5,4},{6,7},{7,6},{8,9},{9,8},{10,11... | collective-permute-start | bytes 98312 | tf_op jit(solution)/shard_map/ppermute | solution.py:314
  26.3 6.0 %collective-permute-start.10 = (bf16[32,2176]{1,0:T(8,128)(2,1)S(1)}, bf16[32,2176]{1,0:T(8,128)(2,1)S(1)}, u32[]{:S(2)}, u32[]{:S(2)}) collective-permute-start(bf16[32,2176]{1,0:T(8,128)(2,1)S(1)} %pad_maximum_fusion.refs_0_), channel_id=1, source_target_pairs={{0,4},{8,0},{16,8},{24,16},{28,24},{20,28},{12,20},{4,12},{1,5},{9... | collective-permute-start | bytes 417800 | tf_op jit(solution)/shard_map/ppermute | solution.py:216
  27.8 5.9 %collective-permute-start.8 = (bf16[32,2176]{1,0:T(8,128)(2,1)S(1)}, bf16[32,2176]{1,0:T(8,128)(2,1)S(1)}, u32[]{:S(2)}, u32[]{:S(2)}) collective-permute-start(bf16[32,2176]{1,0:T(8,128)(2,1)S(1)} %pad_maximum_fusion.refs_0_), channel_id=1, source_target_pairs={{0,8},{8,16},{16,24},{24,28},{28,20},{20,12},{12,4},{4,0},{1,9},{9... | collective-permute-start | bytes 417800 | tf_op jit(solution)/shard_map/ppermute | solution.py:216
  28.4 10.6 %collective-permute-start.12 = (bf16[32,2176]{1,0:T(8,128)(2,1)S(1)}, bf16[32,2176]{1,0:T(8,128)(2,1)S(1)}, u32[]{:S(2)}, u32[]{:S(2)}) collective-permute-start(bf16[32,2176]{1,0:T(8,128)(2,1)S(1)} %pad_maximum_fusion.refs_0_), channel_id=1, source_target_pairs={{0,28},{8,20},{16,12},{24,4},{28,0},{20,8},{12,16},{4,24},{1,29},{... | collective-permute-start | bytes 417800 | tf_op jit(solution)/shard_map/ppermute | solution.py:216
  32.3 7.5 %collective-permute-start.11 = (bf16[32,2176]{1,0:T(8,128)(2,1)S(1)}, bf16[32,2176]{1,0:T(8,128)(2,1)S(1)}, u32[]{:S(2)}, u32[]{:S(2)}) collective-permute-start(bf16[32,2176]{1,0:T(8,128)(2,1)S(1)} %collective-permute-done.10.refs_3_), channel_id=1, source_target_pairs={{0,4},{8,0},{16,8},{24,16},{28,24},{20,28},{12,20},{4,12},{1,5},{9... | collective-permute-start | bytes 417800 | tf_op jit(solution)/shard_map/ppermute | solution.py:216
  33.8 7.1 %collective-permute-start.9 = (bf16[32,2176]{1,0:T(8,128)(2,1)S(1)}, bf16[32,2176]{1,0:T(8,128)(2,1)S(1)}, u32[]{:S(2)}, u32[]{:S(2)}) collective-permute-start(bf16[32,2176]{1,0:T(8,128)(2,1)S(1)} %collective-permute-done.8.after_ref.refs_1_), channel_id=1, source_target_pairs={{0,8},{8,16},{16,24},{24,28},{28,20},{20,12},{12,4},{4,0},{1,9},{9... | collective-permute-start | bytes 417800 | tf_op jit(solution)/shard_map/ppermute | solution.py:216
  40.9 5.1 %collective-permute-start.13 = (bf16[32,2176]{1,0:T(8,128)(2,1)S(1)}, bf16[32,2176]{1,0:T(8,128)(2,1)S(1)}, u32[]{:S(2)}, u32[]{:S(2)}) collective-permute-start(bf16[32,2176]{1,0:T(8,128)(2,1)S(1)} %collective-permute-done.9.refs_2_), channel_id=1, source_target_pairs={{0,8},{8,16},{16,24},{24,28},{28,20},{20,12},{12,4},{4,0},{1,9},{9... | collective-permute-start | bytes 417800 | tf_op jit(solution)/shard_map/ppermute | solution.py:216
  42.3 5.1 %collective-permute-start.14 = (bf16[32,2176]{1,0:T(8,128)(2,1)S(1)}, bf16[32,2176]{1,0:T(8,128)(2,1)S(1)}, u32[]{:S(2)}, u32[]{:S(2)}) collective-permute-start(bf16[32,2176]{1,0:T(8,128)(2,1)S(1)} %collective-permute-done.11.refs_4_), channel_id=1, source_target_pairs={{0,4},{8,0},{16,8},{24,16},{28,24},{20,28},{12,20},{4,12},{1,5},{9... | collective-permute-start | bytes 417800 | tf_op jit(solution)/shard_map/ppermute | solution.py:216
  50.3 5.4 %collective-permute-start.15 = (bf16[32,2048]{1,0:T(8,128)(2,1)S(1)}, bf16[32,2048]{1,0:T(8,128)(2,1)S(1)}, u32[]{:S(2)}, u32[]{:S(2)}) collective-permute-start(bf16[32,2048]{1,0:T(8,128)(2,1)S(1)} %get-tuple-element.84), channel_id=1, source_target_pairs={{0,8},{8,16},{16,24},{24,28},{28,20},{20,12},{12,4},{4,0},{1,9},{9... | collective-permute-start | bytes 393224 | tf_op jit(solution)/shard_map/ppermute | solution.py:216
  51.9 6.5 %collective-permute-start.18 = (bf16[32,2048]{1,0:T(8,128)(2,1)S(1)}, bf16[32,2048]{1,0:T(8,128)(2,1)S(1)}, u32[]{:S(2)}, u32[]{:S(2)}) collective-permute-start(bf16[32,2048]{1,0:T(8,128)(2,1)S(1)} %get-tuple-element.87), channel_id=1, source_target_pairs={{0,4},{8,0},{16,8},{24,16},{28,24},{20,28},{12,20},{4,12},{1,5},{9... | collective-permute-start | bytes 393224 | tf_op jit(solution)/shard_map/ppermute | solution.py:216
  52.4 14.2 %collective-permute-start.21 = (bf16[32,2048]{1,0:T(8,128)(2,1)S(1)}, bf16[32,2048]{1,0:T(8,128)(2,1)S(1)}, u32[]{:S(2)}, u32[]{:S(2)}) collective-permute-start(bf16[32,2048]{1,0:T(8,128)(2,1)S(1)} %get-tuple-element.90), channel_id=1, source_target_pairs={{0,28},{8,20},{16,12},{24,4},{28,0},{20,8},{12,16},{4,24},{1,29},{... | collective-permute-start | bytes 393224 | tf_op jit(solution)/shard_map/ppermute | solution.py:216
  55.8 7.2 %collective-permute-start.16 = (bf16[32,2048]{1,0:T(8,128)(2,1)S(1)}, bf16[32,2048]{1,0:T(8,128)(2,1)S(1)}, u32[]{:S(2)}, u32[]{:S(2)}) collective-permute-start(bf16[32,2048]{1,0:T(8,128)(2,1)S(1)} %add_convert_fusion.3), channel_id=1, source_target_pairs={{0,8},{8,16},{16,24},{24,28},{28,20},{20,12},{12,4},{4,0},{1,9},{9... | collective-permute-start | bytes 393224 | tf_op jit(solution)/shard_map/ppermute | solution.py:216
  58.4 5.6 %collective-permute-start.19 = (bf16[32,2048]{1,0:T(8,128)(2,1)S(1)}, bf16[32,2048]{1,0:T(8,128)(2,1)S(1)}, u32[]{:S(2)}, u32[]{:S(2)}) collective-permute-start(bf16[32,2048]{1,0:T(8,128)(2,1)S(1)} %add_convert_fusion.1), channel_id=1, source_target_pairs={{0,4},{8,0},{16,8},{24,16},{28,24},{20,28},{12,20},{4,12},{1,5},{9... | collective-permute-start | bytes 393224 | tf_op jit(solution)/shard_map/ppermute | solution.py:216
  63.0 5.0 %collective-permute-start.17 = (bf16[32,2048]{1,0:T(8,128)(2,1)S(1)}, bf16[32,2048]{1,0:T(8,128)(2,1)S(1)}, u32[]{:S(2)}, u32[]{:S(2)}) collective-permute-start(bf16[32,2048]{1,0:T(8,128)(2,1)S(1)} %add_convert_fusion.2), channel_id=1, source_target_pairs={{0,8},{8,16},{16,24},{24,28},{28,20},{20,12},{12,4},{4,0},{1,9},{9... | collective-permute-start | bytes 393224 | tf_op jit(solution)/shard_map/ppermute | solution.py:216
  64.0 5.1 %collective-permute-start.20 = (bf16[32,2048]{1,0:T(8,128)(2,1)S(1)}, bf16[32,2048]{1,0:T(8,128)(2,1)S(1)}, u32[]{:S(2)}, u32[]{:S(2)}) collective-permute-start(bf16[32,2048]{1,0:T(8,128)(2,1)S(1)} %add_convert_fusion), channel_id=1, source_target_pairs={{0,4},{8,0},{16,8},{24,16},{28,24},{20,28},{12,20},{4,12},{1,5},{9... | collective-permute-start | bytes 393224 | tf_op jit(solution)/shard_map/ppermute | solution.py:216
  69.2 3.6 %collective-permute-start.22 = (bf16[32,512]{1,0:T(8,128)(2,1)S(1)}, bf16[32,512]{1,0:T(8,128)(2,1)S(1)}, u32[]{:S(2)}, u32[]{:S(2)}) collective-permute-start(bf16[32,512]{1,0:T(8,128)(2,1)S(1)} %get-tuple-element.101), channel_id=1, source_target_pairs={{0,3},{1,2},{2,1},{3,0},{4,7},{5,6},{6,5},{7,4},{8,11},{9,10},{10,... | collective-permute-start | bytes 98312 | tf_op jit(solution)/shard_map/ppermute | solution.py:314
  69.3 4.0 %collective-permute-start.23 = (bf16[32,512]{1,0:T(8,128)(2,1)S(1)}, bf16[32,512]{1,0:T(8,128)(2,1)S(1)}, u32[]{:S(2)}, u32[]{:S(2)}) collective-permute-start(bf16[32,512]{1,0:T(8,128)(2,1)S(1)} %get-tuple-element.102), channel_id=1, source_target_pairs={{0,2},{1,3},{2,0},{3,1},{4,6},{5,7},{6,4},{7,5},{8,10},{9,11},{10,... | collective-permute-start | bytes 98312 | tf_op jit(solution)/shard_map/ppermute | solution.py:314
  70.6 2.7 %collective-permute-start.24 = (bf16[32,512]{1,0:T(8,128)(2,1)S(1)}, bf16[32,512]{1,0:T(8,128)(2,1)S(1)}, u32[]{:S(2)}, u32[]{:S(2)}) collective-permute-start(bf16[32,512]{1,0:T(8,128)(2,1)S(1)} %get-tuple-element.100), channel_id=1, source_target_pairs={{0,1},{1,0},{2,3},{3,2},{4,5},{5,4},{6,7},{7,6},{8,9},{9,8},{10,11... | collective-permute-start | bytes 98312 | tf_op jit(solution)/shard_map/ppermute | solution.py:314

commit v19 on v16

--- a/solution.py
+++ b/solution.py
@@ -132,23 +132,36 @@
         piece[...] = hidden[pl.ds(pl.multiple_of((scalars[0] ^ j) * count, count), count), :]
 
 
-def load_kernel(lead, scalars, source, after_ref, target, done_ref, sems):
+def load_kernel(lead, scalars, pair_ref, down_ref, after_ref, near_ref, part_ref, done_ref, sems):
     done_ref[...] = jnp.zeros_like(done_ref)
-    pieces = sems.shape[0]
-    step = target.shape[0] // pieces
-    cuts = [pl.ds(i * step, step) for i in range(pieces)]
-    run_copies([(source.at[lead, cut], target.at[cut]) for cut in cuts], sems)
-
-
-def load_near(scalars, source, lead, after):
+    pieces = sems.shape[0] // 2
+    pairs = []
+    for source, target, first in (
+        (pair_ref.at[lead], near_ref, 0),
+        (down_ref, part_ref, lead * part_ref.shape[0]),
+    ):
+        step = target.shape[0] // pieces
+        for i in range(pieces):
+            pairs.append(
+                (source.at[pl.ds(first + i * step, step)], target.at[pl.ds(i * step, step)])
+            )
+    run_copies(pairs, sems)
+
+
+def load_near(scalars, expert_in, expert_out, lead, after):
+    units, model = expert_out.shape
     return call(
         functools.partial(load_kernel, lead),
-        [shape(source.shape[1:], source.dtype), shape((8, HEAD), F32)],
-        [scalars, source, after], far=(1,), scratch=[pltpu.SemaphoreType.DMA((8,))],
-    )
-
-
-def expert_kernel(blocks, scalars, sign_ref, gate_ref, up_ref, down_ref, *refs):
+        [
+            shape(expert_in.shape[1:], BF16), shape((units // 2, model), BF16),
+            shape((8, HEAD), F32),
+        ],
+        [scalars, expert_in, expert_out, after], far=(1, 2),
+        scratch=[pltpu.SemaphoreType.DMA((16,))],
+    )
+
+
+def expert_kernel(blocks, scalars, sign_ref, gate_ref, up_ref, top_ref, low_ref, *refs):
     x_refs, out_refs, done_ref = refs[:blocks], refs[blocks:2 * blocks], refs[2 * blocks]
     rows_ref, act_ref, made_ref = refs[2 * blocks + 1:]
     done_ref[...] = jnp.zeros_like(done_ref)
@@ -180,20 +193,22 @@
 
     for step in range(model // wide):
         cut = slice(step * wide, (step + 1) * wide)
-        produced = jnp.dot(act_ref[...], down_ref[:, cut], preferred_element_type=F32)
+        produced = jnp.dot(
+            act_ref[:, :units // 2], top_ref[:, cut], preferred_element_type=F32
+        ) + jnp.dot(act_ref[:, units // 2:], low_ref[:, cut], preferred_element_type=F32)
         made_ref[:, cut] = (produced.astype(BF16).astype(F32) * weight).astype(BF16)
 
     for out_ref, span in zip(out_refs, spans):
         out_ref[...] = made_ref[span, :]
 
 
-def run_expert(scalars, sign, blocks, weights_gate, weights_up, weights_out):
-    units, model = weights_out.shape
+def run_expert(scalars, sign, blocks, weights):
+    model, units = weights[0].shape
     total = max(HEAD, sum(b.shape[0] for b in blocks))
     *made, sign = call(
         functools.partial(expert_kernel, len(blocks)),
         [shape((b.shape[0], model), BF16) for b in blocks] + [shape((8, HEAD), F32)],
-        [scalars, sign, weights_gate, weights_up, weights_out, *blocks],
+        [scalars, sign, *weights, *blocks],
         scratch=[
             pltpu.VMEM((total, model), BF16),
             pltpu.VMEM((total, units), BF16),
@@ -209,7 +224,7 @@
     return list(range(0, count, 2)) + list(range(1, count, 2))[::-1]
 
 
-def dense_experts(block, scalars, weights_gate, weights_up, expert_out):
+def dense_experts(block, scalars, sign, weights):
     count = lax.axis_size("seq")
     order = ring_order(count)
     far = count // 2
@@ -224,15 +239,13 @@
     for distance in range(1, far - 1):
         came, went = hop(ahead[-1], 1), hop(behind[-1], -1)
         if distance == far - 2:
-            weights_out, sign = load_near(scalars, expert_out, 0, ahead[-1])
-            came, went, sign = lax.optimization_barrier((came, went, sign))
+            came, went, farthest = lax.optimization_barrier((came, went, farthest))
         ahead.append(came)
         behind.append(went)
     last = hop(ahead[-1], 1), hop(behind[-1], -1)
-    weights = weights_gate, weights_up, weights_out
-    (own, *near), sign = run_expert(scalars, sign, ahead + behind[1:], *weights)
+    (own, *near), sign = run_expert(scalars, sign, ahead + behind[1:], weights)
     *last, farthest, sign = lax.optimization_barrier((*last, farthest, sign))
-    (back, front, farthest), _ = run_expert(scalars, sign, [*last, farthest], *weights)
+    (back, front, farthest), _ = run_expert(scalars, sign, [*last, farthest], weights)
     to_back, to_front = near[:far - 2] + [back], near[far - 2:] + [front]
     going, coming = hop(to_front[-1], 1), hop(to_back[-1], -1)
     straight = hop(farthest, far)
@@ -372,7 +385,7 @@
     total, within = lax.optimization_barrier((add_rows(kept, partner), within))
     sign = jnp.zeros((8, HEAD), F32)
     if dense:
-        weights_gate, sign = load_near(scalars, expert_in[0], 0, total)
+        gate, top, sign = load_near(scalars, expert_in[0], expert_out[0], 0, total)
     before = sum(
         came.astype(F32) * flags[2 + i:3 + i] for i, came in enumerate(prior_states(total))
     )
@@ -382,7 +395,7 @@
     other = lax.ppermute(lacked, "seq", swap)
     signs = [sign]
     if dense:
-        weights_up, sign = load_near(scalars, expert_in[0], 1, lacked)
+        up, low, sign = load_near(scalars, expert_in[0], expert_out[0], 1, lacked)
         signs.append(sign)
     pieces = call(
         functools.partial(attend_kernel, parts),
@@ -417,9 +430,7 @@
     ).astype(BF16)
     if dense:
         block = jnp.concatenate([normed, pack], axis=1)
-        terms = dense_experts(
-            block, scalars, weights_gate, weights_up, expert_out
-        )
+        terms = dense_experts(block, scalars, sign, [gate, up, top, low])
     else:
         mixed = routed_experts(normed, my_routes, my_gates, expert_in, expert_out)
         terms = [mixed]

time: 74.7 us -> 74.9 us (level)
  waiting for transfers between devices: 21.1 us -> 22.9 us
  Pallas kernels: 17.7 us -> 16.5 us
    ppermute x14, waiting for transfers between devices: 14.6 us -> 17.2 us  [hop(): lax.ppermute(rows, 'seq', [(order[p], order[(p + steps) % count]) for p i...]
    pallas_call x8 -> x7, Pallas kernels: 17.7 us -> 16.5 us  [call(): pl.pallas_call(kernel, out_shape=outs, in_specs=[SCALAR if i == 0 or i in...]
  transfers between devices with their start and end apart: 25 -> 25, of which waited for: 14 -> 17; matrix products, arithmetic and copies ran while one was open for 2% -> 2% of each run, Pallas kernels for 16% -> 14%
where the time goes in v19:
time: 74.9 us; the launch traced here: 74.6 us
  starting transfers between devices  32.5 us (43%)
  waiting for transfers between devices  22.9 us (31%)
  Pallas kernels  16.5 us (22%)
  other arithmetic  1.4 us (2%)
  local copies, waits for them, and re-layouts  1.09 us (1%)
    ppermute x14, starting transfers between devices, hop(): lax.ppermute(rows, 'seq', [(order[p], order[(p + steps) % count]) for p i...  19.3 us
    ppermute x14, waiting for transfers between devices, hop(): lax.ppermute(rows, 'seq', [(order[p], order[(p + steps) % count]) for p i...  17.2 us
    pallas_call x7, Pallas kernels, call(): pl.pallas_call(kernel, out_shape=outs, in_specs=[SCALAR if i == 0 or i in...  16.5 us
    ppermute x3, starting transfers between devices, prior_states(): lax.ppermute(total, 'seq', [(i, i ^ 2 * distance) for i in range(count)])  4.84 us
    ppermute x6, waiting for transfers between devices, exchange(): lax.ppermute(pieces[j], 'exp', [(i, i ^ j) for i in range(parts)])  4.27 us
    ppermute x6, starting transfers between devices, exchange(): lax.ppermute(pieces[j], 'exp', [(i, i ^ j) for i in range(parts)])  3.85 us
    ppermute x1, starting transfers between devices, per_device(): partner = lax.ppermute(given, 'seq', swap)  3.01 us
    ppermute x1, starting transfers between devices, per_device(): other = lax.ppermute(lacked, 'seq', swap)  1.55 us
  transfers between devices with their start and end apart: 25, of which 17 were waited for; matrix products, arithmetic and copies ran while one was open for 2% of the time, Pallas kernels for 14%

profile of v19, /device:TPU:0, one launch (start us, length us, event | category | flops | bytes accessed | tf_op | source)
XLA Modules:
  0.0 74.6 jit_solution(11920418159282155054)
XLA Ops:
  0.0 0.1 stack.24.scalars
  0.1 1.8 %shard_map.100 = (bf16[128,256]{1,0:T(8,128)(2,1)S(1)}, bf16[128,256]{1,0:T(8,128)(2,1)S(1)}, bf16[128,512]{1,0:T(8,128)(2,1)S(1)}, bf16[128,512]{1,0:T(8,128)(2...) custom-call(s32[7]{0:T(128)S(1)} %stack.24.scalars, ...), custom_call_target="tpu_custom_call" | custom-call | flops 16777216 | bytes 1188892 | tf_op jit(solution)/shard_map/pallas_call | solution.py:24
  1.9 3.0 %collective-permute-start = (bf16[128,256]{1,0:T(8,128)(2,1)S(1)}, bf16[128,256]{1,0:T(8,128)(2,1)S(1)}, u32[]{:S(2)}, u32[]{:S(2)}) collective-permute-start(bf16[128,256]{1,0:T(8,128)(2,1)S(1)} %get-tuple-element.51), channel_id=1, source_target_pairs={{0,4},{4,0},{8,12},{12,8},{16,20},{20,16},{24,28},{28,24},{1,5},{5... | collective-permute-start | bytes 196616 | tf_op jit(solution)/shard_map/ppermute | solution.py:379
  4.9 0.1 constant_dynamic-slice_fusion
  5.0 0.9 %shard_map.101.within_ref = f32[128,512]{1,0:T(8,128)S(1)} custom-call(s32[7]{0:T(128)S(1)} %stack.24.scalars, bf16[128,512]{1,0:T(8,128)(2,1)S(1)} %get-tuple-element.52.keys, bf16[128,512]{1,0:T(8,128)(2,1)S(1)} %get-tuple-element.53.values, bf16[128,512]{1,0:T(8,128)(2,1)S(1)} %get-tuple-element.54.queries), custom_call_target="tpu_custom_call" | custom-call | flops 50331648 | bytes 655388 | tf_op jit(solution)/shard_map/pallas_call | solution.py:24
  5.9 0.8 %constant_dynamic-slice_fusion.1 = s32[32,8]{0,1:T(8,128)S(1)} fusion(s32[128,8]{0,1:T(8,128)} %param.16, u32[]{:T(128)S(6)} %convert_element_type.87), kind=kLoop, calls=%fused_computation.54 | loop fusion | bytes 2052 | tf_op jit(solution)/shard_map/dynamic_slice | solution.py:409
  6.7 0.5 collective-permute-done
  7.2 4.2 %collective-permute-start.1 = (bf16[128,256]{1,0:T(8,128)(2,1)S(1)}, bf16[128,256]{1,0:T(8,128)(2,1)S(1)}, u32[]{:S(2)}, u32[]{:S(2)}) collective-permute-start(bf16[128,256]{1,0:T(8,128)(2,1)S(1)} %fusion.6.after_ref), channel_id=1, source_target_pairs={{0,24},{4,28},{8,16},{12,20},{16,8},{20,12},{24,0},{28,4},{1,25},{... | collective-permute-start | bytes 196616 | tf_op jit(solution)/shard_map/ppermute | solution.py:319
  11.4 0.0 collective-permute-start.2
  11.4 0.6 collective-permute-start.3
  12.0 0.1 copy.16
  12.1 0.1 copy.15
  12.2 3.4 %shard_map.102 = (bf16[2048,1024]{1,0:T(8,128)(2,1)S(1)}, bf16[512,2048]{1,0:T(8,128)(2,1)S(1)}, f32[8,128]{1,0:T(8,128)S(1)}) custom-call(s32[7]{0:T(128)S(1)} %stack.24.scalars, bf16[2,2048,1024]{2,1,0:T(8,128)(2,1)} %bitcast.17, bf16[1024,2048]{1,0:T(8,128)(2,1)} %bitcast.19, bf16[128,256]{1,0:T(8,128)(2,1)S(1)} %fusion.6.after_ref), custom_call_target="tpu_custom_call" | custom-call | bytes 18944028 | tf_op jit(solution)/shard_map/pallas_call | solution.py:24
  15.6 0.0 collective-permute-done.1
  15.6 0.9 %collective-permute-done.2 = bf16[128,256]{1,0:T(8,128)(2,1)S(1)} collective-permute-done((bf16[128,256]{1,0:T(8,128)(2,1)S(1)}, bf16[128,256]{1,0:T(8,128)(2,1)S(1)}, u32[]{:S(2)}, u32[]{:S(2)}) %collective-permute-start.2) | collective-permute-done | bytes 65568 | tf_op jit(solution)/shard_map/ppermute | solution.py:319
  16.6 0.0 collective-permute-done.3
  16.6 0.1 fusion.5
  16.6 1.6 %collective-permute-start.4 = (bf16[128,256]{1,0:T(8,128)(2,1)S(1)}, bf16[128,256]{1,0:T(8,128)(2,1)S(1)}, u32[]{:S(2)}, u32[]{:S(2)}) collective-permute-start(bf16[128,256]{1,0:T(8,128)(2,1)S(1)} %get-tuple-element.61.after_ref), channel_id=1, source_target_pairs={{0,4},{4,0},{8,12},{12,8},{16,20},{20,16},{24,28},{28,24},{1,5},{5... | collective-permute-start | bytes 196616 | tf_op jit(solution)/shard_map/ppermute | solution.py:395
  18.2 3.5 %shard_map.103 = (bf16[2048,1024]{1,0:T(8,128)(2,1)S(1)}, bf16[512,2048]{1,0:T(8,128)(2,1)S(1)}, f32[8,128]{1,0:T(8,128)S(1)}) custom-call(s32[7]{0:T(128)S(1)} %stack.24.scalars, bf16[2,2048,1024]{2,1,0:T(8,128)(2,1)} %bitcast.18, bf16[1024,2048]{1,0:T(8,128)(2,1)} %bitcast.20, bf16[128,256]{1,0:T(8,128)(2,1)S(1)} %get-tuple-element.61.after_ref), custom_call_target="tpu_custom_call" | custom-call | bytes 18944028 | tf_op jit(solution)/shard_map/pallas_call | solution.py:24
  21.7 0.9 %shard_map.104 = (bf16[32,512]{1,0:T(8,128)(2,1)S(1)}, bf16[32,512]{1,0:T(8,128)(2,1)S(1)}, bf16[32,512]{1,0:T(8,128)(2,1)S(1)}, bf16[32,512]{1,0:T(8,128)(2,1)S(1)}) custom-call(s32[7]{0:T(128)S(1)} %stack.24.scalars, f32[128,512]{1,0:T(8,128)S(1)} %shard_map.101.within_ref, bf16[128,512]{1,0:T(8,128)(2,1)S(1)} %get-tuple-element.54.queries, ...), custom_call_target="tpu_custom_call" | custom-call | flops 33554432 | bytes 862236 | tf_op jit(solution)/shard_map/pallas_call | solution.py:24
  22.6 0.1 collective-permute-start.5
  22.7 1.6 %collective-permute-start.6 = (bf16[32,512]{1,0:T(8,128)(2,1)S(1)}, bf16[32,512]{1,0:T(8,128)(2,1)S(1)}, u32[]{:S(2)}, u32[]{:S(2)}) collective-permute-start(bf16[32,512]{1,0:T(8,128)(2,1)S(1)} %get-tuple-element.65), channel_id=1, source_target_pairs={{0,2},{1,3},{2,0},{3,1},{4,6},{5,7},{6,4},{7,5},{8,10},{9,11},{10,... | collective-permute-start | bytes 98312 | tf_op jit(solution)/shard_map/ppermute | solution.py:329
  24.3 0.3 collective-permute-start.7
  24.5 0.1 fusion.10
  24.6 1.7 %collective-permute-done.5 = bf16[32,512]{1,0:T(8,128)(2,1)S(1)} collective-permute-done((bf16[32,512]{1,0:T(8,128)(2,1)S(1)}, bf16[32,512]{1,0:T(8,128)(2,1)S(1)}, u32[]{:S(2)}, u32[]{:S(2)}) %collective-permute-start.5) | collective-permute-done | bytes 32800 | tf_op jit(solution)/shard_map/ppermute | solution.py:329
  26.3 0.4 collective-permute-done.6
  26.7 0.1 fusion
  26.9 0.1 fusion.2
  27.0 0.8 %collective-permute-start.10 = (bf16[32,2176]{1,0:T(8,128)(2,1)S(1)}, bf16[32,2176]{1,0:T(8,128)(2,1)S(1)}, u32[]{:S(2)}, u32[]{:S(2)}) collective-permute-start(bf16[32,2176]{1,0:T(8,128)(2,1)S(1)} %pad_maximum_fusion.refs_0_), channel_id=1, source_target_pairs={{0,4},{8,0},{16,8},{24,16},{28,24},{20,28},{12,20},{4,12},{1,5},{9... | collective-permute-start | bytes 417800 | tf_op jit(solution)/shard_map/ppermute | solution.py:233
  27.8 1.3 %collective-permute-start.8 = (bf16[32,2176]{1,0:T(8,128)(2,1)S(1)}, bf16[32,2176]{1,0:T(8,128)(2,1)S(1)}, u32[]{:S(2)}, u32[]{:S(2)}) collective-permute-start(bf16[32,2176]{1,0:T(8,128)(2,1)S(1)} %pad_maximum_fusion.refs_0_), channel_id=1, source_target_pairs={{0,8},{8,16},{16,24},{24,28},{28,20},{20,12},{12,4},{4,0},{1,9},{9... | collective-permute-start | bytes 417800 | tf_op jit(solution)/shard_map/ppermute | solution.py:233
  29.1 3.1 %collective-permute-start.12 = (bf16[32,2176]{1,0:T(8,128)(2,1)S(1)}, bf16[32,2176]{1,0:T(8,128)(2,1)S(1)}, u32[]{:S(2)}, u32[]{:S(2)}) collective-permute-start(bf16[32,2176]{1,0:T(8,128)(2,1)S(1)} %pad_maximum_fusion.refs_0_), channel_id=1, source_target_pairs={{0,28},{8,20},{16,12},{24,4},{28,0},{20,8},{12,16},{4,24},{1,29},{... | collective-permute-start | bytes 417800 | tf_op jit(solution)/shard_map/ppermute | solution.py:233
  32.2 0.8 %collective-permute-done.10.refs_3_ = bf16[32,2176]{1,0:T(8,128)(2,1)S(1)} collective-permute-done((bf16[32,2176]{1,0:T(8,128)(2,1)S(1)}, bf16[32,2176]{1,0:T(8,128)(2,1)S(1)}, u32[]{:S(2)}, u32[]{:S(2)}) %collective-permute-start.10) | collective-permute-done | bytes 139296 | tf_op jit(solution)/shard_map/ppermute | solution.py:233
  33.0 0.8 %collective-permute-start.11 = (bf16[32,2176]{1,0:T(8,128)(2,1)S(1)}, bf16[32,2176]{1,0:T(8,128)(2,1)S(1)}, u32[]{:S(2)}, u32[]{:S(2)}) collective-permute-start(bf16[32,2176]{1,0:T(8,128)(2,1)S(1)} %collective-permute-done.10.refs_3_), channel_id=1, source_target_pairs={{0,4},{8,0},{16,8},{24,16},{28,24},{20,28},{12,20},{4,12},{1,5},{9... | collective-permute-start | bytes 417800 | tf_op jit(solution)/shard_map/ppermute | solution.py:233
  33.8 1.3 %collective-permute-start.9 = (bf16[32,2176]{1,0:T(8,128)(2,1)S(1)}, bf16[32,2176]{1,0:T(8,128)(2,1)S(1)}, u32[]{:S(2)}, u32[]{:S(2)}) collective-permute-start(bf16[32,2176]{1,0:T(8,128)(2,1)S(1)} %collective-permute-done.8.refs_1_), channel_id=1, source_target_pairs={{0,8},{8,16},{16,24},{24,28},{28,20},{20,12},{12,4},{4,0},{1,9},{9... | collective-permute-start | bytes 417800 | tf_op jit(solution)/shard_map/ppermute | solution.py:233
  35.0 4.6 %collective-permute-done.12.refs_2_ = bf16[32,2176]{1,0:T(8,128)(2,1)S(1)} collective-permute-done((bf16[32,2176]{1,0:T(8,128)(2,1)S(1)}, bf16[32,2176]{1,0:T(8,128)(2,1)S(1)}, u32[]{:S(2)}, u32[]{:S(2)}) %collective-permute-start.12) | collective-permute-done | bytes 139296 | tf_op jit(solution)/shard_map/ppermute | solution.py:233
  39.6 0.9 %collective-permute-done.11.refs_4_ = bf16[32,2176]{1,0:T(8,128)(2,1)S(1)} collective-permute-done((bf16[32,2176]{1,0:T(8,128)(2,1)S(1)}, bf16[32,2176]{1,0:T(8,128)(2,1)S(1)}, u32[]{:S(2)}, u32[]{:S(2)}) %collective-permute-start.11) | collective-permute-done | bytes 139296 | tf_op jit(solution)/shard_map/ppermute | solution.py:233
  40.5 0.7 collective-permute-done.9.refs_2_
  41.2 1.6 %collective-permute-start.13 = (bf16[32,2176]{1,0:T(8,128)(2,1)S(1)}, bf16[32,2176]{1,0:T(8,128)(2,1)S(1)}, u32[]{:S(2)}, u32[]{:S(2)}) collective-permute-start(bf16[32,2176]{1,0:T(8,128)(2,1)S(1)} %collective-permute-done.9.refs_2_), channel_id=1, source_target_pairs={{0,8},{8,16},{16,24},{24,28},{28,20},{20,12},{12,4},{4,0},{1,9},{9... | collective-permute-start | bytes 417800 | tf_op jit(solution)/shard_map/ppermute | solution.py:233
  42.8 0.5 collective-permute-start.14
  43.2 2.9 %shard_map.105 = (bf16[32,2048]{1,0:T(8,128)(2,1)S(1)}, bf16[32,2048]{1,0:T(8,128)(2,1)S(1)}, bf16[32,2048]{1,0:T(8,128)(2,1)S(1)}, bf16[32,2048]{1,0:T(8,128)(2...) custom-call(s32[7]{0:T(128)S(1)} %stack.24.scalars, f32[8,128]{1,0:T(8,128)S(1)} %get-tuple-element.63.refs_1_.sign_ref, ...), custom_call_target="tpu_custom_call" | custom-call | flops 2013265920 | bytes 13942812 | tf_op jit(solution)/shard_map/pallas_call | solution.py:24
  46.2 0.1 collective-permute-done.13.refs_0_
  46.3 1.6 %collective-permute-done.14.refs_1_ = bf16[32,2176]{1,0:T(8,128)(2,1)S(1)} collective-permute-done((bf16[32,2176]{1,0:T(8,128)(2,1)S(1)}, bf16[32,2176]{1,0:T(8,128)(2,1)S(1)}, u32[]{:S(2)}, u32[]{:S(2)}) %collective-permute-start.14) | collective-permute-done | bytes 139296 | tf_op jit(solution)/shard_map/ppermute | solution.py:233
  47.9 3.1 %shard_map.106 = (bf16[32,2048]{1,0:T(8,128)(2,1)S(1)}, bf16[32,2048]{1,0:T(8,128)(2,1)S(1)}, bf16[32,2048]{1,0:T(8,128)(2,1)S(1)}, f32[8,128]{1,0:T(8,128)}) custom-call(s32[7]{0:T(128)S(1)} %stack.24.scalars, f32[8,128]{1,0:T(8,128)S(1)} %get-tuple-element.78.sign_ref, bf16[2048,1024]{1,0:T(8,128)(2,1)S(1)} %get-tuple-element.68.gate_ref, ...), custom_call_target="tpu_custom_call" | custom-call | flops 1610612736 | bytes 13402140 | tf_op jit(solution)/shard_map/pallas_call | solution.py:24
  50.9 1.8 %collective-permute-start.15 = (bf16[32,2048]{1,0:T(8,128)(2,1)S(1)}, bf16[32,2048]{1,0:T(8,128)(2,1)S(1)}, u32[]{:S(2)}, u32[]{:S(2)}) collective-permute-start(bf16[32,2048]{1,0:T(8,128)(2,1)S(1)} %get-tuple-element.82), channel_id=1, source_target_pairs={{0,8},{8,16},{16,24},{24,28},{28,20},{20,12},{12,4},{4,0},{1,9},{9... | collective-permute-start | bytes 393224 | tf_op jit(solution)/shard_map/ppermute | solution.py:233
  52.7 0.2 collective-permute-start.18
  53.0 2.8 %collective-permute-start.21 = (bf16[32,2048]{1,0:T(8,128)(2,1)S(1)}, bf16[32,2048]{1,0:T(8,128)(2,1)S(1)}, u32[]{:S(2)}, u32[]{:S(2)}) collective-permute-start(bf16[32,2048]{1,0:T(8,128)(2,1)S(1)} %get-tuple-element.88), channel_id=1, source_target_pairs={{0,28},{8,20},{16,12},{24,4},{28,0},{20,8},{12,16},{4,24},{1,29},{... | collective-permute-start | bytes 393224 | tf_op jit(solution)/shard_map/ppermute | solution.py:233
  55.8 0.7 collective-permute-done.15
  56.5 2.5 %collective-permute-start.16 = (bf16[32,2048]{1,0:T(8,128)(2,1)S(1)}, bf16[32,2048]{1,0:T(8,128)(2,1)S(1)}, u32[]{:S(2)}, u32[]{:S(2)}) collective-permute-start(bf16[32,2048]{1,0:T(8,128)(2,1)S(1)} %add_convert_fusion.3), channel_id=1, source_target_pairs={{0,8},{8,16},{16,24},{24,28},{28,20},{20,12},{12,4},{4,0},{1,9},{9... | collective-permute-start | bytes 393224 | tf_op jit(solution)/shard_map/ppermute | solution.py:233
  59.1 0.0 collective-permute-done.18
  59.1 1.1 %collective-permute-start.19 = (bf16[32,2048]{1,0:T(8,128)(2,1)S(1)}, bf16[32,2048]{1,0:T(8,128)(2,1)S(1)}, u32[]{:S(2)}, u32[]{:S(2)}) collective-permute-start(bf16[32,2048]{1,0:T(8,128)(2,1)S(1)} %add_convert_fusion.1), channel_id=1, source_target_pairs={{0,4},{8,0},{16,8},{24,16},{28,24},{20,28},{12,20},{4,12},{1,5},{9... | collective-permute-start | bytes 393224 | tf_op jit(solution)/shard_map/ppermute | solution.py:233
  60.2 3.3 %collective-permute-done.16 = bf16[32,2048]{1,0:T(8,128)(2,1)S(1)} collective-permute-done((bf16[32,2048]{1,0:T(8,128)(2,1)S(1)}, bf16[32,2048]{1,0:T(8,128)(2,1)S(1)}, u32[]{:S(2)}, u32[]{:S(2)}) %collective-permute-start.16) | collective-permute-done | bytes 131104 | tf_op jit(solution)/shard_map/ppermute | solution.py:233
  63.6 0.6 collective-permute-start.17
  64.1 0.5 collective-permute-done.19
  64.7 1.1 %collective-permute-start.20 = (bf16[32,2048]{1,0:T(8,128)(2,1)S(1)}, bf16[32,2048]{1,0:T(8,128)(2,1)S(1)}, u32[]{:S(2)}, u32[]{:S(2)}) collective-permute-start(bf16[32,2048]{1,0:T(8,128)(2,1)S(1)} %add_convert_fusion), channel_id=1, source_target_pairs={{0,4},{8,0},{16,8},{24,16},{28,24},{20,28},{12,20},{4,12},{1,5},{9... | collective-permute-start | bytes 393224 | tf_op jit(solution)/shard_map/ppermute | solution.py:233
  65.7 0.0 collective-permute-done.21
  65.7 2.8 %collective-permute-done.17 = bf16[32,2048]{1,0:T(8,128)(2,1)S(1)} collective-permute-done((bf16[32,2048]{1,0:T(8,128)(2,1)S(1)}, bf16[32,2048]{1,0:T(8,128)(2,1)S(1)}, u32[]{:S(2)}, u32[]{:S(2)}) %collective-permute-start.17) | collective-permute-done | bytes 131104 | tf_op jit(solution)/shard_map/ppermute | solution.py:233
  68.6 1.1 %collective-permute-done.20 = bf16[32,2048]{1,0:T(8,128)(2,1)S(1)} collective-permute-done((bf16[32,2048]{1,0:T(8,128)(2,1)S(1)}, bf16[32,2048]{1,0:T(8,128)(2,1)S(1)}, u32[]{:S(2)}, u32[]{:S(2)}) %collective-permute-start.20) | collective-permute-done | bytes 131104 | tf_op jit(solution)/shard_map/ppermute | solution.py:233
  69.7 0.1 fusion.3
  69.8 0.1 collective-permute-start.22
  69.9 1.7 %collective-permute-start.23 = (bf16[32,512]{1,0:T(8,128)(2,1)S(1)}, bf16[32,512]{1,0:T(8,128)(2,1)S(1)}, u32[]{:S(2)}, u32[]{:S(2)}) collective-permute-start(bf16[32,512]{1,0:T(8,128)(2,1)S(1)} %get-tuple-element.100), channel_id=1, source_target_pairs={{0,2},{1,3},{2,0},{3,1},{4,6},{5,7},{6,4},{7,5},{8,10},{9,11},{10,... | collective-permute-start | bytes 98312 | tf_op jit(solution)/shard_map/ppermute | solution.py:329
  71.6 0.2 collective-permute-start.24
  71.8 1.6 %collective-permute-done.22 = bf16[32,512]{1,0:T(8,128)(2,1)S(1)} collective-permute-done((bf16[32,512]{1,0:T(8,128)(2,1)S(1)}, bf16[32,512]{1,0:T(8,128)(2,1)S(1)}, u32[]{:S(2)}, u32[]{:S(2)}) %collective-permute-start.22) | collective-permute-done | bytes 32800 | tf_op jit(solution)/shard_map/ppermute | solution.py:329
  73.4 0.5 collective-permute-done.23
  74.0 0.7 pad_maximum_fusion.2
  (22 shorter events, 0.3 us)
Async XLA Ops:
  0.0 4.9 %copy-start = (f32[128,8]{0,1:T(8,128)S(1)}, f32[128,8]{0,1:T(8,128)}, u32[]{:S(2)}) copy-start(f32[128,8]{0,1:T(8,128)} %param.17) | copy-start | bytes 12292
  1.9 5.3 %collective-permute-start = (bf16[128,256]{1,0:T(8,128)(2,1)S(1)}, bf16[128,256]{1,0:T(8,128)(2,1)S(1)}, u32[]{:S(2)}, u32[]{:S(2)}) collective-permute-start(bf16[128,256]{1,0:T(8,128)(2,1)S(1)} %get-tuple-element.51), channel_id=1, source_target_pairs={{0,4},{4,0},{8,12},{12,8},{16,20},{20,16},{24,28},{28,24},{1,5},{5... | collective-permute-start | bytes 196616 | tf_op jit(solution)/shard_map/ppermute | solution.py:379
  7.2 8.5 %collective-permute-start.1 = (bf16[128,256]{1,0:T(8,128)(2,1)S(1)}, bf16[128,256]{1,0:T(8,128)(2,1)S(1)}, u32[]{:S(2)}, u32[]{:S(2)}) collective-permute-start(bf16[128,256]{1,0:T(8,128)(2,1)S(1)} %fusion.6.after_ref), channel_id=1, source_target_pairs={{0,24},{4,28},{8,16},{12,20},{16,8},{20,12},{24,0},{28,4},{1,25},{... | collective-permute-start | bytes 196616 | tf_op jit(solution)/shard_map/ppermute | solution.py:319
  11.4 5.2 %collective-permute-start.2 = (bf16[128,256]{1,0:T(8,128)(2,1)S(1)}, bf16[128,256]{1,0:T(8,128)(2,1)S(1)}, u32[]{:S(2)}, u32[]{:S(2)}) collective-permute-start(bf16[128,256]{1,0:T(8,128)(2,1)S(1)} %fusion.6.after_ref), channel_id=1, source_target_pairs={{0,16},{4,20},{8,24},{12,28},{16,0},{20,4},{24,8},{28,12},{1,17},{... | collective-permute-start | bytes 196616 | tf_op jit(solution)/shard_map/ppermute | solution.py:319
  11.4 5.2 %collective-permute-start.3 = (bf16[128,256]{1,0:T(8,128)(2,1)S(1)}, bf16[128,256]{1,0:T(8,128)(2,1)S(1)}, u32[]{:S(2)}, u32[]{:S(2)}) collective-permute-start(bf16[128,256]{1,0:T(8,128)(2,1)S(1)} %fusion.6.after_ref), channel_id=1, source_target_pairs={{0,8},{4,12},{8,0},{12,4},{16,24},{20,28},{24,16},{28,20},{1,9},{5... | collective-permute-start | bytes 196616 | tf_op jit(solution)/shard_map/ppermute | solution.py:319
  16.6 5.0 %collective-permute-start.4 = (bf16[128,256]{1,0:T(8,128)(2,1)S(1)}, bf16[128,256]{1,0:T(8,128)(2,1)S(1)}, u32[]{:S(2)}, u32[]{:S(2)}) collective-permute-start(bf16[128,256]{1,0:T(8,128)(2,1)S(1)} %get-tuple-element.61.after_ref), channel_id=1, source_target_pairs={{0,4},{4,0},{8,12},{12,8},{16,20},{20,16},{24,28},{28,24},{1,5},{5... | collective-permute-start | bytes 196616 | tf_op jit(solution)/shard_map/ppermute | solution.py:395
  18.2 8.7 %copy-start.1 = (f32[2048]{0:T(1024)S(1)}, f32[2048]{0:T(1024)}, u32[]{:S(2)}) copy-start(f32[2048]{0:T(1024)} %param.15) | copy-start | bytes 24580
  22.6 3.7 %collective-permute-start.5 = (bf16[32,512]{1,0:T(8,128)(2,1)S(1)}, bf16[32,512]{1,0:T(8,128)(2,1)S(1)}, u32[]{:S(2)}, u32[]{:S(2)}) collective-permute-start(bf16[32,512]{1,0:T(8,128)(2,1)S(1)} %get-tuple-element.64), channel_id=1, source_target_pairs={{0,3},{1,2},{2,1},{3,0},{4,7},{5,6},{6,5},{7,4},{8,11},{9,10},{10,... | collective-permute-start | bytes 98312 | tf_op jit(solution)/shard_map/ppermute | solution.py:329
  22.7 4.0 %collective-permute-start.6 = (bf16[32,512]{1,0:T(8,128)(2,1)S(1)}, bf16[32,512]{1,0:T(8,128)(2,1)S(1)}, u32[]{:S(2)}, u32[]{:S(2)}) collective-permute-start(bf16[32,512]{1,0:T(8,128)(2,1)S(1)} %get-tuple-element.65), channel_id=1, source_target_pairs={{0,2},{1,3},{2,0},{3,1},{4,6},{5,7},{6,4},{7,5},{8,10},{9,11},{10,... | collective-permute-start | bytes 98312 | tf_op jit(solution)/shard_map/ppermute | solution.py:329
  24.3 2.4 %collective-permute-start.7 = (bf16[32,512]{1,0:T(8,128)(2,1)S(1)}, bf16[32,512]{1,0:T(8,128)(2,1)S(1)}, u32[]{:S(2)}, u32[]{:S(2)}) collective-permute-start(bf16[32,512]{1,0:T(8,128)(2,1)S(1)} %get-tuple-element.66), channel_id=1, source_target_pairs={{0,1},{1,0},{2,3},{3,2},{4,5},{5,4},{6,7},{7,6},{8,9},{9,8},{10,11... | collective-permute-start | bytes 98312 | tf_op jit(solution)/shard_map/ppermute | solution.py:329
  27.0 6.0 %collective-permute-start.10 = (bf16[32,2176]{1,0:T(8,128)(2,1)S(1)}, bf16[32,2176]{1,0:T(8,128)(2,1)S(1)}, u32[]{:S(2)}, u32[]{:S(2)}) collective-permute-start(bf16[32,2176]{1,0:T(8,128)(2,1)S(1)} %pad_maximum_fusion.refs_0_), channel_id=1, source_target_pairs={{0,4},{8,0},{16,8},{24,16},{28,24},{20,28},{12,20},{4,12},{1,5},{9... | collective-permute-start | bytes 417800 | tf_op jit(solution)/shard_map/ppermute | solution.py:233
  27.8 5.9 %collective-permute-start.8 = (bf16[32,2176]{1,0:T(8,128)(2,1)S(1)}, bf16[32,2176]{1,0:T(8,128)(2,1)S(1)}, u32[]{:S(2)}, u32[]{:S(2)}) collective-permute-start(bf16[32,2176]{1,0:T(8,128)(2,1)S(1)} %pad_maximum_fusion.refs_0_), channel_id=1, source_target_pairs={{0,8},{8,16},{16,24},{24,28},{28,20},{20,12},{12,4},{4,0},{1,9},{9... | collective-permute-start | bytes 417800 | tf_op jit(solution)/shard_map/ppermute | solution.py:233
  29.1 10.5 %collective-permute-start.12 = (bf16[32,2176]{1,0:T(8,128)(2,1)S(1)}, bf16[32,2176]{1,0:T(8,128)(2,1)S(1)}, u32[]{:S(2)}, u32[]{:S(2)}) collective-permute-start(bf16[32,2176]{1,0:T(8,128)(2,1)S(1)} %pad_maximum_fusion.refs_0_), channel_id=1, source_target_pairs={{0,28},{8,20},{16,12},{24,4},{28,0},{20,8},{12,16},{4,24},{1,29},{... | collective-permute-start | bytes 417800 | tf_op jit(solution)/shard_map/ppermute | solution.py:233
  33.0 7.5 %collective-permute-start.11 = (bf16[32,2176]{1,0:T(8,128)(2,1)S(1)}, bf16[32,2176]{1,0:T(8,128)(2,1)S(1)}, u32[]{:S(2)}, u32[]{:S(2)}) collective-permute-start(bf16[32,2176]{1,0:T(8,128)(2,1)S(1)} %collective-permute-done.10.refs_3_), channel_id=1, source_target_pairs={{0,4},{8,0},{16,8},{24,16},{28,24},{20,28},{12,20},{4,12},{1,5},{9... | collective-permute-start | bytes 417800 | tf_op jit(solution)/shard_map/ppermute | solution.py:233
  33.8 7.5 %collective-permute-start.9 = (bf16[32,2176]{1,0:T(8,128)(2,1)S(1)}, bf16[32,2176]{1,0:T(8,128)(2,1)S(1)}, u32[]{:S(2)}, u32[]{:S(2)}) collective-permute-start(bf16[32,2176]{1,0:T(8,128)(2,1)S(1)} %collective-permute-done.8.refs_1_), channel_id=1, source_target_pairs={{0,8},{8,16},{16,24},{24,28},{28,20},{20,12},{12,4},{4,0},{1,9},{9... | collective-permute-start | bytes 417800 | tf_op jit(solution)/shard_map/ppermute | solution.py:233
  41.2 5.1 %collective-permute-start.13 = (bf16[32,2176]{1,0:T(8,128)(2,1)S(1)}, bf16[32,2176]{1,0:T(8,128)(2,1)S(1)}, u32[]{:S(2)}, u32[]{:S(2)}) collective-permute-start(bf16[32,2176]{1,0:T(8,128)(2,1)S(1)} %collective-permute-done.9.refs_2_), channel_id=1, source_target_pairs={{0,8},{8,16},{16,24},{24,28},{28,20},{20,12},{12,4},{4,0},{1,9},{9... | collective-permute-start | bytes 417800 | tf_op jit(solution)/shard_map/ppermute | solution.py:233
  42.8 5.1 %collective-permute-start.14 = (bf16[32,2176]{1,0:T(8,128)(2,1)S(1)}, bf16[32,2176]{1,0:T(8,128)(2,1)S(1)}, u32[]{:S(2)}, u32[]{:S(2)}) collective-permute-start(bf16[32,2176]{1,0:T(8,128)(2,1)S(1)} %collective-permute-done.11.refs_4_), channel_id=1, source_target_pairs={{0,4},{8,0},{16,8},{24,16},{28,24},{20,28},{12,20},{4,12},{1,5},{9... | collective-permute-start | bytes 417800 | tf_op jit(solution)/shard_map/ppermute | solution.py:233
  50.9 5.6 %collective-permute-start.15 = (bf16[32,2048]{1,0:T(8,128)(2,1)S(1)}, bf16[32,2048]{1,0:T(8,128)(2,1)S(1)}, u32[]{:S(2)}, u32[]{:S(2)}) collective-permute-start(bf16[32,2048]{1,0:T(8,128)(2,1)S(1)} %get-tuple-element.82), channel_id=1, source_target_pairs={{0,8},{8,16},{16,24},{24,28},{28,20},{20,12},{12,4},{4,0},{1,9},{9... | collective-permute-start | bytes 393224 | tf_op jit(solution)/shard_map/ppermute | solution.py:233
  52.7 6.4 %collective-permute-start.18 = (bf16[32,2048]{1,0:T(8,128)(2,1)S(1)}, bf16[32,2048]{1,0:T(8,128)(2,1)S(1)}, u32[]{:S(2)}, u32[]{:S(2)}) collective-permute-start(bf16[32,2048]{1,0:T(8,128)(2,1)S(1)} %get-tuple-element.85), channel_id=1, source_target_pairs={{0,4},{8,0},{16,8},{24,16},{28,24},{20,28},{12,20},{4,12},{1,5},{9... | collective-permute-start | bytes 393224 | tf_op jit(solution)/shard_map/ppermute | solution.py:233
  53.0 12.8 %collective-permute-start.21 = (bf16[32,2048]{1,0:T(8,128)(2,1)S(1)}, bf16[32,2048]{1,0:T(8,128)(2,1)S(1)}, u32[]{:S(2)}, u32[]{:S(2)}) collective-permute-start(bf16[32,2048]{1,0:T(8,128)(2,1)S(1)} %get-tuple-element.88), channel_id=1, source_target_pairs={{0,28},{8,20},{16,12},{24,4},{28,0},{20,8},{12,16},{4,24},{1,29},{... | collective-permute-start | bytes 393224 | tf_op jit(solution)/shard_map/ppermute | solution.py:233
  56.5 7.0 %collective-permute-start.16 = (bf16[32,2048]{1,0:T(8,128)(2,1)S(1)}, bf16[32,2048]{1,0:T(8,128)(2,1)S(1)}, u32[]{:S(2)}, u32[]{:S(2)}) collective-permute-start(bf16[32,2048]{1,0:T(8,128)(2,1)S(1)} %add_convert_fusion.3), channel_id=1, source_target_pairs={{0,8},{8,16},{16,24},{24,28},{28,20},{20,12},{12,4},{4,0},{1,9},{9... | collective-permute-start | bytes 393224 | tf_op jit(solution)/shard_map/ppermute | solution.py:233
  59.1 5.5 %collective-permute-start.19 = (bf16[32,2048]{1,0:T(8,128)(2,1)S(1)}, bf16[32,2048]{1,0:T(8,128)(2,1)S(1)}, u32[]{:S(2)}, u32[]{:S(2)}) collective-permute-start(bf16[32,2048]{1,0:T(8,128)(2,1)S(1)} %add_convert_fusion.1), channel_id=1, source_target_pairs={{0,4},{8,0},{16,8},{24,16},{28,24},{20,28},{12,20},{4,12},{1,5},{9... | collective-permute-start | bytes 393224 | tf_op jit(solution)/shard_map/ppermute | solution.py:233
  63.6 5.0 %collective-permute-start.17 = (bf16[32,2048]{1,0:T(8,128)(2,1)S(1)}, bf16[32,2048]{1,0:T(8,128)(2,1)S(1)}, u32[]{:S(2)}, u32[]{:S(2)}) collective-permute-start(bf16[32,2048]{1,0:T(8,128)(2,1)S(1)} %add_convert_fusion.2), channel_id=1, source_target_pairs={{0,8},{8,16},{16,24},{24,28},{28,20},{20,12},{12,4},{4,0},{1,9},{9... | collective-permute-start | bytes 393224 | tf_op jit(solution)/shard_map/ppermute | solution.py:233
  64.7 5.0 %collective-permute-start.20 = (bf16[32,2048]{1,0:T(8,128)(2,1)S(1)}, bf16[32,2048]{1,0:T(8,128)(2,1)S(1)}, u32[]{:S(2)}, u32[]{:S(2)}) collective-permute-start(bf16[32,2048]{1,0:T(8,128)(2,1)S(1)} %add_convert_fusion), channel_id=1, source_target_pairs={{0,4},{8,0},{16,8},{24,16},{28,24},{20,28},{12,20},{4,12},{1,5},{9... | collective-permute-start | bytes 393224 | tf_op jit(solution)/shard_map/ppermute | solution.py:233
  69.8 3.6 %collective-permute-start.22 = (bf16[32,512]{1,0:T(8,128)(2,1)S(1)}, bf16[32,512]{1,0:T(8,128)(2,1)S(1)}, u32[]{:S(2)}, u32[]{:S(2)}) collective-permute-start(bf16[32,512]{1,0:T(8,128)(2,1)S(1)} %get-tuple-element.99), channel_id=1, source_target_pairs={{0,3},{1,2},{2,1},{3,0},{4,7},{5,6},{6,5},{7,4},{8,11},{9,10},{10,... | collective-permute-start | bytes 98312 | tf_op jit(solution)/shard_map/ppermute | solution.py:329
  69.9 4.0 %collective-permute-start.23 = (bf16[32,512]{1,0:T(8,128)(2,1)S(1)}, bf16[32,512]{1,0:T(8,128)(2,1)S(1)}, u32[]{:S(2)}, u32[]{:S(2)}) collective-permute-start(bf16[32,512]{1,0:T(8,128)(2,1)S(1)} %get-tuple-element.100), channel_id=1, source_target_pairs={{0,2},{1,3},{2,0},{3,1},{4,6},{5,7},{6,4},{7,5},{8,10},{9,11},{10,... | collective-permute-start | bytes 98312 | tf_op jit(solution)/shard_map/ppermute | solution.py:329
  71.6 2.3 %collective-permute-start.24 = (bf16[32,512]{1,0:T(8,128)(2,1)S(1)}, bf16[32,512]{1,0:T(8,128)(2,1)S(1)}, u32[]{:S(2)}, u32[]{:S(2)}) collective-permute-start(bf16[32,512]{1,0:T(8,128)(2,1)S(1)} %get-tuple-element.98), channel_id=1, source_target_pairs={{0,1},{1,0},{2,3},{3,2},{4,5},{5,4},{6,7},{7,6},{8,9},{9,8},{10,11... | collective-permute-start | bytes 98312 | tf_op jit(solution)/shard_map/ppermute | solution.py:329

commit v20 on v15

--- a/solution.py
+++ b/solution.py
@@ -235,11 +235,14 @@
     (back, front, farthest), _ = run_expert(scalars, sign, [*last, farthest], *weights)
     to_back, to_front = near[:far - 2] + [back], near[far - 2:] + [front]
     going, coming = hop(to_front[-1], 1), hop(to_back[-1], -1)
-    straight = hop(farthest, far)
     for distance in range(far - 2, -1, -1):
         if distance == 0:
             return own, going, coming, straight
-        going = hop(add_rows(going, to_front[distance - 1]), 1)
+        going = add_rows(going, to_front[distance - 1])
+        if distance == far - 2:
+            going, farthest = lax.optimization_barrier((going, farthest))
+            straight = hop(farthest, far)
+        going = hop(going, 1)
         coming = hop(add_rows(coming, to_back[distance - 1]), -1)
 
 

time: 74.1 us -> 74.3 us (level)
  waiting for transfers between devices: 18.6 us -> 19.5 us
  starting transfers between devices: 35 us -> 34.2 us
    ppermute x14, waiting for transfers between devices: 12.3 us -> 13.2 us  [hop(): lax.ppermute(rows, 'seq', [(order[p], order[(p + steps) % count]) for p i...]
    ppermute x14, starting transfers between devices: 21.8 us -> 20.9 us  [hop(): lax.ppermute(rows, 'seq', [(order[p], order[(p + steps) % count]) for p i...]
  transfers between devices with their start and end apart: 25 -> 25, of which waited for: 17 -> 16; matrix products, arithmetic and copies ran while one was open for 2% -> 2% of each run, Pallas kernels for 16% -> 16%
where the time goes in v20:
time: 74.3 us; the launch traced here: 74.1 us
  starting transfers between devices  34.2 us (46%)
  waiting for transfers between devices  19.5 us (26%)
  Pallas kernels  17.7 us (24%)
  other arithmetic  1.39 us (2%)
  local copies, waits for them, and re-layouts  1.09 us (1%)
    ppermute x14, starting transfers between devices, hop(): lax.ppermute(rows, 'seq', [(order[p], order[(p + steps) % count]) for p i...  20.9 us
    pallas_call x8, Pallas kernels, call(): pl.pallas_call(kernel, out_shape=outs, in_specs=[SCALAR if i == 0 or i in...  17.7 us
    ppermute x14, waiting for transfers between devices, hop(): lax.ppermute(rows, 'seq', [(order[p], order[(p + steps) % count]) for p i...  13.2 us
    ppermute x3, starting transfers between devices, prior_states(): lax.ppermute(total, 'seq', [(i, i ^ 2 * distance) for i in range(count)])  4.84 us
    ppermute x6, waiting for transfers between devices, exchange(): lax.ppermute(pieces[j], 'exp', [(i, i ^ j) for i in range(parts)])  4.24 us
    ppermute x6, starting transfers between devices, exchange(): lax.ppermute(pieces[j], 'exp', [(i, i ^ j) for i in range(parts)])  3.84 us
    ppermute x1, starting transfers between devices, per_device(): partner = lax.ppermute(given, 'seq', swap)  3.01 us
    ppermute x3, waiting for transfers between devices, prior_states(): lax.ppermute(total, 'seq', [(i, i ^ 2 * distance) for i in range(count)])  1.6 us
  transfers between devices with their start and end apart: 25, of which 16 were waited for; matrix products, arithmetic and copies ran while one was open for 2% of the time, Pallas kernels for 16%

profile of v20, /device:TPU:0, one launch (start us, length us, event | category | flops | bytes accessed | tf_op | source)
XLA Modules:
  0.0 74.1 jit_solution(2090576840126242101)
XLA Ops:
  0.0 0.1 stack.24.scalars
  0.1 1.8 %shard_map.100 = (bf16[128,256]{1,0:T(8,128)(2,1)S(1)}, bf16[128,256]{1,0:T(8,128)(2,1)S(1)}, bf16[128,512]{1,0:T(8,128)(2,1)S(1)}, bf16[128,512]{1,0:T(8,128)(2...) custom-call(s32[7]{0:T(128)S(1)} %stack.24.scalars, ...), custom_call_target="tpu_custom_call" | custom-call | flops 16777216 | bytes 1188892 | tf_op jit(solution)/shard_map/pallas_call | solution.py:24
  1.9 3.0 %collective-permute-start = (bf16[128,256]{1,0:T(8,128)(2,1)S(1)}, bf16[128,256]{1,0:T(8,128)(2,1)S(1)}, u32[]{:S(2)}, u32[]{:S(2)}) collective-permute-start(bf16[128,256]{1,0:T(8,128)(2,1)S(1)} %get-tuple-element.54), channel_id=1, source_target_pairs={{0,4},{4,0},{8,12},{12,8},{16,20},{20,16},{24,28},{28,24},{1,5},{5... | collective-permute-start | bytes 196616 | tf_op jit(solution)/shard_map/ppermute | solution.py:369
  4.9 0.1 constant_dynamic-slice_fusion
  5.0 0.9 %shard_map.101.within_ref = f32[128,512]{1,0:T(8,128)S(1)} custom-call(s32[7]{0:T(128)S(1)} %stack.24.scalars, bf16[128,512]{1,0:T(8,128)(2,1)S(1)} %get-tuple-element.55.keys, bf16[128,512]{1,0:T(8,128)(2,1)S(1)} %get-tuple-element.56.values, bf16[128,512]{1,0:T(8,128)(2,1)S(1)} %get-tuple-element.57.queries), custom_call_target="tpu_custom_call" | custom-call | flops 50331648 | bytes 655388 | tf_op jit(solution)/shard_map/pallas_call | solution.py:24
  5.9 0.8 %constant_dynamic-slice_fusion.1 = s32[32,8]{0,1:T(8,128)S(1)} fusion(s32[128,8]{0,1:T(8,128)} %param.16, u32[]{:T(128)S(6)} %convert_element_type.87), kind=kLoop, calls=%fused_computation.54 | loop fusion | bytes 2052 | tf_op jit(solution)/shard_map/dynamic_slice | solution.py:399
  6.7 0.5 collective-permute-done
  7.2 4.2 %collective-permute-start.1 = (bf16[128,256]{1,0:T(8,128)(2,1)S(1)}, bf16[128,256]{1,0:T(8,128)(2,1)S(1)}, u32[]{:S(2)}, u32[]{:S(2)}) collective-permute-start(bf16[128,256]{1,0:T(8,128)(2,1)S(1)} %fusion.6.after_ref), channel_id=1, source_target_pairs={{0,24},{4,28},{8,16},{12,20},{16,8},{20,12},{24,0},{28,4},{1,25},{... | collective-permute-start | bytes 196616 | tf_op jit(solution)/shard_map/ppermute | solution.py:309
  11.4 0.6 collective-permute-start.3
  12.0 0.1 copy.16
  12.1 0.1 copy.15
  12.2 2.8 %shard_map.102 = (bf16[2048,1024]{1,0:T(8,128)(2,1)S(1)}, f32[8,128]{1,0:T(8,128)S(1)}) custom-call(s32[7]{0:T(128)S(1)} %stack.24.scalars, bf16[2,2048,1024]{2,1,0:T(8,128)(2,1)} %bitcast.16, bf16[128,256]{1,0:T(8,128)(2,1)S(1)} %fusion.6.after_ref), custom_call_target="tpu_custom_call" | custom-call | bytes 12652572 | tf_op jit(solution)/shard_map/pallas_call | solution.py:24
  15.0 1.6 %collective-permute-done.2 = bf16[128,256]{1,0:T(8,128)(2,1)S(1)} collective-permute-done((bf16[128,256]{1,0:T(8,128)(2,1)S(1)}, bf16[128,256]{1,0:T(8,128)(2,1)S(1)}, u32[]{:S(2)}, u32[]{:S(2)}) %collective-permute-start.2) | collective-permute-done | bytes 65568 | tf_op jit(solution)/shard_map/ppermute | solution.py:309
  16.6 0.0 collective-permute-done.3
  16.6 0.1 fusion.5
  16.6 1.6 %collective-permute-start.4 = (bf16[128,256]{1,0:T(8,128)(2,1)S(1)}, bf16[128,256]{1,0:T(8,128)(2,1)S(1)}, u32[]{:S(2)}, u32[]{:S(2)}) collective-permute-start(bf16[128,256]{1,0:T(8,128)(2,1)S(1)} %get-tuple-element.64.after_ref), channel_id=1, source_target_pairs={{0,4},{4,0},{8,12},{12,8},{16,20},{20,16},{24,28},{28,24},{1,5},{5... | collective-permute-start | bytes 196616 | tf_op jit(solution)/shard_map/ppermute | solution.py:385
  18.2 2.8 %shard_map.103 = (bf16[2048,1024]{1,0:T(8,128)(2,1)S(1)}, f32[8,128]{1,0:T(8,128)S(1)}) custom-call(s32[7]{0:T(128)S(1)} %stack.24.scalars, bf16[2,2048,1024]{2,1,0:T(8,128)(2,1)} %bitcast.17, bf16[128,256]{1,0:T(8,128)(2,1)S(1)} %get-tuple-element.64.after_ref), custom_call_target="tpu_custom_call" | custom-call | bytes 12652572 | tf_op jit(solution)/shard_map/pallas_call | solution.py:24
  21.0 0.0 collective-permute-done.4.other_ref
  21.0 0.9 %shard_map.104 = (bf16[32,512]{1,0:T(8,128)(2,1)S(1)}, bf16[32,512]{1,0:T(8,128)(2,1)S(1)}, bf16[32,512]{1,0:T(8,128)(2,1)S(1)}, bf16[32,512]{1,0:T(8,128)(2,1)S(1)}) custom-call(s32[7]{0:T(128)S(1)} %stack.24.scalars, f32[128,512]{1,0:T(8,128)S(1)} %shard_map.101.within_ref, bf16[128,512]{1,0:T(8,128)(2,1)S(1)} %get-tuple-element.57.queries, ...), custom_call_target="tpu_custom_call" | custom-call | flops 33554432 | bytes 862236 | tf_op jit(solution)/shard_map/pallas_call | solution.py:24
  21.9 0.1 collective-permute-start.5
  22.0 1.6 %collective-permute-start.6 = (bf16[32,512]{1,0:T(8,128)(2,1)S(1)}, bf16[32,512]{1,0:T(8,128)(2,1)S(1)}, u32[]{:S(2)}, u32[]{:S(2)}) collective-permute-start(bf16[32,512]{1,0:T(8,128)(2,1)S(1)} %get-tuple-element.68), channel_id=1, source_target_pairs={{0,2},{1,3},{2,0},{3,1},{4,6},{5,7},{6,4},{7,5},{8,10},{9,11},{10,... | collective-permute-start | bytes 98312 | tf_op jit(solution)/shard_map/ppermute | solution.py:319
  23.5 0.3 collective-permute-start.7
  23.8 0.1 fusion.10
  23.9 1.7 %collective-permute-done.5 = bf16[32,512]{1,0:T(8,128)(2,1)S(1)} collective-permute-done((bf16[32,512]{1,0:T(8,128)(2,1)S(1)}, bf16[32,512]{1,0:T(8,128)(2,1)S(1)}, u32[]{:S(2)}, u32[]{:S(2)}) %collective-permute-start.5) | collective-permute-done | bytes 32800 | tf_op jit(solution)/shard_map/ppermute | solution.py:319
  25.6 0.4 collective-permute-done.6
  26.0 0.0 collective-permute-done.7
  26.0 0.1 fusion
  26.2 0.1 fusion.2
  26.3 1.5 %collective-permute-start.10 = (bf16[32,2176]{1,0:T(8,128)(2,1)S(1)}, bf16[32,2176]{1,0:T(8,128)(2,1)S(1)}, u32[]{:S(2)}, u32[]{:S(2)}) collective-permute-start(bf16[32,2176]{1,0:T(8,128)(2,1)S(1)} %pad_maximum_fusion.refs_0_), channel_id=1, source_target_pairs={{0,4},{8,0},{16,8},{24,16},{28,24},{20,28},{12,20},{4,12},{1,5},{9... | collective-permute-start | bytes 417800 | tf_op jit(solution)/shard_map/ppermute | solution.py:218
  27.8 0.6 collective-permute-start.8
  28.4 3.1 %collective-permute-start.12 = (bf16[32,2176]{1,0:T(8,128)(2,1)S(1)}, bf16[32,2176]{1,0:T(8,128)(2,1)S(1)}, u32[]{:S(2)}, u32[]{:S(2)}) collective-permute-start(bf16[32,2176]{1,0:T(8,128)(2,1)S(1)} %pad_maximum_fusion.refs_0_), channel_id=1, source_target_pairs={{0,28},{8,20},{16,12},{24,4},{28,0},{20,8},{12,16},{4,24},{1,29},{... | collective-permute-start | bytes 417800 | tf_op jit(solution)/shard_map/ppermute | solution.py:218
  31.5 0.8 %collective-permute-done.10.refs_3_ = bf16[32,2176]{1,0:T(8,128)(2,1)S(1)} collective-permute-done((bf16[32,2176]{1,0:T(8,128)(2,1)S(1)}, bf16[32,2176]{1,0:T(8,128)(2,1)S(1)}, u32[]{:S(2)}, u32[]{:S(2)}) %collective-permute-start.10) | collective-permute-done | bytes 139296 | tf_op jit(solution)/shard_map/ppermute | solution.py:218
  32.3 1.5 %collective-permute-start.11 = (bf16[32,2176]{1,0:T(8,128)(2,1)S(1)}, bf16[32,2176]{1,0:T(8,128)(2,1)S(1)}, u32[]{:S(2)}, u32[]{:S(2)}) collective-permute-start(bf16[32,2176]{1,0:T(8,128)(2,1)S(1)} %collective-permute-done.10.refs_3_), channel_id=1, source_target_pairs={{0,4},{8,0},{16,8},{24,16},{28,24},{20,28},{12,20},{4,12},{1,5},{9... | collective-permute-start | bytes 417800 | tf_op jit(solution)/shard_map/ppermute | solution.py:218
  33.8 0.0 collective-permute-done.8.after_ref.refs_1_
  33.8 0.6 collective-permute-start.9
  34.3 2.8 %shard_map.105 = (bf16[1024,2048]{1,0:T(8,128)(2,1)S(1)}, f32[8,128]{1,0:T(8,128)S(1)}) custom-call(s32[7]{0:T(128)S(1)} %stack.24.scalars, bf16[1,1024,2048]{2,1,0:T(8,128)(2,1)} %source.1, bf16[32,2176]{1,0:T(8,128)(2,1)S(1)} %collective-permute-done.8.after_ref.refs_1_), custom_call_target="tpu_custom_call" | custom-call | bytes 8531996 | tf_op jit(solution)/shard_map/pallas_call | solution.py:24
  37.1 1.9 %collective-permute-done.12.refs_2_ = bf16[32,2176]{1,0:T(8,128)(2,1)S(1)} collective-permute-done((bf16[32,2176]{1,0:T(8,128)(2,1)S(1)}, bf16[32,2176]{1,0:T(8,128)(2,1)S(1)}, u32[]{:S(2)}, u32[]{:S(2)}) %collective-permute-start.12) | collective-permute-done | bytes 139296 | tf_op jit(solution)/shard_map/ppermute | solution.py:218
  38.9 0.8 %collective-permute-done.11.refs_4_ = bf16[32,2176]{1,0:T(8,128)(2,1)S(1)} collective-permute-done((bf16[32,2176]{1,0:T(8,128)(2,1)S(1)}, bf16[32,2176]{1,0:T(8,128)(2,1)S(1)}, u32[]{:S(2)}, u32[]{:S(2)}) %collective-permute-start.11) | collective-permute-done | bytes 139296 | tf_op jit(solution)/shard_map/ppermute | solution.py:218
  39.8 1.1 %collective-permute-done.9.refs_2_ = bf16[32,2176]{1,0:T(8,128)(2,1)S(1)} collective-permute-done((bf16[32,2176]{1,0:T(8,128)(2,1)S(1)}, bf16[32,2176]{1,0:T(8,128)(2,1)S(1)}, u32[]{:S(2)}, u32[]{:S(2)}) %collective-permute-start.9) | collective-permute-done | bytes 139296 | tf_op jit(solution)/shard_map/ppermute | solution.py:218
  40.9 1.5 %collective-permute-start.13 = (bf16[32,2176]{1,0:T(8,128)(2,1)S(1)}, bf16[32,2176]{1,0:T(8,128)(2,1)S(1)}, u32[]{:S(2)}, u32[]{:S(2)}) collective-permute-start(bf16[32,2176]{1,0:T(8,128)(2,1)S(1)} %collective-permute-done.9.refs_2_), channel_id=1, source_target_pairs={{0,8},{8,16},{16,24},{24,28},{28,20},{20,12},{12,4},{4,0},{1,9},{9... | collective-permute-start | bytes 417800 | tf_op jit(solution)/shard_map/ppermute | solution.py:218
  42.3 0.6 collective-permute-start.14
  42.9 2.9 %shard_map.106 = (bf16[32,2048]{1,0:T(8,128)(2,1)S(1)}, bf16[32,2048]{1,0:T(8,128)(2,1)S(1)}, bf16[32,2048]{1,0:T(8,128)(2,1)S(1)}, bf16[32,2048]{1,0:T(8,128)(2...) custom-call(s32[7]{0:T(128)S(1)} %stack.24.scalars, f32[8,128]{1,0:T(8,128)S(1)} %get-tuple-element.73.sign_ref, ...), custom_call_target="tpu_custom_call" | custom-call | flops 2013265920 | bytes 13942812 | tf_op jit(solution)/shard_map/pallas_call | solution.py:24
  45.8 0.2 collective-permute-done.13.refs_0_
  45.9 1.5 %collective-permute-done.14.refs_1_ = bf16[32,2176]{1,0:T(8,128)(2,1)S(1)} collective-permute-done((bf16[32,2176]{1,0:T(8,128)(2,1)S(1)}, bf16[32,2176]{1,0:T(8,128)(2,1)S(1)}, u32[]{:S(2)}, u32[]{:S(2)}) %collective-permute-start.14) | collective-permute-done | bytes 139296 | tf_op jit(solution)/shard_map/ppermute | solution.py:218
  47.4 2.9 %shard_map.107 = (bf16[32,2048]{1,0:T(8,128)(2,1)S(1)}, bf16[32,2048]{1,0:T(8,128)(2,1)S(1)}, bf16[32,2048]{1,0:T(8,128)(2,1)S(1)}, f32[8,128]{1,0:T(8,128)}) custom-call(s32[7]{0:T(128)S(1)} %stack.24.scalars, f32[8,128]{1,0:T(8,128)S(1)} %get-tuple-element.82.sign_ref, bf16[2048,1024]{1,0:T(8,128)(2,1)S(1)} %get-tuple-element.74.gate_ref, ...), custom_call_target="tpu_custom_call" | custom-call | flops 1610612736 | bytes 13402140 | tf_op jit(solution)/shard_map/pallas_call | solution.py:24
  50.3 1.5 %collective-permute-start.15 = (bf16[32,2048]{1,0:T(8,128)(2,1)S(1)}, bf16[32,2048]{1,0:T(8,128)(2,1)S(1)}, u32[]{:S(2)}, u32[]{:S(2)}) collective-permute-start(bf16[32,2048]{1,0:T(8,128)(2,1)S(1)} %get-tuple-element.86), channel_id=1, source_target_pairs={{0,8},{8,16},{16,24},{24,28},{28,20},{20,12},{12,4},{4,0},{1,9},{9... | collective-permute-start | bytes 393224 | tf_op jit(solution)/shard_map/ppermute | solution.py:218
  51.9 0.5 collective-permute-start.18
  52.4 3.0 %collective-permute-done.15 = bf16[32,2048]{1,0:T(8,128)(2,1)S(1)} collective-permute-done((bf16[32,2048]{1,0:T(8,128)(2,1)S(1)}, bf16[32,2048]{1,0:T(8,128)(2,1)S(1)}, u32[]{:S(2)}, u32[]{:S(2)}) %collective-permute-start.15) | collective-permute-done | bytes 131104 | tf_op jit(solution)/shard_map/ppermute | solution.py:218
  55.4 1.6 %collective-permute-start.16 = (bf16[32,2048]{1,0:T(8,128)(2,1)S(1)}, bf16[32,2048]{1,0:T(8,128)(2,1)S(1)}, u32[]{:S(2)}, u32[]{:S(2)}) collective-permute-start(bf16[32,2048]{1,0:T(8,128)(2,1)S(1)} %add_convert_fusion.3), channel_id=1, source_target_pairs={{0,8},{8,16},{16,24},{24,28},{28,20},{20,12},{12,4},{4,0},{1,9},{9... | collective-permute-start | bytes 393224 | tf_op jit(solution)/shard_map/ppermute | solution.py:218
  56.9 0.0 collective-permute-done.18
  57.0 0.7 collective-permute-start.19
  57.6 5.3 %collective-permute-start.21 = (bf16[32,2048]{1,0:T(8,128)(2,1)S(1)}, bf16[32,2048]{1,0:T(8,128)(2,1)S(1)}, u32[]{:S(2)}, u32[]{:S(2)}) collective-permute-start(bf16[32,2048]{1,0:T(8,128)(2,1)S(1)} %get-tuple-element.94), channel_id=1, source_target_pairs={{0,28},{8,20},{16,12},{24,4},{28,0},{20,8},{12,16},{4,24},{1,29},{... | collective-permute-start | bytes 393224 | tf_op jit(solution)/shard_map/ppermute | solution.py:218
  63.0 1.1 %collective-permute-start.17 = (bf16[32,2048]{1,0:T(8,128)(2,1)S(1)}, bf16[32,2048]{1,0:T(8,128)(2,1)S(1)}, u32[]{:S(2)}, u32[]{:S(2)}) collective-permute-start(bf16[32,2048]{1,0:T(8,128)(2,1)S(1)} %add_convert_fusion.2), channel_id=1, source_target_pairs={{0,8},{8,16},{16,24},{24,28},{28,20},{20,12},{12,4},{4,0},{1,9},{9... | collective-permute-start | bytes 393224 | tf_op jit(solution)/shard_map/ppermute | solution.py:218
  64.2 1.0 %collective-permute-start.20 = (bf16[32,2048]{1,0:T(8,128)(2,1)S(1)}, bf16[32,2048]{1,0:T(8,128)(2,1)S(1)}, u32[]{:S(2)}, u32[]{:S(2)}) collective-permute-start(bf16[32,2048]{1,0:T(8,128)(2,1)S(1)} %add_convert_fusion), channel_id=1, source_target_pairs={{0,4},{8,0},{16,8},{24,16},{28,24},{20,28},{12,20},{4,12},{1,5},{9... | collective-permute-start | bytes 393224 | tf_op jit(solution)/shard_map/ppermute | solution.py:218
  65.2 1.3 %collective-permute-done.21 = bf16[32,2048]{1,0:T(8,128)(2,1)S(1)} collective-permute-done((bf16[32,2048]{1,0:T(8,128)(2,1)S(1)}, bf16[32,2048]{1,0:T(8,128)(2,1)S(1)}, u32[]{:S(2)}, u32[]{:S(2)}) %collective-permute-start.21) | collective-permute-done | bytes 131104 | tf_op jit(solution)/shard_map/ppermute | solution.py:218
  66.5 1.5 %collective-permute-done.17 = bf16[32,2048]{1,0:T(8,128)(2,1)S(1)} collective-permute-done((bf16[32,2048]{1,0:T(8,128)(2,1)S(1)}, bf16[32,2048]{1,0:T(8,128)(2,1)S(1)}, u32[]{:S(2)}, u32[]{:S(2)}) %collective-permute-start.17) | collective-permute-done | bytes 131104 | tf_op jit(solution)/shard_map/ppermute | solution.py:218
  68.0 1.1 %collective-permute-done.20 = bf16[32,2048]{1,0:T(8,128)(2,1)S(1)} collective-permute-done((bf16[32,2048]{1,0:T(8,128)(2,1)S(1)}, bf16[32,2048]{1,0:T(8,128)(2,1)S(1)}, u32[]{:S(2)}, u32[]{:S(2)}) %collective-permute-start.20) | collective-permute-done | bytes 131104 | tf_op jit(solution)/shard_map/ppermute | solution.py:218
  69.2 0.1 fusion.3
  69.3 0.1 collective-permute-start.22
  69.4 1.4 %collective-permute-start.23 = (bf16[32,512]{1,0:T(8,128)(2,1)S(1)}, bf16[32,512]{1,0:T(8,128)(2,1)S(1)}, u32[]{:S(2)}, u32[]{:S(2)}) collective-permute-start(bf16[32,512]{1,0:T(8,128)(2,1)S(1)} %get-tuple-element.106), channel_id=1, source_target_pairs={{0,2},{1,3},{2,0},{3,1},{4,6},{5,7},{6,4},{7,5},{8,10},{9,11},{10,... | collective-permute-start | bytes 98312 | tf_op jit(solution)/shard_map/ppermute | solution.py:319
  70.7 0.5 collective-permute-start.24
  71.2 1.7 %collective-permute-done.22 = bf16[32,512]{1,0:T(8,128)(2,1)S(1)} collective-permute-done((bf16[32,512]{1,0:T(8,128)(2,1)S(1)}, bf16[32,512]{1,0:T(8,128)(2,1)S(1)}, u32[]{:S(2)}, u32[]{:S(2)}) %collective-permute-start.22) | collective-permute-done | bytes 32800 | tf_op jit(solution)/shard_map/ppermute | solution.py:319
  72.9 0.5 collective-permute-done.23
  73.4 0.7 pad_maximum_fusion.2
  (23 shorter events, 0.3 us)
Async XLA Ops:
  0.0 4.9 %copy-start = (f32[128,8]{0,1:T(8,128)S(1)}, f32[128,8]{0,1:T(8,128)}, u32[]{:S(2)}) copy-start(f32[128,8]{0,1:T(8,128)} %param.17) | copy-start | bytes 12292
  1.9 5.3 %collective-permute-start = (bf16[128,256]{1,0:T(8,128)(2,1)S(1)}, bf16[128,256]{1,0:T(8,128)(2,1)S(1)}, u32[]{:S(2)}, u32[]{:S(2)}) collective-permute-start(bf16[128,256]{1,0:T(8,128)(2,1)S(1)} %get-tuple-element.54), channel_id=1, source_target_pairs={{0,4},{4,0},{8,12},{12,8},{16,20},{20,16},{24,28},{28,24},{1,5},{5... | collective-permute-start | bytes 196616 | tf_op jit(solution)/shard_map/ppermute | solution.py:369
  7.2 7.8 %collective-permute-start.1 = (bf16[128,256]{1,0:T(8,128)(2,1)S(1)}, bf16[128,256]{1,0:T(8,128)(2,1)S(1)}, u32[]{:S(2)}, u32[]{:S(2)}) collective-permute-start(bf16[128,256]{1,0:T(8,128)(2,1)S(1)} %fusion.6.after_ref), channel_id=1, source_target_pairs={{0,24},{4,28},{8,16},{12,20},{16,8},{20,12},{24,0},{28,4},{1,25},{... | collective-permute-start | bytes 196616 | tf_op jit(solution)/shard_map/ppermute | solution.py:309
  11.4 5.2 %collective-permute-start.2 = (bf16[128,256]{1,0:T(8,128)(2,1)S(1)}, bf16[128,256]{1,0:T(8,128)(2,1)S(1)}, u32[]{:S(2)}, u32[]{:S(2)}) collective-permute-start(bf16[128,256]{1,0:T(8,128)(2,1)S(1)} %fusion.6.after_ref), channel_id=1, source_target_pairs={{0,16},{4,20},{8,24},{12,28},{16,0},{20,4},{24,8},{28,12},{1,17},{... | collective-permute-start | bytes 196616 | tf_op jit(solution)/shard_map/ppermute | solution.py:309
  11.4 5.2 %collective-permute-start.3 = (bf16[128,256]{1,0:T(8,128)(2,1)S(1)}, bf16[128,256]{1,0:T(8,128)(2,1)S(1)}, u32[]{:S(2)}, u32[]{:S(2)}) collective-permute-start(bf16[128,256]{1,0:T(8,128)(2,1)S(1)} %fusion.6.after_ref), channel_id=1, source_target_pairs={{0,8},{4,12},{8,0},{12,4},{16,24},{20,28},{24,16},{28,20},{1,9},{5... | collective-permute-start | bytes 196616 | tf_op jit(solution)/shard_map/ppermute | solution.py:309
  16.6 4.3 %collective-permute-start.4 = (bf16[128,256]{1,0:T(8,128)(2,1)S(1)}, bf16[128,256]{1,0:T(8,128)(2,1)S(1)}, u32[]{:S(2)}, u32[]{:S(2)}) collective-permute-start(bf16[128,256]{1,0:T(8,128)(2,1)S(1)} %get-tuple-element.64.after_ref), channel_id=1, source_target_pairs={{0,4},{4,0},{8,12},{12,8},{16,20},{20,16},{24,28},{28,24},{1,5},{5... | collective-permute-start | bytes 196616 | tf_op jit(solution)/shard_map/ppermute | solution.py:385
  18.2 8.0 %copy-start.1 = (f32[2048]{0:T(1024)S(1)}, f32[2048]{0:T(1024)}, u32[]{:S(2)}) copy-start(f32[2048]{0:T(1024)} %param.15) | copy-start | bytes 24580
  21.9 3.7 %collective-permute-start.5 = (bf16[32,512]{1,0:T(8,128)(2,1)S(1)}, bf16[32,512]{1,0:T(8,128)(2,1)S(1)}, u32[]{:S(2)}, u32[]{:S(2)}) collective-permute-start(bf16[32,512]{1,0:T(8,128)(2,1)S(1)} %get-tuple-element.67), channel_id=1, source_target_pairs={{0,3},{1,2},{2,1},{3,0},{4,7},{5,6},{6,5},{7,4},{8,11},{9,10},{10,... | collective-permute-start | bytes 98312 | tf_op jit(solution)/shard_map/ppermute | solution.py:319
  22.0 4.0 %collective-permute-start.6 = (bf16[32,512]{1,0:T(8,128)(2,1)S(1)}, bf16[32,512]{1,0:T(8,128)(2,1)S(1)}, u32[]{:S(2)}, u32[]{:S(2)}) collective-permute-start(bf16[32,512]{1,0:T(8,128)(2,1)S(1)} %get-tuple-element.68), channel_id=1, source_target_pairs={{0,2},{1,3},{2,0},{3,1},{4,6},{5,7},{6,4},{7,5},{8,10},{9,11},{10,... | collective-permute-start | bytes 98312 | tf_op jit(solution)/shard_map/ppermute | solution.py:319
  23.5 2.4 %collective-permute-start.7 = (bf16[32,512]{1,0:T(8,128)(2,1)S(1)}, bf16[32,512]{1,0:T(8,128)(2,1)S(1)}, u32[]{:S(2)}, u32[]{:S(2)}) collective-permute-start(bf16[32,512]{1,0:T(8,128)(2,1)S(1)} %get-tuple-element.69), channel_id=1, source_target_pairs={{0,1},{1,0},{2,3},{3,2},{4,5},{5,4},{6,7},{7,6},{8,9},{9,8},{10,11... | collective-permute-start | bytes 98312 | tf_op jit(solution)/shard_map/ppermute | solution.py:319
  26.3 6.0 %collective-permute-start.10 = (bf16[32,2176]{1,0:T(8,128)(2,1)S(1)}, bf16[32,2176]{1,0:T(8,128)(2,1)S(1)}, u32[]{:S(2)}, u32[]{:S(2)}) collective-permute-start(bf16[32,2176]{1,0:T(8,128)(2,1)S(1)} %pad_maximum_fusion.refs_0_), channel_id=1, source_target_pairs={{0,4},{8,0},{16,8},{24,16},{28,24},{20,28},{12,20},{4,12},{1,5},{9... | collective-permute-start | bytes 417800 | tf_op jit(solution)/shard_map/ppermute | solution.py:218
  27.8 5.9 %collective-permute-start.8 = (bf16[32,2176]{1,0:T(8,128)(2,1)S(1)}, bf16[32,2176]{1,0:T(8,128)(2,1)S(1)}, u32[]{:S(2)}, u32[]{:S(2)}) collective-permute-start(bf16[32,2176]{1,0:T(8,128)(2,1)S(1)} %pad_maximum_fusion.refs_0_), channel_id=1, source_target_pairs={{0,8},{8,16},{16,24},{24,28},{28,20},{20,12},{12,4},{4,0},{1,9},{9... | collective-permute-start | bytes 417800 | tf_op jit(solution)/shard_map/ppermute | solution.py:218
  28.4 10.6 %collective-permute-start.12 = (bf16[32,2176]{1,0:T(8,128)(2,1)S(1)}, bf16[32,2176]{1,0:T(8,128)(2,1)S(1)}, u32[]{:S(2)}, u32[]{:S(2)}) collective-permute-start(bf16[32,2176]{1,0:T(8,128)(2,1)S(1)} %pad_maximum_fusion.refs_0_), channel_id=1, source_target_pairs={{0,28},{8,20},{16,12},{24,4},{28,0},{20,8},{12,16},{4,24},{1,29},{... | collective-permute-start | bytes 417800 | tf_op jit(solution)/shard_map/ppermute | solution.py:218
  32.3 7.5 %collective-permute-start.11 = (bf16[32,2176]{1,0:T(8,128)(2,1)S(1)}, bf16[32,2176]{1,0:T(8,128)(2,1)S(1)}, u32[]{:S(2)}, u32[]{:S(2)}) collective-permute-start(bf16[32,2176]{1,0:T(8,128)(2,1)S(1)} %collective-permute-done.10.refs_3_), channel_id=1, source_target_pairs={{0,4},{8,0},{16,8},{24,16},{28,24},{20,28},{12,20},{4,12},{1,5},{9... | collective-permute-start | bytes 417800 | tf_op jit(solution)/shard_map/ppermute | solution.py:218
  33.8 7.1 %collective-permute-start.9 = (bf16[32,2176]{1,0:T(8,128)(2,1)S(1)}, bf16[32,2176]{1,0:T(8,128)(2,1)S(1)}, u32[]{:S(2)}, u32[]{:S(2)}) collective-permute-start(bf16[32,2176]{1,0:T(8,128)(2,1)S(1)} %collective-permute-done.8.after_ref.refs_1_), channel_id=1, source_target_pairs={{0,8},{8,16},{16,24},{24,28},{28,20},{20,12},{12,4},{4,0},{1,9},{9... | collective-permute-start | bytes 417800 | tf_op jit(solution)/shard_map/ppermute | solution.py:218
  40.9 5.1 %collective-permute-start.13 = (bf16[32,2176]{1,0:T(8,128)(2,1)S(1)}, bf16[32,2176]{1,0:T(8,128)(2,1)S(1)}, u32[]{:S(2)}, u32[]{:S(2)}) collective-permute-start(bf16[32,2176]{1,0:T(8,128)(2,1)S(1)} %collective-permute-done.9.refs_2_), channel_id=1, source_target_pairs={{0,8},{8,16},{16,24},{24,28},{28,20},{20,12},{12,4},{4,0},{1,9},{9... | collective-permute-start | bytes 417800 | tf_op jit(solution)/shard_map/ppermute | solution.py:218
  42.3 5.1 %collective-permute-start.14 = (bf16[32,2176]{1,0:T(8,128)(2,1)S(1)}, bf16[32,2176]{1,0:T(8,128)(2,1)S(1)}, u32[]{:S(2)}, u32[]{:S(2)}) collective-permute-start(bf16[32,2176]{1,0:T(8,128)(2,1)S(1)} %collective-permute-done.11.refs_4_), channel_id=1, source_target_pairs={{0,4},{8,0},{16,8},{24,16},{28,24},{20,28},{12,20},{4,12},{1,5},{9... | collective-permute-start | bytes 417800 | tf_op jit(solution)/shard_map/ppermute | solution.py:218
  50.3 5.0 %collective-permute-start.15 = (bf16[32,2048]{1,0:T(8,128)(2,1)S(1)}, bf16[32,2048]{1,0:T(8,128)(2,1)S(1)}, u32[]{:S(2)}, u32[]{:S(2)}) collective-permute-start(bf16[32,2048]{1,0:T(8,128)(2,1)S(1)} %get-tuple-element.86), channel_id=1, source_target_pairs={{0,8},{8,16},{16,24},{24,28},{28,20},{20,12},{12,4},{4,0},{1,9},{9... | collective-permute-start | bytes 393224 | tf_op jit(solution)/shard_map/ppermute | solution.py:218
  51.9 5.1 %collective-permute-start.18 = (bf16[32,2048]{1,0:T(8,128)(2,1)S(1)}, bf16[32,2048]{1,0:T(8,128)(2,1)S(1)}, u32[]{:S(2)}, u32[]{:S(2)}) collective-permute-start(bf16[32,2048]{1,0:T(8,128)(2,1)S(1)} %get-tuple-element.91), channel_id=1, source_target_pairs={{0,4},{8,0},{16,8},{24,16},{28,24},{20,28},{12,20},{4,12},{1,5},{9... | collective-permute-start | bytes 393224 | tf_op jit(solution)/shard_map/ppermute | solution.py:218
  55.4 7.6 %collective-permute-start.16 = (bf16[32,2048]{1,0:T(8,128)(2,1)S(1)}, bf16[32,2048]{1,0:T(8,128)(2,1)S(1)}, u32[]{:S(2)}, u32[]{:S(2)}) collective-permute-start(bf16[32,2048]{1,0:T(8,128)(2,1)S(1)} %add_convert_fusion.3), channel_id=1, source_target_pairs={{0,8},{8,16},{16,24},{24,28},{28,20},{20,12},{12,4},{4,0},{1,9},{9... | collective-permute-start | bytes 393224 | tf_op jit(solution)/shard_map/ppermute | solution.py:218
  57.0 7.2 %collective-permute-start.19 = (bf16[32,2048]{1,0:T(8,128)(2,1)S(1)}, bf16[32,2048]{1,0:T(8,128)(2,1)S(1)}, u32[]{:S(2)}, u32[]{:S(2)}) collective-permute-start(bf16[32,2048]{1,0:T(8,128)(2,1)S(1)} %add_convert_fusion.1), channel_id=1, source_target_pairs={{0,4},{8,0},{16,8},{24,16},{28,24},{20,28},{12,20},{4,12},{1,5},{9... | collective-permute-start | bytes 393224 | tf_op jit(solution)/shard_map/ppermute | solution.py:218
  57.6 8.9 %collective-permute-start.21 = (bf16[32,2048]{1,0:T(8,128)(2,1)S(1)}, bf16[32,2048]{1,0:T(8,128)(2,1)S(1)}, u32[]{:S(2)}, u32[]{:S(2)}) collective-permute-start(bf16[32,2048]{1,0:T(8,128)(2,1)S(1)} %get-tuple-element.94), channel_id=1, source_target_pairs={{0,28},{8,20},{16,12},{24,4},{28,0},{20,8},{12,16},{4,24},{1,29},{... | collective-permute-start | bytes 393224 | tf_op jit(solution)/shard_map/ppermute | solution.py:218
  63.0 5.0 %collective-permute-start.17 = (bf16[32,2048]{1,0:T(8,128)(2,1)S(1)}, bf16[32,2048]{1,0:T(8,128)(2,1)S(1)}, u32[]{:S(2)}, u32[]{:S(2)}) collective-permute-start(bf16[32,2048]{1,0:T(8,128)(2,1)S(1)} %add_convert_fusion.2), channel_id=1, source_target_pairs={{0,8},{8,16},{16,24},{24,28},{28,20},{20,12},{12,4},{4,0},{1,9},{9... | collective-permute-start | bytes 393224 | tf_op jit(solution)/shard_map/ppermute | solution.py:218
  64.2 5.0 %collective-permute-start.20 = (bf16[32,2048]{1,0:T(8,128)(2,1)S(1)}, bf16[32,2048]{1,0:T(8,128)(2,1)S(1)}, u32[]{:S(2)}, u32[]{:S(2)}) collective-permute-start(bf16[32,2048]{1,0:T(8,128)(2,1)S(1)} %add_convert_fusion), channel_id=1, source_target_pairs={{0,4},{8,0},{16,8},{24,16},{28,24},{20,28},{12,20},{4,12},{1,5},{9... | collective-permute-start | bytes 393224 | tf_op jit(solution)/shard_map/ppermute | solution.py:218
  69.3 3.6 %collective-permute-start.22 = (bf16[32,512]{1,0:T(8,128)(2,1)S(1)}, bf16[32,512]{1,0:T(8,128)(2,1)S(1)}, u32[]{:S(2)}, u32[]{:S(2)}) collective-permute-start(bf16[32,512]{1,0:T(8,128)(2,1)S(1)} %get-tuple-element.105), channel_id=1, source_target_pairs={{0,3},{1,2},{2,1},{3,0},{4,7},{5,6},{6,5},{7,4},{8,11},{9,10},{10,... | collective-permute-start | bytes 98312 | tf_op jit(solution)/shard_map/ppermute | solution.py:319
  69.4 4.0 %collective-permute-start.23 = (bf16[32,512]{1,0:T(8,128)(2,1)S(1)}, bf16[32,512]{1,0:T(8,128)(2,1)S(1)}, u32[]{:S(2)}, u32[]{:S(2)}) collective-permute-start(bf16[32,512]{1,0:T(8,128)(2,1)S(1)} %get-tuple-element.106), channel_id=1, source_target_pairs={{0,2},{1,3},{2,0},{3,1},{4,6},{5,7},{6,4},{7,5},{8,10},{9,11},{10,... | collective-permute-start | bytes 98312 | tf_op jit(solution)/shard_map/ppermute | solution.py:319
  70.7 2.6 %collective-permute-start.24 = (bf16[32,512]{1,0:T(8,128)(2,1)S(1)}, bf16[32,512]{1,0:T(8,128)(2,1)S(1)}, u32[]{:S(2)}, u32[]{:S(2)}) collective-permute-start(bf16[32,512]{1,0:T(8,128)(2,1)S(1)} %get-tuple-element.104), channel_id=1, source_target_pairs={{0,1},{1,0},{2,3},{3,2},{4,5},{5,4},{6,7},{7,6},{8,9},{9,8},{10,11... | collective-permute-start | bytes 98312 | tf_op jit(solution)/shard_map/ppermute | solution.py:319

commit v21 on v15

--- a/solution.py
+++ b/solution.py
@@ -168,7 +168,7 @@
     lane = lax.broadcasted_iota(jnp.int32, pack.shape, 1)
     chosen = (lane == scalars[3]) | (lane == scalars[3] + scalars[2])
     weight = jnp.sum(jnp.where(chosen, pack, 0.0), axis=-1, keepdims=True)
-    chunk = min(units, 512)
+    chunk = min(units, 256)
 
     for step in range(units // chunk):
         cut = slice(step * chunk, (step + 1) * chunk)
@@ -176,7 +176,7 @@
         up = jnp.dot(rows_ref[...], up_ref[:, cut], preferred_element_type=F32)
         act_ref[:, cut] = (gate / (1.0 + jnp.exp(-gate)) * up).astype(BF16)
 
-    wide = min(model, 1024)
+    wide = min(model, 512)
 
     for step in range(model // wide):
         cut = slice(step * wide, (step + 1) * wide)

time: 74.1 us -> 74.1 us (level)
  no operation moved by 1% of the time
where the time goes in v21:
time: 74.1 us; the launch traced here: 73.9 us
  starting transfers between devices  35 us (47%)
  waiting for transfers between devices  18.5 us (25%)
  Pallas kernels  17.7 us (24%)
  other arithmetic  1.4 us (2%)
  local copies, waits for them, and re-layouts  1.09 us (1%)
    ppermute x14, starting transfers between devices, hop(): lax.ppermute(rows, 'seq', [(order[p], order[(p + steps) % count]) for p i...  21.7 us
    pallas_call x8, Pallas kernels, call(): pl.pallas_call(kernel, out_shape=outs, in_specs=[SCALAR if i == 0 or i in...  17.7 us
    ppermute x14, waiting for transfers between devices, hop(): lax.ppermute(rows, 'seq', [(order[p], order[(p + steps) % count]) for p i...  12.2 us
    ppermute x3, starting transfers between devices, prior_states(): lax.ppermute(total, 'seq', [(i, i ^ 2 * distance) for i in range(count)])  4.84 us
    ppermute x6, waiting for transfers between devices, exchange(): lax.ppermute(pieces[j], 'exp', [(i, i ^ j) for i in range(parts)])  4.24 us
    ppermute x6, starting transfers between devices, exchange(): lax.ppermute(pieces[j], 'exp', [(i, i ^ j) for i in range(parts)])  3.84 us
    ppermute x1, starting transfers between devices, per_device(): partner = lax.ppermute(given, 'seq', swap)  3.01 us
    ppermute x3, waiting for transfers between devices, prior_states(): lax.ppermute(total, 'seq', [(i, i ^ 2 * distance) for i in range(count)])  1.6 us
  transfers between devices with their start and end apart: 25, of which 17 were waited for; matrix products, arithmetic and copies ran while one was open for 2% of the time, Pallas kernels for 16%

profile of v21, /device:TPU:0, one launch (start us, length us, event | category | flops | bytes accessed | tf_op | source)
XLA Modules:
  0.0 73.9 jit_solution(1029629443780142042)
XLA Ops:
  0.0 0.1 stack.24.scalars
  0.1 1.8 %shard_map.100 = (bf16[128,256]{1,0:T(8,128)(2,1)S(1)}, bf16[128,256]{1,0:T(8,128)(2,1)S(1)}, bf16[128,512]{1,0:T(8,128)(2,1)S(1)}, bf16[128,512]{1,0:T(8,128)(2...) custom-call(s32[7]{0:T(128)S(1)} %stack.24.scalars, ...), custom_call_target="tpu_custom_call" | custom-call | flops 16777216 | bytes 1188892 | tf_op jit(solution)/shard_map/pallas_call | solution.py:24
  1.9 3.0 %collective-permute-start = (bf16[128,256]{1,0:T(8,128)(2,1)S(1)}, bf16[128,256]{1,0:T(8,128)(2,1)S(1)}, u32[]{:S(2)}, u32[]{:S(2)}) collective-permute-start(bf16[128,256]{1,0:T(8,128)(2,1)S(1)} %get-tuple-element.52), channel_id=1, source_target_pairs={{0,4},{4,0},{8,12},{12,8},{16,20},{20,16},{24,28},{28,24},{1,5},{5... | collective-permute-start | bytes 196616 | tf_op jit(solution)/shard_map/ppermute | solution.py:366
  4.9 0.1 constant_dynamic-slice_fusion
  5.0 0.9 %shard_map.101.within_ref = f32[128,512]{1,0:T(8,128)S(1)} custom-call(s32[7]{0:T(128)S(1)} %stack.24.scalars, bf16[128,512]{1,0:T(8,128)(2,1)S(1)} %get-tuple-element.53.keys, bf16[128,512]{1,0:T(8,128)(2,1)S(1)} %get-tuple-element.54.values, bf16[128,512]{1,0:T(8,128)(2,1)S(1)} %get-tuple-element.55.queries), custom_call_target="tpu_custom_call" | custom-call | flops 50331648 | bytes 655388 | tf_op jit(solution)/shard_map/pallas_call | solution.py:24
  5.9 0.8 %constant_dynamic-slice_fusion.1 = s32[32,8]{0,1:T(8,128)S(1)} fusion(s32[128,8]{0,1:T(8,128)} %param.16, u32[]{:T(128)S(6)} %convert_element_type.87), kind=kLoop, calls=%fused_computation.54 | loop fusion | bytes 2052 | tf_op jit(solution)/shard_map/dynamic_slice | solution.py:396
  6.7 0.5 collective-permute-done
  7.2 4.2 %collective-permute-start.1 = (bf16[128,256]{1,0:T(8,128)(2,1)S(1)}, bf16[128,256]{1,0:T(8,128)(2,1)S(1)}, u32[]{:S(2)}, u32[]{:S(2)}) collective-permute-start(bf16[128,256]{1,0:T(8,128)(2,1)S(1)} %fusion.6.after_ref), channel_id=1, source_target_pairs={{0,24},{4,28},{8,16},{12,20},{16,8},{20,12},{24,0},{28,4},{1,25},{... | collective-permute-start | bytes 196616 | tf_op jit(solution)/shard_map/ppermute | solution.py:306
  11.4 0.6 collective-permute-start.3
  12.0 0.1 copy.16
  12.1 0.1 copy.15
  12.2 2.8 %shard_map.102 = (bf16[2048,1024]{1,0:T(8,128)(2,1)S(1)}, f32[8,128]{1,0:T(8,128)S(1)}) custom-call(s32[7]{0:T(128)S(1)} %stack.24.scalars, bf16[2,2048,1024]{2,1,0:T(8,128)(2,1)} %bitcast.16, bf16[128,256]{1,0:T(8,128)(2,1)S(1)} %fusion.6.after_ref), custom_call_target="tpu_custom_call" | custom-call | bytes 12652572 | tf_op jit(solution)/shard_map/pallas_call | solution.py:24
  15.0 0.0 collective-permute-done.1
  15.0 1.6 %collective-permute-done.2 = bf16[128,256]{1,0:T(8,128)(2,1)S(1)} collective-permute-done((bf16[128,256]{1,0:T(8,128)(2,1)S(1)}, bf16[128,256]{1,0:T(8,128)(2,1)S(1)}, u32[]{:S(2)}, u32[]{:S(2)}) %collective-permute-start.2) | collective-permute-done | bytes 65568 | tf_op jit(solution)/shard_map/ppermute | solution.py:306
  16.6 0.0 collective-permute-done.3
  16.6 0.1 fusion.5
  16.6 1.6 %collective-permute-start.4 = (bf16[128,256]{1,0:T(8,128)(2,1)S(1)}, bf16[128,256]{1,0:T(8,128)(2,1)S(1)}, u32[]{:S(2)}, u32[]{:S(2)}) collective-permute-start(bf16[128,256]{1,0:T(8,128)(2,1)S(1)} %get-tuple-element.62.after_ref), channel_id=1, source_target_pairs={{0,4},{4,0},{8,12},{12,8},{16,20},{20,16},{24,28},{28,24},{1,5},{5... | collective-permute-start | bytes 196616 | tf_op jit(solution)/shard_map/ppermute | solution.py:382
  18.2 2.8 %shard_map.103 = (bf16[2048,1024]{1,0:T(8,128)(2,1)S(1)}, f32[8,128]{1,0:T(8,128)S(1)}) custom-call(s32[7]{0:T(128)S(1)} %stack.24.scalars, bf16[2,2048,1024]{2,1,0:T(8,128)(2,1)} %bitcast.17, bf16[128,256]{1,0:T(8,128)(2,1)S(1)} %get-tuple-element.62.after_ref), custom_call_target="tpu_custom_call" | custom-call | bytes 12652572 | tf_op jit(solution)/shard_map/pallas_call | solution.py:24
  21.0 0.0 collective-permute-done.4.other_ref
  21.0 0.9 %shard_map.104 = (bf16[32,512]{1,0:T(8,128)(2,1)S(1)}, bf16[32,512]{1,0:T(8,128)(2,1)S(1)}, bf16[32,512]{1,0:T(8,128)(2,1)S(1)}, bf16[32,512]{1,0:T(8,128)(2,1)S(1)}) custom-call(s32[7]{0:T(128)S(1)} %stack.24.scalars, f32[128,512]{1,0:T(8,128)S(1)} %shard_map.101.within_ref, bf16[128,512]{1,0:T(8,128)(2,1)S(1)} %get-tuple-element.55.queries, ...), custom_call_target="tpu_custom_call" | custom-call | flops 33554432 | bytes 862236 | tf_op jit(solution)/shard_map/pallas_call | solution.py:24
  21.9 0.1 collective-permute-start.5
  22.0 1.6 %collective-permute-start.6 = (bf16[32,512]{1,0:T(8,128)(2,1)S(1)}, bf16[32,512]{1,0:T(8,128)(2,1)S(1)}, u32[]{:S(2)}, u32[]{:S(2)}) collective-permute-start(bf16[32,512]{1,0:T(8,128)(2,1)S(1)} %get-tuple-element.66), channel_id=1, source_target_pairs={{0,2},{1,3},{2,0},{3,1},{4,6},{5,7},{6,4},{7,5},{8,10},{9,11},{10,... | collective-permute-start | bytes 98312 | tf_op jit(solution)/shard_map/ppermute | solution.py:316
  23.5 0.3 collective-permute-start.7
  23.8 0.1 fusion.10
  23.9 1.7 %collective-permute-done.5 = bf16[32,512]{1,0:T(8,128)(2,1)S(1)} collective-permute-done((bf16[32,512]{1,0:T(8,128)(2,1)S(1)}, bf16[32,512]{1,0:T(8,128)(2,1)S(1)}, u32[]{:S(2)}, u32[]{:S(2)}) %collective-permute-start.5) | collective-permute-done | bytes 32800 | tf_op jit(solution)/shard_map/ppermute | solution.py:316
  25.6 0.4 collective-permute-done.6
  26.0 0.0 collective-permute-done.7
  26.0 0.1 fusion
  26.2 0.1 fusion.2
  26.3 1.5 %collective-permute-start.10 = (bf16[32,2176]{1,0:T(8,128)(2,1)S(1)}, bf16[32,2176]{1,0:T(8,128)(2,1)S(1)}, u32[]{:S(2)}, u32[]{:S(2)}) collective-permute-start(bf16[32,2176]{1,0:T(8,128)(2,1)S(1)} %pad_maximum_fusion.refs_0_), channel_id=1, source_target_pairs={{0,4},{8,0},{16,8},{24,16},{28,24},{20,28},{12,20},{4,12},{1,5},{9... | collective-permute-start | bytes 417800 | tf_op jit(solution)/shard_map/ppermute | solution.py:218
  27.8 0.6 collective-permute-start.8
  28.4 3.1 %collective-permute-start.12 = (bf16[32,2176]{1,0:T(8,128)(2,1)S(1)}, bf16[32,2176]{1,0:T(8,128)(2,1)S(1)}, u32[]{:S(2)}, u32[]{:S(2)}) collective-permute-start(bf16[32,2176]{1,0:T(8,128)(2,1)S(1)} %pad_maximum_fusion.refs_0_), channel_id=1, source_target_pairs={{0,28},{8,20},{16,12},{24,4},{28,0},{20,8},{12,16},{4,24},{1,29},{... | collective-permute-start | bytes 417800 | tf_op jit(solution)/shard_map/ppermute | solution.py:218
  31.5 0.8 %collective-permute-done.10.refs_3_ = bf16[32,2176]{1,0:T(8,128)(2,1)S(1)} collective-permute-done((bf16[32,2176]{1,0:T(8,128)(2,1)S(1)}, bf16[32,2176]{1,0:T(8,128)(2,1)S(1)}, u32[]{:S(2)}, u32[]{:S(2)}) %collective-permute-start.10) | collective-permute-done | bytes 139296 | tf_op jit(solution)/shard_map/ppermute | solution.py:218
  32.3 1.5 %collective-permute-start.11 = (bf16[32,2176]{1,0:T(8,128)(2,1)S(1)}, bf16[32,2176]{1,0:T(8,128)(2,1)S(1)}, u32[]{:S(2)}, u32[]{:S(2)}) collective-permute-start(bf16[32,2176]{1,0:T(8,128)(2,1)S(1)} %collective-permute-done.10.refs_3_), channel_id=1, source_target_pairs={{0,4},{8,0},{16,8},{24,16},{28,24},{20,28},{12,20},{4,12},{1,5},{9... | collective-permute-start | bytes 417800 | tf_op jit(solution)/shard_map/ppermute | solution.py:218
  33.8 0.6 collective-permute-start.9
  34.3 2.8 %shard_map.105 = (bf16[1024,2048]{1,0:T(8,128)(2,1)S(1)}, f32[8,128]{1,0:T(8,128)S(1)}) custom-call(s32[7]{0:T(128)S(1)} %stack.24.scalars, bf16[1,1024,2048]{2,1,0:T(8,128)(2,1)} %source.1, bf16[32,2176]{1,0:T(8,128)(2,1)S(1)} %collective-permute-done.8.after_ref.refs_1_), custom_call_target="tpu_custom_call" | custom-call | bytes 8531996 | tf_op jit(solution)/shard_map/pallas_call | solution.py:24
  37.1 1.9 %collective-permute-done.12.refs_2_ = bf16[32,2176]{1,0:T(8,128)(2,1)S(1)} collective-permute-done((bf16[32,2176]{1,0:T(8,128)(2,1)S(1)}, bf16[32,2176]{1,0:T(8,128)(2,1)S(1)}, u32[]{:S(2)}, u32[]{:S(2)}) %collective-permute-start.12) | collective-permute-done | bytes 139296 | tf_op jit(solution)/shard_map/ppermute | solution.py:218
  38.9 0.8 %collective-permute-done.11.refs_4_ = bf16[32,2176]{1,0:T(8,128)(2,1)S(1)} collective-permute-done((bf16[32,2176]{1,0:T(8,128)(2,1)S(1)}, bf16[32,2176]{1,0:T(8,128)(2,1)S(1)}, u32[]{:S(2)}, u32[]{:S(2)}) %collective-permute-start.11) | collective-permute-done | bytes 139296 | tf_op jit(solution)/shard_map/ppermute | solution.py:218
  39.8 1.1 %collective-permute-done.9.refs_2_ = bf16[32,2176]{1,0:T(8,128)(2,1)S(1)} collective-permute-done((bf16[32,2176]{1,0:T(8,128)(2,1)S(1)}, bf16[32,2176]{1,0:T(8,128)(2,1)S(1)}, u32[]{:S(2)}, u32[]{:S(2)}) %collective-permute-start.9) | collective-permute-done | bytes 139296 | tf_op jit(solution)/shard_map/ppermute | solution.py:218
  40.9 1.5 %collective-permute-start.13 = (bf16[32,2176]{1,0:T(8,128)(2,1)S(1)}, bf16[32,2176]{1,0:T(8,128)(2,1)S(1)}, u32[]{:S(2)}, u32[]{:S(2)}) collective-permute-start(bf16[32,2176]{1,0:T(8,128)(2,1)S(1)} %collective-permute-done.9.refs_2_), channel_id=1, source_target_pairs={{0,8},{8,16},{16,24},{24,28},{28,20},{20,12},{12,4},{4,0},{1,9},{9... | collective-permute-start | bytes 417800 | tf_op jit(solution)/shard_map/ppermute | solution.py:218
  42.3 0.6 collective-permute-start.14
  42.9 2.9 %shard_map.106 = (bf16[32,2048]{1,0:T(8,128)(2,1)S(1)}, bf16[32,2048]{1,0:T(8,128)(2,1)S(1)}, bf16[32,2048]{1,0:T(8,128)(2,1)S(1)}, bf16[32,2048]{1,0:T(8,128)(2...) custom-call(s32[7]{0:T(128)S(1)} %stack.24.scalars, f32[8,128]{1,0:T(8,128)S(1)} %get-tuple-element.71.sign_ref, ...), custom_call_target="tpu_custom_call" | custom-call | flops 2013265920 | bytes 13942812 | tf_op jit(solution)/shard_map/pallas_call | solution.py:24
  45.8 0.1 collective-permute-done.13.refs_0_
  45.9 1.5 %collective-permute-done.14.refs_1_ = bf16[32,2176]{1,0:T(8,128)(2,1)S(1)} collective-permute-done((bf16[32,2176]{1,0:T(8,128)(2,1)S(1)}, bf16[32,2176]{1,0:T(8,128)(2,1)S(1)}, u32[]{:S(2)}, u32[]{:S(2)}) %collective-permute-start.14) | collective-permute-done | bytes 139296 | tf_op jit(solution)/shard_map/ppermute | solution.py:218
  47.4 2.9 %shard_map.107 = (bf16[32,2048]{1,0:T(8,128)(2,1)S(1)}, bf16[32,2048]{1,0:T(8,128)(2,1)S(1)}, bf16[32,2048]{1,0:T(8,128)(2,1)S(1)}, f32[8,128]{1,0:T(8,128)}) custom-call(s32[7]{0:T(128)S(1)} %stack.24.scalars, f32[8,128]{1,0:T(8,128)S(1)} %get-tuple-element.80.sign_ref, bf16[2048,1024]{1,0:T(8,128)(2,1)S(1)} %get-tuple-element.72.gate_ref, ...), custom_call_target="tpu_custom_call" | custom-call | flops 1610612736 | bytes 13402140 | tf_op jit(solution)/shard_map/pallas_call | solution.py:24
  50.3 1.5 %collective-permute-start.15 = (bf16[32,2048]{1,0:T(8,128)(2,1)S(1)}, bf16[32,2048]{1,0:T(8,128)(2,1)S(1)}, u32[]{:S(2)}, u32[]{:S(2)}) collective-permute-start(bf16[32,2048]{1,0:T(8,128)(2,1)S(1)} %get-tuple-element.84), channel_id=1, source_target_pairs={{0,8},{8,16},{16,24},{24,28},{28,20},{20,12},{12,4},{4,0},{1,9},{9... | collective-permute-start | bytes 393224 | tf_op jit(solution)/shard_map/ppermute | solution.py:218
  51.9 0.5 collective-permute-start.18
  52.4 3.3 %collective-permute-start.21 = (bf16[32,2048]{1,0:T(8,128)(2,1)S(1)}, bf16[32,2048]{1,0:T(8,128)(2,1)S(1)}, u32[]{:S(2)}, u32[]{:S(2)}) collective-permute-start(bf16[32,2048]{1,0:T(8,128)(2,1)S(1)} %get-tuple-element.90), channel_id=1, source_target_pairs={{0,28},{8,20},{16,12},{24,4},{28,0},{20,8},{12,16},{4,24},{1,29},{... | collective-permute-start | bytes 393224 | tf_op jit(solution)/shard_map/ppermute | solution.py:218
  55.6 0.1 collective-permute-done.15
  55.8 2.5 %collective-permute-start.16 = (bf16[32,2048]{1,0:T(8,128)(2,1)S(1)}, bf16[32,2048]{1,0:T(8,128)(2,1)S(1)}, u32[]{:S(2)}, u32[]{:S(2)}) collective-permute-start(bf16[32,2048]{1,0:T(8,128)(2,1)S(1)} %add_convert_fusion.3), channel_id=1, source_target_pairs={{0,8},{8,16},{16,24},{24,28},{28,20},{20,12},{12,4},{4,0},{1,9},{9... | collective-permute-start | bytes 393224 | tf_op jit(solution)/shard_map/ppermute | solution.py:218
  58.4 1.8 %collective-permute-start.19 = (bf16[32,2048]{1,0:T(8,128)(2,1)S(1)}, bf16[32,2048]{1,0:T(8,128)(2,1)S(1)}, u32[]{:S(2)}, u32[]{:S(2)}) collective-permute-start(bf16[32,2048]{1,0:T(8,128)(2,1)S(1)} %add_convert_fusion.1), channel_id=1, source_target_pairs={{0,4},{8,0},{16,8},{24,16},{28,24},{20,28},{12,20},{4,12},{1,5},{9... | collective-permute-start | bytes 393224 | tf_op jit(solution)/shard_map/ppermute | solution.py:218
  60.2 2.8 %collective-permute-done.16 = bf16[32,2048]{1,0:T(8,128)(2,1)S(1)} collective-permute-done((bf16[32,2048]{1,0:T(8,128)(2,1)S(1)}, bf16[32,2048]{1,0:T(8,128)(2,1)S(1)}, u32[]{:S(2)}, u32[]{:S(2)}) %collective-permute-start.16) | collective-permute-done | bytes 131104 | tf_op jit(solution)/shard_map/ppermute | solution.py:218
  63.1 0.3 collective-permute-start.17
  63.4 0.6 collective-permute-done.19
  64.0 2.5 %collective-permute-start.20 = (bf16[32,2048]{1,0:T(8,128)(2,1)S(1)}, bf16[32,2048]{1,0:T(8,128)(2,1)S(1)}, u32[]{:S(2)}, u32[]{:S(2)}) collective-permute-start(bf16[32,2048]{1,0:T(8,128)(2,1)S(1)} %add_convert_fusion), channel_id=1, source_target_pairs={{0,4},{8,0},{16,8},{24,16},{28,24},{20,28},{12,20},{4,12},{1,5},{9... | collective-permute-start | bytes 393224 | tf_op jit(solution)/shard_map/ppermute | solution.py:218
  66.5 1.6 %collective-permute-done.17 = bf16[32,2048]{1,0:T(8,128)(2,1)S(1)} collective-permute-done((bf16[32,2048]{1,0:T(8,128)(2,1)S(1)}, bf16[32,2048]{1,0:T(8,128)(2,1)S(1)}, u32[]{:S(2)}, u32[]{:S(2)}) %collective-permute-start.17) | collective-permute-done | bytes 131104 | tf_op jit(solution)/shard_map/ppermute | solution.py:218
  68.1 0.9 %collective-permute-done.20 = bf16[32,2048]{1,0:T(8,128)(2,1)S(1)} collective-permute-done((bf16[32,2048]{1,0:T(8,128)(2,1)S(1)}, bf16[32,2048]{1,0:T(8,128)(2,1)S(1)}, u32[]{:S(2)}, u32[]{:S(2)}) %collective-permute-start.20) | collective-permute-done | bytes 131104 | tf_op jit(solution)/shard_map/ppermute | solution.py:218
  69.0 0.1 fusion.3
  69.1 0.1 collective-permute-start.22
  69.2 1.4 %collective-permute-start.23 = (bf16[32,512]{1,0:T(8,128)(2,1)S(1)}, bf16[32,512]{1,0:T(8,128)(2,1)S(1)}, u32[]{:S(2)}, u32[]{:S(2)}) collective-permute-start(bf16[32,512]{1,0:T(8,128)(2,1)S(1)} %get-tuple-element.102), channel_id=1, source_target_pairs={{0,2},{1,3},{2,0},{3,1},{4,6},{5,7},{6,4},{7,5},{8,10},{9,11},{10,... | collective-permute-start | bytes 98312 | tf_op jit(solution)/shard_map/ppermute | solution.py:316
  70.6 0.5 collective-permute-start.24
  71.1 1.7 %collective-permute-done.22 = bf16[32,512]{1,0:T(8,128)(2,1)S(1)} collective-permute-done((bf16[32,512]{1,0:T(8,128)(2,1)S(1)}, bf16[32,512]{1,0:T(8,128)(2,1)S(1)}, u32[]{:S(2)}, u32[]{:S(2)}) %collective-permute-start.22) | collective-permute-done | bytes 32800 | tf_op jit(solution)/shard_map/ppermute | solution.py:316
  72.8 0.4 collective-permute-done.23
  73.2 0.7 pad_maximum_fusion.2
  (23 shorter events, 0.3 us)
Async XLA Ops:
  0.0 4.9 %copy-start = (f32[128,8]{0,1:T(8,128)S(1)}, f32[128,8]{0,1:T(8,128)}, u32[]{:S(2)}) copy-start(f32[128,8]{0,1:T(8,128)} %param.17) | copy-start | bytes 12292
  1.9 5.3 %collective-permute-start = (bf16[128,256]{1,0:T(8,128)(2,1)S(1)}, bf16[128,256]{1,0:T(8,128)(2,1)S(1)}, u32[]{:S(2)}, u32[]{:S(2)}) collective-permute-start(bf16[128,256]{1,0:T(8,128)(2,1)S(1)} %get-tuple-element.52), channel_id=1, source_target_pairs={{0,4},{4,0},{8,12},{12,8},{16,20},{20,16},{24,28},{28,24},{1,5},{5... | collective-permute-start | bytes 196616 | tf_op jit(solution)/shard_map/ppermute | solution.py:366
  7.2 7.8 %collective-permute-start.1 = (bf16[128,256]{1,0:T(8,128)(2,1)S(1)}, bf16[128,256]{1,0:T(8,128)(2,1)S(1)}, u32[]{:S(2)}, u32[]{:S(2)}) collective-permute-start(bf16[128,256]{1,0:T(8,128)(2,1)S(1)} %fusion.6.after_ref), channel_id=1, source_target_pairs={{0,24},{4,28},{8,16},{12,20},{16,8},{20,12},{24,0},{28,4},{1,25},{... | collective-permute-start | bytes 196616 | tf_op jit(solution)/shard_map/ppermute | solution.py:306
  11.4 5.2 %collective-permute-start.2 = (bf16[128,256]{1,0:T(8,128)(2,1)S(1)}, bf16[128,256]{1,0:T(8,128)(2,1)S(1)}, u32[]{:S(2)}, u32[]{:S(2)}) collective-permute-start(bf16[128,256]{1,0:T(8,128)(2,1)S(1)} %fusion.6.after_ref), channel_id=1, source_target_pairs={{0,16},{4,20},{8,24},{12,28},{16,0},{20,4},{24,8},{28,12},{1,17},{... | collective-permute-start | bytes 196616 | tf_op jit(solution)/shard_map/ppermute | solution.py:306
  11.4 5.2 %collective-permute-start.3 = (bf16[128,256]{1,0:T(8,128)(2,1)S(1)}, bf16[128,256]{1,0:T(8,128)(2,1)S(1)}, u32[]{:S(2)}, u32[]{:S(2)}) collective-permute-start(bf16[128,256]{1,0:T(8,128)(2,1)S(1)} %fusion.6.after_ref), channel_id=1, source_target_pairs={{0,8},{4,12},{8,0},{12,4},{16,24},{20,28},{24,16},{28,20},{1,9},{5... | collective-permute-start | bytes 196616 | tf_op jit(solution)/shard_map/ppermute | solution.py:306
  16.6 4.3 %collective-permute-start.4 = (bf16[128,256]{1,0:T(8,128)(2,1)S(1)}, bf16[128,256]{1,0:T(8,128)(2,1)S(1)}, u32[]{:S(2)}, u32[]{:S(2)}) collective-permute-start(bf16[128,256]{1,0:T(8,128)(2,1)S(1)} %get-tuple-element.62.after_ref), channel_id=1, source_target_pairs={{0,4},{4,0},{8,12},{12,8},{16,20},{20,16},{24,28},{28,24},{1,5},{5... | collective-permute-start | bytes 196616 | tf_op jit(solution)/shard_map/ppermute | solution.py:382
  18.2 8.0 %copy-start.1 = (f32[2048]{0:T(1024)S(1)}, f32[2048]{0:T(1024)}, u32[]{:S(2)}) copy-start(f32[2048]{0:T(1024)} %param.15) | copy-start | bytes 24580
  21.9 3.7 %collective-permute-start.5 = (bf16[32,512]{1,0:T(8,128)(2,1)S(1)}, bf16[32,512]{1,0:T(8,128)(2,1)S(1)}, u32[]{:S(2)}, u32[]{:S(2)}) collective-permute-start(bf16[32,512]{1,0:T(8,128)(2,1)S(1)} %get-tuple-element.65), channel_id=1, source_target_pairs={{0,3},{1,2},{2,1},{3,0},{4,7},{5,6},{6,5},{7,4},{8,11},{9,10},{10,... | collective-permute-start | bytes 98312 | tf_op jit(solution)/shard_map/ppermute | solution.py:316
  22.0 4.0 %collective-permute-start.6 = (bf16[32,512]{1,0:T(8,128)(2,1)S(1)}, bf16[32,512]{1,0:T(8,128)(2,1)S(1)}, u32[]{:S(2)}, u32[]{:S(2)}) collective-permute-start(bf16[32,512]{1,0:T(8,128)(2,1)S(1)} %get-tuple-element.66), channel_id=1, source_target_pairs={{0,2},{1,3},{2,0},{3,1},{4,6},{5,7},{6,4},{7,5},{8,10},{9,11},{10,... | collective-permute-start | bytes 98312 | tf_op jit(solution)/shard_map/ppermute | solution.py:316
  23.5 2.4 %collective-permute-start.7 = (bf16[32,512]{1,0:T(8,128)(2,1)S(1)}, bf16[32,512]{1,0:T(8,128)(2,1)S(1)}, u32[]{:S(2)}, u32[]{:S(2)}) collective-permute-start(bf16[32,512]{1,0:T(8,128)(2,1)S(1)} %get-tuple-element.67), channel_id=1, source_target_pairs={{0,1},{1,0},{2,3},{3,2},{4,5},{5,4},{6,7},{7,6},{8,9},{9,8},{10,11... | collective-permute-start | bytes 98312 | tf_op jit(solution)/shard_map/ppermute | solution.py:316
  26.3 6.0 %collective-permute-start.10 = (bf16[32,2176]{1,0:T(8,128)(2,1)S(1)}, bf16[32,2176]{1,0:T(8,128)(2,1)S(1)}, u32[]{:S(2)}, u32[]{:S(2)}) collective-permute-start(bf16[32,2176]{1,0:T(8,128)(2,1)S(1)} %pad_maximum_fusion.refs_0_), channel_id=1, source_target_pairs={{0,4},{8,0},{16,8},{24,16},{28,24},{20,28},{12,20},{4,12},{1,5},{9... | collective-permute-start | bytes 417800 | tf_op jit(solution)/shard_map/ppermute | solution.py:218
  27.8 5.9 %collective-permute-start.8 = (bf16[32,2176]{1,0:T(8,128)(2,1)S(1)}, bf16[32,2176]{1,0:T(8,128)(2,1)S(1)}, u32[]{:S(2)}, u32[]{:S(2)}) collective-permute-start(bf16[32,2176]{1,0:T(8,128)(2,1)S(1)} %pad_maximum_fusion.refs_0_), channel_id=1, source_target_pairs={{0,8},{8,16},{16,24},{24,28},{28,20},{20,12},{12,4},{4,0},{1,9},{9... | collective-permute-start | bytes 417800 | tf_op jit(solution)/shard_map/ppermute | solution.py:218
  28.4 10.6 %collective-permute-start.12 = (bf16[32,2176]{1,0:T(8,128)(2,1)S(1)}, bf16[32,2176]{1,0:T(8,128)(2,1)S(1)}, u32[]{:S(2)}, u32[]{:S(2)}) collective-permute-start(bf16[32,2176]{1,0:T(8,128)(2,1)S(1)} %pad_maximum_fusion.refs_0_), channel_id=1, source_target_pairs={{0,28},{8,20},{16,12},{24,4},{28,0},{20,8},{12,16},{4,24},{1,29},{... | collective-permute-start | bytes 417800 | tf_op jit(solution)/shard_map/ppermute | solution.py:218
  32.3 7.5 %collective-permute-start.11 = (bf16[32,2176]{1,0:T(8,128)(2,1)S(1)}, bf16[32,2176]{1,0:T(8,128)(2,1)S(1)}, u32[]{:S(2)}, u32[]{:S(2)}) collective-permute-start(bf16[32,2176]{1,0:T(8,128)(2,1)S(1)} %collective-permute-done.10.refs_3_), channel_id=1, source_target_pairs={{0,4},{8,0},{16,8},{24,16},{28,24},{20,28},{12,20},{4,12},{1,5},{9... | collective-permute-start | bytes 417800 | tf_op jit(solution)/shard_map/ppermute | solution.py:218
  33.8 7.1 %collective-permute-start.9 = (bf16[32,2176]{1,0:T(8,128)(2,1)S(1)}, bf16[32,2176]{1,0:T(8,128)(2,1)S(1)}, u32[]{:S(2)}, u32[]{:S(2)}) collective-permute-start(bf16[32,2176]{1,0:T(8,128)(2,1)S(1)} %collective-permute-done.8.after_ref.refs_1_), channel_id=1, source_target_pairs={{0,8},{8,16},{16,24},{24,28},{28,20},{20,12},{12,4},{4,0},{1,9},{9... | collective-permute-start | bytes 417800 | tf_op jit(solution)/shard_map/ppermute | solution.py:218
  40.9 5.1 %collective-permute-start.13 = (bf16[32,2176]{1,0:T(8,128)(2,1)S(1)}, bf16[32,2176]{1,0:T(8,128)(2,1)S(1)}, u32[]{:S(2)}, u32[]{:S(2)}) collective-permute-start(bf16[32,2176]{1,0:T(8,128)(2,1)S(1)} %collective-permute-done.9.refs_2_), channel_id=1, source_target_pairs={{0,8},{8,16},{16,24},{24,28},{28,20},{20,12},{12,4},{4,0},{1,9},{9... | collective-permute-start | bytes 417800 | tf_op jit(solution)/shard_map/ppermute | solution.py:218
  42.3 5.1 %collective-permute-start.14 = (bf16[32,2176]{1,0:T(8,128)(2,1)S(1)}, bf16[32,2176]{1,0:T(8,128)(2,1)S(1)}, u32[]{:S(2)}, u32[]{:S(2)}) collective-permute-start(bf16[32,2176]{1,0:T(8,128)(2,1)S(1)} %collective-permute-done.11.refs_4_), channel_id=1, source_target_pairs={{0,4},{8,0},{16,8},{24,16},{28,24},{20,28},{12,20},{4,12},{1,5},{9... | collective-permute-start | bytes 417800 | tf_op jit(solution)/shard_map/ppermute | solution.py:218
  50.3 5.4 %collective-permute-start.15 = (bf16[32,2048]{1,0:T(8,128)(2,1)S(1)}, bf16[32,2048]{1,0:T(8,128)(2,1)S(1)}, u32[]{:S(2)}, u32[]{:S(2)}) collective-permute-start(bf16[32,2048]{1,0:T(8,128)(2,1)S(1)} %get-tuple-element.84), channel_id=1, source_target_pairs={{0,8},{8,16},{16,24},{24,28},{28,20},{20,12},{12,4},{4,0},{1,9},{9... | collective-permute-start | bytes 393224 | tf_op jit(solution)/shard_map/ppermute | solution.py:218
  51.9 6.5 %collective-permute-start.18 = (bf16[32,2048]{1,0:T(8,128)(2,1)S(1)}, bf16[32,2048]{1,0:T(8,128)(2,1)S(1)}, u32[]{:S(2)}, u32[]{:S(2)}) collective-permute-start(bf16[32,2048]{1,0:T(8,128)(2,1)S(1)} %get-tuple-element.87), channel_id=1, source_target_pairs={{0,4},{8,0},{16,8},{24,16},{28,24},{20,28},{12,20},{4,12},{1,5},{9... | collective-permute-start | bytes 393224 | tf_op jit(solution)/shard_map/ppermute | solution.py:218
  52.4 14.1 %collective-permute-start.21 = (bf16[32,2048]{1,0:T(8,128)(2,1)S(1)}, bf16[32,2048]{1,0:T(8,128)(2,1)S(1)}, u32[]{:S(2)}, u32[]{:S(2)}) collective-permute-start(bf16[32,2048]{1,0:T(8,128)(2,1)S(1)} %get-tuple-element.90), channel_id=1, source_target_pairs={{0,28},{8,20},{16,12},{24,4},{28,0},{20,8},{12,16},{4,24},{1,29},{... | collective-permute-start | bytes 393224 | tf_op jit(solution)/shard_map/ppermute | solution.py:218
  55.8 7.2 %collective-permute-start.16 = (bf16[32,2048]{1,0:T(8,128)(2,1)S(1)}, bf16[32,2048]{1,0:T(8,128)(2,1)S(1)}, u32[]{:S(2)}, u32[]{:S(2)}) collective-permute-start(bf16[32,2048]{1,0:T(8,128)(2,1)S(1)} %add_convert_fusion.3), channel_id=1, source_target_pairs={{0,8},{8,16},{16,24},{24,28},{28,20},{20,12},{12,4},{4,0},{1,9},{9... | collective-permute-start | bytes 393224 | tf_op jit(solution)/shard_map/ppermute | solution.py:218
  58.4 5.6 %collective-permute-start.19 = (bf16[32,2048]{1,0:T(8,128)(2,1)S(1)}, bf16[32,2048]{1,0:T(8,128)(2,1)S(1)}, u32[]{:S(2)}, u32[]{:S(2)}) collective-permute-start(bf16[32,2048]{1,0:T(8,128)(2,1)S(1)} %add_convert_fusion.1), channel_id=1, source_target_pairs={{0,4},{8,0},{16,8},{24,16},{28,24},{20,28},{12,20},{4,12},{1,5},{9... | collective-permute-start | bytes 393224 | tf_op jit(solution)/shard_map/ppermute | solution.py:218
  63.1 5.0 %collective-permute-start.17 = (bf16[32,2048]{1,0:T(8,128)(2,1)S(1)}, bf16[32,2048]{1,0:T(8,128)(2,1)S(1)}, u32[]{:S(2)}, u32[]{:S(2)}) collective-permute-start(bf16[32,2048]{1,0:T(8,128)(2,1)S(1)} %add_convert_fusion.2), channel_id=1, source_target_pairs={{0,8},{8,16},{16,24},{24,28},{28,20},{20,12},{12,4},{4,0},{1,9},{9... | collective-permute-start | bytes 393224 | tf_op jit(solution)/shard_map/ppermute | solution.py:218
  64.0 5.1 %collective-permute-start.20 = (bf16[32,2048]{1,0:T(8,128)(2,1)S(1)}, bf16[32,2048]{1,0:T(8,128)(2,1)S(1)}, u32[]{:S(2)}, u32[]{:S(2)}) collective-permute-start(bf16[32,2048]{1,0:T(8,128)(2,1)S(1)} %add_convert_fusion), channel_id=1, source_target_pairs={{0,4},{8,0},{16,8},{24,16},{28,24},{20,28},{12,20},{4,12},{1,5},{9... | collective-permute-start | bytes 393224 | tf_op jit(solution)/shard_map/ppermute | solution.py:218
  69.1 3.6 %collective-permute-start.22 = (bf16[32,512]{1,0:T(8,128)(2,1)S(1)}, bf16[32,512]{1,0:T(8,128)(2,1)S(1)}, u32[]{:S(2)}, u32[]{:S(2)}) collective-permute-start(bf16[32,512]{1,0:T(8,128)(2,1)S(1)} %get-tuple-element.101), channel_id=1, source_target_pairs={{0,3},{1,2},{2,1},{3,0},{4,7},{5,6},{6,5},{7,4},{8,11},{9,10},{10,... | collective-permute-start | bytes 98312 | tf_op jit(solution)/shard_map/ppermute | solution.py:316
  69.2 4.0 %collective-permute-start.23 = (bf16[32,512]{1,0:T(8,128)(2,1)S(1)}, bf16[32,512]{1,0:T(8,128)(2,1)S(1)}, u32[]{:S(2)}, u32[]{:S(2)}) collective-permute-start(bf16[32,512]{1,0:T(8,128)(2,1)S(1)} %get-tuple-element.102), channel_id=1, source_target_pairs={{0,2},{1,3},{2,0},{3,1},{4,6},{5,7},{6,4},{7,5},{8,10},{9,11},{10,... | collective-permute-start | bytes 98312 | tf_op jit(solution)/shard_map/ppermute | solution.py:316
  70.6 2.6 %collective-permute-start.24 = (bf16[32,512]{1,0:T(8,128)(2,1)S(1)}, bf16[32,512]{1,0:T(8,128)(2,1)S(1)}, u32[]{:S(2)}, u32[]{:S(2)}) collective-permute-start(bf16[32,512]{1,0:T(8,128)(2,1)S(1)} %get-tuple-element.100), channel_id=1, source_target_pairs={{0,1},{1,0},{2,3},{3,2},{4,5},{5,4},{6,7},{7,6},{8,9},{9,8},{10,11... | collective-permute-start | bytes 98312 | tf_op jit(solution)/shard_map/ppermute | solution.py:316
